TPU v7x, 128 devices: a whole 4x4x4 slice. The times are simulated.
128 devices in a mesh: batch: 8 (over y_hi, x), blk: 16 (over y_lo, z, core).
Axes of the slice: x: 4, y: 4 (y_hi: 2, y_lo: 2; y = y_hi * 2 + y_lo), z: 4, core: 2. Of those that a mesh axis runs over, the one named last changes fastest.
Arguments:
- tokens: bfloat16 [8, 2048, 2048], P('batch', 'blk'), may hold values from -6 to 6
- cotangent: bfloat16 [8, 2048, 2048], P('batch', 'blk'), may hold values from -6 to 6
- block_places: int32 [8, 16], P('batch'), may hold values from 0 to 15, each once within a row
- valid_counts: int32 [8, 16], P('batch'), may hold values from 96 to 128, as said below
- attn_gain: bfloat16 [2048], replicated, may hold values from 0.5 to 1.5
- mlp_gain: bfloat16 [2048], replicated, may hold values from 0.5 to 1.5
- query_weight: bfloat16 [2048, 2048], P('blk'), may hold values from -0.1875 to 0.1875
- key_weight: bfloat16 [2048, 256], P('blk'), may hold values from -0.1875 to 0.1875
- value_weight: bfloat16 [2048, 256], P('blk'), may hold values from -0.125 to 0.125
- output_weight: bfloat16 [2048, 2048], P('blk'), may hold values from -0.1875 to 0.1875
- gate_weight: bfloat16 [2048, 5632], P('blk'), may hold values from -0.125 to 0.125
- up_weight: bfloat16 [2048, 5632], P('blk'), may hold values from -0.125 to 0.125
- down_weight: bfloat16 [5632, 2048], P(None, 'blk'), may hold values from -0.078125 to 0.078125
Outputs:
- layer_out: bfloat16 [8, 2048, 2048], P('batch', 'blk')
- tokens_grad: bfloat16 [8, 2048, 2048], P('batch', 'blk')
- attn_gain_grad: float32 [2048], replicated
- mlp_gain_grad: float32 [2048], replicated
- query_grad: float32 [2048, 2048], P('blk')
- key_grad: float32 [2048, 256], P('blk')
- value_grad: float32 [2048, 256], P('blk')
- output_grad: float32 [2048, 2048], P('blk')
- gate_grad: float32 [2048, 5632], P('blk')
- up_grad: float32 [2048, 5632], P('blk')
- down_grad: float32 [5632, 2048], P(None, 'blk')
Inputs may be any that keep to these rules, and one draw needn't show every extreme that they name: `valid_counts`: tokens in use come first in each block; the rest are padding. In every sequence one block is full and one holds 96 tokens. Each row is a permutation: the blocks of a sequence stand in the array in this order, block b holding positions block_places * 128 onward.
All inputs are finite; a program needn't handle non-finite values.
Results may differ from a plain program's by a relative error of at most 0.029.
Values may be sent and summed in bfloat16 or wider, within the bound.
No kernel may reach another device: no remote copies, remote signals or barrier semaphores. Data moves between devices by JAX's collectives and lax.ppermute only.
A program may use at most 320 MiB of HBM per device.

v0:
```python
import functools
import itertools

import jax
import jax.numpy as jnp
from jax import lax
from jax.experimental import pallas as pl
from jax.experimental.pallas import tpu as pltpu
from jax.sharding import PartitionSpec as P

HEADS = 32
KV_HEADS = 4
HEAD = 64
D = 2048
FF = 5632
TOK = 128
WIDE = FF // 8
QUERY = HEADS * HEAD // 8
QKV = QUERY + HEAD
PACK = QUERY + QKV
epsilon = 1e-05
BOTH = ("batch", "blk")
ZC_GROUPS = [list(range(8)), list(range(8, 16))]
Y_GROUPS = [
    [(yh * 4 + x) * 16 + yl * 8 + zc for yh in range(2) for yl in range(2)] for x in range(4) for zc in range(8)
]
X_GROUPS = [[0, 1, 2, 3], [4, 5, 6, 7]]
BF = jnp.bfloat16
F32 = jnp.float32
MIB = 1024 * 1024
VMEM_MIB = 48
LOG2E = 1.4426950408889634
SCORE = HEAD**-0.5
SHIFT = 11.0


def device_index(yh, x, yl, z, c):
    return (((yh * 4 + x) * 2 + yl) * 4 + z) * 2 + c


def send(value, target):
    pairs = []
    for spot in itertools.product(range(2), range(4), range(2), range(4), range(2)):
        pairs.append((device_index(*spot), device_index(*target(*spot))))
    return lax.ppermute(value, BOTH, pairs)


def step(value, axis, way):
    def target(yh, x, yl, z, c):
        by = way * (1 - 2 * c)
        if axis == "x":
            x = (x + by) % 4
        elif axis == "z":
            z = (z + by) % 4
        else:
            y = (2 * yh + yl + by) % 4
            yh, yl = y // 2, y % 2
        return yh, x, yl, z, c

    return send(value, target)


def across(value, axis):
    def target(yh, x, yl, z, c):
        if axis == "x":
            x = (x + 2) % 4
        elif axis == "z":
            z = (z + 2) % 4
        else:
            yh = 1 - yh
        return yh, x, yl, z, c

    return send(value, target)


def swap(value):
    return send(value, lambda yh, x, yl, z, c: (yh, x, yl, z, 1 - c))


def to_half(value):
    return send(value, lambda yh, x, yl, z, c: (yh, x, 1 - yl, z, c))


def ring_gather(value, axis, forward=False):
    first = step(value, axis, 1)
    second = step(value, axis, -1)
    third = step(first, axis, 1) if forward else across(value, axis)
    return value, first, second, third


def add(*terms):
    total = terms[0].astype(F32)
    for term in terms[1:]:
        total = total + term.astype(F32)
    return total


def ring_scatter(own, before, after, far, axis):
    got = across(far, axis), step(before, axis, -1), step(after, axis, 1)
    return add(own, *got)


def sum_all(value):
    value = value + swap(value)
    for axis in ("z", "y", "x"):
        value = (value + across(value, axis)) + (step(value, axis, 1) + step(value, axis, -1))
    return value


def exchange_z(own, before, after, far):
    return own, step(after, "z", 1), step(before, "z", -1), across(far, "z")


def after(value, *others):
    return lax.optimization_barrier((value,) + others)[0]


def rms_scale(rows):
    return lax.rsqrt(jnp.mean(rows * rows, axis=-1, keepdims=True) + epsilon)


def norm_back(rows, scale, gain, upstream):
    weighted = gain * upstream
    return scale * weighted - rows * scale**3 * jnp.mean(weighted * rows, axis=-1, keepdims=True)


def lookup(entries, holder):
    matches = holder[:, None] == jnp.arange(entries.shape[0], dtype=jnp.int32)[None, :]
    return jnp.sum(jnp.where(matches, entries[None, :], 0), axis=1)


def dot(left, right):
    return jnp.dot(left, right, preferred_element_type=F32)


def dot_last(left, right):
    return lax.dot_general(left, right, (((1,), (1,)), ((), ())), preferred_element_type=F32)


def call(body, tables, grid, in_specs, out_specs, out_shape, scratch, micros, args, aliases=None):
    return pl.pallas_call(
        body,
        grid_spec=pltpu.PrefetchScalarGridSpec(
            num_scalar_prefetch=len(tables), grid=grid, in_specs=in_specs, out_specs=out_specs, scratch_shapes=scratch
        ),
        out_shape=out_shape,
        compiler_params=pltpu.CompilerParams(vmem_limit_bytes=VMEM_MIB * MIB),
        cost_estimate=pl.CostEstimate(flops=1000, bytes_accessed=micros * 3000000, transcendentals=0),
        input_output_aliases=aliases or {},
    )(*tables, *args)


def sds(shape, dtype=BF):
    return jax.ShapeDtypeStruct(shape, dtype)


def at_rows(start, count):
    return pl.ds(pl.multiple_of(start, 16), count)


def pack_kernel(spots, core, gate_ref, up_ref, down_ref, q_ref, k_ref, v_ref, mine_ref, other_ref, turned):
    first = core[0] == 0
    turned[...] = down_ref[...].astype(F32).T
    keys = [k_ref[:, HEAD * h : HEAD * (h + 1)].astype(F32) for h in range(KV_HEADS)]
    vals = [v_ref[:, HEAD * h : HEAD * (h + 1)].astype(F32) for h in range(KV_HEADS)]
    for r in range(4):
        chip = spots[1 + r]
        at = pl.ds(pl.multiple_of(chip * 2 * WIDE, 128), 2 * WIDE)
        parts = (
            gate_ref[:, at].astype(F32),
            up_ref[:, at].astype(F32),
            turned[at_rows(spots[0] * 32, 32), at],
        )
        for m, both in enumerate(parts):
            low, high = both[:, :WIDE], both[:, WIDE:]
            mine_ref[r, m] = jnp.where(first, low, high).astype(BF)
            other_ref[r, m] = jnp.where(first, high, low).astype(BF)
        both = q_ref[:, pl.ds(pl.multiple_of(chip * 2 * QUERY, 128), 2 * QUERY)].astype(F32)
        key, val = keys[0], vals[0]
        for h in range(1, KV_HEADS):
            key = jnp.where(chip == h, keys[h], key)
            val = jnp.where(chip == h, vals[h], val)
        rest = jnp.zeros((32, WIDE - QKV), F32)
        low = jnp.concatenate([both[:, :QUERY], key, rest], axis=1)
        high = jnp.concatenate([both[:, QUERY:], val, rest], axis=1)
        mine_ref[r, 3] = jnp.where(first, low, high).astype(BF)
        other_ref[r, 3] = jnp.where(first, high, low).astype(BF)


def pack(spots, core, gate, up, down, q, k, v):
    rows = lambda i, spots, core: (spots[0], 0)
    whole = lambda i, *_: (0, 0, 0, 0)
    shape = (4, 4, 32, WIDE)
    specs = [pl.BlockSpec((32, w.shape[1]), rows) for w in (gate, up, down, q, k, v)]
    specs[2] = pl.BlockSpec((FF, 128), lambda i, *_: (0, 0))
    return call(
        pack_kernel, (spots, core), (1,), specs, [pl.BlockSpec(shape, whole)] * 2, [sds(shape)] * 2,
        [pltpu.VMEM((128, FF), F32)], 4, (gate, up, down, q, k, v),
    )


def place_attn_kernel(slot, xs, halves, *refs):
    pieces, (qkv_ref, out_ref) = refs[:8], refs[8:]
    for e in range(2):
        for r in range(4):
            piece = pieces[4 * e + r][0]
            rows = at_rows(xs[r] * 32, 32)
            out_ref[halves[e], rows, :] = piece[:, :QUERY]
            qkv_ref[halves[e], 0, rows, :] = piece[:, QUERY:]


def place_attn(slot, xs, halves, pieces):
    qkv, out = call(
        place_attn_kernel, (slot, xs, halves), (8,),
        [pl.BlockSpec((1, 32, PACK), lambda i, *_: (i, 0, 0))] * 8,
        [
            pl.BlockSpec((2, 1, 128, QKV), lambda i, slot, *_: (0, slot[i], 0, 0)),
            pl.BlockSpec((2, 128, QUERY), lambda i, *_: (0, 0, i)),
        ],
        [sds((2, 8, 128, QKV)), sds((2, 128, D))], [], 2, tuple(pieces),
    )
    return qkv.reshape(D, QKV), out.reshape(QUERY, D)


def place_mlp_kernel(slot, halves, own_ref, other_ref, out_ref):
    for e, ref in enumerate((own_ref, other_ref)):
        for r in range(4):
            for m in range(3):
                out_ref[m, halves[e], 0, 32 * r : 32 * (r + 1), :] = ref[r, 0, m]


def place_mlp(slot, halves, own, other):
    out = call(
        place_mlp_kernel, (slot, halves), (8,),
        [pl.BlockSpec((4, 1, 3, 32, WIDE), lambda i, *_: (0, i, 0, 0, 0))] * 2,
        pl.BlockSpec((3, 2, 1, 128, WIDE), lambda i, slot, *_: (0, 0, slot[i], 0, 0)),
        sds((3, 2, 8, 128, WIDE)), [], 6, (own, other),
    )
    return out.reshape(3, D, WIDE)


PART = D // 4


def project_kernel(chunk, *refs):
    parts, w_ref, (q_ref, kv_ref), total = refs[:8], refs[8], refs[9:11], refs[11]
    k = pl.program_id(0)
    term = dot(jnp.concatenate([ref[...] for ref in parts], axis=0), w_ref[...])

    @pl.when(k == 0)
    def _():
        total[...] = term

    @pl.when(k > 0)
    def _():
        total[...] += term

    @pl.when(k == 3)
    def _():
        q_ref[...] = total[:, :QUERY].astype(BF)
        kv = total[:, QUERY:].astype(BF)
        kv_ref[0] = kv
        for r in range(8):
            kv_ref[1, TOK * r : TOK * (r + 1)] = kv[TOK * (r ^ 1) : TOK * ((r ^ 1) + 1)]


def project(chunk, rows, w):
    def rows_spec(r):
        return pl.BlockSpec((TOK, PART), lambda k, chunk: (chunk[r], k))

    return call(
        project_kernel, (chunk,), (4,),
        [rows_spec(r) for r in range(8)] + [pl.BlockSpec((PART, QKV), lambda k, chunk: (k, 0))],
        [
            pl.BlockSpec((8 * TOK, QUERY), lambda k, chunk: (0, 0)),
            pl.BlockSpec((2, 8 * TOK, HEAD), lambda k, chunk: (0, 0, 0)),
        ],
        [sds((8 * TOK, QUERY)), sds((2, 8 * TOK, HEAD))], [pltpu.VMEM((8 * TOK, QKV), F32)],
        5, (rows,) * 8 + (w,),
    )


def project_back_kernel(dq_ref, dkv_ref, w_ref, *out_refs):
    rows = jnp.concatenate([dq_ref[...], dkv_ref[...]], axis=1)
    grad = dot_last(rows, w_ref[...]).astype(BF)
    for r in range(8):
        out_refs[r][...] = grad[TOK * r : TOK * (r + 1)]


def project_back(dq, dkv, w):
    return call(
        project_back_kernel, (), (4,),
        [
            pl.BlockSpec((8 * TOK, QUERY), lambda k: (0, 0)),
            pl.BlockSpec((8 * TOK, HEAD), lambda k: (0, 0)),
            pl.BlockSpec((PART, QKV), lambda k: (k, 0)),
        ],
        [pl.BlockSpec((TOK, PART), lambda k: (0, k))] * 8, [sds((TOK, D))] * 8, [], 4, (dq, dkv, w),
    )


def head_rows(rows):
    return jnp.concatenate([rows[:, HEAD * h : HEAD * (h + 1)] for h in range(4)], axis=0)


def head_columns(rows):
    return jnp.concatenate([rows[TOK * h : TOK * (h + 1)] for h in range(4)], axis=1)


def attend_kernel(group, query_place, key_slot, q_ref, k_ref, v_ref, w_ref, o_ref, mine_ref, peer_ref, total):
    step_at = pl.program_id(0)
    place = query_place[2 * group + step_at]
    queries = head_rows(q_ref[...])

    def block(j, diagonal):
        at = pl.ds(pl.multiple_of(j * TOK, TOK), TOK)
        scores = dot_last(queries, k_ref[at, :])
        weights = 1.0 / (1.0 + jnp.exp2(SHIFT - scores * (SCORE * LOG2E)))
        if diagonal:
            row = lax.broadcasted_iota(jnp.int32, weights.shape, 0) & (TOK - 1)
            column = lax.broadcasted_iota(jnp.int32, weights.shape, 1)
            weights = jnp.where(column <= row, weights, 0.0)
        return dot(weights.astype(BF), v_ref[at, :])

    total[...] = block(key_slot[place], True)

    @pl.loop(0, place // 2)
    def _(p):
        total[...] += block(key_slot[2 * p], False) + block(key_slot[2 * p + 1], False)

    @pl.when(place % 2 == 1)
    def _():
        total[...] += block(key_slot[place - 1], False)

    out = head_columns(total[...]).astype(BF)
    o_ref[...] = out
    part = dot(out, w_ref[...]).astype(BF)

    @pl.when(step_at == 0)
    def _():
        mine_ref[...] = part

    @pl.when(step_at == 1)
    def _():
        peer_ref[...] = part


def attend(group, query_place, key_slot, q, k, v, w):
    whole = lambda i, *_: (0, 0)
    return call(
        functools.partial(attend_kernel, group), (query_place, key_slot), (2,),
        [
            pl.BlockSpec((TOK, QUERY), lambda i, *_: (2 * group + i, 0)),
            pl.BlockSpec(k.shape, whole),
            pl.BlockSpec(v.shape, whole),
            pl.BlockSpec(w.shape, whole),
        ],
        [pl.BlockSpec((TOK, QUERY), lambda i, *_: (i, 0)), pl.BlockSpec((TOK, D), whole), pl.BlockSpec((TOK, D), whole)],
        [sds((2 * TOK, QUERY)), sds((TOK, D)), sds((TOK, D))], [pltpu.VMEM((4 * TOK, HEAD), F32)],
        6, (q, k, v, w),
    )


def attend_back_kernel(query_place, key_slot, core, count, q_ref, g_ref, k_ref, v_ref, kt_ref, dq_ref, keep_ref, give_ref, total, dk_ref, dv_ref):
    step_at = pl.program_id(0)
    place = query_place[step_at]
    queries = head_rows(q_ref[...])
    grads = head_rows(g_ref[...])

    @pl.when(step_at == 0)
    def _():
        dk_ref[...] = jnp.zeros_like(dk_ref)
        dv_ref[...] = jnp.zeros_like(dv_ref)

    def block(j, diagonal):
        at = pl.ds(pl.multiple_of(j * TOK, TOK), TOK)
        scores = dot_last(k_ref[at, :], queries)
        sig = 1.0 / (1.0 + jnp.exp2(SHIFT - scores * (SCORE * LOG2E)))
        weights = sig
        if diagonal:
            row = lax.broadcasted_iota(jnp.int32, sig.shape, 1) & (TOK - 1)
            column = lax.broadcasted_iota(jnp.int32, sig.shape, 0)
            weights = jnp.where(column <= row, sig, 0.0)
        upstream = dot_last(v_ref[at, :], grads)
        score_grad = (upstream * weights * (1.0 - sig)).astype(BF)
        dk_ref[at, :] += dot(score_grad, queries)
        dv_ref[at, :] += dot(weights.astype(BF), grads)
        return dot(kt_ref[:, at], score_grad)

    total[...] = block(key_slot[place], True)

    @pl.loop(0, place // 2)
    def _(p):
        total[...] += block(key_slot[2 * p], False) + block(key_slot[2 * p + 1], False)

    @pl.when(place % 2 == 1)
    def _():
        total[...] += block(key_slot[place - 1], False)

    dq_ref[...] = head_columns((total[...] * SCORE).T).astype(BF)

    @pl.when(step_at == pl.num_programs(0) - 1)
    def _():
        first = core[0] == 0
        for j in range(16):
            key = dk_ref[j * TOK : (j + 1) * TOK, :] * SCORE
            value = dv_ref[j * TOK : (j + 1) * TOK, :]
            row = lax.broadcasted_iota(jnp.int32, value.shape, 0)
            value = jnp.where(row < count[j], value, 0.0)
            keep_ref[j * TOK : (j + 1) * TOK, :] = jnp.where(first, key, value).astype(BF)
            other = j ^ 1
            give_ref[other * TOK : (other + 1) * TOK, :] = jnp.where(first, value, key).astype(BF)


def attend_back(query_place, key_slot, core, count, q, g, k, v):
    rows = q.shape[0]
    whole = lambda i, *_: (0, 0)
    rows_spec = pl.BlockSpec((TOK, QUERY), lambda i, *_: (i, 0))
    kv_spec = pl.BlockSpec(k.shape, whole)
    return call(
        attend_back_kernel, (query_place, key_slot, core, count), (rows // TOK,),
        [rows_spec, rows_spec, kv_spec, kv_spec, pl.BlockSpec((HEAD, k.shape[0]), whole)],
        [rows_spec, kv_spec, kv_spec], [sds(q.shape), sds(k.shape), sds(v.shape)],
        [pltpu.VMEM((HEAD, 4 * TOK), F32), pltpu.VMEM(k.shape, F32), pltpu.VMEM(k.shape, F32)],
        28, (q, g, k, v, k.T),
    )


SPLIT = 2
DEEP = D // SPLIT
ROWS = 4 * TOK


def mlp_kernel(chunk, *refs):
    rows_refs, grads_refs, w_ref = refs[:4], refs[4:8], refs[8]
    z_ref, da_ref, dc_ref = refs[-11:-8]
    grad_refs = refs[-8:-4]
    weights, gate, up, back = refs[-4:]
    k = pl.program_id(0)

    @pl.when(k < SPLIT)
    def _():
        rows = jnp.concatenate([ref[...] for ref in rows_refs], axis=0)
        grads = jnp.concatenate([ref[...] for ref in grads_refs], axis=0)
        terms = (dot(rows, w_ref[0]), dot(rows, w_ref[1]), dot(grads, w_ref[2]))
        weights[k] = w_ref[:2]

        @pl.when(k == 0)
        def _():
            for total, term in zip((gate, up, back), terms):
                total[...] = term

        @pl.when(k > 0)
        def _():
            for total, term in zip((gate, up, back), terms):
                total[...] += term

    @pl.when(k == SPLIT - 1)
    def _():
        a, c, dz = gate[...], up[...], back[...]
        sig = 1.0 / (1.0 + jnp.exp(-a))
        silu = a * sig
        z_ref[...] = (silu * c).astype(BF)
        da_ref[...] = (dz * c * sig * (1.0 + a * (1.0 - sig))).astype(BF)
        dc_ref[...] = (dz * silu).astype(BF)

    @pl.when(k >= SPLIT)
    def _():
        j = k - SPLIT
        grad = dot_last(da_ref[...], weights[j, 0]) + dot_last(dc_ref[...], weights[j, 1])
        for r in range(4):
            grad_refs[r][...] = grad[TOK * r : TOK * (r + 1)].astype(BF)


def mlp_half(part, chunk, rows, grads, weights, kept):
    deep = lambda k: jnp.minimum(k, SPLIT - 1)
    kept_spec = pl.BlockSpec((ROWS, WIDE), lambda k, chunk: (part, 0))

    def grads_spec(r):
        return pl.BlockSpec((TOK, DEEP), lambda k, chunk: (chunk[4 * part + r], deep(k)))

    args = tuple(rows) + (grads,) * 4 + (weights,)
    specs = [pl.BlockSpec((TOK, DEEP), lambda k, chunk: (0, deep(k)))] * 4
    specs += [grads_spec(r) for r in range(4)]
    specs += [pl.BlockSpec((3, DEEP, WIDE), lambda k, chunk: (0, deep(k), 0))]
    aliases = {}
    if kept is not None:
        args = args + tuple(kept)
        specs = specs + [pl.BlockSpec(memory_space=pl.ANY)] * 3
        aliases = {10: 0, 11: 1, 12: 2}
    wide = pltpu.VMEM((ROWS, WIDE), F32)
    out = call(
        mlp_kernel, (chunk,), (2 * SPLIT,), specs,
        [kept_spec] * 3 + [pl.BlockSpec((TOK, DEEP), lambda k, chunk: (0, jnp.maximum(k - SPLIT, 0)))] * 4,
        [sds((8 * TOK, WIDE))] * 3 + [sds((TOK, D))] * 4,
        [pltpu.VMEM((SPLIT, 2, DEEP, WIDE), BF), wide, wide, wide],
        16, args, aliases,
    )
    return out[:3], out[3:]


def grads_specs(tail):
    zeros = (0,) * (1 + len(tail))
    x_first = pl.BlockSpec((2, 1, 2) + tail, lambda h, p, *_: (h, jnp.minimum(p, 1)) + zeros)
    y_own = pl.BlockSpec((4, 1, 2) + tail, lambda h, p, *_: (0, jnp.where(h == 0, jnp.maximum(p - 2, 0), 1)) + zeros)
    y_other = pl.BlockSpec((4, 1, 2) + tail, lambda h, p, *_: (0, jnp.where(h == 1, jnp.maximum(p - 2, 0), 0)) + zeros)
    return [x_first] * 4 + [y_own] * 2 + [y_other] * 2, [sds((4, 2, 2) + tail)] * 8


def write_grads(outs, xs, yhs, core, write):
    half, p = pl.program_id(0), pl.program_id(1)

    def go(pos, r, ref):
        inside = yhs[2 * half + pos] * 64 + xs[r] * 16
        for rc in range(2):
            write(ref.at[rc], inside, jnp.abs(core[0] - rc), rc)

    @pl.when(p < 2)
    def _():
        for r in range(4):
            for pos in range(2):
                go(pos, r, outs[r].at[pos, 0])

    for each in range(2):

        @pl.when((p >= 2) & (half == each))
        def _():
            for r in range(4):
                for pos in range(2):
                    go(pos, r, outs[4 + 2 * each + pos].at[r, 0])


def mlp_grads_kernel(column, halves, core, nat, *refs):
    tokens, (g_ref, da_ref, dc_ref, z_ref), out_ref, (turned, grads) = refs[:8], refs[8:12], refs[12], refs[13:]
    rows = jnp.concatenate([ref[...] for ref in tokens], axis=0).T
    grads[0] = dot(rows, da_ref[...])
    grads[1] = dot(rows, dc_ref[...])
    for r in range(8):
        turned[:, TOK * r : TOK * (r + 1)] = g_ref[pl.ds(pl.multiple_of(nat[r] * TOK, TOK), TOK), :].T
    grads[2] = dot(turned[...], z_ref[...])

    for rc in range(2):
        start = jnp.abs(core[0] - rc) * 128
        for yh in range(2):
            for r in range(4):
                for m in range(3):
                    out_ref[r, yh, 0, 0, rc, m] = grads[m, at_rows(start + 64 * yh + 16 * r, 16), :].astype(BF)


def mlp_grads(column, halves, core, nat, tokens, g, da, dc, z):
    col = lambda h, p, column, *_: (0, column[4 * h + p])
    hidden = pl.BlockSpec((8 * TOK, WIDE), lambda h, p, *_: (0, 0))
    return call(
        mlp_grads_kernel, (column, halves, core, nat), (2, 4),
        [pl.BlockSpec((TOK, 256), col)] * 8 + [pl.BlockSpec((8 * TOK, 256), col), hidden, hidden, hidden],
        pl.BlockSpec((4, 2, 1, 1, 2, 3, 16, WIDE), lambda h, p, column, halves, *_: (0, 0, halves[h], p, 0, 0, 0, 0)),
        sds((4, 2, 2, 4, 2, 3, 16, WIDE)), [pltpu.VMEM((256, 8 * TOK), BF), pltpu.VMEM((3, 256, WIDE), F32)],
        17, tuple(tokens) + (g, da, dc, z),
    )


def attn_grads_kernel(column, xs, yhs, core, halves, chunk, *refs):
    h_refs, g_refs, o_refs, (dq_ref, dkv_ref, w_ref) = refs[:8], refs[8:16], refs[16:20], refs[20:23]
    outs, gain_ref, (first, second) = refs[23:31], refs[31], refs[32:]
    rows = jnp.concatenate([ref[...] for ref in h_refs], axis=0).T
    first[...] = dot(rows, jnp.concatenate([dq_ref[...], dkv_ref[...]], axis=1))
    grads = jnp.concatenate([ref[...] for ref in g_refs], axis=0)
    second[...] = dot(jnp.concatenate([ref[...] for ref in o_refs], axis=0).T, grads)
    gain = jnp.sum(first[...] * w_ref[...].astype(F32), axis=1, keepdims=True)
    gain_ref[0] = jnp.broadcast_to(gain, (256, 128)).T[:8]

    def write(ref, inside, which, rc):
        ref[:, :QUERY] = second[at_rows(inside, 16), QUERY * rc : QUERY * (rc + 1)].astype(BF)
        ref[:, QUERY:] = first[at_rows(which * 128 + inside, 16), :].astype(BF)

    write_grads(outs, xs, yhs, core, write)


def attn_grads(column, xs, yhs, core, halves, chunk, h, g, o, dq, dkv, w):
    def rows_spec(r):
        return pl.BlockSpec((TOK, 256), lambda i, p, column, xs, yhs, core, halves, chunk: (chunk[r], column[4 * i + p]))

    whole = lambda i, p, *_: (0, 0)
    specs, shapes = grads_specs((16, PACK))
    *outs, gain = call(
        attn_grads_kernel, (column, xs, yhs, core, halves, chunk), (2, 4),
        [rows_spec(r) for r in range(8)]
        + [pl.BlockSpec((TOK, 2 * QUERY), lambda i, p, *_: (0, p))] * 8
        + [pl.BlockSpec((2 * TOK, 128), lambda i, p, column, xs, yhs, core, halves, chunk: (0, halves[i]))] * 4
        + [
            pl.BlockSpec((8 * TOK, QUERY), whole),
            pl.BlockSpec((8 * TOK, HEAD), whole),
            pl.BlockSpec((256, QKV), lambda i, p, column, *_: (column[4 * i + p], 0)),
        ],
        specs + [pl.BlockSpec((1, 8, 256), lambda i, p, column, *_: (column[4 * i + p], 0, 0))],
        shapes + [sds((8, 8, 256), F32)],
        [pltpu.VMEM((256, QKV), F32), pltpu.VMEM((128, 2 * QUERY), F32)],
        10, (h,) * 8 + tuple(g) + tuple(o) + (dq, dkv, w),
    )
    return outs, gain[:, 0, :].reshape(D)


def finish_mlp_kernel(spots, core, part_ref, gate_ref, up_ref, down_ref, rows):
    first = core[0] == 0
    for m, out_ref in enumerate((gate_ref, up_ref, rows)):
        for b in range(8):
            own = part_ref[b, 0, 0, m].astype(F32)
            other = part_ref[b, 1, 0, m].astype(F32)
            low, high = jnp.where(first, own, other), jnp.where(first, other, own)
            out_ref[16 * b : 16 * (b + 1), :] = jnp.concatenate([low, high], axis=1)
    down_ref[...] = rows[...].T


def finish_mlp(spots, core, parts):
    side = pl.BlockSpec((128, 2 * WIDE), lambda p, spots, *_: (0, spots[1 + p]))
    return call(
        finish_mlp_kernel, (spots, core), (4,),
        [pl.BlockSpec((8, 2, 1, 3, 16, WIDE), lambda p, *_: (0, 0, p, 0, 0, 0))],
        [side, side, pl.BlockSpec((2 * WIDE, 128), lambda p, spots, *_: (spots[1 + p], 0))],
        [sds((128, FF), F32), sds((128, FF), F32), sds((FF, 128), F32)], [pltpu.VMEM((128, 2 * WIDE), F32)],
        5, (parts,),
    )


def finish_attn_kernel(spots, xs, yhs, core, *refs):
    parts, (q_ref, k_ref, v_ref, o_ref) = refs[:4], refs[4:]
    first = core[0] == 0
    for r in range(4):
        for h in range(2):
            at = at_rows(yhs[h] * 64 + xs[r] * 16, 16)
            keys, vals = [None] * KV_HEADS, [None] * KV_HEADS
            for p in range(4):
                chip = spots[1 + p]
                own = parts[r][h, 0, p].astype(F32)
                other = parts[r][h, 1, p].astype(F32)
                o_ref[at, QUERY * p : QUERY * (p + 1)] = own[:, :QUERY]
                o_ref[at, QUERY * (p + 4) : QUERY * (p + 5)] = other[:, :QUERY]
                low = jnp.where(first, own[:, QUERY:], other[:, QUERY:])
                high = jnp.where(first, other[:, QUERY:], own[:, QUERY:])
                q_ref[at, pl.ds(pl.multiple_of(chip * 2 * QUERY, 128), QUERY)] = low[:, :QUERY]
                q_ref[at, pl.ds(pl.multiple_of(chip * 2 * QUERY + QUERY, 128), QUERY)] = high[:, :QUERY]
                for j in range(KV_HEADS):
                    key, val = low[:, QUERY:], high[:, QUERY:]
                    keys[j] = key if p == 0 else jnp.where(chip == j, key, keys[j])
                    vals[j] = val if p == 0 else jnp.where(chip == j, val, vals[j])
            k_ref[at, :] = jnp.concatenate(keys, axis=1)
            v_ref[at, :] = jnp.concatenate(vals, axis=1)


def finish_attn(spots, xs, yhs, core, parts):
    whole = lambda i, *_: (0, 0)
    shapes = [(128, D), (128, KV_HEADS * HEAD), (128, KV_HEADS * HEAD), (128, D)]
    return call(
        finish_attn_kernel, (spots, xs, yhs, core), (1,),
        [pl.BlockSpec((2, 2, 4, 16, PACK), lambda i, *_: (0, 0, 0, 0, 0))] * 4,
        [pl.BlockSpec(shape, whole) for shape in shapes], [sds(shape, F32) for shape in shapes], [],
        2, tuple(parts),
    )


def on_device(
    tokens,
    cotangent,
    block_places,
    valid_counts,
    attn_gain,
    mlp_gain,
    query_weight,
    key_weight,
    value_weight,
    output_weight,
    gate_weight,
    up_weight,
    down_weight,
):
    replica = lax.axis_index("batch")
    member = lax.axis_index("blk")
    yh, x = replica // 4, replica % 4
    yl, z, c = member // 8, (member // 2) % 4, member % 2
    y = 2 * yh + yl
    s = 1 - 2 * c
    first_core = c == 0

    def table(*entries):
        return jnp.stack([jnp.asarray(entry, jnp.int32) for entry in entries])

    def around(coordinate):
        return [coordinate, (coordinate - s) % 4, (coordinate + s) % 4, (coordinate + 2) % 4]

    chips = around(z)
    core = table(c)
    xs = table(*around(x))
    spots = table(x, *chips)
    halves = table(yl, 1 - yl)
    slot = table(*[2 * chip + each for chip in chips for each in (c, 1 - c)])
    column = table(*[4 * half + chip for half in (yl, 1 - yl) for chip in chips])
    y_around = around(y)
    yhs = table(yh, 1 - yh, y_around[1] // 2, y_around[2] // 2)
    chunk = table(*[
        2 * chip + each
        for pair in ((0, 0), (1, 2), (2, 1), (3, 3))
        for chip, each in zip((chips[pair[0]], chips[pair[1]]), (c, 1 - c))
    ])


    def gather_tokens(rows):
        parts = []
        for part in ring_gather(rows, "z"):
            parts += [part, swap(part)]
        return parts

    def scatter_tokens(mine, peer):
        own, before, forward, far = [add(a, swap(b)) for a, b in zip(mine, peer)]
        got = [
            across(far.astype(BF), "z"),
            step(before.astype(BF), "z", -1),
            step(forward.astype(BF), "z", 1),
        ]
        return add(own, *got)

    def flip(rows):
        return jnp.flip(rows.reshape(-1, 2, TOK, rows.shape[-1]), axis=1).reshape(rows.shape)

    gain_one = attn_gain.astype(F32)
    gain_two = mlp_gain.astype(F32)
    rows_in = tokens[0].astype(F32)
    scale_attn = rms_scale(rows_in)


    def exchange(mine, other):
        got = swap(other)
        own = jnp.stack([mine[0], got[0]])
        before = jnp.stack([mine[1], got[2]])
        forward = jnp.stack([mine[2], got[1]])
        far = jnp.stack([mine[3], got[3]])
        parts = jnp.concatenate(exchange_z(own, before, forward, far))
        return parts

    def spread(part, forward):
        pieces = ring_gather(part, "x", forward)
        return list(pieces) + [step(piece, "y", 1) for piece in pieces]

    normed_attn = lax.all_gather(
        (rows_in * scale_attn * gain_one).astype(BF), "blk", axis=0, tiled=True, axis_index_groups=ZC_GROUPS
    )
    out_rows = lax.dynamic_slice_in_dim(output_weight, x * 32, 32, axis=0)
    out_part = send(
        out_rows.reshape(32, 8, QUERY).transpose(1, 0, 2),
        lambda yh, x, yl, z, c: (yh, x, c, 2 * yl + z // 2, z % 2),
    )
    packs = exchange(
        *pack(spots, core, gate_weight, up_weight, down_weight, query_weight, key_weight, value_weight)
    )
    attn_part = jnp.concatenate([out_part, packs[:, 3, :, :QKV]], axis=-1)
    attn_pieces = spread(attn_part, False)
    w_qkv, w_out = place_attn(slot, xs, halves, attn_pieces)
    mlp_half_rows = lax.all_gather(packs[:, :3], "batch", axis=0, axis_index_groups=X_GROUPS)
    w_mlp = place_mlp(slot, halves, mlp_half_rows, step(mlp_half_rows, "y", 1))

    grad_rows = lax.all_gather(
        after(cotangent[0], mlp_half_rows), "blk", axis=0, tiled=True, axis_index_groups=ZC_GROUPS
    )


    places = block_places[0]
    counts = valid_counts[0]
    key_block = jnp.concatenate([yl * 8 + chunk, (1 - yl) * 8 + chunk])
    key_place = lookup(places, key_block)
    query_place = key_place[:8]
    key_count = lookup(counts, key_block)
    slots = jnp.arange(16, dtype=jnp.int32)
    key_slot = jnp.sum(jnp.where(key_place[None, :] == slots[:, None], slots[None, :], 0), axis=1)
    usable = (jnp.arange(TOK, dtype=jnp.int32)[None, :] < key_count[:, None]).reshape(16 * TOK, 1)

    queries, kv_own = project(chunk, normed_attn, w_qkv)
    kv_half = to_half(kv_own)
    kv_mine = jnp.concatenate([kv_own[0], kv_half[0]], axis=0)
    kv_other = swap(jnp.concatenate([kv_own[1], kv_half[1]], axis=0))
    keys = jnp.where(first_core, kv_mine, kv_other)
    values = jnp.where(usable, jnp.where(first_core, kv_other, kv_mine), 0)
    attended, mine, peer = [None] * 4, [None] * 4, [None] * 4
    for g in (3, 1, 2, 0):
        at = after(query_place, mlp_half_rows) if g == 0 else query_place
        attended[g], mine[g], peer[g] = attend(g, at, key_slot, queries, keys, values, w_out)
    residual = rows_in + scatter_tokens(mine, peer)
    scale_mlp = rms_scale(residual)
    mlp_parts = gather_tokens((residual * scale_mlp * gain_two).astype(BF))


    kept, results = None, []
    for part in range(2):
        kept, result = mlp_half(part, chunk, mlp_parts[4 * part : 4 * part + 4], grad_rows, w_mlp, kept)
        results += result
    hidden, gate_grad_rows, up_grad_rows = kept
    mlp_sums = mlp_grads(
        column, halves, core, chunk, mlp_parts, grad_rows, gate_grad_rows, up_grad_rows, hidden
    )
    normed_grad = after(scatter_tokens(results[::2], results[1::2]), mlp_sums)
    mlp_sums = lax.psum_scatter(mlp_sums, "batch", scatter_dimension=0, axis_index_groups=X_GROUPS)
    mlp_sums = lax.psum_scatter(
        mlp_sums.reshape((4,) + mlp_sums.shape[2:]), BOTH, scatter_dimension=0, axis_index_groups=Y_GROUPS
    )
    residual_grad = cotangent[0].astype(F32) + norm_back(residual, scale_mlp, gain_two, normed_grad)
    mlp_gain_part = jnp.sum(normed_grad * residual * scale_mlp, axis=0)
    branch_parts = gather_tokens(residual_grad.astype(BF))
    branch = dot_last(after(hidden, branch_parts[7]), w_mlp[2]).astype(BF).reshape(4, 2, TOK, D)
    layer_out = (residual + scatter_tokens(branch[:, 0], branch[:, 1])).astype(BF)[None]


    def reduce_planes(outs):
        low = ring_scatter(*outs[:4], "x").astype(BF)
        low = ring_scatter(low[0], low[2], low[3], low[1], "y").astype(BF)
        high = ring_scatter(outs[4], outs[6], outs[7], outs[5], "y").astype(BF)
        high = ring_scatter(high[0], high[1], high[2], high[3], "x").astype(BF)
        return jnp.concatenate([low, high])

    def resplit_back(part):
        got = exchange_z(part[0], part[1], part[2], part[3])
        mine = jnp.stack([each[0] for each in got])
        other = swap(jnp.stack([got[p][1] for p in (0, 2, 1, 3)]))
        return jnp.stack([mine, other])

    def gather_batch(part):
        return ring_gather(jnp.stack([part, across(part, "y")]), "x")


    attn_grad = dot_last(jnp.concatenate(branch_parts), w_out).astype(BF)
    query_grad_rows, kv_keep, kv_give = attend_back(
        query_place, key_slot, core, key_count, queries, attn_grad, keys, values
    )
    kv_terms = add(kv_keep, swap(after(kv_give, layer_out)))
    half_rows = 8 * TOK
    kv_grad_rows = add(kv_terms[:half_rows], to_half(kv_terms[half_rows:].astype(BF))).astype(BF)

    mlp_sums = resplit_back(after(mlp_sums, kv_keep))
    gate_grad, up_grad, down_grad = finish_mlp(spots, core, lax.all_gather(mlp_sums, "batch"))

    attn_partial = project_back(query_grad_rows, kv_grad_rows, w_qkv)
    attn_sums, attn_gain_part = attn_grads(
        column, xs, yhs, core, halves, chunk, normed_attn, branch_parts, attended, query_grad_rows, kv_grad_rows, w_qkv
    )
    gain_grads = sum_all(jnp.stack([attn_gain_part / gain_one, mlp_gain_part]))
    normed_attn_grad = scatter_tokens(attn_partial[::2], attn_partial[1::2])
    attn_sums = after(reduce_planes(attn_sums), normed_attn_grad)
    out_sums = send(
        attn_sums[..., :QUERY], lambda yh, x, yl, z, c: (yh, x, z // 2, 2 * (z % 2) + c, yl)
    )
    qkv_sums = resplit_back(attn_sums[..., QUERY:])
    attn_sums = jnp.concatenate([out_sums.reshape(2, 4, 16, QUERY), qkv_sums], axis=-1)
    query_grad, key_grad, value_grad, output_grad = finish_attn(spots, xs, yhs, core, gather_batch(attn_sums))

    tokens_grad = (
        residual_grad + norm_back(rows_in, scale_attn, gain_one, normed_attn_grad)
    ).astype(BF)[None]
    return (
        layer_out,
        tokens_grad,
        gain_grads[0],
        gain_grads[1],
        query_grad,
        key_grad,
        value_grad,
        output_grad,
        gate_grad,
        up_grad,
        down_grad,
    )


def solution(mesh):
    in_specs = (
        P("batch", "blk", None),
        P("batch", "blk", None),
        P("batch", None),
        P("batch", None),
        P(),
        P(),
        P("blk", None),
        P("blk", None),
        P("blk", None),
        P("blk", None),
        P("blk", None),
        P("blk", None),
        P(None, "blk"),
    )
    out_specs = (
        P("batch", "blk", None),
        P("batch", "blk", None),
        P(),
        P(),
        P("blk", None),
        P("blk", None),
        P("blk", None),
        P("blk", None),
        P("blk", None),
        P("blk", None),
        P(None, "blk"),
    )
    return jax.shard_map(
        on_device, mesh=mesh, in_specs=in_specs, out_specs=out_specs, check_vma=False
    )
```

profile of v0, /device:TPU:24, one launch (start us, length us, event | category | flops | bytes accessed | tf_op | source)
XLA Modules:
  0.0 682.3 jit_solution(5566496171575531594)
XLA Ops:
  12.9 4.0 shard_map.212
  25.7 5.6 collective-permute-done.1
  31.3 9.4 %collective-permute-done.2 = bf16[2,4,32,704]{3,2,0,1:T(8,128)(2,1)S(1)} collective-permute-done((bf16[2,4,32,704]{3,2,0,1:T(8,128)(2,1)S(1)}, bf16[2,4,32,704]{3,2,0,1:T(8,128)(2,1)S(1)}, u32[]{:S(2)}, u32[]{:S(2)}) %collective-permute-start.2) | collective-permute-done | bytes 360480 | tf_op jit(solution)/shard_map/ppermute | solution.py:45
  46.5 49.9 %all-gather.11.cloned.1.call-done = bf16[32,3,32,704]{3,2,0,1:T(8,128)(2,1)} async-done(((bf16[8,3,32,704]{3,2,0,1:T(8,128)(2,1)}), bf16[32,3,32,704]{3,2,0,1:T(8,128)(2,1)}) %all-gather.11.cloned.1.call-update) | async-done | bytes 4325392 | tf_op jit(solution)/shard_map/all_gather | solution.py:757
  96.4 4.8 copy.91
  101.3 5.3 collective-permute-start.4
  113.7 13.6 %collective-permute-done.5.refs_1_ = bf16[8,32,576]{2,1,0:T(8,128)(2,1)S(1)} collective-permute-done((bf16[8,32,576]{2,1,0:T(8,128)(2,1)S(1)}, bf16[8,32,576]{2,1,0:T(8,128)(2,1)S(1)}, u32[]{:S(2)}, u32[]{:S(2)}) %collective-permute-start.5) | collective-permute-done | bytes 294944 | tf_op jit(solution)/shard_map/ppermute | solution.py:45
  129.6 4.8 collective-permute-done.9.refs_5_
  134.4 3.5 collective-permute-done.10.refs_6_
  137.9 3.5 collective-permute-done.11.refs_7_
  145.4 6.0 shard_map.214
  152.0 6.1 collective-permute-done.12
  160.4 9.3 %shard_map.218 = (bf16[256,256]{1,0:T(8,128)(2,1)S(1)}, bf16[128,2048]{1,0:T(8,128)(2,1)S(1)}, bf16[128,2048]{1,0:T(8,128)(2,1)S(1)}) custom-call(s32[8]{0:T(128)S(1)} %bitcast.179, s32[16]{0:T(128)S(1)} %select_reduce_fusion.1.key_slot, bf16[1024,256]{1,0:T(8,128)(2,1)S(1)} %get-tuple-element.81.q_ref, bf16[2048,64]{1,0:T(8,128)(2,1)S(1)} %copy.96.k_ref, ...), custom_call_target="tpu_custom_call" | custom-call | flops 1000 | bytes 18000000 | tf_op jit(solution)/shard_map/pallas_call | solution.py:141
  174.2 5.0 shard_map.216
  179.9 4.6 shard_map.215
  185.1 4.0 collective-permute-start.20
  189.3 4.1 collective-permute-start.18
  195.2 8.0 %collective-permute-done.20 = bf16[128,2048]{1,0:T(8,128)(2,1)S(1)} collective-permute-done((bf16[128,2048]{1,0:T(8,128)(2,1)S(1)}, bf16[128,2048]{1,0:T(8,128)(2,1)S(1)}, u32[]{:S(2)}, u32[]{:S(2)}) %collective-permute-start.20) | collective-permute-done | bytes 524320 | tf_op jit(solution)/shard_map/ppermute | solution.py:45
  203.2 13.0 %collective-permute-done.18 = bf16[128,2048]{1,0:T(8,128)(2,1)S(1)} collective-permute-done((bf16[128,2048]{1,0:T(8,128)(2,1)S(1)}, bf16[128,2048]{1,0:T(8,128)(2,1)S(1)}, u32[]{:S(2)}, u32[]{:S(2)}) %collective-permute-start.18) | collective-permute-done | bytes 524320 | tf_op jit(solution)/shard_map/ppermute | solution.py:45
  223.1 23.9 %collective-permute-done.27.refs_2_ = bf16[128,2048]{1,0:T(8,128)(2,1)} collective-permute-done((bf16[128,2048]{1,0:T(8,128)(2,1)S(1)}, bf16[128,2048]{1,0:T(8,128)(2,1)}, u32[]{:S(2)}, u32[]{:S(2)}) %collective-permute-start.27) | collective-permute-done | bytes 524320 | tf_op jit(solution)/shard_map/ppermute | solution.py:45
  251.3 8.7 %shard_map.219 = bf16[3,2,8,128,704]{4,3,2,1,0:T(8,128)(2,1)} custom-call(s32[8]{0:T(128)S(1)} %copy-done.38, s32[2]{0:T(128)S(1)} %pad_add_fusion.2.halves, bf16[4,8,3,32,704]{4,3,2,1,0:T(8,128)(2,1)S(1)} %bitcast.168, bf16[4,8,3,32,704]{4,3,2,1,0:T(8,128)(2,1)} %collective-permute-done.25.other_ref), custom_call_target="tpu_custom_call" | custom-call | flops 1000 | bytes 18000000 | tf_op jit(solution)/shard_map/pallas_call | solution.py:141
  260.1 15.9 %shard_map.220 = (bf16[1024,704]{1,0:T(8,128)(2,1)S(1)}, bf16[1024,704]{1,0:T(8,128)(2,1)}, bf16[1024,704]{1,0:T(8,128)(2,1)}, bf16[128,2048]{1,0:T(8,128)(2,1)S...) custom-call(s32[8]{0:T(128)S(1)} %stack.188.chunk.nat, ...), custom_call_target="tpu_custom_call" | custom-call | flops 1000 | bytes 48000000 | tf_op jit(solution)/shard_map/pallas_call | solution.py:141
  279.2 16.0 %shard_map.221 = (bf16[1024,704]{1,0:T(8,128)(2,1)S(1)}, bf16[1024,704]{1,0:T(8,128)(2,1)}, bf16[1024,704]{1,0:T(8,128)(2,1)}, bf16[128,2048]{1,0:T(8,128)(2,1)S...) custom-call(s32[8]{0:T(128)S(1)} %stack.188.chunk.nat, ...), custom_call_target="tpu_custom_call", output_to_operand_aliasing={{0}: (10, {}), {1}: (11, {}), {2}: (12, {})} | custom-call | flops 1000 | bytes 48000000 | tf_op jit(solution)/shard_map/pallas_call | solution.py:141
  300.9 18.0 %shard_map.222 = bf16[4,2,2,4,2,3,16,704]{7,6,5,4,3,2,1,0:T(8,128)(2,1)} custom-call(s32[8]{0:T(128)S(1)} %copy-done.39, s32[2]{0:T(128)S(1)} %pad_add_fusion.2.halves, s32[1]{0:T(128)} %bitcast.15.core, s32[8]{0:T(128)S(1)} %stack.188.chunk.nat, bf16[128,2048]{1,0:T(8,128)(2,1)S(1)} %multiply_convert_fusion.refs_0_, ...), custom_call_target="tpu_custom_call" | custom-call | flops 1000 | bytes 51000000 | tf_op jit(solution)/shard_map/pallas_call | solution.py:141
  328.5 20.7 %collective-permute-done.35 = bf16[128,2048]{1,0:T(8,128)(2,1)S(1)} collective-permute-done((bf16[128,2048]{1,0:T(8,128)(2,1)S(1)}, bf16[128,2048]{1,0:T(8,128)(2,1)S(1)}, u32[]{:S(2)}, u32[]{:S(2)}) %collective-permute-start.35) | collective-permute-done | bytes 524320 | tf_op jit(solution)/shard_map/ppermute | solution.py:45
  355.2 13.1 %collective-permute-done.36.refs_14_ = bf16[128,2048]{1,0:T(8,128)(2,1)S(1)} collective-permute-done((bf16[128,2048]{1,0:T(8,128)(2,1)S(1)}, bf16[128,2048]{1,0:T(8,128)(2,1)S(1)}, u32[]{:S(2)}, u32[]{:S(2)}) %collective-permute-start.36) | collective-permute-done | bytes 524320 | tf_op jit(solution)/shard_map/ppermute | solution.py:45
  370.7 8.2 %collective-permute-done.46.refs_10_ = bf16[128,2048]{1,0:T(8,128)(2,1)S(1)} collective-permute-done((bf16[128,2048]{1,0:T(8,128)(2,1)S(1)}, bf16[128,2048]{1,0:T(8,128)(2,1)S(1)}, u32[]{:S(2)}, u32[]{:S(2)}) %collective-permute-start.46) | collective-permute-done | bytes 524320 | tf_op jit(solution)/shard_map/ppermute | solution.py:45
  383.2 5.1 convolution_convert_fusion
  388.3 17.8 %reduce-scatter.3.cloned.1.call-done = bf16[1,2,2,4,2,3,16,704]{7,6,5,4,3,2,1,0:T(8,128)(2,1)} async-done(((bf16[4,2,2,4,2,3,16,704]{7,6,5,4,3,2,1,0:T(8,128)(2,1)}), bf16[1,2,2,4,2,3,16,704]{7,6,5,4,3,2,1,0:T(8,128)(2,1)}) %reduce-scatter.3.cloned.1.call-update) | async-done | bytes 2162704 | tf_op jit(solution)/shard_map/reduce_scatter | solution.py:799
  423.1 26.1 %shard_map.223 = (bf16[1024,256]{1,0:T(8,128)(2,1)S(1)}, bf16[2048,64]{1,0:T(8,128)(2,1)S(1)}, bf16[2048,64]{1,0:T(8,128)(2,1)S(1)}) custom-call(s32[8]{0:T(128)S(1)} %bitcast.183, s32[16]{0:T(128)S(1)} %select_reduce_fusion.1.key_slot, s32[1]{0:T(128)} %bitcast.15.core, s32[16]{0:T(128)S(1)} %copy-done.42, bf16[1024,256]{1,0:T(8,128)(2,1)S(1)} %get-tuple-element.81.q_ref, ...), custom_call_target="tpu_custom_call" | custom-call | flops 1000 | bytes 84000000 | tf_op jit(solution)/shard_map/pallas_call | solution.py:141
  453.5 6.8 collective-permute-start.51
  460.3 6.5 collective-permute-done.51
  469.4 11.4 %shard_map.225 = (bf16[4,2,2,16,576]{4,3,2,1,0:T(8,128)(2,1)S(1)}, bf16[4,2,2,16,576]{4,3,2,1,0:T(8,128)(2,1)S(1)}, bf16[4,2,2,16,576]{4,3,2,1,0:T(8,128)(2,1)S(...) custom-call(s32[8]{0:T(128)S(1)} %copy-done.40, ...), custom_call_target="tpu_custom_call" | custom-call | flops 1000 | bytes 30000000 | tf_op jit(solution)/shard_map/pallas_call | solution.py:141
  504.2 3.5 collective-permute-done.60
  507.8 3.4 collective-permute-start.64
  522.2 4.5 shard_map.224
  532.1 5.7 collective-permute-done.77
  539.4 31.5 %collective-permute-done.76 = bf16[4,2,2,16,576]{4,3,2,1,0:T(8,128)(2,1)S(1)} collective-permute-done((bf16[4,2,2,16,576]{4,3,2,1,0:T(8,128)(2,1)}, bf16[4,2,2,16,576]{4,3,2,1,0:T(8,128)(2,1)S(1)}, u32[]{:S(2)}, u32[]{:S(2)}) %collective-permute-start.76) | collective-permute-done | bytes 294944 | tf_op jit(solution)/shard_map/ppermute | solution.py:45
  571.0 3.3 collective-permute-start.69
  574.6 12.0 %collective-permute-done.70 = bf16[4,2,2,16,576]{4,3,2,1,0:T(8,128)(2,1)S(1)} collective-permute-done((bf16[4,2,2,16,576]{4,3,2,1,0:T(8,128)(2,1)}, bf16[4,2,2,16,576]{4,3,2,1,0:T(8,128)(2,1)S(1)}, u32[]{:S(2)}, u32[]{:S(2)}) %collective-permute-start.70) | collective-permute-done | bytes 294944 | tf_op jit(solution)/shard_map/ppermute | solution.py:45
  586.6 6.3 collective-permute-start.80
  593.2 4.4 collective-permute-start.78
  597.8 3.7 collective-permute-start.74
  609.2 20.7 %collective-permute-done.58 = bf16[128,2048]{1,0:T(8,128)(2,1)S(1)} collective-permute-done((bf16[128,2048]{1,0:T(8,128)(2,1)S(1)}, bf16[128,2048]{1,0:T(8,128)(2,1)S(1)}, u32[]{:S(2)}, u32[]{:S(2)}) %collective-permute-start.58) | collective-permute-done | bytes 524320 | tf_op jit(solution)/shard_map/ppermute | solution.py:45
  638.3 4.3 collective-permute-done.81
  644.9 4.7 collective-permute-done.86
  654.7 11.3 %collective-permute-done.87.refs_1_ = bf16[2,2,4,16,576]{4,3,2,1,0:T(8,128)(2,1)S(1)} collective-permute-done((bf16[2,2,4,16,576]{4,3,2,1,0:T(8,128)(2,1)S(1)}, bf16[2,2,4,16,576]{4,3,2,1,0:T(8,128)(2,1)S(1)}, u32[]{:S(2)}, u32[]{:S(2)}) %collective-permute-start.87) | collective-permute-done | bytes 294944 | tf_op jit(solution)/shard_map/ppermute | solution.py:45
  670.5 4.5 shard_map.227
  (453 shorter events, 179.7 us)
Async XLA Ops:
  7.2 89.2 %all-gather.11.cloned.1.call-start = ((), (), s32[]{:S(2)}) async-start(), calls=%async_computation.6 | async-start | bytes 5898240 | tf_op jit(solution)/shard_map/all_gather | solution.py:757
  21.5 19.2 %collective-permute-start.2 = (bf16[2,4,32,704]{3,2,0,1:T(8,128)(2,1)S(1)}, bf16[2,4,32,704]{3,2,0,1:T(8,128)(2,1)S(1)}, u32[]{:S(2)}, u32[]{:S(2)}) collective-permute-start(bf16[2,4,32,704]{3,2,0,1:T(8,128)(2,1)S(1)} %pad_maximum_fusion.2), channel_id=1, source_target_pairs={{0,6},{1,3},{2,0},{3,5},{4,2},{5,7},{6,4},{7,1},{8,14},{9,11},{10,... | collective-permute-start | bytes 1081352 | tf_op jit(solution)/shard_map/ppermute | solution.py:45
  23.8 19.1 %collective-permute-start.3 = (bf16[2,4,32,704]{3,2,0,1:T(8,128)(2,1)S(1)}, bf16[2,4,32,704]{3,2,0,1:T(8,128)(2,1)S(1)}, u32[]{:S(2)}, u32[]{:S(2)}) collective-permute-start(bf16[2,4,32,704]{3,2,0,1:T(8,128)(2,1)S(1)} %pad_maximum_fusion.3), channel_id=1, source_target_pairs={{0,4},{1,5},{2,6},{3,7},{4,0},{5,1},{6,2},{7,3},{8,12},{9,13},{10,... | collective-permute-start | bytes 1081352 | tf_op jit(solution)/shard_map/ppermute | solution.py:45
  44.0 99.9 %all-gather.7.cloned.1.call-start = ((), (), s32[]{:S(2)}) async-start(), calls=%async_computation.2 | async-start | bytes 4718592 | tf_op jit(solution)/shard_map/all_gather | solution.py:743
  46.5 213.6 %all-gather.9.cloned.1.call-start = ((), (), s32[]{:S(2)}) async-start(), calls=%async_computation.3 | async-start | bytes 4718592 | tf_op jit(solution)/shard_map/all_gather | solution.py:760
  101.2 304.8 %reduce-scatter.3.cloned.1.call-start = ((), (), s32[]{:S(2)}) async-start(), calls=%async_computation.4 | async-start | bytes 11796480 | tf_op jit(solution)/shard_map/reduce_scatter | solution.py:799
  109.2 18.1 %collective-permute-start.5 = (bf16[8,32,576]{2,1,0:T(8,128)(2,1)S(1)}, bf16[8,32,576]{2,1,0:T(8,128)(2,1)S(1)}, u32[]{:S(2)}, u32[]{:S(2)}) collective-permute-start(bf16[8,32,576]{2,1,0:T(8,128)(2,1)S(1)} %pad_maximum_fusion.4.refs_0_), channel_id=1, source_target_pairs={{0,16},{1,49},{2,18},{3,51},{4,20},{5,53},{6,22},{7,55},{8,24},{9,... | collective-permute-start | bytes 884744 | tf_op jit(solution)/shard_map/ppermute | solution.py:45
  110.2 17.1 %collective-permute-start.6 = (bf16[8,32,576]{2,1,0:T(8,128)(2,1)S(1)}, bf16[8,32,576]{2,1,0:T(8,128)(2,1)S(1)}, u32[]{:S(2)}, u32[]{:S(2)}) collective-permute-start(bf16[8,32,576]{2,1,0:T(8,128)(2,1)S(1)} %pad_maximum_fusion.4.refs_0_), channel_id=1, source_target_pairs={{0,48},{1,17},{2,50},{3,19},{4,52},{5,21},{6,54},{7,23},{8,56},{9,... | collective-permute-start | bytes 884744 | tf_op jit(solution)/shard_map/ppermute | solution.py:45
  112.5 16.8 %collective-permute-start.7 = (bf16[8,32,576]{2,1,0:T(8,128)(2,1)S(1)}, bf16[8,32,576]{2,1,0:T(8,128)(2,1)S(1)}, u32[]{:S(2)}, u32[]{:S(2)}) collective-permute-start(bf16[8,32,576]{2,1,0:T(8,128)(2,1)S(1)} %pad_maximum_fusion.4.refs_0_), channel_id=1, source_target_pairs={{0,32},{1,33},{2,34},{3,35},{4,36},{5,37},{6,38},{7,39},{8,40},{9,... | collective-permute-start | bytes 884744 | tf_op jit(solution)/shard_map/ppermute | solution.py:45
  113.7 16.0 %collective-permute-start.8 = (bf16[8,32,576]{2,1,0:T(8,128)(2,1)S(1)}, bf16[8,32,576]{2,1,0:T(8,128)(2,1)S(1)}, u32[]{:S(2)}, u32[]{:S(2)}) collective-permute-start(bf16[8,32,576]{2,1,0:T(8,128)(2,1)S(1)} %pad_maximum_fusion.4.refs_0_), channel_id=1, source_target_pairs={{0,8},{1,73},{2,10},{3,75},{4,12},{5,77},{6,14},{7,79},{8,64},{9,1... | collective-permute-start | bytes 884744 | tf_op jit(solution)/shard_map/ppermute | solution.py:45
  169.9 78.4 %collective-permute-start.25 = (bf16[4,8,3,32,704]{4,3,2,1,0:T(8,128)(2,1)}, bf16[4,8,3,32,704]{4,3,2,1,0:T(8,128)(2,1)}, u32[]{:S(2)}, u32[]{:S(2)}) collective-permute-start(bf16[4,8,3,32,704]{4,3,2,1,0:T(8,128)(2,1)} %bitcast.167), channel_id=1, source_target_pairs={{0,8},{1,73},{2,10},{3,75},{4,12},{5,77},{6,14},{7,79},{8,64},{9,1... | collective-permute-start | bytes 12976136 | tf_op jit(solution)/shard_map/ppermute | solution.py:45
  185.1 18.1 %collective-permute-start.20 = (bf16[128,2048]{1,0:T(8,128)(2,1)S(1)}, bf16[128,2048]{1,0:T(8,128)(2,1)S(1)}, u32[]{:S(2)}, u32[]{:S(2)}) collective-permute-start(bf16[128,2048]{1,0:T(8,128)(2,1)S(1)} %add_convert_fusion.6), channel_id=1, source_target_pairs={{0,2},{1,7},{2,4},{3,1},{4,6},{5,3},{6,0},{7,5},{8,10},{9,15},{10,... | collective-permute-start | bytes 1572872 | tf_op jit(solution)/shard_map/ppermute | solution.py:45
  189.3 27.0 %collective-permute-start.18 = (bf16[128,2048]{1,0:T(8,128)(2,1)S(1)}, bf16[128,2048]{1,0:T(8,128)(2,1)S(1)}, u32[]{:S(2)}, u32[]{:S(2)}) collective-permute-start(bf16[128,2048]{1,0:T(8,128)(2,1)S(1)} %add_convert_fusion.7), channel_id=1, source_target_pairs={{0,6},{1,3},{2,0},{3,5},{4,2},{5,7},{6,4},{7,1},{8,14},{9,11},{10,... | collective-permute-start | bytes 1572872 | tf_op jit(solution)/shard_map/ppermute | solution.py:45
  193.5 24.9 %collective-permute-start.16 = (bf16[128,2048]{1,0:T(8,128)(2,1)S(1)}, bf16[128,2048]{1,0:T(8,128)(2,1)S(1)}, u32[]{:S(2)}, u32[]{:S(2)}) collective-permute-start(bf16[128,2048]{1,0:T(8,128)(2,1)S(1)} %add_convert_fusion.8), channel_id=1, source_target_pairs={{0,4},{1,5},{2,6},{3,7},{4,0},{5,1},{6,2},{7,3},{8,12},{9,13},{10,... | collective-permute-start | bytes 1572872 | tf_op jit(solution)/shard_map/ppermute | solution.py:45
  219.8 27.2 %collective-permute-start.27 = (bf16[128,2048]{1,0:T(8,128)(2,1)S(1)}, bf16[128,2048]{1,0:T(8,128)(2,1)}, u32[]{:S(2)}, u32[]{:S(2)}) collective-permute-start(bf16[128,2048]{1,0:T(8,128)(2,1)S(1)} %multiply_convert_fusion.refs_0_), channel_id=1, source_target_pairs={{0,2},{1,7},{2,4},{3,1},{4,6},{5,3},{6,0},{7,5},{8,10},{9,15},{10,... | collective-permute-start | bytes 1572872 | tf_op jit(solution)/shard_map/ppermute | solution.py:45
  219.9 27.1 %collective-permute-start.21 = (bf16[128,2048]{1,0:T(8,128)(2,1)S(1)}, bf16[128,2048]{1,0:T(8,128)(2,1)}, u32[]{:S(2)}, u32[]{:S(2)}) collective-permute-start(bf16[128,2048]{1,0:T(8,128)(2,1)S(1)} %multiply_convert_fusion.refs_0_), channel_id=1, source_target_pairs={{0,6},{1,3},{2,0},{3,5},{4,2},{5,7},{6,4},{7,1},{8,14},{9,11},{10,... | collective-permute-start | bytes 1572872 | tf_op jit(solution)/shard_map/ppermute | solution.py:45
  223.1 24.4 %collective-permute-start.23 = (bf16[128,2048]{1,0:T(8,128)(2,1)S(1)}, bf16[128,2048]{1,0:T(8,128)(2,1)}, u32[]{:S(2)}, u32[]{:S(2)}) collective-permute-start(bf16[128,2048]{1,0:T(8,128)(2,1)S(1)} %multiply_convert_fusion.refs_0_), channel_id=1, source_target_pairs={{0,4},{1,5},{2,6},{3,7},{4,0},{5,1},{6,2},{7,3},{8,12},{9,13},{10,... | collective-permute-start | bytes 1572872 | tf_op jit(solution)/shard_map/ppermute | solution.py:45
  223.1 36.9 %collective-permute-start.26 = (bf16[128,2048]{1,0:T(8,128)(2,1)S(1)}, bf16[128,2048]{1,0:T(8,128)(2,1)}, u32[]{:S(2)}, u32[]{:S(2)}) collective-permute-start(bf16[128,2048]{1,0:T(8,128)(2,1)S(1)} %multiply_convert_fusion.refs_0_), channel_id=1, source_target_pairs={{0,1},{1,0},{2,3},{3,2},{4,5},{5,4},{6,7},{7,6},{8,9},{9,8},{10,11... | collective-permute-start | bytes 1572872 | tf_op jit(solution)/shard_map/ppermute | solution.py:45
  247.0 32.2 %collective-permute-start.22 = (bf16[128,2048]{1,0:T(8,128)(2,1)}, bf16[128,2048]{1,0:T(8,128)(2,1)}, u32[]{:S(2)}, u32[]{:S(2)}) collective-permute-start(bf16[128,2048]{1,0:T(8,128)(2,1)} %collective-permute-done.21.refs_0_.refs_4_), channel_id=1, source_target_pairs={{0,1},{1,0},{2,3},{3,2},{4,5},{5,4},{6,7},{7,6},{8,9},{9,8},{10,11... | collective-permute-start | bytes 1572872 | tf_op jit(solution)/shard_map/ppermute | solution.py:45
  247.5 31.7 %collective-permute-start.24 = (bf16[128,2048]{1,0:T(8,128)(2,1)}, bf16[128,2048]{1,0:T(8,128)(2,1)}, u32[]{:S(2)}, u32[]{:S(2)}) collective-permute-start(bf16[128,2048]{1,0:T(8,128)(2,1)} %collective-permute-done.23.refs_2_.refs_6_), channel_id=1, source_target_pairs={{0,1},{1,0},{2,3},{3,2},{4,5},{5,4},{6,7},{7,6},{8,9},{9,8},{10,11... | collective-permute-start | bytes 1572872 | tf_op jit(solution)/shard_map/ppermute | solution.py:45
  318.9 167.3 %reduce-scatter.5.cloned.1.call-start = ((), (), s32[]{:S(2)}) async-start(), calls=%async_computation.5 | async-start | bytes 2949120 | tf_op jit(solution)/shard_map/reduce_scatter | solution.py:800
  322.6 26.6 %collective-permute-start.35 = (bf16[128,2048]{1,0:T(8,128)(2,1)S(1)}, bf16[128,2048]{1,0:T(8,128)(2,1)S(1)}, u32[]{:S(2)}, u32[]{:S(2)}) collective-permute-start(bf16[128,2048]{1,0:T(8,128)(2,1)S(1)} %add_convert_fusion.3), channel_id=1, source_target_pairs={{0,2},{1,7},{2,4},{3,1},{4,6},{5,3},{6,0},{7,5},{8,10},{9,15},{10,... | collective-permute-start | bytes 1572872 | tf_op jit(solution)/shard_map/ppermute | solution.py:45
  324.0 25.3 %collective-permute-start.33 = (bf16[128,2048]{1,0:T(8,128)(2,1)S(1)}, bf16[128,2048]{1,0:T(8,128)(2,1)S(1)}, u32[]{:S(2)}, u32[]{:S(2)}) collective-permute-start(bf16[128,2048]{1,0:T(8,128)(2,1)S(1)} %add_convert_fusion.4), channel_id=1, source_target_pairs={{0,6},{1,3},{2,0},{3,5},{4,2},{5,7},{6,4},{7,1},{8,14},{9,11},{10,... | collective-permute-start | bytes 1572872 | tf_op jit(solution)/shard_map/ppermute | solution.py:45
  328.4 20.8 %collective-permute-start.31 = (bf16[128,2048]{1,0:T(8,128)(2,1)S(1)}, bf16[128,2048]{1,0:T(8,128)(2,1)S(1)}, u32[]{:S(2)}, u32[]{:S(2)}) collective-permute-start(bf16[128,2048]{1,0:T(8,128)(2,1)S(1)} %add_convert_fusion.5), channel_id=1, source_target_pairs={{0,4},{1,5},{2,6},{3,7},{4,0},{5,1},{6,2},{7,3},{8,12},{9,13},{10,... | collective-permute-start | bytes 1572872 | tf_op jit(solution)/shard_map/ppermute | solution.py:45
  351.9 16.4 %collective-permute-start.36 = (bf16[128,2048]{1,0:T(8,128)(2,1)S(1)}, bf16[128,2048]{1,0:T(8,128)(2,1)S(1)}, u32[]{:S(2)}, u32[]{:S(2)}) collective-permute-start(bf16[128,2048]{1,0:T(8,128)(2,1)S(1)} %get-tuple-element.150.refs_8_), channel_id=1, source_target_pairs={{0,4},{1,5},{2,6},{3,7},{4,0},{5,1},{6,2},{7,3},{8,12},{9,13},{10,... | collective-permute-start | bytes 1572872 | tf_op jit(solution)/shard_map/ppermute | solution.py:45
  351.9 26.9 %collective-permute-start.46 = (bf16[128,2048]{1,0:T(8,128)(2,1)S(1)}, bf16[128,2048]{1,0:T(8,128)(2,1)S(1)}, u32[]{:S(2)}, u32[]{:S(2)}) collective-permute-start(bf16[128,2048]{1,0:T(8,128)(2,1)S(1)} %get-tuple-element.150.refs_8_), channel_id=1, source_target_pairs={{0,2},{1,7},{2,4},{3,1},{4,6},{5,3},{6,0},{7,5},{8,10},{9,15},{10,... | collective-permute-start | bytes 1572872 | tf_op jit(solution)/shard_map/ppermute | solution.py:45
  354.4 24.5 %collective-permute-start.48 = (bf16[128,2048]{1,0:T(8,128)(2,1)S(1)}, bf16[128,2048]{1,0:T(8,128)(2,1)}, u32[]{:S(2)}, u32[]{:S(2)}) collective-permute-start(bf16[128,2048]{1,0:T(8,128)(2,1)S(1)} %get-tuple-element.150.refs_8_), channel_id=1, source_target_pairs={{0,6},{1,3},{2,0},{3,5},{4,2},{5,7},{6,4},{7,1},{8,14},{9,11},{10,... | collective-permute-start | bytes 1572872 | tf_op jit(solution)/shard_map/ppermute | solution.py:45
  355.2 24.2 %collective-permute-start.45 = (bf16[128,2048]{1,0:T(8,128)(2,1)S(1)}, bf16[128,2048]{1,0:T(8,128)(2,1)S(1)}, u32[]{:S(2)}, u32[]{:S(2)}) collective-permute-start(bf16[128,2048]{1,0:T(8,128)(2,1)S(1)} %get-tuple-element.150.refs_8_), channel_id=1, source_target_pairs={{0,1},{1,0},{2,3},{3,2},{4,5},{5,4},{6,7},{7,6},{8,9},{9,8},{10,11... | collective-permute-start | bytes 1572872 | tf_op jit(solution)/shard_map/ppermute | solution.py:45
  378.8 29.8 %collective-permute-start.47 = (bf16[128,2048]{1,0:T(8,128)(2,1)S(1)}, bf16[128,2048]{1,0:T(8,128)(2,1)}, u32[]{:S(2)}, u32[]{:S(2)}) collective-permute-start(bf16[128,2048]{1,0:T(8,128)(2,1)S(1)} %collective-permute-done.46.refs_10_), channel_id=1, source_target_pairs={{0,1},{1,0},{2,3},{3,2},{4,5},{5,4},{6,7},{7,6},{8,9},{9,8},{10,11... | collective-permute-start | bytes 1572872 | tf_op jit(solution)/shard_map/ppermute | solution.py:45
  378.9 34.0 %collective-permute-start.49 = (bf16[128,2048]{1,0:T(8,128)(2,1)}, bf16[128,2048]{1,0:T(8,128)(2,1)}, u32[]{:S(2)}, u32[]{:S(2)}) collective-permute-start(bf16[128,2048]{1,0:T(8,128)(2,1)} %collective-permute-done.48.refs_12_), channel_id=1, source_target_pairs={{0,1},{1,0},{2,3},{3,2},{4,5},{5,4},{6,7},{7,6},{8,9},{9,8},{10,11... | collective-permute-start | bytes 1572872 | tf_op jit(solution)/shard_map/ppermute | solution.py:45
  406.1 262.1 %all-gather.13.cloned.1.call-start = ((), (), s32[]{:S(2)}) async-start(), calls=%async_computation.7 | async-start | bytes 5308416 | tf_op jit(solution)/shard_map/all_gather | solution.py:836
  408.6 41.5 %collective-permute-start.38 = (bf16[128,2048]{1,0:T(8,128)(2,1)S(1)}, bf16[128,2048]{1,0:T(8,128)(2,1)S(1)}, u32[]{:S(2)}, u32[]{:S(2)}) collective-permute-start(bf16[128,2048]{1,0:T(8,128)(2,1)S(1)} %get-tuple-element.154), channel_id=1, source_target_pairs={{0,1},{1,0},{2,3},{3,2},{4,5},{5,4},{6,7},{7,6},{8,9},{9,8},{10,11... | collective-permute-start | bytes 1572872 | tf_op jit(solution)/shard_map/ppermute | solution.py:45
  416.3 33.8 %collective-permute-start.44 = (bf16[128,2048]{1,0:T(8,128)(2,1)S(1)}, bf16[128,2048]{1,0:T(8,128)(2,1)S(1)}, u32[]{:S(2)}, u32[]{:S(2)}) collective-permute-start(bf16[128,2048]{1,0:T(8,128)(2,1)S(1)} %get-tuple-element.159), channel_id=1, source_target_pairs={{0,2},{1,7},{2,4},{3,1},{4,6},{5,3},{6,0},{7,5},{8,10},{9,15},{10,... | collective-permute-start | bytes 1572872 | tf_op jit(solution)/shard_map/ppermute | solution.py:45
  417.9 32.2 %collective-permute-start.42 = (bf16[128,2048]{1,0:T(8,128)(2,1)S(1)}, bf16[128,2048]{1,0:T(8,128)(2,1)S(1)}, u32[]{:S(2)}, u32[]{:S(2)}) collective-permute-start(bf16[128,2048]{1,0:T(8,128)(2,1)S(1)} %get-tuple-element.160), channel_id=1, source_target_pairs={{0,6},{1,3},{2,0},{3,5},{4,2},{5,7},{6,4},{7,1},{8,14},{9,11},{10,... | collective-permute-start | bytes 1572872 | tf_op jit(solution)/shard_map/ppermute | solution.py:45
  419.6 30.5 %collective-permute-start.40 = (bf16[128,2048]{1,0:T(8,128)(2,1)S(1)}, bf16[128,2048]{1,0:T(8,128)(2,1)S(1)}, u32[]{:S(2)}, u32[]{:S(2)}) collective-permute-start(bf16[128,2048]{1,0:T(8,128)(2,1)S(1)} %get-tuple-element.158), channel_id=1, source_target_pairs={{0,4},{1,5},{2,6},{3,7},{4,0},{5,1},{6,2},{7,3},{8,12},{9,13},{10,... | collective-permute-start | bytes 1572872 | tf_op jit(solution)/shard_map/ppermute | solution.py:45
  526.7 66.5 %collective-permute-start.57 = (bf16[128,2048]{1,0:T(8,128)(2,1)S(1)}, bf16[128,2048]{1,0:T(8,128)(2,1)S(1)}, u32[]{:S(2)}, u32[]{:S(2)}) collective-permute-start(bf16[128,2048]{1,0:T(8,128)(2,1)S(1)} %get-tuple-element.120), channel_id=1, source_target_pairs={{0,1},{1,0},{2,3},{3,2},{4,5},{5,4},{6,7},{7,6},{8,9},{9,8},{10,11... | collective-permute-start | bytes 1572872 | tf_op jit(solution)/shard_map/ppermute | solution.py:45
  526.8 71.0 %collective-permute-start.55 = (bf16[128,2048]{1,0:T(8,128)(2,1)S(1)}, bf16[128,2048]{1,0:T(8,128)(2,1)S(1)}, u32[]{:S(2)}, u32[]{:S(2)}) collective-permute-start(bf16[128,2048]{1,0:T(8,128)(2,1)S(1)} %get-tuple-element.118), channel_id=1, source_target_pairs={{0,1},{1,0},{2,3},{3,2},{4,5},{5,4},{6,7},{7,6},{8,9},{9,8},{10,11... | collective-permute-start | bytes 1572872 | tf_op jit(solution)/shard_map/ppermute | solution.py:45
  528.8 42.2 %collective-permute-start.76 = (bf16[4,2,2,16,576]{4,3,2,1,0:T(8,128)(2,1)}, bf16[4,2,2,16,576]{4,3,2,1,0:T(8,128)(2,1)S(1)}, u32[]{:S(2)}, u32[]{:S(2)}) collective-permute-start(bf16[4,2,2,16,576]{4,3,2,1,0:T(8,128)(2,1)} %copy-done.52), channel_id=1, source_target_pairs={{0,72},{1,9},{2,74},{3,11},{4,76},{5,13},{6,78},{7,15},{8,0},{9,65... | collective-permute-start | bytes 884744 | tf_op jit(solution)/shard_map/ppermute | solution.py:45
  529.6 41.4 %collective-permute-start.75 = (bf16[4,2,2,16,576]{4,3,2,1,0:T(8,128)(2,1)}, bf16[4,2,2,16,576]{4,3,2,1,0:T(8,128)(2,1)S(1)}, u32[]{:S(2)}, u32[]{:S(2)}) collective-permute-start(bf16[4,2,2,16,576]{4,3,2,1,0:T(8,128)(2,1)} %copy-done.51), channel_id=1, source_target_pairs={{0,64},{1,65},{2,66},{3,67},{4,68},{5,69},{6,70},{7,71},{8,72},{9,... | collective-permute-start | bytes 884744 | tf_op jit(solution)/shard_map/ppermute | solution.py:45
  537.8 36.8 %collective-permute-start.71 = (bf16[4,2,2,16,576]{4,3,2,1,0:T(8,128)(2,1)}, bf16[4,2,2,16,576]{4,3,2,1,0:T(8,128)(2,1)S(1)}, u32[]{:S(2)}, u32[]{:S(2)}) collective-permute-start(bf16[4,2,2,16,576]{4,3,2,1,0:T(8,128)(2,1)} %copy-done.50), channel_id=1, source_target_pairs={{0,16},{1,49},{2,18},{3,51},{4,20},{5,53},{6,22},{7,55},{8,24},{9,... | collective-permute-start | bytes 884744 | tf_op jit(solution)/shard_map/ppermute | solution.py:45
  571.0 15.7 %collective-permute-start.70 = (bf16[4,2,2,16,576]{4,3,2,1,0:T(8,128)(2,1)}, bf16[4,2,2,16,576]{4,3,2,1,0:T(8,128)(2,1)S(1)}, u32[]{:S(2)}, u32[]{:S(2)}) collective-permute-start(bf16[4,2,2,16,576]{4,3,2,1,0:T(8,128)(2,1)} %copy-done.49), channel_id=1, source_target_pairs={{0,48},{1,17},{2,50},{3,19},{4,52},{5,21},{6,54},{7,23},{8,56},{9,... | collective-permute-start | bytes 884744 | tf_op jit(solution)/shard_map/ppermute | solution.py:45
  571.0 21.9 %collective-permute-start.69 = (bf16[4,2,2,16,576]{4,3,2,1,0:T(8,128)(2,1)S(1)}, bf16[4,2,2,16,576]{4,3,2,1,0:T(8,128)(2,1)S(1)}, u32[]{:S(2)}, u32[]{:S(2)}) collective-permute-start(bf16[4,2,2,16,576]{4,3,2,1,0:T(8,128)(2,1)S(1)} %copy-done.48), channel_id=1, source_target_pairs={{0,32},{1,33},{2,34},{3,35},{4,36},{5,37},{6,38},{7,39},{8,40},{9,... | collective-permute-start | bytes 884744 | tf_op jit(solution)/shard_map/ppermute | solution.py:45
  574.5 27.0 %collective-permute-start.53 = (bf16[128,2048]{1,0:T(8,128)(2,1)S(1)}, bf16[128,2048]{1,0:T(8,128)(2,1)S(1)}, u32[]{:S(2)}, u32[]{:S(2)}) collective-permute-start(bf16[128,2048]{1,0:T(8,128)(2,1)S(1)} %get-tuple-element.116), channel_id=1, source_target_pairs={{0,1},{1,0},{2,3},{3,2},{4,5},{5,4},{6,7},{7,6},{8,9},{9,8},{10,11... | collective-permute-start | bytes 1572872 | tf_op jit(solution)/shard_map/ppermute | solution.py:45
  603.5 26.5 %collective-permute-start.58 = (bf16[128,2048]{1,0:T(8,128)(2,1)S(1)}, bf16[128,2048]{1,0:T(8,128)(2,1)S(1)}, u32[]{:S(2)}, u32[]{:S(2)}) collective-permute-start(bf16[128,2048]{1,0:T(8,128)(2,1)S(1)} %add_convert_fusion), channel_id=1, source_target_pairs={{0,2},{1,7},{2,4},{3,1},{4,6},{5,3},{6,0},{7,5},{8,10},{9,15},{10,... | collective-permute-start | bytes 1572872 | tf_op jit(solution)/shard_map/ppermute | solution.py:45
  603.5 26.5 %collective-permute-start.56 = (bf16[128,2048]{1,0:T(8,128)(2,1)S(1)}, bf16[128,2048]{1,0:T(8,128)(2,1)S(1)}, u32[]{:S(2)}, u32[]{:S(2)}) collective-permute-start(bf16[128,2048]{1,0:T(8,128)(2,1)S(1)} %add_convert_fusion.1), channel_id=1, source_target_pairs={{0,6},{1,3},{2,0},{3,5},{4,2},{5,7},{6,4},{7,1},{8,14},{9,11},{10,... | collective-permute-start | bytes 1572872 | tf_op jit(solution)/shard_map/ppermute | solution.py:45
  609.1 20.9 %collective-permute-start.54 = (bf16[128,2048]{1,0:T(8,128)(2,1)S(1)}, bf16[128,2048]{1,0:T(8,128)(2,1)S(1)}, u32[]{:S(2)}, u32[]{:S(2)}) collective-permute-start(bf16[128,2048]{1,0:T(8,128)(2,1)S(1)} %add_convert_fusion.2), channel_id=1, source_target_pairs={{0,4},{1,5},{2,6},{3,7},{4,0},{5,1},{6,2},{7,3},{8,12},{9,13},{10,... | collective-permute-start | bytes 1572872 | tf_op jit(solution)/shard_map/ppermute | solution.py:45
  649.7 16.3 %collective-permute-start.87 = (bf16[2,2,4,16,576]{4,3,2,1,0:T(8,128)(2,1)S(1)}, bf16[2,2,4,16,576]{4,3,2,1,0:T(8,128)(2,1)S(1)}, u32[]{:S(2)}, u32[]{:S(2)}) collective-permute-start(bf16[2,2,4,16,576]{4,3,2,1,0:T(8,128)(2,1)S(1)} %pad_maximum_fusion.5.refs_0_), channel_id=1, source_target_pairs={{0,16},{1,49},{2,18},{3,51},{4,20},{5,53},{6,22},{7,55},{8,24},{9,... | collective-permute-start | bytes 884744 | tf_op jit(solution)/shard_map/ppermute | solution.py:45
  650.6 15.4 %collective-permute-start.88 = (bf16[2,2,4,16,576]{4,3,2,1,0:T(8,128)(2,1)S(1)}, bf16[2,2,4,16,576]{4,3,2,1,0:T(8,128)(2,1)S(1)}, u32[]{:S(2)}, u32[]{:S(2)}) collective-permute-start(bf16[2,2,4,16,576]{4,3,2,1,0:T(8,128)(2,1)S(1)} %pad_maximum_fusion.5.refs_0_), channel_id=1, source_target_pairs={{0,48},{1,17},{2,50},{3,19},{4,52},{5,21},{6,54},{7,23},{8,56},{9,... | collective-permute-start | bytes 884744 | tf_op jit(solution)/shard_map/ppermute | solution.py:45
  (138 other events, 1876.4 us)
Sparse Core Ops, SparseCore 0:
  44.1 52.2 all-gather.10
  98.7 32.7 all-gather.6
  133.2 32.1 all-gather.8
  319.0 86.9 reduce-scatter.2
  408.3 29.6 reduce-scatter.4
  504.0 83.3 all-gather.12
where the time goes:
time: 690 us; the launch traced here: 682 us
  waiting for transfers between devices  326 us (47%)
  Pallas kernels  141 us (20%)
  starting transfers between devices  118 us (17%)
  local copies, waits for them, and re-layouts  58 us (8%)
  other arithmetic  17.5 us (3%)
  between operations  16.2 us (2%)
    ppermute x94, waiting for transfers between devices, send(): return lax.ppermute(value, BOTH, pairs)  258 us
    pallas_call x16, Pallas kernels, call(): pl.pallas_call(body, grid_spec=pltpu.PrefetchScalarGridSpec(num_scalar_pr...  141 us
    ppermute x94, starting transfers between devices, send(): return lax.ppermute(value, BOTH, pairs)  118 us
    all_gather x1, waiting for transfers between devices, on_device(): lax.all_gather(packs[:, :3], 'batch', axis=0, axis_index_groups=X_GROUPS)  49.9 us
    unnamed x180, local copies, waits for them, and re-layouts  43.1 us
    reduce_scatter x1, waiting for transfers between devices, on_device(): lax.psum_scatter(mlp_sums, 'batch', scatter_dimension=0, axis_index_group...  17.8 us
  transfers between devices with their start and end apart: 100, of which 38 were waited for; matrix products, arithmetic and copies ran while one was open for 6% of the time, Pallas kernels for 14%

commit v1 on v0

--- a/solution.py
+++ b/solution.py
@@ -280,8 +280,9 @@
     )
 
 
-def project_back_kernel(dq_ref, dkv_ref, w_ref, *out_refs):
-    rows = jnp.concatenate([dq_ref[...], dkv_ref[...]], axis=1)
+def project_back_kernel(dq0_ref, dq1_ref, dq2_ref, dkv_ref, w_ref, *out_refs):
+    queries = jnp.concatenate([dq0_ref[...], dq1_ref[...], dq2_ref[...]], axis=0)
+    rows = jnp.concatenate([queries, dkv_ref[...]], axis=1)
     grad = dot_last(rows, w_ref[...]).astype(BF)
     for r in range(8):
         out_refs[r][...] = grad[TOK * r : TOK * (r + 1)]
@@ -290,12 +291,9 @@
 def project_back(dq, dkv, w):
     return call(
         project_back_kernel, (), (4,),
-        [
-            pl.BlockSpec((8 * TOK, QUERY), lambda k: (0, 0)),
-            pl.BlockSpec((8 * TOK, HEAD), lambda k: (0, 0)),
-            pl.BlockSpec((PART, QKV), lambda k: (k, 0)),
-        ],
-        [pl.BlockSpec((TOK, PART), lambda k: (0, k))] * 8, [sds((TOK, D))] * 8, [], 4, (dq, dkv, w),
+        [pl.BlockSpec(each.shape, lambda k: (0, 0)) for each in tuple(dq) + (dkv,)]
+        + [pl.BlockSpec((PART, QKV), lambda k: (k, 0))],
+        [pl.BlockSpec((TOK, PART), lambda k: (0, k))] * 8, [sds((TOK, D))] * 8, [], 4, tuple(dq) + (dkv, w),
     )
 
 
@@ -361,16 +359,30 @@
     )
 
 
-def attend_back_kernel(query_place, key_slot, core, count, q_ref, g_ref, k_ref, v_ref, kt_ref, dq_ref, keep_ref, give_ref, total, dk_ref, dv_ref):
+def attend_back_kernel(start, count, first_call, last_call, query_place, key_slot, core, used, *refs):
+    q_ref, g_refs, w_ref = refs[0], refs[1 : 1 + count], refs[1 + count]
+    k_ref, v_ref, kt_ref = refs[2 + count : 5 + count]
+    refs = refs[5 + count :]
+    if not first_call:
+        dk_in, dv_in = refs[:2]
+        refs = refs[2:]
+    dq_ref, refs = refs[0], refs[1:]
+    if last_call:
+        keep_ref, give_ref, grads_all, total, dk_ref, dv_ref = refs
+    else:
+        dk_ref, dv_ref, grads_all, total = refs
     step_at = pl.program_id(0)
-    place = query_place[step_at]
+    place = query_place[start + step_at]
+
+    @pl.when(step_at == 0)
+    def _():
+        rows = jnp.concatenate([ref[...] for ref in g_refs], axis=0)
+        grads_all[...] = dot_last(rows, w_ref[...]).astype(BF)
+        dk_ref[...] = jnp.zeros_like(dk_ref) if first_call else dk_in[...]
+        dv_ref[...] = jnp.zeros_like(dv_ref) if first_call else dv_in[...]
+
     queries = head_rows(q_ref[...])
-    grads = head_rows(g_ref[...])
-
-    @pl.when(step_at == 0)
-    def _():
-        dk_ref[...] = jnp.zeros_like(dk_ref)
-        dv_ref[...] = jnp.zeros_like(dv_ref)
+    grads = head_rows(grads_all[pl.ds(pl.multiple_of(step_at * TOK, TOK), TOK), :])
 
     def block(j, diagonal):
         at = pl.ds(pl.multiple_of(j * TOK, TOK), TOK)
@@ -399,30 +411,40 @@
 
     dq_ref[...] = head_columns((total[...] * SCORE).T).astype(BF)
 
-    @pl.when(step_at == pl.num_programs(0) - 1)
-    def _():
-        first = core[0] == 0
-        for j in range(16):
-            key = dk_ref[j * TOK : (j + 1) * TOK, :] * SCORE
-            value = dv_ref[j * TOK : (j + 1) * TOK, :]
-            row = lax.broadcasted_iota(jnp.int32, value.shape, 0)
-            value = jnp.where(row < count[j], value, 0.0)
-            keep_ref[j * TOK : (j + 1) * TOK, :] = jnp.where(first, key, value).astype(BF)
-            other = j ^ 1
-            give_ref[other * TOK : (other + 1) * TOK, :] = jnp.where(first, value, key).astype(BF)
-
-
-def attend_back(query_place, key_slot, core, count, q, g, k, v):
-    rows = q.shape[0]
+    if last_call:
+
+        @pl.when(step_at == count - 1)
+        def _():
+            first = core[0] == 0
+            for j in range(16):
+                key = dk_ref[j * TOK : (j + 1) * TOK, :] * SCORE
+                value = dv_ref[j * TOK : (j + 1) * TOK, :]
+                row = lax.broadcasted_iota(jnp.int32, value.shape, 0)
+                value = jnp.where(row < used[j], value, 0.0)
+                keep_ref[j * TOK : (j + 1) * TOK, :] = jnp.where(first, key, value).astype(BF)
+                other = j ^ 1
+                give_ref[other * TOK : (other + 1) * TOK, :] = jnp.where(first, value, key).astype(BF)
+
+
+def attend_back(start, g, sums, last, query_place, key_slot, core, used, q, w, k, v, kt):
+    count = len(g)
     whole = lambda i, *_: (0, 0)
-    rows_spec = pl.BlockSpec((TOK, QUERY), lambda i, *_: (i, 0))
     kv_spec = pl.BlockSpec(k.shape, whole)
+    kv_type = BF if last else F32
+    sums = tuple(sums)
+    scratch = [pltpu.VMEM((count * TOK, QUERY), BF), pltpu.VMEM((HEAD, 4 * TOK), F32)]
+    if last:
+        scratch += [pltpu.VMEM(k.shape, F32)] * 2
     return call(
-        attend_back_kernel, (query_place, key_slot, core, count), (rows // TOK,),
-        [rows_spec, rows_spec, kv_spec, kv_spec, pl.BlockSpec((HEAD, k.shape[0]), whole)],
-        [rows_spec, kv_spec, kv_spec], [sds(q.shape), sds(k.shape), sds(v.shape)],
-        [pltpu.VMEM((HEAD, 4 * TOK), F32), pltpu.VMEM(k.shape, F32), pltpu.VMEM(k.shape, F32)],
-        28, (q, g, k, v, k.T),
+        functools.partial(attend_back_kernel, start, count, not sums, last),
+        (query_place, key_slot, core, used), (count,),
+        [pl.BlockSpec((TOK, QUERY), lambda i, *_: (start + i, 0))]
+        + [pl.BlockSpec((TOK, D), whole)] * count
+        + [pl.BlockSpec(w.shape, whole), kv_spec, kv_spec, pl.BlockSpec((HEAD, k.shape[0]), whole)]
+        + [kv_spec] * len(sums),
+        [pl.BlockSpec((TOK, QUERY), lambda i, *_: (i, 0)), kv_spec, kv_spec],
+        [sds((count * TOK, QUERY)), sds(k.shape, kv_type), sds(v.shape, kv_type)], scratch,
+        4 * count, (q,) + tuple(g) + (w, k, v, kt) + sums,
     )
 
 
@@ -507,11 +529,11 @@
     return [x_first] * 4 + [y_own] * 2 + [y_other] * 2, [sds((4, 2, 2) + tail)] * 8
 
 
-def write_grads(outs, xs, yhs, core, write):
+def write_grads(outs, xs, yhs, core, write, first_rows=None):
     half, p = pl.program_id(0), pl.program_id(1)
 
-    def go(pos, r, ref):
-        inside = yhs[2 * half + pos] * 64 + xs[r] * 16
+    def go(pos, r, ref, first=False):
+        inside = yhs[2 * half + pos] * 64 + (first_rows(r) if first and first_rows else xs[r] * 16)
         for rc in range(2):
             write(ref.at[rc], inside, jnp.abs(core[0] - rc), rc)
 
@@ -519,7 +541,7 @@
     def _():
         for r in range(4):
             for pos in range(2):
-                go(pos, r, outs[r].at[pos, 0])
+                go(pos, r, outs[r].at[pos, 0], True)
 
     for each in range(2):
 
@@ -530,8 +552,8 @@
                     go(pos, r, outs[4 + 2 * each + pos].at[r, 0])
 
 
-def mlp_grads_kernel(column, halves, core, nat, *refs):
-    tokens, (g_ref, da_ref, dc_ref, z_ref), out_ref, (turned, grads) = refs[:8], refs[8:12], refs[12], refs[13:]
+def mlp_grads_kernel(column, xs, yhs, core, nat, *refs):
+    tokens, (g_ref, da_ref, dc_ref, z_ref), outs, (turned, grads) = refs[:8], refs[8:12], refs[12:17], refs[17:]
     rows = jnp.concatenate([ref[...] for ref in tokens], axis=0).T
     grads[0] = dot(rows, da_ref[...])
     grads[1] = dot(rows, dc_ref[...])
@@ -539,31 +561,34 @@
         turned[:, TOK * r : TOK * (r + 1)] = g_ref[pl.ds(pl.multiple_of(nat[r] * TOK, TOK), TOK), :].T
     grads[2] = dot(turned[...], z_ref[...])
 
-    for rc in range(2):
-        start = jnp.abs(core[0] - rc) * 128
-        for yh in range(2):
-            for r in range(4):
-                for m in range(3):
-                    out_ref[r, yh, 0, 0, rc, m] = grads[m, at_rows(start + 64 * yh + 16 * r, 16), :].astype(BF)
-
-
-def mlp_grads(column, halves, core, nat, tokens, g, da, dc, z):
+    def write(ref, inside, which, rc):
+        for m in range(3):
+            ref[m] = grads[m, at_rows(which * 128 + inside, 16), :].astype(BF)
+
+    write_grads([outs[0].at[r] for r in range(4)] + list(outs[1:]), xs, yhs, core, write, lambda r: 16 * r)
+
+
+def mlp_grads(column, xs, yhs, core, nat, tokens, g, da, dc, z):
     col = lambda h, p, column, *_: (0, column[4 * h + p])
     hidden = pl.BlockSpec((8 * TOK, WIDE), lambda h, p, *_: (0, 0))
+    tail = (3, 16, WIDE)
+    specs, shapes = grads_specs(tail)
+    x_first = pl.BlockSpec((4, 2, 1, 2) + tail, lambda h, p, *_: (0, h, jnp.minimum(p, 1), 0, 0, 0, 0))
     return call(
-        mlp_grads_kernel, (column, halves, core, nat), (2, 4),
+        mlp_grads_kernel, (column, xs, yhs, core, nat), (2, 4),
         [pl.BlockSpec((TOK, 256), col)] * 8 + [pl.BlockSpec((8 * TOK, 256), col), hidden, hidden, hidden],
-        pl.BlockSpec((4, 2, 1, 1, 2, 3, 16, WIDE), lambda h, p, column, halves, *_: (0, 0, halves[h], p, 0, 0, 0, 0)),
-        sds((4, 2, 2, 4, 2, 3, 16, WIDE)), [pltpu.VMEM((256, 8 * TOK), BF), pltpu.VMEM((3, 256, WIDE), F32)],
+        [x_first] + specs[4:], [sds((4, 4, 2, 2) + tail)] + shapes[4:],
+        [pltpu.VMEM((256, 8 * TOK), BF), pltpu.VMEM((3, 256, WIDE), F32)],
         17, tuple(tokens) + (g, da, dc, z),
     )
 
 
 def attn_grads_kernel(column, xs, yhs, core, halves, chunk, *refs):
-    h_refs, g_refs, o_refs, (dq_ref, dkv_ref, w_ref) = refs[:8], refs[8:16], refs[16:20], refs[20:23]
-    outs, gain_ref, (first, second) = refs[23:31], refs[31], refs[32:]
+    h_refs, g_refs, o_refs, dq_refs, (dkv_ref, w_ref) = refs[:8], refs[8:16], refs[16:20], refs[20:23], refs[23:25]
+    outs, gain_ref, (first, second) = refs[25:33], refs[33], refs[34:]
     rows = jnp.concatenate([ref[...] for ref in h_refs], axis=0).T
-    first[...] = dot(rows, jnp.concatenate([dq_ref[...], dkv_ref[...]], axis=1))
+    queries = jnp.concatenate([ref[...] for ref in dq_refs], axis=0)
+    first[...] = dot(rows, jnp.concatenate([queries, dkv_ref[...]], axis=1))
     grads = jnp.concatenate([ref[...] for ref in g_refs], axis=0)
     second[...] = dot(jnp.concatenate([ref[...] for ref in o_refs], axis=0).T, grads)
     gain = jnp.sum(first[...] * w_ref[...].astype(F32), axis=1, keepdims=True)
@@ -588,37 +613,40 @@
         + [pl.BlockSpec((TOK, 2 * QUERY), lambda i, p, *_: (0, p))] * 8
         + [pl.BlockSpec((2 * TOK, 128), lambda i, p, column, xs, yhs, core, halves, chunk: (0, halves[i]))] * 4
         + [
-            pl.BlockSpec((8 * TOK, QUERY), whole),
+            *[pl.BlockSpec(each.shape, whole) for each in dq],
             pl.BlockSpec((8 * TOK, HEAD), whole),
             pl.BlockSpec((256, QKV), lambda i, p, column, *_: (column[4 * i + p], 0)),
         ],
         specs + [pl.BlockSpec((1, 8, 256), lambda i, p, column, *_: (column[4 * i + p], 0, 0))],
         shapes + [sds((8, 8, 256), F32)],
         [pltpu.VMEM((256, QKV), F32), pltpu.VMEM((128, 2 * QUERY), F32)],
-        10, (h,) * 8 + tuple(g) + tuple(o) + (dq, dkv, w),
+        10, (h,) * 8 + tuple(g) + tuple(o) + tuple(dq) + (dkv, w),
     )
     return outs, gain[:, 0, :].reshape(D)
 
 
-def finish_mlp_kernel(spots, core, part_ref, gate_ref, up_ref, down_ref, rows):
+def finish_mlp_kernel(spots, xs, yhs, core, *refs):
+    parts, (gate_ref, up_ref, down_ref), (rows,) = refs[:4], refs[4:7], refs[7:]
     first = core[0] == 0
     for m, out_ref in enumerate((gate_ref, up_ref, rows)):
-        for b in range(8):
-            own = part_ref[b, 0, 0, m].astype(F32)
-            other = part_ref[b, 1, 0, m].astype(F32)
-            low, high = jnp.where(first, own, other), jnp.where(first, other, own)
-            out_ref[16 * b : 16 * (b + 1), :] = jnp.concatenate([low, high], axis=1)
+        for r in range(4):
+            for h in range(2):
+                at = at_rows(yhs[h] * 64 + xs[r] * 16, 16)
+                own = parts[r][h, 0, 0, m].astype(F32)
+                other = parts[r][h, 1, 0, m].astype(F32)
+                low, high = jnp.where(first, own, other), jnp.where(first, other, own)
+                out_ref[at, :] = jnp.concatenate([low, high], axis=1)
     down_ref[...] = rows[...].T
 
 
-def finish_mlp(spots, core, parts):
+def finish_mlp(spots, xs, yhs, core, parts):
     side = pl.BlockSpec((128, 2 * WIDE), lambda p, spots, *_: (0, spots[1 + p]))
     return call(
-        finish_mlp_kernel, (spots, core), (4,),
-        [pl.BlockSpec((8, 2, 1, 3, 16, WIDE), lambda p, *_: (0, 0, p, 0, 0, 0))],
+        finish_mlp_kernel, (spots, xs, yhs, core), (4,),
+        [pl.BlockSpec((2, 2, 1, 3, 16, WIDE), lambda p, *_: (0, 0, p, 0, 0, 0))] * 4,
         [side, side, pl.BlockSpec((2 * WIDE, 128), lambda p, spots, *_: (spots[1 + p], 0))],
         [sds((128, FF), F32), sds((128, FF), F32), sds((FF, 128), F32)], [pltpu.VMEM((128, 2 * WIDE), F32)],
-        5, (parts,),
+        5, tuple(parts),
     )
 
 
@@ -709,17 +737,13 @@
             parts += [part, swap(part)]
         return parts
 
+    def give(group, total):
+        value = total.astype(BF)
+        return across(value, "z") if group == 3 else step(value, "z", -1 if group == 1 else 1)
+
     def scatter_tokens(mine, peer):
-        own, before, forward, far = [add(a, swap(b)) for a, b in zip(mine, peer)]
-        got = [
-            across(far.astype(BF), "z"),
-            step(before.astype(BF), "z", -1),
-            step(forward.astype(BF), "z", 1),
-        ]
-        return add(own, *got)
-
-    def flip(rows):
-        return jnp.flip(rows.reshape(-1, 2, TOK, rows.shape[-1]), axis=1).reshape(rows.shape)
+        sums = [add(a, swap(b)) for a, b in zip(mine, peer)]
+        return add(sums[0], *[give(g, sums[g]) for g in (3, 1, 2)])
 
     gain_one = attn_gain.astype(F32)
     gain_two = mlp_gain.astype(F32)
@@ -740,8 +764,9 @@
         pieces = ring_gather(part, "x", forward)
         return list(pieces) + [step(piece, "y", 1) for piece in pieces]
 
+    normed_own = (rows_in * scale_attn * gain_one).astype(BF)
     normed_attn = lax.all_gather(
-        (rows_in * scale_attn * gain_one).astype(BF), "blk", axis=0, tiled=True, axis_index_groups=ZC_GROUPS
+        normed_own, "blk", axis=0, tiled=True, axis_index_groups=ZC_GROUPS
     )
     out_rows = lax.dynamic_slice_in_dim(output_weight, x * 32, 32, axis=0)
     out_part = send(
@@ -749,7 +774,7 @@
         lambda yh, x, yl, z, c: (yh, x, c, 2 * yl + z // 2, z % 2),
     )
     packs = exchange(
-        *pack(spots, core, gate_weight, up_weight, down_weight, query_weight, key_weight, value_weight)
+        *pack(after(spots, normed_own), core, gate_weight, up_weight, down_weight, query_weight, key_weight, value_weight)
     )
     attn_part = jnp.concatenate([out_part, packs[:, 3, :, :QKV]], axis=-1)
     attn_pieces = spread(attn_part, False)
@@ -758,7 +783,7 @@
     w_mlp = place_mlp(slot, halves, mlp_half_rows, step(mlp_half_rows, "y", 1))
 
     grad_rows = lax.all_gather(
-        after(cotangent[0], mlp_half_rows), "blk", axis=0, tiled=True, axis_index_groups=ZC_GROUPS
+        after(cotangent[0], attn_pieces[7]), "blk", axis=0, tiled=True, axis_index_groups=ZC_GROUPS
     )
 
 
@@ -778,39 +803,52 @@
     kv_other = swap(jnp.concatenate([kv_own[1], kv_half[1]], axis=0))
     keys = jnp.where(first_core, kv_mine, kv_other)
     values = jnp.where(usable, jnp.where(first_core, kv_other, kv_mine), 0)
-    attended, mine, peer = [None] * 4, [None] * 4, [None] * 4
+    attended, sums, got = [None] * 4, [None] * 4, [None] * 4
     for g in (3, 1, 2, 0):
-        at = after(query_place, mlp_half_rows) if g == 0 else query_place
-        attended[g], mine[g], peer[g] = attend(g, at, key_slot, queries, keys, values, w_out)
-    residual = rows_in + scatter_tokens(mine, peer)
+        at = after(query_place, mlp_half_rows, got[3]) if g == 0 else query_place
+        attended[g], mine, peer = attend(g, at, key_slot, queries, keys, values, w_out)
+        sums[g] = add(mine, swap(peer))
+        if g:
+            got[g] = give(g, sums[g])
+    residual = rows_in + add(sums[0], *got[1:])
     scale_mlp = rms_scale(residual)
     mlp_parts = gather_tokens((residual * scale_mlp * gain_two).astype(BF))
 
 
-    kept, results = None, []
+    order = [6, 7, 2, 3, 4, 5, 0, 1]
+    mlp_parts = [mlp_parts[r] for r in order]
+    mlp_chunk = jnp.stack([chunk[r] for r in order])
+    kept, sums, got, at = None, [None] * 4, [None] * 4, mlp_chunk
     for part in range(2):
-        kept, result = mlp_half(part, chunk, mlp_parts[4 * part : 4 * part + 4], grad_rows, w_mlp, kept)
-        results += result
+        kept, result = mlp_half(part, at, mlp_parts[4 * part : 4 * part + 4], grad_rows, w_mlp, kept)
+        for g, mine, peer in zip(((3, 1), (2, 0))[part], result[::2], result[1::2]):
+            sums[g] = add(mine, swap(peer))
+            if g:
+                got[g] = give(g, sums[g])
+        at = after(mlp_chunk, sums[3], sums[1])
     hidden, gate_grad_rows, up_grad_rows = kept
-    mlp_sums = mlp_grads(
-        column, halves, core, chunk, mlp_parts, grad_rows, gate_grad_rows, up_grad_rows, hidden
-    )
-    normed_grad = after(scatter_tokens(results[::2], results[1::2]), mlp_sums)
-    mlp_sums = lax.psum_scatter(mlp_sums, "batch", scatter_dimension=0, axis_index_groups=X_GROUPS)
-    mlp_sums = lax.psum_scatter(
-        mlp_sums.reshape((4,) + mlp_sums.shape[2:]), BOTH, scatter_dimension=0, axis_index_groups=Y_GROUPS
-    )
+    mlp_outs = mlp_grads(
+        column, xs, yhs, core, after(mlp_chunk, got[3], got[1]), mlp_parts, grad_rows,
+        gate_grad_rows, up_grad_rows, hidden,
+    )
+    normed_grad = after(add(sums[0], *got[1:]), mlp_outs[0])
+    mlp_low = lax.psum_scatter(mlp_outs[0], "batch", scatter_dimension=0, axis_index_groups=X_GROUPS)
+    high_far = step(mlp_outs[2], "y", 1)
+    high_after = step(mlp_outs[3], "y", -1)
+
     residual_grad = cotangent[0].astype(F32) + norm_back(residual, scale_mlp, gain_two, normed_grad)
     mlp_gain_part = jnp.sum(normed_grad * residual * scale_mlp, axis=0)
     branch_parts = gather_tokens(residual_grad.astype(BF))
-    branch = dot_last(after(hidden, branch_parts[7]), w_mlp[2]).astype(BF).reshape(4, 2, TOK, D)
-    layer_out = (residual + scatter_tokens(branch[:, 0], branch[:, 1])).astype(BF)[None]
-
-
-    def reduce_planes(outs):
-        low = ring_scatter(*outs[:4], "x").astype(BF)
+    high_before = step(add(after(mlp_outs[4], branch_parts[7]), high_far).astype(BF), "y", 1)
+    branch = dot_last(after(hidden, branch_parts[7]), w_mlp[2]).astype(BF).reshape(8, TOK, D)
+    branch = [branch[order.index(r)] for r in range(8)]
+    layer_out = (residual + scatter_tokens(branch[::2], branch[1::2])).astype(BF)[None]
+
+
+    def reduce_planes(outs, other):
+        low = after(ring_scatter(*outs[:4], "x").astype(BF), other)
         low = ring_scatter(low[0], low[2], low[3], low[1], "y").astype(BF)
-        high = ring_scatter(outs[4], outs[6], outs[7], outs[5], "y").astype(BF)
+        high = after(ring_scatter(outs[4], outs[6], outs[7], outs[5], "y").astype(BF), other)
         high = ring_scatter(high[0], high[1], high[2], high[3], "x").astype(BF)
         return jnp.concatenate([low, high])
 
@@ -820,20 +858,29 @@
         other = swap(jnp.stack([got[p][1] for p in (0, 2, 1, 3)]))
         return jnp.stack([mine, other])
 
-    def gather_batch(part):
-        return ring_gather(jnp.stack([part, across(part, "y")]), "x")
-
-
-    attn_grad = dot_last(jnp.concatenate(branch_parts), w_out).astype(BF)
-    query_grad_rows, kv_keep, kv_give = attend_back(
-        query_place, key_slot, core, key_count, queries, attn_grad, keys, values
-    )
+    def gather_batch(part, forward):
+        return ring_gather(jnp.stack([part, across(part, "y")]), "x", forward)
+
+
+    query_grad_rows, sums = [], ()
+    for start, stop in ((0, 2), (2, 6), (6, 8)):
+        rows, *sums = attend_back(
+            start, branch_parts[start:stop], sums, stop == 8,
+            query_place, key_slot, core, key_count, queries, w_out, keys, values, keys.T,
+        )
+        query_grad_rows.append(rows)
+    kv_keep, kv_give = sums
     kv_terms = add(kv_keep, swap(after(kv_give, layer_out)))
     half_rows = 8 * TOK
     kv_grad_rows = add(kv_terms[:half_rows], to_half(kv_terms[half_rows:].astype(BF))).astype(BF)
 
-    mlp_sums = resplit_back(after(mlp_sums, kv_keep))
-    gate_grad, up_grad, down_grad = finish_mlp(spots, core, lax.all_gather(mlp_sums, "batch"))
+    low = after(mlp_low, kv_keep)
+    low = ring_scatter(low[0], low[2], low[3], low[1], "y").astype(BF)
+    high = add(mlp_outs[1], high_after, after(high_before, kv_keep)).astype(BF)
+    high = ring_scatter(high[0], high[1], high[2], high[3], "x").astype(BF)
+    mlp_sums = resplit_back(jnp.concatenate([low, high]))
+    mlp_sums = gather_batch(mlp_sums, True)
+    gate_grad, up_grad, down_grad = finish_mlp(spots, xs, yhs, core, mlp_sums)
 
     attn_partial = project_back(query_grad_rows, kv_grad_rows, w_qkv)
     attn_sums, attn_gain_part = attn_grads(
@@ -841,13 +888,13 @@
     )
     gain_grads = sum_all(jnp.stack([attn_gain_part / gain_one, mlp_gain_part]))
     normed_attn_grad = scatter_tokens(attn_partial[::2], attn_partial[1::2])
-    attn_sums = after(reduce_planes(attn_sums), normed_attn_grad)
+    attn_sums = reduce_planes(attn_sums, normed_attn_grad)
     out_sums = send(
         attn_sums[..., :QUERY], lambda yh, x, yl, z, c: (yh, x, z // 2, 2 * (z % 2) + c, yl)
     )
     qkv_sums = resplit_back(attn_sums[..., QUERY:])
     attn_sums = jnp.concatenate([out_sums.reshape(2, 4, 16, QUERY), qkv_sums], axis=-1)
-    query_grad, key_grad, value_grad, output_grad = finish_attn(spots, xs, yhs, core, gather_batch(attn_sums))
+    query_grad, key_grad, value_grad, output_grad = finish_attn(spots, xs, yhs, core, gather_batch(attn_sums, False))
 
     tokens_grad = (
         residual_grad + norm_back(rows_in, scale_attn, gain_one, normed_attn_grad)

time: 690 us -> 675 us (0.978)
  waiting for transfers between devices: 326 us -> 285 us
  local copies, waits for them, and re-layouts: 58 us -> 27.8 us
  starting transfers between devices: 118 us -> 146 us
  Pallas kernels: 141 us -> 156 us
  other arithmetic: 17.5 us -> 30.7 us
    all_gather x1, waiting for transfers between devices: 49.9 us -> 0.01 us  [on_device(): lax.all_gather(packs[:, :3], 'batch', axis=0, axis_index_groups=X_GROUPS)]
    unnamed x180 -> x156, local copies, waits for them, and re-layouts: 43.1 us -> 14.3 us
    ppermute x94 -> x107, starting transfers between devices: 118 us -> 146 us  [send(): return lax.ppermute(value, BOTH, pairs)]
    ppermute x94 -> x107, waiting for transfers between devices: 258 us -> 285 us  [send(): return lax.ppermute(value, BOTH, pairs)]
    reduce_scatter x2 -> x1, waiting for transfers between devices: 17.8 us -> 0.02 us  [on_device(): lax.psum_scatter(mlp_outs[0], 'batch', scatter_dimension=0, axis_index_gr...]
    pallas_call x16 -> x18, Pallas kernels: 141 us -> 156 us  [call(): pl.pallas_call(body, grid_spec=pltpu.PrefetchScalarGridSpec(num_scalar_pr...]
    convert_element_type x13 -> x18, other arithmetic: 6.36 us -> 14.4 us  [the longest x10 6.05 us: give(): value = total.astype(BF)]
  transfers between devices with their start and end apart: 100 -> 111, of which waited for: 38 -> 42; matrix products, arithmetic and copies ran while one was open for 6% -> 5% of each run, Pallas kernels for 14% -> 20%
where the time goes in v1:
time: 675 us; the launch traced here: 666 us
  waiting for transfers between devices  285 us (42%)
  Pallas kernels  156 us (23%)
  starting transfers between devices  146 us (22%)
  other arithmetic  30.7 us (5%)
  local copies, waits for them, and re-layouts  27.8 us (4%)
  between operations  15.9 us (2%)
    ppermute x107, waiting for transfers between devices, send(): return lax.ppermute(value, BOTH, pairs)  285 us
    pallas_call x18, Pallas kernels, call(): pl.pallas_call(body, grid_spec=pltpu.PrefetchScalarGridSpec(num_scalar_pr...  156 us
    ppermute x107, starting transfers between devices, send(): return lax.ppermute(value, BOTH, pairs)  146 us
    unnamed x156, local copies, waits for them, and re-layouts  14.3 us
  transfers between devices with their start and end apart: 111, of which 42 were waited for; matrix products, arithmetic and copies ran while one was open for 5% of the time, Pallas kernels for 20%

profile of v1, /device:TPU:24, one launch (start us, length us, event | category | flops | bytes accessed | tf_op | source)
XLA Modules:
  0.0 665.6 jit_solution(2452899024542870993)
XLA Ops:
  26.4 9.5 %collective-permute-done.1 = bf16[2,4,32,704]{3,2,0,1:T(8,128)(2,1)S(1)} collective-permute-done((bf16[2,4,32,704]{3,2,0,1:T(8,128)(2,1)S(1)}, bf16[2,4,32,704]{3,2,0,1:T(8,128)(2,1)S(1)}, u32[]{:S(2)}, u32[]{:S(2)}) %collective-permute-start.1) | collective-permute-done | bytes 360480 | tf_op jit(solution)/shard_map/ppermute | solution.py:45
  35.9 10.9 %collective-permute-done.2 = bf16[2,4,32,704]{3,2,0,1:T(8,128)(2,1)S(1)} collective-permute-done((bf16[2,4,32,704]{3,2,0,1:T(8,128)(2,1)S(1)}, bf16[2,4,32,704]{3,2,0,1:T(8,128)(2,1)S(1)}, u32[]{:S(2)}, u32[]{:S(2)}) %collective-permute-start.2) | collective-permute-done | bytes 360480 | tf_op jit(solution)/shard_map/ppermute | solution.py:45
  46.9 12.6 %collective-permute-done.3 = bf16[2,4,32,704]{3,2,0,1:T(8,128)(2,1)S(1)} collective-permute-done((bf16[2,4,32,704]{3,2,0,1:T(8,128)(2,1)S(1)}, bf16[2,4,32,704]{3,2,0,1:T(8,128)(2,1)S(1)}, u32[]{:S(2)}, u32[]{:S(2)}) %collective-permute-start.3) | collective-permute-done | bytes 360480 | tf_op jit(solution)/shard_map/ppermute | solution.py:45
  70.2 8.0 %collective-permute-done.7.refs_3_ = bf16[8,32,576]{2,1,0:T(8,128)(2,1)S(1)} collective-permute-done((bf16[8,32,576]{2,1,0:T(8,128)(2,1)S(1)}, bf16[8,32,576]{2,1,0:T(8,128)(2,1)S(1)}, u32[]{:S(2)}, u32[]{:S(2)}) %collective-permute-start.7) | collective-permute-done | bytes 294944 | tf_op jit(solution)/shard_map/ppermute | solution.py:45
  78.2 7.1 %collective-permute-done.11.refs_7_ = bf16[8,32,576]{2,1,0:T(8,128)(2,1)S(1)} collective-permute-done((bf16[8,32,576]{2,1,0:T(8,128)(2,1)S(1)}, bf16[8,32,576]{2,1,0:T(8,128)(2,1)S(1)}, u32[]{:S(2)}, u32[]{:S(2)}) %collective-permute-start.11) | collective-permute-done | bytes 294944 | tf_op jit(solution)/shard_map/ppermute | solution.py:45
  90.1 13.6 %collective-permute-done.5.refs_1_ = bf16[8,32,576]{2,1,0:T(8,128)(2,1)S(1)} collective-permute-done((bf16[8,32,576]{2,1,0:T(8,128)(2,1)S(1)}, bf16[8,32,576]{2,1,0:T(8,128)(2,1)S(1)}, u32[]{:S(2)}, u32[]{:S(2)}) %collective-permute-start.5) | collective-permute-done | bytes 294944 | tf_op jit(solution)/shard_map/ppermute | solution.py:45
  104.6 6.2 collective-permute-done.9.refs_5_
  118.6 6.0 shard_map.214
  125.2 6.1 collective-permute-done.12
  133.7 5.6 shard_map.215
  139.4 4.9 copy.79
  148.0 8.9 %shard_map.218 = (bf16[256,256]{1,0:T(8,128)(2,1)S(1)}, bf16[128,2048]{1,0:T(8,128)(2,1)S(1)}, bf16[128,2048]{1,0:T(8,128)(2,1)S(1)}) custom-call(s32[8]{0:T(128)S(1)} %bitcast.167, s32[16]{0:T(128)S(1)} %select_reduce_fusion.1.key_slot, bf16[1024,256]{1,0:T(8,128)(2,1)S(1)} %get-tuple-element.98.q_ref.refs_0_, ...), custom_call_target="tpu_custom_call" | custom-call | flops 1000 | bytes 18000000 | tf_op jit(solution)/shard_map/pallas_call | solution.py:141
  157.5 4.5 shard_map.217
  163.8 5.8 collective-permute-start.15
  173.3 9.1 %collective-permute-done.15 = bf16[128,2048]{1,0:T(8,128)(2,1)S(1)} collective-permute-done((bf16[128,2048]{1,0:T(8,128)(2,1)S(1)}, bf16[128,2048]{1,0:T(8,128)(2,1)S(1)}, u32[]{:S(2)}, u32[]{:S(2)}) %collective-permute-start.15) | collective-permute-done | bytes 524320 | tf_op jit(solution)/shard_map/ppermute | solution.py:45
  182.4 5.8 shard_map.216
  188.3 4.6 collective-permute-done.20
  200.2 10.7 %collective-permute-done.21.refs_0_ = bf16[128,2048]{1,0:T(8,128)(2,1)} collective-permute-done((bf16[128,2048]{1,0:T(8,128)(2,1)S(1)}, bf16[128,2048]{1,0:T(8,128)(2,1)}, u32[]{:S(2)}, u32[]{:S(2)}) %collective-permute-start.21) | collective-permute-done | bytes 524320 | tf_op jit(solution)/shard_map/ppermute | solution.py:45
  210.9 10.2 %collective-permute-done.23.refs_2_ = bf16[128,2048]{1,0:T(8,128)(2,1)} collective-permute-done((bf16[128,2048]{1,0:T(8,128)(2,1)S(1)}, bf16[128,2048]{1,0:T(8,128)(2,1)}, u32[]{:S(2)}, u32[]{:S(2)}) %collective-permute-start.23) | collective-permute-done | bytes 524320 | tf_op jit(solution)/shard_map/ppermute | solution.py:45
  223.3 10.1 %shard_map.219 = bf16[3,2,8,128,704]{4,3,2,1,0:T(8,128)(2,1)} custom-call(s32[8]{0:T(128)S(1)} %copy-done.52, s32[2]{0:T(128)S(1)} %copy-done.49, bf16[4,8,3,32,704]{4,3,2,1,0:T(8,128)(2,1)} %bitcast.17.own_ref, bf16[4,8,3,32,704]{4,3,2,1,0:T(8,128)(2,1)} %collective-permute-done.25.other_ref), custom_call_target="tpu_custom_call" | custom-call | flops 1000 | bytes 18000000 | tf_op jit(solution)/shard_map/pallas_call | solution.py:141
  233.4 16.0 %shard_map.220 = (bf16[1024,704]{1,0:T(8,128)(2,1)S(1)}, bf16[1024,704]{1,0:T(8,128)(2,1)}, bf16[1024,704]{1,0:T(8,128)(2,1)}, bf16[128,2048]{1,0:T(8,128)(2,1)S...) custom-call(s32[8]{0:T(128)S(1)} %stack.219.chunk.nat, ...), custom_call_target="tpu_custom_call" | custom-call | flops 1000 | bytes 48000000 | tf_op jit(solution)/shard_map/pallas_call | solution.py:141
  250.0 16.0 %shard_map.221 = (bf16[1024,704]{1,0:T(8,128)(2,1)S(1)}, bf16[1024,704]{1,0:T(8,128)(2,1)}, bf16[1024,704]{1,0:T(8,128)(2,1)}, bf16[128,2048]{1,0:T(8,128)(2,1)S...) custom-call(s32[8]{0:T(128)S(1)} %stack.219.chunk.nat, ...), custom_call_target="tpu_custom_call", output_to_operand_aliasing={{0}: (10, {}), {1}: (11, {}), {2}: (12, {})} | custom-call | flops 1000 | bytes 48000000 | tf_op jit(solution)/shard_map/pallas_call | solution.py:141
  275.3 9.2 %collective-permute-done.35 = bf16[128,2048]{1,0:T(8,128)(2,1)} collective-permute-done((bf16[128,2048]{1,0:T(8,128)(2,1)}, bf16[128,2048]{1,0:T(8,128)(2,1)}, u32[]{:S(2)}, u32[]{:S(2)}) %collective-permute-start.35) | collective-permute-done | bytes 524320 | tf_op jit(solution)/shard_map/ppermute | solution.py:45
  284.5 9.1 %collective-permute-done.32 = bf16[128,2048]{1,0:T(8,128)(2,1)} collective-permute-done((bf16[128,2048]{1,0:T(8,128)(2,1)}, bf16[128,2048]{1,0:T(8,128)(2,1)}, u32[]{:S(2)}, u32[]{:S(2)}) %collective-permute-start.32) | collective-permute-done | bytes 524320 | tf_op jit(solution)/shard_map/ppermute | solution.py:45
  298.3 19.7 %shard_map.222 = (bf16[4,4,2,2,3,16,704]{6,5,4,3,2,1,0:T(8,128)(2,1)}, bf16[4,2,2,3,16,704]{5,4,3,2,1,0:T(8,128)(2,1)S(1)}, bf16[4,2,2,3,16,704]{5,4,3,2,1,0:T(8...) custom-call(s32[8]{0:T(128)S(1)} %copy-done.53, s32[4]{0:T(128)S(1)} %pad_add_fusion.1.xs, ...), custom_call_target="tpu_custom_call" | custom-call | flops 1000 | bytes 51000000 | tf_op jit(solution)/shard_map/pallas_call | solution.py:141
  326.7 12.7 %collective-permute-done.36.refs_1_.refs_14_ = bf16[128,2048]{1,0:T(8,128)(2,1)S(1)} collective-permute-done((bf16[128,2048]{1,0:T(8,128)(2,1)S(1)}, bf16[128,2048]{1,0:T(8,128)(2,1)S(1)}, u32[]{:S(2)}, u32[]{:S(2)}) %collective-permute-start.36) | collective-permute-done | bytes 524320 | tf_op jit(solution)/shard_map/ppermute | solution.py:45
  351.2 6.5 collective-permute-done.46.refs_1_.refs_10_
  369.1 7.7 %shard_map.223 = (bf16[256,256]{1,0:T(8,128)(2,1)S(1)}, f32[2048,64]{1,0:T(8,128)S(1)}, f32[2048,64]{1,0:T(8,128)S(1)}) custom-call(s32[8]{0:T(128)S(1)} %bitcast.170, s32[16]{0:T(128)S(1)} %select_reduce_fusion.1.key_slot, s32[1]{0:T(128)} %bitcast.16.core, s32[16]{0:T(128)S(1)} %copy-done.40, bf16[1024,256]{1,0:T(8,128)(2,1)S(1)} %get-tuple-element.98.q_ref.refs_0_, ...), custom_call_target="tpu_custom_call" | custom-call | flops 1000 | bytes 24000000 | tf_op jit(solution)/shard_map/pallas_call | solution.py:141
  378.8 20.2 %shard_map.224 = (bf16[512,256]{1,0:T(8,128)(2,1)S(1)}, f32[2048,64]{1,0:T(8,128)S(1)}, f32[2048,64]{1,0:T(8,128)}) custom-call(s32[8]{0:T(128)S(1)} %bitcast.171, s32[16]{0:T(128)S(1)} %select_reduce_fusion.1.key_slot, s32[1]{0:T(128)} %bitcast.16.core, s32[16]{0:T(128)S(1)} %copy-done.41, bf16[1024,256]{1,0:T(8,128)(2,1)S(1)} %get-tuple-element.98.q_ref.refs_0_, ...), custom_call_target="tpu_custom_call" | custom-call | flops 1000 | bytes 48000000 | tf_op jit(solution)/shard_map/pallas_call | solution.py:141
  399.0 7.8 %shard_map.225 = (bf16[256,256]{1,0:T(8,128)(2,1)S(1)}, bf16[2048,64]{1,0:T(8,128)(2,1)S(1)}, bf16[2048,64]{1,0:T(8,128)(2,1)S(1)}) custom-call(s32[8]{0:T(128)S(1)} %bitcast.172, s32[16]{0:T(128)S(1)} %select_reduce_fusion.1.key_slot, s32[1]{0:T(128)} %bitcast.16.core, s32[16]{0:T(128)S(1)} %copy-done.41, ...), custom_call_target="tpu_custom_call" | custom-call | flops 1000 | bytes 24000000 | tf_op jit(solution)/shard_map/pallas_call | solution.py:141
  408.6 4.8 collective-permute-start.95
  418.6 18.2 %collective-permute-done.95 = bf16[4,2,2,3,16,704]{5,4,3,2,1,0:T(8,128)(2,1)S(1)} collective-permute-done((bf16[4,2,2,3,16,704]{5,4,3,2,1,0:T(8,128)(2,1)S(1)}, bf16[4,2,2,3,16,704]{5,4,3,2,1,0:T(8,128)(2,1)S(1)}, u32[]{:S(2)}, u32[]{:S(2)}) %collective-permute-start.95) | collective-permute-done | bytes 1081376 | tf_op jit(solution)/shard_map/ppermute | solution.py:45
  439.8 11.3 %shard_map.227 = (bf16[4,2,2,16,576]{4,3,2,1,0:T(8,128)(2,1)S(1)}, bf16[4,2,2,16,576]{4,3,2,1,0:T(8,128)(2,1)S(1)}, bf16[4,2,2,16,576]{4,3,2,1,0:T(8,128)(2,1)S(...) custom-call(s32[8]{0:T(128)S(1)} %copy-done.54, ...), custom_call_target="tpu_custom_call" | custom-call | flops 1000 | bytes 30000000 | tf_op jit(solution)/shard_map/pallas_call | solution.py:141
  464.7 7.2 %collective-permute-start.96 = (bf16[2,2,3,16,704]{4,3,2,1,0:T(8,128)(2,1)S(1)}, bf16[2,2,3,16,704]{4,3,2,1,0:T(8,128)(2,1)S(1)}, u32[]{:S(2)}, u32[]{:S(2)}) collective-permute-start(bf16[2,2,3,16,704]{4,3,2,1,0:T(8,128)(2,1)S(1)} %get-tuple-element.197), channel_id=1, source_target_pairs={{0,32},{1,33},{2,34},{3,35},{4,36},{5,37},{6,38},{7,39},{8,40},{9,... | collective-permute-start | bytes 811016 | tf_op jit(solution)/shard_map/ppermute | solution.py:45
  474.0 7.5 %collective-permute-start.63 = (f32[2,2048]{1,0:T(2,128)S(1)}, f32[2,2048]{1,0:T(2,128)S(1)}, u32[]{:S(2)}, u32[]{:S(2)}) collective-permute-start(f32[2,2048]{1,0:T(2,128)S(1)} %add_add_fusion.2), channel_id=1, source_target_pairs={{0,64},{1,65},{2,66},{3,67},{4,68},{5,69},{6,70},{7,71},{8,72},{9,... | collective-permute-start | bytes 49160 | tf_op jit(solution)/shard_map/ppermute | solution.py:45
  487.5 4.5 collective-permute-start.66
  494.0 4.5 shard_map.226
  502.4 7.9 %collective-permute-done.77 = bf16[4,2,2,16,576]{4,3,2,1,0:T(8,128)(2,1)S(1)} collective-permute-done((bf16[4,2,2,16,576]{4,3,2,1,0:T(8,128)(2,1)S(1)}, bf16[4,2,2,16,576]{4,3,2,1,0:T(8,128)(2,1)S(1)}, u32[]{:S(2)}, u32[]{:S(2)}) %collective-permute-start.77) | collective-permute-done | bytes 294944 | tf_op jit(solution)/shard_map/ppermute | solution.py:45
  512.0 6.1 collective-permute-done.76
  524.0 9.9 %collective-permute-done.58 = bf16[128,2048]{1,0:T(8,128)(2,1)S(1)} collective-permute-done((bf16[128,2048]{1,0:T(8,128)(2,1)S(1)}, bf16[128,2048]{1,0:T(8,128)(2,1)S(1)}, u32[]{:S(2)}, u32[]{:S(2)}) %collective-permute-start.58) | collective-permute-done | bytes 524320 | tf_op jit(solution)/shard_map/ppermute | solution.py:45
  533.9 9.8 %collective-permute-done.56 = bf16[128,2048]{1,0:T(8,128)(2,1)S(1)} collective-permute-done((bf16[128,2048]{1,0:T(8,128)(2,1)S(1)}, bf16[128,2048]{1,0:T(8,128)(2,1)S(1)}, u32[]{:S(2)}, u32[]{:S(2)}) %collective-permute-start.56) | collective-permute-done | bytes 524320 | tf_op jit(solution)/shard_map/ppermute | solution.py:45
  553.8 4.5 collective-permute-done.92
  560.0 4.9 collective-permute-done.91
  580.2 13.3 %collective-permute-done.103 = bf16[2,4,3,16,704]{4,3,2,1,0:T(8,128)(2,1)S(1)} collective-permute-done((bf16[2,4,3,16,704]{4,3,2,1,0:T(8,128)(2,1)S(1)}, bf16[2,4,3,16,704]{4,3,2,1,0:T(8,128)(2,1)S(1)}, u32[]{:S(2)}, u32[]{:S(2)}) %collective-permute-start.103) | collective-permute-done | bytes 540704 | tf_op jit(solution)/shard_map/ppermute | solution.py:45
  602.5 13.4 %collective-permute-done.104.refs_1_ = bf16[2,2,4,3,16,704]{5,4,3,2,1,0:T(8,128)(2,1)S(1)} collective-permute-done((bf16[2,2,4,3,16,704]{5,4,3,2,1,0:T(8,128)(2,1)S(1)}, bf16[2,2,4,3,16,704]{5,4,3,2,1,0:T(8,128)(2,1)S(1)}, u32[]{:S(2)}, u32[]{:S(2)}) %collective-permute-start.104) | collective-permute-done | bytes 1081376 | tf_op jit(solution)/shard_map/ppermute | solution.py:45
  632.1 14.9 %collective-permute-done.87.refs_1_ = bf16[2,2,4,16,576]{4,3,2,1,0:T(8,128)(2,1)S(1)} collective-permute-done((bf16[2,2,4,16,576]{4,3,2,1,0:T(8,128)(2,1)S(1)}, bf16[2,2,4,16,576]{4,3,2,1,0:T(8,128)(2,1)S(1)}, u32[]{:S(2)}, u32[]{:S(2)}) %collective-permute-start.87) | collective-permute-done | bytes 294944 | tf_op jit(solution)/shard_map/ppermute | solution.py:45
  647.0 4.7 collective-permute-done.89.refs_3_
  653.8 4.8 shard_map.229
  (458 shorter events, 212.4 us)
Async XLA Ops:
  7.2 109.6 %all-gather.5.cloned.1.call-start = ((), (), s32[]{:S(2)}) async-start(), calls=%async_computation.1 | async-start | bytes 4718592 | tf_op jit(solution)/shard_map/all_gather | solution.py:768
  11.9 127.5 %all-gather.9.cloned.1.call-start = ((), (), s32[]{:S(2)}) async-start(), calls=%async_computation.4 | async-start | bytes 5898240 | tf_op jit(solution)/shard_map/all_gather | solution.py:782
  22.2 24.6 %collective-permute-start.2 = (bf16[2,4,32,704]{3,2,0,1:T(8,128)(2,1)S(1)}, bf16[2,4,32,704]{3,2,0,1:T(8,128)(2,1)S(1)}, u32[]{:S(2)}, u32[]{:S(2)}) collective-permute-start(bf16[2,4,32,704]{3,2,0,1:T(8,128)(2,1)S(1)} %pad_maximum_fusion.3), channel_id=1, source_target_pairs={{0,6},{1,3},{2,0},{3,5},{4,2},{5,7},{6,4},{7,1},{8,14},{9,11},{10,... | collective-permute-start | bytes 1081352 | tf_op jit(solution)/shard_map/ppermute | solution.py:45
  24.5 35.0 %collective-permute-start.3 = (bf16[2,4,32,704]{3,2,0,1:T(8,128)(2,1)S(1)}, bf16[2,4,32,704]{3,2,0,1:T(8,128)(2,1)S(1)}, u32[]{:S(2)}, u32[]{:S(2)}) collective-permute-start(bf16[2,4,32,704]{3,2,0,1:T(8,128)(2,1)S(1)} %pad_maximum_fusion.4), channel_id=1, source_target_pairs={{0,4},{1,5},{2,6},{3,7},{4,0},{5,1},{6,2},{7,3},{8,12},{9,13},{10,... | collective-permute-start | bytes 1081352 | tf_op jit(solution)/shard_map/ppermute | solution.py:45
  60.6 172.8 %all-gather.7.cloned.1.call-start = ((), (), s32[]{:S(2)}) async-start(), calls=%async_computation.2 | async-start | bytes 4718592 | tf_op jit(solution)/shard_map/all_gather | solution.py:785
  85.3 461.8 %reduce-scatter.2.cloned.1.call-start = ((), (), s32[]{:S(2)}) async-start(), calls=%async_computation.3 | async-start | bytes 5898240 | tf_op jit(solution)/shard_map/reduce_scatter | solution.py:835
  85.3 18.4 %collective-permute-start.5 = (bf16[8,32,576]{2,1,0:T(8,128)(2,1)S(1)}, bf16[8,32,576]{2,1,0:T(8,128)(2,1)S(1)}, u32[]{:S(2)}, u32[]{:S(2)}) collective-permute-start(bf16[8,32,576]{2,1,0:T(8,128)(2,1)S(1)} %pad_maximum_fusion.5.refs_0_), channel_id=1, source_target_pairs={{0,16},{1,49},{2,18},{3,51},{4,20},{5,53},{6,22},{7,55},{8,24},{9,... | collective-permute-start | bytes 884744 | tf_op jit(solution)/shard_map/ppermute | solution.py:45
  85.7 18.6 %collective-permute-start.6 = (bf16[8,32,576]{2,1,0:T(8,128)(2,1)S(1)}, bf16[8,32,576]{2,1,0:T(8,128)(2,1)S(1)}, u32[]{:S(2)}, u32[]{:S(2)}) collective-permute-start(bf16[8,32,576]{2,1,0:T(8,128)(2,1)S(1)} %pad_maximum_fusion.5.refs_0_), channel_id=1, source_target_pairs={{0,48},{1,17},{2,50},{3,19},{4,52},{5,21},{6,54},{7,23},{8,56},{9,... | collective-permute-start | bytes 884744 | tf_op jit(solution)/shard_map/ppermute | solution.py:45
  139.3 23.3 %collective-permute-start.14 = (bf16[128,2048]{1,0:T(8,128)(2,1)}, bf16[128,2048]{1,0:T(8,128)(2,1)}, u32[]{:S(2)}, u32[]{:S(2)}) collective-permute-start(bf16[128,2048]{1,0:T(8,128)(2,1)} %get-tuple-element.102), channel_id=1, source_target_pairs={{0,1},{1,0},{2,3},{3,2},{4,5},{5,4},{6,7},{7,6},{8,9},{9,8},{10,11... | collective-permute-start | bytes 1572872 | tf_op jit(solution)/shard_map/ppermute | solution.py:45
  144.4 77.7 %collective-permute-start.25 = (bf16[4,8,3,32,704]{4,3,2,1,0:T(8,128)(2,1)}, bf16[4,8,3,32,704]{4,3,2,1,0:T(8,128)(2,1)}, u32[]{:S(2)}, u32[]{:S(2)}) collective-permute-start(bf16[4,8,3,32,704]{4,3,2,1,0:T(8,128)(2,1)} %bitcast.17.own_ref), channel_id=1, source_target_pairs={{0,8},{1,73},{2,10},{3,75},{4,12},{5,77},{6,14},{7,79},{8,64},{9,1... | collective-permute-start | bytes 12976136 | tf_op jit(solution)/shard_map/ppermute | solution.py:45
  163.8 18.6 %collective-permute-start.15 = (bf16[128,2048]{1,0:T(8,128)(2,1)S(1)}, bf16[128,2048]{1,0:T(8,128)(2,1)S(1)}, u32[]{:S(2)}, u32[]{:S(2)}) collective-permute-start(bf16[128,2048]{1,0:T(8,128)(2,1)S(1)} %add_convert_fusion.12), channel_id=1, source_target_pairs={{0,4},{1,5},{2,6},{3,7},{4,0},{5,1},{6,2},{7,3},{8,12},{9,13},{10,... | collective-permute-start | bytes 1572872 | tf_op jit(solution)/shard_map/ppermute | solution.py:45
  169.7 23.2 %collective-permute-start.20 = (bf16[128,2048]{1,0:T(8,128)(2,1)S(1)}, bf16[128,2048]{1,0:T(8,128)(2,1)S(1)}, u32[]{:S(2)}, u32[]{:S(2)}) collective-permute-start(bf16[128,2048]{1,0:T(8,128)(2,1)S(1)} %add_convert_fusion.10), channel_id=1, source_target_pairs={{0,2},{1,7},{2,4},{3,1},{4,6},{5,3},{6,0},{7,5},{8,10},{9,15},{10,... | collective-permute-start | bytes 1572872 | tf_op jit(solution)/shard_map/ppermute | solution.py:45
  170.0 23.0 %collective-permute-start.18 = (bf16[128,2048]{1,0:T(8,128)(2,1)S(1)}, bf16[128,2048]{1,0:T(8,128)(2,1)S(1)}, u32[]{:S(2)}, u32[]{:S(2)}) collective-permute-start(bf16[128,2048]{1,0:T(8,128)(2,1)S(1)} %add_convert_fusion.11), channel_id=1, source_target_pairs={{0,6},{1,3},{2,0},{3,5},{4,2},{5,7},{6,4},{7,1},{8,14},{9,11},{10,... | collective-permute-start | bytes 1572872 | tf_op jit(solution)/shard_map/ppermute | solution.py:45
  196.9 24.2 %collective-permute-start.23 = (bf16[128,2048]{1,0:T(8,128)(2,1)S(1)}, bf16[128,2048]{1,0:T(8,128)(2,1)}, u32[]{:S(2)}, u32[]{:S(2)}) collective-permute-start(bf16[128,2048]{1,0:T(8,128)(2,1)S(1)} %multiply_convert_fusion.refs_2_.refs_6_), channel_id=1, source_target_pairs={{0,2},{1,7},{2,4},{3,1},{4,6},{5,3},{6,0},{7,5},{8,10},{9,15},{10,... | collective-permute-start | bytes 1572872 | tf_op jit(solution)/shard_map/ppermute | solution.py:45
  196.9 24.7 %collective-permute-start.28 = (bf16[128,2048]{1,0:T(8,128)(2,1)S(1)}, bf16[128,2048]{1,0:T(8,128)(2,1)}, u32[]{:S(2)}, u32[]{:S(2)}) collective-permute-start(bf16[128,2048]{1,0:T(8,128)(2,1)S(1)} %multiply_convert_fusion.refs_2_.refs_6_), channel_id=1, source_target_pairs={{0,6},{1,3},{2,0},{3,5},{4,2},{5,7},{6,4},{7,1},{8,14},{9,11},{10,... | collective-permute-start | bytes 1572872 | tf_op jit(solution)/shard_map/ppermute | solution.py:45
  210.9 22.5 %collective-permute-start.22 = (bf16[128,2048]{1,0:T(8,128)(2,1)}, bf16[128,2048]{1,0:T(8,128)(2,1)}, u32[]{:S(2)}, u32[]{:S(2)}) collective-permute-start(bf16[128,2048]{1,0:T(8,128)(2,1)} %collective-permute-done.21.refs_0_), channel_id=1, source_target_pairs={{0,1},{1,0},{2,3},{3,2},{4,5},{5,4},{6,7},{7,6},{8,9},{9,8},{10,11... | collective-permute-start | bytes 1572872 | tf_op jit(solution)/shard_map/ppermute | solution.py:45
  221.1 28.9 %collective-permute-start.30 = (bf16[128,2048]{1,0:T(8,128)(2,1)S(1)}, bf16[128,2048]{1,0:T(8,128)(2,1)}, u32[]{:S(2)}, u32[]{:S(2)}) collective-permute-start(bf16[128,2048]{1,0:T(8,128)(2,1)S(1)} %multiply_convert_fusion.refs_2_.refs_6_), channel_id=1, source_target_pairs={{0,1},{1,0},{2,3},{3,2},{4,5},{5,4},{6,7},{7,6},{8,9},{9,8},{10,11... | collective-permute-start | bytes 1572872 | tf_op jit(solution)/shard_map/ppermute | solution.py:45
  221.6 28.4 %collective-permute-start.29 = (bf16[128,2048]{1,0:T(8,128)(2,1)}, bf16[128,2048]{1,0:T(8,128)(2,1)}, u32[]{:S(2)}, u32[]{:S(2)}) collective-permute-start(bf16[128,2048]{1,0:T(8,128)(2,1)} %collective-permute-done.28.refs_0_.refs_4_), channel_id=1, source_target_pairs={{0,1},{1,0},{2,3},{3,2},{4,5},{5,4},{6,7},{7,6},{8,9},{9,8},{10,11... | collective-permute-start | bytes 1572872 | tf_op jit(solution)/shard_map/ppermute | solution.py:45
  249.4 17.2 %collective-permute-start.26 = (bf16[128,2048]{1,0:T(8,128)(2,1)S(1)}, bf16[128,2048]{1,0:T(8,128)(2,1)S(1)}, u32[]{:S(2)}, u32[]{:S(2)}) collective-permute-start(bf16[128,2048]{1,0:T(8,128)(2,1)S(1)} %get-tuple-element.112), channel_id=1, source_target_pairs={{0,1},{1,0},{2,3},{3,2},{4,5},{5,4},{6,7},{7,6},{8,9},{9,8},{10,11... | collective-permute-start | bytes 1572872 | tf_op jit(solution)/shard_map/ppermute | solution.py:45
  249.9 20.8 %collective-permute-start.27 = (bf16[128,2048]{1,0:T(8,128)(2,1)S(1)}, bf16[128,2048]{1,0:T(8,128)(2,1)S(1)}, u32[]{:S(2)}, u32[]{:S(2)}) collective-permute-start(bf16[128,2048]{1,0:T(8,128)(2,1)S(1)} %get-tuple-element.114), channel_id=1, source_target_pairs={{0,1},{1,0},{2,3},{3,2},{4,5},{5,4},{6,7},{7,6},{8,9},{9,8},{10,11... | collective-permute-start | bytes 1572872 | tf_op jit(solution)/shard_map/ppermute | solution.py:45
  266.5 27.1 %collective-permute-start.31 = (bf16[128,2048]{1,0:T(8,128)(2,1)}, bf16[128,2048]{1,0:T(8,128)(2,1)}, u32[]{:S(2)}, u32[]{:S(2)}) collective-permute-start(bf16[128,2048]{1,0:T(8,128)(2,1)} %get-tuple-element.121), channel_id=1, source_target_pairs={{0,1},{1,0},{2,3},{3,2},{4,5},{5,4},{6,7},{7,6},{8,9},{9,8},{10,11... | collective-permute-start | bytes 1572872 | tf_op jit(solution)/shard_map/ppermute | solution.py:45
  271.7 22.0 %collective-permute-start.32 = (bf16[128,2048]{1,0:T(8,128)(2,1)}, bf16[128,2048]{1,0:T(8,128)(2,1)}, u32[]{:S(2)}, u32[]{:S(2)}) collective-permute-start(bf16[128,2048]{1,0:T(8,128)(2,1)} %fusion.26), channel_id=1, source_target_pairs={{0,6},{1,3},{2,0},{3,5},{4,2},{5,7},{6,4},{7,1},{8,14},{9,11},{10,... | collective-permute-start | bytes 1572872 | tf_op jit(solution)/shard_map/ppermute | solution.py:45
  274.1 21.1 %collective-permute-start.34 = (bf16[128,2048]{1,0:T(8,128)(2,1)}, bf16[128,2048]{1,0:T(8,128)(2,1)}, u32[]{:S(2)}, u32[]{:S(2)}) collective-permute-start(bf16[128,2048]{1,0:T(8,128)(2,1)} %add_convert_fusion.9), channel_id=1, source_target_pairs={{0,2},{1,7},{2,4},{3,1},{4,6},{5,3},{6,0},{7,5},{8,10},{9,15},{10,... | collective-permute-start | bytes 1572872 | tf_op jit(solution)/shard_map/ppermute | solution.py:45
  357.7 49.2 %collective-permute-start.94 = (bf16[4,2,2,3,16,704]{5,4,3,2,1,0:T(8,128)(2,1)}, bf16[4,2,2,3,16,704]{5,4,3,2,1,0:T(8,128)(2,1)}, u32[]{:S(2)}, u32[]{:S(2)}) collective-permute-start(bf16[4,2,2,3,16,704]{5,4,3,2,1,0:T(8,128)(2,1)} %get-tuple-element.172), channel_id=1, source_target_pairs={{0,8},{1,73},{2,10},{3,75},{4,12},{5,77},{6,14},{7,79},{8,64},{9,1... | collective-permute-start | bytes 3244040 | tf_op jit(solution)/shard_map/ppermute | solution.py:45
  359.5 53.9 %collective-permute-start.38 = (bf16[128,2048]{1,0:T(8,128)(2,1)}, bf16[128,2048]{1,0:T(8,128)(2,1)}, u32[]{:S(2)}, u32[]{:S(2)}) collective-permute-start(bf16[128,2048]{1,0:T(8,128)(2,1)} %get-tuple-element.187), channel_id=1, source_target_pairs={{0,1},{1,0},{2,3},{3,2},{4,5},{5,4},{6,7},{7,6},{8,9},{9,8},{10,11... | collective-permute-start | bytes 1572872 | tf_op jit(solution)/shard_map/ppermute | solution.py:45
  362.2 51.2 %collective-permute-start.44 = (bf16[128,2048]{1,0:T(8,128)(2,1)}, bf16[128,2048]{1,0:T(8,128)(2,1)}, u32[]{:S(2)}, u32[]{:S(2)}) collective-permute-start(bf16[128,2048]{1,0:T(8,128)(2,1)} %get-tuple-element.192), channel_id=1, source_target_pairs={{0,2},{1,7},{2,4},{3,1},{4,6},{5,3},{6,0},{7,5},{8,10},{9,15},{10,... | collective-permute-start | bytes 1572872 | tf_op jit(solution)/shard_map/ppermute | solution.py:45
  363.2 50.2 %collective-permute-start.42 = (bf16[128,2048]{1,0:T(8,128)(2,1)}, bf16[128,2048]{1,0:T(8,128)(2,1)}, u32[]{:S(2)}, u32[]{:S(2)}) collective-permute-start(bf16[128,2048]{1,0:T(8,128)(2,1)} %get-tuple-element.193), channel_id=1, source_target_pairs={{0,6},{1,3},{2,0},{3,5},{4,2},{5,7},{6,4},{7,1},{8,14},{9,11},{10,... | collective-permute-start | bytes 1572872 | tf_op jit(solution)/shard_map/ppermute | solution.py:45
  367.1 46.4 %collective-permute-start.40 = (bf16[128,2048]{1,0:T(8,128)(2,1)}, bf16[128,2048]{1,0:T(8,128)(2,1)}, u32[]{:S(2)}, u32[]{:S(2)}) collective-permute-start(bf16[128,2048]{1,0:T(8,128)(2,1)} %get-tuple-element.191), channel_id=1, source_target_pairs={{0,4},{1,5},{2,6},{3,7},{4,0},{5,1},{6,2},{7,3},{8,12},{9,13},{10,... | collective-permute-start | bytes 1572872 | tf_op jit(solution)/shard_map/ppermute | solution.py:45
  408.6 28.2 %collective-permute-start.95 = (bf16[4,2,2,3,16,704]{5,4,3,2,1,0:T(8,128)(2,1)S(1)}, bf16[4,2,2,3,16,704]{5,4,3,2,1,0:T(8,128)(2,1)S(1)}, u32[]{:S(2)}, u32[]{:S(2)}) collective-permute-start(bf16[4,2,2,3,16,704]{5,4,3,2,1,0:T(8,128)(2,1)S(1)} %add_convert_fusion.1), channel_id=1, source_target_pairs={{0,8},{1,73},{2,10},{3,75},{4,12},{5,77},{6,14},{7,79},{8,64},{9,1... | collective-permute-start | bytes 3244040 | tf_op jit(solution)/shard_map/ppermute | solution.py:45
  416.4 38.2 %collective-permute-start.93 = (bf16[4,2,2,3,16,704]{5,4,3,2,1,0:T(8,128)(2,1)S(1)}, bf16[4,2,2,3,16,704]{5,4,3,2,1,0:T(8,128)(2,1)S(1)}, u32[]{:S(2)}, u32[]{:S(2)}) collective-permute-start(bf16[4,2,2,3,16,704]{5,4,3,2,1,0:T(8,128)(2,1)S(1)} %copy-done.76), channel_id=1, source_target_pairs={{0,72},{1,9},{2,74},{3,11},{4,76},{5,13},{6,78},{7,15},{8,0},{9,65... | collective-permute-start | bytes 3244040 | tf_op jit(solution)/shard_map/ppermute | solution.py:45
  418.6 21.1 %collective-permute-start.51 = (bf16[1024,64]{1,0:T(8,128)(2,1)S(1)}, bf16[1024,64]{1,0:T(8,128)(2,1)S(1)}, u32[]{:S(2)}, u32[]{:S(2)}) collective-permute-start(bf16[1024,64]{1,0:T(8,128)(2,1)S(1)} %slice.409), channel_id=1, source_target_pairs={{0,8},{1,9},{2,10},{3,11},{4,12},{5,13},{6,14},{7,15},{8,0},{9,1},... | collective-permute-start | bytes 393224 | tf_op jit(solution)/shard_map/ppermute | solution.py:45
  461.3 20.3 %collective-permute-start.97 = (bf16[2,2,3,16,704]{4,3,2,1,0:T(8,128)(2,1)S(1)}, bf16[2,2,3,16,704]{4,3,2,1,0:T(8,128)(2,1)S(1)}, u32[]{:S(2)}, u32[]{:S(2)}) collective-permute-start(bf16[2,2,3,16,704]{4,3,2,1,0:T(8,128)(2,1)S(1)} %get-tuple-element.199), channel_id=1, source_target_pairs={{0,48},{1,17},{2,50},{3,19},{4,52},{5,21},{6,54},{7,23},{8,56},{9,... | collective-permute-start | bytes 811016 | tf_op jit(solution)/shard_map/ppermute | solution.py:45
  464.7 18.8 %collective-permute-start.96 = (bf16[2,2,3,16,704]{4,3,2,1,0:T(8,128)(2,1)S(1)}, bf16[2,2,3,16,704]{4,3,2,1,0:T(8,128)(2,1)S(1)}, u32[]{:S(2)}, u32[]{:S(2)}) collective-permute-start(bf16[2,2,3,16,704]{4,3,2,1,0:T(8,128)(2,1)S(1)} %get-tuple-element.197), channel_id=1, source_target_pairs={{0,32},{1,33},{2,34},{3,35},{4,36},{5,37},{6,38},{7,39},{8,40},{9,... | collective-permute-start | bytes 811016 | tf_op jit(solution)/shard_map/ppermute | solution.py:45
  500.4 17.7 %collective-permute-start.76 = (bf16[4,2,2,16,576]{4,3,2,1,0:T(8,128)(2,1)S(1)}, bf16[4,2,2,16,576]{4,3,2,1,0:T(8,128)(2,1)S(1)}, u32[]{:S(2)}, u32[]{:S(2)}) collective-permute-start(bf16[4,2,2,16,576]{4,3,2,1,0:T(8,128)(2,1)S(1)} %get-tuple-element.160), channel_id=1, source_target_pairs={{0,72},{1,9},{2,74},{3,11},{4,76},{5,13},{6,78},{7,15},{8,0},{9,65... | collective-permute-start | bytes 884744 | tf_op jit(solution)/shard_map/ppermute | solution.py:45
  502.2 18.8 %collective-permute-start.71 = (bf16[4,2,2,16,576]{4,3,2,1,0:T(8,128)(2,1)S(1)}, bf16[4,2,2,16,576]{4,3,2,1,0:T(8,128)(2,1)S(1)}, u32[]{:S(2)}, u32[]{:S(2)}) collective-permute-start(bf16[4,2,2,16,576]{4,3,2,1,0:T(8,128)(2,1)S(1)} %get-tuple-element.156), channel_id=1, source_target_pairs={{0,16},{1,49},{2,18},{3,51},{4,20},{5,53},{6,22},{7,55},{8,24},{9,... | collective-permute-start | bytes 884744 | tf_op jit(solution)/shard_map/ppermute | solution.py:45
  521.0 22.7 %collective-permute-start.56 = (bf16[128,2048]{1,0:T(8,128)(2,1)S(1)}, bf16[128,2048]{1,0:T(8,128)(2,1)S(1)}, u32[]{:S(2)}, u32[]{:S(2)}) collective-permute-start(bf16[128,2048]{1,0:T(8,128)(2,1)S(1)} %add_convert_fusion.3), channel_id=1, source_target_pairs={{0,6},{1,3},{2,0},{3,5},{4,2},{5,7},{6,4},{7,1},{8,14},{9,11},{10,... | collective-permute-start | bytes 1572872 | tf_op jit(solution)/shard_map/ppermute | solution.py:45
  522.1 24.3 %collective-permute-start.54 = (bf16[128,2048]{1,0:T(8,128)(2,1)S(1)}, bf16[128,2048]{1,0:T(8,128)(2,1)S(1)}, u32[]{:S(2)}, u32[]{:S(2)}) collective-permute-start(bf16[128,2048]{1,0:T(8,128)(2,1)S(1)} %add_convert_fusion.4), channel_id=1, source_target_pairs={{0,4},{1,5},{2,6},{3,7},{4,0},{5,1},{6,2},{7,3},{8,12},{9,13},{10,... | collective-permute-start | bytes 1572872 | tf_op jit(solution)/shard_map/ppermute | solution.py:45
  550.4 23.1 %collective-permute-start.80 = (bf16[2,2,16,576]{3,2,1,0:T(8,128)(2,1)S(1)}, bf16[2,2,16,576]{3,2,1,0:T(8,128)(2,1)S(1)}, u32[]{:S(2)}, u32[]{:S(2)}) collective-permute-start(bf16[2,2,16,576]{3,2,1,0:T(8,128)(2,1)S(1)} %get-tuple-element.216), channel_id=1, source_target_pairs={{0,16},{1,49},{2,18},{3,51},{4,20},{5,53},{6,22},{7,55},{8,24},{9,... | collective-permute-start | bytes 221192 | tf_op jit(solution)/shard_map/ppermute | solution.py:45
  552.5 21.9 %collective-permute-start.79 = (bf16[2,2,16,576]{3,2,1,0:T(8,128)(2,1)S(1)}, bf16[2,2,16,576]{3,2,1,0:T(8,128)(2,1)S(1)}, u32[]{:S(2)}, u32[]{:S(2)}) collective-permute-start(bf16[2,2,16,576]{3,2,1,0:T(8,128)(2,1)S(1)} %get-tuple-element.217), channel_id=1, source_target_pairs={{0,48},{1,17},{2,50},{3,19},{4,52},{5,21},{6,54},{7,23},{8,56},{9,... | collective-permute-start | bytes 221192 | tf_op jit(solution)/shard_map/ppermute | solution.py:45
  576.4 17.2 %collective-permute-start.103 = (bf16[2,4,3,16,704]{4,3,2,1,0:T(8,128)(2,1)S(1)}, bf16[2,4,3,16,704]{4,3,2,1,0:T(8,128)(2,1)S(1)}, u32[]{:S(2)}, u32[]{:S(2)}) collective-permute-start(bf16[2,4,3,16,704]{4,3,2,1,0:T(8,128)(2,1)S(1)} %get-tuple-element.209), channel_id=1, source_target_pairs={{0,64},{1,65},{2,66},{3,67},{4,68},{5,69},{6,70},{7,71},{8,72},{9,... | collective-permute-start | bytes 1622024 | tf_op jit(solution)/shard_map/ppermute | solution.py:45
  579.6 22.2 %collective-permute-start.84 = (bf16[2,16,320]{2,1,0:T(8,128)(2,1)S(1)}, bf16[2,16,320]{2,1,0:T(8,128)(2,1)S(1)}, u32[]{:S(2)}, u32[]{:S(2)}) collective-permute-start(bf16[2,16,320]{2,1,0:T(8,128)(2,1)S(1)} %get-tuple-element.237), channel_id=1, source_target_pairs={{0,4},{1,5},{2,6},{3,7},{4,0},{5,1},{6,2},{7,3},{8,12},{9,13},{10,... | collective-permute-start | bytes 61448 | tf_op jit(solution)/shard_map/ppermute | solution.py:45
  593.7 22.3 %collective-permute-start.104 = (bf16[2,2,4,3,16,704]{5,4,3,2,1,0:T(8,128)(2,1)S(1)}, bf16[2,2,4,3,16,704]{5,4,3,2,1,0:T(8,128)(2,1)S(1)}, u32[]{:S(2)}, u32[]{:S(2)}) collective-permute-start(bf16[2,2,4,3,16,704]{5,4,3,2,1,0:T(8,128)(2,1)S(1)} %pad_maximum_fusion.refs_0_), channel_id=1, source_target_pairs={{0,16},{1,49},{2,18},{3,51},{4,20},{5,53},{6,22},{7,55},{8,24},{9,... | collective-permute-start | bytes 3244040 | tf_op jit(solution)/shard_map/ppermute | solution.py:45
  598.6 18.9 %collective-permute-start.81 = (bf16[4,2,16,256]{3,2,1,0:T(8,128)(2,1)S(1)}, bf16[4,2,16,256]{3,2,1,0:T(8,128)(2,1)S(1)}, u32[]{:S(2)}, u32[]{:S(2)}) collective-permute-start(bf16[4,2,16,256]{3,2,1,0:T(8,128)(2,1)S(1)} %pad_maximum_fusion.10), channel_id=1, source_target_pairs={{0,0},{1,2},{2,4},{3,6},{4,8},{5,10},{6,12},{7,14},{8,1},{9,3},{10... | collective-permute-start | bytes 196616 | tf_op jit(solution)/shard_map/ppermute | solution.py:45
  602.0 51.8 %collective-permute-start.105 = (bf16[2,2,4,3,16,704]{5,4,3,2,1,0:T(8,128)(2,1)S(1)}, bf16[2,2,4,3,16,704]{5,4,3,2,1,0:T(8,128)(2,1)S(1)}, u32[]{:S(2)}, u32[]{:S(2)}) collective-permute-start(bf16[2,2,4,3,16,704]{5,4,3,2,1,0:T(8,128)(2,1)S(1)} %pad_maximum_fusion.refs_0_), channel_id=1, source_target_pairs={{0,48},{1,17},{2,50},{3,19},{4,52},{5,21},{6,54},{7,23},{8,56},{9,... | collective-permute-start | bytes 3244040 | tf_op jit(solution)/shard_map/ppermute | solution.py:45
  615.9 37.9 %collective-permute-start.106 = (bf16[2,2,4,3,16,704]{5,4,3,2,1,0:T(8,128)(2,1)S(1)}, bf16[2,2,4,3,16,704]{5,4,3,2,1,0:T(8,128)(2,1)S(1)}, u32[]{:S(2)}, u32[]{:S(2)}) collective-permute-start(bf16[2,2,4,3,16,704]{5,4,3,2,1,0:T(8,128)(2,1)S(1)} %collective-permute-done.104.refs_1_), channel_id=1, source_target_pairs={{0,16},{1,49},{2,18},{3,51},{4,20},{5,53},{6,22},{7,55},{8,24},{9,... | collective-permute-start | bytes 3244040 | tf_op jit(solution)/shard_map/ppermute | solution.py:45
  625.7 21.3 %collective-permute-start.87 = (bf16[2,2,4,16,576]{4,3,2,1,0:T(8,128)(2,1)S(1)}, bf16[2,2,4,16,576]{4,3,2,1,0:T(8,128)(2,1)S(1)}, u32[]{:S(2)}, u32[]{:S(2)}) collective-permute-start(bf16[2,2,4,16,576]{4,3,2,1,0:T(8,128)(2,1)S(1)} %pad_maximum_fusion.6.refs_0_), channel_id=1, source_target_pairs={{0,16},{1,49},{2,18},{3,51},{4,20},{5,53},{6,22},{7,55},{8,24},{9,... | collective-permute-start | bytes 884744 | tf_op jit(solution)/shard_map/ppermute | solution.py:45
  626.2 20.7 %collective-permute-start.88 = (bf16[2,2,4,16,576]{4,3,2,1,0:T(8,128)(2,1)S(1)}, bf16[2,2,4,16,576]{4,3,2,1,0:T(8,128)(2,1)S(1)}, u32[]{:S(2)}, u32[]{:S(2)}) collective-permute-start(bf16[2,2,4,16,576]{4,3,2,1,0:T(8,128)(2,1)S(1)} %pad_maximum_fusion.6.refs_0_), channel_id=1, source_target_pairs={{0,48},{1,17},{2,50},{3,19},{4,52},{5,21},{6,54},{7,23},{8,56},{9,... | collective-permute-start | bytes 884744 | tf_op jit(solution)/shard_map/ppermute | solution.py:45
  629.0 22.7 %collective-permute-start.89 = (bf16[2,2,4,16,576]{4,3,2,1,0:T(8,128)(2,1)S(1)}, bf16[2,2,4,16,576]{4,3,2,1,0:T(8,128)(2,1)S(1)}, u32[]{:S(2)}, u32[]{:S(2)}) collective-permute-start(bf16[2,2,4,16,576]{4,3,2,1,0:T(8,128)(2,1)S(1)} %pad_maximum_fusion.6.refs_0_), channel_id=1, source_target_pairs={{0,32},{1,33},{2,34},{3,35},{4,36},{5,37},{6,38},{7,39},{8,40},{9,... | collective-permute-start | bytes 884744 | tf_op jit(solution)/shard_map/ppermute | solution.py:45
  (140 other events, 1773.2 us)
Sparse Core Ops, SparseCore 0:
  12.1 49.0 all-gather.4
  63.4 59.9 all-gather.8
  125.2 34.2 all-gather.6
  367.5 51.7 reduce-scatter.1

commit v2 on v1

--- a/solution.py
+++ b/solution.py
@@ -100,19 +100,12 @@
     return add(own, *got)
 
 
-def sum_all(value):
-    value = value + swap(value)
-    for axis in ("z", "y", "x"):
-        value = (value + across(value, axis)) + (step(value, axis, 1) + step(value, axis, -1))
-    return value
-
-
 def exchange_z(own, before, after, far):
     return own, step(after, "z", 1), step(before, "z", -1), across(far, "z")
 
 
 def after(value, *others):
-    return lax.optimization_barrier((value,) + others)[0]
+    return lax.optimization_barrier((value, others))[0]
 
 
 def rms_scale(rows):
@@ -145,7 +138,7 @@
         ),
         out_shape=out_shape,
         compiler_params=pltpu.CompilerParams(vmem_limit_bytes=VMEM_MIB * MIB),
-        cost_estimate=pl.CostEstimate(flops=1000, bytes_accessed=micros * 3000000, transcendentals=0),
+        cost_estimate=pl.CostEstimate(flops=1000, bytes_accessed=micros * 300000, transcendentals=0),
         input_output_aliases=aliases or {},
     )(*tables, *args)
 
@@ -226,13 +219,13 @@
     for e, ref in enumerate((own_ref, other_ref)):
         for r in range(4):
             for m in range(3):
-                out_ref[m, halves[e], 0, 32 * r : 32 * (r + 1), :] = ref[r, 0, m]
+                out_ref[m, halves[e], 0, 32 * r : 32 * (r + 1), :] = ref[r, m, 0]
 
 
 def place_mlp(slot, halves, own, other):
     out = call(
         place_mlp_kernel, (slot, halves), (8,),
-        [pl.BlockSpec((4, 1, 3, 32, WIDE), lambda i, *_: (0, i, 0, 0, 0))] * 2,
+        [pl.BlockSpec((4, 3, 1, 32, WIDE), lambda i, *_: (0, 0, i, 0, 0))] * 2,
         pl.BlockSpec((3, 2, 1, 128, WIDE), lambda i, slot, *_: (0, 0, slot[i], 0, 0)),
         sds((3, 2, 8, 128, WIDE)), [], 6, (own, other),
     )
@@ -732,10 +725,9 @@
 
 
     def gather_tokens(rows):
-        parts = []
-        for part in ring_gather(rows, "z"):
-            parts += [part, swap(part)]
-        return parts
+        own, first, second, third = ring_gather(rows, "z")
+        parts = [own, swap(own), first, swap(first), second, swap(second)]
+        return parts + [third, swap(after(third, first, second))]
 
     def give(group, total):
         value = total.astype(BF)
@@ -753,33 +745,34 @@
 
     def exchange(mine, other):
         got = swap(other)
-        own = jnp.stack([mine[0], got[0]])
-        before = jnp.stack([mine[1], got[2]])
-        forward = jnp.stack([mine[2], got[1]])
-        far = jnp.stack([mine[3], got[3]])
-        parts = jnp.concatenate(exchange_z(own, before, forward, far))
-        return parts
-
-    def spread(part, forward):
-        pieces = ring_gather(part, "x", forward)
-        return list(pieces) + [step(piece, "y", 1) for piece in pieces]
+        own = jnp.stack([mine[0], got[0]], axis=1)
+        before = jnp.stack([mine[1], got[2]], axis=1)
+        forward = jnp.stack([mine[2], got[1]], axis=1)
+        far = jnp.stack([mine[3], got[3]], axis=1)
+        return jnp.concatenate(exchange_z(own, before, forward, far), axis=1)
+
+    def spread(part):
+        pieces = list(ring_gather(part, "x"))
+        there = [step(pieces[0], "y", 1)]
+        there += [step(piece, "y", 1) for piece in after(pieces[1:], pieces[1])]
+        return pieces + there
 
     normed_own = (rows_in * scale_attn * gain_one).astype(BF)
-    normed_attn = lax.all_gather(
-        normed_own, "blk", axis=0, tiled=True, axis_index_groups=ZC_GROUPS
-    )
     out_rows = lax.dynamic_slice_in_dim(output_weight, x * 32, 32, axis=0)
     out_part = send(
         out_rows.reshape(32, 8, QUERY).transpose(1, 0, 2),
         lambda yh, x, yl, z, c: (yh, x, c, 2 * yl + z // 2, z % 2),
     )
     packs = exchange(
-        *pack(after(spots, normed_own), core, gate_weight, up_weight, down_weight, query_weight, key_weight, value_weight)
-    )
-    attn_part = jnp.concatenate([out_part, packs[:, 3, :, :QKV]], axis=-1)
-    attn_pieces = spread(attn_part, False)
+        *pack(spots, core, gate_weight, up_weight, down_weight, query_weight, key_weight, value_weight)
+    )
+    normed_attn = lax.all_gather(
+        after(normed_own, packs), "blk", axis=0, tiled=True, axis_index_groups=ZC_GROUPS
+    )
+    attn_part = jnp.concatenate([out_part, packs[3, :, :, :QKV]], axis=-1)
+    attn_pieces = spread(attn_part)
     w_qkv, w_out = place_attn(slot, xs, halves, attn_pieces)
-    mlp_half_rows = lax.all_gather(packs[:, :3], "batch", axis=0, axis_index_groups=X_GROUPS)
+    mlp_half_rows = lax.all_gather(packs[:3], "batch", axis=0, axis_index_groups=X_GROUPS)
     w_mlp = place_mlp(slot, halves, mlp_half_rows, step(mlp_half_rows, "y", 1))
 
     grad_rows = lax.all_gather(
@@ -821,11 +814,12 @@
     kept, sums, got, at = None, [None] * 4, [None] * 4, mlp_chunk
     for part in range(2):
         kept, result = mlp_half(part, at, mlp_parts[4 * part : 4 * part + 4], grad_rows, w_mlp, kept)
-        for g, mine, peer in zip(((3, 1), (2, 0))[part], result[::2], result[1::2]):
-            sums[g] = add(mine, swap(peer))
+        swapped = [swap(peer) for peer in result[1::2]]
+        for g, mine, peer in zip(((3, 1), (2, 0))[part], result[::2], swapped):
+            sums[g] = add(mine, peer)
             if g:
                 got[g] = give(g, sums[g])
-        at = after(mlp_chunk, sums[3], sums[1])
+        at = after(mlp_chunk, *swapped)
     hidden, gate_grad_rows, up_grad_rows = kept
     mlp_outs = mlp_grads(
         column, xs, yhs, core, after(mlp_chunk, got[3], got[1]), mlp_parts, grad_rows,
@@ -845,28 +839,19 @@
     layer_out = (residual + scatter_tokens(branch[::2], branch[1::2])).astype(BF)[None]
 
 
-    def reduce_planes(outs, other):
-        low = after(ring_scatter(*outs[:4], "x").astype(BF), other)
-        low = ring_scatter(low[0], low[2], low[3], low[1], "y").astype(BF)
-        high = after(ring_scatter(outs[4], outs[6], outs[7], outs[5], "y").astype(BF), other)
-        high = ring_scatter(high[0], high[1], high[2], high[3], "x").astype(BF)
-        return jnp.concatenate([low, high])
-
     def resplit_back(part):
         got = exchange_z(part[0], part[1], part[2], part[3])
         mine = jnp.stack([each[0] for each in got])
         other = swap(jnp.stack([got[p][1] for p in (0, 2, 1, 3)]))
         return jnp.stack([mine, other])
 
-    def gather_batch(part, forward):
-        return ring_gather(jnp.stack([part, across(part, "y")]), "x", forward)
-
 
     query_grad_rows, sums = [], ()
     for start, stop in ((0, 2), (2, 6), (6, 8)):
+        at = after(query_place, mlp_low) if stop == 8 else query_place
         rows, *sums = attend_back(
             start, branch_parts[start:stop], sums, stop == 8,
-            query_place, key_slot, core, key_count, queries, w_out, keys, values, keys.T,
+            at, key_slot, core, key_count, queries, w_out, keys, values, keys.T,
         )
         query_grad_rows.append(rows)
     kv_keep, kv_give = sums
@@ -878,24 +863,36 @@
     low = ring_scatter(low[0], low[2], low[3], low[1], "y").astype(BF)
     high = add(mlp_outs[1], high_after, after(high_before, kv_keep)).astype(BF)
     high = ring_scatter(high[0], high[1], high[2], high[3], "x").astype(BF)
-    mlp_sums = resplit_back(jnp.concatenate([low, high]))
-    mlp_sums = gather_batch(mlp_sums, True)
-    gate_grad, up_grad, down_grad = finish_mlp(spots, xs, yhs, core, mlp_sums)
+    kv_grad_rows = after(kv_grad_rows, low, high)
+    mlp_sums = resplit_back([low[0], low[1], high[0], high[1]])
 
     attn_partial = project_back(query_grad_rows, kv_grad_rows, w_qkv)
-    attn_sums, attn_gain_part = attn_grads(
+    attn_outs, attn_gain_part = attn_grads(
         column, xs, yhs, core, halves, chunk, normed_attn, branch_parts, attended, query_grad_rows, kv_grad_rows, w_qkv
     )
-    gain_grads = sum_all(jnp.stack([attn_gain_part / gain_one, mlp_gain_part]))
+    gain_grads = jnp.stack([attn_gain_part / gain_one, mlp_gain_part])
+    gain_grads = jnp.sum(lax.all_gather(jnp.pad(gain_grads, ((0, 6), (0, 0))), "blk"), axis=0)
+
+    attn_outs = after(attn_outs, mlp_sums)
+    mlp_sums = jnp.stack([mlp_sums, across(mlp_sums, "y")])
     normed_attn_grad = scatter_tokens(attn_partial[::2], attn_partial[1::2])
-    attn_sums = reduce_planes(attn_sums, normed_attn_grad)
+    low = after(ring_scatter(*attn_outs[:4], "x").astype(BF), normed_attn_grad, mlp_sums)
+    high = after(
+        ring_scatter(attn_outs[4], attn_outs[6], attn_outs[7], attn_outs[5], "y").astype(BF), normed_attn_grad, mlp_sums
+    )
+    low = ring_scatter(low[0], low[2], low[3], low[1], "y").astype(BF)
+    high = ring_scatter(high[0], high[1], high[2], high[3], "x").astype(BF)
+    mlp_sums = ring_gather(mlp_sums, "x", True)
+    attn_sums = after(jnp.concatenate([low, high]), mlp_sums[1], mlp_sums[2], gain_grads)
+    gain_grads = jnp.sum(lax.all_gather(gain_grads, "batch"), axis=0)[:2]
     out_sums = send(
         attn_sums[..., :QUERY], lambda yh, x, yl, z, c: (yh, x, z // 2, 2 * (z % 2) + c, yl)
     )
     qkv_sums = resplit_back(attn_sums[..., QUERY:])
     attn_sums = jnp.concatenate([out_sums.reshape(2, 4, 16, QUERY), qkv_sums], axis=-1)
-    query_grad, key_grad, value_grad, output_grad = finish_attn(spots, xs, yhs, core, gather_batch(attn_sums, False))
-
+    attn_sums = ring_gather(jnp.stack([attn_sums, across(attn_sums, "y")]), "x")
+    gate_grad, up_grad, down_grad = finish_mlp(spots, xs, yhs, core, mlp_sums)
+    query_grad, key_grad, value_grad, output_grad = finish_attn(spots, xs, yhs, core, attn_sums)
     tokens_grad = (
         residual_grad + norm_back(rows_in, scale_attn, gain_one, normed_attn_grad)
     ).astype(BF)[None]

time: 675 us -> 649 us (0.961)
  waiting for transfers between devices: 285 us -> 228 us
  blocking collectives: 0 us -> 36.1 us
  starting transfers between devices: 146 us -> 129 us
  local copies, waits for them, and re-layouts: 27.8 us -> 42 us
    ppermute x107 -> x97, waiting for transfers between devices: 285 us -> 218 us  [send(): return lax.ppermute(value, BOTH, pairs)]
    all_gather x0 -> x1, blocking collectives: none -> 36.1 us  [on_device(): gain_grads = jnp.sum(lax.all_gather(gain_grads, 'batch'), axis=0)[:2]]
    unnamed x156 -> x200, local copies, waits for them, and re-layouts: 14.3 us -> 34.4 us
    ppermute x107 -> x97, starting transfers between devices: 146 us -> 129 us  [send(): return lax.ppermute(value, BOTH, pairs)]
    all_gather x2 -> x3, waiting for transfers between devices: 0.01 us -> 9.97 us  [the longest x1 9.97 us: on_device(): lax.all_gather(packs[:3], 'batch', axis=0, axis_index_groups=X_GROUPS)]
  transfers between devices with their start and end apart: 111 -> 102, of which waited for: 42 -> 44; matrix products, arithmetic and copies ran while one was open for 5% -> 6% of each run, Pallas kernels for 20% -> 18%
where the time goes in v2:
time: 649 us; the launch traced here: 643 us
  waiting for transfers between devices  228 us (35%)
  Pallas kernels  161 us (25%)
  starting transfers between devices  129 us (20%)
  local copies, waits for them, and re-layouts  42 us (6%)
  blocking collectives  36.1 us (6%)
  other arithmetic  27.3 us (4%)
  between operations  15.6 us (2%)
    ppermute x97, waiting for transfers between devices, send(): return lax.ppermute(value, BOTH, pairs)  218 us
    pallas_call x18, Pallas kernels, call(): pl.pallas_call(body, grid_spec=pltpu.PrefetchScalarGridSpec(num_scalar_pr...  161 us
    ppermute x97, starting transfers between devices, send(): return lax.ppermute(value, BOTH, pairs)  129 us
    all_gather x1, blocking collectives, on_device(): gain_grads = jnp.sum(lax.all_gather(gain_grads, 'batch'), axis=0)[:2]  36.1 us
    unnamed x200, local copies, waits for them, and re-layouts  34.4 us
  transfers between devices with their start and end apart: 102, of which 44 were waited for; matrix products, arithmetic and copies ran while one was open for 6% of the time, Pallas kernels for 18%

profile of v2, /device:TPU:24, one launch (start us, length us, event | category | flops | bytes accessed | tf_op | source)
XLA Modules:
  0.0 642.7 jit_solution(17639216533892259580)
XLA Ops:
  12.9 4.0 shard_map.212
  27.8 4.3 collective-permute-done.1
  32.1 10.1 %collective-permute-done.2 = bf16[4,2,32,704]{3,2,0,1:T(8,128)(2,1)S(1)} collective-permute-done((bf16[4,2,32,704]{3,2,0,1:T(8,128)(2,1)S(1)}, bf16[4,2,32,704]{3,2,0,1:T(8,128)(2,1)S(1)}, u32[]{:S(2)}, u32[]{:S(2)}) %collective-permute-start.2) | collective-permute-done | bytes 360480 | tf_op jit(solution)/shard_map/ppermute | solution.py:45
  47.6 4.3 collective-permute-done.4
  57.1 5.0 collective-permute-done.5.refs_1_
  62.1 7.1 %collective-permute-done.6.refs_2_ = bf16[8,32,576]{2,1,0:T(8,128)(2,1)S(1)} collective-permute-done((bf16[8,32,576]{2,1,0:T(8,128)(2,1)S(1)}, bf16[8,32,576]{2,1,0:T(8,128)(2,1)S(1)}, u32[]{:S(2)}, u32[]{:S(2)}) %collective-permute-start.6) | collective-permute-done | bytes 294944 | tf_op jit(solution)/shard_map/ppermute | solution.py:45
  71.7 7.1 %collective-permute-done.11.refs_7_ = bf16[8,32,576]{2,1,0:T(8,128)(2,1)S(1)} collective-permute-done((bf16[8,32,576]{2,1,0:T(8,128)(2,1)S(1)}, bf16[8,32,576]{2,1,0:T(8,128)(2,1)S(1)}, u32[]{:S(2)}, u32[]{:S(2)}) %collective-permute-start.11) | collective-permute-done | bytes 294944 | tf_op jit(solution)/shard_map/ppermute | solution.py:45
  81.5 4.7 collective-permute-done.8.refs_4_
  86.2 3.5 collective-permute-done.9.refs_5_
  89.7 3.5 collective-permute-done.10.refs_6_
  97.5 6.1 shard_map.214
  104.1 8.0 %collective-permute-done.12 = bf16[2,1024,64]{1,2,0:T(8,128)(2,1)S(1)} collective-permute-done((bf16[2,1024,64]{1,2,0:T(8,128)(2,1)S(1)}, bf16[2,1024,64]{1,2,0:T(8,128)(2,1)S(1)}, u32[]{:S(2)}, u32[]{:S(2)}) %collective-permute-start.12) | collective-permute-done | bytes 262176 | tf_op jit(solution)/shard_map/ppermute | solution.py:45
  114.5 6.1 shard_map.215
  121.3 10.0 %all-gather.12.cloned.1.call-done = bf16[12,8,32,704]{3,2,1,0:T(8,128)(2,1)} async-done(((bf16[3,8,32,704]{3,2,1,0:T(8,128)(2,1)}), bf16[12,8,32,704]{3,2,1,0:T(8,128)(2,1)}) %all-gather.12.cloned.1.call-update) | async-done | bytes 4325392 | tf_op jit(solution)/shard_map/all_gather | solution.py:775
  132.0 8.9 %shard_map.218 = (bf16[256,256]{1,0:T(8,128)(2,1)S(1)}, bf16[128,2048]{1,0:T(8,128)(2,1)S(1)}, bf16[128,2048]{1,0:T(8,128)(2,1)S(1)}) custom-call(s32[8]{0:T(128)S(1)} %bitcast.193, s32[16]{0:T(128)S(1)} %select_reduce_fusion.1.key_slot, bf16[1024,256]{1,0:T(8,128)(2,1)S(1)} %get-tuple-element.117.q_ref.refs_0_, ...), custom_call_target="tpu_custom_call" | custom-call | flops 1000 | bytes 1800000 | tf_op jit(solution)/shard_map/pallas_call | solution.py:134
  141.6 5.9 shard_map.217
  156.3 19.7 %collective-permute-done.15 = bf16[128,2048]{1,0:T(8,128)(2,1)S(1)} collective-permute-done((bf16[128,2048]{1,0:T(8,128)(2,1)S(1)}, bf16[128,2048]{1,0:T(8,128)(2,1)S(1)}, u32[]{:S(2)}, u32[]{:S(2)}) %collective-permute-start.15) | collective-permute-done | bytes 524320 | tf_op jit(solution)/shard_map/ppermute | solution.py:45
  175.9 5.1 shard_map.216
  181.1 5.5 collective-permute-done.20
  192.5 11.5 %collective-permute-done.21.refs_0_ = bf16[128,2048]{1,0:T(8,128)(2,1)} collective-permute-done((bf16[128,2048]{1,0:T(8,128)(2,1)S(1)}, bf16[128,2048]{1,0:T(8,128)(2,1)}, u32[]{:S(2)}, u32[]{:S(2)}) %collective-permute-start.21) | collective-permute-done | bytes 524320 | tf_op jit(solution)/shard_map/ppermute | solution.py:45
  204.0 10.2 %collective-permute-done.22.refs_2_ = bf16[128,2048]{1,0:T(8,128)(2,1)} collective-permute-done((bf16[128,2048]{1,0:T(8,128)(2,1)S(1)}, bf16[128,2048]{1,0:T(8,128)(2,1)}, u32[]{:S(2)}, u32[]{:S(2)}) %collective-permute-start.22) | collective-permute-done | bytes 524320 | tf_op jit(solution)/shard_map/ppermute | solution.py:45
  217.1 8.4 %shard_map.219 = bf16[3,2,8,128,704]{4,3,2,1,0:T(8,128)(2,1)} custom-call(s32[8]{0:T(128)S(1)} %stack.211.slot, s32[2]{0:T(128)S(1)} %pad_add_fusion.2.halves, bf16[4,3,8,32,704]{4,3,2,1,0:T(8,128)(2,1)S(1)} %bitcast.191, bf16[4,3,8,32,704]{4,3,2,1,0:T(8,128)(2,1)} %collective-permute-done.26.other_ref), custom_call_target="tpu_custom_call" | custom-call | flops 1000 | bytes 1800000 | tf_op jit(solution)/shard_map/pallas_call | solution.py:134
  225.5 16.0 %shard_map.220 = (bf16[1024,704]{1,0:T(8,128)(2,1)S(1)}, bf16[1024,704]{1,0:T(8,128)(2,1)}, bf16[1024,704]{1,0:T(8,128)(2,1)}, bf16[128,2048]{1,0:T(8,128)(2,1)S...) custom-call(s32[8]{0:T(128)S(1)} %stack.219.chunk.nat, ...), custom_call_target="tpu_custom_call" | custom-call | flops 1000 | bytes 4800000 | tf_op jit(solution)/shard_map/pallas_call | solution.py:134
  247.0 9.4 %collective-permute-start.32 = (bf16[128,2048]{1,0:T(8,128)(2,1)}, bf16[128,2048]{1,0:T(8,128)(2,1)}, u32[]{:S(2)}, u32[]{:S(2)}) collective-permute-start(bf16[128,2048]{1,0:T(8,128)(2,1)} %add_convert_fusion.11), channel_id=1, source_target_pairs={{0,6},{1,3},{2,0},{3,5},{4,2},{5,7},{6,4},{7,1},{8,14},{9,11},{10,... | collective-permute-start | bytes 1572872 | tf_op jit(solution)/shard_map/ppermute | solution.py:45
  258.0 15.9 %shard_map.221 = (bf16[1024,704]{1,0:T(8,128)(2,1)S(1)}, bf16[1024,704]{1,0:T(8,128)(2,1)}, bf16[1024,704]{1,0:T(8,128)(2,1)}, bf16[128,2048]{1,0:T(8,128)(2,1)S...) custom-call(s32[8]{0:T(128)S(1)} %stack.219.chunk.nat, ...), custom_call_target="tpu_custom_call", output_to_operand_aliasing={{0}: (10, {}), {1}: (11, {}), {2}: (12, {})} | custom-call | flops 1000 | bytes 4800000 | tf_op jit(solution)/shard_map/pallas_call | solution.py:134
  277.6 19.5 %shard_map.222 = (bf16[4,4,2,2,3,16,704]{6,5,4,3,2,1,0:T(8,128)(2,1)}, bf16[4,2,2,3,16,704]{5,4,3,2,1,0:T(8,128)(2,1)S(1)}, bf16[4,2,2,3,16,704]{5,4,3,2,1,0:T(8...) custom-call(s32[8]{0:T(128)S(1)} %stack.228.column, s32[4]{0:T(128)S(1)} %pad_add_fusion.1.xs, ...), custom_call_target="tpu_custom_call" | custom-call | flops 1000 | bytes 5100000 | tf_op jit(solution)/shard_map/pallas_call | solution.py:134
  302.5 9.6 %collective-permute-done.34 = bf16[128,2048]{1,0:T(8,128)(2,1)S(1)} collective-permute-done((bf16[128,2048]{1,0:T(8,128)(2,1)S(1)}, bf16[128,2048]{1,0:T(8,128)(2,1)S(1)}, u32[]{:S(2)}, u32[]{:S(2)}) %collective-permute-start.34) | collective-permute-done | bytes 524320 | tf_op jit(solution)/shard_map/ppermute | solution.py:45
  319.5 13.2 %collective-permute-done.36.refs_1_.refs_14_ = bf16[128,2048]{1,0:T(8,128)(2,1)S(1)} collective-permute-done((bf16[128,2048]{1,0:T(8,128)(2,1)S(1)}, bf16[128,2048]{1,0:T(8,128)(2,1)S(1)}, u32[]{:S(2)}, u32[]{:S(2)}) %collective-permute-start.36) | collective-permute-done | bytes 524320 | tf_op jit(solution)/shard_map/ppermute | solution.py:45
  332.7 8.3 %collective-permute-done.37.refs_1_.refs_10_ = bf16[128,2048]{1,0:T(8,128)(2,1)S(1)} collective-permute-done((bf16[128,2048]{1,0:T(8,128)(2,1)S(1)}, bf16[128,2048]{1,0:T(8,128)(2,1)S(1)}, u32[]{:S(2)}, u32[]{:S(2)}) %collective-permute-start.37) | collective-permute-done | bytes 524320 | tf_op jit(solution)/shard_map/ppermute | solution.py:45
  345.5 3.7 convolution_convert_fusion
  354.3 5.9 collective-permute-done.56
  366.8 6.8 %shard_map.223 = (bf16[256,256]{1,0:T(8,128)(2,1)S(1)}, f32[2048,64]{1,0:T(8,128)S(1)}, f32[2048,64]{1,0:T(8,128)S(1)}) custom-call(s32[8]{0:T(128)S(1)} %bitcast.196, s32[16]{0:T(128)S(1)} %select_reduce_fusion.1.key_slot, s32[1]{0:T(128)} %bitcast.15.core, s32[16]{0:T(128)S(1)} %copy-done.52, bf16[1024,256]{1,0:T(8,128)(2,1)S(1)} %get-tuple-element.117.q_ref.refs_0_, ...), custom_call_target="tpu_custom_call" | custom-call | flops 1000 | bytes 2400000 | tf_op jit(solution)/shard_map/pallas_call | solution.py:134
  375.7 22.3 %shard_map.224 = (bf16[512,256]{1,0:T(8,128)(2,1)S(1)}, f32[2048,64]{1,0:T(8,128)S(1)}, f32[2048,64]{1,0:T(8,128)}) custom-call(s32[8]{0:T(128)S(1)} %bitcast.197, s32[16]{0:T(128)S(1)} %select_reduce_fusion.1.key_slot, s32[1]{0:T(128)} %bitcast.15.core, s32[16]{0:T(128)S(1)} %copy-done.52, bf16[1024,256]{1,0:T(8,128)(2,1)S(1)} %get-tuple-element.117.q_ref.refs_0_, ...), custom_call_target="tpu_custom_call" | custom-call | flops 1000 | bytes 4800000 | tf_op jit(solution)/shard_map/pallas_call | solution.py:134
  406.0 8.5 %shard_map.225 = (bf16[256,256]{1,0:T(8,128)(2,1)S(1)}, bf16[2048,64]{1,0:T(8,128)(2,1)S(1)}, bf16[2048,64]{1,0:T(8,128)(2,1)S(1)}) custom-call(s32[8]{0:T(128)S(1)} %bitcast.198, s32[16]{0:T(128)S(1)} %select_reduce_fusion.1.key_slot, s32[1]{0:T(128)} %bitcast.15.core, s32[16]{0:T(128)S(1)} %copy-done.53, ...), custom_call_target="tpu_custom_call" | custom-call | flops 1000 | bytes 2400000 | tf_op jit(solution)/shard_map/pallas_call | solution.py:134
  419.8 6.8 %collective-permute-start.60 = (bf16[2,2,3,16,704]{4,3,2,1,0:T(8,128)(2,1)S(1)}, bf16[2,2,3,16,704]{4,3,2,1,0:T(8,128)(2,1)S(1)}, u32[]{:S(2)}, u32[]{:S(2)}) collective-permute-start(bf16[2,2,3,16,704]{4,3,2,1,0:T(8,128)(2,1)S(1)} %get-tuple-element.227), channel_id=1, source_target_pairs={{0,16},{1,49},{2,18},{3,51},{4,20},{5,53},{6,22},{7,55},{8,24},{9,... | collective-permute-start | bytes 811016 | tf_op jit(solution)/shard_map/ppermute | solution.py:45
  428.9 5.1 collective-permute-done.60
  449.6 5.4 shard_map.226
  456.5 11.9 %shard_map.227 = (bf16[4,2,2,16,576]{4,3,2,1,0:T(8,128)(2,1)S(1)}, bf16[4,2,2,16,576]{4,3,2,1,0:T(8,128)(2,1)S(1)}, bf16[4,2,2,16,576]{4,3,2,1,0:T(8,128)(2,1)S(...) custom-call(s32[8]{0:T(128)S(1)} %copy-done.61, ...), custom_call_target="tpu_custom_call" | custom-call | flops 1000 | bytes 3000000 | tf_op jit(solution)/shard_map/pallas_call | solution.py:134
  486.5 16.9 %collective-permute-done.81 = bf16[4,2,2,16,576]{4,3,2,1,0:T(8,128)(2,1)S(1)} collective-permute-done((bf16[4,2,2,16,576]{4,3,2,1,0:T(8,128)(2,1)}, bf16[4,2,2,16,576]{4,3,2,1,0:T(8,128)(2,1)S(1)}, u32[]{:S(2)}, u32[]{:S(2)}) %collective-permute-start.81) | collective-permute-done | bytes 294944 | tf_op jit(solution)/shard_map/ppermute | solution.py:45
  505.8 3.8 collective-permute-start.72
  517.8 5.9 collective-permute-start.85
  523.7 14.4 %collective-permute-done.67 = bf16[128,2048]{1,0:T(8,128)(2,1)S(1)} collective-permute-done((bf16[128,2048]{1,0:T(8,128)(2,1)S(1)}, bf16[128,2048]{1,0:T(8,128)(2,1)S(1)}, u32[]{:S(2)}, u32[]{:S(2)}) %collective-permute-start.67) | collective-permute-done | bytes 524320 | tf_op jit(solution)/shard_map/ppermute | solution.py:45
  542.1 3.6 collective-permute-start.82
  559.9 3.6 collective-permute-start.90
  570.4 5.2 collective-permute-done.87
  576.6 36.1 %all-gather.2 = f32[64,2048]{1,0:T(8,128)S(1)} all-gather(f32[8,2048]{1,0:T(8,128)S(1)} %bitcast_reduce_fusion), channel_id=4, replica_groups=mesh['batch'=8,'blk'=16] {'batch'}, dimensions={0}, use_global_device_ids=true | all-gather | bytes 589824 | tf_op jit(solution)/shard_map/all_gather | solution.py:887
  613.3 4.2 collective-permute-start.94
  629.6 6.4 shard_map.229
  (482 shorter events, 200.0 us)
Async XLA Ops:
  7.2 88.5 %all-gather.8.cloned.1.call-start = ((), (), s32[]{:S(2)}) async-start(), calls=%async_computation.1 | async-start | bytes 4718592 | tf_op jit(solution)/shard_map/all_gather | solution.py:769
  22.7 19.5 %collective-permute-start.2 = (bf16[4,2,32,704]{3,2,0,1:T(8,128)(2,1)S(1)}, bf16[4,2,32,704]{3,2,0,1:T(8,128)(2,1)S(1)}, u32[]{:S(2)}, u32[]{:S(2)}) collective-permute-start(bf16[4,2,32,704]{3,2,0,1:T(8,128)(2,1)S(1)} %pad_maximum_fusion.3), channel_id=1, source_target_pairs={{0,6},{1,3},{2,0},{3,5},{4,2},{5,7},{6,4},{7,1},{8,14},{9,11},{10,... | collective-permute-start | bytes 1081352 | tf_op jit(solution)/shard_map/ppermute | solution.py:45
  24.9 19.4 %collective-permute-start.3 = (bf16[4,2,32,704]{3,2,1,0:T(8,128)(2,1)S(1)}, bf16[4,2,32,704]{3,2,1,0:T(8,128)(2,1)S(1)}, u32[]{:S(2)}, u32[]{:S(2)}) collective-permute-start(bf16[4,2,32,704]{3,2,1,0:T(8,128)(2,1)S(1)} %pad_maximum_fusion.4), channel_id=1, source_target_pairs={{0,4},{1,5},{2,6},{3,7},{4,0},{5,1},{6,2},{7,3},{8,12},{9,13},{10,... | collective-permute-start | bytes 1081352 | tf_op jit(solution)/shard_map/ppermute | solution.py:45
  44.4 86.9 %all-gather.12.cloned.1.call-start = ((), (), s32[]{:S(2)}) async-start(), calls=%async_computation.4 | async-start | bytes 5898240 | tf_op jit(solution)/shard_map/all_gather | solution.py:775
  45.6 179.9 %all-gather.10.cloned.1.call-start = ((), (), s32[]{:S(2)}) async-start(), calls=%async_computation.2 | async-start | bytes 4718592 | tf_op jit(solution)/shard_map/all_gather | solution.py:778
  53.6 15.6 %collective-permute-start.6 = (bf16[8,32,576]{2,1,0:T(8,128)(2,1)S(1)}, bf16[8,32,576]{2,1,0:T(8,128)(2,1)S(1)}, u32[]{:S(2)}, u32[]{:S(2)}) collective-permute-start(bf16[8,32,576]{2,1,0:T(8,128)(2,1)S(1)} %pad_maximum_fusion.5.refs_0_), channel_id=1, source_target_pairs={{0,48},{1,17},{2,50},{3,19},{4,52},{5,21},{6,54},{7,23},{8,56},{9,... | collective-permute-start | bytes 884744 | tf_op jit(solution)/shard_map/ppermute | solution.py:45
  55.3 16.3 %collective-permute-start.7 = (bf16[8,32,576]{2,1,0:T(8,128)(2,1)S(1)}, bf16[8,32,576]{2,1,0:T(8,128)(2,1)S(1)}, u32[]{:S(2)}, u32[]{:S(2)}) collective-permute-start(bf16[8,32,576]{2,1,0:T(8,128)(2,1)S(1)} %pad_maximum_fusion.5.refs_0_), channel_id=1, source_target_pairs={{0,32},{1,33},{2,34},{3,35},{4,36},{5,37},{6,38},{7,39},{8,40},{9,... | collective-permute-start | bytes 884744 | tf_op jit(solution)/shard_map/ppermute | solution.py:45
  78.8 323.3 %reduce-scatter.2.cloned.1.call-start = ((), (), s32[]{:S(2)}) async-start(), calls=%async_computation.3 | async-start | bytes 5898240 | tf_op jit(solution)/shard_map/reduce_scatter | solution.py:829
  121.2 27.0 %collective-permute-start.14 = (bf16[128,2048]{1,0:T(8,128)(2,1)}, bf16[128,2048]{1,0:T(8,128)(2,1)}, u32[]{:S(2)}, u32[]{:S(2)}) collective-permute-start(bf16[128,2048]{1,0:T(8,128)(2,1)} %get-tuple-element.121), channel_id=1, source_target_pairs={{0,1},{1,0},{2,3},{3,2},{4,5},{5,4},{6,7},{7,6},{8,9},{9,8},{10,11... | collective-permute-start | bytes 1572872 | tf_op jit(solution)/shard_map/ppermute | solution.py:45
  131.3 83.5 %collective-permute-start.26 = (bf16[4,3,8,32,704]{4,3,2,1,0:T(8,128)(2,1)}, bf16[4,3,8,32,704]{4,3,2,1,0:T(8,128)(2,1)}, u32[]{:S(2)}, u32[]{:S(2)}) collective-permute-start(bf16[4,3,8,32,704]{4,3,2,1,0:T(8,128)(2,1)} %bitcast.190), channel_id=1, source_target_pairs={{0,8},{1,73},{2,10},{3,75},{4,12},{5,77},{6,14},{7,79},{8,64},{9,1... | collective-permute-start | bytes 12976136 | tf_op jit(solution)/shard_map/ppermute | solution.py:45
  149.3 26.6 %collective-permute-start.15 = (bf16[128,2048]{1,0:T(8,128)(2,1)S(1)}, bf16[128,2048]{1,0:T(8,128)(2,1)S(1)}, u32[]{:S(2)}, u32[]{:S(2)}) collective-permute-start(bf16[128,2048]{1,0:T(8,128)(2,1)S(1)} %add_convert_fusion.14), channel_id=1, source_target_pairs={{0,4},{1,5},{2,6},{3,7},{4,0},{5,1},{6,2},{7,3},{8,12},{9,13},{10,... | collective-permute-start | bytes 1572872 | tf_op jit(solution)/shard_map/ppermute | solution.py:45
  152.7 33.9 %collective-permute-start.20 = (bf16[128,2048]{1,0:T(8,128)(2,1)S(1)}, bf16[128,2048]{1,0:T(8,128)(2,1)S(1)}, u32[]{:S(2)}, u32[]{:S(2)}) collective-permute-start(bf16[128,2048]{1,0:T(8,128)(2,1)S(1)} %add_convert_fusion.12), channel_id=1, source_target_pairs={{0,2},{1,7},{2,4},{3,1},{4,6},{5,3},{6,0},{7,5},{8,10},{9,15},{10,... | collective-permute-start | bytes 1572872 | tf_op jit(solution)/shard_map/ppermute | solution.py:45
  153.0 33.7 %collective-permute-start.18 = (bf16[128,2048]{1,0:T(8,128)(2,1)S(1)}, bf16[128,2048]{1,0:T(8,128)(2,1)S(1)}, u32[]{:S(2)}, u32[]{:S(2)}) collective-permute-start(bf16[128,2048]{1,0:T(8,128)(2,1)S(1)} %add_convert_fusion.13), channel_id=1, source_target_pairs={{0,6},{1,3},{2,0},{3,5},{4,2},{5,7},{6,4},{7,1},{8,14},{9,11},{10,... | collective-permute-start | bytes 1572872 | tf_op jit(solution)/shard_map/ppermute | solution.py:45
  187.5 16.5 %collective-permute-start.21 = (bf16[128,2048]{1,0:T(8,128)(2,1)S(1)}, bf16[128,2048]{1,0:T(8,128)(2,1)}, u32[]{:S(2)}, u32[]{:S(2)}) collective-permute-start(bf16[128,2048]{1,0:T(8,128)(2,1)S(1)} %multiply_convert_fusion.refs_2_.refs_6_), channel_id=1, source_target_pairs={{0,4},{1,5},{2,6},{3,7},{4,0},{5,1},{6,2},{7,3},{8,12},{9,13},{10,... | collective-permute-start | bytes 1572872 | tf_op jit(solution)/shard_map/ppermute | solution.py:45
  189.3 24.9 %collective-permute-start.22 = (bf16[128,2048]{1,0:T(8,128)(2,1)S(1)}, bf16[128,2048]{1,0:T(8,128)(2,1)}, u32[]{:S(2)}, u32[]{:S(2)}) collective-permute-start(bf16[128,2048]{1,0:T(8,128)(2,1)S(1)} %multiply_convert_fusion.refs_2_.refs_6_), channel_id=1, source_target_pairs={{0,2},{1,7},{2,4},{3,1},{4,6},{5,3},{6,0},{7,5},{8,10},{9,15},{10,... | collective-permute-start | bytes 1572872 | tf_op jit(solution)/shard_map/ppermute | solution.py:45
  189.3 24.9 %collective-permute-start.23 = (bf16[128,2048]{1,0:T(8,128)(2,1)S(1)}, bf16[128,2048]{1,0:T(8,128)(2,1)}, u32[]{:S(2)}, u32[]{:S(2)}) collective-permute-start(bf16[128,2048]{1,0:T(8,128)(2,1)S(1)} %multiply_convert_fusion.refs_2_.refs_6_), channel_id=1, source_target_pairs={{0,6},{1,3},{2,0},{3,5},{4,2},{5,7},{6,4},{7,1},{8,14},{9,11},{10,... | collective-permute-start | bytes 1572872 | tf_op jit(solution)/shard_map/ppermute | solution.py:45
  244.4 32.2 %collective-permute-start.35 = (bf16[128,2048]{1,0:T(8,128)(2,1)}, bf16[128,2048]{1,0:T(8,128)(2,1)}, u32[]{:S(2)}, u32[]{:S(2)}) collective-permute-start(bf16[128,2048]{1,0:T(8,128)(2,1)} %add_convert_fusion.9), channel_id=1, source_target_pairs={{0,4},{1,5},{2,6},{3,7},{4,0},{5,1},{6,2},{7,3},{8,12},{9,13},{10,... | collective-permute-start | bytes 1572872 | tf_op jit(solution)/shard_map/ppermute | solution.py:45
  247.0 29.6 %collective-permute-start.32 = (bf16[128,2048]{1,0:T(8,128)(2,1)}, bf16[128,2048]{1,0:T(8,128)(2,1)}, u32[]{:S(2)}, u32[]{:S(2)}) collective-permute-start(bf16[128,2048]{1,0:T(8,128)(2,1)} %add_convert_fusion.11), channel_id=1, source_target_pairs={{0,6},{1,3},{2,0},{3,5},{4,2},{5,7},{6,4},{7,1},{8,14},{9,11},{10,... | collective-permute-start | bytes 1572872 | tf_op jit(solution)/shard_map/ppermute | solution.py:45
  298.2 260.4 %all-gather.14.cloned.1.call-start = ((), (), s32[]{:S(2)}) async-start(), calls=%async_computation.5 | async-start | bytes 1114112 | tf_op jit(solution)/shard_map/all_gather | solution.py:874
  316.3 16.4 %collective-permute-start.36 = (bf16[128,2048]{1,0:T(8,128)(2,1)S(1)}, bf16[128,2048]{1,0:T(8,128)(2,1)S(1)}, u32[]{:S(2)}, u32[]{:S(2)}) collective-permute-start(bf16[128,2048]{1,0:T(8,128)(2,1)S(1)} %get-tuple-element.215.refs_1_.refs_8_), channel_id=1, source_target_pairs={{0,4},{1,5},{2,6},{3,7},{4,0},{5,1},{6,2},{7,3},{8,12},{9,13},{10,... | collective-permute-start | bytes 1572872 | tf_op jit(solution)/shard_map/ppermute | solution.py:45
  316.3 24.7 %collective-permute-start.37 = (bf16[128,2048]{1,0:T(8,128)(2,1)S(1)}, bf16[128,2048]{1,0:T(8,128)(2,1)S(1)}, u32[]{:S(2)}, u32[]{:S(2)}) collective-permute-start(bf16[128,2048]{1,0:T(8,128)(2,1)S(1)} %get-tuple-element.215.refs_1_.refs_8_), channel_id=1, source_target_pairs={{0,2},{1,7},{2,4},{3,1},{4,6},{5,3},{6,0},{7,5},{8,10},{9,15},{10,... | collective-permute-start | bytes 1572872 | tf_op jit(solution)/shard_map/ppermute | solution.py:45
  317.1 23.9 %collective-permute-start.38 = (bf16[128,2048]{1,0:T(8,128)(2,1)S(1)}, bf16[128,2048]{1,0:T(8,128)(2,1)S(1)}, u32[]{:S(2)}, u32[]{:S(2)}) collective-permute-start(bf16[128,2048]{1,0:T(8,128)(2,1)S(1)} %get-tuple-element.215.refs_1_.refs_8_), channel_id=1, source_target_pairs={{0,6},{1,3},{2,0},{3,5},{4,2},{5,7},{6,4},{7,1},{8,14},{9,11},{10,... | collective-permute-start | bytes 1572872 | tf_op jit(solution)/shard_map/ppermute | solution.py:45
  343.6 16.7 %collective-permute-start.56 = (bf16[4,2,2,3,16,704]{5,4,3,2,1,0:T(8,128)(2,1)S(1)}, bf16[4,2,2,3,16,704]{5,4,3,2,1,0:T(8,128)(2,1)S(1)}, u32[]{:S(2)}, u32[]{:S(2)}) collective-permute-start(bf16[4,2,2,3,16,704]{5,4,3,2,1,0:T(8,128)(2,1)S(1)} %copy-done.97), channel_id=1, source_target_pairs={{0,8},{1,73},{2,10},{3,75},{4,12},{5,77},{6,14},{7,79},{8,64},{9,1... | collective-permute-start | bytes 3244040 | tf_op jit(solution)/shard_map/ppermute | solution.py:45
  353.6 46.0 %collective-permute-start.46 = (bf16[128,2048]{1,0:T(8,128)(2,1)S(1)}, bf16[128,2048]{1,0:T(8,128)(2,1)S(1)}, u32[]{:S(2)}, u32[]{:S(2)}) collective-permute-start(bf16[128,2048]{1,0:T(8,128)(2,1)S(1)} %get-tuple-element.224), channel_id=1, source_target_pairs={{0,2},{1,7},{2,4},{3,1},{4,6},{5,3},{6,0},{7,5},{8,10},{9,15},{10,... | collective-permute-start | bytes 1572872 | tf_op jit(solution)/shard_map/ppermute | solution.py:45
  360.2 39.4 %collective-permute-start.44 = (bf16[128,2048]{1,0:T(8,128)(2,1)S(1)}, bf16[128,2048]{1,0:T(8,128)(2,1)S(1)}, u32[]{:S(2)}, u32[]{:S(2)}) collective-permute-start(bf16[128,2048]{1,0:T(8,128)(2,1)S(1)} %get-tuple-element.225), channel_id=1, source_target_pairs={{0,6},{1,3},{2,0},{3,5},{4,2},{5,7},{6,4},{7,1},{8,14},{9,11},{10,... | collective-permute-start | bytes 1572872 | tf_op jit(solution)/shard_map/ppermute | solution.py:45
  362.2 37.4 %collective-permute-start.42 = (bf16[128,2048]{1,0:T(8,128)(2,1)S(1)}, bf16[128,2048]{1,0:T(8,128)(2,1)}, u32[]{:S(2)}, u32[]{:S(2)}) collective-permute-start(bf16[128,2048]{1,0:T(8,128)(2,1)S(1)} %get-tuple-element.223), channel_id=1, source_target_pairs={{0,4},{1,5},{2,6},{3,7},{4,0},{5,1},{6,2},{7,3},{8,12},{9,13},{10,... | collective-permute-start | bytes 1572872 | tf_op jit(solution)/shard_map/ppermute | solution.py:45
  364.2 53.5 %collective-permute-start.57 = (bf16[4,2,2,3,16,704]{5,4,3,2,1,0:T(8,128)(2,1)}, bf16[4,2,2,3,16,704]{5,4,3,2,1,0:T(8,128)(2,1)}, u32[]{:S(2)}, u32[]{:S(2)}) collective-permute-start(bf16[4,2,2,3,16,704]{5,4,3,2,1,0:T(8,128)(2,1)} %add_convert_fusion.1), channel_id=1, source_target_pairs={{0,8},{1,73},{2,10},{3,75},{4,12},{5,77},{6,14},{7,79},{8,64},{9,1... | collective-permute-start | bytes 3244040 | tf_op jit(solution)/shard_map/ppermute | solution.py:45
  366.0 51.6 %collective-permute-start.55 = (bf16[4,2,2,3,16,704]{5,4,3,2,1,0:T(8,128)(2,1)}, bf16[4,2,2,3,16,704]{5,4,3,2,1,0:T(8,128)(2,1)}, u32[]{:S(2)}, u32[]{:S(2)}) collective-permute-start(bf16[4,2,2,3,16,704]{5,4,3,2,1,0:T(8,128)(2,1)} %get-tuple-element.164), channel_id=1, source_target_pairs={{0,72},{1,9},{2,74},{3,11},{4,76},{5,13},{6,78},{7,15},{8,0},{9,65... | collective-permute-start | bytes 3244040 | tf_op jit(solution)/shard_map/ppermute | solution.py:45
  415.5 29.8 %collective-permute-start.54 = (bf16[2,2,3,16,704]{4,3,2,1,0:T(8,128)(2,1)S(1)}, bf16[2,2,3,16,704]{4,3,2,1,0:T(8,128)(2,1)S(1)}, u32[]{:S(2)}, u32[]{:S(2)}) collective-permute-start(bf16[2,2,3,16,704]{4,3,2,1,0:T(8,128)(2,1)S(1)} %get-tuple-element.230), channel_id=1, source_target_pairs={{0,8},{1,73},{2,10},{3,75},{4,12},{5,77},{6,14},{7,79},{8,64},{9,1... | collective-permute-start | bytes 811016 | tf_op jit(solution)/shard_map/ppermute | solution.py:45
  415.6 29.7 %collective-permute-start.53 = (bf16[2,2,3,16,704]{4,3,2,1,0:T(8,128)(2,1)S(1)}, bf16[2,2,3,16,704]{4,3,2,1,0:T(8,128)(2,1)S(1)}, u32[]{:S(2)}, u32[]{:S(2)}) collective-permute-start(bf16[2,2,3,16,704]{4,3,2,1,0:T(8,128)(2,1)S(1)} %get-tuple-element.231), channel_id=1, source_target_pairs={{0,72},{1,9},{2,74},{3,11},{4,76},{5,13},{6,78},{7,15},{8,0},{9,65... | collective-permute-start | bytes 811016 | tf_op jit(solution)/shard_map/ppermute | solution.py:45
  426.6 15.4 %collective-permute-start.58 = (bf16[2,2,3,16,704]{4,3,2,1,0:T(8,128)(2,1)S(1)}, bf16[2,2,3,16,704]{4,3,2,1,0:T(8,128)(2,1)S(1)}, u32[]{:S(2)}, u32[]{:S(2)}) collective-permute-start(bf16[2,2,3,16,704]{4,3,2,1,0:T(8,128)(2,1)S(1)} %get-tuple-element.226), channel_id=1, source_target_pairs={{0,32},{1,33},{2,34},{3,35},{4,36},{5,37},{6,38},{7,39},{8,40},{9,... | collective-permute-start | bytes 811016 | tf_op jit(solution)/shard_map/ppermute | solution.py:45
  442.2 30.6 %collective-permute-start.70 = (bf16[2,3,16,704]{3,2,1,0:T(8,128)(2,1)S(1)}, bf16[2,3,16,704]{3,2,1,0:T(8,128)(2,1)S(1)}, u32[]{:S(2)}, u32[]{:S(2)}) collective-permute-start(bf16[2,3,16,704]{3,2,1,0:T(8,128)(2,1)S(1)} %get-tuple-element.251), channel_id=1, source_target_pairs={{0,4},{1,5},{2,6},{3,7},{4,0},{5,1},{6,2},{7,3},{8,12},{9,13},{10,... | collective-permute-start | bytes 405512 | tf_op jit(solution)/shard_map/ppermute | solution.py:45
  445.3 27.7 %collective-permute-start.68 = (bf16[2,3,16,704]{3,2,1,0:T(8,128)(2,1)S(1)}, bf16[2,3,16,704]{3,2,1,0:T(8,128)(2,1)S(1)}, u32[]{:S(2)}, u32[]{:S(2)}) collective-permute-start(bf16[2,3,16,704]{3,2,1,0:T(8,128)(2,1)S(1)} %get-tuple-element.250), channel_id=1, source_target_pairs={{0,2},{1,7},{2,4},{3,1},{4,6},{5,3},{6,0},{7,5},{8,10},{9,15},{10,... | collective-permute-start | bytes 405512 | tf_op jit(solution)/shard_map/ppermute | solution.py:45
  445.5 27.5 %collective-permute-start.69 = (bf16[2,3,16,704]{3,2,1,0:T(8,128)(2,1)S(1)}, bf16[2,3,16,704]{3,2,1,0:T(8,128)(2,1)S(1)}, u32[]{:S(2)}, u32[]{:S(2)}) collective-permute-start(bf16[2,3,16,704]{3,2,1,0:T(8,128)(2,1)S(1)} %slice_bitcast_fusion.16), channel_id=1, source_target_pairs={{0,6},{1,3},{2,0},{3,5},{4,2},{5,7},{6,4},{7,1},{8,14},{9,11},{10,... | collective-permute-start | bytes 405512 | tf_op jit(solution)/shard_map/ppermute | solution.py:45
  455.8 22.4 %collective-permute-start.66 = (bf16[128,2048]{1,0:T(8,128)(2,1)}, bf16[128,2048]{1,0:T(8,128)(2,1)}, u32[]{:S(2)}, u32[]{:S(2)}) collective-permute-start(bf16[128,2048]{1,0:T(8,128)(2,1)} %get-tuple-element.177), channel_id=1, source_target_pairs={{0,1},{1,0},{2,3},{3,2},{4,5},{5,4},{6,7},{7,6},{8,9},{9,8},{10,11... | collective-permute-start | bytes 1572872 | tf_op jit(solution)/shard_map/ppermute | solution.py:45
  455.8 24.4 %collective-permute-start.64 = (bf16[128,2048]{1,0:T(8,128)(2,1)}, bf16[128,2048]{1,0:T(8,128)(2,1)}, u32[]{:S(2)}, u32[]{:S(2)}) collective-permute-start(bf16[128,2048]{1,0:T(8,128)(2,1)} %get-tuple-element.175), channel_id=1, source_target_pairs={{0,1},{1,0},{2,3},{3,2},{4,5},{5,4},{6,7},{7,6},{8,9},{9,8},{10,11... | collective-permute-start | bytes 1572872 | tf_op jit(solution)/shard_map/ppermute | solution.py:45
  475.3 42.3 %collective-permute-start.75 = (bf16[2,4,3,16,704]{4,3,2,1,0:T(8,128)(2,1)S(1)}, bf16[2,4,3,16,704]{4,3,2,1,0:T(8,128)(2,1)S(1)}, u32[]{:S(2)}, u32[]{:S(2)}) collective-permute-start(bf16[2,4,3,16,704]{4,3,2,1,0:T(8,128)(2,1)S(1)} %get-tuple-element.239), channel_id=1, source_target_pairs={{0,64},{1,65},{2,66},{3,67},{4,68},{5,69},{6,70},{7,71},{8,72},{9,... | collective-permute-start | bytes 1622024 | tf_op jit(solution)/shard_map/ppermute | solution.py:45
  476.8 26.6 %collective-permute-start.81 = (bf16[4,2,2,16,576]{4,3,2,1,0:T(8,128)(2,1)}, bf16[4,2,2,16,576]{4,3,2,1,0:T(8,128)(2,1)S(1)}, u32[]{:S(2)}, u32[]{:S(2)}) collective-permute-start(bf16[4,2,2,16,576]{4,3,2,1,0:T(8,128)(2,1)} %get-tuple-element.199), channel_id=1, source_target_pairs={{0,8},{1,73},{2,10},{3,75},{4,12},{5,77},{6,14},{7,79},{8,64},{9,1... | collective-permute-start | bytes 884744 | tf_op jit(solution)/shard_map/ppermute | solution.py:45
  478.2 27.6 %collective-permute-start.80 = (bf16[4,2,2,16,576]{4,3,2,1,0:T(8,128)(2,1)}, bf16[4,2,2,16,576]{4,3,2,1,0:T(8,128)(2,1)S(1)}, u32[]{:S(2)}, u32[]{:S(2)}) collective-permute-start(bf16[4,2,2,16,576]{4,3,2,1,0:T(8,128)(2,1)} %get-tuple-element.198), channel_id=1, source_target_pairs={{0,72},{1,9},{2,74},{3,11},{4,76},{5,13},{6,78},{7,15},{8,0},{9,65... | collective-permute-start | bytes 884744 | tf_op jit(solution)/shard_map/ppermute | solution.py:45
  480.1 31.2 %collective-permute-start.79 = (bf16[4,2,2,16,576]{4,3,2,1,0:T(8,128)(2,1)S(1)}, bf16[4,2,2,16,576]{4,3,2,1,0:T(8,128)(2,1)S(1)}, u32[]{:S(2)}, u32[]{:S(2)}) collective-permute-start(bf16[4,2,2,16,576]{4,3,2,1,0:T(8,128)(2,1)S(1)} %copy-done.73), channel_id=1, source_target_pairs={{0,64},{1,65},{2,66},{3,67},{4,68},{5,69},{6,70},{7,71},{8,72},{9,... | collective-permute-start | bytes 884744 | tf_op jit(solution)/shard_map/ppermute | solution.py:45
  483.6 27.7 %collective-permute-start.74 = (bf16[4,2,2,16,576]{4,3,2,1,0:T(8,128)(2,1)S(1)}, bf16[4,2,2,16,576]{4,3,2,1,0:T(8,128)(2,1)S(1)}, u32[]{:S(2)}, u32[]{:S(2)}) collective-permute-start(bf16[4,2,2,16,576]{4,3,2,1,0:T(8,128)(2,1)S(1)} %copy-done.71), channel_id=1, source_target_pairs={{0,16},{1,49},{2,18},{3,51},{4,20},{5,53},{6,22},{7,55},{8,24},{9,... | collective-permute-start | bytes 884744 | tf_op jit(solution)/shard_map/ppermute | solution.py:45
  511.3 26.8 %collective-permute-start.67 = (bf16[128,2048]{1,0:T(8,128)(2,1)S(1)}, bf16[128,2048]{1,0:T(8,128)(2,1)S(1)}, u32[]{:S(2)}, u32[]{:S(2)}) collective-permute-start(bf16[128,2048]{1,0:T(8,128)(2,1)S(1)} %add_convert_fusion.2), channel_id=1, source_target_pairs={{0,2},{1,7},{2,4},{3,1},{4,6},{5,3},{6,0},{7,5},{8,10},{9,15},{10,... | collective-permute-start | bytes 1572872 | tf_op jit(solution)/shard_map/ppermute | solution.py:45
  514.0 24.1 %collective-permute-start.65 = (bf16[128,2048]{1,0:T(8,128)(2,1)S(1)}, bf16[128,2048]{1,0:T(8,128)(2,1)S(1)}, u32[]{:S(2)}, u32[]{:S(2)}) collective-permute-start(bf16[128,2048]{1,0:T(8,128)(2,1)S(1)} %add_convert_fusion.3), channel_id=1, source_target_pairs={{0,6},{1,3},{2,0},{3,5},{4,2},{5,7},{6,4},{7,1},{8,14},{9,11},{10,... | collective-permute-start | bytes 1572872 | tf_op jit(solution)/shard_map/ppermute | solution.py:45
  516.1 22.0 %collective-permute-start.63 = (bf16[128,2048]{1,0:T(8,128)(2,1)S(1)}, bf16[128,2048]{1,0:T(8,128)(2,1)S(1)}, u32[]{:S(2)}, u32[]{:S(2)}) collective-permute-start(bf16[128,2048]{1,0:T(8,128)(2,1)S(1)} %add_convert_fusion.4), channel_id=1, source_target_pairs={{0,4},{1,5},{2,6},{3,7},{4,0},{5,1},{6,2},{7,3},{8,12},{9,13},{10,... | collective-permute-start | bytes 1572872 | tf_op jit(solution)/shard_map/ppermute | solution.py:45
  517.8 39.8 %collective-permute-start.85 = (bf16[2,2,4,3,16,704]{5,4,3,2,1,0:T(8,128)(2,1)S(1)}, bf16[2,2,4,3,16,704]{5,4,3,2,1,0:T(8,128)(2,1)S(1)}, u32[]{:S(2)}, u32[]{:S(2)}) collective-permute-start(bf16[2,2,4,3,16,704]{5,4,3,2,1,0:T(8,128)(2,1)S(1)} %pad_maximum_fusion.refs_0_), channel_id=1, source_target_pairs={{0,16},{1,49},{2,18},{3,51},{4,20},{5,53},{6,22},{7,55},{8,24},{9,... | collective-permute-start | bytes 3244040 | tf_op jit(solution)/shard_map/ppermute | solution.py:45
  523.7 36.2 %collective-permute-start.86 = (bf16[2,2,4,3,16,704]{5,4,3,2,1,0:T(8,128)(2,1)S(1)}, bf16[2,2,4,3,16,704]{5,4,3,2,1,0:T(8,128)(2,1)}, u32[]{:S(2)}, u32[]{:S(2)}) collective-permute-start(bf16[2,2,4,3,16,704]{5,4,3,2,1,0:T(8,128)(2,1)S(1)} %pad_maximum_fusion.refs_0_), channel_id=1, source_target_pairs={{0,48},{1,17},{2,50},{3,19},{4,52},{5,21},{6,54},{7,23},{8,56},{9,... | collective-permute-start | bytes 3244040 | tf_op jit(solution)/shard_map/ppermute | solution.py:45
  557.6 72.0 %collective-permute-start.96 = (bf16[2,2,4,3,16,704]{5,4,3,2,1,0:T(8,128)(2,1)S(1)}, bf16[2,2,4,3,16,704]{5,4,3,2,1,0:T(8,128)(2,1)}, u32[]{:S(2)}, u32[]{:S(2)}) collective-permute-start(bf16[2,2,4,3,16,704]{5,4,3,2,1,0:T(8,128)(2,1)S(1)} %collective-permute-done.85.refs_1_), channel_id=1, source_target_pairs={{0,16},{1,49},{2,18},{3,51},{4,20},{5,53},{6,22},{7,55},{8,24},{9,... | collective-permute-start | bytes 3244040 | tf_op jit(solution)/shard_map/ppermute | solution.py:45
  575.6 37.1 %collective-permute-start.92 = (bf16[2,4,16,576]{3,2,1,0:T(8,128)(2,1)S(1)}, bf16[2,4,16,576]{3,2,1,0:T(8,128)(2,1)S(1)}, u32[]{:S(2)}, u32[]{:S(2)}) collective-permute-start(bf16[2,4,16,576]{3,2,1,0:T(8,128)(2,1)S(1)} %get-tuple-element.257), channel_id=1, source_target_pairs={{0,64},{1,65},{2,66},{3,67},{4,68},{5,69},{6,70},{7,71},{8,72},{9,... | collective-permute-start | bytes 442376 | tf_op jit(solution)/shard_map/ppermute | solution.py:45
  (152 other events, 1737.1 us)
Sparse Core Ops, SparseCore 0:
  44.5 31.9 all-gather.7
  78.8 52.4 all-gather.11
  133.0 53.0 all-gather.9
  298.3 50.3 reduce-scatter.1
  474.4 34.6 all-gather.13

commit v3 on v2

--- a/solution.py
+++ b/solution.py
@@ -192,25 +192,24 @@
     )
 
 
-def place_attn_kernel(slot, xs, halves, *refs):
-    pieces, (qkv_ref, out_ref) = refs[:8], refs[8:]
-    for e in range(2):
+def place_attn_kernel(slot, xs, halves, own_ref, other_ref, qkv_ref, out_ref):
+    for e, ref in enumerate((own_ref, other_ref)):
         for r in range(4):
-            piece = pieces[4 * e + r][0]
+            piece = ref[r, 0]
             rows = at_rows(xs[r] * 32, 32)
             out_ref[halves[e], rows, :] = piece[:, :QUERY]
             qkv_ref[halves[e], 0, rows, :] = piece[:, QUERY:]
 
 
-def place_attn(slot, xs, halves, pieces):
+def place_attn(slot, xs, halves, own, other):
     qkv, out = call(
         place_attn_kernel, (slot, xs, halves), (8,),
-        [pl.BlockSpec((1, 32, PACK), lambda i, *_: (i, 0, 0))] * 8,
+        [pl.BlockSpec((4, 1, 32, PACK), lambda i, *_: (0, i, 0, 0))] * 2,
         [
             pl.BlockSpec((2, 1, 128, QKV), lambda i, slot, *_: (0, slot[i], 0, 0)),
             pl.BlockSpec((2, 128, QUERY), lambda i, *_: (0, 0, i)),
         ],
-        [sds((2, 8, 128, QKV)), sds((2, 128, D))], [], 2, tuple(pieces),
+        [sds((2, 8, 128, QKV)), sds((2, 128, D))], [], 2, (own, other),
     )
     return qkv.reshape(D, QKV), out.reshape(QUERY, D)
 
@@ -522,11 +521,11 @@
     return [x_first] * 4 + [y_own] * 2 + [y_other] * 2, [sds((4, 2, 2) + tail)] * 8
 
 
-def write_grads(outs, xs, yhs, core, write, first_rows=None):
+def write_grads(outs, xs, yhs, core, write):
     half, p = pl.program_id(0), pl.program_id(1)
 
-    def go(pos, r, ref, first=False):
-        inside = yhs[2 * half + pos] * 64 + (first_rows(r) if first and first_rows else xs[r] * 16)
+    def go(pos, r, ref):
+        inside = yhs[2 * half + pos] * 64 + xs[r] * 16
         for rc in range(2):
             write(ref.at[rc], inside, jnp.abs(core[0] - rc), rc)
 
@@ -534,7 +533,7 @@
     def _():
         for r in range(4):
             for pos in range(2):
-                go(pos, r, outs[r].at[pos, 0], True)
+                go(pos, r, outs[r].at[pos, 0])
 
     for each in range(2):
 
@@ -545,32 +544,31 @@
                     go(pos, r, outs[4 + 2 * each + pos].at[r, 0])
 
 
-def mlp_grads_kernel(column, xs, yhs, core, nat, *refs):
-    tokens, (g_ref, da_ref, dc_ref, z_ref), outs, (turned, grads) = refs[:8], refs[8:12], refs[12:17], refs[17:]
+def mlp_grads_kernel(column, yhs, core, nat, *refs):
+    tokens, (g_ref, da_ref, dc_ref, z_ref), out_ref, (turned, grads) = refs[:8], refs[8:12], refs[12], refs[13:]
+    half = pl.program_id(0)
     rows = jnp.concatenate([ref[...] for ref in tokens], axis=0).T
     grads[0] = dot(rows, da_ref[...])
     grads[1] = dot(rows, dc_ref[...])
     for r in range(8):
         turned[:, TOK * r : TOK * (r + 1)] = g_ref[pl.ds(pl.multiple_of(nat[r] * TOK, TOK), TOK), :].T
     grads[2] = dot(turned[...], z_ref[...])
-
-    def write(ref, inside, which, rc):
-        for m in range(3):
-            ref[m] = grads[m, at_rows(which * 128 + inside, 16), :].astype(BF)
-
-    write_grads([outs[0].at[r] for r in range(4)] + list(outs[1:]), xs, yhs, core, write, lambda r: 16 * r)
-
-
-def mlp_grads(column, xs, yhs, core, nat, tokens, g, da, dc, z):
+    for pos in range(2):
+        for rc in range(2):
+            start = jnp.abs(core[0] - rc) * 128 + yhs[2 * half + pos] * 64
+            for r in range(4):
+                for m in range(3):
+                    out_ref[r, pos, 0, rc, m] = grads[m, at_rows(start + 16 * r, 16), :].astype(BF)
+
+
+def mlp_grads(column, yhs, core, nat, tokens, g, da, dc, z):
     col = lambda h, p, column, *_: (0, column[4 * h + p])
     hidden = pl.BlockSpec((8 * TOK, WIDE), lambda h, p, *_: (0, 0))
-    tail = (3, 16, WIDE)
-    specs, shapes = grads_specs(tail)
-    x_first = pl.BlockSpec((4, 2, 1, 2) + tail, lambda h, p, *_: (0, h, jnp.minimum(p, 1), 0, 0, 0, 0))
     return call(
-        mlp_grads_kernel, (column, xs, yhs, core, nat), (2, 4),
+        mlp_grads_kernel, (column, yhs, core, nat), (2, 4),
         [pl.BlockSpec((TOK, 256), col)] * 8 + [pl.BlockSpec((8 * TOK, 256), col), hidden, hidden, hidden],
-        [x_first] + specs[4:], [sds((4, 4, 2, 2) + tail)] + shapes[4:],
+        pl.BlockSpec((4, 2, 1, 2, 3, 16, WIDE), lambda h, p, *_: (0, h, p, 0, 0, 0, 0)),
+        sds((4, 4, 4, 2, 3, 16, WIDE)),
         [pltpu.VMEM((256, 8 * TOK), BF), pltpu.VMEM((3, 256, WIDE), F32)],
         17, tuple(tokens) + (g, da, dc, z),
     )
@@ -724,17 +722,11 @@
     ])
 
 
-    def gather_tokens(rows):
-        own, first, second, third = ring_gather(rows, "z")
-        parts = [own, swap(own), first, swap(first), second, swap(second)]
-        return parts + [third, swap(after(third, first, second))]
-
     def give(group, total):
-        value = total.astype(BF)
-        return across(value, "z") if group == 3 else step(value, "z", -1 if group == 1 else 1)
+        return across(total, "z") if group == 3 else step(total, "z", -1 if group == 1 else 1)
 
     def scatter_tokens(mine, peer):
-        sums = [add(a, swap(b)) for a, b in zip(mine, peer)]
+        sums = [add(a, swap(b)).astype(BF) for a, b in zip(mine, peer)]
         return add(sums[0], *[give(g, sums[g]) for g in (3, 1, 2)])
 
     gain_one = attn_gain.astype(F32)
@@ -751,12 +743,6 @@
         far = jnp.stack([mine[3], got[3]], axis=1)
         return jnp.concatenate(exchange_z(own, before, forward, far), axis=1)
 
-    def spread(part):
-        pieces = list(ring_gather(part, "x"))
-        there = [step(pieces[0], "y", 1)]
-        there += [step(piece, "y", 1) for piece in after(pieces[1:], pieces[1])]
-        return pieces + there
-
     normed_own = (rows_in * scale_attn * gain_one).astype(BF)
     out_rows = lax.dynamic_slice_in_dim(output_weight, x * 32, 32, axis=0)
     out_part = send(
@@ -770,13 +756,14 @@
         after(normed_own, packs), "blk", axis=0, tiled=True, axis_index_groups=ZC_GROUPS
     )
     attn_part = jnp.concatenate([out_part, packs[3, :, :, :QKV]], axis=-1)
-    attn_pieces = spread(attn_part)
-    w_qkv, w_out = place_attn(slot, xs, halves, attn_pieces)
+    attn_half_rows = jnp.stack(ring_gather(attn_part, "x"))
+    attn_other_rows = step(attn_half_rows, "y", 1)
+    w_qkv, w_out = place_attn(slot, xs, halves, attn_half_rows, attn_other_rows)
     mlp_half_rows = lax.all_gather(packs[:3], "batch", axis=0, axis_index_groups=X_GROUPS)
     w_mlp = place_mlp(slot, halves, mlp_half_rows, step(mlp_half_rows, "y", 1))
 
     grad_rows = lax.all_gather(
-        after(cotangent[0], attn_pieces[7]), "blk", axis=0, tiled=True, axis_index_groups=ZC_GROUPS
+        after(cotangent[0], attn_other_rows), "blk", axis=0, tiled=True, axis_index_groups=ZC_GROUPS
     )
 
 
@@ -798,99 +785,101 @@
     values = jnp.where(usable, jnp.where(first_core, kv_other, kv_mine), 0)
     attended, sums, got = [None] * 4, [None] * 4, [None] * 4
     for g in (3, 1, 2, 0):
-        at = after(query_place, mlp_half_rows, got[3]) if g == 0 else query_place
+        at = after(query_place, mlp_half_rows, *sums[1:]) if g == 0 else query_place
         attended[g], mine, peer = attend(g, at, key_slot, queries, keys, values, w_out)
-        sums[g] = add(mine, swap(peer))
+        sums[g] = add(mine, swap(peer)).astype(BF)
         if g:
             got[g] = give(g, sums[g])
     residual = rows_in + add(sums[0], *got[1:])
     scale_mlp = rms_scale(residual)
-    mlp_parts = gather_tokens((residual * scale_mlp * gain_two).astype(BF))
-
-
-    order = [6, 7, 2, 3, 4, 5, 0, 1]
-    mlp_parts = [mlp_parts[r] for r in order]
-    mlp_chunk = jnp.stack([chunk[r] for r in order])
-    kept, sums, got, at = None, [None] * 4, [None] * 4, mlp_chunk
+    own, first, second, third = ring_gather((residual * scale_mlp * gain_two).astype(BF), "z")
+    mlp_parts = [own, swap(own), first, swap(after(first, w_mlp)), second, swap(after(second, w_mlp)), third, None]
+
+
+    kept, sums, got, at = None, [None] * 4, [None] * 4, chunk
     for part in range(2):
         kept, result = mlp_half(part, at, mlp_parts[4 * part : 4 * part + 4], grad_rows, w_mlp, kept)
         swapped = [swap(peer) for peer in result[1::2]]
-        for g, mine, peer in zip(((3, 1), (2, 0))[part], result[::2], swapped):
-            sums[g] = add(mine, peer)
+        for each in range(2):
+            g = 2 * part + each
+            sums[g] = add(result[2 * each], swapped[each]).astype(BF)
             if g:
                 got[g] = give(g, sums[g])
-        at = after(mlp_chunk, *swapped)
+        if part == 0:
+            mlp_parts[7] = swap(after(third, kept[0]))
+        at = after(chunk, *swapped)
     hidden, gate_grad_rows, up_grad_rows = kept
-    mlp_outs = mlp_grads(
-        column, xs, yhs, core, after(mlp_chunk, got[3], got[1]), mlp_parts, grad_rows,
-        gate_grad_rows, up_grad_rows, hidden,
-    )
-    normed_grad = after(add(sums[0], *got[1:]), mlp_outs[0])
-    mlp_low = lax.psum_scatter(mlp_outs[0], "batch", scatter_dimension=0, axis_index_groups=X_GROUPS)
-    high_far = step(mlp_outs[2], "y", 1)
-    high_after = step(mlp_outs[3], "y", -1)
+    mlp_sums = mlp_grads(
+        column, yhs, core, after(at, got[1], sums[2], sums[3]), mlp_parts, grad_rows, gate_grad_rows, up_grad_rows, hidden
+    )
+    normed_grad = add(sums[0], *got[1:])
+    mlp_sums = after(mlp_sums, got[2], got[3])
+    mlp_sums = lax.psum_scatter(mlp_sums, "batch", scatter_dimension=0, axis_index_groups=X_GROUPS)
 
     residual_grad = cotangent[0].astype(F32) + norm_back(residual, scale_mlp, gain_two, normed_grad)
     mlp_gain_part = jnp.sum(normed_grad * residual * scale_mlp, axis=0)
-    branch_parts = gather_tokens(residual_grad.astype(BF))
-    high_before = step(add(after(mlp_outs[4], branch_parts[7]), high_far).astype(BF), "y", 1)
-    branch = dot_last(after(hidden, branch_parts[7]), w_mlp[2]).astype(BF).reshape(8, TOK, D)
-    branch = [branch[order.index(r)] for r in range(8)]
-    layer_out = (residual + scatter_tokens(branch[::2], branch[1::2])).astype(BF)[None]
+    own, first, second, third = ring_gather(residual_grad.astype(BF), "z")
 
 
     def resplit_back(part):
         got = exchange_z(part[0], part[1], part[2], part[3])
         mine = jnp.stack([each[0] for each in got])
         other = swap(jnp.stack([got[p][1] for p in (0, 2, 1, 3)]))
-        return jnp.stack([mine, other])
-
-
-    query_grad_rows, sums = [], ()
-    for start, stop in ((0, 2), (2, 6), (6, 8)):
-        at = after(query_place, mlp_low) if stop == 8 else query_place
-        rows, *sums = attend_back(
-            start, branch_parts[start:stop], sums, stop == 8,
-            at, key_slot, core, key_count, queries, w_out, keys, values, keys.T,
+        return jnp.stack([mine, other]), other
+
+
+    def back(start, parts, sums, last):
+        return attend_back(
+            start, parts, sums, last, query_place, key_slot, core, key_count, queries, w_out, keys, values, keys.T
         )
-        query_grad_rows.append(rows)
-    kv_keep, kv_give = sums
-    kv_terms = add(kv_keep, swap(after(kv_give, layer_out)))
+
+    branch_parts = [own, swap(own)]
+    rows_0, *sums = back(0, branch_parts, (), False)
+    branch_parts += [first, swap(after(first, rows_0)), second, swap(after(second, rows_0))]
+    rows_1, *sums = back(2, branch_parts[2:], sums, False)
+    branch_parts += [third, swap(after(third, rows_1))]
+    rows_2, kv_keep, kv_give = back(6, branch_parts[6:], sums, True)
+    query_grad_rows = [rows_0, rows_1, rows_2]
+    kv_terms = add(kv_keep, swap(kv_give))
     half_rows = 8 * TOK
-    kv_grad_rows = add(kv_terms[:half_rows], to_half(kv_terms[half_rows:].astype(BF))).astype(BF)
-
-    low = after(mlp_low, kv_keep)
-    low = ring_scatter(low[0], low[2], low[3], low[1], "y").astype(BF)
-    high = add(mlp_outs[1], high_after, after(high_before, kv_keep)).astype(BF)
-    high = ring_scatter(high[0], high[1], high[2], high[3], "x").astype(BF)
-    kv_grad_rows = after(kv_grad_rows, low, high)
-    mlp_sums = resplit_back([low[0], low[1], high[0], high[1]])
+    kv_half = to_half(kv_terms[half_rows:].astype(BF))
+    kv_grad_rows = add(kv_terms[:half_rows], kv_half).astype(BF)
+    mlp_sums = after(mlp_sums, kv_half)
+    mlp_sums = ring_scatter(mlp_sums[0], mlp_sums[2], mlp_sums[3], mlp_sums[1], "y").astype(BF)
+    mlp_rows = mlp_sums
+    mlp_sums, mlp_swapped = resplit_back(mlp_sums)
+    branch = dot_last(after(hidden, mlp_swapped), w_mlp[2]).astype(BF).reshape(8, TOK, D)
+    layer_out = (residual + scatter_tokens(branch[::2], branch[1::2])).astype(BF)[None]
 
     attn_partial = project_back(query_grad_rows, kv_grad_rows, w_qkv)
     attn_outs, attn_gain_part = attn_grads(
         column, xs, yhs, core, halves, chunk, normed_attn, branch_parts, attended, query_grad_rows, kv_grad_rows, w_qkv
     )
     gain_grads = jnp.stack([attn_gain_part / gain_one, mlp_gain_part])
-    gain_grads = jnp.sum(lax.all_gather(jnp.pad(gain_grads, ((0, 6), (0, 0))), "blk"), axis=0)
-
-    attn_outs = after(attn_outs, mlp_sums)
-    mlp_sums = jnp.stack([mlp_sums, across(mlp_sums, "y")])
+    gain_grads = lax.all_gather(jnp.pad(gain_grads, ((0, 6), (0, 0))), "blk")
+    gain_grads = jnp.sum(after(gain_grads, mlp_swapped), axis=0)
+
+    mlp_across = across(mlp_sums, "y")
+    mlp_sums = ring_gather(jnp.stack([mlp_sums, mlp_across]), "x", True)
+    attn_partial = after(attn_partial, mlp_rows)
     normed_attn_grad = scatter_tokens(attn_partial[::2], attn_partial[1::2])
-    low = after(ring_scatter(*attn_outs[:4], "x").astype(BF), normed_attn_grad, mlp_sums)
-    high = after(
-        ring_scatter(attn_outs[4], attn_outs[6], attn_outs[7], attn_outs[5], "y").astype(BF), normed_attn_grad, mlp_sums
-    )
-    low = ring_scatter(low[0], low[2], low[3], low[1], "y").astype(BF)
-    high = ring_scatter(high[0], high[1], high[2], high[3], "x").astype(BF)
-    mlp_sums = ring_gather(mlp_sums, "x", True)
-    attn_sums = after(jnp.concatenate([low, high]), mlp_sums[1], mlp_sums[2], gain_grads)
-    gain_grads = jnp.sum(lax.all_gather(gain_grads, "batch"), axis=0)[:2]
+    tied = (mlp_swapped,)
+    low = after(ring_scatter(*attn_outs[:4], "x").astype(BF), *tied)
+    attn_outs[4:] = after(attn_outs[4:], mlp_rows)
+    high = after(ring_scatter(attn_outs[4], attn_outs[6], attn_outs[7], attn_outs[5], "y").astype(BF), *tied)
+    gain_grads = lax.all_gather(jnp.pad(gain_grads, ((0, 8), (0, 0))), "batch")
+    low = ring_scatter(after(low[0], mlp_across), low[2], low[3], low[1], "y").astype(BF)
+    high = ring_scatter(after(high[0], mlp_across), high[1], high[2], high[3], "x").astype(BF)
+    low, high = after((low, high), mlp_across, normed_attn_grad)
+    attn_sums = jnp.concatenate([low, high])
     out_sums = send(
         attn_sums[..., :QUERY], lambda yh, x, yl, z, c: (yh, x, z // 2, 2 * (z % 2) + c, yl)
     )
-    qkv_sums = resplit_back(attn_sums[..., QUERY:])
+    qkv_sums, _ = resplit_back(attn_sums[..., QUERY:])
     attn_sums = jnp.concatenate([out_sums.reshape(2, 4, 16, QUERY), qkv_sums], axis=-1)
-    attn_sums = ring_gather(jnp.stack([attn_sums, across(attn_sums, "y")]), "x")
+    attn_across = after(across(attn_sums, "y"), mlp_sums[1])
+    attn_sums = ring_gather(jnp.stack([attn_sums, attn_across]), "x")
+    gain_grads = jnp.sum(after(gain_grads, attn_across), axis=0)[:2]
     gate_grad, up_grad, down_grad = finish_mlp(spots, xs, yhs, core, mlp_sums)
     query_grad, key_grad, value_grad, output_grad = finish_attn(spots, xs, yhs, core, attn_sums)
     tokens_grad = (

time: 649 us -> 598 us (0.921)
  blocking collectives: 36.1 us -> 0 us
  starting transfers between devices: 129 us -> 95.4 us
  waiting for transfers between devices: 228 us -> 245 us
    all_gather x1 -> x0, blocking collectives: 36.1 us -> none  [on_device(): gain_grads = jnp.sum(lax.all_gather(gain_grads, 'batch'), axis=0)[:2]]
    ppermute x97 -> x88, starting transfers between devices: 129 us -> 95 us  [send(): return lax.ppermute(value, BOTH, pairs)]
    all_gather x1, waiting for transfers between devices: 9.97 us -> 21.1 us  [on_device(): lax.all_gather(packs[:3], 'batch', axis=0, axis_index_groups=X_GROUPS)]
    unnamed x200 -> x160, local copies, waits for them, and re-layouts: 34.4 us -> 23.7 us
    reduce_scatter x1, waiting for transfers between devices: 0.01 us -> 10.3 us  [on_device(): lax.psum_scatter(mlp_sums, 'batch', scatter_dimension=0, axis_index_group...]
    ppermute x97 -> x88, waiting for transfers between devices: 218 us -> 213 us  [send(): return lax.ppermute(value, BOTH, pairs)]
    convert_element_type x20 -> x17, other arithmetic: 14.4 us -> 13 us  [the longest x4 4.23 us: scatter_tokens(): sums = [add(a, swap(b)).astype(BF) for a, b in zip(mine, peer)]]
  transfers between devices with their start and end apart: 102 -> 94, of which waited for: 44 -> 45; matrix products, arithmetic and copies ran while one was open for 6% -> 8% of each run, Pallas kernels for 18% -> 22%
where the time goes in v3:
time: 598 us; the launch traced here: 587 us
  waiting for transfers between devices  245 us (41%)
  Pallas kernels  156 us (26%)
  starting transfers between devices  95.4 us (16%)
  local copies, waits for them, and re-layouts  39 us (7%)
  other arithmetic  29.7 us (5%)
  between operations  16 us (3%)
    ppermute x88, waiting for transfers between devices, send(): return lax.ppermute(value, BOTH, pairs)  213 us
    pallas_call x18, Pallas kernels, call(): pl.pallas_call(body, grid_spec=pltpu.PrefetchScalarGridSpec(num_scalar_pr...  156 us
    ppermute x88, starting transfers between devices, send(): return lax.ppermute(value, BOTH, pairs)  95 us
    unnamed x160, local copies, waits for them, and re-layouts  23.7 us
    all_gather x1, waiting for transfers between devices, on_device(): lax.all_gather(packs[:3], 'batch', axis=0, axis_index_groups=X_GROUPS)  21.1 us
  transfers between devices with their start and end apart: 94, of which 45 were waited for; matrix products, arithmetic and copies ran while one was open for 8% of the time, Pallas kernels for 22%

profile of v3, /device:TPU:24, one launch (start us, length us, event | category | flops | bytes accessed | tf_op | source)
XLA Modules:
  0.0 586.6 jit_solution(10665551919076657051)
XLA Ops:
  12.9 4.0 shard_map.212
  28.8 4.3 collective-permute-done.1
  33.1 10.1 %collective-permute-done.2 = bf16[4,2,32,704]{3,2,0,1:T(8,128)(2,1)S(1)} collective-permute-done((bf16[4,2,32,704]{3,2,0,1:T(8,128)(2,1)S(1)}, bf16[4,2,32,704]{3,2,0,1:T(8,128)(2,1)S(1)}, u32[]{:S(2)}, u32[]{:S(2)}) %collective-permute-start.2) | collective-permute-done | bytes 360480 | tf_op jit(solution)/shard_map/ppermute | solution.py:45
  48.6 4.3 collective-permute-done.4
  58.1 12.3 %collective-permute-done.6 = bf16[8,32,576]{2,1,0:T(8,128)(2,1)S(1)} collective-permute-done((bf16[8,32,576]{2,1,0:T(8,128)(2,1)S(1)}, bf16[8,32,576]{2,1,0:T(8,128)(2,1)S(1)}, u32[]{:S(2)}, u32[]{:S(2)}) %collective-permute-start.6) | collective-permute-done | bytes 294944 | tf_op jit(solution)/shard_map/ppermute | solution.py:45
  72.5 17.6 %collective-permute-done.8.other_ref = bf16[4,8,32,576]{3,2,1,0:T(8,128)(2,1)S(1)} collective-permute-done((bf16[4,8,32,576]{3,2,1,0:T(8,128)(2,1)S(1)}, bf16[4,8,32,576]{3,2,1,0:T(8,128)(2,1)S(1)}, u32[]{:S(2)}, u32[]{:S(2)}) %collective-permute-start.8) | collective-permute-done | bytes 1179680 | tf_op jit(solution)/shard_map/ppermute | solution.py:45
  97.7 6.1 %shard_map.214 = (bf16[1024,256]{1,0:T(8,128)(2,1)S(1)}, bf16[2,1024,64]{2,1,0:T(8,128)(2,1)S(1)}) custom-call(s32[8]{0:T(128)S(1)} %stack.212.chunk.nat, bf16[1024,2048]{1,0:T(8,128)(2,1)} %all-gather.9.cloned.1.call-done.refs_0_.refs_1_.refs_2_.refs_3_.refs_4_.refs_5_.refs_6_.refs_7_, ...), custom_call_target="tpu_custom_call" | custom-call | flops 1000 | bytes 1500000 | tf_op jit(solution)/shard_map/pallas_call | solution.py:134
  104.3 6.4 %collective-permute-done.9 = bf16[2,1024,64]{1,2,0:T(8,128)(2,1)S(1)} collective-permute-done((bf16[2,1024,64]{1,2,0:T(8,128)(2,1)S(1)}, bf16[2,1024,64]{1,2,0:T(8,128)(2,1)S(1)}, u32[]{:S(2)}, u32[]{:S(2)}) %collective-permute-start.9) | collective-permute-done | bytes 262176 | tf_op jit(solution)/shard_map/ppermute | solution.py:45
  111.1 21.1 %all-gather.13.cloned.1.call-done = bf16[12,8,32,704]{3,2,1,0:T(8,128)(2,1)} async-done(((bf16[3,8,32,704]{3,2,1,0:T(8,128)(2,1)}), bf16[12,8,32,704]{3,2,1,0:T(8,128)(2,1)}) %all-gather.13.cloned.1.call-update) | async-done | bytes 4325392 | tf_op jit(solution)/shard_map/all_gather | solution.py:762
  133.4 4.6 shard_map.217
  138.7 8.8 %shard_map.216 = (bf16[256,256]{1,0:T(8,128)(2,1)S(1)}, bf16[128,2048]{1,0:T(8,128)(2,1)S(1)}, bf16[128,2048]{1,0:T(8,128)(2,1)S(1)}) custom-call(s32[8]{0:T(128)S(1)} %bitcast.214, s32[16]{0:T(128)S(1)} %select_reduce_fusion.1.key_slot, bf16[1024,256]{1,0:T(8,128)(2,1)S(1)} %get-tuple-element.116.q_ref.refs_0_, ...), custom_call_target="tpu_custom_call" | custom-call | flops 1000 | bytes 1800000 | tf_op jit(solution)/shard_map/pallas_call | solution.py:134
  148.8 4.3 shard_map.215
  153.4 5.2 collective-permute-start.17
  159.0 3.3 collective-permute-start.15
  162.3 6.6 %shard_map.218 = (bf16[256,256]{1,0:T(8,128)(2,1)S(1)}, bf16[128,2048]{1,0:T(8,128)(2,1)S(1)}, bf16[128,2048]{1,0:T(8,128)(2,1)S(1)}) custom-call(s32[8]{0:T(128)S(1)} %bitcast.216, s32[16]{0:T(128)S(1)} %select_reduce_fusion.1.key_slot, bf16[1024,256]{1,0:T(8,128)(2,1)S(1)} %get-tuple-element.116.q_ref.refs_0_, ...), custom_call_target="tpu_custom_call" | custom-call | flops 1000 | bytes 1800000 | tf_op jit(solution)/shard_map/pallas_call | solution.py:134
  169.0 7.6 %collective-permute-done.17 = bf16[128,2048]{1,0:T(8,128)(2,1)S(1)} collective-permute-done((bf16[128,2048]{1,0:T(8,128)(2,1)S(1)}, bf16[128,2048]{1,0:T(8,128)(2,1)S(1)}, u32[]{:S(2)}, u32[]{:S(2)}) %collective-permute-start.17) | collective-permute-done | bytes 524320 | tf_op jit(solution)/shard_map/ppermute | solution.py:45
  176.6 11.0 %collective-permute-done.16 = bf16[128,2048]{1,0:T(8,128)(2,1)S(1)} collective-permute-done((bf16[128,2048]{1,0:T(8,128)(2,1)S(1)}, bf16[128,2048]{1,0:T(8,128)(2,1)S(1)}, u32[]{:S(2)}, u32[]{:S(2)}) %collective-permute-start.16) | collective-permute-done | bytes 524320 | tf_op jit(solution)/shard_map/ppermute | solution.py:45
  191.7 8.4 %shard_map.219 = bf16[3,2,8,128,704]{4,3,2,1,0:T(8,128)(2,1)} custom-call(s32[8]{0:T(128)S(1)} %stack.223.slot, s32[2]{0:T(128)S(1)} %pad_add_fusion.2.halves, bf16[4,3,8,32,704]{4,3,2,1,0:T(8,128)(2,1)S(1)} %bitcast.212, bf16[4,3,8,32,704]{4,3,2,1,0:T(8,128)(2,1)} %collective-permute-done.20.other_ref), custom_call_target="tpu_custom_call" | custom-call | flops 1000 | bytes 1800000 | tf_op jit(solution)/shard_map/pallas_call | solution.py:134
  200.1 4.1 collective-permute-done.19.refs_2_
  206.4 15.9 %shard_map.220 = (bf16[1024,704]{1,0:T(8,128)(2,1)S(1)}, bf16[1024,704]{1,0:T(8,128)(2,1)}, bf16[1024,704]{1,0:T(8,128)(2,1)}, bf16[128,2048]{1,0:T(8,128)(2,1)S...) custom-call(s32[8]{0:T(128)S(1)} %stack.212.chunk.nat, ...), custom_call_target="tpu_custom_call" | custom-call | flops 1000 | bytes 4800000 | tf_op jit(solution)/shard_map/pallas_call | solution.py:134
  227.2 15.9 %shard_map.221 = (bf16[1024,704]{1,0:T(8,128)(2,1)S(1)}, bf16[1024,704]{1,0:T(8,128)(2,1)}, bf16[1024,704]{1,0:T(8,128)(2,1)}, bf16[128,2048]{1,0:T(8,128)(2,1)S...) custom-call(s32[8]{0:T(128)S(1)} %stack.212.chunk.nat, ...), custom_call_target="tpu_custom_call", output_to_operand_aliasing={{0}: (10, {}), {1}: (11, {}), {2}: (12, {})} | custom-call | flops 1000 | bytes 4800000 | tf_op jit(solution)/shard_map/pallas_call | solution.py:134
  250.2 9.0 %collective-permute-done.30 = bf16[128,2048]{1,0:T(8,128)(2,1)} collective-permute-done((bf16[128,2048]{1,0:T(8,128)(2,1)}, bf16[128,2048]{1,0:T(8,128)(2,1)}, u32[]{:S(2)}, u32[]{:S(2)}) %collective-permute-start.30) | collective-permute-done | bytes 524320 | tf_op jit(solution)/shard_map/ppermute | solution.py:45
  261.6 17.7 %shard_map.222 = bf16[4,4,4,2,3,16,704]{6,5,4,3,2,1,0:T(8,128)(2,1)} custom-call(s32[8]{0:T(128)S(1)} %stack.244.column, s32[4]{0:T(128)S(1)} %pad_add_fusion.3.yhs, s32[1]{0:T(128)} %bitcast.15.core, s32[8]{0:T(128)S(1)} %stack.212.chunk.nat, bf16[128,2048]{1,0:T(8,128)(2,1)S(1)} %multiply_convert_fusion.refs_0_, ...), custom_call_target="tpu_custom_call" | custom-call | flops 1000 | bytes 5100000 | tf_op jit(solution)/shard_map/pallas_call | solution.py:134
  287.5 9.0 %shard_map.223 = (bf16[256,256]{1,0:T(8,128)(2,1)S(1)}, f32[2048,64]{1,0:T(8,128)S(1)}, f32[2048,64]{1,0:T(8,128)S(1)}) custom-call(s32[8]{0:T(128)S(1)} %bitcast.217, s32[16]{0:T(128)S(1)} %select_reduce_fusion.1.key_slot, s32[1]{0:T(128)} %bitcast.15.core, s32[16]{0:T(128)S(1)} %get-tuple-element.215.used, ...), custom_call_target="tpu_custom_call" | custom-call | flops 1000 | bytes 2400000 | tf_op jit(solution)/shard_map/pallas_call | solution.py:134
  303.0 19.6 %shard_map.224 = (bf16[512,256]{1,0:T(8,128)(2,1)S(1)}, f32[2048,64]{1,0:T(8,128)S(1)}, f32[2048,64]{1,0:T(8,128)}) custom-call(s32[8]{0:T(128)S(1)} %bitcast.218, s32[16]{0:T(128)S(1)} %select_reduce_fusion.1.key_slot, s32[1]{0:T(128)} %bitcast.15.core, s32[16]{0:T(128)S(1)} %get-tuple-element.215.used, ...), custom_call_target="tpu_custom_call" | custom-call | flops 1000 | bytes 4800000 | tf_op jit(solution)/shard_map/pallas_call | solution.py:134
  324.6 7.6 %shard_map.225 = (bf16[256,256]{1,0:T(8,128)(2,1)S(1)}, bf16[2048,64]{1,0:T(8,128)(2,1)S(1)}, bf16[2048,64]{1,0:T(8,128)(2,1)S(1)}) custom-call(s32[8]{0:T(128)S(1)} %bitcast.219, s32[16]{0:T(128)S(1)} %select_reduce_fusion.1.key_slot, s32[1]{0:T(128)} %bitcast.15.core, s32[16]{0:T(128)S(1)} %get-tuple-element.215.used, ...), custom_call_target="tpu_custom_call" | custom-call | flops 1000 | bytes 2400000 | tf_op jit(solution)/shard_map/pallas_call | solution.py:134
  334.4 5.3 collective-permute-start.41
  339.7 6.6 %collective-permute-done.41 = bf16[1024,64]{1,0:T(8,128)(2,1)S(1)} collective-permute-done((bf16[1024,64]{1,0:T(8,128)(2,1)S(1)}, bf16[1024,64]{1,0:T(8,128)(2,1)S(1)}, u32[]{:S(2)}, u32[]{:S(2)}) %collective-permute-start.41) | collective-permute-done | bytes 131104 | tf_op jit(solution)/shard_map/ppermute | solution.py:45
  346.4 11.5 %shard_map.227 = (bf16[4,2,2,16,576]{4,3,2,1,0:T(8,128)(2,1)S(1)}, bf16[4,2,2,16,576]{4,3,2,1,0:T(8,128)(2,1)}, bf16[4,2,2,16,576]{4,3,2,1,0:T(8,128)(2,1)}, bf1...) custom-call(s32[8]{0:T(128)S(1)} %stack.244.column, ...), custom_call_target="tpu_custom_call" | custom-call | flops 1000 | bytes 3000000 | tf_op jit(solution)/shard_map/pallas_call | solution.py:134
  359.8 3.8 slice.286
  365.7 10.3 %reduce-scatter.2.cloned.1.call-done = bf16[1,4,4,2,3,16,704]{6,5,4,3,2,1,0:T(8,128)(2,1)} async-done(((bf16[4,4,4,2,3,16,704]{6,5,4,3,2,1,0:T(8,128)(2,1)}), bf16[1,4,4,2,3,16,704]{6,5,4,3,2,1,0:T(8,128)(2,1)}) %reduce-scatter.2.cloned.1.call-update) | async-done | bytes 2162704 | tf_op jit(solution)/shard_map/reduce_scatter | solution.py:817
  382.8 5.2 shard_map.226
  393.5 3.4 collective-permute-done.42
  396.9 9.7 %collective-permute-done.44 = bf16[4,2,3,16,704]{4,3,2,1,0:T(8,128)(2,1)} collective-permute-done((bf16[4,2,3,16,704]{4,3,2,1,0:T(8,128)(2,1)}, bf16[4,2,3,16,704]{4,3,2,1,0:T(8,128)(2,1)}, u32[]{:S(2)}, u32[]{:S(2)}) %collective-permute-start.44) | collective-permute-done | bytes 540704 | tf_op jit(solution)/shard_map/ppermute | solution.py:45
  415.5 8.0 %collective-permute-start.45 = (bf16[2,3,16,704]{3,2,1,0:T(8,128)(2,1)S(1)}, bf16[2,3,16,704]{3,2,1,0:T(8,128)(2,1)S(1)}, u32[]{:S(2)}, u32[]{:S(2)}) collective-permute-start(bf16[2,3,16,704]{3,2,1,0:T(8,128)(2,1)S(1)} %get-tuple-element.246), channel_id=1, source_target_pairs={{0,6},{1,3},{2,0},{3,5},{4,2},{5,7},{6,4},{7,1},{8,14},{9,11},{10,... | collective-permute-start | bytes 405512 | tf_op jit(solution)/shard_map/ppermute | solution.py:45
  423.5 5.6 collective-permute-done.45
  430.2 5.7 collective-permute-done.46
  438.4 5.6 convolution_convert_fusion
  455.6 3.1 collective-permute-start.74
  460.4 13.6 %collective-permute-done.66 = bf16[2,4,3,16,704]{4,3,2,1,0:T(8,128)(2,1)S(1)} collective-permute-done((bf16[2,4,3,16,704]{4,3,2,1,0:T(8,128)(2,1)S(1)}, bf16[2,4,3,16,704]{4,3,2,1,0:T(8,128)(2,1)S(1)}, u32[]{:S(2)}, u32[]{:S(2)}) %collective-permute-start.66) | collective-permute-done | bytes 540704 | tf_op jit(solution)/shard_map/ppermute | solution.py:45
  482.7 4.7 collective-permute-done.67
  494.1 8.8 %collective-permute-done.60 = bf16[128,2048]{1,0:T(8,128)(2,1)S(1)} collective-permute-done((bf16[128,2048]{1,0:T(8,128)(2,1)S(1)}, bf16[128,2048]{1,0:T(8,128)(2,1)S(1)}, u32[]{:S(2)}, u32[]{:S(2)}) %collective-permute-start.60) | collective-permute-done | bytes 524320 | tf_op jit(solution)/shard_map/ppermute | solution.py:45
  507.3 8.0 %collective-permute-done.77 = bf16[2,16,320]{2,1,0:T(8,128)(2,1)S(1)} collective-permute-done((bf16[2,16,320]{2,1,0:T(8,128)(2,1)S(1)}, bf16[2,16,320]{2,1,0:T(8,128)(2,1)S(1)}, u32[]{:S(2)}, u32[]{:S(2)}) %collective-permute-start.77) | collective-permute-done | bytes 20512 | tf_op jit(solution)/shard_map/ppermute | solution.py:45
  520.6 3.9 collective-permute-done.76
  529.8 5.1 collective-permute-done.55
  543.3 21.3 %collective-permute-done.85.refs_3_ = bf16[2,2,4,16,576]{4,3,2,1,0:T(8,128)(2,1)S(1)} collective-permute-done((bf16[2,2,4,16,576]{4,3,2,1,0:T(8,128)(2,1)S(1)}, bf16[2,2,4,16,576]{4,3,2,1,0:T(8,128)(2,1)S(1)}, u32[]{:S(2)}, u32[]{:S(2)}) %collective-permute-start.85) | collective-permute-done | bytes 294944 | tf_op jit(solution)/shard_map/ppermute | solution.py:45
  564.6 3.5 collective-permute-done.84.refs_2_
  573.0 6.4 %shard_map.229 = (f32[128,5632]{1,0:T(8,128)}, f32[128,5632]{1,0:T(8,128)}, f32[5632,128]{1,0:T(8,128)}) custom-call(s32[5]{0:T(128)S(1)} %stack.218.spots, s32[4]{0:T(128)S(1)} %pad_add_fusion.1.xs, s32[4]{0:T(128)S(1)} %pad_add_fusion.3.yhs, s32[1]{0:T(128)} %bitcast.15.core, bf16[2,2,4,3,16,704]{5,4,3,2,1,0:T(8,128)(2,1)S(1)} %pad_maximum_fusion.1.refs_0_, ...), custom_call_target="tpu_custom_call" | custom-call | flops 1000 | bytes 1500000 | tf_op jit(solution)/shard_map/pallas_call | solution.py:134
  (423 shorter events, 166.7 us)
Async XLA Ops:
  7.2 88.7 %all-gather.9.cloned.1.call-start = ((), (), s32[]{:S(2)}) async-start(), calls=%async_computation.1 | async-start | bytes 4718592 | tf_op jit(solution)/shard_map/all_gather | solution.py:755
  23.7 19.5 %collective-permute-start.2 = (bf16[4,2,32,704]{3,2,0,1:T(8,128)(2,1)S(1)}, bf16[4,2,32,704]{3,2,0,1:T(8,128)(2,1)S(1)}, u32[]{:S(2)}, u32[]{:S(2)}) collective-permute-start(bf16[4,2,32,704]{3,2,0,1:T(8,128)(2,1)S(1)} %pad_maximum_fusion.4), channel_id=1, source_target_pairs={{0,6},{1,3},{2,0},{3,5},{4,2},{5,7},{6,4},{7,1},{8,14},{9,11},{10,... | collective-permute-start | bytes 1081352 | tf_op jit(solution)/shard_map/ppermute | solution.py:45
  25.9 19.4 %collective-permute-start.3 = (bf16[4,2,32,704]{3,2,1,0:T(8,128)(2,1)S(1)}, bf16[4,2,32,704]{3,2,1,0:T(8,128)(2,1)S(1)}, u32[]{:S(2)}, u32[]{:S(2)}) collective-permute-start(bf16[4,2,32,704]{3,2,1,0:T(8,128)(2,1)S(1)} %pad_maximum_fusion.5), channel_id=1, source_target_pairs={{0,4},{1,5},{2,6},{3,7},{4,0},{5,1},{6,2},{7,3},{8,12},{9,13},{10,... | collective-permute-start | bytes 1081352 | tf_op jit(solution)/shard_map/ppermute | solution.py:45
  45.4 86.8 %all-gather.13.cloned.1.call-start = ((), (), s32[]{:S(2)}) async-start(), calls=%async_computation.4 | async-start | bytes 5898240 | tf_op jit(solution)/shard_map/all_gather | solution.py:762
  46.6 158.1 %all-gather.11.cloned.1.call-start = ((), (), s32[]{:S(2)}) async-start(), calls=%async_computation.2 | async-start | bytes 4718592 | tf_op jit(solution)/shard_map/all_gather | solution.py:765
  53.0 17.4 %collective-permute-start.6 = (bf16[8,32,576]{2,1,0:T(8,128)(2,1)S(1)}, bf16[8,32,576]{2,1,0:T(8,128)(2,1)S(1)}, u32[]{:S(2)}, u32[]{:S(2)}) collective-permute-start(bf16[8,32,576]{2,1,0:T(8,128)(2,1)S(1)} %get-tuple-element.260), channel_id=1, source_target_pairs={{0,48},{1,17},{2,50},{3,19},{4,52},{5,21},{6,54},{7,23},{8,56},{9,... | collective-permute-start | bytes 884744 | tf_op jit(solution)/shard_map/ppermute | solution.py:45
  55.9 16.2 %collective-permute-start.7 = (bf16[8,32,576]{2,1,0:T(8,128)(2,1)S(1)}, bf16[8,32,576]{2,1,0:T(8,128)(2,1)S(1)}, u32[]{:S(2)}, u32[]{:S(2)}) collective-permute-start(bf16[8,32,576]{2,1,0:T(8,128)(2,1)S(1)} %get-tuple-element.260), channel_id=1, source_target_pairs={{0,32},{1,33},{2,34},{3,35},{4,36},{5,37},{6,38},{7,39},{8,40},{9,... | collective-permute-start | bytes 884744 | tf_op jit(solution)/shard_map/ppermute | solution.py:45
  72.4 17.7 %collective-permute-start.8 = (bf16[4,8,32,576]{3,2,1,0:T(8,128)(2,1)S(1)}, bf16[4,8,32,576]{3,2,1,0:T(8,128)(2,1)S(1)}, u32[]{:S(2)}, u32[]{:S(2)}) collective-permute-start(bf16[4,8,32,576]{3,2,1,0:T(8,128)(2,1)S(1)} %pad_maximum_fusion.own_ref), channel_id=1, source_target_pairs={{0,8},{1,73},{2,10},{3,75},{4,12},{5,77},{6,14},{7,79},{8,64},{9,1... | collective-permute-start | bytes 3538952 | tf_op jit(solution)/shard_map/ppermute | solution.py:45
  91.1 284.9 %reduce-scatter.2.cloned.1.call-start = ((), (), s32[]{:S(2)}) async-start(), calls=%async_computation.3 | async-start | bytes 11796480 | tf_op jit(solution)/shard_map/reduce_scatter | solution.py:817
  110.8 21.9 %collective-permute-start.10 = (bf16[2048,64]{0,1:T(8,128)(2,1)S(1)}, bf16[2048,64]{0,1:T(8,128)(2,1)S(1)}, u32[]{:S(2)}, u32[]{:S(2)}) collective-permute-start(bf16[2048,64]{0,1:T(8,128)(2,1)S(1)} %pad_maximum_fusion.10), channel_id=1, source_target_pairs={{0,1},{1,0},{2,3},{3,2},{4,5},{5,4},{6,7},{7,6},{8,9},{9,8},{10,11... | collective-permute-start | bytes 786440 | tf_op jit(solution)/shard_map/ppermute | solution.py:45
  132.2 59.4 %collective-permute-start.20 = (bf16[4,3,8,32,704]{4,3,2,1,0:T(8,128)(2,1)}, bf16[4,3,8,32,704]{4,3,2,1,0:T(8,128)(2,1)}, u32[]{:S(2)}, u32[]{:S(2)}) collective-permute-start(bf16[4,3,8,32,704]{4,3,2,1,0:T(8,128)(2,1)} %bitcast.209), channel_id=1, source_target_pairs={{0,8},{1,73},{2,10},{3,75},{4,12},{5,77},{6,14},{7,79},{8,64},{9,1... | collective-permute-start | bytes 12976136 | tf_op jit(solution)/shard_map/ppermute | solution.py:45
  153.4 23.2 %collective-permute-start.17 = (bf16[128,2048]{1,0:T(8,128)(2,1)S(1)}, bf16[128,2048]{1,0:T(8,128)(2,1)S(1)}, u32[]{:S(2)}, u32[]{:S(2)}) collective-permute-start(bf16[128,2048]{1,0:T(8,128)(2,1)S(1)} %add_convert_fusion.10), channel_id=1, source_target_pairs={{0,4},{1,5},{2,6},{3,7},{4,0},{5,1},{6,2},{7,3},{8,12},{9,13},{10,... | collective-permute-start | bytes 1572872 | tf_op jit(solution)/shard_map/ppermute | solution.py:45
  158.7 28.8 %collective-permute-start.16 = (bf16[128,2048]{1,0:T(8,128)(2,1)S(1)}, bf16[128,2048]{1,0:T(8,128)(2,1)S(1)}, u32[]{:S(2)}, u32[]{:S(2)}) collective-permute-start(bf16[128,2048]{1,0:T(8,128)(2,1)S(1)} %add_convert_fusion.11), channel_id=1, source_target_pairs={{0,2},{1,7},{2,4},{3,1},{4,6},{5,3},{6,0},{7,5},{8,10},{9,15},{10,... | collective-permute-start | bytes 1572872 | tf_op jit(solution)/shard_map/ppermute | solution.py:45
  159.0 28.6 %collective-permute-start.15 = (bf16[128,2048]{1,0:T(8,128)(2,1)S(1)}, bf16[128,2048]{1,0:T(8,128)(2,1)S(1)}, u32[]{:S(2)}, u32[]{:S(2)}) collective-permute-start(bf16[128,2048]{1,0:T(8,128)(2,1)S(1)} %add_convert_fusion.12), channel_id=1, source_target_pairs={{0,6},{1,3},{2,0},{3,5},{4,2},{5,7},{6,4},{7,1},{8,14},{9,11},{10,... | collective-permute-start | bytes 1572872 | tf_op jit(solution)/shard_map/ppermute | solution.py:45
  168.9 18.7 %collective-permute-start.14 = (bf16[128,2048]{1,0:T(8,128)(2,1)S(1)}, bf16[128,2048]{1,0:T(8,128)(2,1)S(1)}, u32[]{:S(2)}, u32[]{:S(2)}) collective-permute-start(bf16[128,2048]{1,0:T(8,128)(2,1)S(1)} %get-tuple-element.127), channel_id=1, source_target_pairs={{0,1},{1,0},{2,3},{3,2},{4,5},{5,4},{6,7},{7,6},{8,9},{9,8},{10,11... | collective-permute-start | bytes 1572872 | tf_op jit(solution)/shard_map/ppermute | solution.py:45
  204.2 19.8 %collective-permute-start.26 = (bf16[128,2048]{1,0:T(8,128)(2,1)S(1)}, bf16[128,2048]{1,0:T(8,128)(2,1)}, u32[]{:S(2)}, u32[]{:S(2)}) collective-permute-start(bf16[128,2048]{1,0:T(8,128)(2,1)S(1)} %multiply_convert_fusion.refs_0_), channel_id=1, source_target_pairs={{0,4},{1,5},{2,6},{3,7},{4,0},{5,1},{6,2},{7,3},{8,12},{9,13},{10,... | collective-permute-start | bytes 1572872 | tf_op jit(solution)/shard_map/ppermute | solution.py:45
  204.5 22.5 %collective-permute-start.25 = (bf16[128,2048]{1,0:T(8,128)(2,1)}, bf16[128,2048]{1,0:T(8,128)(2,1)}, u32[]{:S(2)}, u32[]{:S(2)}) collective-permute-start(bf16[128,2048]{1,0:T(8,128)(2,1)} %collective-permute-done.24.refs_0_.refs_4_), channel_id=1, source_target_pairs={{0,1},{1,0},{2,3},{3,2},{4,5},{5,4},{6,7},{7,6},{8,9},{9,8},{10,11... | collective-permute-start | bytes 1572872 | tf_op jit(solution)/shard_map/ppermute | solution.py:45
  246.0 33.3 %collective-permute-start.31 = (bf16[128,2048]{1,0:T(8,128)(2,1)}, bf16[128,2048]{1,0:T(8,128)(2,1)}, u32[]{:S(2)}, u32[]{:S(2)}) collective-permute-start(bf16[128,2048]{1,0:T(8,128)(2,1)} %add_convert_fusion.7), channel_id=1, source_target_pairs={{0,2},{1,7},{2,4},{3,1},{4,6},{5,3},{6,0},{7,5},{8,10},{9,15},{10,... | collective-permute-start | bytes 1572872 | tf_op jit(solution)/shard_map/ppermute | solution.py:45
  248.4 30.9 %collective-permute-start.32 = (bf16[128,2048]{1,0:T(8,128)(2,1)}, bf16[128,2048]{1,0:T(8,128)(2,1)}, u32[]{:S(2)}, u32[]{:S(2)}) collective-permute-start(bf16[128,2048]{1,0:T(8,128)(2,1)} %add_convert_fusion.6), channel_id=1, source_target_pairs={{0,4},{1,5},{2,6},{3,7},{4,0},{5,1},{6,2},{7,3},{8,12},{9,13},{10,... | collective-permute-start | bytes 1572872 | tf_op jit(solution)/shard_map/ppermute | solution.py:45
  279.4 159.0 %all-gather.15.cloned.1.call-start = ((), (), s32[]{:S(2)}) async-start(), calls=%async_computation.5 | async-start | bytes 1114112 | tf_op jit(solution)/shard_map/all_gather | solution.py:859
  300.8 21.7 %collective-permute-start.33 = (bf16[128,2048]{1,0:T(8,128)(2,1)S(1)}, bf16[128,2048]{1,0:T(8,128)(2,1)S(1)}, u32[]{:S(2)}, u32[]{:S(2)}) collective-permute-start(bf16[128,2048]{1,0:T(8,128)(2,1)S(1)} %get-tuple-element.219.refs_1_.refs_8_), channel_id=1, source_target_pairs={{0,4},{1,5},{2,6},{3,7},{4,0},{5,1},{6,2},{7,3},{8,12},{9,13},{10,... | collective-permute-start | bytes 1572872 | tf_op jit(solution)/shard_map/ppermute | solution.py:45
  358.0 24.1 %collective-permute-start.63 = (bf16[4,2,2,16,576]{4,3,2,1,0:T(8,128)(2,1)S(1)}, bf16[4,2,2,16,576]{4,3,2,1,0:T(8,128)(2,1)S(1)}, u32[]{:S(2)}, u32[]{:S(2)}) collective-permute-start(bf16[4,2,2,16,576]{4,3,2,1,0:T(8,128)(2,1)S(1)} %get-tuple-element.187), channel_id=1, source_target_pairs={{0,32},{1,33},{2,34},{3,35},{4,36},{5,37},{6,38},{7,39},{8,40},{9,... | collective-permute-start | bytes 884744 | tf_op jit(solution)/shard_map/ppermute | solution.py:45
  363.6 27.8 %collective-permute-start.64 = (bf16[4,2,2,16,576]{4,3,2,1,0:T(8,128)(2,1)}, bf16[4,2,2,16,576]{4,3,2,1,0:T(8,128)(2,1)}, u32[]{:S(2)}, u32[]{:S(2)}) collective-permute-start(bf16[4,2,2,16,576]{4,3,2,1,0:T(8,128)(2,1)} %get-tuple-element.188), channel_id=1, source_target_pairs={{0,48},{1,17},{2,50},{3,19},{4,52},{5,21},{6,54},{7,23},{8,56},{9,... | collective-permute-start | bytes 884744 | tf_op jit(solution)/shard_map/ppermute | solution.py:45
  364.8 26.6 %collective-permute-start.65 = (bf16[4,2,2,16,576]{4,3,2,1,0:T(8,128)(2,1)}, bf16[4,2,2,16,576]{4,3,2,1,0:T(8,128)(2,1)}, u32[]{:S(2)}, u32[]{:S(2)}) collective-permute-start(bf16[4,2,2,16,576]{4,3,2,1,0:T(8,128)(2,1)} %get-tuple-element.189), channel_id=1, source_target_pairs={{0,16},{1,49},{2,18},{3,51},{4,20},{5,53},{6,22},{7,55},{8,24},{9,... | collective-permute-start | bytes 884744 | tf_op jit(solution)/shard_map/ppermute | solution.py:45
  378.7 18.1 %collective-permute-start.42 = (bf16[4,2,3,16,704]{4,3,2,1,0:T(8,128)(2,1)}, bf16[4,2,3,16,704]{4,3,2,1,0:T(8,128)(2,1)}, u32[]{:S(2)}, u32[]{:S(2)}) collective-permute-start(bf16[4,2,3,16,704]{4,3,2,1,0:T(8,128)(2,1)} %get-tuple-element.226), channel_id=1, source_target_pairs={{0,64},{1,65},{2,66},{3,67},{4,68},{5,69},{6,70},{7,71},{8,72},{9,... | collective-permute-start | bytes 1622024 | tf_op jit(solution)/shard_map/ppermute | solution.py:45
  380.7 25.9 %collective-permute-start.44 = (bf16[4,2,3,16,704]{4,3,2,1,0:T(8,128)(2,1)}, bf16[4,2,3,16,704]{4,3,2,1,0:T(8,128)(2,1)}, u32[]{:S(2)}, u32[]{:S(2)}) collective-permute-start(bf16[4,2,3,16,704]{4,3,2,1,0:T(8,128)(2,1)} %get-tuple-element.227), channel_id=1, source_target_pairs={{0,8},{1,73},{2,10},{3,75},{4,12},{5,77},{6,14},{7,79},{8,64},{9,1... | collective-permute-start | bytes 1622024 | tf_op jit(solution)/shard_map/ppermute | solution.py:45
  382.1 25.7 %collective-permute-start.43 = (bf16[4,2,3,16,704]{4,3,2,1,0:T(8,128)(2,1)}, bf16[4,2,3,16,704]{4,3,2,1,0:T(8,128)(2,1)}, u32[]{:S(2)}, u32[]{:S(2)}) collective-permute-start(bf16[4,2,3,16,704]{4,3,2,1,0:T(8,128)(2,1)} %get-tuple-element.228), channel_id=1, source_target_pairs={{0,72},{1,9},{2,74},{3,11},{4,76},{5,13},{6,78},{7,15},{8,0},{9,65... | collective-permute-start | bytes 1622024 | tf_op jit(solution)/shard_map/ppermute | solution.py:45
  391.1 150.3 %all-gather.17.cloned.1.call-start = ((), (), s32[]{:S(2)}) async-start(), calls=%async_computation.6 | async-start | bytes 1179648 | tf_op jit(solution)/shard_map/all_gather | solution.py:870
  409.7 27.1 %collective-permute-start.70 = (bf16[4,2,2,16,576]{4,3,2,1,0:T(8,128)(2,1)S(1)}, bf16[4,2,2,16,576]{4,3,2,1,0:T(8,128)(2,1)S(1)}, u32[]{:S(2)}, u32[]{:S(2)}) collective-permute-start(bf16[4,2,2,16,576]{4,3,2,1,0:T(8,128)(2,1)S(1)} %copy-done.49), channel_id=1, source_target_pairs={{0,64},{1,65},{2,66},{3,67},{4,68},{5,69},{6,70},{7,71},{8,72},{9,... | collective-permute-start | bytes 884744 | tf_op jit(solution)/shard_map/ppermute | solution.py:45
  412.2 25.1 %collective-permute-start.71 = (bf16[4,2,2,16,576]{4,3,2,1,0:T(8,128)(2,1)S(1)}, bf16[4,2,2,16,576]{4,3,2,1,0:T(8,128)(2,1)S(1)}, u32[]{:S(2)}, u32[]{:S(2)}) collective-permute-start(bf16[4,2,2,16,576]{4,3,2,1,0:T(8,128)(2,1)S(1)} %copy-done.47), channel_id=1, source_target_pairs={{0,72},{1,9},{2,74},{3,11},{4,76},{5,13},{6,78},{7,15},{8,0},{9,65... | collective-permute-start | bytes 884744 | tf_op jit(solution)/shard_map/ppermute | solution.py:45
  412.7 24.8 %collective-permute-start.72 = (bf16[4,2,2,16,576]{4,3,2,1,0:T(8,128)(2,1)S(1)}, bf16[4,2,2,16,576]{4,3,2,1,0:T(8,128)(2,1)S(1)}, u32[]{:S(2)}, u32[]{:S(2)}) collective-permute-start(bf16[4,2,2,16,576]{4,3,2,1,0:T(8,128)(2,1)S(1)} %copy-done.45), channel_id=1, source_target_pairs={{0,8},{1,73},{2,10},{3,75},{4,12},{5,77},{6,14},{7,79},{8,64},{9,1... | collective-permute-start | bytes 884744 | tf_op jit(solution)/shard_map/ppermute | solution.py:45
  430.1 20.8 %collective-permute-start.57 = (bf16[128,2048]{1,0:T(8,128)(2,1)}, bf16[128,2048]{1,0:T(8,128)(2,1)}, u32[]{:S(2)}, u32[]{:S(2)}) collective-permute-start(bf16[128,2048]{1,0:T(8,128)(2,1)} %get-tuple-element.175), channel_id=1, source_target_pairs={{0,1},{1,0},{2,3},{3,2},{4,5},{5,4},{6,7},{7,6},{8,9},{9,8},{10,11... | collective-permute-start | bytes 1572872 | tf_op jit(solution)/shard_map/ppermute | solution.py:45
  437.3 16.8 %collective-permute-start.61 = (bf16[128,2048]{1,0:T(8,128)(2,1)S(1)}, bf16[128,2048]{1,0:T(8,128)(2,1)}, u32[]{:S(2)}, u32[]{:S(2)}) collective-permute-start(bf16[128,2048]{1,0:T(8,128)(2,1)S(1)} %copy-done.43), channel_id=1, source_target_pairs={{0,1},{1,0},{2,3},{3,2},{4,5},{5,4},{6,7},{7,6},{8,9},{9,8},{10,11... | collective-permute-start | bytes 1572872 | tf_op jit(solution)/shard_map/ppermute | solution.py:45
  449.2 24.9 %collective-permute-start.69 = (bf16[2,2,16,576]{3,2,1,0:T(8,128)(2,1)S(1)}, bf16[2,2,16,576]{3,2,1,0:T(8,128)(2,1)S(1)}, u32[]{:S(2)}, u32[]{:S(2)}) collective-permute-start(bf16[2,2,16,576]{3,2,1,0:T(8,128)(2,1)S(1)} %get-tuple-element.256), channel_id=1, source_target_pairs={{0,8},{1,73},{2,10},{3,75},{4,12},{5,77},{6,14},{7,79},{8,64},{9,1... | collective-permute-start | bytes 221192 | tf_op jit(solution)/shard_map/ppermute | solution.py:45
  454.1 21.9 %collective-permute-start.75 = (bf16[2,2,16,576]{3,2,1,0:T(8,128)(2,1)S(1)}, bf16[2,2,16,576]{3,2,1,0:T(8,128)(2,1)S(1)}, u32[]{:S(2)}, u32[]{:S(2)}) collective-permute-start(bf16[2,2,16,576]{3,2,1,0:T(8,128)(2,1)S(1)} %get-tuple-element.252), channel_id=1, source_target_pairs={{0,16},{1,49},{2,18},{3,51},{4,20},{5,53},{6,22},{7,55},{8,24},{9,... | collective-permute-start | bytes 221192 | tf_op jit(solution)/shard_map/ppermute | solution.py:45
  455.6 21.5 %collective-permute-start.74 = (bf16[2,2,16,576]{3,2,1,0:T(8,128)(2,1)S(1)}, bf16[2,2,16,576]{3,2,1,0:T(8,128)(2,1)S(1)}, u32[]{:S(2)}, u32[]{:S(2)}) collective-permute-start(bf16[2,2,16,576]{3,2,1,0:T(8,128)(2,1)S(1)} %get-tuple-element.253), channel_id=1, source_target_pairs={{0,48},{1,17},{2,50},{3,19},{4,52},{5,21},{6,54},{7,23},{8,56},{9,... | collective-permute-start | bytes 221192 | tf_op jit(solution)/shard_map/ppermute | solution.py:45
  458.7 19.5 %collective-permute-start.73 = (bf16[2,2,16,576]{3,2,1,0:T(8,128)(2,1)S(1)}, bf16[2,2,16,576]{3,2,1,0:T(8,128)(2,1)S(1)}, u32[]{:S(2)}, u32[]{:S(2)}) collective-permute-start(bf16[2,2,16,576]{3,2,1,0:T(8,128)(2,1)S(1)} %get-tuple-element.254), channel_id=1, source_target_pairs={{0,32},{1,33},{2,34},{3,35},{4,36},{5,37},{6,38},{7,39},{8,40},{9,... | collective-permute-start | bytes 221192 | tf_op jit(solution)/shard_map/ppermute | solution.py:45
  476.1 16.3 %collective-permute-start.58 = (bf16[128,2048]{1,0:T(8,128)(2,1)S(1)}, bf16[128,2048]{1,0:T(8,128)(2,1)S(1)}, u32[]{:S(2)}, u32[]{:S(2)}) collective-permute-start(bf16[128,2048]{1,0:T(8,128)(2,1)S(1)} %add_convert_fusion.2), channel_id=1, source_target_pairs={{0,4},{1,5},{2,6},{3,7},{4,0},{5,1},{6,2},{7,3},{8,12},{9,13},{10,... | collective-permute-start | bytes 1572872 | tf_op jit(solution)/shard_map/ppermute | solution.py:45
  477.1 25.8 %collective-permute-start.60 = (bf16[128,2048]{1,0:T(8,128)(2,1)S(1)}, bf16[128,2048]{1,0:T(8,128)(2,1)S(1)}, u32[]{:S(2)}, u32[]{:S(2)}) collective-permute-start(bf16[128,2048]{1,0:T(8,128)(2,1)S(1)} %add_convert_fusion.1), channel_id=1, source_target_pairs={{0,6},{1,3},{2,0},{3,5},{4,2},{5,7},{6,4},{7,1},{8,14},{9,11},{10,... | collective-permute-start | bytes 1572872 | tf_op jit(solution)/shard_map/ppermute | solution.py:45
  478.2 25.5 %collective-permute-start.62 = (bf16[128,2048]{1,0:T(8,128)(2,1)S(1)}, bf16[128,2048]{1,0:T(8,128)(2,1)S(1)}, u32[]{:S(2)}, u32[]{:S(2)}) collective-permute-start(bf16[128,2048]{1,0:T(8,128)(2,1)S(1)} %add_convert_fusion), channel_id=1, source_target_pairs={{0,2},{1,7},{2,4},{3,1},{4,6},{5,3},{6,0},{7,5},{8,10},{9,15},{10,... | collective-permute-start | bytes 1572872 | tf_op jit(solution)/shard_map/ppermute | solution.py:45
  487.4 38.4 %collective-permute-start.49 = (bf16[128,2048]{1,0:T(8,128)(2,1)S(1)}, bf16[128,2048]{1,0:T(8,128)(2,1)S(1)}, u32[]{:S(2)}, u32[]{:S(2)}) collective-permute-start(bf16[128,2048]{1,0:T(8,128)(2,1)S(1)} %copy-done.62), channel_id=1, source_target_pairs={{0,1},{1,0},{2,3},{3,2},{4,5},{5,4},{6,7},{7,6},{8,9},{9,8},{10,11... | collective-permute-start | bytes 1572872 | tf_op jit(solution)/shard_map/ppermute | solution.py:45
  489.6 38.9 %collective-permute-start.51 = (bf16[128,2048]{1,0:T(8,128)(2,1)S(1)}, bf16[128,2048]{1,0:T(8,128)(2,1)S(1)}, u32[]{:S(2)}, u32[]{:S(2)}) collective-permute-start(bf16[128,2048]{1,0:T(8,128)(2,1)S(1)} %get-tuple-element.233), channel_id=1, source_target_pairs={{0,4},{1,5},{2,6},{3,7},{4,0},{5,1},{6,2},{7,3},{8,12},{9,13},{10,... | collective-permute-start | bytes 1572872 | tf_op jit(solution)/shard_map/ppermute | solution.py:45
  492.3 37.5 %collective-permute-start.82 = (bf16[2,2,4,3,16,704]{5,4,3,2,1,0:T(8,128)(2,1)S(1)}, bf16[2,2,4,3,16,704]{5,4,3,2,1,0:T(8,128)(2,1)S(1)}, u32[]{:S(2)}, u32[]{:S(2)}) collective-permute-start(bf16[2,2,4,3,16,704]{5,4,3,2,1,0:T(8,128)(2,1)S(1)} %pad_maximum_fusion.1.refs_0_), channel_id=1, source_target_pairs={{0,16},{1,49},{2,18},{3,51},{4,20},{5,53},{6,22},{7,55},{8,24},{9,... | collective-permute-start | bytes 3244040 | tf_op jit(solution)/shard_map/ppermute | solution.py:45
  525.9 47.1 %collective-permute-start.86 = (bf16[2,2,4,3,16,704]{5,4,3,2,1,0:T(8,128)(2,1)S(1)}, bf16[2,2,4,3,16,704]{5,4,3,2,1,0:T(8,128)(2,1)}, u32[]{:S(2)}, u32[]{:S(2)}) collective-permute-start(bf16[2,2,4,3,16,704]{5,4,3,2,1,0:T(8,128)(2,1)S(1)} %pad_maximum_fusion.1.refs_0_), channel_id=1, source_target_pairs={{0,48},{1,17},{2,50},{3,19},{4,52},{5,21},{6,54},{7,23},{8,56},{9,... | collective-permute-start | bytes 3244040 | tf_op jit(solution)/shard_map/ppermute | solution.py:45
  529.8 43.1 %collective-permute-start.87 = (bf16[2,2,4,3,16,704]{5,4,3,2,1,0:T(8,128)(2,1)S(1)}, bf16[2,2,4,3,16,704]{5,4,3,2,1,0:T(8,128)(2,1)}, u32[]{:S(2)}, u32[]{:S(2)}) collective-permute-start(bf16[2,2,4,3,16,704]{5,4,3,2,1,0:T(8,128)(2,1)S(1)} %collective-permute-done.82.refs_1_), channel_id=1, source_target_pairs={{0,16},{1,49},{2,18},{3,51},{4,20},{5,53},{6,22},{7,55},{8,24},{9,... | collective-permute-start | bytes 3244040 | tf_op jit(solution)/shard_map/ppermute | solution.py:45
  536.3 28.3 %collective-permute-start.85 = (bf16[2,2,4,16,576]{4,3,2,1,0:T(8,128)(2,1)S(1)}, bf16[2,2,4,16,576]{4,3,2,1,0:T(8,128)(2,1)S(1)}, u32[]{:S(2)}, u32[]{:S(2)}) collective-permute-start(bf16[2,2,4,16,576]{4,3,2,1,0:T(8,128)(2,1)S(1)} %pad_maximum_fusion.7.refs_0_), channel_id=1, source_target_pairs={{0,32},{1,33},{2,34},{3,35},{4,36},{5,37},{6,38},{7,39},{8,40},{9,... | collective-permute-start | bytes 884744 | tf_op jit(solution)/shard_map/ppermute | solution.py:45
  539.4 28.8 %collective-permute-start.84 = (bf16[2,2,4,16,576]{4,3,2,1,0:T(8,128)(2,1)S(1)}, bf16[2,2,4,16,576]{4,3,2,1,0:T(8,128)(2,1)S(1)}, u32[]{:S(2)}, u32[]{:S(2)}) collective-permute-start(bf16[2,2,4,16,576]{4,3,2,1,0:T(8,128)(2,1)S(1)} %pad_maximum_fusion.7.refs_0_), channel_id=1, source_target_pairs={{0,48},{1,17},{2,50},{3,19},{4,52},{5,21},{6,54},{7,23},{8,56},{9,... | collective-permute-start | bytes 884744 | tf_op jit(solution)/shard_map/ppermute | solution.py:45
  540.9 28.0 %collective-permute-start.83 = (bf16[2,2,4,16,576]{4,3,2,1,0:T(8,128)(2,1)S(1)}, bf16[2,2,4,16,576]{4,3,2,1,0:T(8,128)(2,1)}, u32[]{:S(2)}, u32[]{:S(2)}) collective-permute-start(bf16[2,2,4,16,576]{4,3,2,1,0:T(8,128)(2,1)S(1)} %pad_maximum_fusion.7.refs_0_), channel_id=1, source_target_pairs={{0,16},{1,49},{2,18},{3,51},{4,20},{5,53},{6,22},{7,55},{8,24},{9,... | collective-permute-start | bytes 884744 | tf_op jit(solution)/shard_map/ppermute | solution.py:45
  (124 other events, 1337.6 us)
Sparse Core Ops, SparseCore 0:
  45.5 31.9 all-gather.8
  79.8 52.3 all-gather.12
  133.9 47.7 all-gather.10
  279.5 96.5 reduce-scatter.1
  391.2 35.3 all-gather.14
  449.2 44.6 all-gather.16

commit v4 on v3

--- a/solution.py
+++ b/solution.py
@@ -95,9 +95,11 @@
     return total
 
 
-def ring_scatter(own, before, after, far, axis):
-    got = across(far, axis), step(before, axis, -1), step(after, axis, 1)
-    return add(own, *got)
+def ring_scatter(own, before, beyond, far, axis, first=None):
+    if first is not None:
+        got_far = step(far, axis, 1)
+        return add(own, step(before, axis, -1), step(add(after(beyond, first), got_far).astype(BF), axis, 1))
+    return add(own, across(far, axis), step(before, axis, -1), step(beyond, axis, 1))
 
 
 def exchange_z(own, before, after, far):
@@ -276,8 +278,9 @@
     queries = jnp.concatenate([dq0_ref[...], dq1_ref[...], dq2_ref[...]], axis=0)
     rows = jnp.concatenate([queries, dkv_ref[...]], axis=1)
     grad = dot_last(rows, w_ref[...]).astype(BF)
-    for r in range(8):
-        out_refs[r][...] = grad[TOK * r : TOK * (r + 1)]
+    for r in range(4):
+        out_refs[r][...] = grad[2 * r * TOK : (2 * r + 1) * TOK]
+        out_refs[4][r] = grad[(2 * r + 1) * TOK : (2 * r + 2) * TOK]
 
 
 def project_back(dq, dkv, w):
@@ -285,7 +288,8 @@
         project_back_kernel, (), (4,),
         [pl.BlockSpec(each.shape, lambda k: (0, 0)) for each in tuple(dq) + (dkv,)]
         + [pl.BlockSpec((PART, QKV), lambda k: (k, 0))],
-        [pl.BlockSpec((TOK, PART), lambda k: (0, k))] * 8, [sds((TOK, D))] * 8, [], 4, tuple(dq) + (dkv, w),
+        [pl.BlockSpec((TOK, PART), lambda k: (0, k))] * 4 + [pl.BlockSpec((4, TOK, PART), lambda k: (0, 0, k))],
+        [sds((TOK, D))] * 4 + [sds((4, TOK, D))], [], 4, tuple(dq) + (dkv, w),
     )
 
 
@@ -447,8 +451,8 @@
 
 def mlp_kernel(chunk, *refs):
     rows_refs, grads_refs, w_ref = refs[:4], refs[4:8], refs[8]
-    z_ref, da_ref, dc_ref = refs[-11:-8]
-    grad_refs = refs[-8:-4]
+    z_ref, da_ref, dc_ref = refs[-12:-9]
+    mine_refs, peer_ref = refs[-9:-5], refs[-5]
     weights, gate, up, back = refs[-4:]
     k = pl.program_id(0)
 
@@ -457,7 +461,7 @@
         rows = jnp.concatenate([ref[...] for ref in rows_refs], axis=0)
         grads = jnp.concatenate([ref[...] for ref in grads_refs], axis=0)
         terms = (dot(rows, w_ref[0]), dot(rows, w_ref[1]), dot(grads, w_ref[2]))
-        weights[k] = w_ref[:2]
+        weights[k] = w_ref[...]
 
         @pl.when(k == 0)
         def _():
@@ -482,8 +486,12 @@
     def _():
         j = k - SPLIT
         grad = dot_last(da_ref[...], weights[j, 0]) + dot_last(dc_ref[...], weights[j, 1])
-        for r in range(4):
-            grad_refs[r][...] = grad[TOK * r : TOK * (r + 1)].astype(BF)
+        out = dot_last(z_ref[...], weights[j, 2])
+        for r in range(2):
+            mine_refs[r][...] = grad[2 * r * TOK : (2 * r + 1) * TOK].astype(BF)
+            mine_refs[2 + r][...] = out[2 * r * TOK : (2 * r + 1) * TOK].astype(BF)
+            peer_ref[r] = grad[(2 * r + 1) * TOK : (2 * r + 2) * TOK].astype(BF)
+            peer_ref[2 + r] = out[(2 * r + 1) * TOK : (2 * r + 2) * TOK].astype(BF)
 
 
 def mlp_half(part, chunk, rows, grads, weights, kept):
@@ -505,43 +513,14 @@
     wide = pltpu.VMEM((ROWS, WIDE), F32)
     out = call(
         mlp_kernel, (chunk,), (2 * SPLIT,), specs,
-        [kept_spec] * 3 + [pl.BlockSpec((TOK, DEEP), lambda k, chunk: (0, jnp.maximum(k - SPLIT, 0)))] * 4,
-        [sds((8 * TOK, WIDE))] * 3 + [sds((TOK, D))] * 4,
-        [pltpu.VMEM((SPLIT, 2, DEEP, WIDE), BF), wide, wide, wide],
-        16, args, aliases,
-    )
-    return out[:3], out[3:]
-
-
-def grads_specs(tail):
-    zeros = (0,) * (1 + len(tail))
-    x_first = pl.BlockSpec((2, 1, 2) + tail, lambda h, p, *_: (h, jnp.minimum(p, 1)) + zeros)
-    y_own = pl.BlockSpec((4, 1, 2) + tail, lambda h, p, *_: (0, jnp.where(h == 0, jnp.maximum(p - 2, 0), 1)) + zeros)
-    y_other = pl.BlockSpec((4, 1, 2) + tail, lambda h, p, *_: (0, jnp.where(h == 1, jnp.maximum(p - 2, 0), 0)) + zeros)
-    return [x_first] * 4 + [y_own] * 2 + [y_other] * 2, [sds((4, 2, 2) + tail)] * 8
-
-
-def write_grads(outs, xs, yhs, core, write):
-    half, p = pl.program_id(0), pl.program_id(1)
-
-    def go(pos, r, ref):
-        inside = yhs[2 * half + pos] * 64 + xs[r] * 16
-        for rc in range(2):
-            write(ref.at[rc], inside, jnp.abs(core[0] - rc), rc)
-
-    @pl.when(p < 2)
-    def _():
-        for r in range(4):
-            for pos in range(2):
-                go(pos, r, outs[r].at[pos, 0])
-
-    for each in range(2):
-
-        @pl.when((p >= 2) & (half == each))
-        def _():
-            for r in range(4):
-                for pos in range(2):
-                    go(pos, r, outs[4 + 2 * each + pos].at[r, 0])
+        [kept_spec] * 3
+        + [pl.BlockSpec((TOK, DEEP), lambda k, chunk: (0, jnp.maximum(k - SPLIT, 0)))] * 4
+        + [pl.BlockSpec((4, TOK, DEEP), lambda k, chunk: (0, 0, jnp.maximum(k - SPLIT, 0)))],
+        [sds((8 * TOK, WIDE))] * 3 + [sds((TOK, D))] * 4 + [sds((4, TOK, D))],
+        [pltpu.VMEM((SPLIT, 3, DEEP, WIDE), BF), wide, wide, wide],
+        18, args, aliases,
+    )
+    return out[:3], out[3:7], out[7]
 
 
 def mlp_grads_kernel(column, yhs, core, nat, *refs):
@@ -576,7 +555,7 @@
 
 def attn_grads_kernel(column, xs, yhs, core, halves, chunk, *refs):
     h_refs, g_refs, o_refs, dq_refs, (dkv_ref, w_ref) = refs[:8], refs[8:16], refs[16:20], refs[20:23], refs[23:25]
-    outs, gain_ref, (first, second) = refs[25:33], refs[33], refs[34:]
+    outs, gain_ref, (first, second) = refs[25:29], refs[29], refs[30:]
     rows = jnp.concatenate([ref[...] for ref in h_refs], axis=0).T
     queries = jnp.concatenate([ref[...] for ref in dq_refs], axis=0)
     first[...] = dot(rows, jnp.concatenate([queries, dkv_ref[...]], axis=1))
@@ -585,11 +564,14 @@
     gain = jnp.sum(first[...] * w_ref[...].astype(F32), axis=1, keepdims=True)
     gain_ref[0] = jnp.broadcast_to(gain, (256, 128)).T[:8]
 
-    def write(ref, inside, which, rc):
-        ref[:, :QUERY] = second[at_rows(inside, 16), QUERY * rc : QUERY * (rc + 1)].astype(BF)
-        ref[:, QUERY:] = first[at_rows(which * 128 + inside, 16), :].astype(BF)
-
-    write_grads(outs, xs, yhs, core, write)
+    half = pl.program_id(0)
+    for r in range(4):
+        for pos in range(2):
+            inside = yhs[2 * half + pos] * 64 + xs[r] * 16
+            for rc in range(2):
+                start = jnp.abs(core[0] - rc) * 128 + inside
+                outs[r][pos, 0, rc, :, :QUERY] = second[at_rows(inside, 16), QUERY * rc : QUERY * (rc + 1)].astype(BF)
+                outs[r][pos, 0, rc, :, QUERY:] = first[at_rows(start, 16), :].astype(BF)
 
 
 def attn_grads(column, xs, yhs, core, halves, chunk, h, g, o, dq, dkv, w):
@@ -597,7 +579,7 @@
         return pl.BlockSpec((TOK, 256), lambda i, p, column, xs, yhs, core, halves, chunk: (chunk[r], column[4 * i + p]))
 
     whole = lambda i, p, *_: (0, 0)
-    specs, shapes = grads_specs((16, PACK))
+    out = pl.BlockSpec((2, 1, 2, 16, PACK), lambda i, p, *_: (i, p, 0, 0, 0))
     *outs, gain = call(
         attn_grads_kernel, (column, xs, yhs, core, halves, chunk), (2, 4),
         [rows_spec(r) for r in range(8)]
@@ -608,8 +590,8 @@
             pl.BlockSpec((8 * TOK, HEAD), whole),
             pl.BlockSpec((256, QKV), lambda i, p, column, *_: (column[4 * i + p], 0)),
         ],
-        specs + [pl.BlockSpec((1, 8, 256), lambda i, p, column, *_: (column[4 * i + p], 0, 0))],
-        shapes + [sds((8, 8, 256), F32)],
+        [out] * 4 + [pl.BlockSpec((1, 8, 256), lambda i, p, column, *_: (column[4 * i + p], 0, 0))],
+        [sds((4, 4, 2, 16, PACK))] * 4 + [sds((8, 8, 256), F32)],
         [pltpu.VMEM((256, QKV), F32), pltpu.VMEM((128, 2 * QUERY), F32)],
         10, (h,) * 8 + tuple(g) + tuple(o) + tuple(dq) + (dkv, w),
     )
@@ -725,10 +707,6 @@
     def give(group, total):
         return across(total, "z") if group == 3 else step(total, "z", -1 if group == 1 else 1)
 
-    def scatter_tokens(mine, peer):
-        sums = [add(a, swap(b)).astype(BF) for a, b in zip(mine, peer)]
-        return add(sums[0], *[give(g, sums[g]) for g in (3, 1, 2)])
-
     gain_one = attn_gain.astype(F32)
     gain_two = mlp_gain.astype(F32)
     rows_in = tokens[0].astype(F32)
@@ -760,8 +738,6 @@
     attn_other_rows = step(attn_half_rows, "y", 1)
     w_qkv, w_out = place_attn(slot, xs, halves, attn_half_rows, attn_other_rows)
     mlp_half_rows = lax.all_gather(packs[:3], "batch", axis=0, axis_index_groups=X_GROUPS)
-    w_mlp = place_mlp(slot, halves, mlp_half_rows, step(mlp_half_rows, "y", 1))
-
     grad_rows = lax.all_gather(
         after(cotangent[0], attn_other_rows), "blk", axis=0, tiled=True, axis_index_groups=ZC_GROUPS
     )
@@ -785,9 +761,14 @@
     values = jnp.where(usable, jnp.where(first_core, kv_other, kv_mine), 0)
     attended, sums, got = [None] * 4, [None] * 4, [None] * 4
     for g in (3, 1, 2, 0):
-        at = after(query_place, mlp_half_rows, *sums[1:]) if g == 0 else query_place
+        at = after(query_place, *sums[1:]) if g == 0 else query_place
         attended[g], mine, peer = attend(g, at, key_slot, queries, keys, values, w_out)
-        sums[g] = add(mine, swap(peer)).astype(BF)
+        peer = swap(peer)
+        if g == 1:
+            mlp_half_rows = after(mlp_half_rows, peer)
+            mlp_other_rows = step(mlp_half_rows, "y", 1)
+            w_mlp = place_mlp(slot, halves, mlp_half_rows, mlp_other_rows)
+        sums[g] = add(mine, peer).astype(BF)
         if g:
             got[g] = give(g, sums[g])
     residual = rows_in + add(sums[0], *got[1:])
@@ -796,18 +777,19 @@
     mlp_parts = [own, swap(own), first, swap(after(first, w_mlp)), second, swap(after(second, w_mlp)), third, None]
 
 
-    kept, sums, got, at = None, [None] * 4, [None] * 4, chunk
+    kept, sums, got, outs, at = None, [None] * 4, [None] * 4, [None] * 4, chunk
     for part in range(2):
-        kept, result = mlp_half(part, at, mlp_parts[4 * part : 4 * part + 4], grad_rows, w_mlp, kept)
-        swapped = [swap(peer) for peer in result[1::2]]
+        kept, mine, peer = mlp_half(part, at, mlp_parts[4 * part : 4 * part + 4], grad_rows, w_mlp, kept)
+        swapped = swap(after(peer, second, third))
         for each in range(2):
             g = 2 * part + each
-            sums[g] = add(result[2 * each], swapped[each]).astype(BF)
+            sums[g] = add(mine[each], swapped[each]).astype(BF)
+            outs[g] = add(mine[2 + each], swapped[2 + each]).astype(BF)
             if g:
                 got[g] = give(g, sums[g])
         if part == 0:
             mlp_parts[7] = swap(after(third, kept[0]))
-        at = after(chunk, *swapped)
+        at = after(chunk, swapped)
     hidden, gate_grad_rows, up_grad_rows = kept
     mlp_sums = mlp_grads(
         column, yhs, core, after(at, got[1], sums[2], sums[3]), mlp_parts, grad_rows, gate_grad_rows, up_grad_rows, hidden
@@ -838,6 +820,9 @@
     branch_parts += [first, swap(after(first, rows_0)), second, swap(after(second, rows_0))]
     rows_1, *sums = back(2, branch_parts[2:], sums, False)
     branch_parts += [third, swap(after(third, rows_1))]
+    outs = after(outs, third)
+    got_outs = [give(g, outs[g]) for g in (3, 1, 2)]
+    layer_out = (residual + add(outs[0], *got_outs)).astype(BF)[None]
     rows_2, kv_keep, kv_give = back(6, branch_parts[6:], sums, True)
     query_grad_rows = [rows_0, rows_1, rows_2]
     kv_terms = add(kv_keep, swap(kv_give))
@@ -848,8 +833,6 @@
     mlp_sums = ring_scatter(mlp_sums[0], mlp_sums[2], mlp_sums[3], mlp_sums[1], "y").astype(BF)
     mlp_rows = mlp_sums
     mlp_sums, mlp_swapped = resplit_back(mlp_sums)
-    branch = dot_last(after(hidden, mlp_swapped), w_mlp[2]).astype(BF).reshape(8, TOK, D)
-    layer_out = (residual + scatter_tokens(branch[::2], branch[1::2])).astype(BF)[None]
 
     attn_partial = project_back(query_grad_rows, kv_grad_rows, w_qkv)
     attn_outs, attn_gain_part = attn_grads(
@@ -857,21 +840,17 @@
     )
     gain_grads = jnp.stack([attn_gain_part / gain_one, mlp_gain_part])
     gain_grads = lax.all_gather(jnp.pad(gain_grads, ((0, 6), (0, 0))), "blk")
-    gain_grads = jnp.sum(after(gain_grads, mlp_swapped), axis=0)
 
     mlp_across = across(mlp_sums, "y")
     mlp_sums = ring_gather(jnp.stack([mlp_sums, mlp_across]), "x", True)
-    attn_partial = after(attn_partial, mlp_rows)
-    normed_attn_grad = scatter_tokens(attn_partial[::2], attn_partial[1::2])
-    tied = (mlp_swapped,)
-    low = after(ring_scatter(*attn_outs[:4], "x").astype(BF), *tied)
-    attn_outs[4:] = after(attn_outs[4:], mlp_rows)
-    high = after(ring_scatter(attn_outs[4], attn_outs[6], attn_outs[7], attn_outs[5], "y").astype(BF), *tied)
+    swapped = swap(attn_partial[4])
+    sums = after([add(attn_partial[g], swapped[g]).astype(BF) for g in range(4)], mlp_rows, got_outs)
+    normed_attn_grad = add(sums[0], *[give(g, sums[g]) for g in (3, 1, 2)])
+    attn_sums = after(ring_scatter(*attn_outs, "x", mlp_rows).astype(BF), mlp_swapped)
+    gain_grads = jnp.sum(after(gain_grads, mlp_across), axis=0)
     gain_grads = lax.all_gather(jnp.pad(gain_grads, ((0, 8), (0, 0))), "batch")
-    low = ring_scatter(after(low[0], mlp_across), low[2], low[3], low[1], "y").astype(BF)
-    high = ring_scatter(after(high[0], mlp_across), high[1], high[2], high[3], "x").astype(BF)
-    low, high = after((low, high), mlp_across, normed_attn_grad)
-    attn_sums = jnp.concatenate([low, high])
+    attn_sums = ring_scatter(attn_sums[0], attn_sums[2], attn_sums[3], attn_sums[1], "y").astype(BF)
+    attn_sums = after(attn_sums, mlp_across, normed_attn_grad)
     out_sums = send(
         attn_sums[..., :QUERY], lambda yh, x, yl, z, c: (yh, x, z // 2, 2 * (z % 2) + c, yl)
     )

time: 598 us -> 555 us (0.928)
  waiting for transfers between devices: 245 us -> 218 us
    all_gather x1, waiting for transfers between devices: 21.1 us -> 10.3 us  [on_device(): lax.all_gather(packs[:3], 'batch', axis=0, axis_index_groups=X_GROUPS)]
    ppermute x88 -> x73, waiting for transfers between devices: 213 us -> 203 us  [send(): return lax.ppermute(value, BOTH, pairs)]
    ppermute x88 -> x73, starting transfers between devices: 95 us -> 91.1 us  [send(): return lax.ppermute(value, BOTH, pairs)]
    unnamed x160 -> x196, local copies, waits for them, and re-layouts: 23.7 us -> 25.3 us
  transfers between devices with their start and end apart: 94 -> 79, of which waited for: 45 -> 43; matrix products, arithmetic and copies ran while one was open for 8% -> 6% of each run, Pallas kernels for 22% -> 24%
where the time goes in v4:
time: 555 us; the launch traced here: 546 us
  waiting for transfers between devices  218 us (39%)
  Pallas kernels  157 us (28%)
  starting transfers between devices  91.3 us (16%)
  local copies, waits for them, and re-layouts  33.1 us (6%)
  other arithmetic  30.8 us (6%)
  between operations  15.8 us (3%)
    ppermute x73, waiting for transfers between devices, send(): return lax.ppermute(value, BOTH, pairs)  203 us
    pallas_call x18, Pallas kernels, call(): pl.pallas_call(body, grid_spec=pltpu.PrefetchScalarGridSpec(num_scalar_pr...  157 us
    ppermute x73, starting transfers between devices, send(): return lax.ppermute(value, BOTH, pairs)  91.1 us
    unnamed x196, local copies, waits for them, and re-layouts  25.3 us
  transfers between devices with their start and end apart: 79, of which 43 were waited for; matrix products, arithmetic and copies ran while one was open for 6% of the time, Pallas kernels for 24%

profile of v4, /device:TPU:24, one launch (start us, length us, event | category | flops | bytes accessed | tf_op | source)
XLA Modules:
  0.0 546.3 jit_solution(18441688020469905928)
XLA Ops:
  12.9 4.0 shard_map.212
  27.8 4.3 collective-permute-done.1
  32.1 10.1 %collective-permute-done.2 = bf16[4,2,32,704]{3,2,0,1:T(8,128)(2,1)S(1)} collective-permute-done((bf16[4,2,32,704]{3,2,0,1:T(8,128)(2,1)S(1)}, bf16[4,2,32,704]{3,2,0,1:T(8,128)(2,1)S(1)}, u32[]{:S(2)}, u32[]{:S(2)}) %collective-permute-start.2) | collective-permute-done | bytes 360480 | tf_op jit(solution)/shard_map/ppermute | solution.py:45
  47.7 4.3 collective-permute-done.4
  57.2 12.3 %collective-permute-done.6 = bf16[8,32,576]{2,1,0:T(8,128)(2,1)S(1)} collective-permute-done((bf16[8,32,576]{2,1,0:T(8,128)(2,1)S(1)}, bf16[8,32,576]{2,1,0:T(8,128)(2,1)S(1)}, u32[]{:S(2)}, u32[]{:S(2)}) %collective-permute-start.6) | collective-permute-done | bytes 294944 | tf_op jit(solution)/shard_map/ppermute | solution.py:45
  71.6 17.6 %collective-permute-done.8.other_ref = bf16[4,8,32,576]{3,2,1,0:T(8,128)(2,1)} collective-permute-done((bf16[4,8,32,576]{3,2,1,0:T(8,128)(2,1)S(1)}, bf16[4,8,32,576]{3,2,1,0:T(8,128)(2,1)}, u32[]{:S(2)}, u32[]{:S(2)}) %collective-permute-start.8) | collective-permute-done | bytes 1179680 | tf_op jit(solution)/shard_map/ppermute | solution.py:45
  89.6 4.9 shard_map.213
  97.5 6.1 %shard_map.214 = (bf16[1024,256]{1,0:T(8,128)(2,1)S(1)}, bf16[2,1024,64]{2,1,0:T(8,128)(2,1)S(1)}) custom-call(s32[8]{0:T(128)S(1)} %stack.212.chunk.nat, bf16[1024,2048]{1,0:T(8,128)(2,1)} %all-gather.9.cloned.1.call-done.refs_0_.refs_1_.refs_2_.refs_3_.refs_4_.refs_5_.refs_6_.refs_7_, ...), custom_call_target="tpu_custom_call" | custom-call | flops 1000 | bytes 1500000 | tf_op jit(solution)/shard_map/pallas_call | solution.py:136
  104.1 6.5 %collective-permute-done.9 = bf16[2,1024,64]{1,2,0:T(8,128)(2,1)S(1)} collective-permute-done((bf16[2,1024,64]{1,2,0:T(8,128)(2,1)S(1)}, bf16[2,1024,64]{1,2,0:T(8,128)(2,1)S(1)}, u32[]{:S(2)}, u32[]{:S(2)}) %collective-permute-start.9) | collective-permute-done | bytes 262176 | tf_op jit(solution)/shard_map/ppermute | solution.py:45
  112.9 7.2 %shard_map.215 = (bf16[256,256]{1,0:T(8,128)(2,1)S(1)}, bf16[128,2048]{1,0:T(8,128)(2,1)S(1)}, bf16[128,2048]{1,0:T(8,128)(2,1)}) custom-call(s32[8]{0:T(128)S(1)} %bitcast.235, s32[16]{0:T(128)S(1)} %select_reduce_fusion.1.key_slot, bf16[1024,256]{1,0:T(8,128)(2,1)S(1)} %get-tuple-element.106.q_ref.refs_0_, ...), custom_call_target="tpu_custom_call" | custom-call | flops 1000 | bytes 1800000 | tf_op jit(solution)/shard_map/pallas_call | solution.py:136
  120.9 10.3 %all-gather.13.cloned.1.call-done = bf16[12,8,32,704]{3,2,1,0:T(8,128)(2,1)} async-done(((bf16[3,8,32,704]{3,2,1,0:T(8,128)(2,1)}), bf16[12,8,32,704]{3,2,1,0:T(8,128)(2,1)}) %all-gather.13.cloned.1.call-update) | async-done | bytes 4325392 | tf_op jit(solution)/shard_map/all_gather | solution.py:740
  131.7 7.1 %shard_map.217 = (bf16[256,256]{1,0:T(8,128)(2,1)S(1)}, bf16[128,2048]{1,0:T(8,128)(2,1)S(1)}, bf16[128,2048]{1,0:T(8,128)(2,1)S(1)}) custom-call(s32[8]{0:T(128)S(1)} %bitcast.236, s32[16]{0:T(128)S(1)} %select_reduce_fusion.1.key_slot, bf16[1024,256]{1,0:T(8,128)(2,1)S(1)} %get-tuple-element.106.q_ref.refs_0_, ...), custom_call_target="tpu_custom_call" | custom-call | flops 1000 | bytes 1800000 | tf_op jit(solution)/shard_map/pallas_call | solution.py:136
  139.7 4.5 shard_map.216
  154.4 4.3 shard_map.218
  158.8 14.1 %collective-permute-done.17 = bf16[128,2048]{1,0:T(8,128)(2,1)S(1)} collective-permute-done((bf16[128,2048]{1,0:T(8,128)(2,1)S(1)}, bf16[128,2048]{1,0:T(8,128)(2,1)S(1)}, u32[]{:S(2)}, u32[]{:S(2)}) %collective-permute-start.17) | collective-permute-done | bytes 524320 | tf_op jit(solution)/shard_map/ppermute | solution.py:45
  172.9 12.2 %collective-permute-done.16 = bf16[128,2048]{1,0:T(8,128)(2,1)S(1)} collective-permute-done((bf16[128,2048]{1,0:T(8,128)(2,1)}, bf16[128,2048]{1,0:T(8,128)(2,1)S(1)}, u32[]{:S(2)}, u32[]{:S(2)}) %collective-permute-start.16) | collective-permute-done | bytes 524320 | tf_op jit(solution)/shard_map/ppermute | solution.py:45
  191.8 8.4 %shard_map.219 = bf16[3,2,8,128,704]{4,3,2,1,0:T(8,128)(2,1)} custom-call(s32[8]{0:T(128)S(1)} %stack.223.slot, s32[2]{0:T(128)S(1)} %pad_add_fusion.2.halves, bf16[4,3,8,32,704]{4,3,2,1,0:T(8,128)(2,1)S(1)} %bitcast.234, bf16[4,3,8,32,704]{4,3,2,1,0:T(8,128)(2,1)} %copy-done.69), custom_call_target="tpu_custom_call" | custom-call | flops 1000 | bytes 1800000 | tf_op jit(solution)/shard_map/pallas_call | solution.py:136
  204.6 18.1 %shard_map.220 = (bf16[1024,704]{1,0:T(8,128)(2,1)S(1)}, bf16[1024,704]{1,0:T(8,128)(2,1)}, bf16[1024,704]{1,0:T(8,128)(2,1)}, bf16[128,2048]{1,0:T(8,128)(2,1)S...) custom-call(s32[8]{0:T(128)S(1)} %stack.212.chunk.nat, ...), custom_call_target="tpu_custom_call" | custom-call | flops 1000 | bytes 5400000 | tf_op jit(solution)/shard_map/pallas_call | solution.py:136
  225.6 8.7 %collective-permute-start.26 = (bf16[128,2048]{1,0:T(8,128)(2,1)}, bf16[128,2048]{1,0:T(8,128)(2,1)S(1)}, u32[]{:S(2)}, u32[]{:S(2)}) collective-permute-start(bf16[128,2048]{1,0:T(8,128)(2,1)} %collective-permute-done.23.refs_2_.refs_6_), channel_id=1, source_target_pairs={{0,1},{1,0},{2,3},{3,2},{4,5},{5,4},{6,7},{7,6},{8,9},{9,8},{10,11... | collective-permute-start | bytes 1572872 | tf_op jit(solution)/shard_map/ppermute | solution.py:45
  236.3 18.0 %shard_map.221 = (bf16[1024,704]{1,0:T(8,128)(2,1)S(1)}, bf16[1024,704]{1,0:T(8,128)(2,1)}, bf16[1024,704]{1,0:T(8,128)(2,1)}, bf16[128,2048]{1,0:T(8,128)(2,1)S...) custom-call(s32[8]{0:T(128)S(1)} %stack.212.chunk.nat, ...), custom_call_target="tpu_custom_call", output_to_operand_aliasing={{0}: (10, {}), {1}: (11, {}), {2}: (12, {})} | custom-call | flops 1000 | bytes 5400000 | tf_op jit(solution)/shard_map/pallas_call | solution.py:136
  262.5 4.0 collective-permute-done.28
  269.9 17.7 %shard_map.226 = bf16[4,4,4,2,3,16,704]{6,5,4,3,2,1,0:T(8,128)(2,1)} custom-call(s32[8]{0:T(128)S(1)} %stack.244.column, s32[4]{0:T(128)S(1)} %pad_add_fusion.3.yhs, s32[1]{0:T(128)} %bitcast.16.core, s32[8]{0:T(128)S(1)} %stack.212.chunk.nat, bf16[128,2048]{1,0:T(8,128)(2,1)S(1)} %multiply_convert_fusion.refs_0_, ...), custom_call_target="tpu_custom_call" | custom-call | flops 1000 | bytes 5100000 | tf_op jit(solution)/shard_map/pallas_call | solution.py:136
  288.7 4.1 multiply_reduce_fusion
  296.6 5.5 %shard_map.222 = (bf16[256,256]{1,0:T(8,128)(2,1)S(1)}, f32[2048,64]{1,0:T(8,128)S(1)}, f32[2048,64]{1,0:T(8,128)S(1)}) custom-call(s32[8]{0:T(128)S(1)} %bitcast.239, s32[16]{0:T(128)S(1)} %select_reduce_fusion.1.key_slot, s32[1]{0:T(128)} %bitcast.16.core, s32[16]{0:T(128)S(1)} %copy-done.55, bf16[1024,256]{1,0:T(8,128)(2,1)S(1)} %get-tuple-element.106.q_ref.refs_0_, ...), custom_call_target="tpu_custom_call" | custom-call | flops 1000 | bytes 2400000 | tf_op jit(solution)/shard_map/pallas_call | solution.py:136
  304.1 4.8 collective-permute-done.38.refs_3_.refs_12_
  312.4 16.6 %shard_map.223 = (bf16[512,256]{1,0:T(8,128)(2,1)S(1)}, f32[2048,64]{1,0:T(8,128)S(1)}, f32[2048,64]{1,0:T(8,128)}) custom-call(s32[8]{0:T(128)S(1)} %bitcast.240, s32[16]{0:T(128)S(1)} %select_reduce_fusion.1.key_slot, s32[1]{0:T(128)} %bitcast.16.core, s32[16]{0:T(128)S(1)} %copy-done.55, bf16[1024,256]{1,0:T(8,128)(2,1)S(1)} %get-tuple-element.106.q_ref.refs_0_, ...), custom_call_target="tpu_custom_call" | custom-call | flops 1000 | bytes 4800000 | tf_op jit(solution)/shard_map/pallas_call | solution.py:136
  331.6 11.3 %shard_map.224 = (bf16[256,256]{1,0:T(8,128)(2,1)S(1)}, bf16[2048,64]{1,0:T(8,128)(2,1)S(1)}, bf16[2048,64]{1,0:T(8,128)(2,1)S(1)}) custom-call(s32[8]{0:T(128)S(1)} %bitcast.241, s32[16]{0:T(128)S(1)} %select_reduce_fusion.1.key_slot, s32[1]{0:T(128)} %bitcast.16.core, s32[16]{0:T(128)S(1)} %copy-done.55, ...), custom_call_target="tpu_custom_call" | custom-call | flops 1000 | bytes 2400000 | tf_op jit(solution)/shard_map/pallas_call | solution.py:136
  343.1 3.9 collective-permute-start.33
  347.2 7.4 %collective-permute-start.42 = (bf16[1024,64]{1,0:T(8,128)(2,1)S(1)}, bf16[1024,64]{1,0:T(8,128)(2,1)}, u32[]{:S(2)}, u32[]{:S(2)}) collective-permute-start(bf16[1024,64]{1,0:T(8,128)(2,1)S(1)} %slice.399), channel_id=1, source_target_pairs={{0,8},{1,9},{2,10},{3,11},{4,12},{5,13},{6,14},{7,15},{8,0},{9,1},... | collective-permute-start | bytes 393224 | tf_op jit(solution)/shard_map/ppermute | solution.py:45
  354.6 4.8 collective-permute-done.32
  359.5 8.6 %collective-permute-done.33 = bf16[128,2048]{1,0:T(8,128)(2,1)S(1)} collective-permute-done((bf16[128,2048]{1,0:T(8,128)(2,1)S(1)}, bf16[128,2048]{1,0:T(8,128)(2,1)S(1)}, u32[]{:S(2)}, u32[]{:S(2)}) %collective-permute-start.33) | collective-permute-done | bytes 524320 | tf_op jit(solution)/shard_map/ppermute | solution.py:45
  371.3 4.9 reduce-scatter.2.cloned.1.call-done
  384.0 3.9 shard_map.225
  388.1 11.0 %shard_map.227 = (bf16[4,4,2,16,576]{4,3,2,1,0:T(8,128)(2,1)}, bf16[4,4,2,16,576]{4,3,2,1,0:T(8,128)(2,1)}, bf16[4,4,2,16,576]{4,3,2,1,0:T(8,128)(2,1)}, bf16[4,...) custom-call(s32[8]{0:T(128)S(1)} %copy-done.63, s32[4]{0:T(128)S(1)} %copy-done.57, s32[4]{0:T(128)S(1)} %pad_add_fusion.3.yhs, ...), custom_call_target="tpu_custom_call" | custom-call | flops 1000 | bytes 3000000 | tf_op jit(solution)/shard_map/pallas_call | solution.py:136
  400.5 3.1 collective-permute-start.55
  403.5 3.0 collective-permute-done.46
  410.6 3.0 collective-permute-start.51
  425.6 3.7 collective-permute-start.47
  435.6 7.3 %collective-permute-done.47 = bf16[128,2048]{1,0:T(8,128)(2,1)S(1)} collective-permute-done((bf16[128,2048]{1,0:T(8,128)(2,1)S(1)}, bf16[128,2048]{1,0:T(8,128)(2,1)S(1)}, u32[]{:S(2)}, u32[]{:S(2)}) %collective-permute-start.47) | collective-permute-done | bytes 524320 | tf_op jit(solution)/shard_map/ppermute | solution.py:45
  445.6 7.8 %collective-permute-done.48 = bf16[128,2048]{1,0:T(8,128)(2,1)S(1)} collective-permute-done((bf16[128,2048]{1,0:T(8,128)(2,1)S(1)}, bf16[128,2048]{1,0:T(8,128)(2,1)S(1)}, u32[]{:S(2)}, u32[]{:S(2)}) %collective-permute-start.48) | collective-permute-done | bytes 524320 | tf_op jit(solution)/shard_map/ppermute | solution.py:45
  455.0 5.0 collective-permute-done.59
  473.3 4.2 collective-permute-done.61
  477.6 3.7 collective-permute-start.71
  481.3 3.1 collective-permute-done.66
  484.4 6.6 %collective-permute-done.67.refs_1_ = bf16[2,2,4,3,16,704]{5,4,3,2,1,0:T(8,128)(2,1)S(1)} collective-permute-done((bf16[2,2,4,3,16,704]{5,4,3,2,1,0:T(8,128)(2,1)S(1)}, bf16[2,2,4,3,16,704]{5,4,3,2,1,0:T(8,128)(2,1)S(1)}, u32[]{:S(2)}, u32[]{:S(2)}) %collective-permute-start.67) | collective-permute-done | bytes 1081376 | tf_op jit(solution)/shard_map/ppermute | solution.py:45
  496.5 27.4 %collective-permute-done.70.refs_3_ = bf16[2,2,4,16,576]{4,3,2,1,0:T(8,128)(2,1)S(1)} collective-permute-done((bf16[2,2,4,16,576]{4,3,2,1,0:T(8,128)(2,1)S(1)}, bf16[2,2,4,16,576]{4,3,2,1,0:T(8,128)(2,1)S(1)}, u32[]{:S(2)}, u32[]{:S(2)}) %collective-permute-start.70) | collective-permute-done | bytes 294944 | tf_op jit(solution)/shard_map/ppermute | solution.py:45
  524.9 3.8 collective-permute-done.68.refs_1_
  532.9 6.4 %shard_map.229 = (f32[128,5632]{1,0:T(8,128)}, f32[128,5632]{1,0:T(8,128)}, f32[5632,128]{1,0:T(8,128)}) custom-call(s32[5]{0:T(128)S(1)} %copy-done.59, s32[4]{0:T(128)S(1)} %copy-done.57, s32[4]{0:T(128)S(1)} %pad_add_fusion.3.yhs, s32[1]{0:T(128)} %bitcast.16.core, bf16[2,2,4,3,16,704]{5,4,3,2,1,0:T(8,128)(2,1)S(1)} %pad_maximum_fusion.1.refs_0_, ...), custom_call_target="tpu_custom_call" | custom-call | flops 1000 | bytes 1500000 | tf_op jit(solution)/shard_map/pallas_call | solution.py:136
  (418 shorter events, 151.2 us)
Async XLA Ops:
  7.2 88.5 %all-gather.9.cloned.1.call-start = ((), (), s32[]{:S(2)}) async-start(), calls=%async_computation.1 | async-start | bytes 4718592 | tf_op jit(solution)/shard_map/all_gather | solution.py:733
  22.7 19.5 %collective-permute-start.2 = (bf16[4,2,32,704]{3,2,0,1:T(8,128)(2,1)S(1)}, bf16[4,2,32,704]{3,2,0,1:T(8,128)(2,1)S(1)}, u32[]{:S(2)}, u32[]{:S(2)}) collective-permute-start(bf16[4,2,32,704]{3,2,0,1:T(8,128)(2,1)S(1)} %pad_maximum_fusion.4), channel_id=1, source_target_pairs={{0,6},{1,3},{2,0},{3,5},{4,2},{5,7},{6,4},{7,1},{8,14},{9,11},{10,... | collective-permute-start | bytes 1081352 | tf_op jit(solution)/shard_map/ppermute | solution.py:45
  24.9 19.4 %collective-permute-start.3 = (bf16[4,2,32,704]{3,2,1,0:T(8,128)(2,1)S(1)}, bf16[4,2,32,704]{3,2,1,0:T(8,128)(2,1)S(1)}, u32[]{:S(2)}, u32[]{:S(2)}) collective-permute-start(bf16[4,2,32,704]{3,2,1,0:T(8,128)(2,1)S(1)} %pad_maximum_fusion.5), channel_id=1, source_target_pairs={{0,4},{1,5},{2,6},{3,7},{4,0},{5,1},{6,2},{7,3},{8,12},{9,13},{10,... | collective-permute-start | bytes 1081352 | tf_op jit(solution)/shard_map/ppermute | solution.py:45
  44.4 86.8 %all-gather.13.cloned.1.call-start = ((), (), s32[]{:S(2)}) async-start(), calls=%async_computation.4 | async-start | bytes 5898240 | tf_op jit(solution)/shard_map/all_gather | solution.py:740
  45.6 159.0 %all-gather.11.cloned.1.call-start = ((), (), s32[]{:S(2)}) async-start(), calls=%async_computation.2 | async-start | bytes 4718592 | tf_op jit(solution)/shard_map/all_gather | solution.py:741
  52.0 17.4 %collective-permute-start.6 = (bf16[8,32,576]{2,1,0:T(8,128)(2,1)S(1)}, bf16[8,32,576]{2,1,0:T(8,128)(2,1)S(1)}, u32[]{:S(2)}, u32[]{:S(2)}) collective-permute-start(bf16[8,32,576]{2,1,0:T(8,128)(2,1)S(1)} %get-tuple-element.236), channel_id=1, source_target_pairs={{0,48},{1,17},{2,50},{3,19},{4,52},{5,21},{6,54},{7,23},{8,56},{9,... | collective-permute-start | bytes 884744 | tf_op jit(solution)/shard_map/ppermute | solution.py:45
  54.9 14.6 %collective-permute-start.5 = (bf16[8,32,576]{2,1,0:T(8,128)(2,1)S(1)}, bf16[8,32,576]{2,1,0:T(8,128)(2,1)S(1)}, u32[]{:S(2)}, u32[]{:S(2)}) collective-permute-start(bf16[8,32,576]{2,1,0:T(8,128)(2,1)S(1)} %get-tuple-element.236), channel_id=1, source_target_pairs={{0,16},{1,49},{2,18},{3,51},{4,20},{5,53},{6,22},{7,55},{8,24},{9,... | collective-permute-start | bytes 884744 | tf_op jit(solution)/shard_map/ppermute | solution.py:45
  54.9 16.2 %collective-permute-start.7 = (bf16[8,32,576]{2,1,0:T(8,128)(2,1)S(1)}, bf16[8,32,576]{2,1,0:T(8,128)(2,1)S(1)}, u32[]{:S(2)}, u32[]{:S(2)}) collective-permute-start(bf16[8,32,576]{2,1,0:T(8,128)(2,1)S(1)} %get-tuple-element.236), channel_id=1, source_target_pairs={{0,32},{1,33},{2,34},{3,35},{4,36},{5,37},{6,38},{7,39},{8,40},{9,... | collective-permute-start | bytes 884744 | tf_op jit(solution)/shard_map/ppermute | solution.py:45
  71.4 17.8 %collective-permute-start.8 = (bf16[4,8,32,576]{3,2,1,0:T(8,128)(2,1)S(1)}, bf16[4,8,32,576]{3,2,1,0:T(8,128)(2,1)}, u32[]{:S(2)}, u32[]{:S(2)}) collective-permute-start(bf16[4,8,32,576]{3,2,1,0:T(8,128)(2,1)S(1)} %pad_maximum_fusion.own_ref), channel_id=1, source_target_pairs={{0,8},{1,73},{2,10},{3,75},{4,12},{5,77},{6,14},{7,79},{8,64},{9,1... | collective-permute-start | bytes 3538952 | tf_op jit(solution)/shard_map/ppermute | solution.py:45
  89.2 287.0 %reduce-scatter.2.cloned.1.call-start = ((), (), s32[]{:S(2)}) async-start(), calls=%async_computation.3 | async-start | bytes 11796480 | tf_op jit(solution)/shard_map/reduce_scatter | solution.py:799
  131.2 58.4 %collective-permute-start.20 = (bf16[4,3,8,32,704]{4,3,2,1,0:T(8,128)(2,1)}, bf16[4,3,8,32,704]{4,3,2,1,0:T(8,128)(2,1)S(1)}, u32[]{:S(2)}, u32[]{:S(2)}) collective-permute-start(bf16[4,3,8,32,704]{4,3,2,1,0:T(8,128)(2,1)} %bitcast.231), channel_id=1, source_target_pairs={{0,8},{1,73},{2,10},{3,75},{4,12},{5,77},{6,14},{7,79},{8,64},{9,1... | collective-permute-start | bytes 12976136 | tf_op jit(solution)/shard_map/ppermute | solution.py:45
  145.4 27.5 %collective-permute-start.17 = (bf16[128,2048]{1,0:T(8,128)(2,1)S(1)}, bf16[128,2048]{1,0:T(8,128)(2,1)S(1)}, u32[]{:S(2)}, u32[]{:S(2)}) collective-permute-start(bf16[128,2048]{1,0:T(8,128)(2,1)S(1)} %add_convert_fusion.4), channel_id=1, source_target_pairs={{0,4},{1,5},{2,6},{3,7},{4,0},{5,1},{6,2},{7,3},{8,12},{9,13},{10,... | collective-permute-start | bytes 1572872 | tf_op jit(solution)/shard_map/ppermute | solution.py:45
  148.8 36.3 %collective-permute-start.16 = (bf16[128,2048]{1,0:T(8,128)(2,1)}, bf16[128,2048]{1,0:T(8,128)(2,1)S(1)}, u32[]{:S(2)}, u32[]{:S(2)}) collective-permute-start(bf16[128,2048]{1,0:T(8,128)(2,1)} %add_convert_fusion.5), channel_id=1, source_target_pairs={{0,2},{1,7},{2,4},{3,1},{4,6},{5,3},{6,0},{7,5},{8,10},{9,15},{10,... | collective-permute-start | bytes 1572872 | tf_op jit(solution)/shard_map/ppermute | solution.py:45
  153.0 32.4 %collective-permute-start.15 = (bf16[128,2048]{1,0:T(8,128)(2,1)}, bf16[128,2048]{1,0:T(8,128)(2,1)S(1)}, u32[]{:S(2)}, u32[]{:S(2)}) collective-permute-start(bf16[128,2048]{1,0:T(8,128)(2,1)} %add_convert_fusion.6), channel_id=1, source_target_pairs={{0,6},{1,3},{2,0},{3,5},{4,2},{5,7},{6,4},{7,1},{8,14},{9,11},{10,... | collective-permute-start | bytes 1572872 | tf_op jit(solution)/shard_map/ppermute | solution.py:45
  158.7 26.8 %collective-permute-start.14 = (bf16[128,2048]{1,0:T(8,128)(2,1)S(1)}, bf16[128,2048]{1,0:T(8,128)(2,1)S(1)}, u32[]{:S(2)}, u32[]{:S(2)}) collective-permute-start(bf16[128,2048]{1,0:T(8,128)(2,1)S(1)} %get-tuple-element.117), channel_id=1, source_target_pairs={{0,1},{1,0},{2,3},{3,2},{4,5},{5,4},{6,7},{7,6},{8,9},{9,8},{10,11... | collective-permute-start | bytes 1572872 | tf_op jit(solution)/shard_map/ppermute | solution.py:45
  188.0 12.1 %collective-permute-start.19 = (bf16[128,2048]{1,0:T(8,128)(2,1)S(1)}, bf16[128,2048]{1,0:T(8,128)(2,1)}, u32[]{:S(2)}, u32[]{:S(2)}) collective-permute-start(bf16[128,2048]{1,0:T(8,128)(2,1)S(1)} %multiply_convert_fusion.refs_0_), channel_id=1, source_target_pairs={{0,2},{1,7},{2,4},{3,1},{4,6},{5,3},{6,0},{7,5},{8,10},{9,15},{10,... | collective-permute-start | bytes 1572872 | tf_op jit(solution)/shard_map/ppermute | solution.py:45
  189.7 15.0 %collective-permute-start.18 = (bf16[128,2048]{1,0:T(8,128)(2,1)S(1)}, bf16[128,2048]{1,0:T(8,128)(2,1)}, u32[]{:S(2)}, u32[]{:S(2)}) collective-permute-start(bf16[128,2048]{1,0:T(8,128)(2,1)S(1)} %multiply_convert_fusion.refs_0_), channel_id=1, source_target_pairs={{0,1},{1,0},{2,3},{3,2},{4,5},{5,4},{6,7},{7,6},{8,9},{9,8},{10,11... | collective-permute-start | bytes 1572872 | tf_op jit(solution)/shard_map/ppermute | solution.py:45
  200.6 24.5 %collective-permute-start.23 = (bf16[128,2048]{1,0:T(8,128)(2,1)S(1)}, bf16[128,2048]{1,0:T(8,128)(2,1)}, u32[]{:S(2)}, u32[]{:S(2)}) collective-permute-start(bf16[128,2048]{1,0:T(8,128)(2,1)S(1)} %multiply_convert_fusion.refs_0_), channel_id=1, source_target_pairs={{0,4},{1,5},{2,6},{3,7},{4,0},{5,1},{6,2},{7,3},{8,12},{9,13},{10,... | collective-permute-start | bytes 1572872 | tf_op jit(solution)/shard_map/ppermute | solution.py:45
  202.4 22.7 %collective-permute-start.22 = (bf16[128,2048]{1,0:T(8,128)(2,1)S(1)}, bf16[128,2048]{1,0:T(8,128)(2,1)}, u32[]{:S(2)}, u32[]{:S(2)}) collective-permute-start(bf16[128,2048]{1,0:T(8,128)(2,1)S(1)} %multiply_convert_fusion.refs_0_), channel_id=1, source_target_pairs={{0,6},{1,3},{2,0},{3,5},{4,2},{5,7},{6,4},{7,1},{8,14},{9,11},{10,... | collective-permute-start | bytes 1572872 | tf_op jit(solution)/shard_map/ppermute | solution.py:45
  260.7 27.0 %collective-permute-start.29 = (bf16[128,2048]{1,0:T(8,128)(2,1)}, bf16[128,2048]{1,0:T(8,128)(2,1)}, u32[]{:S(2)}, u32[]{:S(2)}) collective-permute-start(bf16[128,2048]{1,0:T(8,128)(2,1)} %get-tuple-element.213), channel_id=1, source_target_pairs={{0,2},{1,7},{2,4},{3,1},{4,6},{5,3},{6,0},{7,5},{8,10},{9,15},{10,... | collective-permute-start | bytes 1572872 | tf_op jit(solution)/shard_map/ppermute | solution.py:45
  260.7 27.0 %collective-permute-start.30 = (bf16[128,2048]{1,0:T(8,128)(2,1)}, bf16[128,2048]{1,0:T(8,128)(2,1)}, u32[]{:S(2)}, u32[]{:S(2)}) collective-permute-start(bf16[128,2048]{1,0:T(8,128)(2,1)} %get-tuple-element.214), channel_id=1, source_target_pairs={{0,4},{1,5},{2,6},{3,7},{4,0},{5,1},{6,2},{7,3},{8,12},{9,13},{10,... | collective-permute-start | bytes 1572872 | tf_op jit(solution)/shard_map/ppermute | solution.py:45
  287.7 172.5 %all-gather.15.cloned.1.call-start = ((), (), s32[]{:S(2)}) async-start(), calls=%async_computation.5 | async-start | bytes 1114112 | tf_op jit(solution)/shard_map/all_gather | solution.py:842
  294.2 14.7 %collective-permute-start.38 = (bf16[128,2048]{1,0:T(8,128)(2,1)S(1)}, bf16[128,2048]{1,0:T(8,128)(2,1)S(1)}, u32[]{:S(2)}, u32[]{:S(2)}) collective-permute-start(bf16[128,2048]{1,0:T(8,128)(2,1)S(1)} %get-tuple-element.199.refs_1_.refs_8_), channel_id=1, source_target_pairs={{0,6},{1,3},{2,0},{3,5},{4,2},{5,7},{6,4},{7,1},{8,14},{9,11},{10,... | collective-permute-start | bytes 1572872 | tf_op jit(solution)/shard_map/ppermute | solution.py:45
  295.5 14.2 %collective-permute-start.36 = (bf16[128,2048]{1,0:T(8,128)(2,1)S(1)}, bf16[128,2048]{1,0:T(8,128)(2,1)S(1)}, u32[]{:S(2)}, u32[]{:S(2)}) collective-permute-start(bf16[128,2048]{1,0:T(8,128)(2,1)S(1)} %get-tuple-element.199.refs_1_.refs_8_), channel_id=1, source_target_pairs={{0,2},{1,7},{2,4},{3,1},{4,6},{5,3},{6,0},{7,5},{8,10},{9,15},{10,... | collective-permute-start | bytes 1572872 | tf_op jit(solution)/shard_map/ppermute | solution.py:45
  310.2 19.4 %collective-permute-start.31 = (bf16[128,2048]{1,0:T(8,128)(2,1)S(1)}, bf16[128,2048]{1,0:T(8,128)(2,1)S(1)}, u32[]{:S(2)}, u32[]{:S(2)}) collective-permute-start(bf16[128,2048]{1,0:T(8,128)(2,1)S(1)} %get-tuple-element.199.refs_1_.refs_8_), channel_id=1, source_target_pairs={{0,4},{1,5},{2,6},{3,7},{4,0},{5,1},{6,2},{7,3},{8,12},{9,13},{10,... | collective-permute-start | bytes 1572872 | tf_op jit(solution)/shard_map/ppermute | solution.py:45
  343.1 16.3 %collective-permute-start.32 = (bf16[128,2048]{1,0:T(8,128)(2,1)S(1)}, bf16[128,2048]{1,0:T(8,128)(2,1)S(1)}, u32[]{:S(2)}, u32[]{:S(2)}) collective-permute-start(bf16[128,2048]{1,0:T(8,128)(2,1)S(1)} %copy-done.81), channel_id=1, source_target_pairs={{0,4},{1,5},{2,6},{3,7},{4,0},{5,1},{6,2},{7,3},{8,12},{9,13},{10,... | collective-permute-start | bytes 1572872 | tf_op jit(solution)/shard_map/ppermute | solution.py:45
  343.1 24.9 %collective-permute-start.33 = (bf16[128,2048]{1,0:T(8,128)(2,1)S(1)}, bf16[128,2048]{1,0:T(8,128)(2,1)S(1)}, u32[]{:S(2)}, u32[]{:S(2)}) collective-permute-start(bf16[128,2048]{1,0:T(8,128)(2,1)S(1)} %get-tuple-element.141), channel_id=1, source_target_pairs={{0,6},{1,3},{2,0},{3,5},{4,2},{5,7},{6,4},{7,1},{8,14},{9,11},{10,... | collective-permute-start | bytes 1572872 | tf_op jit(solution)/shard_map/ppermute | solution.py:45
  347.0 23.1 %collective-permute-start.34 = (bf16[128,2048]{1,0:T(8,128)(2,1)S(1)}, bf16[128,2048]{1,0:T(8,128)(2,1)S(1)}, u32[]{:S(2)}, u32[]{:S(2)}) collective-permute-start(bf16[128,2048]{1,0:T(8,128)(2,1)S(1)} %copy-done.80), channel_id=1, source_target_pairs={{0,2},{1,7},{2,4},{3,1},{4,6},{5,3},{6,0},{7,5},{8,10},{9,15},{10,... | collective-permute-start | bytes 1572872 | tf_op jit(solution)/shard_map/ppermute | solution.py:45
  347.2 24.1 %collective-permute-start.42 = (bf16[1024,64]{1,0:T(8,128)(2,1)S(1)}, bf16[1024,64]{1,0:T(8,128)(2,1)}, u32[]{:S(2)}, u32[]{:S(2)}) collective-permute-start(bf16[1024,64]{1,0:T(8,128)(2,1)S(1)} %slice.399), channel_id=1, source_target_pairs={{0,8},{1,9},{2,10},{3,11},{4,12},{5,13},{6,14},{7,15},{8,0},{9,1},... | collective-permute-start | bytes 393224 | tf_op jit(solution)/shard_map/ppermute | solution.py:45
  379.1 21.3 %collective-permute-start.44 = (bf16[4,2,3,16,704]{4,3,2,1,0:T(8,128)(2,1)}, bf16[4,2,3,16,704]{4,3,2,1,0:T(8,128)(2,1)}, u32[]{:S(2)}, u32[]{:S(2)}) collective-permute-start(bf16[4,2,3,16,704]{4,3,2,1,0:T(8,128)(2,1)} %get-tuple-element.204), channel_id=1, source_target_pairs={{0,64},{1,65},{2,66},{3,67},{4,68},{5,69},{6,70},{7,71},{8,72},{9,... | collective-permute-start | bytes 1622024 | tf_op jit(solution)/shard_map/ppermute | solution.py:45
  380.5 26.0 %collective-permute-start.46 = (bf16[4,2,3,16,704]{4,3,2,1,0:T(8,128)(2,1)}, bf16[4,2,3,16,704]{4,3,2,1,0:T(8,128)(2,1)}, u32[]{:S(2)}, u32[]{:S(2)}) collective-permute-start(bf16[4,2,3,16,704]{4,3,2,1,0:T(8,128)(2,1)} %get-tuple-element.205), channel_id=1, source_target_pairs={{0,8},{1,73},{2,10},{3,75},{4,12},{5,77},{6,14},{7,79},{8,64},{9,1... | collective-permute-start | bytes 1622024 | tf_op jit(solution)/shard_map/ppermute | solution.py:45
  382.7 26.0 %collective-permute-start.45 = (bf16[4,2,3,16,704]{4,3,2,1,0:T(8,128)(2,1)}, bf16[4,2,3,16,704]{4,3,2,1,0:T(8,128)(2,1)}, u32[]{:S(2)}, u32[]{:S(2)}) collective-permute-start(bf16[4,2,3,16,704]{4,3,2,1,0:T(8,128)(2,1)} %get-tuple-element.206), channel_id=1, source_target_pairs={{0,72},{1,9},{2,74},{3,11},{4,76},{5,13},{6,78},{7,15},{8,0},{9,65... | collective-permute-start | bytes 1622024 | tf_op jit(solution)/shard_map/ppermute | solution.py:45
  399.1 25.7 %collective-permute-start.43 = (bf16[4,128,2048]{2,1,0:T(8,128)(2,1)}, bf16[4,128,2048]{2,1,0:T(8,128)(2,1)S(1)}, u32[]{:S(2)}, u32[]{:S(2)}) collective-permute-start(bf16[4,128,2048]{2,1,0:T(8,128)(2,1)} %get-tuple-element.156), channel_id=1, source_target_pairs={{0,1},{1,0},{2,3},{3,2},{4,5},{5,4},{6,7},{7,6},{8,9},{9,8},{10,11... | collective-permute-start | bytes 6291464 | tf_op jit(solution)/shard_map/ppermute | solution.py:45
  399.4 17.7 %collective-permute-start.56 = (bf16[4,4,2,16,576]{4,3,2,1,0:T(8,128)(2,1)}, bf16[4,4,2,16,576]{4,3,2,1,0:T(8,128)(2,1)S(1)}, u32[]{:S(2)}, u32[]{:S(2)}) collective-permute-start(bf16[4,4,2,16,576]{4,3,2,1,0:T(8,128)(2,1)} %get-tuple-element.181), channel_id=1, source_target_pairs={{0,16},{1,49},{2,18},{3,51},{4,20},{5,53},{6,22},{7,55},{8,24},{9,... | collective-permute-start | bytes 1769480 | tf_op jit(solution)/shard_map/ppermute | solution.py:45
  400.4 130.5 %all-gather.17.cloned.1.call-start = ((), (), s32[]{:S(2)}) async-start(), calls=%async_computation.6 | async-start | bytes 1179648 | tf_op jit(solution)/shard_map/all_gather | solution.py:851
  400.5 31.1 %collective-permute-start.55 = (bf16[4,4,2,16,576]{4,3,2,1,0:T(8,128)(2,1)}, bf16[4,4,2,16,576]{4,3,2,1,0:T(8,128)(2,1)S(1)}, u32[]{:S(2)}, u32[]{:S(2)}) collective-permute-start(bf16[4,4,2,16,576]{4,3,2,1,0:T(8,128)(2,1)} %get-tuple-element.178), channel_id=1, source_target_pairs={{0,48},{1,17},{2,50},{3,19},{4,52},{5,21},{6,54},{7,23},{8,56},{9,... | collective-permute-start | bytes 1769480 | tf_op jit(solution)/shard_map/ppermute | solution.py:45
  420.7 12.1 %collective-permute-start.57 = (bf16[4,4,2,16,576]{4,3,2,1,0:T(8,128)(2,1)S(1)}, bf16[4,4,2,16,576]{4,3,2,1,0:T(8,128)(2,1)S(1)}, u32[]{:S(2)}, u32[]{:S(2)}) collective-permute-start(bf16[4,4,2,16,576]{4,3,2,1,0:T(8,128)(2,1)S(1)} %add_convert_fusion.1), channel_id=1, source_target_pairs={{0,16},{1,49},{2,18},{3,51},{4,20},{5,53},{6,22},{7,55},{8,24},{9,... | collective-permute-start | bytes 1769480 | tf_op jit(solution)/shard_map/ppermute | solution.py:45
  425.6 17.2 %collective-permute-start.47 = (bf16[128,2048]{1,0:T(8,128)(2,1)S(1)}, bf16[128,2048]{1,0:T(8,128)(2,1)S(1)}, u32[]{:S(2)}, u32[]{:S(2)}) collective-permute-start(bf16[128,2048]{1,0:T(8,128)(2,1)S(1)} %get-tuple-element.168), channel_id=1, source_target_pairs={{0,4},{1,5},{2,6},{3,7},{4,0},{5,1},{6,2},{7,3},{8,12},{9,13},{10,... | collective-permute-start | bytes 1572872 | tf_op jit(solution)/shard_map/ppermute | solution.py:45
  429.3 24.1 %collective-permute-start.48 = (bf16[128,2048]{1,0:T(8,128)(2,1)S(1)}, bf16[128,2048]{1,0:T(8,128)(2,1)S(1)}, u32[]{:S(2)}, u32[]{:S(2)}) collective-permute-start(bf16[128,2048]{1,0:T(8,128)(2,1)S(1)} %get-tuple-element.169), channel_id=1, source_target_pairs={{0,6},{1,3},{2,0},{3,5},{4,2},{5,7},{6,4},{7,1},{8,14},{9,11},{10,... | collective-permute-start | bytes 1572872 | tf_op jit(solution)/shard_map/ppermute | solution.py:45
  429.5 24.0 %collective-permute-start.49 = (bf16[128,2048]{1,0:T(8,128)(2,1)S(1)}, bf16[128,2048]{1,0:T(8,128)(2,1)S(1)}, u32[]{:S(2)}, u32[]{:S(2)}) collective-permute-start(bf16[128,2048]{1,0:T(8,128)(2,1)S(1)} %get-tuple-element.170), channel_id=1, source_target_pairs={{0,2},{1,7},{2,4},{3,1},{4,6},{5,3},{6,0},{7,5},{8,10},{9,15},{10,... | collective-permute-start | bytes 1572872 | tf_op jit(solution)/shard_map/ppermute | solution.py:45
  431.6 28.5 %collective-permute-start.54 = (bf16[2,4,3,16,704]{4,3,2,1,0:T(8,128)(2,1)S(1)}, bf16[2,4,3,16,704]{4,3,2,1,0:T(8,128)(2,1)S(1)}, u32[]{:S(2)}, u32[]{:S(2)}) collective-permute-start(bf16[2,4,3,16,704]{4,3,2,1,0:T(8,128)(2,1)S(1)} %get-tuple-element.227), channel_id=1, source_target_pairs={{0,64},{1,65},{2,66},{3,67},{4,68},{5,69},{6,70},{7,71},{8,72},{9,... | collective-permute-start | bytes 1622024 | tf_op jit(solution)/shard_map/ppermute | solution.py:45
  433.2 21.8 %collective-permute-start.58 = (bf16[4,2,16,576]{3,2,1,0:T(8,128)(2,1)S(1)}, bf16[4,2,16,576]{3,2,1,0:T(8,128)(2,1)S(1)}, u32[]{:S(2)}, u32[]{:S(2)}) collective-permute-start(bf16[4,2,16,576]{3,2,1,0:T(8,128)(2,1)S(1)} %get-tuple-element.223), channel_id=1, source_target_pairs={{0,64},{1,65},{2,66},{3,67},{4,68},{5,69},{6,70},{7,71},{8,72},{9,... | collective-permute-start | bytes 442376 | tf_op jit(solution)/shard_map/ppermute | solution.py:45
  465.6 25.3 %collective-permute-start.67 = (bf16[2,2,4,3,16,704]{5,4,3,2,1,0:T(8,128)(2,1)S(1)}, bf16[2,2,4,3,16,704]{5,4,3,2,1,0:T(8,128)(2,1)S(1)}, u32[]{:S(2)}, u32[]{:S(2)}) collective-permute-start(bf16[2,2,4,3,16,704]{5,4,3,2,1,0:T(8,128)(2,1)S(1)} %pad_maximum_fusion.1.refs_0_), channel_id=1, source_target_pairs={{0,16},{1,49},{2,18},{3,51},{4,20},{5,53},{6,22},{7,55},{8,24},{9,... | collective-permute-start | bytes 3244040 | tf_op jit(solution)/shard_map/ppermute | solution.py:45
  477.6 55.2 %collective-permute-start.71 = (bf16[2,2,4,3,16,704]{5,4,3,2,1,0:T(8,128)(2,1)S(1)}, bf16[2,2,4,3,16,704]{5,4,3,2,1,0:T(8,128)(2,1)}, u32[]{:S(2)}, u32[]{:S(2)}) collective-permute-start(bf16[2,2,4,3,16,704]{5,4,3,2,1,0:T(8,128)(2,1)S(1)} %pad_maximum_fusion.1.refs_0_), channel_id=1, source_target_pairs={{0,48},{1,17},{2,50},{3,19},{4,52},{5,21},{6,54},{7,23},{8,56},{9,... | collective-permute-start | bytes 3244040 | tf_op jit(solution)/shard_map/ppermute | solution.py:45
  491.0 41.9 %collective-permute-start.72 = (bf16[2,2,4,3,16,704]{5,4,3,2,1,0:T(8,128)(2,1)S(1)}, bf16[2,2,4,3,16,704]{5,4,3,2,1,0:T(8,128)(2,1)}, u32[]{:S(2)}, u32[]{:S(2)}) collective-permute-start(bf16[2,2,4,3,16,704]{5,4,3,2,1,0:T(8,128)(2,1)S(1)} %collective-permute-done.67.refs_1_), channel_id=1, source_target_pairs={{0,16},{1,49},{2,18},{3,51},{4,20},{5,53},{6,22},{7,55},{8,24},{9,... | collective-permute-start | bytes 3244040 | tf_op jit(solution)/shard_map/ppermute | solution.py:45
  491.0 32.8 %collective-permute-start.70 = (bf16[2,2,4,16,576]{4,3,2,1,0:T(8,128)(2,1)S(1)}, bf16[2,2,4,16,576]{4,3,2,1,0:T(8,128)(2,1)S(1)}, u32[]{:S(2)}, u32[]{:S(2)}) collective-permute-start(bf16[2,2,4,16,576]{4,3,2,1,0:T(8,128)(2,1)S(1)} %pad_maximum_fusion.7.refs_0_), channel_id=1, source_target_pairs={{0,32},{1,33},{2,34},{3,35},{4,36},{5,37},{6,38},{7,39},{8,40},{9,... | collective-permute-start | bytes 884744 | tf_op jit(solution)/shard_map/ppermute | solution.py:45
  492.1 32.8 %collective-permute-start.69 = (bf16[2,2,4,16,576]{4,3,2,1,0:T(8,128)(2,1)S(1)}, bf16[2,2,4,16,576]{4,3,2,1,0:T(8,128)(2,1)S(1)}, u32[]{:S(2)}, u32[]{:S(2)}) collective-permute-start(bf16[2,2,4,16,576]{4,3,2,1,0:T(8,128)(2,1)S(1)} %pad_maximum_fusion.7.refs_0_), channel_id=1, source_target_pairs={{0,48},{1,17},{2,50},{3,19},{4,52},{5,21},{6,54},{7,23},{8,56},{9,... | collective-permute-start | bytes 884744 | tf_op jit(solution)/shard_map/ppermute | solution.py:45
  494.4 34.3 %collective-permute-start.68 = (bf16[2,2,4,16,576]{4,3,2,1,0:T(8,128)(2,1)S(1)}, bf16[2,2,4,16,576]{4,3,2,1,0:T(8,128)(2,1)S(1)}, u32[]{:S(2)}, u32[]{:S(2)}) collective-permute-start(bf16[2,2,4,16,576]{4,3,2,1,0:T(8,128)(2,1)S(1)} %pad_maximum_fusion.7.refs_0_), channel_id=1, source_target_pairs={{0,16},{1,49},{2,18},{3,51},{4,20},{5,53},{6,22},{7,55},{8,24},{9,... | collective-permute-start | bytes 884744 | tf_op jit(solution)/shard_map/ppermute | solution.py:45
  (127 other events, 1482.8 us)
Sparse Core Ops, SparseCore 0:
  44.5 31.9 all-gather.8
  78.8 52.3 all-gather.12
  132.9 55.1 all-gather.10
  287.8 88.4 reduce-scatter.1
  400.5 35.5 all-gather.14
  462.4 46.8 all-gather.16

commit v5 on v4

--- a/solution.py
+++ b/solution.py
@@ -523,31 +523,63 @@
     return out[:3], out[3:7], out[7]
 
 
-def mlp_grads_kernel(column, yhs, core, nat, *refs):
-    tokens, (g_ref, da_ref, dc_ref, z_ref), out_ref, (turned, grads) = refs[:8], refs[8:12], refs[12], refs[13:]
-    half = pl.program_id(0)
+def grads_specs(tail):
+    zeros = (0,) * (1 + len(tail))
+    x_first = pl.BlockSpec((2, 1, 2) + tail, lambda h, p, *_: (h, jnp.minimum(p, 1)) + zeros)
+    y_own = pl.BlockSpec((4, 1, 2) + tail, lambda h, p, *_: (0, jnp.where(h == 0, jnp.maximum(p - 2, 0), 1)) + zeros)
+    y_other = pl.BlockSpec((4, 1, 2) + tail, lambda h, p, *_: (0, jnp.where(h == 1, jnp.maximum(p - 2, 0), 0)) + zeros)
+    return [x_first] * 4 + [y_own] * 2 + [y_other] * 2, [sds((4, 2, 2) + tail)] * 8
+
+
+def write_grads(outs, xs, yhs, core, write, first_rows=None):
+    half, p = pl.program_id(0), pl.program_id(1)
+
+    def go(pos, r, ref, first=False):
+        inside = yhs[2 * half + pos] * 64 + (first_rows(r) if first and first_rows else xs[r] * 16)
+        for rc in range(2):
+            write(ref.at[rc], inside, jnp.abs(core[0] - rc), rc)
+
+    @pl.when(p < 2)
+    def _():
+        for r in range(4):
+            for pos in range(2):
+                go(pos, r, outs[r].at[pos, 0], True)
+
+    for each in range(2):
+
+        @pl.when((p >= 2) & (half == each))
+        def _():
+            for r in range(4):
+                for pos in range(2):
+                    go(pos, r, outs[4 + 2 * each + pos].at[r, 0])
+
+
+def mlp_grads_kernel(column, xs, yhs, core, nat, *refs):
+    tokens, (g_ref, da_ref, dc_ref, z_ref), outs, (turned, grads) = refs[:8], refs[8:12], refs[12:17], refs[17:]
     rows = jnp.concatenate([ref[...] for ref in tokens], axis=0).T
     grads[0] = dot(rows, da_ref[...])
     grads[1] = dot(rows, dc_ref[...])
     for r in range(8):
         turned[:, TOK * r : TOK * (r + 1)] = g_ref[pl.ds(pl.multiple_of(nat[r] * TOK, TOK), TOK), :].T
     grads[2] = dot(turned[...], z_ref[...])
-    for pos in range(2):
-        for rc in range(2):
-            start = jnp.abs(core[0] - rc) * 128 + yhs[2 * half + pos] * 64
-            for r in range(4):
-                for m in range(3):
-                    out_ref[r, pos, 0, rc, m] = grads[m, at_rows(start + 16 * r, 16), :].astype(BF)
-
-
-def mlp_grads(column, yhs, core, nat, tokens, g, da, dc, z):
+
+    def write(ref, inside, which, rc):
+        for m in range(3):
+            ref[m] = grads[m, at_rows(which * 128 + inside, 16), :].astype(BF)
+
+    write_grads([outs[0].at[r] for r in range(4)] + list(outs[1:]), xs, yhs, core, write, lambda r: 16 * r)
+
+
+def mlp_grads(column, xs, yhs, core, nat, tokens, g, da, dc, z):
     col = lambda h, p, column, *_: (0, column[4 * h + p])
     hidden = pl.BlockSpec((8 * TOK, WIDE), lambda h, p, *_: (0, 0))
+    tail = (3, 16, WIDE)
+    specs, shapes = grads_specs(tail)
+    x_first = pl.BlockSpec((4, 2, 1, 2) + tail, lambda h, p, *_: (0, h, jnp.minimum(p, 1), 0, 0, 0, 0))
     return call(
-        mlp_grads_kernel, (column, yhs, core, nat), (2, 4),
+        mlp_grads_kernel, (column, xs, yhs, core, nat), (2, 4),
         [pl.BlockSpec((TOK, 256), col)] * 8 + [pl.BlockSpec((8 * TOK, 256), col), hidden, hidden, hidden],
-        pl.BlockSpec((4, 2, 1, 2, 3, 16, WIDE), lambda h, p, *_: (0, h, p, 0, 0, 0, 0)),
-        sds((4, 4, 4, 2, 3, 16, WIDE)),
+        [x_first] + specs[4:], [sds((4, 4, 2, 2) + tail)] + shapes[4:],
         [pltpu.VMEM((256, 8 * TOK), BF), pltpu.VMEM((3, 256, WIDE), F32)],
         17, tuple(tokens) + (g, da, dc, z),
     )
@@ -791,12 +823,13 @@
             mlp_parts[7] = swap(after(third, kept[0]))
         at = after(chunk, swapped)
     hidden, gate_grad_rows, up_grad_rows = kept
-    mlp_sums = mlp_grads(
-        column, yhs, core, after(at, got[1], sums[2], sums[3]), mlp_parts, grad_rows, gate_grad_rows, up_grad_rows, hidden
+    mlp_outs = mlp_grads(
+        column, xs, yhs, core, after(at, got[1], sums[2], sums[3]), mlp_parts, grad_rows, gate_grad_rows, up_grad_rows, hidden
     )
     normed_grad = add(sums[0], *got[1:])
-    mlp_sums = after(mlp_sums, got[2], got[3])
-    mlp_sums = lax.psum_scatter(mlp_sums, "batch", scatter_dimension=0, axis_index_groups=X_GROUPS)
+    mlp_outs = after(mlp_outs, got[2], got[3])
+    mlp_low = lax.psum_scatter(mlp_outs[0], "batch", scatter_dimension=0, axis_index_groups=X_GROUPS)
+    high_far = step(mlp_outs[2], "y", 1)
 
     residual_grad = cotangent[0].astype(F32) + norm_back(residual, scale_mlp, gain_two, normed_grad)
     mlp_gain_part = jnp.sum(normed_grad * residual * scale_mlp, axis=0)
@@ -818,21 +851,24 @@
     branch_parts = [own, swap(own)]
     rows_0, *sums = back(0, branch_parts, (), False)
     branch_parts += [first, swap(after(first, rows_0)), second, swap(after(second, rows_0))]
-    rows_1, *sums = back(2, branch_parts[2:], sums, False)
+    high_after = step(after(mlp_outs[3], branch_parts[3]), "y", -1)
+    high_before = step(add(after(mlp_outs[4], branch_parts[3]), high_far).astype(BF), "y", 1)
+    rows_1, *sums = back(2, after(branch_parts[2:], high_far), sums, False)
     branch_parts += [third, swap(after(third, rows_1))]
     outs = after(outs, third)
     got_outs = [give(g, outs[g]) for g in (3, 1, 2)]
-    layer_out = (residual + add(outs[0], *got_outs)).astype(BF)[None]
-    rows_2, kv_keep, kv_give = back(6, branch_parts[6:], sums, True)
+    rows_2, kv_keep, kv_give = back(6, after(branch_parts[6:], high_after), sums, True)
     query_grad_rows = [rows_0, rows_1, rows_2]
-    kv_terms = add(kv_keep, swap(kv_give))
+    kv_terms = add(after(kv_keep, got_outs), swap(kv_give))
     half_rows = 8 * TOK
     kv_half = to_half(kv_terms[half_rows:].astype(BF))
     kv_grad_rows = add(kv_terms[:half_rows], kv_half).astype(BF)
-    mlp_sums = after(mlp_sums, kv_half)
-    mlp_sums = ring_scatter(mlp_sums[0], mlp_sums[2], mlp_sums[3], mlp_sums[1], "y").astype(BF)
-    mlp_rows = mlp_sums
-    mlp_sums, mlp_swapped = resplit_back(mlp_sums)
+    high = add(mlp_outs[1], high_after, after(high_before, rows_2)).astype(BF)
+    high = ring_scatter(high[0], high[1], high[2], high[3], "x").astype(BF)
+    mlp_low = after(mlp_low, rows_2)
+    low = ring_scatter(mlp_low[0], mlp_low[2], mlp_low[3], mlp_low[1], "y").astype(BF)
+    kv_grad_rows = after(kv_grad_rows, low, high)
+    mlp_sums, mlp_swapped = resplit_back([low[0], low[1], high[0], high[1]])
 
     attn_partial = project_back(query_grad_rows, kv_grad_rows, w_qkv)
     attn_outs, attn_gain_part = attn_grads(
@@ -841,16 +877,18 @@
     gain_grads = jnp.stack([attn_gain_part / gain_one, mlp_gain_part])
     gain_grads = lax.all_gather(jnp.pad(gain_grads, ((0, 6), (0, 0))), "blk")
 
+    layer_out = (residual + add(after(outs[0], attn_outs[0]), *got_outs)).astype(BF)[None]
     mlp_across = across(mlp_sums, "y")
     mlp_sums = ring_gather(jnp.stack([mlp_sums, mlp_across]), "x", True)
     swapped = swap(attn_partial[4])
-    sums = after([add(attn_partial[g], swapped[g]).astype(BF) for g in range(4)], mlp_rows, got_outs)
-    normed_attn_grad = add(sums[0], *[give(g, sums[g]) for g in (3, 1, 2)])
-    attn_sums = after(ring_scatter(*attn_outs, "x", mlp_rows).astype(BF), mlp_swapped)
-    gain_grads = jnp.sum(after(gain_grads, mlp_across), axis=0)
+    sums = [add(attn_partial[g], swapped[g]).astype(BF) for g in range(4)]
+    got = [give(g, sums[g]) for g in (3, 1, 2)]
+    normed_attn_grad = add(sums[0], *got)
+    attn_sums = after(ring_scatter(*attn_outs, "x", mlp_swapped).astype(BF), *got)
+    gain_grads = jnp.sum(after(gain_grads, attn_sums), axis=0)
     gain_grads = lax.all_gather(jnp.pad(gain_grads, ((0, 8), (0, 0))), "batch")
     attn_sums = ring_scatter(attn_sums[0], attn_sums[2], attn_sums[3], attn_sums[1], "y").astype(BF)
-    attn_sums = after(attn_sums, mlp_across, normed_attn_grad)
+    attn_sums = after(attn_sums, mlp_across)
     out_sums = send(
         attn_sums[..., :QUERY], lambda yh, x, yl, z, c: (yh, x, z // 2, 2 * (z % 2) + c, yl)
     )

time: 555 us -> 549 us (0.989)
  the two profiles are of different devices: /device:TPU:24 before, /device:TPU:1 now
where the time goes in v5:
time: 549 us; the launch traced here: 538 us
  waiting for transfers between devices  191 us (35%)
  Pallas kernels  159 us (29%)
  starting transfers between devices  114 us (21%)
  other arithmetic  31.8 us (6%)
  local copies, waits for them, and re-layouts  26.1 us (5%)
  between operations  15.9 us (3%)
    ppermute x79, waiting for transfers between devices, send(): return lax.ppermute(value, BOTH, pairs)  180 us
    pallas_call x18, Pallas kernels, call(): pl.pallas_call(body, grid_spec=pltpu.PrefetchScalarGridSpec(num_scalar_pr...  159 us
    ppermute x79, starting transfers between devices, send(): return lax.ppermute(value, BOTH, pairs)  114 us
    unnamed x204, local copies, waits for them, and re-layouts  16.7 us
  transfers between devices with their start and end apart: 85, of which 39 were waited for; matrix products, arithmetic and copies ran while one was open for 7% of the time, Pallas kernels for 25%

profile of v5, /device:TPU:1, one launch (start us, length us, event | category | flops | bytes accessed | tf_op | source)
XLA Modules:
  0.0 538.1 jit_solution(10627353237178947952)
XLA Ops:
  12.9 4.0 shard_map.212
  22.1 3.9 collective-permute-start.1
  28.5 14.3 %collective-permute-done.1 = bf16[4,2,32,704]{3,2,0,1:T(8,128)(2,1)S(1)} collective-permute-done((bf16[4,2,32,704]{3,2,0,1:T(8,128)(2,1)S(1)}, bf16[4,2,32,704]{3,2,0,1:T(8,128)(2,1)S(1)}, u32[]{:S(2)}, u32[]{:S(2)}) %collective-permute-start.1) | collective-permute-done | bytes 360480 | tf_op jit(solution)/shard_map/ppermute | solution.py:45
  46.6 3.7 collective-permute-start.4
  57.5 11.9 %collective-permute-done.6 = bf16[8,32,576]{2,1,0:T(8,128)(2,1)S(1)} collective-permute-done((bf16[8,32,576]{2,1,0:T(8,128)(2,1)S(1)}, bf16[8,32,576]{2,1,0:T(8,128)(2,1)S(1)}, u32[]{:S(2)}, u32[]{:S(2)}) %collective-permute-start.6) | collective-permute-done | bytes 294944 | tf_op jit(solution)/shard_map/ppermute | solution.py:45
  69.6 4.0 collective-permute-start.8
  73.7 14.5 %collective-permute-done.8.other_ref = bf16[4,8,32,576]{3,2,1,0:T(8,128)(2,1)} collective-permute-done((bf16[4,8,32,576]{3,2,1,0:T(8,128)(2,1)S(1)}, bf16[4,8,32,576]{3,2,1,0:T(8,128)(2,1)}, u32[]{:S(2)}, u32[]{:S(2)}) %collective-permute-start.8) | collective-permute-done | bytes 1179680 | tf_op jit(solution)/shard_map/ppermute | solution.py:45
  88.6 5.0 shard_map.213
  96.5 6.0 %shard_map.214 = (bf16[1024,256]{1,0:T(8,128)(2,1)S(1)}, bf16[2,1024,64]{2,1,0:T(8,128)(2,1)S(1)}) custom-call(s32[8]{0:T(128)S(1)} %stack.212.chunk.nat, bf16[1024,2048]{1,0:T(8,128)(2,1)} %all-gather.9.cloned.1.call-done.refs_0_.refs_1_.refs_2_.refs_3_.refs_4_.refs_5_.refs_6_.refs_7_, ...), custom_call_target="tpu_custom_call" | custom-call | flops 1000 | bytes 1500000 | tf_op jit(solution)/shard_map/pallas_call | solution.py:136
  104.0 4.5 collective-permute-done.9
  108.5 4.3 collective-permute-start.10
  114.7 6.1 %shard_map.215 = (bf16[256,256]{1,0:T(8,128)(2,1)S(1)}, bf16[128,2048]{1,0:T(8,128)(2,1)S(1)}, bf16[128,2048]{1,0:T(8,128)(2,1)}) custom-call(s32[8]{0:T(128)S(1)} %bitcast.250, s32[16]{0:T(128)S(1)} %select_reduce_fusion.1.key_slot, bf16[1024,256]{1,0:T(8,128)(2,1)S(1)} %get-tuple-element.123.q_ref.refs_0_, ...), custom_call_target="tpu_custom_call" | custom-call | flops 1000 | bytes 1800000 | tf_op jit(solution)/shard_map/pallas_call | solution.py:136
  121.8 10.5 %all-gather.13.cloned.1.call-done = bf16[12,8,32,704]{3,2,1,0:T(8,128)(2,1)} async-done(((bf16[3,8,32,704]{3,2,1,0:T(8,128)(2,1)}), bf16[12,8,32,704]{3,2,1,0:T(8,128)(2,1)}) %all-gather.13.cloned.1.call-update) | async-done | bytes 4325392 | tf_op jit(solution)/shard_map/all_gather | solution.py:772
  134.8 6.9 %shard_map.217 = (bf16[256,256]{1,0:T(8,128)(2,1)S(1)}, bf16[128,2048]{1,0:T(8,128)(2,1)S(1)}, bf16[128,2048]{1,0:T(8,128)(2,1)S(1)}) custom-call(s32[8]{0:T(128)S(1)} %bitcast.251, s32[16]{0:T(128)S(1)} %select_reduce_fusion.1.key_slot, bf16[1024,256]{1,0:T(8,128)(2,1)S(1)} %get-tuple-element.123.q_ref.refs_0_, ...), custom_call_target="tpu_custom_call" | custom-call | flops 1000 | bytes 1800000 | tf_op jit(solution)/shard_map/pallas_call | solution.py:136
  142.3 6.6 %shard_map.216 = (bf16[256,256]{1,0:T(8,128)(2,1)S(1)}, bf16[128,2048]{1,0:T(8,128)(2,1)S(1)}, bf16[128,2048]{1,0:T(8,128)(2,1)S(1)}) custom-call(s32[8]{0:T(128)S(1)} %bitcast.252, s32[16]{0:T(128)S(1)} %select_reduce_fusion.1.key_slot, bf16[1024,256]{1,0:T(8,128)(2,1)S(1)} %get-tuple-element.123.q_ref.refs_0_, ...), custom_call_target="tpu_custom_call" | custom-call | flops 1000 | bytes 1800000 | tf_op jit(solution)/shard_map/pallas_call | solution.py:136
  154.0 3.5 shard_map.218
  159.7 15.0 %collective-permute-done.17 = bf16[128,2048]{1,0:T(8,128)(2,1)S(1)} collective-permute-done((bf16[128,2048]{1,0:T(8,128)(2,1)S(1)}, bf16[128,2048]{1,0:T(8,128)(2,1)S(1)}, u32[]{:S(2)}, u32[]{:S(2)}) %collective-permute-start.17) | collective-permute-done | bytes 524320 | tf_op jit(solution)/shard_map/ppermute | solution.py:45
  174.6 12.2 %collective-permute-done.16 = bf16[128,2048]{1,0:T(8,128)(2,1)S(1)} collective-permute-done((bf16[128,2048]{1,0:T(8,128)(2,1)S(1)}, bf16[128,2048]{1,0:T(8,128)(2,1)S(1)}, u32[]{:S(2)}, u32[]{:S(2)}) %collective-permute-start.16) | collective-permute-done | bytes 524320 | tf_op jit(solution)/shard_map/ppermute | solution.py:45
  189.7 8.5 %shard_map.219 = bf16[3,2,8,128,704]{4,3,2,1,0:T(8,128)(2,1)} custom-call(s32[8]{0:T(128)S(1)} %stack.223.slot, s32[2]{0:T(128)S(1)} %pad_add_fusion.2.halves, bf16[4,3,8,32,704]{4,3,2,1,0:T(8,128)(2,1)S(1)} %bitcast.249, bf16[4,3,8,32,704]{4,3,2,1,0:T(8,128)(2,1)} %collective-permute-done.20.other_ref), custom_call_target="tpu_custom_call" | custom-call | flops 1000 | bytes 1800000 | tf_op jit(solution)/shard_map/pallas_call | solution.py:136
  201.6 18.0 %shard_map.220 = (bf16[1024,704]{1,0:T(8,128)(2,1)S(1)}, bf16[1024,704]{1,0:T(8,128)(2,1)}, bf16[1024,704]{1,0:T(8,128)(2,1)}, bf16[128,2048]{1,0:T(8,128)(2,1)S...) custom-call(s32[8]{0:T(128)S(1)} %stack.212.chunk.nat, ...), custom_call_target="tpu_custom_call" | custom-call | flops 1000 | bytes 5400000 | tf_op jit(solution)/shard_map/pallas_call | solution.py:136
  222.3 3.3 collective-permute-done.24
  227.1 18.0 %shard_map.221 = (bf16[1024,704]{1,0:T(8,128)(2,1)S(1)}, bf16[1024,704]{1,0:T(8,128)(2,1)}, bf16[1024,704]{1,0:T(8,128)(2,1)}, bf16[128,2048]{1,0:T(8,128)(2,1)S...) custom-call(s32[8]{0:T(128)S(1)} %stack.212.chunk.nat, ...), custom_call_target="tpu_custom_call", output_to_operand_aliasing={{0}: (10, {}), {1}: (11, {}), {2}: (12, {})} | custom-call | flops 1000 | bytes 5400000 | tf_op jit(solution)/shard_map/pallas_call | solution.py:136
  246.5 3.1 collective-permute-done.27
  258.2 19.5 %shard_map.223 = (bf16[4,4,2,2,3,16,704]{6,5,4,3,2,1,0:T(8,128)(2,1)}, bf16[4,2,2,3,16,704]{5,4,3,2,1,0:T(8,128)(2,1)S(1)}, bf16[4,2,2,3,16,704]{5,4,3,2,1,0:T(8...) custom-call(s32[8]{0:T(128)S(1)} %stack.244.column, s32[4]{0:T(128)S(1)} %pad_add_fusion.1.xs, ...), custom_call_target="tpu_custom_call" | custom-call | flops 1000 | bytes 5100000 | tf_op jit(solution)/shard_map/pallas_call | solution.py:136
  281.2 5.1 multiply_reduce_fusion
  290.4 4.3 shard_map.222
  295.7 6.3 %collective-permute-done.33.refs_1_.refs_10_ = bf16[128,2048]{1,0:T(8,128)(2,1)S(1)} collective-permute-done((bf16[128,2048]{1,0:T(8,128)(2,1)S(1)}, bf16[128,2048]{1,0:T(8,128)(2,1)S(1)}, u32[]{:S(2)}, u32[]{:S(2)}) %collective-permute-start.33) | collective-permute-done | bytes 524320 | tf_op jit(solution)/shard_map/ppermute | solution.py:45
  307.9 18.1 %shard_map.224 = (bf16[512,256]{1,0:T(8,128)(2,1)S(1)}, f32[2048,64]{1,0:T(8,128)S(1)}, f32[2048,64]{1,0:T(8,128)}) custom-call(s32[8]{0:T(128)S(1)} %bitcast.255, s32[16]{0:T(128)S(1)} %select_reduce_fusion.1.key_slot, s32[1]{0:T(128)} %bitcast.16.core, s32[16]{0:T(128)S(1)} %copy-done.56, bf16[1024,256]{1,0:T(8,128)(2,1)S(1)} %get-tuple-element.123.q_ref.refs_0_, ...), custom_call_target="tpu_custom_call" | custom-call | flops 1000 | bytes 4800000 | tf_op jit(solution)/shard_map/pallas_call | solution.py:136
  331.6 11.0 %shard_map.225 = (bf16[256,256]{1,0:T(8,128)(2,1)S(1)}, bf16[2048,64]{1,0:T(8,128)(2,1)S(1)}, bf16[2048,64]{1,0:T(8,128)(2,1)S(1)}) custom-call(s32[8]{0:T(128)S(1)} %bitcast.256, s32[16]{0:T(128)S(1)} %select_reduce_fusion.1.key_slot, s32[1]{0:T(128)} %bitcast.16.core, s32[16]{0:T(128)S(1)} %copy-done.56, ...), custom_call_target="tpu_custom_call" | custom-call | flops 1000 | bytes 2400000 | tf_op jit(solution)/shard_map/pallas_call | solution.py:136
  342.7 10.2 %collective-permute-done.41 = bf16[128,2048]{1,0:T(8,128)(2,1)S(1)} collective-permute-done((bf16[128,2048]{1,0:T(8,128)(2,1)}, bf16[128,2048]{1,0:T(8,128)(2,1)S(1)}, u32[]{:S(2)}, u32[]{:S(2)}) %collective-permute-start.41) | collective-permute-done | bytes 524320 | tf_op jit(solution)/shard_map/ppermute | solution.py:45
  353.9 4.8 collective-permute-start.49
  365.9 6.7 %collective-permute-done.51 = bf16[2,2,3,16,704]{4,3,2,1,0:T(8,128)(2,1)S(1)} collective-permute-done((bf16[2,2,3,16,704]{4,3,2,1,0:T(8,128)(2,1)S(1)}, bf16[2,2,3,16,704]{4,3,2,1,0:T(8,128)(2,1)S(1)}, u32[]{:S(2)}, u32[]{:S(2)}) %collective-permute-start.51) | collective-permute-done | bytes 270368 | tf_op jit(solution)/shard_map/ppermute | solution.py:45
  381.4 3.7 collective-permute-start.47
  388.4 7.7 %collective-permute-done.47 = bf16[2,2,3,16,704]{4,3,2,1,0:T(8,128)(2,1)S(1)} collective-permute-done((bf16[2,2,3,16,704]{4,3,2,1,0:T(8,128)(2,1)S(1)}, bf16[2,2,3,16,704]{4,3,2,1,0:T(8,128)(2,1)S(1)}, u32[]{:S(2)}, u32[]{:S(2)}) %collective-permute-start.47) | collective-permute-done | bytes 270368 | tf_op jit(solution)/shard_map/ppermute | solution.py:45
  397.4 4.0 shard_map.227
  403.6 5.2 collective-permute-done.57
  409.3 11.0 %shard_map.226 = (bf16[4,4,2,16,576]{4,3,2,1,0:T(8,128)(2,1)}, bf16[4,4,2,16,576]{4,3,2,1,0:T(8,128)(2,1)}, bf16[4,4,2,16,576]{4,3,2,1,0:T(8,128)(2,1)}, bf16[4,...) custom-call(s32[8]{0:T(128)S(1)} %copy-done.62, s32[4]{0:T(128)S(1)} %pad_add_fusion.1.xs, s32[4]{0:T(128)S(1)} %copy-done.54, ...), custom_call_target="tpu_custom_call" | custom-call | flops 1000 | bytes 3000000 | tf_op jit(solution)/shard_map/pallas_call | solution.py:136
  427.6 3.1 collective-permute-done.61
  430.9 3.4 collective-permute-start.62
  434.3 6.5 %collective-permute-done.66 = bf16[2,4,3,16,704]{4,3,2,1,0:T(8,128)(2,1)S(1)} collective-permute-done((bf16[2,4,3,16,704]{4,3,2,1,0:T(8,128)(2,1)}, bf16[2,4,3,16,704]{4,3,2,1,0:T(8,128)(2,1)S(1)}, u32[]{:S(2)}, u32[]{:S(2)}) %collective-permute-start.66) | collective-permute-done | bytes 540704 | tf_op jit(solution)/shard_map/ppermute | solution.py:45
  448.2 14.9 %collective-permute-done.73.refs_1_ = bf16[2,2,4,3,16,704]{5,4,3,2,1,0:T(8,128)(2,1)S(1)} collective-permute-done((bf16[2,2,4,3,16,704]{5,4,3,2,1,0:T(8,128)(2,1)S(1)}, bf16[2,2,4,3,16,704]{5,4,3,2,1,0:T(8,128)(2,1)S(1)}, u32[]{:S(2)}, u32[]{:S(2)}) %collective-permute-start.73) | collective-permute-done | bytes 1081376 | tf_op jit(solution)/shard_map/ppermute | solution.py:45
  463.0 3.5 collective-permute-start.78
  480.5 3.3 collective-permute-done.64
  490.6 4.4 collective-permute-start.67
  496.8 3.7 collective-permute-start.72
  500.6 4.2 collective-permute-done.72
  512.5 6.4 %shard_map.229 = (f32[128,5632]{1,0:T(8,128)}, f32[128,5632]{1,0:T(8,128)}, f32[5632,128]{1,0:T(8,128)}) custom-call(s32[5]{0:T(128)S(1)} %copy-done.58, s32[4]{0:T(128)S(1)} %pad_add_fusion.1.xs, s32[4]{0:T(128)S(1)} %copy-done.54, s32[1]{0:T(128)} %bitcast.16.core, bf16[2,2,4,3,16,704]{5,4,3,2,1,0:T(8,128)(2,1)S(1)} %pad_maximum_fusion.1.refs_0_, ...), custom_call_target="tpu_custom_call" | custom-call | flops 1000 | bytes 1500000 | tf_op jit(solution)/shard_map/pallas_call | solution.py:136
  518.9 8.0 %collective-permute-done.75.refs_2_ = bf16[2,2,4,16,576]{4,3,2,1,0:T(8,128)(2,1)S(1)} collective-permute-done((bf16[2,2,4,16,576]{4,3,2,1,0:T(8,128)(2,1)S(1)}, bf16[2,2,4,16,576]{4,3,2,1,0:T(8,128)(2,1)S(1)}, u32[]{:S(2)}, u32[]{:S(2)}) %collective-permute-start.75) | collective-permute-done | bytes 294944 | tf_op jit(solution)/shard_map/ppermute | solution.py:45
  (443 shorter events, 155.6 us)
Async XLA Ops:
  7.2 87.5 %all-gather.9.cloned.1.call-start = ((), (), s32[]{:S(2)}) async-start(), calls=%async_computation.1 | async-start | bytes 4718592 | tf_op jit(solution)/shard_map/all_gather | solution.py:765
  22.1 20.7 %collective-permute-start.1 = (bf16[4,2,32,704]{3,2,0,1:T(8,128)(2,1)S(1)}, bf16[4,2,32,704]{3,2,0,1:T(8,128)(2,1)S(1)}, u32[]{:S(2)}, u32[]{:S(2)}) collective-permute-start(bf16[4,2,32,704]{3,2,0,1:T(8,128)(2,1)S(1)} %pad_maximum_fusion.3), channel_id=1, source_target_pairs={{0,2},{1,7},{2,4},{3,1},{4,6},{5,3},{6,0},{7,5},{8,10},{9,15},{10,... | collective-permute-start | bytes 1081352 | tf_op jit(solution)/shard_map/ppermute | solution.py:45
  26.0 16.8 %collective-permute-start.2 = (bf16[4,2,32,704]{3,2,0,1:T(8,128)(2,1)S(1)}, bf16[4,2,32,704]{3,2,0,1:T(8,128)(2,1)S(1)}, u32[]{:S(2)}, u32[]{:S(2)}) collective-permute-start(bf16[4,2,32,704]{3,2,0,1:T(8,128)(2,1)S(1)} %pad_maximum_fusion.4), channel_id=1, source_target_pairs={{0,6},{1,3},{2,0},{3,5},{4,2},{5,7},{6,4},{7,1},{8,14},{9,11},{10,... | collective-permute-start | bytes 1081352 | tf_op jit(solution)/shard_map/ppermute | solution.py:45
  26.1 19.1 %collective-permute-start.3 = (bf16[4,2,32,704]{3,2,1,0:T(8,128)(2,1)S(1)}, bf16[4,2,32,704]{3,2,1,0:T(8,128)(2,1)S(1)}, u32[]{:S(2)}, u32[]{:S(2)}) collective-permute-start(bf16[4,2,32,704]{3,2,1,0:T(8,128)(2,1)S(1)} %pad_maximum_fusion.5), channel_id=1, source_target_pairs={{0,4},{1,5},{2,6},{3,7},{4,0},{5,1},{6,2},{7,3},{8,12},{9,13},{10,... | collective-permute-start | bytes 1081352 | tf_op jit(solution)/shard_map/ppermute | solution.py:45
  45.3 87.0 %all-gather.13.cloned.1.call-start = ((), (), s32[]{:S(2)}) async-start(), calls=%async_computation.4 | async-start | bytes 5898240 | tf_op jit(solution)/shard_map/all_gather | solution.py:772
  46.5 154.7 %all-gather.11.cloned.1.call-start = ((), (), s32[]{:S(2)}) async-start(), calls=%async_computation.2 | async-start | bytes 4718592 | tf_op jit(solution)/shard_map/all_gather | solution.py:773
  53.2 16.1 %collective-permute-start.6 = (bf16[8,32,576]{2,1,0:T(8,128)(2,1)S(1)}, bf16[8,32,576]{2,1,0:T(8,128)(2,1)S(1)}, u32[]{:S(2)}, u32[]{:S(2)}) collective-permute-start(bf16[8,32,576]{2,1,0:T(8,128)(2,1)S(1)} %get-tuple-element.265), channel_id=1, source_target_pairs={{0,48},{1,17},{2,50},{3,19},{4,52},{5,21},{6,54},{7,23},{8,56},{9,... | collective-permute-start | bytes 884744 | tf_op jit(solution)/shard_map/ppermute | solution.py:45
  54.5 14.9 %collective-permute-start.5 = (bf16[8,32,576]{2,1,0:T(8,128)(2,1)S(1)}, bf16[8,32,576]{2,1,0:T(8,128)(2,1)S(1)}, u32[]{:S(2)}, u32[]{:S(2)}) collective-permute-start(bf16[8,32,576]{2,1,0:T(8,128)(2,1)S(1)} %get-tuple-element.265), channel_id=1, source_target_pairs={{0,16},{1,49},{2,18},{3,51},{4,20},{5,53},{6,22},{7,55},{8,24},{9,... | collective-permute-start | bytes 884744 | tf_op jit(solution)/shard_map/ppermute | solution.py:45
  69.6 18.6 %collective-permute-start.8 = (bf16[4,8,32,576]{3,2,1,0:T(8,128)(2,1)S(1)}, bf16[4,8,32,576]{3,2,1,0:T(8,128)(2,1)}, u32[]{:S(2)}, u32[]{:S(2)}) collective-permute-start(bf16[4,8,32,576]{3,2,1,0:T(8,128)(2,1)S(1)} %pad_maximum_fusion.own_ref), channel_id=1, source_target_pairs={{0,8},{1,73},{2,10},{3,75},{4,12},{5,77},{6,14},{7,79},{8,64},{9,1... | collective-permute-start | bytes 3538952 | tf_op jit(solution)/shard_map/ppermute | solution.py:45
  88.2 289.7 %reduce-scatter.2.cloned.1.call-start = ((), (), s32[]{:S(2)}) async-start(), calls=%async_computation.3 | async-start | bytes 5898240 | tf_op jit(solution)/shard_map/reduce_scatter | solution.py:831
  132.3 57.3 %collective-permute-start.20 = (bf16[4,3,8,32,704]{4,3,2,1,0:T(8,128)(2,1)}, bf16[4,3,8,32,704]{4,3,2,1,0:T(8,128)(2,1)}, u32[]{:S(2)}, u32[]{:S(2)}) collective-permute-start(bf16[4,3,8,32,704]{4,3,2,1,0:T(8,128)(2,1)} %bitcast.246), channel_id=1, source_target_pairs={{0,8},{1,73},{2,10},{3,75},{4,12},{5,77},{6,14},{7,79},{8,64},{9,1... | collective-permute-start | bytes 12976136 | tf_op jit(solution)/shard_map/ppermute | solution.py:45
  149.6 25.0 %collective-permute-start.17 = (bf16[128,2048]{1,0:T(8,128)(2,1)S(1)}, bf16[128,2048]{1,0:T(8,128)(2,1)S(1)}, u32[]{:S(2)}, u32[]{:S(2)}) collective-permute-start(bf16[128,2048]{1,0:T(8,128)(2,1)S(1)} %add_convert_fusion.6), channel_id=1, source_target_pairs={{0,4},{1,5},{2,6},{3,7},{4,0},{5,1},{6,2},{7,3},{8,12},{9,13},{10,... | collective-permute-start | bytes 1572872 | tf_op jit(solution)/shard_map/ppermute | solution.py:45
  151.1 35.7 %collective-permute-start.16 = (bf16[128,2048]{1,0:T(8,128)(2,1)S(1)}, bf16[128,2048]{1,0:T(8,128)(2,1)S(1)}, u32[]{:S(2)}, u32[]{:S(2)}) collective-permute-start(bf16[128,2048]{1,0:T(8,128)(2,1)S(1)} %add_convert_fusion.7), channel_id=1, source_target_pairs={{0,2},{1,7},{2,4},{3,1},{4,6},{5,3},{6,0},{7,5},{8,10},{9,15},{10,... | collective-permute-start | bytes 1572872 | tf_op jit(solution)/shard_map/ppermute | solution.py:45
  152.8 35.3 %collective-permute-start.15 = (bf16[128,2048]{1,0:T(8,128)(2,1)S(1)}, bf16[128,2048]{1,0:T(8,128)(2,1)S(1)}, u32[]{:S(2)}, u32[]{:S(2)}) collective-permute-start(bf16[128,2048]{1,0:T(8,128)(2,1)S(1)} %add_convert_fusion.8), channel_id=1, source_target_pairs={{0,6},{1,3},{2,0},{3,5},{4,2},{5,7},{6,4},{7,1},{8,14},{9,11},{10,... | collective-permute-start | bytes 1572872 | tf_op jit(solution)/shard_map/ppermute | solution.py:45
  157.4 30.7 %collective-permute-start.14 = (bf16[128,2048]{1,0:T(8,128)(2,1)S(1)}, bf16[128,2048]{1,0:T(8,128)(2,1)S(1)}, u32[]{:S(2)}, u32[]{:S(2)}) collective-permute-start(bf16[128,2048]{1,0:T(8,128)(2,1)S(1)} %get-tuple-element.134), channel_id=1, source_target_pairs={{0,1},{1,0},{2,3},{3,2},{4,5},{5,4},{6,7},{7,6},{8,9},{9,8},{10,11... | collective-permute-start | bytes 1572872 | tf_op jit(solution)/shard_map/ppermute | solution.py:45
  199.7 20.8 %collective-permute-start.23 = (bf16[128,2048]{1,0:T(8,128)(2,1)S(1)}, bf16[128,2048]{1,0:T(8,128)(2,1)}, u32[]{:S(2)}, u32[]{:S(2)}) collective-permute-start(bf16[128,2048]{1,0:T(8,128)(2,1)S(1)} %multiply_convert_fusion.refs_0_), channel_id=1, source_target_pairs={{0,4},{1,5},{2,6},{3,7},{4,0},{5,1},{6,2},{7,3},{8,12},{9,13},{10,... | collective-permute-start | bytes 1572872 | tf_op jit(solution)/shard_map/ppermute | solution.py:45
  200.1 20.5 %collective-permute-start.22 = (bf16[128,2048]{1,0:T(8,128)(2,1)S(1)}, bf16[128,2048]{1,0:T(8,128)(2,1)}, u32[]{:S(2)}, u32[]{:S(2)}) collective-permute-start(bf16[128,2048]{1,0:T(8,128)(2,1)S(1)} %multiply_convert_fusion.refs_0_), channel_id=1, source_target_pairs={{0,6},{1,3},{2,0},{3,5},{4,2},{5,7},{6,4},{7,1},{8,14},{9,11},{10,... | collective-permute-start | bytes 1572872 | tf_op jit(solution)/shard_map/ppermute | solution.py:45
  251.4 27.2 %collective-permute-start.29 = (bf16[128,2048]{1,0:T(8,128)(2,1)}, bf16[128,2048]{1,0:T(8,128)(2,1)}, u32[]{:S(2)}, u32[]{:S(2)}) collective-permute-start(bf16[128,2048]{1,0:T(8,128)(2,1)} %get-tuple-element.241), channel_id=1, source_target_pairs={{0,2},{1,7},{2,4},{3,1},{4,6},{5,3},{6,0},{7,5},{8,10},{9,15},{10,... | collective-permute-start | bytes 1572872 | tf_op jit(solution)/shard_map/ppermute | solution.py:45
  252.3 26.4 %collective-permute-start.30 = (bf16[128,2048]{1,0:T(8,128)(2,1)}, bf16[128,2048]{1,0:T(8,128)(2,1)}, u32[]{:S(2)}, u32[]{:S(2)}) collective-permute-start(bf16[128,2048]{1,0:T(8,128)(2,1)} %get-tuple-element.242), channel_id=1, source_target_pairs={{0,4},{1,5},{2,6},{3,7},{4,0},{5,1},{6,2},{7,3},{8,12},{9,13},{10,... | collective-permute-start | bytes 1572872 | tf_op jit(solution)/shard_map/ppermute | solution.py:45
  278.7 192.2 %all-gather.15.cloned.1.call-start = ((), (), s32[]{:S(2)}) async-start(), calls=%async_computation.5 | async-start | bytes 1114112 | tf_op jit(solution)/shard_map/all_gather | solution.py:878
  278.8 27.5 %collective-permute-start.37 = (bf16[4,2,2,3,16,704]{5,4,3,2,1,0:T(8,128)(2,1)}, bf16[4,2,2,3,16,704]{5,4,3,2,1,0:T(8,128)(2,1)S(1)}, u32[]{:S(2)}, u32[]{:S(2)}) collective-permute-start(bf16[4,2,2,3,16,704]{5,4,3,2,1,0:T(8,128)(2,1)} %get-tuple-element.170), channel_id=1, source_target_pairs={{0,8},{1,73},{2,10},{3,75},{4,12},{5,77},{6,14},{7,79},{8,64},{9,1... | collective-permute-start | bytes 3244040 | tf_op jit(solution)/shard_map/ppermute | solution.py:45
  288.5 13.5 %collective-permute-start.33 = (bf16[128,2048]{1,0:T(8,128)(2,1)S(1)}, bf16[128,2048]{1,0:T(8,128)(2,1)S(1)}, u32[]{:S(2)}, u32[]{:S(2)}) collective-permute-start(bf16[128,2048]{1,0:T(8,128)(2,1)S(1)} %get-tuple-element.231.refs_1_.refs_8_), channel_id=1, source_target_pairs={{0,2},{1,7},{2,4},{3,1},{4,6},{5,3},{6,0},{7,5},{8,10},{9,15},{10,... | collective-permute-start | bytes 1572872 | tf_op jit(solution)/shard_map/ppermute | solution.py:45
  290.4 14.0 %collective-permute-start.35 = (bf16[128,2048]{1,0:T(8,128)(2,1)S(1)}, bf16[128,2048]{1,0:T(8,128)(2,1)S(1)}, u32[]{:S(2)}, u32[]{:S(2)}) collective-permute-start(bf16[128,2048]{1,0:T(8,128)(2,1)S(1)} %get-tuple-element.231.refs_1_.refs_8_), channel_id=1, source_target_pairs={{0,6},{1,3},{2,0},{3,5},{4,2},{5,7},{6,4},{7,1},{8,14},{9,11},{10,... | collective-permute-start | bytes 1572872 | tf_op jit(solution)/shard_map/ppermute | solution.py:45
  304.3 21.7 %collective-permute-start.31 = (bf16[128,2048]{1,0:T(8,128)(2,1)S(1)}, bf16[128,2048]{1,0:T(8,128)(2,1)S(1)}, u32[]{:S(2)}, u32[]{:S(2)}) collective-permute-start(bf16[128,2048]{1,0:T(8,128)(2,1)S(1)} %get-tuple-element.231.refs_1_.refs_8_), channel_id=1, source_target_pairs={{0,4},{1,5},{2,6},{3,7},{4,0},{5,1},{6,2},{7,3},{8,12},{9,13},{10,... | collective-permute-start | bytes 1572872 | tf_op jit(solution)/shard_map/ppermute | solution.py:45
  304.8 26.8 %collective-permute-start.39 = (bf16[4,2,2,3,16,704]{5,4,3,2,1,0:T(8,128)(2,1)}, bf16[4,2,2,3,16,704]{5,4,3,2,1,0:T(8,128)(2,1)S(1)}, u32[]{:S(2)}, u32[]{:S(2)}) collective-permute-start(bf16[4,2,2,3,16,704]{5,4,3,2,1,0:T(8,128)(2,1)} %get-tuple-element.184), channel_id=1, source_target_pairs={{0,72},{1,9},{2,74},{3,11},{4,76},{5,13},{6,78},{7,15},{8,0},{9,65... | collective-permute-start | bytes 3244040 | tf_op jit(solution)/shard_map/ppermute | solution.py:45
  306.6 46.7 %collective-permute-start.48 = (bf16[4,2,2,3,16,704]{5,4,3,2,1,0:T(8,128)(2,1)S(1)}, bf16[4,2,2,3,16,704]{5,4,3,2,1,0:T(8,128)(2,1)S(1)}, u32[]{:S(2)}, u32[]{:S(2)}) collective-permute-start(bf16[4,2,2,3,16,704]{5,4,3,2,1,0:T(8,128)(2,1)S(1)} %add_convert_fusion.1), channel_id=1, source_target_pairs={{0,8},{1,73},{2,10},{3,75},{4,12},{5,77},{6,14},{7,79},{8,64},{9,1... | collective-permute-start | bytes 3244040 | tf_op jit(solution)/shard_map/ppermute | solution.py:45
  326.1 16.5 %collective-permute-start.40 = (bf16[128,2048]{1,0:T(8,128)(2,1)S(1)}, bf16[128,2048]{1,0:T(8,128)(2,1)S(1)}, u32[]{:S(2)}, u32[]{:S(2)}) collective-permute-start(bf16[128,2048]{1,0:T(8,128)(2,1)S(1)} %copy-done.80), channel_id=1, source_target_pairs={{0,4},{1,5},{2,6},{3,7},{4,0},{5,1},{6,2},{7,3},{8,12},{9,13},{10,... | collective-permute-start | bytes 1572872 | tf_op jit(solution)/shard_map/ppermute | solution.py:45
  328.9 24.0 %collective-permute-start.41 = (bf16[128,2048]{1,0:T(8,128)(2,1)}, bf16[128,2048]{1,0:T(8,128)(2,1)S(1)}, u32[]{:S(2)}, u32[]{:S(2)}) collective-permute-start(bf16[128,2048]{1,0:T(8,128)(2,1)} %get-tuple-element.192), channel_id=1, source_target_pairs={{0,6},{1,3},{2,0},{3,5},{4,2},{5,7},{6,4},{7,1},{8,14},{9,11},{10,... | collective-permute-start | bytes 1572872 | tf_op jit(solution)/shard_map/ppermute | solution.py:45
  328.9 24.0 %collective-permute-start.42 = (bf16[128,2048]{1,0:T(8,128)(2,1)S(1)}, bf16[128,2048]{1,0:T(8,128)(2,1)S(1)}, u32[]{:S(2)}, u32[]{:S(2)}) collective-permute-start(bf16[128,2048]{1,0:T(8,128)(2,1)S(1)} %copy-done.79), channel_id=1, source_target_pairs={{0,2},{1,7},{2,4},{3,1},{4,6},{5,3},{6,0},{7,5},{8,10},{9,15},{10,... | collective-permute-start | bytes 1572872 | tf_op jit(solution)/shard_map/ppermute | solution.py:45
  358.7 13.9 %collective-permute-start.51 = (bf16[2,2,3,16,704]{4,3,2,1,0:T(8,128)(2,1)S(1)}, bf16[2,2,3,16,704]{4,3,2,1,0:T(8,128)(2,1)S(1)}, u32[]{:S(2)}, u32[]{:S(2)}) collective-permute-start(bf16[2,2,3,16,704]{4,3,2,1,0:T(8,128)(2,1)S(1)} %get-tuple-element.246), channel_id=1, source_target_pairs={{0,16},{1,49},{2,18},{3,51},{4,20},{5,53},{6,22},{7,55},{8,24},{9,... | collective-permute-start | bytes 811016 | tf_op jit(solution)/shard_map/ppermute | solution.py:45
  361.1 24.0 %collective-permute-start.44 = (bf16[1024,64]{1,0:T(8,128)(2,1)}, bf16[1024,64]{1,0:T(8,128)(2,1)}, u32[]{:S(2)}, u32[]{:S(2)}) collective-permute-start(bf16[1024,64]{1,0:T(8,128)(2,1)} %slice.429), channel_id=1, source_target_pairs={{0,8},{1,9},{2,10},{3,11},{4,12},{5,13},{6,14},{7,15},{8,0},{9,1},... | collective-permute-start | bytes 393224 | tf_op jit(solution)/shard_map/ppermute | solution.py:45
  375.9 26.7 %collective-permute-start.59 = (bf16[2,3,16,704]{3,2,1,0:T(8,128)(2,1)}, bf16[2,3,16,704]{3,2,1,0:T(8,128)(2,1)}, u32[]{:S(2)}, u32[]{:S(2)}) collective-permute-start(bf16[2,3,16,704]{3,2,1,0:T(8,128)(2,1)} %get-tuple-element.269), channel_id=1, source_target_pairs={{0,4},{1,5},{2,6},{3,7},{4,0},{5,1},{6,2},{7,3},{8,12},{9,13},{10,... | collective-permute-start | bytes 405512 | tf_op jit(solution)/shard_map/ppermute | solution.py:45
  381.4 14.7 %collective-permute-start.47 = (bf16[2,2,3,16,704]{4,3,2,1,0:T(8,128)(2,1)S(1)}, bf16[2,2,3,16,704]{4,3,2,1,0:T(8,128)(2,1)S(1)}, u32[]{:S(2)}, u32[]{:S(2)}) collective-permute-start(bf16[2,2,3,16,704]{4,3,2,1,0:T(8,128)(2,1)S(1)} %get-tuple-element.249), channel_id=1, source_target_pairs={{0,8},{1,73},{2,10},{3,75},{4,12},{5,77},{6,14},{7,79},{8,64},{9,1... | collective-permute-start | bytes 811016 | tf_op jit(solution)/shard_map/ppermute | solution.py:45
  402.2 38.8 %collective-permute-start.52 = (bf16[4,128,2048]{2,1,0:T(8,128)(2,1)}, bf16[4,128,2048]{2,1,0:T(8,128)(2,1)}, u32[]{:S(2)}, u32[]{:S(2)}) collective-permute-start(bf16[4,128,2048]{2,1,0:T(8,128)(2,1)} %get-tuple-element.206), channel_id=1, source_target_pairs={{0,1},{1,0},{2,3},{3,2},{4,5},{5,4},{6,7},{7,6},{8,9},{9,8},{10,11... | collective-permute-start | bytes 6291464 | tf_op jit(solution)/shard_map/ppermute | solution.py:45
  408.9 14.1 %collective-permute-start.60 = (bf16[4,3,16,704]{3,2,1,0:T(8,128)(2,1)S(1)}, bf16[4,3,16,704]{3,2,1,0:T(8,128)(2,1)S(1)}, u32[]{:S(2)}, u32[]{:S(2)}) collective-permute-start(bf16[4,3,16,704]{3,2,1,0:T(8,128)(2,1)S(1)} %pad_maximum_fusion.8), channel_id=1, source_target_pairs={{0,1},{1,0},{2,3},{3,2},{4,5},{5,4},{6,7},{7,6},{8,9},{9,8},{10,11... | collective-permute-start | bytes 811016 | tf_op jit(solution)/shard_map/ppermute | solution.py:45
  423.8 17.0 %collective-permute-start.66 = (bf16[2,4,3,16,704]{4,3,2,1,0:T(8,128)(2,1)}, bf16[2,4,3,16,704]{4,3,2,1,0:T(8,128)(2,1)S(1)}, u32[]{:S(2)}, u32[]{:S(2)}) collective-permute-start(bf16[2,4,3,16,704]{4,3,2,1,0:T(8,128)(2,1)} %get-tuple-element.261), channel_id=1, source_target_pairs={{0,64},{1,65},{2,66},{3,67},{4,68},{5,69},{6,70},{7,71},{8,72},{9,... | collective-permute-start | bytes 1622024 | tf_op jit(solution)/shard_map/ppermute | solution.py:45
  426.0 103.1 %all-gather.17.cloned.1.call-start = ((), (), s32[]{:S(2)}) async-start(), calls=%async_computation.6 | async-start | bytes 1179648 | tf_op jit(solution)/shard_map/all_gather | solution.py:889
  426.1 18.6 %collective-permute-start.56 = (bf16[4,4,2,16,576]{4,3,2,1,0:T(8,128)(2,1)}, bf16[4,4,2,16,576]{4,3,2,1,0:T(8,128)(2,1)S(1)}, u32[]{:S(2)}, u32[]{:S(2)}) collective-permute-start(bf16[4,4,2,16,576]{4,3,2,1,0:T(8,128)(2,1)} %get-tuple-element.211), channel_id=1, source_target_pairs={{0,48},{1,17},{2,50},{3,19},{4,52},{5,21},{6,54},{7,23},{8,56},{9,... | collective-permute-start | bytes 1769480 | tf_op jit(solution)/shard_map/ppermute | solution.py:45
  430.9 16.2 %collective-permute-start.62 = (bf16[4,4,2,16,576]{4,3,2,1,0:T(8,128)(2,1)S(1)}, bf16[4,4,2,16,576]{4,3,2,1,0:T(8,128)(2,1)S(1)}, u32[]{:S(2)}, u32[]{:S(2)}) collective-permute-start(bf16[4,4,2,16,576]{4,3,2,1,0:T(8,128)(2,1)S(1)} %add_convert_fusion.3), channel_id=1, source_target_pairs={{0,16},{1,49},{2,18},{3,51},{4,20},{5,53},{6,22},{7,55},{8,24},{9,... | collective-permute-start | bytes 1769480 | tf_op jit(solution)/shard_map/ppermute | solution.py:45
  440.9 22.1 %collective-permute-start.73 = (bf16[2,2,4,3,16,704]{5,4,3,2,1,0:T(8,128)(2,1)S(1)}, bf16[2,2,4,3,16,704]{5,4,3,2,1,0:T(8,128)(2,1)S(1)}, u32[]{:S(2)}, u32[]{:S(2)}) collective-permute-start(bf16[2,2,4,3,16,704]{5,4,3,2,1,0:T(8,128)(2,1)S(1)} %pad_maximum_fusion.1.refs_0_), channel_id=1, source_target_pairs={{0,16},{1,49},{2,18},{3,51},{4,20},{5,53},{6,22},{7,55},{8,24},{9,... | collective-permute-start | bytes 3244040 | tf_op jit(solution)/shard_map/ppermute | solution.py:45
  443.2 23.3 %collective-permute-start.53 = (bf16[128,2048]{1,0:T(8,128)(2,1)S(1)}, bf16[128,2048]{1,0:T(8,128)(2,1)}, u32[]{:S(2)}, u32[]{:S(2)}) collective-permute-start(bf16[128,2048]{1,0:T(8,128)(2,1)S(1)} %get-tuple-element.236), channel_id=1, source_target_pairs={{0,4},{1,5},{2,6},{3,7},{4,0},{5,1},{6,2},{7,3},{8,12},{9,13},{10,... | collective-permute-start | bytes 1572872 | tf_op jit(solution)/shard_map/ppermute | solution.py:45
  444.4 25.1 %collective-permute-start.55 = (bf16[128,2048]{1,0:T(8,128)(2,1)S(1)}, bf16[128,2048]{1,0:T(8,128)(2,1)}, u32[]{:S(2)}, u32[]{:S(2)}) collective-permute-start(bf16[128,2048]{1,0:T(8,128)(2,1)S(1)} %get-tuple-element.237), channel_id=1, source_target_pairs={{0,2},{1,7},{2,4},{3,1},{4,6},{5,3},{6,0},{7,5},{8,10},{9,15},{10,... | collective-permute-start | bytes 1572872 | tf_op jit(solution)/shard_map/ppermute | solution.py:45
  444.7 25.4 %collective-permute-start.54 = (bf16[128,2048]{1,0:T(8,128)(2,1)S(1)}, bf16[128,2048]{1,0:T(8,128)(2,1)}, u32[]{:S(2)}, u32[]{:S(2)}) collective-permute-start(bf16[128,2048]{1,0:T(8,128)(2,1)S(1)} %get-tuple-element.238), channel_id=1, source_target_pairs={{0,6},{1,3},{2,0},{3,5},{4,2},{5,7},{6,4},{7,1},{8,14},{9,11},{10,... | collective-permute-start | bytes 1572872 | tf_op jit(solution)/shard_map/ppermute | solution.py:45
  447.1 65.4 %collective-permute-start.77 = (bf16[2,2,4,3,16,704]{5,4,3,2,1,0:T(8,128)(2,1)S(1)}, bf16[2,2,4,3,16,704]{5,4,3,2,1,0:T(8,128)(2,1)}, u32[]{:S(2)}, u32[]{:S(2)}) collective-permute-start(bf16[2,2,4,3,16,704]{5,4,3,2,1,0:T(8,128)(2,1)S(1)} %pad_maximum_fusion.1.refs_0_), channel_id=1, source_target_pairs={{0,48},{1,17},{2,50},{3,19},{4,52},{5,21},{6,54},{7,23},{8,56},{9,... | collective-permute-start | bytes 3244040 | tf_op jit(solution)/shard_map/ppermute | solution.py:45
  463.0 49.5 %collective-permute-start.78 = (bf16[2,2,4,3,16,704]{5,4,3,2,1,0:T(8,128)(2,1)S(1)}, bf16[2,2,4,3,16,704]{5,4,3,2,1,0:T(8,128)(2,1)}, u32[]{:S(2)}, u32[]{:S(2)}) collective-permute-start(bf16[2,2,4,3,16,704]{5,4,3,2,1,0:T(8,128)(2,1)S(1)} %collective-permute-done.73.refs_1_), channel_id=1, source_target_pairs={{0,16},{1,49},{2,18},{3,51},{4,20},{5,53},{6,22},{7,55},{8,24},{9,... | collective-permute-start | bytes 3244040 | tf_op jit(solution)/shard_map/ppermute | solution.py:45
  504.8 14.1 %collective-permute-start.76 = (bf16[2,2,4,16,576]{4,3,2,1,0:T(8,128)(2,1)S(1)}, bf16[2,2,4,16,576]{4,3,2,1,0:T(8,128)(2,1)S(1)}, u32[]{:S(2)}, u32[]{:S(2)}) collective-permute-start(bf16[2,2,4,16,576]{4,3,2,1,0:T(8,128)(2,1)S(1)} %pad_maximum_fusion.7.refs_0_), channel_id=1, source_target_pairs={{0,32},{1,33},{2,34},{3,35},{4,36},{5,37},{6,38},{7,39},{8,40},{9,... | collective-permute-start | bytes 884744 | tf_op jit(solution)/shard_map/ppermute | solution.py:45
  506.8 20.2 %collective-permute-start.75 = (bf16[2,2,4,16,576]{4,3,2,1,0:T(8,128)(2,1)S(1)}, bf16[2,2,4,16,576]{4,3,2,1,0:T(8,128)(2,1)S(1)}, u32[]{:S(2)}, u32[]{:S(2)}) collective-permute-start(bf16[2,2,4,16,576]{4,3,2,1,0:T(8,128)(2,1)S(1)} %pad_maximum_fusion.7.refs_0_), channel_id=1, source_target_pairs={{0,48},{1,17},{2,50},{3,19},{4,52},{5,21},{6,54},{7,23},{8,56},{9,... | collective-permute-start | bytes 884744 | tf_op jit(solution)/shard_map/ppermute | solution.py:45
  508.4 18.5 %collective-permute-start.74 = (bf16[2,2,4,16,576]{4,3,2,1,0:T(8,128)(2,1)S(1)}, bf16[2,2,4,16,576]{4,3,2,1,0:T(8,128)(2,1)S(1)}, u32[]{:S(2)}, u32[]{:S(2)}) collective-permute-start(bf16[2,2,4,16,576]{4,3,2,1,0:T(8,128)(2,1)S(1)} %pad_maximum_fusion.7.refs_0_), channel_id=1, source_target_pairs={{0,16},{1,49},{2,18},{3,51},{4,20},{5,53},{6,22},{7,55},{8,24},{9,... | collective-permute-start | bytes 884744 | tf_op jit(solution)/shard_map/ppermute | solution.py:45
  (137 other events, 1708.0 us)
Sparse Core Ops, SparseCore 0:
  45.4 32.6 all-gather.8
  80.3 51.9 all-gather.12
  134.1 55.0 all-gather.10
  278.8 52.2 reduce-scatter.1
  426.1 38.7 all-gather.14
  473.0 52.2 all-gather.16

commit v6 on v5

--- a/solution.py
+++ b/solution.py
@@ -274,23 +274,32 @@
     )
 
 
-def project_back_kernel(dq0_ref, dq1_ref, dq2_ref, dkv_ref, w_ref, *out_refs):
+def project_back_kernel(chunk, dq0_ref, dq1_ref, dq2_ref, dkv_ref, w_ref, *refs):
+    rows_refs, out_ref, gain_ref = refs[:8], refs[8], refs[9]
     queries = jnp.concatenate([dq0_ref[...], dq1_ref[...], dq2_ref[...]], axis=0)
     rows = jnp.concatenate([queries, dkv_ref[...]], axis=1)
-    grad = dot_last(rows, w_ref[...]).astype(BF)
-    for r in range(4):
-        out_refs[r][...] = grad[2 * r * TOK : (2 * r + 1) * TOK]
-        out_refs[4][r] = grad[(2 * r + 1) * TOK : (2 * r + 2) * TOK]
-
-
-def project_back(dq, dkv, w):
-    return call(
-        project_back_kernel, (), (4,),
-        [pl.BlockSpec(each.shape, lambda k: (0, 0)) for each in tuple(dq) + (dkv,)]
-        + [pl.BlockSpec((PART, QKV), lambda k: (k, 0))],
-        [pl.BlockSpec((TOK, PART), lambda k: (0, k))] * 4 + [pl.BlockSpec((4, TOK, PART), lambda k: (0, 0, k))],
-        [sds((TOK, D))] * 4 + [sds((4, TOK, D))], [], 4, tuple(dq) + (dkv, w),
-    )
+    grad = dot_last(rows, w_ref[...])
+    gain = jnp.zeros((1, PART), F32)
+    for r in range(8):
+        term = grad[TOK * r : TOK * (r + 1)]
+        out_ref[chunk[r]] = term.astype(BF)
+        gain += jnp.sum(term * rows_refs[r][...].astype(F32), axis=0, keepdims=True)
+    gain_ref[...] = jnp.broadcast_to(gain, (8, PART))
+
+
+def project_back(chunk, dq, dkv, w, rows):
+    def rows_spec(r):
+        return pl.BlockSpec((TOK, PART), lambda k, chunk: (chunk[r], k))
+
+    grad, gain = call(
+        project_back_kernel, (chunk,), (4,),
+        [pl.BlockSpec(each.shape, lambda k, chunk: (0, 0)) for each in tuple(dq) + (dkv,)]
+        + [pl.BlockSpec((PART, QKV), lambda k, chunk: (k, 0))]
+        + [rows_spec(r) for r in range(8)],
+        [pl.BlockSpec((8, TOK, PART), lambda k, chunk: (0, 0, k)), pl.BlockSpec((8, PART), lambda k, chunk: (0, k))],
+        [sds((8, TOK, D)), sds((8, D), F32)], [], 5, tuple(dq) + (dkv, w) + (rows,) * 8,
+    )
+    return grad, gain[0]
 
 
 def head_rows(rows):
@@ -449,12 +458,21 @@
 ROWS = 4 * TOK
 
 
-def mlp_kernel(chunk, *refs):
+def mlp_kernel(part, chunk, *refs):
     rows_refs, grads_refs, w_ref = refs[:4], refs[4:8], refs[8]
-    z_ref, da_ref, dc_ref = refs[-12:-9]
-    mine_refs, peer_ref = refs[-9:-5], refs[-5]
-    weights, gate, up, back = refs[-4:]
+    z_ref, da_ref, dc_ref = refs[-13:-10]
+    mine_refs, peer_ref, out_ref = refs[-10:-8], refs[-8], refs[-7]
+    weights, gate, up, back, terms_out, sems = refs[-6:]
     k = pl.program_id(0)
+
+    def copies(j):
+        columns = pl.ds(pl.multiple_of(j * DEEP, DEEP), DEEP)
+        return [
+            pltpu.make_async_copy(
+                terms_out.at[j, r], out_ref.at[chunk[4 * part + r], :, columns], sems.at[j, r]
+            )
+            for r in range(4)
+        ]
 
     @pl.when(k < SPLIT)
     def _():
@@ -487,11 +505,19 @@
         j = k - SPLIT
         grad = dot_last(da_ref[...], weights[j, 0]) + dot_last(dc_ref[...], weights[j, 1])
         out = dot_last(z_ref[...], weights[j, 2])
+        for r in range(4):
+            terms_out[j, r] = out[r * TOK : (r + 1) * TOK].astype(BF)
+        for copy in copies(j):
+            copy.start()
         for r in range(2):
             mine_refs[r][...] = grad[2 * r * TOK : (2 * r + 1) * TOK].astype(BF)
-            mine_refs[2 + r][...] = out[2 * r * TOK : (2 * r + 1) * TOK].astype(BF)
             peer_ref[r] = grad[(2 * r + 1) * TOK : (2 * r + 2) * TOK].astype(BF)
-            peer_ref[2 + r] = out[(2 * r + 1) * TOK : (2 * r + 2) * TOK].astype(BF)
+
+    @pl.when(k == 2 * SPLIT - 1)
+    def _():
+        for j in range(SPLIT):
+            for copy in copies(j):
+                copy.wait()
 
 
 def mlp_half(part, chunk, rows, grads, weights, kept):
@@ -508,19 +534,23 @@
     aliases = {}
     if kept is not None:
         args = args + tuple(kept)
-        specs = specs + [pl.BlockSpec(memory_space=pl.ANY)] * 3
-        aliases = {10: 0, 11: 1, 12: 2}
+        specs = specs + [pl.BlockSpec(memory_space=pl.ANY)] * 4
+        aliases = {10: 0, 11: 1, 12: 2, 13: 6}
     wide = pltpu.VMEM((ROWS, WIDE), F32)
     out = call(
-        mlp_kernel, (chunk,), (2 * SPLIT,), specs,
+        functools.partial(mlp_kernel, part), (chunk,), (2 * SPLIT,), specs,
         [kept_spec] * 3
-        + [pl.BlockSpec((TOK, DEEP), lambda k, chunk: (0, jnp.maximum(k - SPLIT, 0)))] * 4
-        + [pl.BlockSpec((4, TOK, DEEP), lambda k, chunk: (0, 0, jnp.maximum(k - SPLIT, 0)))],
-        [sds((8 * TOK, WIDE))] * 3 + [sds((TOK, D))] * 4 + [sds((4, TOK, D))],
-        [pltpu.VMEM((SPLIT, 3, DEEP, WIDE), BF), wide, wide, wide],
+        + [pl.BlockSpec((TOK, DEEP), lambda k, chunk: (0, jnp.maximum(k - SPLIT, 0)))] * 2
+        + [pl.BlockSpec((2, TOK, DEEP), lambda k, chunk: (0, 0, jnp.maximum(k - SPLIT, 0)))]
+        + [pl.BlockSpec(memory_space=pl.ANY)],
+        [sds((8 * TOK, WIDE))] * 3 + [sds((TOK, D))] * 2 + [sds((2, TOK, D)), sds((8, TOK, D))],
+        [
+            pltpu.VMEM((SPLIT, 3, DEEP, WIDE), BF), wide, wide, wide,
+            pltpu.VMEM((SPLIT, 4, TOK, DEEP), BF), pltpu.SemaphoreType.DMA((SPLIT, 4)),
+        ],
         18, args, aliases,
     )
-    return out[:3], out[3:7], out[7]
+    return out[:3] + out[6:], out[3:5], out[5]
 
 
 def grads_specs(tail):
@@ -586,16 +616,13 @@
 
 
 def attn_grads_kernel(column, xs, yhs, core, halves, chunk, *refs):
-    h_refs, g_refs, o_refs, dq_refs, (dkv_ref, w_ref) = refs[:8], refs[8:16], refs[16:20], refs[20:23], refs[23:25]
-    outs, gain_ref, (first, second) = refs[25:29], refs[29], refs[30:]
+    h_refs, g_refs, o_refs, dq_refs, dkv_ref = refs[:8], refs[8:16], refs[16:20], refs[20:23], refs[23]
+    outs, (first, second) = refs[24:28], refs[28:]
     rows = jnp.concatenate([ref[...] for ref in h_refs], axis=0).T
     queries = jnp.concatenate([ref[...] for ref in dq_refs], axis=0)
     first[...] = dot(rows, jnp.concatenate([queries, dkv_ref[...]], axis=1))
     grads = jnp.concatenate([ref[...] for ref in g_refs], axis=0)
     second[...] = dot(jnp.concatenate([ref[...] for ref in o_refs], axis=0).T, grads)
-    gain = jnp.sum(first[...] * w_ref[...].astype(F32), axis=1, keepdims=True)
-    gain_ref[0] = jnp.broadcast_to(gain, (256, 128)).T[:8]
-
     half = pl.program_id(0)
     for r in range(4):
         for pos in range(2):
@@ -606,28 +633,23 @@
                 outs[r][pos, 0, rc, :, QUERY:] = first[at_rows(start, 16), :].astype(BF)
 
 
-def attn_grads(column, xs, yhs, core, halves, chunk, h, g, o, dq, dkv, w):
+def attn_grads(column, xs, yhs, core, halves, chunk, h, g, o, dq, dkv):
     def rows_spec(r):
         return pl.BlockSpec((TOK, 256), lambda i, p, column, xs, yhs, core, halves, chunk: (chunk[r], column[4 * i + p]))
 
     whole = lambda i, p, *_: (0, 0)
     out = pl.BlockSpec((2, 1, 2, 16, PACK), lambda i, p, *_: (i, p, 0, 0, 0))
-    *outs, gain = call(
+    return call(
         attn_grads_kernel, (column, xs, yhs, core, halves, chunk), (2, 4),
         [rows_spec(r) for r in range(8)]
         + [pl.BlockSpec((TOK, 2 * QUERY), lambda i, p, *_: (0, p))] * 8
         + [pl.BlockSpec((2 * TOK, 128), lambda i, p, column, xs, yhs, core, halves, chunk: (0, halves[i]))] * 4
-        + [
-            *[pl.BlockSpec(each.shape, whole) for each in dq],
-            pl.BlockSpec((8 * TOK, HEAD), whole),
-            pl.BlockSpec((256, QKV), lambda i, p, column, *_: (column[4 * i + p], 0)),
-        ],
-        [out] * 4 + [pl.BlockSpec((1, 8, 256), lambda i, p, column, *_: (column[4 * i + p], 0, 0))],
-        [sds((4, 4, 2, 16, PACK))] * 4 + [sds((8, 8, 256), F32)],
+        + [pl.BlockSpec(each.shape, whole) for each in dq]
+        + [pl.BlockSpec((8 * TOK, HEAD), whole)],
+        [out] * 4, [sds((4, 4, 2, 16, PACK))] * 4,
         [pltpu.VMEM((256, QKV), F32), pltpu.VMEM((128, 2 * QUERY), F32)],
-        10, (h,) * 8 + tuple(g) + tuple(o) + tuple(dq) + (dkv, w),
-    )
-    return outs, gain[:, 0, :].reshape(D)
+        10, (h,) * 8 + tuple(g) + tuple(o) + tuple(dq) + (dkv,),
+    )
 
 
 def finish_mlp_kernel(spots, xs, yhs, core, *refs):
@@ -809,26 +831,26 @@
     mlp_parts = [own, swap(own), first, swap(after(first, w_mlp)), second, swap(after(second, w_mlp)), third, None]
 
 
-    kept, sums, got, outs, at = None, [None] * 4, [None] * 4, [None] * 4, chunk
+    kept, sums, got, at = None, [None] * 4, [None] * 4, chunk
     for part in range(2):
         kept, mine, peer = mlp_half(part, at, mlp_parts[4 * part : 4 * part + 4], grad_rows, w_mlp, kept)
         swapped = swap(after(peer, second, third))
         for each in range(2):
             g = 2 * part + each
             sums[g] = add(mine[each], swapped[each]).astype(BF)
-            outs[g] = add(mine[2 + each], swapped[2 + each]).astype(BF)
             if g:
                 got[g] = give(g, sums[g])
         if part == 0:
             mlp_parts[7] = swap(after(third, kept[0]))
         at = after(chunk, swapped)
-    hidden, gate_grad_rows, up_grad_rows = kept
+    hidden, gate_grad_rows, up_grad_rows, branch = kept
     mlp_outs = mlp_grads(
         column, xs, yhs, core, after(at, got[1], sums[2], sums[3]), mlp_parts, grad_rows, gate_grad_rows, up_grad_rows, hidden
     )
     normed_grad = add(sums[0], *got[1:])
     mlp_outs = after(mlp_outs, got[2], got[3])
     mlp_low = lax.psum_scatter(mlp_outs[0], "batch", scatter_dimension=0, axis_index_groups=X_GROUPS)
+    branch = lax.psum_scatter(after(branch, mlp_outs), "blk", scatter_dimension=0, axis_index_groups=ZC_GROUPS)
     high_far = step(mlp_outs[2], "y", 1)
 
     residual_grad = cotangent[0].astype(F32) + norm_back(residual, scale_mlp, gain_two, normed_grad)
@@ -850,16 +872,14 @@
 
     branch_parts = [own, swap(own)]
     rows_0, *sums = back(0, branch_parts, (), False)
-    branch_parts += [first, swap(after(first, rows_0)), second, swap(after(second, rows_0))]
+    branch_parts += [first, swap(after(first, second, rows_0)), second, swap(after(second, rows_0))]
     high_after = step(after(mlp_outs[3], branch_parts[3]), "y", -1)
     high_before = step(add(after(mlp_outs[4], branch_parts[3]), high_far).astype(BF), "y", 1)
     rows_1, *sums = back(2, after(branch_parts[2:], high_far), sums, False)
     branch_parts += [third, swap(after(third, rows_1))]
-    outs = after(outs, third)
-    got_outs = [give(g, outs[g]) for g in (3, 1, 2)]
     rows_2, kv_keep, kv_give = back(6, after(branch_parts[6:], high_after), sums, True)
     query_grad_rows = [rows_0, rows_1, rows_2]
-    kv_terms = add(after(kv_keep, got_outs), swap(kv_give))
+    kv_terms = add(kv_keep, swap(kv_give))
     half_rows = 8 * TOK
     kv_half = to_half(kv_terms[half_rows:].astype(BF))
     kv_grad_rows = add(kv_terms[:half_rows], kv_half).astype(BF)
@@ -867,40 +887,41 @@
     high = ring_scatter(high[0], high[1], high[2], high[3], "x").astype(BF)
     mlp_low = after(mlp_low, rows_2)
     low = ring_scatter(mlp_low[0], mlp_low[2], mlp_low[3], mlp_low[1], "y").astype(BF)
-    kv_grad_rows = after(kv_grad_rows, low, high)
     mlp_sums, mlp_swapped = resplit_back([low[0], low[1], high[0], high[1]])
-
-    attn_partial = project_back(query_grad_rows, kv_grad_rows, w_qkv)
-    attn_outs, attn_gain_part = attn_grads(
-        column, xs, yhs, core, halves, chunk, normed_attn, branch_parts, attended, query_grad_rows, kv_grad_rows, w_qkv
-    )
+    kv_grad_rows = after(kv_grad_rows, mlp_low)
+
+    attn_partial, attn_gain_part = project_back(chunk, query_grad_rows, kv_grad_rows, w_qkv, normed_attn)
     gain_grads = jnp.stack([attn_gain_part / gain_one, mlp_gain_part])
     gain_grads = lax.all_gather(jnp.pad(gain_grads, ((0, 6), (0, 0))), "blk")
-
-    layer_out = (residual + add(after(outs[0], attn_outs[0]), *got_outs)).astype(BF)[None]
+    attn_outs = attn_grads(
+        column, xs, yhs, core, halves, chunk, normed_attn, branch_parts, attended, query_grad_rows, kv_grad_rows
+    )
+    attn_partial, attn_outs = after((attn_partial, attn_outs), low, high)
+    normed_attn_grad = lax.psum_scatter(attn_partial, "blk", scatter_dimension=0, axis_index_groups=ZC_GROUPS)
+
+    layer_out = (residual + after(branch, attn_outs[0]).astype(F32)).astype(BF)[None]
     mlp_across = across(mlp_sums, "y")
-    mlp_sums = ring_gather(jnp.stack([mlp_sums, mlp_across]), "x", True)
-    swapped = swap(attn_partial[4])
-    sums = [add(attn_partial[g], swapped[g]).astype(BF) for g in range(4)]
-    got = [give(g, sums[g]) for g in (3, 1, 2)]
-    normed_attn_grad = add(sums[0], *got)
-    attn_sums = after(ring_scatter(*attn_outs, "x", mlp_swapped).astype(BF), *got)
-    gain_grads = jnp.sum(after(gain_grads, attn_sums), axis=0)
-    gain_grads = lax.all_gather(jnp.pad(gain_grads, ((0, 8), (0, 0))), "batch")
+    mlp_sums = jnp.stack([mlp_sums, mlp_across])
+    mlp_first, mlp_second = step(mlp_sums, "x", 1), step(mlp_sums, "x", -1)
+    attn_sums = ring_scatter(*attn_outs, "x", mlp_swapped).astype(BF)
     attn_sums = ring_scatter(attn_sums[0], attn_sums[2], attn_sums[3], attn_sums[1], "y").astype(BF)
+    gain_grads = jnp.sum(after(gain_grads, attn_sums), axis=0)[:2]
+    mlp_sums = (mlp_sums, mlp_first, mlp_second, step(after(mlp_first, attn_sums), "x", 1))
+    gain_grads = gain_grads + across(gain_grads, "y")
     attn_sums = after(attn_sums, mlp_across)
     out_sums = send(
         attn_sums[..., :QUERY], lambda yh, x, yl, z, c: (yh, x, z // 2, 2 * (z % 2) + c, yl)
     )
     qkv_sums, _ = resplit_back(attn_sums[..., QUERY:])
     attn_sums = jnp.concatenate([out_sums.reshape(2, 4, 16, QUERY), qkv_sums], axis=-1)
-    attn_across = after(across(attn_sums, "y"), mlp_sums[1])
+    attn_across = across(attn_sums, "y")
+    gain_grads = gain_grads + across(gain_grads, "x")
+    gain_grads = gain_grads + step(gain_grads, "x", 1)
     attn_sums = ring_gather(jnp.stack([attn_sums, attn_across]), "x")
-    gain_grads = jnp.sum(after(gain_grads, attn_across), axis=0)[:2]
     gate_grad, up_grad, down_grad = finish_mlp(spots, xs, yhs, core, mlp_sums)
     query_grad, key_grad, value_grad, output_grad = finish_attn(spots, xs, yhs, core, attn_sums)
     tokens_grad = (
-        residual_grad + norm_back(rows_in, scale_attn, gain_one, normed_attn_grad)
+        residual_grad + norm_back(rows_in, scale_attn, gain_one, after(normed_attn_grad, attn_across).astype(F32))
     ).astype(BF)[None]
     return (
         layer_out,

time: 549 us -> 546 us (level)
  the two profiles are of different devices: /device:TPU:1 before, /device:TPU:24 now
where the time goes in v6:
time: 546 us; the launch traced here: 541 us
  waiting for transfers between devices  208 us (38%)
  Pallas kernels  158 us (29%)
  starting transfers between devices  99.6 us (18%)
  other arithmetic  30.8 us (6%)
  local copies, waits for them, and re-layouts  28.3 us (5%)
  between operations  15.8 us (3%)
    ppermute x75, waiting for transfers between devices, send(): return lax.ppermute(value, BOTH, pairs)  199 us
    pallas_call x18, Pallas kernels, call(): pl.pallas_call(body, grid_spec=pltpu.PrefetchScalarGridSpec(num_scalar_pr...  158 us
    ppermute x75, starting transfers between devices, send(): return lax.ppermute(value, BOTH, pairs)  99.3 us
    unnamed x182, local copies, waits for them, and re-layouts  23.1 us
  transfers between devices with their start and end apart: 82, of which 46 were waited for; matrix products, arithmetic and copies ran while one was open for 6% of the time, Pallas kernels for 25%

profile of v6, /device:TPU:24, one launch (start us, length us, event | category | flops | bytes accessed | tf_op | source)
XLA Modules:
  0.0 540.7 jit_solution(11882300406653007549)
XLA Ops:
  12.9 4.0 shard_map.212
  27.8 4.4 collective-permute-done.1
  32.2 9.9 %collective-permute-done.2 = bf16[4,2,32,704]{3,2,0,1:T(8,128)(2,1)S(1)} collective-permute-done((bf16[4,2,32,704]{3,2,0,1:T(8,128)(2,1)S(1)}, bf16[4,2,32,704]{3,2,0,1:T(8,128)(2,1)S(1)}, u32[]{:S(2)}, u32[]{:S(2)}) %collective-permute-start.2) | collective-permute-done | bytes 360480 | tf_op jit(solution)/shard_map/ppermute | solution.py:45
  47.5 4.3 collective-permute-done.4
  57.0 12.3 %collective-permute-done.6 = bf16[8,32,576]{2,1,0:T(8,128)(2,1)S(1)} collective-permute-done((bf16[8,32,576]{2,1,0:T(8,128)(2,1)S(1)}, bf16[8,32,576]{2,1,0:T(8,128)(2,1)S(1)}, u32[]{:S(2)}, u32[]{:S(2)}) %collective-permute-start.6) | collective-permute-done | bytes 294944 | tf_op jit(solution)/shard_map/ppermute | solution.py:45
  71.5 17.6 %collective-permute-done.8.other_ref = bf16[4,8,32,576]{3,2,1,0:T(8,128)(2,1)} collective-permute-done((bf16[4,8,32,576]{3,2,1,0:T(8,128)(2,1)S(1)}, bf16[4,8,32,576]{3,2,1,0:T(8,128)(2,1)}, u32[]{:S(2)}, u32[]{:S(2)}) %collective-permute-start.8) | collective-permute-done | bytes 1179680 | tf_op jit(solution)/shard_map/ppermute | solution.py:45
  89.4 4.9 shard_map.213
  97.3 6.1 %shard_map.214 = (bf16[1024,256]{1,0:T(8,128)(2,1)S(1)}, bf16[2,1024,64]{2,1,0:T(8,128)(2,1)S(1)}) custom-call(s32[8]{0:T(128)S(1)} %stack.212.chunk.nat, bf16[1024,2048]{1,0:T(8,128)(2,1)} %all-gather.7.cloned.1.call-done.refs_0_.refs_1_.refs_2_.refs_3_.refs_4_.refs_5_.refs_6_.refs_7_, ...), custom_call_target="tpu_custom_call" | custom-call | flops 1000 | bytes 1500000 | tf_op jit(solution)/shard_map/pallas_call | solution.py:136
  103.9 6.4 %collective-permute-done.9 = bf16[2,1024,64]{1,2,0:T(8,128)(2,1)S(1)} collective-permute-done((bf16[2,1024,64]{1,2,0:T(8,128)(2,1)S(1)}, bf16[2,1024,64]{1,2,0:T(8,128)(2,1)S(1)}, u32[]{:S(2)}, u32[]{:S(2)}) %collective-permute-start.9) | collective-permute-done | bytes 262176 | tf_op jit(solution)/shard_map/ppermute | solution.py:45
  112.8 8.3 %shard_map.215 = (bf16[256,256]{1,0:T(8,128)(2,1)S(1)}, bf16[128,2048]{1,0:T(8,128)(2,1)S(1)}, bf16[128,2048]{1,0:T(8,128)(2,1)}) custom-call(s32[8]{0:T(128)S(1)} %bitcast.208, s32[16]{0:T(128)S(1)} %select_reduce_fusion.1.key_slot, bf16[1024,256]{1,0:T(8,128)(2,1)S(1)} %get-tuple-element.117.q_ref.refs_0_, ...), custom_call_target="tpu_custom_call" | custom-call | flops 1000 | bytes 1800000 | tf_op jit(solution)/shard_map/pallas_call | solution.py:136
  121.9 9.2 %all-gather.11.cloned.1.call-done = bf16[12,8,32,704]{3,2,1,0:T(8,128)(2,1)} async-done(((bf16[3,8,32,704]{3,2,1,0:T(8,128)(2,1)}), bf16[12,8,32,704]{3,2,1,0:T(8,128)(2,1)}) %all-gather.11.cloned.1.call-update) | async-done | bytes 4325392 | tf_op jit(solution)/shard_map/all_gather | solution.py:794
  135.0 5.4 %shard_map.216 = (bf16[256,256]{1,0:T(8,128)(2,1)S(1)}, bf16[128,2048]{1,0:T(8,128)(2,1)S(1)}, bf16[128,2048]{1,0:T(8,128)(2,1)S(1)}) custom-call(s32[8]{0:T(128)S(1)} %bitcast.210, s32[16]{0:T(128)S(1)} %select_reduce_fusion.1.key_slot, bf16[1024,256]{1,0:T(8,128)(2,1)S(1)} %get-tuple-element.117.q_ref.refs_0_, ...), custom_call_target="tpu_custom_call" | custom-call | flops 1000 | bytes 1800000 | tf_op jit(solution)/shard_map/pallas_call | solution.py:136
  141.7 7.8 %collective-permute-start.17 = (bf16[128,2048]{1,0:T(8,128)(2,1)S(1)}, bf16[128,2048]{1,0:T(8,128)(2,1)S(1)}, u32[]{:S(2)}, u32[]{:S(2)}) collective-permute-start(bf16[128,2048]{1,0:T(8,128)(2,1)S(1)} %add_convert_fusion.6), channel_id=1, source_target_pairs={{0,4},{1,5},{2,6},{3,7},{4,0},{5,1},{6,2},{7,3},{8,12},{9,13},{10,... | collective-permute-start | bytes 1572872 | tf_op jit(solution)/shard_map/ppermute | solution.py:45
  152.4 3.2 collective-permute-start.15
  155.7 5.0 shard_map.218
  160.8 12.5 %collective-permute-done.17 = bf16[128,2048]{1,0:T(8,128)(2,1)S(1)} collective-permute-done((bf16[128,2048]{1,0:T(8,128)(2,1)S(1)}, bf16[128,2048]{1,0:T(8,128)(2,1)S(1)}, u32[]{:S(2)}, u32[]{:S(2)}) %collective-permute-start.17) | collective-permute-done | bytes 524320 | tf_op jit(solution)/shard_map/ppermute | solution.py:45
  173.3 13.0 %collective-permute-done.16 = bf16[128,2048]{1,0:T(8,128)(2,1)S(1)} collective-permute-done((bf16[128,2048]{1,0:T(8,128)(2,1)}, bf16[128,2048]{1,0:T(8,128)(2,1)S(1)}, u32[]{:S(2)}, u32[]{:S(2)}) %collective-permute-start.16) | collective-permute-done | bytes 524320 | tf_op jit(solution)/shard_map/ppermute | solution.py:45
  191.7 8.5 %shard_map.219 = bf16[3,2,8,128,704]{4,3,2,1,0:T(8,128)(2,1)} custom-call(s32[8]{0:T(128)S(1)} %stack.223.slot, s32[2]{0:T(128)S(1)} %pad_add_fusion.2.halves, bf16[4,3,8,32,704]{4,3,2,1,0:T(8,128)(2,1)S(1)} %bitcast.207, bf16[4,3,8,32,704]{4,3,2,1,0:T(8,128)(2,1)} %copy-done.63), custom_call_target="tpu_custom_call" | custom-call | flops 1000 | bytes 1800000 | tf_op jit(solution)/shard_map/pallas_call | solution.py:136
  204.5 18.8 %shard_map.220 = (bf16[1024,704]{1,0:T(8,128)(2,1)S(1)}, bf16[1024,704]{1,0:T(8,128)(2,1)}, bf16[1024,704]{1,0:T(8,128)(2,1)}, bf16[128,2048]{1,0:T(8,128)(2,1)S...) custom-call(s32[8]{0:T(128)S(1)} %stack.212.chunk.nat, ...), custom_call_target="tpu_custom_call" | custom-call | flops 1000 | bytes 5400000 | tf_op jit(solution)/shard_map/pallas_call | solution.py:136
  224.6 8.7 %collective-permute-start.26 = (bf16[128,2048]{1,0:T(8,128)(2,1)}, bf16[128,2048]{1,0:T(8,128)(2,1)S(1)}, u32[]{:S(2)}, u32[]{:S(2)}) collective-permute-start(bf16[128,2048]{1,0:T(8,128)(2,1)} %collective-permute-done.23.refs_2_.refs_6_), channel_id=1, source_target_pairs={{0,1},{1,0},{2,3},{3,2},{4,5},{5,4},{6,7},{7,6},{8,9},{9,8},{10,11... | collective-permute-start | bytes 1572872 | tf_op jit(solution)/shard_map/ppermute | solution.py:45
  235.3 18.6 %shard_map.221 = (bf16[1024,704]{1,0:T(8,128)(2,1)S(1)}, bf16[1024,704]{1,0:T(8,128)(2,1)}, bf16[1024,704]{1,0:T(8,128)(2,1)}, bf16[128,2048]{1,0:T(8,128)(2,1)S...) custom-call(s32[8]{0:T(128)S(1)} %stack.212.chunk.nat, ...), custom_call_target="tpu_custom_call", output_to_operand_aliasing={{0}: (10, {}), {1}: (11, {}), {2}: (12, {}), {6}: (13, {})} | custom-call | flops 1000 | bytes 5400000 | tf_op jit(solution)/shard_map/pallas_call | solution.py:136
  260.0 13.8 %collective-permute-done.28 = bf16[128,2048]{1,0:T(8,128)(2,1)} collective-permute-done((bf16[128,2048]{1,0:T(8,128)(2,1)}, bf16[128,2048]{1,0:T(8,128)(2,1)}, u32[]{:S(2)}, u32[]{:S(2)}) %collective-permute-start.28) | collective-permute-done | bytes 524320 | tf_op jit(solution)/shard_map/ppermute | solution.py:45
  275.9 19.5 %shard_map.222 = (bf16[4,4,2,2,3,16,704]{6,5,4,3,2,1,0:T(8,128)(2,1)}, bf16[4,2,2,3,16,704]{5,4,3,2,1,0:T(8,128)(2,1)S(1)}, bf16[4,2,2,3,16,704]{5,4,3,2,1,0:T(8...) custom-call(s32[8]{0:T(128)S(1)} %stack.244.column, s32[4]{0:T(128)S(1)} %pad_add_fusion.1.xs, ...), custom_call_target="tpu_custom_call" | custom-call | flops 1000 | bytes 5100000 | tf_op jit(solution)/shard_map/pallas_call | solution.py:136
  297.6 3.1 multiply_reduce_fusion
  302.2 3.7 collective-permute-start.31
  309.1 6.5 %shard_map.223 = (bf16[256,256]{1,0:T(8,128)(2,1)S(1)}, f32[2048,64]{1,0:T(8,128)S(1)}, f32[2048,64]{1,0:T(8,128)S(1)}) custom-call(s32[8]{0:T(128)S(1)} %bitcast.212, s32[16]{0:T(128)S(1)} %select_reduce_fusion.1.key_slot, s32[1]{0:T(128)} %bitcast.16.core, s32[16]{0:T(128)S(1)} %copy-done.51, bf16[1024,256]{1,0:T(8,128)(2,1)S(1)} %get-tuple-element.117.q_ref.refs_0_, ...), custom_call_target="tpu_custom_call" | custom-call | flops 1000 | bytes 2400000 | tf_op jit(solution)/shard_map/pallas_call | solution.py:136
  322.9 4.3 collective-permute-start.39
  329.1 19.8 %shard_map.224 = (bf16[512,256]{1,0:T(8,128)(2,1)S(1)}, f32[2048,64]{1,0:T(8,128)S(1)}, f32[2048,64]{1,0:T(8,128)}) custom-call(s32[8]{0:T(128)S(1)} %bitcast.213, s32[16]{0:T(128)S(1)} %select_reduce_fusion.1.key_slot, s32[1]{0:T(128)} %bitcast.16.core, s32[16]{0:T(128)S(1)} %copy-done.51, bf16[1024,256]{1,0:T(8,128)(2,1)S(1)} %get-tuple-element.117.q_ref.refs_0_, ...), custom_call_target="tpu_custom_call" | custom-call | flops 1000 | bytes 4800000 | tf_op jit(solution)/shard_map/pallas_call | solution.py:136
  350.9 4.4 shard_map.225
  357.5 3.5 collective-permute-start.41
  362.5 5.2 collective-permute-done.41
  368.7 7.0 %shard_map.226 = (bf16[8,128,2048]{2,1,0:T(8,128)(2,1)}, f32[8,2048]{1,0:T(8,128)S(1)}) custom-call(s32[8]{0:T(128)S(1)} %stack.212.chunk.nat, bf16[256,256]{1,0:T(8,128)(2,1)S(1)} %get-tuple-element.164.dq0_ref.refs_20_, bf16[512,256]{1,0:T(8,128)(2,1)S(1)} %copy-done.30, bf16[256,256]{1,0:T(8,128)(2,1)S(1)} %copy-done.34, ...), custom_call_target="tpu_custom_call" | custom-call | flops 1000 | bytes 1500000 | tf_op jit(solution)/shard_map/pallas_call | solution.py:136
  376.5 3.9 collective-permute-done.45
  383.2 6.7 %collective-permute-start.46 = (bf16[2,2,3,16,704]{4,3,2,1,0:T(8,128)(2,1)S(1)}, bf16[2,2,3,16,704]{4,3,2,1,0:T(8,128)(2,1)S(1)}, u32[]{:S(2)}, u32[]{:S(2)}) collective-permute-start(bf16[2,2,3,16,704]{4,3,2,1,0:T(8,128)(2,1)S(1)} %get-tuple-element.224), channel_id=1, source_target_pairs={{0,32},{1,33},{2,34},{3,35},{4,36},{5,37},{6,38},{7,39},{8,40},{9,... | collective-permute-start | bytes 811016 | tf_op jit(solution)/shard_map/ppermute | solution.py:45
  390.0 3.3 collective-permute-start.47
  397.8 4.9 collective-permute-done.48
  403.7 10.2 %shard_map.227 = (bf16[4,4,2,16,576]{4,3,2,1,0:T(8,128)(2,1)S(1)}, bf16[4,4,2,16,576]{4,3,2,1,0:T(8,128)(2,1)}, bf16[4,4,2,16,576]{4,3,2,1,0:T(8,128)(2,1)}, bf16[4,4,2,16,576]{4,3,2,1,0:T(8,128)(2,1)}) custom-call(s32[8]{0:T(128)S(1)} %copy-done.57, s32[4]{0:T(128)S(1)} %pad_add_fusion.1.xs, s32[4]{0:T(128)S(1)} %copy-done.49, s32[1]{0:T(128)} %bitcast.16.core, ...), custom_call_target="tpu_custom_call" | custom-call | flops 1000 | bytes 3000000 | tf_op jit(solution)/shard_map/pallas_call | solution.py:136
  416.0 4.8 collective-permute-start.52
  421.5 5.2 collective-permute-done.52
  428.0 4.0 collective-permute-done.50
  433.7 9.8 %collective-permute-done.54 = bf16[4,4,2,16,576]{4,3,2,1,0:T(8,128)(2,1)S(1)} collective-permute-done((bf16[4,4,2,16,576]{4,3,2,1,0:T(8,128)(2,1)}, bf16[4,4,2,16,576]{4,3,2,1,0:T(8,128)(2,1)S(1)}, u32[]{:S(2)}, u32[]{:S(2)}) %collective-permute-start.54) | collective-permute-done | bytes 589856 | tf_op jit(solution)/shard_map/ppermute | solution.py:45
  446.9 8.6 %collective-permute-done.55 = bf16[4,4,2,16,576]{4,3,2,1,0:T(8,128)(2,1)S(1)} collective-permute-done((bf16[4,4,2,16,576]{4,3,2,1,0:T(8,128)(2,1)S(1)}, bf16[4,4,2,16,576]{4,3,2,1,0:T(8,128)(2,1)S(1)}, u32[]{:S(2)}, u32[]{:S(2)}) %collective-permute-start.55) | collective-permute-done | bytes 589856 | tf_op jit(solution)/shard_map/ppermute | solution.py:45
  480.9 5.9 %collective-permute-done.72.refs_1_ = bf16[2,2,4,3,16,704]{5,4,3,2,1,0:T(8,128)(2,1)} collective-permute-done((bf16[2,2,4,3,16,704]{5,4,3,2,1,0:T(8,128)(2,1)S(1)}, bf16[2,2,4,3,16,704]{5,4,3,2,1,0:T(8,128)(2,1)}, u32[]{:S(2)}, u32[]{:S(2)}) %collective-permute-start.72) | collective-permute-done | bytes 1081376 | tf_op jit(solution)/shard_map/ppermute | solution.py:45
  486.8 3.3 collective-permute-start.67
  492.3 12.4 %collective-permute-done.67 = f32[2,2048]{1,0:T(2,128)S(1)} collective-permute-done((f32[2,2048]{1,0:T(2,128)S(1)}, f32[2,2048]{1,0:T(2,128)S(1)}, u32[]{:S(2)}, u32[]{:S(2)}) %collective-permute-start.67) | collective-permute-done | bytes 16416 | tf_op jit(solution)/shard_map/ppermute | solution.py:45
  508.2 4.3 collective-permute-done.68
  513.2 4.0 collective-permute-done.71.refs_3_
  523.8 6.0 %shard_map.229 = (f32[128,5632]{1,0:T(8,128)}, f32[128,5632]{1,0:T(8,128)}, f32[5632,128]{1,0:T(8,128)}) custom-call(s32[5]{0:T(128)S(1)} %copy-done.53, s32[4]{0:T(128)S(1)} %pad_add_fusion.1.xs, s32[4]{0:T(128)S(1)} %copy-done.49, s32[1]{0:T(128)} %bitcast.16.core, bf16[2,2,4,3,16,704]{5,4,3,2,1,0:T(8,128)(2,1)S(1)} %pad_maximum_fusion.1.refs_0_, ...), custom_call_target="tpu_custom_call" | custom-call | flops 1000 | bytes 1500000 | tf_op jit(solution)/shard_map/pallas_call | solution.py:136
  (417 shorter events, 147.6 us)
Async XLA Ops:
  7.2 88.3 %all-gather.7.cloned.1.call-start = ((), (), s32[]{:S(2)}) async-start(), calls=%async_computation.3 | async-start | bytes 4718592 | tf_op jit(solution)/shard_map/all_gather | solution.py:787
  20.6 11.5 %collective-permute-start.1 = (bf16[4,2,32,704]{3,2,0,1:T(8,128)(2,1)S(1)}, bf16[4,2,32,704]{3,2,0,1:T(8,128)(2,1)S(1)}, u32[]{:S(2)}, u32[]{:S(2)}) collective-permute-start(bf16[4,2,32,704]{3,2,0,1:T(8,128)(2,1)S(1)} %pad_maximum_fusion.3), channel_id=1, source_target_pairs={{0,2},{1,7},{2,4},{3,1},{4,6},{5,3},{6,0},{7,5},{8,10},{9,15},{10,... | collective-permute-start | bytes 1081352 | tf_op jit(solution)/shard_map/ppermute | solution.py:45
  22.7 19.4 %collective-permute-start.2 = (bf16[4,2,32,704]{3,2,0,1:T(8,128)(2,1)S(1)}, bf16[4,2,32,704]{3,2,0,1:T(8,128)(2,1)S(1)}, u32[]{:S(2)}, u32[]{:S(2)}) collective-permute-start(bf16[4,2,32,704]{3,2,0,1:T(8,128)(2,1)S(1)} %pad_maximum_fusion.4), channel_id=1, source_target_pairs={{0,6},{1,3},{2,0},{3,5},{4,2},{5,7},{6,4},{7,1},{8,14},{9,11},{10,... | collective-permute-start | bytes 1081352 | tf_op jit(solution)/shard_map/ppermute | solution.py:45
  24.9 19.3 %collective-permute-start.3 = (bf16[4,2,32,704]{3,2,1,0:T(8,128)(2,1)S(1)}, bf16[4,2,32,704]{3,2,1,0:T(8,128)(2,1)S(1)}, u32[]{:S(2)}, u32[]{:S(2)}) collective-permute-start(bf16[4,2,32,704]{3,2,1,0:T(8,128)(2,1)S(1)} %pad_maximum_fusion.5), channel_id=1, source_target_pairs={{0,4},{1,5},{2,6},{3,7},{4,0},{5,1},{6,2},{7,3},{8,12},{9,13},{10,... | collective-permute-start | bytes 1081352 | tf_op jit(solution)/shard_map/ppermute | solution.py:45
  44.3 86.8 %all-gather.11.cloned.1.call-start = ((), (), s32[]{:S(2)}) async-start(), calls=%async_computation.8 | async-start | bytes 5898240 | tf_op jit(solution)/shard_map/all_gather | solution.py:794
  45.5 159.0 %all-gather.9.cloned.1.call-start = ((), (), s32[]{:S(2)}) async-start(), calls=%async_computation.4 | async-start | bytes 4718592 | tf_op jit(solution)/shard_map/all_gather | solution.py:795
  51.9 17.4 %collective-permute-start.6 = (bf16[8,32,576]{2,1,0:T(8,128)(2,1)S(1)}, bf16[8,32,576]{2,1,0:T(8,128)(2,1)S(1)}, u32[]{:S(2)}, u32[]{:S(2)}) collective-permute-start(bf16[8,32,576]{2,1,0:T(8,128)(2,1)S(1)} %get-tuple-element.246), channel_id=1, source_target_pairs={{0,48},{1,17},{2,50},{3,19},{4,52},{5,21},{6,54},{7,23},{8,56},{9,... | collective-permute-start | bytes 884744 | tf_op jit(solution)/shard_map/ppermute | solution.py:45
  54.8 14.5 %collective-permute-start.5 = (bf16[8,32,576]{2,1,0:T(8,128)(2,1)S(1)}, bf16[8,32,576]{2,1,0:T(8,128)(2,1)S(1)}, u32[]{:S(2)}, u32[]{:S(2)}) collective-permute-start(bf16[8,32,576]{2,1,0:T(8,128)(2,1)S(1)} %get-tuple-element.246), channel_id=1, source_target_pairs={{0,16},{1,49},{2,18},{3,51},{4,20},{5,53},{6,22},{7,55},{8,24},{9,... | collective-permute-start | bytes 884744 | tf_op jit(solution)/shard_map/ppermute | solution.py:45
  54.8 16.2 %collective-permute-start.7 = (bf16[8,32,576]{2,1,0:T(8,128)(2,1)S(1)}, bf16[8,32,576]{2,1,0:T(8,128)(2,1)S(1)}, u32[]{:S(2)}, u32[]{:S(2)}) collective-permute-start(bf16[8,32,576]{2,1,0:T(8,128)(2,1)S(1)} %get-tuple-element.246), channel_id=1, source_target_pairs={{0,32},{1,33},{2,34},{3,35},{4,36},{5,37},{6,38},{7,39},{8,40},{9,... | collective-permute-start | bytes 884744 | tf_op jit(solution)/shard_map/ppermute | solution.py:45
  71.3 17.8 %collective-permute-start.8 = (bf16[4,8,32,576]{3,2,1,0:T(8,128)(2,1)S(1)}, bf16[4,8,32,576]{3,2,1,0:T(8,128)(2,1)}, u32[]{:S(2)}, u32[]{:S(2)}) collective-permute-start(bf16[4,8,32,576]{3,2,1,0:T(8,128)(2,1)S(1)} %pad_maximum_fusion.own_ref), channel_id=1, source_target_pairs={{0,8},{1,73},{2,10},{3,75},{4,12},{5,77},{6,14},{7,79},{8,64},{9,1... | collective-permute-start | bytes 3538952 | tf_op jit(solution)/shard_map/ppermute | solution.py:45
  89.1 278.7 %reduce-scatter.6.cloned.1.call-start = ((), (), s32[]{:S(2)}) async-start(), calls=%async_computation.6 | async-start | bytes 5898240 | tf_op jit(solution)/shard_map/reduce_scatter | solution.py:852
  131.1 58.5 %collective-permute-start.20 = (bf16[4,3,8,32,704]{4,3,2,1,0:T(8,128)(2,1)}, bf16[4,3,8,32,704]{4,3,2,1,0:T(8,128)(2,1)S(1)}, u32[]{:S(2)}, u32[]{:S(2)}) collective-permute-start(bf16[4,3,8,32,704]{4,3,2,1,0:T(8,128)(2,1)} %bitcast.204), channel_id=1, source_target_pairs={{0,8},{1,73},{2,10},{3,75},{4,12},{5,77},{6,14},{7,79},{8,64},{9,1... | collective-permute-start | bytes 12976136 | tf_op jit(solution)/shard_map/ppermute | solution.py:45
  141.7 31.6 %collective-permute-start.17 = (bf16[128,2048]{1,0:T(8,128)(2,1)S(1)}, bf16[128,2048]{1,0:T(8,128)(2,1)S(1)}, u32[]{:S(2)}, u32[]{:S(2)}) collective-permute-start(bf16[128,2048]{1,0:T(8,128)(2,1)S(1)} %add_convert_fusion.6), channel_id=1, source_target_pairs={{0,4},{1,5},{2,6},{3,7},{4,0},{5,1},{6,2},{7,3},{8,12},{9,13},{10,... | collective-permute-start | bytes 1572872 | tf_op jit(solution)/shard_map/ppermute | solution.py:45
  150.5 35.8 %collective-permute-start.16 = (bf16[128,2048]{1,0:T(8,128)(2,1)}, bf16[128,2048]{1,0:T(8,128)(2,1)S(1)}, u32[]{:S(2)}, u32[]{:S(2)}) collective-permute-start(bf16[128,2048]{1,0:T(8,128)(2,1)} %add_convert_fusion.7), channel_id=1, source_target_pairs={{0,2},{1,7},{2,4},{3,1},{4,6},{5,3},{6,0},{7,5},{8,10},{9,15},{10,... | collective-permute-start | bytes 1572872 | tf_op jit(solution)/shard_map/ppermute | solution.py:45
  152.4 33.8 %collective-permute-start.15 = (bf16[128,2048]{1,0:T(8,128)(2,1)}, bf16[128,2048]{1,0:T(8,128)(2,1)S(1)}, u32[]{:S(2)}, u32[]{:S(2)}) collective-permute-start(bf16[128,2048]{1,0:T(8,128)(2,1)} %add_convert_fusion.8), channel_id=1, source_target_pairs={{0,6},{1,3},{2,0},{3,5},{4,2},{5,7},{6,4},{7,1},{8,14},{9,11},{10,... | collective-permute-start | bytes 1572872 | tf_op jit(solution)/shard_map/ppermute | solution.py:45
  160.6 25.6 %collective-permute-start.14 = (bf16[128,2048]{1,0:T(8,128)(2,1)S(1)}, bf16[128,2048]{1,0:T(8,128)(2,1)S(1)}, u32[]{:S(2)}, u32[]{:S(2)}) collective-permute-start(bf16[128,2048]{1,0:T(8,128)(2,1)S(1)} %get-tuple-element.128), channel_id=1, source_target_pairs={{0,1},{1,0},{2,3},{3,2},{4,5},{5,4},{6,7},{7,6},{8,9},{9,8},{10,11... | collective-permute-start | bytes 1572872 | tf_op jit(solution)/shard_map/ppermute | solution.py:45
  189.6 14.9 %collective-permute-start.18 = (bf16[128,2048]{1,0:T(8,128)(2,1)S(1)}, bf16[128,2048]{1,0:T(8,128)(2,1)}, u32[]{:S(2)}, u32[]{:S(2)}) collective-permute-start(bf16[128,2048]{1,0:T(8,128)(2,1)S(1)} %multiply_convert_fusion.refs_0_), channel_id=1, source_target_pairs={{0,1},{1,0},{2,3},{3,2},{4,5},{5,4},{6,7},{7,6},{8,9},{9,8},{10,11... | collective-permute-start | bytes 1572872 | tf_op jit(solution)/shard_map/ppermute | solution.py:45
  200.5 23.6 %collective-permute-start.23 = (bf16[128,2048]{1,0:T(8,128)(2,1)S(1)}, bf16[128,2048]{1,0:T(8,128)(2,1)}, u32[]{:S(2)}, u32[]{:S(2)}) collective-permute-start(bf16[128,2048]{1,0:T(8,128)(2,1)S(1)} %multiply_convert_fusion.refs_0_), channel_id=1, source_target_pairs={{0,4},{1,5},{2,6},{3,7},{4,0},{5,1},{6,2},{7,3},{8,12},{9,13},{10,... | collective-permute-start | bytes 1572872 | tf_op jit(solution)/shard_map/ppermute | solution.py:45
  202.3 21.8 %collective-permute-start.22 = (bf16[128,2048]{1,0:T(8,128)(2,1)S(1)}, bf16[128,2048]{1,0:T(8,128)(2,1)}, u32[]{:S(2)}, u32[]{:S(2)}) collective-permute-start(bf16[128,2048]{1,0:T(8,128)(2,1)S(1)} %multiply_convert_fusion.refs_0_), channel_id=1, source_target_pairs={{0,6},{1,3},{2,0},{3,5},{4,2},{5,7},{6,4},{7,1},{8,14},{9,11},{10,... | collective-permute-start | bytes 1572872 | tf_op jit(solution)/shard_map/ppermute | solution.py:45
  255.3 18.5 %collective-permute-start.28 = (bf16[128,2048]{1,0:T(8,128)(2,1)}, bf16[128,2048]{1,0:T(8,128)(2,1)}, u32[]{:S(2)}, u32[]{:S(2)}) collective-permute-start(bf16[128,2048]{1,0:T(8,128)(2,1)} %fusion.11), channel_id=1, source_target_pairs={{0,6},{1,3},{2,0},{3,5},{4,2},{5,7},{6,4},{7,1},{8,14},{9,11},{10,... | collective-permute-start | bytes 1572872 | tf_op jit(solution)/shard_map/ppermute | solution.py:45
  258.1 38.4 %collective-permute-start.30 = (bf16[128,2048]{1,0:T(8,128)(2,1)}, bf16[128,2048]{1,0:T(8,128)(2,1)}, u32[]{:S(2)}, u32[]{:S(2)}) collective-permute-start(bf16[128,2048]{1,0:T(8,128)(2,1)} %get-tuple-element.230), channel_id=1, source_target_pairs={{0,4},{1,5},{2,6},{3,7},{4,0},{5,1},{6,2},{7,3},{8,12},{9,13},{10,... | collective-permute-start | bytes 1572872 | tf_op jit(solution)/shard_map/ppermute | solution.py:45
  259.8 36.7 %collective-permute-start.29 = (bf16[128,2048]{1,0:T(8,128)(2,1)}, bf16[128,2048]{1,0:T(8,128)(2,1)}, u32[]{:S(2)}, u32[]{:S(2)}) collective-permute-start(bf16[128,2048]{1,0:T(8,128)(2,1)} %get-tuple-element.231), channel_id=1, source_target_pairs={{0,2},{1,7},{2,4},{3,1},{4,6},{5,3},{6,0},{7,5},{8,10},{9,15},{10,... | collective-permute-start | bytes 1572872 | tf_op jit(solution)/shard_map/ppermute | solution.py:45
  296.5 163.5 %reduce-scatter.4.cloned.1.call-start = ((), (), s32[]{:S(2)}) async-start(), calls=%async_computation.5 | async-start | bytes 4718592 | tf_op jit(solution)/shard_map/reduce_scatter | solution.py:853
  297.1 178.8 %all-gather.13.cloned.1.call-start = ((), (), s32[]{:S(2)}) async-start(), calls=%async_computation.9 | async-start | bytes 1114112 | tf_op jit(solution)/shard_map/all_gather | solution.py:895
  305.9 13.8 %collective-permute-start.33 = (bf16[128,2048]{1,0:T(8,128)(2,1)S(1)}, bf16[128,2048]{1,0:T(8,128)(2,1)S(1)}, u32[]{:S(2)}, u32[]{:S(2)}) collective-permute-start(bf16[128,2048]{1,0:T(8,128)(2,1)S(1)} %get-tuple-element.219.refs_1_.refs_8_), channel_id=1, source_target_pairs={{0,6},{1,3},{2,0},{3,5},{4,2},{5,7},{6,4},{7,1},{8,14},{9,11},{10,... | collective-permute-start | bytes 1572872 | tf_op jit(solution)/shard_map/ppermute | solution.py:45
  306.4 14.6 %collective-permute-start.32 = (bf16[128,2048]{1,0:T(8,128)(2,1)S(1)}, bf16[128,2048]{1,0:T(8,128)(2,1)S(1)}, u32[]{:S(2)}, u32[]{:S(2)}) collective-permute-start(bf16[128,2048]{1,0:T(8,128)(2,1)S(1)} %get-tuple-element.219.refs_1_.refs_8_), channel_id=1, source_target_pairs={{0,2},{1,7},{2,4},{3,1},{4,6},{5,3},{6,0},{7,5},{8,10},{9,15},{10,... | collective-permute-start | bytes 1572872 | tf_op jit(solution)/shard_map/ppermute | solution.py:45
  307.9 21.1 %collective-permute-start.36 = (bf16[4,2,2,3,16,704]{5,4,3,2,1,0:T(8,128)(2,1)S(1)}, bf16[4,2,2,3,16,704]{5,4,3,2,1,0:T(8,128)(2,1)S(1)}, u32[]{:S(2)}, u32[]{:S(2)}) collective-permute-start(bf16[4,2,2,3,16,704]{5,4,3,2,1,0:T(8,128)(2,1)S(1)} %copy-done.85), channel_id=1, source_target_pairs={{0,8},{1,73},{2,10},{3,75},{4,12},{5,77},{6,14},{7,79},{8,64},{9,1... | collective-permute-start | bytes 3244040 | tf_op jit(solution)/shard_map/ppermute | solution.py:45
  322.9 28.0 %collective-permute-start.39 = (bf16[4,2,2,3,16,704]{5,4,3,2,1,0:T(8,128)(2,1)S(1)}, bf16[4,2,2,3,16,704]{5,4,3,2,1,0:T(8,128)(2,1)S(1)}, u32[]{:S(2)}, u32[]{:S(2)}) collective-permute-start(bf16[4,2,2,3,16,704]{5,4,3,2,1,0:T(8,128)(2,1)S(1)} %copy-done.84), channel_id=1, source_target_pairs={{0,72},{1,9},{2,74},{3,11},{4,76},{5,13},{6,78},{7,15},{8,0},{9,65... | collective-permute-start | bytes 3244040 | tf_op jit(solution)/shard_map/ppermute | solution.py:45
  327.1 21.7 %collective-permute-start.37 = (bf16[128,2048]{1,0:T(8,128)(2,1)S(1)}, bf16[128,2048]{1,0:T(8,128)(2,1)S(1)}, u32[]{:S(2)}, u32[]{:S(2)}) collective-permute-start(bf16[128,2048]{1,0:T(8,128)(2,1)S(1)} %get-tuple-element.219.refs_1_.refs_8_), channel_id=1, source_target_pairs={{0,4},{1,5},{2,6},{3,7},{4,0},{5,1},{6,2},{7,3},{8,12},{9,13},{10,... | collective-permute-start | bytes 1572872 | tf_op jit(solution)/shard_map/ppermute | solution.py:45
  362.4 18.0 %collective-permute-start.45 = (bf16[4,2,2,3,16,704]{5,4,3,2,1,0:T(8,128)(2,1)}, bf16[4,2,2,3,16,704]{5,4,3,2,1,0:T(8,128)(2,1)}, u32[]{:S(2)}, u32[]{:S(2)}) collective-permute-start(bf16[4,2,2,3,16,704]{5,4,3,2,1,0:T(8,128)(2,1)} %add_convert_fusion.1), channel_id=1, source_target_pairs={{0,8},{1,73},{2,10},{3,75},{4,12},{5,77},{6,14},{7,79},{8,64},{9,1... | collective-permute-start | bytes 3244040 | tf_op jit(solution)/shard_map/ppermute | solution.py:45
  376.4 153.4 %reduce-scatter.8.cloned.1.call-start = ((), (), s32[]{:S(2)}) async-start(), calls=%async_computation.7 | async-start | bytes 4718592 | tf_op jit(solution)/shard_map/reduce_scatter | solution.py:900
  383.2 14.7 %collective-permute-start.46 = (bf16[2,2,3,16,704]{4,3,2,1,0:T(8,128)(2,1)S(1)}, bf16[2,2,3,16,704]{4,3,2,1,0:T(8,128)(2,1)S(1)}, u32[]{:S(2)}, u32[]{:S(2)}) collective-permute-start(bf16[2,2,3,16,704]{4,3,2,1,0:T(8,128)(2,1)S(1)} %get-tuple-element.224), channel_id=1, source_target_pairs={{0,32},{1,33},{2,34},{3,35},{4,36},{5,37},{6,38},{7,39},{8,40},{9,... | collective-permute-start | bytes 811016 | tf_op jit(solution)/shard_map/ppermute | solution.py:45
  389.9 12.8 %collective-permute-start.48 = (bf16[2,2,3,16,704]{4,3,2,1,0:T(8,128)(2,1)S(1)}, bf16[2,2,3,16,704]{4,3,2,1,0:T(8,128)(2,1)S(1)}, u32[]{:S(2)}, u32[]{:S(2)}) collective-permute-start(bf16[2,2,3,16,704]{4,3,2,1,0:T(8,128)(2,1)S(1)} %get-tuple-element.225), channel_id=1, source_target_pairs={{0,16},{1,49},{2,18},{3,51},{4,20},{5,53},{6,22},{7,55},{8,24},{9,... | collective-permute-start | bytes 811016 | tf_op jit(solution)/shard_map/ppermute | solution.py:45
  390.0 12.8 %collective-permute-start.47 = (bf16[2,2,3,16,704]{4,3,2,1,0:T(8,128)(2,1)S(1)}, bf16[2,2,3,16,704]{4,3,2,1,0:T(8,128)(2,1)S(1)}, u32[]{:S(2)}, u32[]{:S(2)}) collective-permute-start(bf16[2,2,3,16,704]{4,3,2,1,0:T(8,128)(2,1)S(1)} %get-tuple-element.226), channel_id=1, source_target_pairs={{0,48},{1,17},{2,50},{3,19},{4,52},{5,21},{6,54},{7,23},{8,56},{9,... | collective-permute-start | bytes 811016 | tf_op jit(solution)/shard_map/ppermute | solution.py:45
  393.3 20.6 %collective-permute-start.42 = (bf16[2,2,3,16,704]{4,3,2,1,0:T(8,128)(2,1)S(1)}, bf16[2,2,3,16,704]{4,3,2,1,0:T(8,128)(2,1)S(1)}, u32[]{:S(2)}, u32[]{:S(2)}) collective-permute-start(bf16[2,2,3,16,704]{4,3,2,1,0:T(8,128)(2,1)S(1)} %get-tuple-element.227), channel_id=1, source_target_pairs={{0,64},{1,65},{2,66},{3,67},{4,68},{5,69},{6,70},{7,71},{8,72},{9,... | collective-permute-start | bytes 811016 | tf_op jit(solution)/shard_map/ppermute | solution.py:45
  394.3 19.6 %collective-permute-start.44 = (bf16[2,2,3,16,704]{4,3,2,1,0:T(8,128)(2,1)S(1)}, bf16[2,2,3,16,704]{4,3,2,1,0:T(8,128)(2,1)S(1)}, u32[]{:S(2)}, u32[]{:S(2)}) collective-permute-start(bf16[2,2,3,16,704]{4,3,2,1,0:T(8,128)(2,1)S(1)} %get-tuple-element.228), channel_id=1, source_target_pairs={{0,8},{1,73},{2,10},{3,75},{4,12},{5,77},{6,14},{7,79},{8,64},{9,1... | collective-permute-start | bytes 811016 | tf_op jit(solution)/shard_map/ppermute | solution.py:45
  397.8 16.1 %collective-permute-start.43 = (bf16[2,2,3,16,704]{4,3,2,1,0:T(8,128)(2,1)S(1)}, bf16[2,2,3,16,704]{4,3,2,1,0:T(8,128)(2,1)S(1)}, u32[]{:S(2)}, u32[]{:S(2)}) collective-permute-start(bf16[2,2,3,16,704]{4,3,2,1,0:T(8,128)(2,1)S(1)} %get-tuple-element.229), channel_id=1, source_target_pairs={{0,72},{1,9},{2,74},{3,11},{4,76},{5,13},{6,78},{7,15},{8,0},{9,65... | collective-permute-start | bytes 811016 | tf_op jit(solution)/shard_map/ppermute | solution.py:45
  428.0 15.5 %collective-permute-start.54 = (bf16[4,4,2,16,576]{4,3,2,1,0:T(8,128)(2,1)}, bf16[4,4,2,16,576]{4,3,2,1,0:T(8,128)(2,1)S(1)}, u32[]{:S(2)}, u32[]{:S(2)}) collective-permute-start(bf16[4,4,2,16,576]{4,3,2,1,0:T(8,128)(2,1)} %get-tuple-element.202), channel_id=1, source_target_pairs={{0,16},{1,49},{2,18},{3,51},{4,20},{5,53},{6,22},{7,55},{8,24},{9,... | collective-permute-start | bytes 1769480 | tf_op jit(solution)/shard_map/ppermute | solution.py:45
  432.2 14.7 %collective-permute-start.49 = (bf16[4,4,2,16,576]{4,3,2,1,0:T(8,128)(2,1)S(1)}, bf16[4,4,2,16,576]{4,3,2,1,0:T(8,128)(2,1)S(1)}, u32[]{:S(2)}, u32[]{:S(2)}) collective-permute-start(bf16[4,4,2,16,576]{4,3,2,1,0:T(8,128)(2,1)S(1)} %copy-done.86), channel_id=1, source_target_pairs={{0,48},{1,17},{2,50},{3,19},{4,52},{5,21},{6,54},{7,23},{8,56},{9,... | collective-permute-start | bytes 1769480 | tf_op jit(solution)/shard_map/ppermute | solution.py:45
  443.7 11.9 %collective-permute-start.55 = (bf16[4,4,2,16,576]{4,3,2,1,0:T(8,128)(2,1)S(1)}, bf16[4,4,2,16,576]{4,3,2,1,0:T(8,128)(2,1)S(1)}, u32[]{:S(2)}, u32[]{:S(2)}) collective-permute-start(bf16[4,4,2,16,576]{4,3,2,1,0:T(8,128)(2,1)S(1)} %add_convert_fusion.3), channel_id=1, source_target_pairs={{0,16},{1,49},{2,18},{3,51},{4,20},{5,53},{6,22},{7,55},{8,24},{9,... | collective-permute-start | bytes 1769480 | tf_op jit(solution)/shard_map/ppermute | solution.py:45
  443.9 16.1 %collective-permute-start.59 = (bf16[2,4,3,16,704]{4,3,2,1,0:T(8,128)(2,1)S(1)}, bf16[2,4,3,16,704]{4,3,2,1,0:T(8,128)(2,1)}, u32[]{:S(2)}, u32[]{:S(2)}) collective-permute-start(bf16[2,4,3,16,704]{4,3,2,1,0:T(8,128)(2,1)S(1)} %get-tuple-element.242), channel_id=1, source_target_pairs={{0,64},{1,65},{2,66},{3,67},{4,68},{5,69},{6,70},{7,71},{8,72},{9,... | collective-permute-start | bytes 1622024 | tf_op jit(solution)/shard_map/ppermute | solution.py:45
  461.2 62.6 %collective-permute-start.73 = (bf16[2,2,4,3,16,704]{5,4,3,2,1,0:T(8,128)(2,1)S(1)}, bf16[2,2,4,3,16,704]{5,4,3,2,1,0:T(8,128)(2,1)S(1)}, u32[]{:S(2)}, u32[]{:S(2)}) collective-permute-start(bf16[2,2,4,3,16,704]{5,4,3,2,1,0:T(8,128)(2,1)S(1)} %pad_maximum_fusion.1.refs_0_), channel_id=1, source_target_pairs={{0,48},{1,17},{2,50},{3,19},{4,52},{5,21},{6,54},{7,23},{8,56},{9,... | collective-permute-start | bytes 3244040 | tf_op jit(solution)/shard_map/ppermute | solution.py:45
  461.4 25.3 %collective-permute-start.72 = (bf16[2,2,4,3,16,704]{5,4,3,2,1,0:T(8,128)(2,1)S(1)}, bf16[2,2,4,3,16,704]{5,4,3,2,1,0:T(8,128)(2,1)}, u32[]{:S(2)}, u32[]{:S(2)}) collective-permute-start(bf16[2,2,4,3,16,704]{5,4,3,2,1,0:T(8,128)(2,1)S(1)} %pad_maximum_fusion.1.refs_0_), channel_id=1, source_target_pairs={{0,16},{1,49},{2,18},{3,51},{4,20},{5,53},{6,22},{7,55},{8,24},{9,... | collective-permute-start | bytes 3244040 | tf_op jit(solution)/shard_map/ppermute | solution.py:45
  479.8 25.0 %collective-permute-start.65 = (bf16[2,4,16,576]{3,2,1,0:T(8,128)(2,1)S(1)}, bf16[2,4,16,576]{3,2,1,0:T(8,128)(2,1)S(1)}, u32[]{:S(2)}, u32[]{:S(2)}) collective-permute-start(bf16[2,4,16,576]{3,2,1,0:T(8,128)(2,1)S(1)} %get-tuple-element.256), channel_id=1, source_target_pairs={{0,64},{1,65},{2,66},{3,67},{4,68},{5,69},{6,70},{7,71},{8,72},{9,... | collective-permute-start | bytes 442376 | tf_op jit(solution)/shard_map/ppermute | solution.py:45
  486.7 37.1 %collective-permute-start.74 = (bf16[2,2,4,3,16,704]{5,4,3,2,1,0:T(8,128)(2,1)}, bf16[2,2,4,3,16,704]{5,4,3,2,1,0:T(8,128)(2,1)S(1)}, u32[]{:S(2)}, u32[]{:S(2)}) collective-permute-start(bf16[2,2,4,3,16,704]{5,4,3,2,1,0:T(8,128)(2,1)} %collective-permute-done.72.refs_1_), channel_id=1, source_target_pairs={{0,16},{1,49},{2,18},{3,51},{4,20},{5,53},{6,22},{7,55},{8,24},{9,... | collective-permute-start | bytes 3244040 | tf_op jit(solution)/shard_map/ppermute | solution.py:45
  486.8 17.9 %collective-permute-start.67 = (f32[2,2048]{1,0:T(2,128)S(1)}, f32[2,2048]{1,0:T(2,128)S(1)}, u32[]{:S(2)}, u32[]{:S(2)}) collective-permute-start(f32[2,2048]{1,0:T(2,128)S(1)} %slice_add_fusion.1), channel_id=1, source_target_pairs={{0,32},{1,33},{2,34},{3,35},{4,36},{5,37},{6,38},{7,39},{8,40},{9,... | collective-permute-start | bytes 49160 | tf_op jit(solution)/shard_map/ppermute | solution.py:45
  504.9 12.3 %collective-permute-start.71 = (bf16[2,2,4,16,576]{4,3,2,1,0:T(8,128)(2,1)S(1)}, bf16[2,2,4,16,576]{4,3,2,1,0:T(8,128)(2,1)S(1)}, u32[]{:S(2)}, u32[]{:S(2)}) collective-permute-start(bf16[2,2,4,16,576]{4,3,2,1,0:T(8,128)(2,1)S(1)} %pad_maximum_fusion.7.refs_0_), channel_id=1, source_target_pairs={{0,32},{1,33},{2,34},{3,35},{4,36},{5,37},{6,38},{7,39},{8,40},{9,... | collective-permute-start | bytes 884744 | tf_op jit(solution)/shard_map/ppermute | solution.py:45
  505.2 13.9 %collective-permute-start.70 = (bf16[2,2,4,16,576]{4,3,2,1,0:T(8,128)(2,1)S(1)}, bf16[2,2,4,16,576]{4,3,2,1,0:T(8,128)(2,1)S(1)}, u32[]{:S(2)}, u32[]{:S(2)}) collective-permute-start(bf16[2,2,4,16,576]{4,3,2,1,0:T(8,128)(2,1)S(1)} %pad_maximum_fusion.7.refs_0_), channel_id=1, source_target_pairs={{0,48},{1,17},{2,50},{3,19},{4,52},{5,21},{6,54},{7,23},{8,56},{9,... | collective-permute-start | bytes 884744 | tf_op jit(solution)/shard_map/ppermute | solution.py:45
  (123 other events, 1539.8 us)
Sparse Core Ops, SparseCore 0:
  44.4 31.9 all-gather.6
  78.7 52.3 all-gather.10
  132.8 55.1 all-gather.8
  296.6 53.4 reduce-scatter.5
  352.4 37.9 reduce-scatter.3
  392.5 31.3 all-gather.12
  426.3 41.4 reduce-scatter.7

commit v7 on v6

--- a/solution.py
+++ b/solution.py
@@ -153,14 +153,39 @@
     return pl.ds(pl.multiple_of(start, 16), count)
 
 
-def pack_kernel(spots, core, gate_ref, up_ref, down_ref, q_ref, k_ref, v_ref, mine_ref, other_ref, turned):
+def pack_attn_kernel(spots, core, q_ref, k_ref, v_ref, mine_ref, other_ref):
     first = core[0] == 0
-    turned[...] = down_ref[...].astype(F32).T
     keys = [k_ref[:, HEAD * h : HEAD * (h + 1)].astype(F32) for h in range(KV_HEADS)]
     vals = [v_ref[:, HEAD * h : HEAD * (h + 1)].astype(F32) for h in range(KV_HEADS)]
     for r in range(4):
         chip = spots[1 + r]
-        at = pl.ds(pl.multiple_of(chip * 2 * WIDE, 128), 2 * WIDE)
+        both = q_ref[:, pl.ds(pl.multiple_of(chip * 2 * QUERY, 128), 2 * QUERY)].astype(F32)
+        key, val = keys[0], vals[0]
+        for h in range(1, KV_HEADS):
+            key = jnp.where(chip == h, keys[h], key)
+            val = jnp.where(chip == h, vals[h], val)
+        low = jnp.concatenate([both[:, :QUERY], key], axis=1)
+        high = jnp.concatenate([both[:, QUERY:], val], axis=1)
+        mine_ref[r] = jnp.where(first, low, high).astype(BF)
+        other_ref[r] = jnp.where(first, high, low).astype(BF)
+
+
+def pack_attn(spots, core, q, k, v):
+    rows = lambda i, spots, core: (spots[0], 0)
+    whole = lambda i, *_: (0, 0, 0)
+    shape = (4, 32, QKV)
+    return call(
+        pack_attn_kernel, (spots, core), (1,),
+        [pl.BlockSpec((32, w.shape[1]), rows) for w in (q, k, v)],
+        [pl.BlockSpec(shape, whole)] * 2, [sds(shape)] * 2, [], 1, (q, k, v),
+    )
+
+
+def pack_mlp_kernel(spots, core, gate_ref, up_ref, down_ref, mine_ref, other_ref, turned):
+    first = core[0] == 0
+    turned[...] = down_ref[...].astype(F32).T
+    for r in range(4):
+        at = pl.ds(pl.multiple_of(spots[1 + r] * 2 * WIDE, 128), 2 * WIDE)
         parts = (
             gate_ref[:, at].astype(F32),
             up_ref[:, at].astype(F32),
@@ -170,50 +195,50 @@
             low, high = both[:, :WIDE], both[:, WIDE:]
             mine_ref[r, m] = jnp.where(first, low, high).astype(BF)
             other_ref[r, m] = jnp.where(first, high, low).astype(BF)
-        both = q_ref[:, pl.ds(pl.multiple_of(chip * 2 * QUERY, 128), 2 * QUERY)].astype(F32)
-        key, val = keys[0], vals[0]
-        for h in range(1, KV_HEADS):
-            key = jnp.where(chip == h, keys[h], key)
-            val = jnp.where(chip == h, vals[h], val)
-        rest = jnp.zeros((32, WIDE - QKV), F32)
-        low = jnp.concatenate([both[:, :QUERY], key, rest], axis=1)
-        high = jnp.concatenate([both[:, QUERY:], val, rest], axis=1)
-        mine_ref[r, 3] = jnp.where(first, low, high).astype(BF)
-        other_ref[r, 3] = jnp.where(first, high, low).astype(BF)
-
-
-def pack(spots, core, gate, up, down, q, k, v):
+
+
+def pack_mlp(spots, core, gate, up, down):
     rows = lambda i, spots, core: (spots[0], 0)
     whole = lambda i, *_: (0, 0, 0, 0)
-    shape = (4, 4, 32, WIDE)
-    specs = [pl.BlockSpec((32, w.shape[1]), rows) for w in (gate, up, down, q, k, v)]
-    specs[2] = pl.BlockSpec((FF, 128), lambda i, *_: (0, 0))
+    shape = (4, 3, 32, WIDE)
     return call(
-        pack_kernel, (spots, core), (1,), specs, [pl.BlockSpec(shape, whole)] * 2, [sds(shape)] * 2,
-        [pltpu.VMEM((128, FF), F32)], 4, (gate, up, down, q, k, v),
-    )
-
-
-def place_attn_kernel(slot, xs, halves, own_ref, other_ref, qkv_ref, out_ref):
+        pack_mlp_kernel, (spots, core), (1,),
+        [pl.BlockSpec((32, FF), rows), pl.BlockSpec((32, FF), rows), pl.BlockSpec((FF, 128), lambda i, *_: (0, 0))],
+        [pl.BlockSpec(shape, whole)] * 2, [sds(shape)] * 2, [pltpu.VMEM((128, FF), F32)],
+        3, (gate, up, down),
+    )
+
+
+def place_qkv_kernel(slot, xs, halves, own_ref, other_ref, out_ref):
     for e, ref in enumerate((own_ref, other_ref)):
         for r in range(4):
-            piece = ref[r, 0]
-            rows = at_rows(xs[r] * 32, 32)
-            out_ref[halves[e], rows, :] = piece[:, :QUERY]
-            qkv_ref[halves[e], 0, rows, :] = piece[:, QUERY:]
-
-
-def place_attn(slot, xs, halves, own, other):
-    qkv, out = call(
-        place_attn_kernel, (slot, xs, halves), (8,),
-        [pl.BlockSpec((4, 1, 32, PACK), lambda i, *_: (0, i, 0, 0))] * 2,
-        [
-            pl.BlockSpec((2, 1, 128, QKV), lambda i, slot, *_: (0, slot[i], 0, 0)),
-            pl.BlockSpec((2, 128, QUERY), lambda i, *_: (0, 0, i)),
-        ],
-        [sds((2, 8, 128, QKV)), sds((2, 128, D))], [], 2, (own, other),
-    )
-    return qkv.reshape(D, QKV), out.reshape(QUERY, D)
+            out_ref[halves[e], 0, at_rows(xs[r] * 32, 32), :] = ref[r, 0]
+
+
+def place_qkv(slot, xs, halves, own, other):
+    out = call(
+        place_qkv_kernel, (slot, xs, halves), (8,),
+        [pl.BlockSpec((4, 1, 32, QKV), lambda i, *_: (0, i, 0, 0))] * 2,
+        pl.BlockSpec((2, 1, 128, QKV), lambda i, slot, *_: (0, slot[i], 0, 0)),
+        sds((2, 8, 128, QKV)), [], 2, (own, other),
+    )
+    return out.reshape(D, QKV)
+
+
+def place_out_kernel(xs, halves, own_ref, other_ref, out_ref):
+    for e, ref in enumerate((own_ref, other_ref)):
+        for r in range(4):
+            out_ref[halves[e], at_rows(xs[r] * 32, 32), :] = ref[r, 0]
+
+
+def place_out(xs, halves, own, other):
+    out = call(
+        place_out_kernel, (xs, halves), (8,),
+        [pl.BlockSpec((4, 1, 32, QUERY), lambda i, *_: (0, i, 0, 0))] * 2,
+        pl.BlockSpec((2, 128, QUERY), lambda i, *_: (0, 0, i)),
+        sds((2, 128, D)), [], 2, (own, other),
+    )
+    return out.reshape(QUERY, D)
 
 
 def place_mlp_kernel(slot, halves, own_ref, other_ref, out_ref):
@@ -767,33 +792,40 @@
     scale_attn = rms_scale(rows_in)
 
 
-    def exchange(mine, other):
+    def exchange(mine, other, axis, *first):
         got = swap(other)
-        own = jnp.stack([mine[0], got[0]], axis=1)
-        before = jnp.stack([mine[1], got[2]], axis=1)
-        forward = jnp.stack([mine[2], got[1]], axis=1)
-        far = jnp.stack([mine[3], got[3]], axis=1)
-        return jnp.concatenate(exchange_z(own, before, forward, far), axis=1)
+        own = jnp.stack([mine[0], got[0]], axis)
+        before = jnp.stack([mine[1], got[2]], axis)
+        forward = jnp.stack([mine[2], got[1]], axis)
+        far = jnp.stack([mine[3], got[3]], axis)
+        return jnp.concatenate(after(exchange_z(own, before, forward, far), first), axis)
+
+    def spread(part):
+        half_rows = jnp.stack(ring_gather(part, "x"))
+        return half_rows, step(half_rows, "y", 1)
 
     normed_own = (rows_in * scale_attn * gain_one).astype(BF)
+    attn_part = exchange(*pack_attn(spots, core, query_weight, key_weight, value_weight), 0)
+    normed_attn = lax.all_gather(
+        after(normed_own, attn_part), "blk", axis=0, tiled=True, axis_index_groups=ZC_GROUPS
+    )
+    qkv_rows = spread(attn_part)
+    w_qkv = place_qkv(slot, xs, halves, *qkv_rows)
+
+    mlp_mine, mlp_other = pack_mlp(after(spots, attn_part), core, gate_weight, up_weight, down_weight)
+    mlp_half_rows = lax.all_gather(
+        exchange(mlp_mine, mlp_other, 1, qkv_rows[1]), "batch", axis=0, axis_index_groups=X_GROUPS
+    )
+
     out_rows = lax.dynamic_slice_in_dim(output_weight, x * 32, 32, axis=0)
     out_part = send(
         out_rows.reshape(32, 8, QUERY).transpose(1, 0, 2),
         lambda yh, x, yl, z, c: (yh, x, c, 2 * yl + z // 2, z % 2),
     )
-    packs = exchange(
-        *pack(spots, core, gate_weight, up_weight, down_weight, query_weight, key_weight, value_weight)
-    )
-    normed_attn = lax.all_gather(
-        after(normed_own, packs), "blk", axis=0, tiled=True, axis_index_groups=ZC_GROUPS
-    )
-    attn_part = jnp.concatenate([out_part, packs[3, :, :, :QKV]], axis=-1)
-    attn_half_rows = jnp.stack(ring_gather(attn_part, "x"))
-    attn_other_rows = step(attn_half_rows, "y", 1)
-    w_qkv, w_out = place_attn(slot, xs, halves, attn_half_rows, attn_other_rows)
-    mlp_half_rows = lax.all_gather(packs[:3], "batch", axis=0, axis_index_groups=X_GROUPS)
+    w_out = place_out(xs, halves, *spread(after(out_part, qkv_rows[0])))
+
     grad_rows = lax.all_gather(
-        after(cotangent[0], attn_other_rows), "blk", axis=0, tiled=True, axis_index_groups=ZC_GROUPS
+        after(cotangent[0], qkv_rows[1]), "blk", axis=0, tiled=True, axis_index_groups=ZC_GROUPS
     )
 
 
@@ -845,10 +877,10 @@
         at = after(chunk, swapped)
     hidden, gate_grad_rows, up_grad_rows, branch = kept
     mlp_outs = mlp_grads(
-        column, xs, yhs, core, after(at, got[1], sums[2], sums[3]), mlp_parts, grad_rows, gate_grad_rows, up_grad_rows, hidden
+        column, xs, yhs, core, after(at, *sums[1:]), mlp_parts, grad_rows, gate_grad_rows, up_grad_rows, hidden
     )
     normed_grad = add(sums[0], *got[1:])
-    mlp_outs = after(mlp_outs, got[2], got[3])
+    mlp_outs = after(mlp_outs, *got[1:])
     mlp_low = lax.psum_scatter(mlp_outs[0], "batch", scatter_dimension=0, axis_index_groups=X_GROUPS)
     branch = lax.psum_scatter(after(branch, mlp_outs), "blk", scatter_dimension=0, axis_index_groups=ZC_GROUPS)
     high_far = step(mlp_outs[2], "y", 1)
@@ -879,7 +911,7 @@
     branch_parts += [third, swap(after(third, rows_1))]
     rows_2, kv_keep, kv_give = back(6, after(branch_parts[6:], high_after), sums, True)
     query_grad_rows = [rows_0, rows_1, rows_2]
-    kv_terms = add(kv_keep, swap(kv_give))
+    kv_terms = add(after(kv_keep, high_before), swap(kv_give))
     half_rows = 8 * TOK
     kv_half = to_half(kv_terms[half_rows:].astype(BF))
     kv_grad_rows = add(kv_terms[:half_rows], kv_half).astype(BF)
@@ -887,8 +919,7 @@
     high = ring_scatter(high[0], high[1], high[2], high[3], "x").astype(BF)
     mlp_low = after(mlp_low, rows_2)
     low = ring_scatter(mlp_low[0], mlp_low[2], mlp_low[3], mlp_low[1], "y").astype(BF)
-    mlp_sums, mlp_swapped = resplit_back([low[0], low[1], high[0], high[1]])
-    kv_grad_rows = after(kv_grad_rows, mlp_low)
+    kv_grad_rows = after(kv_grad_rows, mlp_low, high)
 
     attn_partial, attn_gain_part = project_back(chunk, query_grad_rows, kv_grad_rows, w_qkv, normed_attn)
     gain_grads = jnp.stack([attn_gain_part / gain_one, mlp_gain_part])
@@ -896,7 +927,9 @@
     attn_outs = attn_grads(
         column, xs, yhs, core, halves, chunk, normed_attn, branch_parts, attended, query_grad_rows, kv_grad_rows
     )
-    attn_partial, attn_outs = after((attn_partial, attn_outs), low, high)
+    low, high = after((low, high), attn_outs[0], branch)
+    mlp_sums, mlp_swapped = resplit_back([low[0], low[1], high[0], high[1]])
+    attn_partial = after(attn_partial, attn_outs[0])
     normed_attn_grad = lax.psum_scatter(attn_partial, "blk", scatter_dimension=0, axis_index_groups=ZC_GROUPS)
 
     layer_out = (residual + after(branch, attn_outs[0]).astype(F32)).astype(BF)[None]
@@ -915,14 +948,15 @@
     qkv_sums, _ = resplit_back(attn_sums[..., QUERY:])
     attn_sums = jnp.concatenate([out_sums.reshape(2, 4, 16, QUERY), qkv_sums], axis=-1)
     attn_across = across(attn_sums, "y")
-    gain_grads = gain_grads + across(gain_grads, "x")
-    gain_grads = gain_grads + step(gain_grads, "x", 1)
     attn_sums = ring_gather(jnp.stack([attn_sums, attn_across]), "x")
-    gate_grad, up_grad, down_grad = finish_mlp(spots, xs, yhs, core, mlp_sums)
-    query_grad, key_grad, value_grad, output_grad = finish_attn(spots, xs, yhs, core, attn_sums)
     tokens_grad = (
         residual_grad + norm_back(rows_in, scale_attn, gain_one, after(normed_attn_grad, attn_across).astype(F32))
     ).astype(BF)[None]
+    gain_grads = after(gain_grads, *attn_sums[1:])
+    gain_grads = gain_grads + across(gain_grads, "x")
+    gain_grads = gain_grads + step(gain_grads, "x", 1)
+    gate_grad, up_grad, down_grad = finish_mlp(spots, xs, yhs, core, mlp_sums)
+    query_grad, key_grad, value_grad, output_grad = finish_attn(after(spots, tokens_grad), xs, yhs, core, attn_sums)
     return (
         layer_out,
         tokens_grad,

time: 546 us -> 547 us (level)
  waiting for transfers between devices: 208 us -> 198 us
  local copies, waits for them, and re-layouts: 28.3 us -> 34.5 us
    ppermute x75 -> x83, waiting for transfers between devices: 199 us -> 187 us  [send(): return lax.ppermute(value, BOTH, pairs)]
    unnamed x182 -> x181, local copies, waits for them, and re-layouts: 23.1 us -> 28.2 us
    ppermute x75 -> x83, starting transfers between devices: 99.3 us -> 104 us  [send(): return lax.ppermute(value, BOTH, pairs)]
    pallas_call x18 -> x20, Pallas kernels: 158 us -> 158 us  [call(): pl.pallas_call(body, grid_spec=pltpu.PrefetchScalarGridSpec(num_scalar_pr...]
  transfers between devices with their start and end apart: 82 -> 90, of which waited for: 46 -> 43; matrix products, arithmetic and copies ran while one was open for 6% -> 6% of each run, Pallas kernels for 25% -> 25%
where the time goes in v7:
time: 547 us; the launch traced here: 540 us
  waiting for transfers between devices  198 us (36%)
  Pallas kernels  158 us (29%)
  starting transfers between devices  104 us (19%)
  local copies, waits for them, and re-layouts  34.5 us (6%)
  other arithmetic  29.4 us (5%)
  between operations  15.8 us (3%)
    ppermute x83, waiting for transfers between devices, send(): return lax.ppermute(value, BOTH, pairs)  187 us
    pallas_call x20, Pallas kernels, call(): pl.pallas_call(body, grid_spec=pltpu.PrefetchScalarGridSpec(num_scalar_pr...  158 us
    ppermute x83, starting transfers between devices, send(): return lax.ppermute(value, BOTH, pairs)  104 us
    unnamed x181, local copies, waits for them, and re-layouts  28.2 us
  transfers between devices with their start and end apart: 90, of which 43 were waited for; matrix products, arithmetic and copies ran while one was open for 6% of the time, Pallas kernels for 25%

profile of v7, /device:TPU:24, one launch (start us, length us, event | category | flops | bytes accessed | tf_op | source)
XLA Modules:
  0.0 540.1 jit_solution(16369714915572616003)
XLA Ops:
  22.1 3.7 collective-permute-done.3
  37.2 4.3 collective-permute-done.6
  41.5 3.9 collective-permute-done.5
  51.1 13.0 %collective-permute-done.25 = bf16[3,2,32,704]{3,2,0,1:T(8,128)(2,1)S(1)} collective-permute-done((bf16[3,2,32,704]{3,2,0,1:T(8,128)(2,1)S(1)}, bf16[3,2,32,704]{3,2,0,1:T(8,128)(2,1)S(1)}, u32[]{:S(2)}, u32[]{:S(2)}) %collective-permute-start.25) | collective-permute-done | bytes 270368 | tf_op jit(solution)/shard_map/ppermute | solution.py:45
  64.1 8.3 %collective-permute-done.27 = bf16[3,2,32,704]{3,2,0,1:T(8,128)(2,1)S(1)} collective-permute-done((bf16[3,2,32,704]{3,2,0,1:T(8,128)(2,1)S(1)}, bf16[3,2,32,704]{3,2,0,1:T(8,128)(2,1)S(1)}, u32[]{:S(2)}, u32[]{:S(2)}) %collective-permute-start.27) | collective-permute-done | bytes 270368 | tf_op jit(solution)/shard_map/ppermute | solution.py:45
  76.8 3.2 collective-permute-done.10
  86.8 6.1 %shard_map.214 = (bf16[1024,256]{1,0:T(8,128)(2,1)S(1)}, bf16[2,1024,64]{2,1,0:T(8,128)(2,1)S(1)}) custom-call(s32[8]{0:T(128)S(1)} %stack.242.chunk.nat, bf16[1024,2048]{1,0:T(8,128)(2,1)} %all-gather.7.cloned.1.call-done.refs_0_.refs_1_.refs_2_.refs_3_.refs_4_.refs_5_.refs_6_.refs_7_, ...), custom_call_target="tpu_custom_call" | custom-call | flops 1000 | bytes 1500000 | tf_op jit(solution)/shard_map/pallas_call | solution.py:136
  96.3 5.5 %collective-permute-done.8 = bf16[2,1024,64]{1,2,0:T(8,128)(2,1)S(1)} collective-permute-done((bf16[2,1024,64]{1,2,0:T(8,128)(2,1)S(1)}, bf16[2,1024,64]{1,2,0:T(8,128)(2,1)S(1)}, u32[]{:S(2)}, u32[]{:S(2)}) %collective-permute-start.8) | collective-permute-done | bytes 262176 | tf_op jit(solution)/shard_map/ppermute | solution.py:45
  103.0 4.4 collective-permute-done.14.other_ref
  110.9 6.2 %shard_map.216 = (bf16[256,256]{1,0:T(8,128)(2,1)S(1)}, bf16[128,2048]{1,0:T(8,128)(2,1)S(1)}, bf16[128,2048]{1,0:T(8,128)(2,1)}) custom-call(s32[8]{0:T(128)S(1)} %bitcast.203, s32[16]{0:T(128)S(1)} %select_reduce_fusion.1.key_slot, bf16[1024,256]{1,0:T(8,128)(2,1)S(1)} %get-tuple-element.131.q_ref.refs_0_, ...), custom_call_target="tpu_custom_call" | custom-call | flops 1000 | bytes 1800000 | tf_op jit(solution)/shard_map/pallas_call | solution.py:136
  117.7 10.7 %all-gather.11.cloned.1.call-done = bf16[12,8,32,704]{3,2,0,1:T(8,128)(2,1)} async-done(((bf16[3,8,32,704]{3,2,0,1:T(8,128)(2,1)}), bf16[12,8,32,704]{3,2,0,1:T(8,128)(2,1)}) %all-gather.11.cloned.1.call-update) | async-done | bytes 4325392 | tf_op jit(solution)/shard_map/all_gather | solution.py:816
  131.2 5.6 %shard_map.218 = (bf16[256,256]{1,0:T(8,128)(2,1)S(1)}, bf16[128,2048]{1,0:T(8,128)(2,1)S(1)}, bf16[128,2048]{1,0:T(8,128)(2,1)S(1)}) custom-call(s32[8]{0:T(128)S(1)} %bitcast.204, s32[16]{0:T(128)S(1)} %select_reduce_fusion.1.key_slot, bf16[1024,256]{1,0:T(8,128)(2,1)S(1)} %get-tuple-element.131.q_ref.refs_0_, ...), custom_call_target="tpu_custom_call" | custom-call | flops 1000 | bytes 1800000 | tf_op jit(solution)/shard_map/pallas_call | solution.py:136
  136.9 5.4 %shard_map.217 = (bf16[256,256]{1,0:T(8,128)(2,1)S(1)}, bf16[128,2048]{1,0:T(8,128)(2,1)S(1)}, bf16[128,2048]{1,0:T(8,128)(2,1)S(1)}) custom-call(s32[8]{0:T(128)S(1)} %bitcast.205, s32[16]{0:T(128)S(1)} %select_reduce_fusion.1.key_slot, bf16[1024,256]{1,0:T(8,128)(2,1)S(1)} %get-tuple-element.131.q_ref.refs_0_, ...), custom_call_target="tpu_custom_call" | custom-call | flops 1000 | bytes 1800000 | tf_op jit(solution)/shard_map/pallas_call | solution.py:136
  143.1 3.7 collective-permute-start.21
  151.5 5.3 shard_map.219
  157.0 13.6 %collective-permute-done.21 = bf16[128,2048]{1,0:T(8,128)(2,1)S(1)} collective-permute-done((bf16[128,2048]{1,0:T(8,128)(2,1)S(1)}, bf16[128,2048]{1,0:T(8,128)(2,1)S(1)}, u32[]{:S(2)}, u32[]{:S(2)}) %collective-permute-start.21) | collective-permute-done | bytes 524320 | tf_op jit(solution)/shard_map/ppermute | solution.py:45
  170.5 12.6 %collective-permute-done.20 = bf16[128,2048]{1,0:T(8,128)(2,1)S(1)} collective-permute-done((bf16[128,2048]{1,0:T(8,128)(2,1)S(1)}, bf16[128,2048]{1,0:T(8,128)(2,1)S(1)}, u32[]{:S(2)}, u32[]{:S(2)}) %collective-permute-start.20) | collective-permute-done | bytes 524320 | tf_op jit(solution)/shard_map/ppermute | solution.py:45
  185.5 8.4 %shard_map.221 = bf16[3,2,8,128,704]{4,3,2,1,0:T(8,128)(2,1)} custom-call(s32[8]{0:T(128)S(1)} %stack.254.slot, s32[2]{0:T(128)S(1)} %pad_add_fusion.2.halves, bf16[4,3,8,32,704]{4,3,2,1,0:T(8,128)(2,1)S(1)} %bitcast.197, bf16[4,3,8,32,704]{4,3,2,1,0:T(8,128)(2,1)} %collective-permute-done.28.other_ref), custom_call_target="tpu_custom_call" | custom-call | flops 1000 | bytes 1800000 | tf_op jit(solution)/shard_map/pallas_call | solution.py:136
  196.2 3.2 collective-permute-start.30
  199.4 18.7 %shard_map.222 = (bf16[1024,704]{1,0:T(8,128)(2,1)S(1)}, bf16[1024,704]{1,0:T(8,128)(2,1)}, bf16[1024,704]{1,0:T(8,128)(2,1)}, bf16[128,2048]{1,0:T(8,128)(2,1)S...) custom-call(s32[8]{0:T(128)S(1)} %stack.242.chunk.nat, ...), custom_call_target="tpu_custom_call" | custom-call | flops 1000 | bytes 5400000 | tf_op jit(solution)/shard_map/pallas_call | solution.py:136
  219.5 8.6 %collective-permute-start.34 = (bf16[128,2048]{1,0:T(8,128)(2,1)}, bf16[128,2048]{1,0:T(8,128)(2,1)S(1)}, u32[]{:S(2)}, u32[]{:S(2)}) collective-permute-start(bf16[128,2048]{1,0:T(8,128)(2,1)} %collective-permute-done.31.refs_2_.refs_6_), channel_id=1, source_target_pairs={{0,1},{1,0},{2,3},{3,2},{4,5},{5,4},{6,7},{7,6},{8,9},{9,8},{10,11... | collective-permute-start | bytes 1572872 | tf_op jit(solution)/shard_map/ppermute | solution.py:45
  230.2 18.6 %shard_map.223 = (bf16[1024,704]{1,0:T(8,128)(2,1)S(1)}, bf16[1024,704]{1,0:T(8,128)(2,1)}, bf16[1024,704]{1,0:T(8,128)(2,1)}, bf16[128,2048]{1,0:T(8,128)(2,1)S...) custom-call(s32[8]{0:T(128)S(1)} %stack.242.chunk.nat, ...), custom_call_target="tpu_custom_call", output_to_operand_aliasing={{0}: (10, {}), {1}: (11, {}), {2}: (12, {}), {6}: (13, {})} | custom-call | flops 1000 | bytes 5400000 | tf_op jit(solution)/shard_map/pallas_call | solution.py:136
  256.3 19.5 %shard_map.224 = (bf16[4,4,2,2,3,16,704]{6,5,4,3,2,1,0:T(8,128)(2,1)}, bf16[4,2,2,3,16,704]{5,4,3,2,1,0:T(8,128)(2,1)S(1)}, bf16[4,2,2,3,16,704]{5,4,3,2,1,0:T(8...) custom-call(s32[8]{0:T(128)S(1)} %stack.284.column, s32[4]{0:T(128)S(1)} %pad_add_fusion.1.xs, ...), custom_call_target="tpu_custom_call" | custom-call | flops 1000 | bytes 5100000 | tf_op jit(solution)/shard_map/pallas_call | solution.py:136
  279.8 3.1 multiply_reduce_fusion
  287.1 7.0 %shard_map.225 = (bf16[256,256]{1,0:T(8,128)(2,1)S(1)}, f32[2048,64]{1,0:T(8,128)S(1)}, f32[2048,64]{1,0:T(8,128)S(1)}) custom-call(s32[8]{0:T(128)S(1)} %bitcast.207, s32[16]{0:T(128)S(1)} %select_reduce_fusion.1.key_slot, s32[1]{0:T(128)} %bitcast.16.core, s32[16]{0:T(128)S(1)} %copy-done.58, bf16[1024,256]{1,0:T(8,128)(2,1)S(1)} %get-tuple-element.131.q_ref.refs_0_, ...), custom_call_target="tpu_custom_call" | custom-call | flops 1000 | bytes 2400000 | tf_op jit(solution)/shard_map/pallas_call | solution.py:136
  295.1 3.3 collective-permute-done.41.refs_3_.refs_12_
  302.1 3.3 collective-permute-start.48
  307.3 16.5 %shard_map.226 = (bf16[512,256]{1,0:T(8,128)(2,1)S(1)}, f32[2048,64]{1,0:T(8,128)S(1)}, f32[2048,64]{1,0:T(8,128)}) custom-call(s32[8]{0:T(128)S(1)} %bitcast.208, s32[16]{0:T(128)S(1)} %select_reduce_fusion.1.key_slot, s32[1]{0:T(128)} %bitcast.16.core, s32[16]{0:T(128)S(1)} %copy-done.58, bf16[1024,256]{1,0:T(8,128)(2,1)S(1)} %get-tuple-element.131.q_ref.refs_0_, ...), custom_call_target="tpu_custom_call" | custom-call | flops 1000 | bytes 4800000 | tf_op jit(solution)/shard_map/pallas_call | solution.py:136
  326.4 5.1 collective-permute-done.47
  331.5 9.1 %shard_map.227 = (bf16[256,256]{1,0:T(8,128)(2,1)S(1)}, bf16[2048,64]{1,0:T(8,128)(2,1)S(1)}, bf16[2048,64]{1,0:T(8,128)(2,1)S(1)}) custom-call(s32[8]{0:T(128)S(1)} %bitcast.209, s32[16]{0:T(128)S(1)} %select_reduce_fusion.1.key_slot, s32[1]{0:T(128)} %bitcast.16.core, s32[16]{0:T(128)S(1)} %copy-done.58, ...), custom_call_target="tpu_custom_call" | custom-call | flops 1000 | bytes 2400000 | tf_op jit(solution)/shard_map/pallas_call | solution.py:136
  341.4 5.0 collective-permute-start.51
  346.4 3.2 collective-permute-start.52
  349.9 4.4 collective-permute-done.51
  354.3 6.1 %collective-permute-done.53 = bf16[2,2,3,16,704]{4,3,2,1,0:T(8,128)(2,1)S(1)} collective-permute-done((bf16[2,2,3,16,704]{4,3,2,1,0:T(8,128)(2,1)S(1)}, bf16[2,2,3,16,704]{4,3,2,1,0:T(8,128)(2,1)S(1)}, u32[]{:S(2)}, u32[]{:S(2)}) %collective-permute-start.53) | collective-permute-done | bytes 270368 | tf_op jit(solution)/shard_map/ppermute | solution.py:45
  363.2 7.0 %shard_map.229 = (bf16[8,128,2048]{2,1,0:T(8,128)(2,1)}, f32[8,2048]{1,0:T(8,128)S(1)}) custom-call(s32[8]{0:T(128)S(1)} %stack.242.chunk.nat, bf16[256,256]{1,0:T(8,128)(2,1)S(1)} %get-tuple-element.185.refs_20_.dq0_ref, bf16[512,256]{1,0:T(8,128)(2,1)S(1)} %copy-done.31, bf16[256,256]{1,0:T(8,128)(2,1)S(1)} %copy-done.36, ...), custom_call_target="tpu_custom_call" | custom-call | flops 1000 | bytes 1500000 | tf_op jit(solution)/shard_map/pallas_call | solution.py:136
  382.5 10.2 %shard_map.228 = (bf16[4,4,2,16,576]{4,3,2,1,0:T(8,128)(2,1)S(1)}, bf16[4,4,2,16,576]{4,3,2,1,0:T(8,128)(2,1)}, bf16[4,4,2,16,576]{4,3,2,1,0:T(8,128)(2,1)}, bf16[4,4,2,16,576]{4,3,2,1,0:T(8,128)(2,1)}) custom-call(s32[8]{0:T(128)S(1)} %copy-done.62, s32[4]{0:T(128)S(1)} %pad_add_fusion.1.xs, s32[4]{0:T(128)S(1)} %copy-done.54, s32[1]{0:T(128)} %bitcast.16.core, ...), custom_call_target="tpu_custom_call" | custom-call | flops 1000 | bytes 3000000 | tf_op jit(solution)/shard_map/pallas_call | solution.py:136
  398.3 7.6 %collective-permute-done.55 = bf16[2,2,3,16,704]{4,3,2,1,0:T(8,128)(2,1)S(1)} collective-permute-done((bf16[2,2,3,16,704]{4,3,2,1,0:T(8,128)(2,1)S(1)}, bf16[2,2,3,16,704]{4,3,2,1,0:T(8,128)(2,1)S(1)}, u32[]{:S(2)}, u32[]{:S(2)}) %collective-permute-start.55) | collective-permute-done | bytes 270368 | tf_op jit(solution)/shard_map/ppermute | solution.py:45
  405.9 4.0 collective-permute-done.57
  415.0 5.7 %collective-permute-done.58 = bf16[2,3,16,704]{3,2,1,0:T(8,128)(2,1)S(1)} collective-permute-done((bf16[2,3,16,704]{3,2,1,0:T(8,128)(2,1)S(1)}, bf16[2,3,16,704]{3,2,1,0:T(8,128)(2,1)S(1)}, u32[]{:S(2)}, u32[]{:S(2)}) %collective-permute-start.58) | collective-permute-done | bytes 135200 | tf_op jit(solution)/shard_map/ppermute | solution.py:45
  420.7 3.7 collective-permute-done.59
  429.3 12.1 %collective-permute-done.54 = bf16[4,4,2,16,576]{4,3,2,1,0:T(8,128)(2,1)S(1)} collective-permute-done((bf16[4,4,2,16,576]{4,3,2,1,0:T(8,128)(2,1)S(1)}, bf16[4,4,2,16,576]{4,3,2,1,0:T(8,128)(2,1)S(1)}, u32[]{:S(2)}, u32[]{:S(2)}) %collective-permute-start.54) | collective-permute-done | bytes 589856 | tf_op jit(solution)/shard_map/ppermute | solution.py:45
  448.2 3.8 collective-permute-done.64
  458.0 3.4 collective-permute-start.68
  462.9 3.6 collective-permute-done.68
  478.1 7.7 %collective-permute-done.77.refs_3_ = bf16[2,2,4,16,576]{4,3,2,1,0:T(8,128)(2,1)S(1)} collective-permute-done((bf16[2,2,4,16,576]{4,3,2,1,0:T(8,128)(2,1)S(1)}, bf16[2,2,4,16,576]{4,3,2,1,0:T(8,128)(2,1)S(1)}, u32[]{:S(2)}, u32[]{:S(2)}) %collective-permute-start.77) | collective-permute-done | bytes 294944 | tf_op jit(solution)/shard_map/ppermute | solution.py:45
  485.7 23.9 %collective-permute-done.76.refs_2_ = bf16[2,2,4,16,576]{4,3,2,1,0:T(8,128)(2,1)S(1)} collective-permute-done((bf16[2,2,4,16,576]{4,3,2,1,0:T(8,128)(2,1)S(1)}, bf16[2,2,4,16,576]{4,3,2,1,0:T(8,128)(2,1)S(1)}, u32[]{:S(2)}, u32[]{:S(2)}) %collective-permute-start.76) | collective-permute-done | bytes 294944 | tf_op jit(solution)/shard_map/ppermute | solution.py:45
  511.5 3.5 collective-permute-done.78
  520.6 6.0 %shard_map.231 = (f32[128,5632]{1,0:T(8,128)}, f32[128,5632]{1,0:T(8,128)}, f32[5632,128]{1,0:T(8,128)}) custom-call(s32[5]{0:T(128)S(1)} %copy-done.56, s32[4]{0:T(128)S(1)} %pad_add_fusion.1.xs, s32[4]{0:T(128)S(1)} %copy-done.54, s32[1]{0:T(128)} %bitcast.16.core, bf16[2,2,4,3,16,704]{5,4,3,2,1,0:T(8,128)(2,1)S(1)} %pad_maximum_fusion.1.refs_0_, ...), custom_call_target="tpu_custom_call" | custom-call | flops 1000 | bytes 1500000 | tf_op jit(solution)/shard_map/pallas_call | solution.py:136
  (440 shorter events, 163.3 us)
Async XLA Ops:
  7.2 79.6 %all-gather.7.cloned.1.call-start = ((), (), s32[]{:S(2)}) async-start(), calls=%async_computation.3 | async-start | bytes 4718592 | tf_op jit(solution)/shard_map/all_gather | solution.py:809
  28.4 100.0 %all-gather.11.cloned.1.call-start = ((), (), s32[]{:S(2)}) async-start(), calls=%async_computation.8 | async-start | bytes 5898240 | tf_op jit(solution)/shard_map/all_gather | solution.py:816
  31.9 14.9 %collective-permute-start.24 = (bf16[4,3,32,704]{3,2,1,0:T(8,128)(2,1)S(1)}, bf16[4,3,32,704]{3,2,1,0:T(8,128)(2,1)S(1)}, u32[]{:S(2)}, u32[]{:S(2)}) collective-permute-start(bf16[4,3,32,704]{3,2,1,0:T(8,128)(2,1)S(1)} %get-tuple-element.145), channel_id=1, source_target_pairs={{0,1},{1,0},{2,3},{3,2},{4,5},{5,4},{6,7},{7,6},{8,9},{9,8},{10,11... | collective-permute-start | bytes 1622024 | tf_op jit(solution)/shard_map/ppermute | solution.py:45
  46.5 25.9 %collective-permute-start.7 = (bf16[4,8,32,320]{3,2,1,0:T(8,128)(2,1)S(1)}, bf16[4,8,32,320]{3,2,1,0:T(8,128)(2,1)S(1)}, u32[]{:S(2)}, u32[]{:S(2)}) collective-permute-start(bf16[4,8,32,320]{3,2,1,0:T(8,128)(2,1)S(1)} %pad_maximum_fusion.2.own_ref), channel_id=1, source_target_pairs={{0,8},{1,73},{2,10},{3,75},{4,12},{5,77},{6,14},{7,79},{8,64},{9,1... | collective-permute-start | bytes 1966088 | tf_op jit(solution)/shard_map/ppermute | solution.py:45
  46.9 17.2 %collective-permute-start.25 = (bf16[3,2,32,704]{3,2,0,1:T(8,128)(2,1)S(1)}, bf16[3,2,32,704]{3,2,0,1:T(8,128)(2,1)S(1)}, u32[]{:S(2)}, u32[]{:S(2)}) collective-permute-start(bf16[3,2,32,704]{3,2,0,1:T(8,128)(2,1)S(1)} %pad_maximum_fusion.7), channel_id=1, source_target_pairs={{0,2},{1,7},{2,4},{3,1},{4,6},{5,3},{6,0},{7,5},{8,10},{9,15},{10,... | collective-permute-start | bytes 811016 | tf_op jit(solution)/shard_map/ppermute | solution.py:45
  47.4 16.8 %collective-permute-start.26 = (bf16[3,2,32,704]{3,2,0,1:T(8,128)(2,1)S(1)}, bf16[3,2,32,704]{3,2,0,1:T(8,128)(2,1)S(1)}, u32[]{:S(2)}, u32[]{:S(2)}) collective-permute-start(bf16[3,2,32,704]{3,2,0,1:T(8,128)(2,1)S(1)} %pad_maximum_fusion.8), channel_id=1, source_target_pairs={{0,6},{1,3},{2,0},{3,5},{4,2},{5,7},{6,4},{7,1},{8,14},{9,11},{10,... | collective-permute-start | bytes 811016 | tf_op jit(solution)/shard_map/ppermute | solution.py:45
  50.3 22.1 %collective-permute-start.27 = (bf16[3,2,32,704]{3,2,0,1:T(8,128)(2,1)S(1)}, bf16[3,2,32,704]{3,2,0,1:T(8,128)(2,1)S(1)}, u32[]{:S(2)}, u32[]{:S(2)}) collective-permute-start(bf16[3,2,32,704]{3,2,0,1:T(8,128)(2,1)S(1)} %pad_maximum_fusion.9), channel_id=1, source_target_pairs={{0,4},{1,5},{2,6},{3,7},{4,0},{5,1},{6,2},{7,3},{8,12},{9,13},{10,... | collective-permute-start | bytes 811016 | tf_op jit(solution)/shard_map/ppermute | solution.py:45
  73.7 125.7 %all-gather.9.cloned.1.call-start = ((), (), s32[]{:S(2)}) async-start(), calls=%async_computation.4 | async-start | bytes 4718592 | tf_op jit(solution)/shard_map/all_gather | solution.py:827
  76.7 284.6 %reduce-scatter.6.cloned.1.call-start = ((), (), s32[]{:S(2)}) async-start(), calls=%async_computation.6 | async-start | bytes 5898240 | tf_op jit(solution)/shard_map/reduce_scatter | solution.py:884
  80.0 13.1 %collective-permute-start.13 = (bf16[8,32,256]{2,1,0:T(8,128)(2,1)S(1)}, bf16[8,32,256]{2,1,0:T(8,128)(2,1)}, u32[]{:S(2)}, u32[]{:S(2)}) collective-permute-start(bf16[8,32,256]{2,1,0:T(8,128)(2,1)S(1)} %collective-permute-done.10), channel_id=1, source_target_pairs={{0,32},{1,33},{2,34},{3,35},{4,36},{5,37},{6,38},{7,39},{8,40},{9,... | collective-permute-start | bytes 393224 | tf_op jit(solution)/shard_map/ppermute | solution.py:45
  95.3 12.2 %collective-permute-start.14 = (bf16[4,8,32,256]{3,2,1,0:T(8,128)(2,1)S(1)}, bf16[4,8,32,256]{3,2,1,0:T(8,128)(2,1)S(1)}, u32[]{:S(2)}, u32[]{:S(2)}) collective-permute-start(bf16[4,8,32,256]{3,2,1,0:T(8,128)(2,1)S(1)} %pad_maximum_fusion.4.own_ref), channel_id=1, source_target_pairs={{0,8},{1,73},{2,10},{3,75},{4,12},{5,77},{6,14},{7,79},{8,64},{9,1... | collective-permute-start | bytes 1572872 | tf_op jit(solution)/shard_map/ppermute | solution.py:45
  117.7 13.4 %collective-permute-start.15 = (bf16[128,2048]{1,0:T(8,128)(2,1)}, bf16[128,2048]{1,0:T(8,128)(2,1)}, u32[]{:S(2)}, u32[]{:S(2)}) collective-permute-start(bf16[128,2048]{1,0:T(8,128)(2,1)} %get-tuple-element.135), channel_id=1, source_target_pairs={{0,1},{1,0},{2,3},{3,2},{4,5},{5,4},{6,7},{7,6},{8,9},{9,8},{10,11... | collective-permute-start | bytes 1572872 | tf_op jit(solution)/shard_map/ppermute | solution.py:45
  131.1 54.4 %collective-permute-start.28 = (bf16[4,3,8,32,704]{4,3,2,1,0:T(8,128)(2,1)S(1)}, bf16[4,3,8,32,704]{4,3,2,1,0:T(8,128)(2,1)}, u32[]{:S(2)}, u32[]{:S(2)}) collective-permute-start(bf16[4,3,8,32,704]{4,3,2,1,0:T(8,128)(2,1)S(1)} %bitcast.196), channel_id=1, source_target_pairs={{0,8},{1,73},{2,10},{3,75},{4,12},{5,77},{6,14},{7,79},{8,64},{9,1... | collective-permute-start | bytes 12976136 | tf_op jit(solution)/shard_map/ppermute | solution.py:45
  143.1 27.5 %collective-permute-start.21 = (bf16[128,2048]{1,0:T(8,128)(2,1)S(1)}, bf16[128,2048]{1,0:T(8,128)(2,1)S(1)}, u32[]{:S(2)}, u32[]{:S(2)}) collective-permute-start(bf16[128,2048]{1,0:T(8,128)(2,1)S(1)} %add_convert_fusion.6), channel_id=1, source_target_pairs={{0,4},{1,5},{2,6},{3,7},{4,0},{5,1},{6,2},{7,3},{8,12},{9,13},{10,... | collective-permute-start | bytes 1572872 | tf_op jit(solution)/shard_map/ppermute | solution.py:45
  147.0 36.2 %collective-permute-start.20 = (bf16[128,2048]{1,0:T(8,128)(2,1)S(1)}, bf16[128,2048]{1,0:T(8,128)(2,1)S(1)}, u32[]{:S(2)}, u32[]{:S(2)}) collective-permute-start(bf16[128,2048]{1,0:T(8,128)(2,1)S(1)} %add_convert_fusion.7), channel_id=1, source_target_pairs={{0,2},{1,7},{2,4},{3,1},{4,6},{5,3},{6,0},{7,5},{8,10},{9,15},{10,... | collective-permute-start | bytes 1572872 | tf_op jit(solution)/shard_map/ppermute | solution.py:45
  149.3 33.9 %collective-permute-start.19 = (bf16[128,2048]{1,0:T(8,128)(2,1)S(1)}, bf16[128,2048]{1,0:T(8,128)(2,1)S(1)}, u32[]{:S(2)}, u32[]{:S(2)}) collective-permute-start(bf16[128,2048]{1,0:T(8,128)(2,1)S(1)} %add_convert_fusion.8), channel_id=1, source_target_pairs={{0,6},{1,3},{2,0},{3,5},{4,2},{5,7},{6,4},{7,1},{8,14},{9,11},{10,... | collective-permute-start | bytes 1572872 | tf_op jit(solution)/shard_map/ppermute | solution.py:45
  156.9 26.3 %collective-permute-start.18 = (bf16[128,2048]{1,0:T(8,128)(2,1)S(1)}, bf16[128,2048]{1,0:T(8,128)(2,1)S(1)}, u32[]{:S(2)}, u32[]{:S(2)}) collective-permute-start(bf16[128,2048]{1,0:T(8,128)(2,1)S(1)} %get-tuple-element.142), channel_id=1, source_target_pairs={{0,1},{1,0},{2,3},{3,2},{4,5},{5,4},{6,7},{7,6},{8,9},{9,8},{10,11... | collective-permute-start | bytes 1572872 | tf_op jit(solution)/shard_map/ppermute | solution.py:45
  185.5 13.9 %collective-permute-start.22 = (bf16[128,2048]{1,0:T(8,128)(2,1)S(1)}, bf16[128,2048]{1,0:T(8,128)(2,1)}, u32[]{:S(2)}, u32[]{:S(2)}) collective-permute-start(bf16[128,2048]{1,0:T(8,128)(2,1)S(1)} %multiply_convert_fusion.refs_0_), channel_id=1, source_target_pairs={{0,1},{1,0},{2,3},{3,2},{4,5},{5,4},{6,7},{7,6},{8,9},{9,8},{10,11... | collective-permute-start | bytes 1572872 | tf_op jit(solution)/shard_map/ppermute | solution.py:45
  194.5 24.4 %collective-permute-start.31 = (bf16[128,2048]{1,0:T(8,128)(2,1)S(1)}, bf16[128,2048]{1,0:T(8,128)(2,1)}, u32[]{:S(2)}, u32[]{:S(2)}) collective-permute-start(bf16[128,2048]{1,0:T(8,128)(2,1)S(1)} %multiply_convert_fusion.refs_0_), channel_id=1, source_target_pairs={{0,4},{1,5},{2,6},{3,7},{4,0},{5,1},{6,2},{7,3},{8,12},{9,13},{10,... | collective-permute-start | bytes 1572872 | tf_op jit(solution)/shard_map/ppermute | solution.py:45
  196.2 22.8 %collective-permute-start.30 = (bf16[128,2048]{1,0:T(8,128)(2,1)S(1)}, bf16[128,2048]{1,0:T(8,128)(2,1)}, u32[]{:S(2)}, u32[]{:S(2)}) collective-permute-start(bf16[128,2048]{1,0:T(8,128)(2,1)S(1)} %multiply_convert_fusion.refs_0_), channel_id=1, source_target_pairs={{0,6},{1,3},{2,0},{3,5},{4,2},{5,7},{6,4},{7,1},{8,14},{9,11},{10,... | collective-permute-start | bytes 1572872 | tf_op jit(solution)/shard_map/ppermute | solution.py:45
  250.2 26.6 %collective-permute-start.36 = (bf16[128,2048]{1,0:T(8,128)(2,1)}, bf16[128,2048]{1,0:T(8,128)(2,1)}, u32[]{:S(2)}, u32[]{:S(2)}) collective-permute-start(bf16[128,2048]{1,0:T(8,128)(2,1)} %fusion.11), channel_id=1, source_target_pairs={{0,6},{1,3},{2,0},{3,5},{4,2},{5,7},{6,4},{7,1},{8,14},{9,11},{10,... | collective-permute-start | bytes 1572872 | tf_op jit(solution)/shard_map/ppermute | solution.py:45
  252.9 23.9 %collective-permute-start.38 = (bf16[128,2048]{1,0:T(8,128)(2,1)}, bf16[128,2048]{1,0:T(8,128)(2,1)}, u32[]{:S(2)}, u32[]{:S(2)}) collective-permute-start(bf16[128,2048]{1,0:T(8,128)(2,1)} %get-tuple-element.252), channel_id=1, source_target_pairs={{0,4},{1,5},{2,6},{3,7},{4,0},{5,1},{6,2},{7,3},{8,12},{9,13},{10,... | collective-permute-start | bytes 1572872 | tf_op jit(solution)/shard_map/ppermute | solution.py:45
  254.0 23.0 %collective-permute-start.37 = (bf16[128,2048]{1,0:T(8,128)(2,1)}, bf16[128,2048]{1,0:T(8,128)(2,1)}, u32[]{:S(2)}, u32[]{:S(2)}) collective-permute-start(bf16[128,2048]{1,0:T(8,128)(2,1)} %get-tuple-element.253), channel_id=1, source_target_pairs={{0,2},{1,7},{2,4},{3,1},{4,6},{5,3},{6,0},{7,5},{8,10},{9,15},{10,... | collective-permute-start | bytes 1572872 | tf_op jit(solution)/shard_map/ppermute | solution.py:45
  277.0 134.6 %reduce-scatter.4.cloned.1.call-start = ((), (), s32[]{:S(2)}) async-start(), calls=%async_computation.5 | async-start | bytes 4718592 | tf_op jit(solution)/shard_map/reduce_scatter | solution.py:885
  277.6 192.9 %all-gather.13.cloned.1.call-start = ((), (), s32[]{:S(2)}) async-start(), calls=%async_computation.9 | async-start | bytes 1114112 | tf_op jit(solution)/shard_map/all_gather | solution.py:926
  277.6 24.2 %collective-permute-start.45 = (bf16[4,2,2,3,16,704]{5,4,3,2,1,0:T(8,128)(2,1)}, bf16[4,2,2,3,16,704]{5,4,3,2,1,0:T(8,128)(2,1)S(1)}, u32[]{:S(2)}, u32[]{:S(2)}) collective-permute-start(bf16[4,2,2,3,16,704]{5,4,3,2,1,0:T(8,128)(2,1)} %get-tuple-element.180), channel_id=1, source_target_pairs={{0,8},{1,73},{2,10},{3,75},{4,12},{5,77},{6,14},{7,79},{8,64},{9,1... | collective-permute-start | bytes 3244040 | tf_op jit(solution)/shard_map/ppermute | solution.py:45
  284.3 14.1 %collective-permute-start.41 = (bf16[128,2048]{1,0:T(8,128)(2,1)S(1)}, bf16[128,2048]{1,0:T(8,128)(2,1)S(1)}, u32[]{:S(2)}, u32[]{:S(2)}) collective-permute-start(bf16[128,2048]{1,0:T(8,128)(2,1)S(1)} %get-tuple-element.241.refs_1_.refs_8_), channel_id=1, source_target_pairs={{0,6},{1,3},{2,0},{3,5},{4,2},{5,7},{6,4},{7,1},{8,14},{9,11},{10,... | collective-permute-start | bytes 1572872 | tf_op jit(solution)/shard_map/ppermute | solution.py:45
  286.6 13.2 %collective-permute-start.40 = (bf16[128,2048]{1,0:T(8,128)(2,1)S(1)}, bf16[128,2048]{1,0:T(8,128)(2,1)S(1)}, u32[]{:S(2)}, u32[]{:S(2)}) collective-permute-start(bf16[128,2048]{1,0:T(8,128)(2,1)S(1)} %get-tuple-element.241.refs_1_.refs_8_), channel_id=1, source_target_pairs={{0,2},{1,7},{2,4},{3,1},{4,6},{5,3},{6,0},{7,5},{8,10},{9,15},{10,... | collective-permute-start | bytes 1572872 | tf_op jit(solution)/shard_map/ppermute | solution.py:45
  301.7 29.8 %collective-permute-start.47 = (bf16[4,2,2,3,16,704]{5,4,3,2,1,0:T(8,128)(2,1)S(1)}, bf16[4,2,2,3,16,704]{5,4,3,2,1,0:T(8,128)(2,1)S(1)}, u32[]{:S(2)}, u32[]{:S(2)}) collective-permute-start(bf16[4,2,2,3,16,704]{5,4,3,2,1,0:T(8,128)(2,1)S(1)} %copy-done.87), channel_id=1, source_target_pairs={{0,72},{1,9},{2,74},{3,11},{4,76},{5,13},{6,78},{7,15},{8,0},{9,65... | collective-permute-start | bytes 3244040 | tf_op jit(solution)/shard_map/ppermute | solution.py:45
  302.1 38.7 %collective-permute-start.48 = (bf16[4,2,2,3,16,704]{5,4,3,2,1,0:T(8,128)(2,1)S(1)}, bf16[4,2,2,3,16,704]{5,4,3,2,1,0:T(8,128)(2,1)S(1)}, u32[]{:S(2)}, u32[]{:S(2)}) collective-permute-start(bf16[4,2,2,3,16,704]{5,4,3,2,1,0:T(8,128)(2,1)S(1)} %add_convert_fusion.1), channel_id=1, source_target_pairs={{0,8},{1,73},{2,10},{3,75},{4,12},{5,77},{6,14},{7,79},{8,64},{9,1... | collective-permute-start | bytes 3244040 | tf_op jit(solution)/shard_map/ppermute | solution.py:45
  305.4 19.1 %collective-permute-start.44 = (bf16[128,2048]{1,0:T(8,128)(2,1)S(1)}, bf16[128,2048]{1,0:T(8,128)(2,1)S(1)}, u32[]{:S(2)}, u32[]{:S(2)}) collective-permute-start(bf16[128,2048]{1,0:T(8,128)(2,1)S(1)} %get-tuple-element.241.refs_1_.refs_8_), channel_id=1, source_target_pairs={{0,4},{1,5},{2,6},{3,7},{4,0},{5,1},{6,2},{7,3},{8,12},{9,13},{10,... | collective-permute-start | bytes 1572872 | tf_op jit(solution)/shard_map/ppermute | solution.py:45
  341.4 12.9 %collective-permute-start.51 = (bf16[2,2,3,16,704]{4,3,2,1,0:T(8,128)(2,1)S(1)}, bf16[2,2,3,16,704]{4,3,2,1,0:T(8,128)(2,1)S(1)}, u32[]{:S(2)}, u32[]{:S(2)}) collective-permute-start(bf16[2,2,3,16,704]{4,3,2,1,0:T(8,128)(2,1)S(1)} %get-tuple-element.249), channel_id=1, source_target_pairs={{0,32},{1,33},{2,34},{3,35},{4,36},{5,37},{6,38},{7,39},{8,40},{9,... | collective-permute-start | bytes 811016 | tf_op jit(solution)/shard_map/ppermute | solution.py:45
  346.4 14.0 %collective-permute-start.53 = (bf16[2,2,3,16,704]{4,3,2,1,0:T(8,128)(2,1)S(1)}, bf16[2,2,3,16,704]{4,3,2,1,0:T(8,128)(2,1)S(1)}, u32[]{:S(2)}, u32[]{:S(2)}) collective-permute-start(bf16[2,2,3,16,704]{4,3,2,1,0:T(8,128)(2,1)S(1)} %get-tuple-element.250), channel_id=1, source_target_pairs={{0,16},{1,49},{2,18},{3,51},{4,20},{5,53},{6,22},{7,55},{8,24},{9,... | collective-permute-start | bytes 811016 | tf_op jit(solution)/shard_map/ppermute | solution.py:45
  346.4 14.0 %collective-permute-start.52 = (bf16[2,2,3,16,704]{4,3,2,1,0:T(8,128)(2,1)S(1)}, bf16[2,2,3,16,704]{4,3,2,1,0:T(8,128)(2,1)S(1)}, u32[]{:S(2)}, u32[]{:S(2)}) collective-permute-start(bf16[2,2,3,16,704]{4,3,2,1,0:T(8,128)(2,1)S(1)} %get-tuple-element.251), channel_id=1, source_target_pairs={{0,48},{1,17},{2,50},{3,19},{4,52},{5,21},{6,54},{7,23},{8,56},{9,... | collective-permute-start | bytes 811016 | tf_op jit(solution)/shard_map/ppermute | solution.py:45
  370.9 155.8 %reduce-scatter.8.cloned.1.call-start = ((), (), s32[]{:S(2)}) async-start(), calls=%async_computation.7 | async-start | bytes 4718592 | tf_op jit(solution)/shard_map/reduce_scatter | solution.py:933
  394.1 11.8 %collective-permute-start.55 = (bf16[2,2,3,16,704]{4,3,2,1,0:T(8,128)(2,1)S(1)}, bf16[2,2,3,16,704]{4,3,2,1,0:T(8,128)(2,1)S(1)}, u32[]{:S(2)}, u32[]{:S(2)}) collective-permute-start(bf16[2,2,3,16,704]{4,3,2,1,0:T(8,128)(2,1)S(1)} %get-tuple-element.246), channel_id=1, source_target_pairs={{0,64},{1,65},{2,66},{3,67},{4,68},{5,69},{6,70},{7,71},{8,72},{9,... | collective-permute-start | bytes 811016 | tf_op jit(solution)/shard_map/ppermute | solution.py:45
  395.7 14.2 %collective-permute-start.57 = (bf16[2,2,3,16,704]{4,3,2,1,0:T(8,128)(2,1)S(1)}, bf16[2,2,3,16,704]{4,3,2,1,0:T(8,128)(2,1)S(1)}, u32[]{:S(2)}, u32[]{:S(2)}) collective-permute-start(bf16[2,2,3,16,704]{4,3,2,1,0:T(8,128)(2,1)S(1)} %get-tuple-element.247), channel_id=1, source_target_pairs={{0,8},{1,73},{2,10},{3,75},{4,12},{5,77},{6,14},{7,79},{8,64},{9,1... | collective-permute-start | bytes 811016 | tf_op jit(solution)/shard_map/ppermute | solution.py:45
  395.7 15.7 %collective-permute-start.56 = (bf16[2,2,3,16,704]{4,3,2,1,0:T(8,128)(2,1)S(1)}, bf16[2,2,3,16,704]{4,3,2,1,0:T(8,128)(2,1)S(1)}, u32[]{:S(2)}, u32[]{:S(2)}) collective-permute-start(bf16[2,2,3,16,704]{4,3,2,1,0:T(8,128)(2,1)S(1)} %get-tuple-element.248), channel_id=1, source_target_pairs={{0,72},{1,9},{2,74},{3,11},{4,76},{5,13},{6,78},{7,15},{8,0},{9,65... | collective-permute-start | bytes 811016 | tf_op jit(solution)/shard_map/ppermute | solution.py:45
  397.7 28.4 %collective-permute-start.62 = (bf16[4,4,2,16,576]{4,3,2,1,0:T(8,128)(2,1)}, bf16[4,4,2,16,576]{4,3,2,1,0:T(8,128)(2,1)S(1)}, u32[]{:S(2)}, u32[]{:S(2)}) collective-permute-start(bf16[4,4,2,16,576]{4,3,2,1,0:T(8,128)(2,1)} %get-tuple-element.222), channel_id=1, source_target_pairs={{0,16},{1,49},{2,18},{3,51},{4,20},{5,53},{6,22},{7,55},{8,24},{9,... | collective-permute-start | bytes 1769480 | tf_op jit(solution)/shard_map/ppermute | solution.py:45
  424.6 16.8 %collective-permute-start.54 = (bf16[4,4,2,16,576]{4,3,2,1,0:T(8,128)(2,1)S(1)}, bf16[4,4,2,16,576]{4,3,2,1,0:T(8,128)(2,1)S(1)}, u32[]{:S(2)}, u32[]{:S(2)}) collective-permute-start(bf16[4,4,2,16,576]{4,3,2,1,0:T(8,128)(2,1)S(1)} %copy-done.88), channel_id=1, source_target_pairs={{0,48},{1,17},{2,50},{3,19},{4,52},{5,21},{6,54},{7,23},{8,56},{9,... | collective-permute-start | bytes 1769480 | tf_op jit(solution)/shard_map/ppermute | solution.py:45
  426.3 16.6 %collective-permute-start.63 = (bf16[4,4,2,16,576]{4,3,2,1,0:T(8,128)(2,1)S(1)}, bf16[4,4,2,16,576]{4,3,2,1,0:T(8,128)(2,1)S(1)}, u32[]{:S(2)}, u32[]{:S(2)}) collective-permute-start(bf16[4,4,2,16,576]{4,3,2,1,0:T(8,128)(2,1)S(1)} %add_convert_fusion.3), channel_id=1, source_target_pairs={{0,16},{1,49},{2,18},{3,51},{4,20},{5,53},{6,22},{7,55},{8,24},{9,... | collective-permute-start | bytes 1769480 | tf_op jit(solution)/shard_map/ppermute | solution.py:45
  427.6 20.2 %collective-permute-start.67 = (bf16[2,4,3,16,704]{4,3,2,1,0:T(8,128)(2,1)S(1)}, bf16[2,4,3,16,704]{4,3,2,1,0:T(8,128)(2,1)S(1)}, u32[]{:S(2)}, u32[]{:S(2)}) collective-permute-start(bf16[2,4,3,16,704]{4,3,2,1,0:T(8,128)(2,1)S(1)} %get-tuple-element.258), channel_id=1, source_target_pairs={{0,64},{1,65},{2,66},{3,67},{4,68},{5,69},{6,70},{7,71},{8,72},{9,... | collective-permute-start | bytes 1622024 | tf_op jit(solution)/shard_map/ppermute | solution.py:45
  447.9 29.8 %collective-permute-start.80 = (bf16[2,2,4,3,16,704]{5,4,3,2,1,0:T(8,128)(2,1)S(1)}, bf16[2,2,4,3,16,704]{5,4,3,2,1,0:T(8,128)(2,1)S(1)}, u32[]{:S(2)}, u32[]{:S(2)}) collective-permute-start(bf16[2,2,4,3,16,704]{5,4,3,2,1,0:T(8,128)(2,1)S(1)} %pad_maximum_fusion.1.refs_0_), channel_id=1, source_target_pairs={{0,16},{1,49},{2,18},{3,51},{4,20},{5,53},{6,22},{7,55},{8,24},{9,... | collective-permute-start | bytes 3244040 | tf_op jit(solution)/shard_map/ppermute | solution.py:45
  468.6 52.0 %collective-permute-start.81 = (bf16[2,2,4,3,16,704]{5,4,3,2,1,0:T(8,128)(2,1)S(1)}, bf16[2,2,4,3,16,704]{5,4,3,2,1,0:T(8,128)(2,1)}, u32[]{:S(2)}, u32[]{:S(2)}) collective-permute-start(bf16[2,2,4,3,16,704]{5,4,3,2,1,0:T(8,128)(2,1)S(1)} %pad_maximum_fusion.1.refs_0_), channel_id=1, source_target_pairs={{0,48},{1,17},{2,50},{3,19},{4,52},{5,21},{6,54},{7,23},{8,56},{9,... | collective-permute-start | bytes 3244040 | tf_op jit(solution)/shard_map/ppermute | solution.py:45
  473.5 12.2 %collective-permute-start.77 = (bf16[2,2,4,16,576]{4,3,2,1,0:T(8,128)(2,1)S(1)}, bf16[2,2,4,16,576]{4,3,2,1,0:T(8,128)(2,1)S(1)}, u32[]{:S(2)}, u32[]{:S(2)}) collective-permute-start(bf16[2,2,4,16,576]{4,3,2,1,0:T(8,128)(2,1)S(1)} %pad_maximum_fusion.5.refs_0_), channel_id=1, source_target_pairs={{0,32},{1,33},{2,34},{3,35},{4,36},{5,37},{6,38},{7,39},{8,40},{9,... | collective-permute-start | bytes 884744 | tf_op jit(solution)/shard_map/ppermute | solution.py:45
  475.9 33.8 %collective-permute-start.76 = (bf16[2,2,4,16,576]{4,3,2,1,0:T(8,128)(2,1)S(1)}, bf16[2,2,4,16,576]{4,3,2,1,0:T(8,128)(2,1)S(1)}, u32[]{:S(2)}, u32[]{:S(2)}) collective-permute-start(bf16[2,2,4,16,576]{4,3,2,1,0:T(8,128)(2,1)S(1)} %pad_maximum_fusion.5.refs_0_), channel_id=1, source_target_pairs={{0,48},{1,17},{2,50},{3,19},{4,52},{5,21},{6,54},{7,23},{8,56},{9,... | collective-permute-start | bytes 884744 | tf_op jit(solution)/shard_map/ppermute | solution.py:45
  477.6 32.0 %collective-permute-start.75 = (bf16[2,2,4,16,576]{4,3,2,1,0:T(8,128)(2,1)S(1)}, bf16[2,2,4,16,576]{4,3,2,1,0:T(8,128)(2,1)S(1)}, u32[]{:S(2)}, u32[]{:S(2)}) collective-permute-start(bf16[2,2,4,16,576]{4,3,2,1,0:T(8,128)(2,1)S(1)} %pad_maximum_fusion.5.refs_0_), channel_id=1, source_target_pairs={{0,16},{1,49},{2,18},{3,51},{4,20},{5,53},{6,22},{7,55},{8,24},{9,... | collective-permute-start | bytes 884744 | tf_op jit(solution)/shard_map/ppermute | solution.py:45
  477.9 42.7 %collective-permute-start.82 = (bf16[2,2,4,3,16,704]{5,4,3,2,1,0:T(8,128)(2,1)S(1)}, bf16[2,2,4,3,16,704]{5,4,3,2,1,0:T(8,128)(2,1)S(1)}, u32[]{:S(2)}, u32[]{:S(2)}) collective-permute-start(bf16[2,2,4,3,16,704]{5,4,3,2,1,0:T(8,128)(2,1)S(1)} %collective-permute-done.80.refs_1_), channel_id=1, source_target_pairs={{0,16},{1,49},{2,18},{3,51},{4,20},{5,53},{6,22},{7,55},{8,24},{9,... | collective-permute-start | bytes 3244040 | tf_op jit(solution)/shard_map/ppermute | solution.py:45
  (131 other events, 1323.0 us)
Sparse Core Ops, SparseCore 0:
  28.5 40.7 all-gather.6
  73.8 54.5 all-gather.10
  130.1 55.6 all-gather.8
  277.1 52.1 reduce-scatter.5
  331.5 38.1 reduce-scatter.3
  371.3 32.2 all-gather.12
  406.0 43.2 reduce-scatter.7

commit v8 on v7

--- a/solution.py
+++ b/solution.py
@@ -132,14 +132,14 @@
     return lax.dot_general(left, right, (((1,), (1,)), ((), ())), preferred_element_type=F32)
 
 
-def call(body, tables, grid, in_specs, out_specs, out_shape, scratch, micros, args, aliases=None):
+def call(body, tables, grid, in_specs, out_specs, out_shape, scratch, micros, args, aliases=None, mib=VMEM_MIB):
     return pl.pallas_call(
         body,
         grid_spec=pltpu.PrefetchScalarGridSpec(
             num_scalar_prefetch=len(tables), grid=grid, in_specs=in_specs, out_specs=out_specs, scratch_shapes=scratch
         ),
         out_shape=out_shape,
-        compiler_params=pltpu.CompilerParams(vmem_limit_bytes=VMEM_MIB * MIB),
+        compiler_params=pltpu.CompilerParams(vmem_limit_bytes=mib * MIB),
         cost_estimate=pl.CostEstimate(flops=1000, bytes_accessed=micros * 300000, transcendentals=0),
         input_output_aliases=aliases or {},
     )(*tables, *args)
@@ -673,7 +673,7 @@
         + [pl.BlockSpec((8 * TOK, HEAD), whole)],
         [out] * 4, [sds((4, 4, 2, 16, PACK))] * 4,
         [pltpu.VMEM((256, QKV), F32), pltpu.VMEM((128, 2 * QUERY), F32)],
-        10, (h,) * 8 + tuple(g) + tuple(o) + tuple(dq) + (dkv,),
+        10, (h,) * 8 + tuple(g) + tuple(o) + tuple(dq) + (dkv,), mib=60,
     )
 
 
@@ -813,10 +813,6 @@
     w_qkv = place_qkv(slot, xs, halves, *qkv_rows)
 
     mlp_mine, mlp_other = pack_mlp(after(spots, attn_part), core, gate_weight, up_weight, down_weight)
-    mlp_half_rows = lax.all_gather(
-        exchange(mlp_mine, mlp_other, 1, qkv_rows[1]), "batch", axis=0, axis_index_groups=X_GROUPS
-    )
-
     out_rows = lax.dynamic_slice_in_dim(output_weight, x * 32, 32, axis=0)
     out_part = send(
         out_rows.reshape(32, 8, QUERY).transpose(1, 0, 2),
@@ -840,6 +836,9 @@
     usable = (jnp.arange(TOK, dtype=jnp.int32)[None, :] < key_count[:, None]).reshape(16 * TOK, 1)
 
     queries, kv_own = project(chunk, normed_attn, w_qkv)
+    mlp_half_rows = lax.all_gather(
+        exchange(mlp_mine, mlp_other, 1, kv_own), "batch", axis=0, axis_index_groups=X_GROUPS
+    )
     kv_half = to_half(kv_own)
     kv_mine = jnp.concatenate([kv_own[0], kv_half[0]], axis=0)
     kv_other = swap(jnp.concatenate([kv_own[1], kv_half[1]], axis=0))
@@ -933,15 +932,18 @@
     normed_attn_grad = lax.psum_scatter(attn_partial, "blk", scatter_dimension=0, axis_index_groups=ZC_GROUPS)
 
     layer_out = (residual + after(branch, attn_outs[0]).astype(F32)).astype(BF)[None]
+    gain_grads = jnp.sum(after(gain_grads, mlp_swapped), axis=0)[:2]
+    gain_grads = gain_grads + across(gain_grads, "y")
     mlp_across = across(mlp_sums, "y")
     mlp_sums = jnp.stack([mlp_sums, mlp_across])
     mlp_first, mlp_second = step(mlp_sums, "x", 1), step(mlp_sums, "x", -1)
-    attn_sums = ring_scatter(*attn_outs, "x", mlp_swapped).astype(BF)
+    attn_sums = ring_scatter(*attn_outs, "x", attn_outs[0]).astype(BF)
+    attn_sums = after(attn_sums, gain_grads)
+    gain_grads = gain_grads + across(gain_grads, "x")
     attn_sums = ring_scatter(attn_sums[0], attn_sums[2], attn_sums[3], attn_sums[1], "y").astype(BF)
-    gain_grads = jnp.sum(after(gain_grads, attn_sums), axis=0)[:2]
+    attn_sums = after(attn_sums, gain_grads)
+    gain_grads = gain_grads + step(gain_grads, "x", 1)
     mlp_sums = (mlp_sums, mlp_first, mlp_second, step(after(mlp_first, attn_sums), "x", 1))
-    gain_grads = gain_grads + across(gain_grads, "y")
-    attn_sums = after(attn_sums, mlp_across)
     out_sums = send(
         attn_sums[..., :QUERY], lambda yh, x, yl, z, c: (yh, x, z // 2, 2 * (z % 2) + c, yl)
     )
@@ -952,9 +954,6 @@
     tokens_grad = (
         residual_grad + norm_back(rows_in, scale_attn, gain_one, after(normed_attn_grad, attn_across).astype(F32))
     ).astype(BF)[None]
-    gain_grads = after(gain_grads, *attn_sums[1:])
-    gain_grads = gain_grads + across(gain_grads, "x")
-    gain_grads = gain_grads + step(gain_grads, "x", 1)
     gate_grad, up_grad, down_grad = finish_mlp(spots, xs, yhs, core, mlp_sums)
     query_grad, key_grad, value_grad, output_grad = finish_attn(after(spots, tokens_grad), xs, yhs, core, attn_sums)
     return (

time: 547 us -> 530 us (0.969)
  waiting for transfers between devices: 198 us -> 180 us
  local copies, waits for them, and re-layouts: 34.5 us -> 26.5 us
    ppermute x83, waiting for transfers between devices: 187 us -> 162 us  [send(): return lax.ppermute(value, BOTH, pairs)]
    unnamed x181 -> x167, local copies, waits for them, and re-layouts: 28.2 us -> 17.9 us
  transfers between devices with their start and end apart: 90 -> 90, of which waited for: 43 -> 42; matrix products, arithmetic and copies ran while one was open for 6% -> 7% of each run, Pallas kernels for 25% -> 27%
where the time goes in v8:
time: 530 us; the launch traced here: 523 us
  waiting for transfers between devices  180 us (34%)
  Pallas kernels  162 us (31%)
  starting transfers between devices  105 us (20%)
  other arithmetic  34.3 us (6%)
  local copies, waits for them, and re-layouts  26.5 us (5%)
  between operations  15.8 us (3%)
    ppermute x83, waiting for transfers between devices, send(): return lax.ppermute(value, BOTH, pairs)  162 us
    pallas_call x20, Pallas kernels, call(): pl.pallas_call(body, grid_spec=pltpu.PrefetchScalarGridSpec(num_scalar_pr...  162 us
    ppermute x83, starting transfers between devices, send(): return lax.ppermute(value, BOTH, pairs)  104 us
    unnamed x167, local copies, waits for them, and re-layouts  17.9 us
    all_gather x1, waiting for transfers between devices, on_device(): lax.all_gather(exchange(mlp_mine, mlp_other, 1, kv_own), 'batch', axis=0,...  15.7 us
  transfers between devices with their start and end apart: 90, of which 42 were waited for; matrix products, arithmetic and copies ran while one was open for 7% of the time, Pallas kernels for 27%

profile of v8, /device:TPU:24, one launch (start us, length us, event | category | flops | bytes accessed | tf_op | source)
XLA Modules:
  0.0 523.2 jit_solution(15730930251678941914)
XLA Ops:
  22.1 3.7 collective-permute-done.3
  29.8 2.9 shard_map.220
  33.5 3.0 collective-permute-start.6
  39.8 3.2 collective-permute-done.6
  42.9 4.0 collective-permute-done.5
  56.7 3.4 collective-permute-done.7.other_ref
  65.3 6.0 %shard_map.214 = (bf16[1024,256]{1,0:T(8,128)(2,1)S(1)}, bf16[2,1024,64]{2,1,0:T(8,128)(2,1)S(1)}) custom-call(s32[8]{0:T(128)S(1)} %stack.242.chunk.nat, bf16[1024,2048]{1,0:T(8,128)(2,1)} %all-gather.7.cloned.1.call-done.refs_0_.refs_1_.refs_2_.refs_3_.refs_4_.refs_5_.refs_6_.refs_7_, ...), custom_call_target="tpu_custom_call" | custom-call | flops 1000 | bytes 1500000 | tf_op jit(solution)/shard_map/pallas_call | solution.py:136
  75.0 4.1 collective-permute-start.10
  81.6 3.9 collective-permute-start.13
  88.0 3.4 collective-permute-done.13
  97.1 7.9 %collective-permute-done.14.other_ref = bf16[4,8,32,256]{3,2,1,0:T(8,128)(2,1)S(1)} collective-permute-done((bf16[4,8,32,256]{3,2,1,0:T(8,128)(2,1)S(1)}, bf16[4,8,32,256]{3,2,1,0:T(8,128)(2,1)S(1)}, u32[]{:S(2)}, u32[]{:S(2)}) %collective-permute-start.14) | collective-permute-done | bytes 524320 | tf_op jit(solution)/shard_map/ppermute | solution.py:45
  108.4 5.2 %shard_map.216 = (bf16[256,256]{1,0:T(8,128)(2,1)S(1)}, bf16[128,2048]{1,0:T(8,128)(2,1)S(1)}, bf16[128,2048]{1,0:T(8,128)(2,1)}) custom-call(s32[8]{0:T(128)S(1)} %bitcast.201, s32[16]{0:T(128)S(1)} %select_reduce_fusion.1.key_slot, bf16[1024,256]{1,0:T(8,128)(2,1)S(1)} %get-tuple-element.131.q_ref.refs_0_, ...), custom_call_target="tpu_custom_call" | custom-call | flops 1000 | bytes 1800000 | tf_op jit(solution)/shard_map/pallas_call | solution.py:136
  114.3 15.7 %all-gather.11.cloned.1.call-done = bf16[12,8,32,704]{3,2,0,1:T(8,128)(2,1)} async-done(((bf16[3,8,32,704]{3,2,0,1:T(8,128)(2,1)}), bf16[12,8,32,704]{3,2,0,1:T(8,128)(2,1)}) %all-gather.11.cloned.1.call-update) | async-done | bytes 4325392 | tf_op jit(solution)/shard_map/all_gather | solution.py:839
  132.8 5.6 %shard_map.218 = (bf16[256,256]{1,0:T(8,128)(2,1)S(1)}, bf16[128,2048]{1,0:T(8,128)(2,1)S(1)}, bf16[128,2048]{1,0:T(8,128)(2,1)S(1)}) custom-call(s32[8]{0:T(128)S(1)} %bitcast.202, s32[16]{0:T(128)S(1)} %select_reduce_fusion.1.key_slot, bf16[1024,256]{1,0:T(8,128)(2,1)S(1)} %get-tuple-element.131.q_ref.refs_0_, ...), custom_call_target="tpu_custom_call" | custom-call | flops 1000 | bytes 1800000 | tf_op jit(solution)/shard_map/pallas_call | solution.py:136
  138.6 5.9 %shard_map.217 = (bf16[256,256]{1,0:T(8,128)(2,1)S(1)}, bf16[128,2048]{1,0:T(8,128)(2,1)S(1)}, bf16[128,2048]{1,0:T(8,128)(2,1)S(1)}) custom-call(s32[8]{0:T(128)S(1)} %bitcast.203, s32[16]{0:T(128)S(1)} %select_reduce_fusion.1.key_slot, bf16[1024,256]{1,0:T(8,128)(2,1)S(1)} %get-tuple-element.131.q_ref.refs_0_, ...), custom_call_target="tpu_custom_call" | custom-call | flops 1000 | bytes 1800000 | tf_op jit(solution)/shard_map/pallas_call | solution.py:136
  145.2 4.2 collective-permute-start.21
  154.1 6.9 %shard_map.219 = (bf16[256,256]{1,0:T(8,128)(2,1)S(1)}, bf16[128,2048]{1,0:T(8,128)(2,1)S(1)}, bf16[128,2048]{1,0:T(8,128)(2,1)S(1)}) custom-call(s32[8]{0:T(128)S(1)} %bitcast.204, s32[16]{0:T(128)S(1)} %select_reduce_fusion.1.key_slot, bf16[1024,256]{1,0:T(8,128)(2,1)S(1)} %get-tuple-element.131.q_ref.refs_0_, ...), custom_call_target="tpu_custom_call" | custom-call | flops 1000 | bytes 1800000 | tf_op jit(solution)/shard_map/pallas_call | solution.py:136
  161.2 12.0 %collective-permute-done.21 = bf16[128,2048]{1,0:T(8,128)(2,1)S(1)} collective-permute-done((bf16[128,2048]{1,0:T(8,128)(2,1)S(1)}, bf16[128,2048]{1,0:T(8,128)(2,1)S(1)}, u32[]{:S(2)}, u32[]{:S(2)}) %collective-permute-start.21) | collective-permute-done | bytes 524320 | tf_op jit(solution)/shard_map/ppermute | solution.py:45
  173.2 12.5 %collective-permute-done.20 = bf16[128,2048]{1,0:T(8,128)(2,1)S(1)} collective-permute-done((bf16[128,2048]{1,0:T(8,128)(2,1)S(1)}, bf16[128,2048]{1,0:T(8,128)(2,1)S(1)}, u32[]{:S(2)}, u32[]{:S(2)}) %collective-permute-start.20) | collective-permute-done | bytes 524320 | tf_op jit(solution)/shard_map/ppermute | solution.py:45
  188.1 8.4 %shard_map.221 = bf16[3,2,8,128,704]{4,3,2,1,0:T(8,128)(2,1)} custom-call(s32[8]{0:T(128)S(1)} %stack.254.slot, s32[2]{0:T(128)S(1)} %pad_add_fusion.2.halves, bf16[4,3,8,32,704]{4,3,2,1,0:T(8,128)(2,1)S(1)} %bitcast.195, bf16[4,3,8,32,704]{4,3,2,1,0:T(8,128)(2,1)} %collective-permute-done.28.other_ref), custom_call_target="tpu_custom_call" | custom-call | flops 1000 | bytes 1800000 | tf_op jit(solution)/shard_map/pallas_call | solution.py:136
  200.9 18.8 %shard_map.222 = (bf16[1024,704]{1,0:T(8,128)(2,1)S(1)}, bf16[1024,704]{1,0:T(8,128)(2,1)}, bf16[1024,704]{1,0:T(8,128)(2,1)}, bf16[128,2048]{1,0:T(8,128)(2,1)S...) custom-call(s32[8]{0:T(128)S(1)} %stack.242.chunk.nat, ...), custom_call_target="tpu_custom_call" | custom-call | flops 1000 | bytes 5400000 | tf_op jit(solution)/shard_map/pallas_call | solution.py:136
  221.0 8.7 %collective-permute-start.34 = (bf16[128,2048]{1,0:T(8,128)(2,1)}, bf16[128,2048]{1,0:T(8,128)(2,1)S(1)}, u32[]{:S(2)}, u32[]{:S(2)}) collective-permute-start(bf16[128,2048]{1,0:T(8,128)(2,1)} %collective-permute-done.31.refs_2_.refs_6_), channel_id=1, source_target_pairs={{0,1},{1,0},{2,3},{3,2},{4,5},{5,4},{6,7},{7,6},{8,9},{9,8},{10,11... | collective-permute-start | bytes 1572872 | tf_op jit(solution)/shard_map/ppermute | solution.py:45
  231.7 18.6 %shard_map.223 = (bf16[1024,704]{1,0:T(8,128)(2,1)S(1)}, bf16[1024,704]{1,0:T(8,128)(2,1)}, bf16[1024,704]{1,0:T(8,128)(2,1)}, bf16[128,2048]{1,0:T(8,128)(2,1)S...) custom-call(s32[8]{0:T(128)S(1)} %stack.242.chunk.nat, ...), custom_call_target="tpu_custom_call", output_to_operand_aliasing={{0}: (10, {}), {1}: (11, {}), {2}: (12, {}), {6}: (13, {})} | custom-call | flops 1000 | bytes 5400000 | tf_op jit(solution)/shard_map/pallas_call | solution.py:136
  258.1 19.5 %shard_map.224 = (bf16[4,4,2,2,3,16,704]{6,5,4,3,2,1,0:T(8,128)(2,1)}, bf16[4,2,2,3,16,704]{5,4,3,2,1,0:T(8,128)(2,1)S(1)}, bf16[4,2,2,3,16,704]{5,4,3,2,1,0:T(8...) custom-call(s32[8]{0:T(128)S(1)} %stack.284.column, s32[4]{0:T(128)S(1)} %pad_add_fusion.1.xs, ...), custom_call_target="tpu_custom_call" | custom-call | flops 1000 | bytes 5100000 | tf_op jit(solution)/shard_map/pallas_call | solution.py:136
  281.2 3.1 multiply_reduce_fusion
  288.6 9.5 %shard_map.225 = (bf16[256,256]{1,0:T(8,128)(2,1)S(1)}, f32[2048,64]{1,0:T(8,128)S(1)}, f32[2048,64]{1,0:T(8,128)S(1)}) custom-call(s32[8]{0:T(128)S(1)} %bitcast.205, s32[16]{0:T(128)S(1)} %select_reduce_fusion.1.key_slot, s32[1]{0:T(128)} %bitcast.16.core, s32[16]{0:T(128)S(1)} %copy-done.52, bf16[1024,256]{1,0:T(8,128)(2,1)S(1)} %get-tuple-element.131.q_ref.refs_0_, ...), custom_call_target="tpu_custom_call" | custom-call | flops 1000 | bytes 2400000 | tf_op jit(solution)/shard_map/pallas_call | solution.py:136
  308.7 15.8 %shard_map.226 = (bf16[512,256]{1,0:T(8,128)(2,1)S(1)}, f32[2048,64]{1,0:T(8,128)S(1)}, f32[2048,64]{1,0:T(8,128)}) custom-call(s32[8]{0:T(128)S(1)} %bitcast.206, s32[16]{0:T(128)S(1)} %select_reduce_fusion.1.key_slot, s32[1]{0:T(128)} %bitcast.16.core, s32[16]{0:T(128)S(1)} %copy-done.52, bf16[1024,256]{1,0:T(8,128)(2,1)S(1)} %get-tuple-element.131.q_ref.refs_0_, ...), custom_call_target="tpu_custom_call" | custom-call | flops 1000 | bytes 4800000 | tf_op jit(solution)/shard_map/pallas_call | solution.py:136
  327.1 5.5 %collective-permute-done.47 = bf16[4,2,2,3,16,704]{5,4,3,2,1,0:T(8,128)(2,1)S(1)} collective-permute-done((bf16[4,2,2,3,16,704]{5,4,3,2,1,0:T(8,128)(2,1)S(1)}, bf16[4,2,2,3,16,704]{5,4,3,2,1,0:T(8,128)(2,1)S(1)}, u32[]{:S(2)}, u32[]{:S(2)}) %collective-permute-start.47) | collective-permute-done | bytes 1081376 | tf_op jit(solution)/shard_map/ppermute | solution.py:45
  332.6 9.1 %shard_map.227 = (bf16[256,256]{1,0:T(8,128)(2,1)S(1)}, bf16[2048,64]{1,0:T(8,128)(2,1)S(1)}, bf16[2048,64]{1,0:T(8,128)(2,1)S(1)}) custom-call(s32[8]{0:T(128)S(1)} %bitcast.207, s32[16]{0:T(128)S(1)} %select_reduce_fusion.1.key_slot, s32[1]{0:T(128)} %bitcast.16.core, s32[16]{0:T(128)S(1)} %copy-done.52, ...), custom_call_target="tpu_custom_call" | custom-call | flops 1000 | bytes 2400000 | tf_op jit(solution)/shard_map/pallas_call | solution.py:136
  343.6 5.0 collective-permute-start.53
  348.9 5.0 collective-permute-done.51
  353.9 5.7 %collective-permute-done.53 = bf16[2,2,3,16,704]{4,3,2,1,0:T(8,128)(2,1)S(1)} collective-permute-done((bf16[2,2,3,16,704]{4,3,2,1,0:T(8,128)(2,1)S(1)}, bf16[2,2,3,16,704]{4,3,2,1,0:T(8,128)(2,1)S(1)}, u32[]{:S(2)}, u32[]{:S(2)}) %collective-permute-start.53) | collective-permute-done | bytes 270368 | tf_op jit(solution)/shard_map/ppermute | solution.py:45
  363.4 7.0 %shard_map.229 = (bf16[8,128,2048]{2,1,0:T(8,128)(2,1)}, f32[8,2048]{1,0:T(8,128)S(1)}) custom-call(s32[8]{0:T(128)S(1)} %stack.242.chunk.nat, bf16[256,256]{1,0:T(8,128)(2,1)S(1)} %get-tuple-element.185.refs_20_.dq0_ref, bf16[512,256]{1,0:T(8,128)(2,1)S(1)} %copy-done.26, bf16[256,256]{1,0:T(8,128)(2,1)S(1)} %copy-done.34, ...), custom_call_target="tpu_custom_call" | custom-call | flops 1000 | bytes 1500000 | tf_op jit(solution)/shard_map/pallas_call | solution.py:136
  371.3 11.8 %shard_map.228 = (bf16[4,4,2,16,576]{4,3,2,1,0:T(8,128)(2,1)}, bf16[4,4,2,16,576]{4,3,2,1,0:T(8,128)(2,1)}, bf16[4,4,2,16,576]{4,3,2,1,0:T(8,128)(2,1)}, bf16[4,4,2,16,576]{4,3,2,1,0:T(8,128)(2,1)}) custom-call(s32[8]{0:T(128)} %copy-done.54, s32[4]{0:T(128)} %copy-done.45, s32[4]{0:T(128)} %copy-done.47, s32[1]{0:T(128)} %bitcast.16.core, s32[2]{0:T(128)} %copy-done.53, ...), custom_call_target="tpu_custom_call" | custom-call | flops 1000 | bytes 3000000 | tf_op jit(solution)/shard_map/pallas_call | solution.py:136
  390.5 7.2 %collective-permute-done.57 = bf16[2,2,3,16,704]{4,3,2,1,0:T(8,128)(2,1)S(1)} collective-permute-done((bf16[2,2,3,16,704]{4,3,2,1,0:T(8,128)(2,1)S(1)}, bf16[2,2,3,16,704]{4,3,2,1,0:T(8,128)(2,1)S(1)}, u32[]{:S(2)}, u32[]{:S(2)}) %collective-permute-start.57) | collective-permute-done | bytes 270368 | tf_op jit(solution)/shard_map/ppermute | solution.py:45
  397.7 4.9 collective-permute-done.59
  403.2 4.5 collective-permute-start.60
  412.0 4.4 collective-permute-done.61
  427.3 3.2 collective-permute-done.56
  430.8 9.1 %collective-permute-done.64 = f32[2,2048]{1,0:T(2,128)S(1)} collective-permute-done((f32[2,2048]{1,0:T(2,128)S(1)}, f32[2,2048]{1,0:T(2,128)S(1)}, u32[]{:S(2)}, u32[]{:S(2)}) %collective-permute-start.64) | collective-permute-done | bytes 16416 | tf_op jit(solution)/shard_map/ppermute | solution.py:45
  439.9 3.1 collective-permute-start.68
  448.2 3.1 collective-permute-start.81
  459.4 17.2 %collective-permute-done.80.refs_1_ = bf16[2,2,4,3,16,704]{5,4,3,2,1,0:T(8,128)(2,1)S(1)} collective-permute-done((bf16[2,2,4,3,16,704]{5,4,3,2,1,0:T(8,128)(2,1)S(1)}, bf16[2,2,4,3,16,704]{5,4,3,2,1,0:T(8,128)(2,1)S(1)}, u32[]{:S(2)}, u32[]{:S(2)}) %collective-permute-start.80) | collective-permute-done | bytes 1081376 | tf_op jit(solution)/shard_map/ppermute | solution.py:45
  480.2 6.7 %collective-permute-done.74 = bf16[2,4,16,576]{3,2,1,0:T(8,128)(2,1)S(1)} collective-permute-done((bf16[2,4,16,576]{3,2,1,0:T(8,128)(2,1)S(1)}, bf16[2,4,16,576]{3,2,1,0:T(8,128)(2,1)S(1)}, u32[]{:S(2)}, u32[]{:S(2)}) %collective-permute-start.74) | collective-permute-done | bytes 147488 | tf_op jit(solution)/shard_map/ppermute | solution.py:45
  487.4 3.1 collective-permute-start.77
  490.5 14.1 %collective-permute-done.82.refs_3_ = bf16[2,2,4,3,16,704]{5,4,3,2,1,0:T(8,128)(2,1)S(1)} collective-permute-done((bf16[2,2,4,3,16,704]{5,4,3,2,1,0:T(8,128)(2,1)S(1)}, bf16[2,2,4,3,16,704]{5,4,3,2,1,0:T(8,128)(2,1)S(1)}, u32[]{:S(2)}, u32[]{:S(2)}) %collective-permute-start.82) | collective-permute-done | bytes 1081376 | tf_op jit(solution)/shard_map/ppermute | solution.py:45
  504.6 4.8 shard_map.231
  510.8 3.2 fusion.18
  (425 shorter events, 153.7 us)
Async XLA Ops:
  7.2 58.1 %all-gather.7.cloned.1.call-start = ((), (), s32[]{:S(2)}) async-start(), calls=%async_computation.3 | async-start | bytes 4718592 | tf_op jit(solution)/shard_map/all_gather | solution.py:809
  28.4 101.7 %all-gather.11.cloned.1.call-start = ((), (), s32[]{:S(2)}) async-start(), calls=%async_computation.8 | async-start | bytes 5898240 | tf_op jit(solution)/shard_map/all_gather | solution.py:839
  33.5 14.8 %collective-permute-start.24 = (bf16[4,3,32,704]{3,2,1,0:T(8,128)(2,1)}, bf16[4,3,32,704]{3,2,1,0:T(8,128)(2,1)}, u32[]{:S(2)}, u32[]{:S(2)}) collective-permute-start(bf16[4,3,32,704]{3,2,1,0:T(8,128)(2,1)} %get-tuple-element.145), channel_id=1, source_target_pairs={{0,1},{1,0},{2,3},{3,2},{4,5},{5,4},{6,7},{7,6},{8,9},{9,8},{10,11... | collective-permute-start | bytes 1622024 | tf_op jit(solution)/shard_map/ppermute | solution.py:45
  48.0 12.1 %collective-permute-start.7 = (bf16[4,8,32,320]{3,2,1,0:T(8,128)(2,1)S(1)}, bf16[4,8,32,320]{3,2,1,0:T(8,128)(2,1)S(1)}, u32[]{:S(2)}, u32[]{:S(2)}) collective-permute-start(bf16[4,8,32,320]{3,2,1,0:T(8,128)(2,1)S(1)} %pad_maximum_fusion.2.own_ref), channel_id=1, source_target_pairs={{0,8},{1,73},{2,10},{3,75},{4,12},{5,77},{6,14},{7,79},{8,64},{9,1... | collective-permute-start | bytes 1966088 | tf_op jit(solution)/shard_map/ppermute | solution.py:45
  50.2 21.1 %collective-permute-start.25 = (bf16[3,2,32,704]{3,2,0,1:T(8,128)(2,1)}, bf16[3,2,32,704]{3,2,0,1:T(8,128)(2,1)}, u32[]{:S(2)}, u32[]{:S(2)}) collective-permute-start(bf16[3,2,32,704]{3,2,0,1:T(8,128)(2,1)} %pad_maximum_fusion.7), channel_id=1, source_target_pairs={{0,2},{1,7},{2,4},{3,1},{4,6},{5,3},{6,0},{7,5},{8,10},{9,15},{10,... | collective-permute-start | bytes 811016 | tf_op jit(solution)/shard_map/ppermute | solution.py:45
  51.3 20.0 %collective-permute-start.26 = (bf16[3,2,32,704]{3,2,0,1:T(8,128)(2,1)}, bf16[3,2,32,704]{3,2,0,1:T(8,128)(2,1)}, u32[]{:S(2)}, u32[]{:S(2)}) collective-permute-start(bf16[3,2,32,704]{3,2,0,1:T(8,128)(2,1)} %pad_maximum_fusion.8), channel_id=1, source_target_pairs={{0,6},{1,3},{2,0},{3,5},{4,2},{5,7},{6,4},{7,1},{8,14},{9,11},{10,... | collective-permute-start | bytes 811016 | tf_op jit(solution)/shard_map/ppermute | solution.py:45
  54.9 17.6 %collective-permute-start.27 = (bf16[3,2,32,704]{3,2,0,1:T(8,128)(2,1)}, bf16[3,2,32,704]{3,2,0,1:T(8,128)(2,1)}, u32[]{:S(2)}, u32[]{:S(2)}) collective-permute-start(bf16[3,2,32,704]{3,2,0,1:T(8,128)(2,1)} %pad_maximum_fusion.9), channel_id=1, source_target_pairs={{0,4},{1,5},{2,6},{3,7},{4,0},{5,1},{6,2},{7,3},{8,12},{9,13},{10,... | collective-permute-start | bytes 811016 | tf_op jit(solution)/shard_map/ppermute | solution.py:45
  74.9 126.0 %all-gather.9.cloned.1.call-start = ((), (), s32[]{:S(2)}) async-start(), calls=%async_computation.4 | async-start | bytes 4718592 | tf_op jit(solution)/shard_map/all_gather | solution.py:823
  79.1 284.2 %reduce-scatter.6.cloned.1.call-start = ((), (), s32[]{:S(2)}) async-start(), calls=%async_computation.6 | async-start | bytes 5898240 | tf_op jit(solution)/shard_map/reduce_scatter | solution.py:883
  114.3 18.4 %collective-permute-start.15 = (bf16[128,2048]{1,0:T(8,128)(2,1)}, bf16[128,2048]{1,0:T(8,128)(2,1)}, u32[]{:S(2)}, u32[]{:S(2)}) collective-permute-start(bf16[128,2048]{1,0:T(8,128)(2,1)} %get-tuple-element.135), channel_id=1, source_target_pairs={{0,1},{1,0},{2,3},{3,2},{4,5},{5,4},{6,7},{7,6},{8,9},{9,8},{10,11... | collective-permute-start | bytes 1572872 | tf_op jit(solution)/shard_map/ppermute | solution.py:45
  132.8 55.3 %collective-permute-start.28 = (bf16[4,3,8,32,704]{4,3,2,1,0:T(8,128)(2,1)S(1)}, bf16[4,3,8,32,704]{4,3,2,1,0:T(8,128)(2,1)}, u32[]{:S(2)}, u32[]{:S(2)}) collective-permute-start(bf16[4,3,8,32,704]{4,3,2,1,0:T(8,128)(2,1)S(1)} %bitcast.194), channel_id=1, source_target_pairs={{0,8},{1,73},{2,10},{3,75},{4,12},{5,77},{6,14},{7,79},{8,64},{9,1... | collective-permute-start | bytes 12976136 | tf_op jit(solution)/shard_map/ppermute | solution.py:45
  145.2 28.0 %collective-permute-start.21 = (bf16[128,2048]{1,0:T(8,128)(2,1)S(1)}, bf16[128,2048]{1,0:T(8,128)(2,1)S(1)}, u32[]{:S(2)}, u32[]{:S(2)}) collective-permute-start(bf16[128,2048]{1,0:T(8,128)(2,1)S(1)} %add_convert_fusion.6), channel_id=1, source_target_pairs={{0,4},{1,5},{2,6},{3,7},{4,0},{5,1},{6,2},{7,3},{8,12},{9,13},{10,... | collective-permute-start | bytes 1572872 | tf_op jit(solution)/shard_map/ppermute | solution.py:45
  149.5 36.2 %collective-permute-start.20 = (bf16[128,2048]{1,0:T(8,128)(2,1)S(1)}, bf16[128,2048]{1,0:T(8,128)(2,1)S(1)}, u32[]{:S(2)}, u32[]{:S(2)}) collective-permute-start(bf16[128,2048]{1,0:T(8,128)(2,1)S(1)} %add_convert_fusion.7), channel_id=1, source_target_pairs={{0,2},{1,7},{2,4},{3,1},{4,6},{5,3},{6,0},{7,5},{8,10},{9,15},{10,... | collective-permute-start | bytes 1572872 | tf_op jit(solution)/shard_map/ppermute | solution.py:45
  152.5 33.2 %collective-permute-start.19 = (bf16[128,2048]{1,0:T(8,128)(2,1)S(1)}, bf16[128,2048]{1,0:T(8,128)(2,1)S(1)}, u32[]{:S(2)}, u32[]{:S(2)}) collective-permute-start(bf16[128,2048]{1,0:T(8,128)(2,1)S(1)} %add_convert_fusion.8), channel_id=1, source_target_pairs={{0,6},{1,3},{2,0},{3,5},{4,2},{5,7},{6,4},{7,1},{8,14},{9,11},{10,... | collective-permute-start | bytes 1572872 | tf_op jit(solution)/shard_map/ppermute | solution.py:45
  161.0 24.7 %collective-permute-start.18 = (bf16[128,2048]{1,0:T(8,128)(2,1)S(1)}, bf16[128,2048]{1,0:T(8,128)(2,1)S(1)}, u32[]{:S(2)}, u32[]{:S(2)}) collective-permute-start(bf16[128,2048]{1,0:T(8,128)(2,1)S(1)} %get-tuple-element.142), channel_id=1, source_target_pairs={{0,1},{1,0},{2,3},{3,2},{4,5},{5,4},{6,7},{7,6},{8,9},{9,8},{10,11... | collective-permute-start | bytes 1572872 | tf_op jit(solution)/shard_map/ppermute | solution.py:45
  187.9 13.0 %collective-permute-start.22 = (bf16[128,2048]{1,0:T(8,128)(2,1)S(1)}, bf16[128,2048]{1,0:T(8,128)(2,1)}, u32[]{:S(2)}, u32[]{:S(2)}) collective-permute-start(bf16[128,2048]{1,0:T(8,128)(2,1)S(1)} %multiply_convert_fusion.refs_0_), channel_id=1, source_target_pairs={{0,1},{1,0},{2,3},{3,2},{4,5},{5,4},{6,7},{7,6},{8,9},{9,8},{10,11... | collective-permute-start | bytes 1572872 | tf_op jit(solution)/shard_map/ppermute | solution.py:45
  197.1 23.3 %collective-permute-start.31 = (bf16[128,2048]{1,0:T(8,128)(2,1)S(1)}, bf16[128,2048]{1,0:T(8,128)(2,1)}, u32[]{:S(2)}, u32[]{:S(2)}) collective-permute-start(bf16[128,2048]{1,0:T(8,128)(2,1)S(1)} %multiply_convert_fusion.refs_0_), channel_id=1, source_target_pairs={{0,4},{1,5},{2,6},{3,7},{4,0},{5,1},{6,2},{7,3},{8,12},{9,13},{10,... | collective-permute-start | bytes 1572872 | tf_op jit(solution)/shard_map/ppermute | solution.py:45
  198.7 21.8 %collective-permute-start.30 = (bf16[128,2048]{1,0:T(8,128)(2,1)S(1)}, bf16[128,2048]{1,0:T(8,128)(2,1)}, u32[]{:S(2)}, u32[]{:S(2)}) collective-permute-start(bf16[128,2048]{1,0:T(8,128)(2,1)S(1)} %multiply_convert_fusion.refs_0_), channel_id=1, source_target_pairs={{0,6},{1,3},{2,0},{3,5},{4,2},{5,7},{6,4},{7,1},{8,14},{9,11},{10,... | collective-permute-start | bytes 1572872 | tf_op jit(solution)/shard_map/ppermute | solution.py:45
  251.7 26.9 %collective-permute-start.36 = (bf16[128,2048]{1,0:T(8,128)(2,1)}, bf16[128,2048]{1,0:T(8,128)(2,1)}, u32[]{:S(2)}, u32[]{:S(2)}) collective-permute-start(bf16[128,2048]{1,0:T(8,128)(2,1)} %fusion.11), channel_id=1, source_target_pairs={{0,6},{1,3},{2,0},{3,5},{4,2},{5,7},{6,4},{7,1},{8,14},{9,11},{10,... | collective-permute-start | bytes 1572872 | tf_op jit(solution)/shard_map/ppermute | solution.py:45
  254.5 24.2 %collective-permute-start.38 = (bf16[128,2048]{1,0:T(8,128)(2,1)}, bf16[128,2048]{1,0:T(8,128)(2,1)}, u32[]{:S(2)}, u32[]{:S(2)}) collective-permute-start(bf16[128,2048]{1,0:T(8,128)(2,1)} %get-tuple-element.252), channel_id=1, source_target_pairs={{0,4},{1,5},{2,6},{3,7},{4,0},{5,1},{6,2},{7,3},{8,12},{9,13},{10,... | collective-permute-start | bytes 1572872 | tf_op jit(solution)/shard_map/ppermute | solution.py:45
  255.4 23.3 %collective-permute-start.37 = (bf16[128,2048]{1,0:T(8,128)(2,1)}, bf16[128,2048]{1,0:T(8,128)(2,1)}, u32[]{:S(2)}, u32[]{:S(2)}) collective-permute-start(bf16[128,2048]{1,0:T(8,128)(2,1)} %get-tuple-element.253), channel_id=1, source_target_pairs={{0,2},{1,7},{2,4},{3,1},{4,6},{5,3},{6,0},{7,5},{8,10},{9,15},{10,... | collective-permute-start | bytes 1572872 | tf_op jit(solution)/shard_map/ppermute | solution.py:45
  278.7 124.5 %reduce-scatter.4.cloned.1.call-start = ((), (), s32[]{:S(2)}) async-start(), calls=%async_computation.5 | async-start | bytes 4718592 | tf_op jit(solution)/shard_map/reduce_scatter | solution.py:884
  279.3 144.6 %all-gather.13.cloned.1.call-start = ((), (), s32[]{:S(2)}) async-start(), calls=%async_computation.9 | async-start | bytes 1114112 | tf_op jit(solution)/shard_map/all_gather | solution.py:925
  279.3 24.5 %collective-permute-start.45 = (bf16[4,2,2,3,16,704]{5,4,3,2,1,0:T(8,128)(2,1)}, bf16[4,2,2,3,16,704]{5,4,3,2,1,0:T(8,128)(2,1)S(1)}, u32[]{:S(2)}, u32[]{:S(2)}) collective-permute-start(bf16[4,2,2,3,16,704]{5,4,3,2,1,0:T(8,128)(2,1)} %get-tuple-element.180), channel_id=1, source_target_pairs={{0,8},{1,73},{2,10},{3,75},{4,12},{5,77},{6,14},{7,79},{8,64},{9,1... | collective-permute-start | bytes 3244040 | tf_op jit(solution)/shard_map/ppermute | solution.py:45
  286.2 14.2 %collective-permute-start.41 = (bf16[128,2048]{1,0:T(8,128)(2,1)S(1)}, bf16[128,2048]{1,0:T(8,128)(2,1)S(1)}, u32[]{:S(2)}, u32[]{:S(2)}) collective-permute-start(bf16[128,2048]{1,0:T(8,128)(2,1)S(1)} %get-tuple-element.241.refs_1_.refs_8_), channel_id=1, source_target_pairs={{0,6},{1,3},{2,0},{3,5},{4,2},{5,7},{6,4},{7,1},{8,14},{9,11},{10,... | collective-permute-start | bytes 1572872 | tf_op jit(solution)/shard_map/ppermute | solution.py:45
  288.0 13.2 %collective-permute-start.40 = (bf16[128,2048]{1,0:T(8,128)(2,1)S(1)}, bf16[128,2048]{1,0:T(8,128)(2,1)S(1)}, u32[]{:S(2)}, u32[]{:S(2)}) collective-permute-start(bf16[128,2048]{1,0:T(8,128)(2,1)S(1)} %get-tuple-element.241.refs_1_.refs_8_), channel_id=1, source_target_pairs={{0,2},{1,7},{2,4},{3,1},{4,6},{5,3},{6,0},{7,5},{8,10},{9,15},{10,... | collective-permute-start | bytes 1572872 | tf_op jit(solution)/shard_map/ppermute | solution.py:45
  303.1 29.5 %collective-permute-start.47 = (bf16[4,2,2,3,16,704]{5,4,3,2,1,0:T(8,128)(2,1)S(1)}, bf16[4,2,2,3,16,704]{5,4,3,2,1,0:T(8,128)(2,1)S(1)}, u32[]{:S(2)}, u32[]{:S(2)}) collective-permute-start(bf16[4,2,2,3,16,704]{5,4,3,2,1,0:T(8,128)(2,1)S(1)} %copy-done.81), channel_id=1, source_target_pairs={{0,72},{1,9},{2,74},{3,11},{4,76},{5,13},{6,78},{7,15},{8,0},{9,65... | collective-permute-start | bytes 3244040 | tf_op jit(solution)/shard_map/ppermute | solution.py:45
  304.2 37.7 %collective-permute-start.48 = (bf16[4,2,2,3,16,704]{5,4,3,2,1,0:T(8,128)(2,1)S(1)}, bf16[4,2,2,3,16,704]{5,4,3,2,1,0:T(8,128)(2,1)S(1)}, u32[]{:S(2)}, u32[]{:S(2)}) collective-permute-start(bf16[4,2,2,3,16,704]{5,4,3,2,1,0:T(8,128)(2,1)S(1)} %add_convert_fusion.1), channel_id=1, source_target_pairs={{0,8},{1,73},{2,10},{3,75},{4,12},{5,77},{6,14},{7,79},{8,64},{9,1... | collective-permute-start | bytes 3244040 | tf_op jit(solution)/shard_map/ppermute | solution.py:45
  306.8 18.4 %collective-permute-start.44 = (bf16[128,2048]{1,0:T(8,128)(2,1)S(1)}, bf16[128,2048]{1,0:T(8,128)(2,1)S(1)}, u32[]{:S(2)}, u32[]{:S(2)}) collective-permute-start(bf16[128,2048]{1,0:T(8,128)(2,1)S(1)} %get-tuple-element.241.refs_1_.refs_8_), channel_id=1, source_target_pairs={{0,4},{1,5},{2,6},{3,7},{4,0},{5,1},{6,2},{7,3},{8,12},{9,13},{10,... | collective-permute-start | bytes 1572872 | tf_op jit(solution)/shard_map/ppermute | solution.py:45
  343.6 16.0 %collective-permute-start.53 = (bf16[2,2,3,16,704]{4,3,2,1,0:T(8,128)(2,1)S(1)}, bf16[2,2,3,16,704]{4,3,2,1,0:T(8,128)(2,1)S(1)}, u32[]{:S(2)}, u32[]{:S(2)}) collective-permute-start(bf16[2,2,3,16,704]{4,3,2,1,0:T(8,128)(2,1)S(1)} %get-tuple-element.250), channel_id=1, source_target_pairs={{0,16},{1,49},{2,18},{3,51},{4,20},{5,53},{6,22},{7,55},{8,24},{9,... | collective-permute-start | bytes 811016 | tf_op jit(solution)/shard_map/ppermute | solution.py:45
  348.7 13.7 %collective-permute-start.52 = (bf16[2,2,3,16,704]{4,3,2,1,0:T(8,128)(2,1)S(1)}, bf16[2,2,3,16,704]{4,3,2,1,0:T(8,128)(2,1)S(1)}, u32[]{:S(2)}, u32[]{:S(2)}) collective-permute-start(bf16[2,2,3,16,704]{4,3,2,1,0:T(8,128)(2,1)S(1)} %get-tuple-element.251), channel_id=1, source_target_pairs={{0,48},{1,17},{2,50},{3,19},{4,52},{5,21},{6,54},{7,23},{8,56},{9,... | collective-permute-start | bytes 811016 | tf_op jit(solution)/shard_map/ppermute | solution.py:45
  348.8 14.4 %collective-permute-start.50 = (bf16[1024,64]{1,0:T(8,128)(2,1)S(1)}, bf16[1024,64]{1,0:T(8,128)(2,1)S(1)}, u32[]{:S(2)}, u32[]{:S(2)}) collective-permute-start(bf16[1024,64]{1,0:T(8,128)(2,1)S(1)} %slice.382), channel_id=1, source_target_pairs={{0,8},{1,9},{2,10},{3,11},{4,12},{5,13},{6,14},{7,15},{8,0},{9,1},... | collective-permute-start | bytes 393224 | tf_op jit(solution)/shard_map/ppermute | solution.py:45
  371.1 138.2 %reduce-scatter.8.cloned.1.call-start = ((), (), s32[]{:S(2)}) async-start(), calls=%async_computation.7 | async-start | bytes 4718592 | tf_op jit(solution)/shard_map/reduce_scatter | solution.py:932
  384.5 13.2 %collective-permute-start.57 = (bf16[2,2,3,16,704]{4,3,2,1,0:T(8,128)(2,1)S(1)}, bf16[2,2,3,16,704]{4,3,2,1,0:T(8,128)(2,1)S(1)}, u32[]{:S(2)}, u32[]{:S(2)}) collective-permute-start(bf16[2,2,3,16,704]{4,3,2,1,0:T(8,128)(2,1)S(1)} %get-tuple-element.246), channel_id=1, source_target_pairs={{0,64},{1,65},{2,66},{3,67},{4,68},{5,69},{6,70},{7,71},{8,72},{9,... | collective-permute-start | bytes 811016 | tf_op jit(solution)/shard_map/ppermute | solution.py:45
  386.5 16.2 %collective-permute-start.59 = (bf16[2,2,3,16,704]{4,3,2,1,0:T(8,128)(2,1)S(1)}, bf16[2,2,3,16,704]{4,3,2,1,0:T(8,128)(2,1)S(1)}, u32[]{:S(2)}, u32[]{:S(2)}) collective-permute-start(bf16[2,2,3,16,704]{4,3,2,1,0:T(8,128)(2,1)S(1)} %get-tuple-element.247), channel_id=1, source_target_pairs={{0,8},{1,73},{2,10},{3,75},{4,12},{5,77},{6,14},{7,79},{8,64},{9,1... | collective-permute-start | bytes 811016 | tf_op jit(solution)/shard_map/ppermute | solution.py:45
  386.5 16.5 %collective-permute-start.58 = (bf16[2,2,3,16,704]{4,3,2,1,0:T(8,128)(2,1)S(1)}, bf16[2,2,3,16,704]{4,3,2,1,0:T(8,128)(2,1)S(1)}, u32[]{:S(2)}, u32[]{:S(2)}) collective-permute-start(bf16[2,2,3,16,704]{4,3,2,1,0:T(8,128)(2,1)S(1)} %get-tuple-element.248), channel_id=1, source_target_pairs={{0,72},{1,9},{2,74},{3,11},{4,76},{5,13},{6,78},{7,15},{8,0},{9,65... | collective-permute-start | bytes 811016 | tf_op jit(solution)/shard_map/ppermute | solution.py:45
  388.5 38.9 %collective-permute-start.54 = (bf16[4,4,2,16,576]{4,3,2,1,0:T(8,128)(2,1)}, bf16[4,4,2,16,576]{4,3,2,1,0:T(8,128)(2,1)S(1)}, u32[]{:S(2)}, u32[]{:S(2)}) collective-permute-start(bf16[4,4,2,16,576]{4,3,2,1,0:T(8,128)(2,1)} %get-tuple-element.217), channel_id=1, source_target_pairs={{0,48},{1,17},{2,50},{3,19},{4,52},{5,21},{6,54},{7,23},{8,56},{9,... | collective-permute-start | bytes 1769480 | tf_op jit(solution)/shard_map/ppermute | solution.py:45
  389.4 27.0 %collective-permute-start.55 = (bf16[4,4,2,16,576]{4,3,2,1,0:T(8,128)(2,1)}, bf16[4,4,2,16,576]{4,3,2,1,0:T(8,128)(2,1)}, u32[]{:S(2)}, u32[]{:S(2)}) collective-permute-start(bf16[4,4,2,16,576]{4,3,2,1,0:T(8,128)(2,1)} %get-tuple-element.220), channel_id=1, source_target_pairs={{0,16},{1,49},{2,18},{3,51},{4,20},{5,53},{6,22},{7,55},{8,24},{9,... | collective-permute-start | bytes 1769480 | tf_op jit(solution)/shard_map/ppermute | solution.py:45
  422.4 24.6 %collective-permute-start.79 = (bf16[2,4,3,16,704]{4,3,2,1,0:T(8,128)(2,1)}, bf16[2,4,3,16,704]{4,3,2,1,0:T(8,128)(2,1)}, u32[]{:S(2)}, u32[]{:S(2)}) collective-permute-start(bf16[2,4,3,16,704]{4,3,2,1,0:T(8,128)(2,1)} %get-tuple-element.258), channel_id=1, source_target_pairs={{0,64},{1,65},{2,66},{3,67},{4,68},{5,69},{6,70},{7,71},{8,72},{9,... | collective-permute-start | bytes 1622024 | tf_op jit(solution)/shard_map/ppermute | solution.py:45
  425.1 14.7 %collective-permute-start.64 = (f32[2,2048]{1,0:T(2,128)S(1)}, f32[2,2048]{1,0:T(2,128)S(1)}, u32[]{:S(2)}, u32[]{:S(2)}) collective-permute-start(f32[2,2048]{1,0:T(2,128)S(1)} %slice.317), channel_id=1, source_target_pairs={{0,64},{1,65},{2,66},{3,67},{4,68},{5,69},{6,70},{7,71},{8,72},{9,... | collective-permute-start | bytes 49160 | tf_op jit(solution)/shard_map/ppermute | solution.py:45
  448.2 42.3 %collective-permute-start.81 = (bf16[2,2,4,3,16,704]{5,4,3,2,1,0:T(8,128)(2,1)S(1)}, bf16[2,2,4,3,16,704]{5,4,3,2,1,0:T(8,128)(2,1)S(1)}, u32[]{:S(2)}, u32[]{:S(2)}) collective-permute-start(bf16[2,2,4,3,16,704]{5,4,3,2,1,0:T(8,128)(2,1)S(1)} %pad_maximum_fusion.1.refs_0_), channel_id=1, source_target_pairs={{0,48},{1,17},{2,50},{3,19},{4,52},{5,21},{6,54},{7,23},{8,56},{9,... | collective-permute-start | bytes 3244040 | tf_op jit(solution)/shard_map/ppermute | solution.py:45
  451.9 24.8 %collective-permute-start.80 = (bf16[2,2,4,3,16,704]{5,4,3,2,1,0:T(8,128)(2,1)S(1)}, bf16[2,2,4,3,16,704]{5,4,3,2,1,0:T(8,128)(2,1)S(1)}, u32[]{:S(2)}, u32[]{:S(2)}) collective-permute-start(bf16[2,2,4,3,16,704]{5,4,3,2,1,0:T(8,128)(2,1)S(1)} %pad_maximum_fusion.1.refs_0_), channel_id=1, source_target_pairs={{0,16},{1,49},{2,18},{3,51},{4,20},{5,53},{6,22},{7,55},{8,24},{9,... | collective-permute-start | bytes 3244040 | tf_op jit(solution)/shard_map/ppermute | solution.py:45
  453.6 23.4 %collective-permute-start.70 = (bf16[2,16,320]{2,1,0:T(8,128)(2,1)S(1)}, bf16[2,16,320]{2,1,0:T(8,128)(2,1)S(1)}, u32[]{:S(2)}, u32[]{:S(2)}) collective-permute-start(bf16[2,16,320]{2,1,0:T(8,128)(2,1)S(1)} %get-tuple-element.283), channel_id=1, source_target_pairs={{0,2},{1,7},{2,4},{3,1},{4,6},{5,3},{6,0},{7,5},{8,10},{9,15},{10,... | collective-permute-start | bytes 61448 | tf_op jit(solution)/shard_map/ppermute | solution.py:45
  457.3 21.5 %collective-permute-start.69 = (bf16[4,2,16,256]{3,2,1,0:T(8,128)(2,1)S(1)}, bf16[4,2,16,256]{3,2,1,0:T(8,128)(2,1)S(1)}, u32[]{:S(2)}, u32[]{:S(2)}) collective-permute-start(bf16[4,2,16,256]{3,2,1,0:T(8,128)(2,1)S(1)} %slice.271), channel_id=1, source_target_pairs={{0,0},{1,2},{2,4},{3,6},{4,8},{5,10},{6,12},{7,14},{8,1},{9,3},{10... | collective-permute-start | bytes 196616 | tf_op jit(solution)/shard_map/ppermute | solution.py:45
  476.7 27.9 %collective-permute-start.82 = (bf16[2,2,4,3,16,704]{5,4,3,2,1,0:T(8,128)(2,1)S(1)}, bf16[2,2,4,3,16,704]{5,4,3,2,1,0:T(8,128)(2,1)S(1)}, u32[]{:S(2)}, u32[]{:S(2)}) collective-permute-start(bf16[2,2,4,3,16,704]{5,4,3,2,1,0:T(8,128)(2,1)S(1)} %collective-permute-done.80.refs_1_), channel_id=1, source_target_pairs={{0,16},{1,49},{2,18},{3,51},{4,20},{5,53},{6,22},{7,55},{8,24},{9,... | collective-permute-start | bytes 3244040 | tf_op jit(solution)/shard_map/ppermute | solution.py:45
  487.0 27.0 %collective-permute-start.78 = (bf16[2,2,4,16,576]{4,3,2,1,0:T(8,128)(2,1)S(1)}, bf16[2,2,4,16,576]{4,3,2,1,0:T(8,128)(2,1)S(1)}, u32[]{:S(2)}, u32[]{:S(2)}) collective-permute-start(bf16[2,2,4,16,576]{4,3,2,1,0:T(8,128)(2,1)S(1)} %pad_maximum_fusion.5.refs_0_), channel_id=1, source_target_pairs={{0,32},{1,33},{2,34},{3,35},{4,36},{5,37},{6,38},{7,39},{8,40},{9,... | collective-permute-start | bytes 884744 | tf_op jit(solution)/shard_map/ppermute | solution.py:45
  487.4 26.6 %collective-permute-start.77 = (bf16[2,2,4,16,576]{4,3,2,1,0:T(8,128)(2,1)S(1)}, bf16[2,2,4,16,576]{4,3,2,1,0:T(8,128)(2,1)S(1)}, u32[]{:S(2)}, u32[]{:S(2)}) collective-permute-start(bf16[2,2,4,16,576]{4,3,2,1,0:T(8,128)(2,1)S(1)} %pad_maximum_fusion.5.refs_0_), channel_id=1, source_target_pairs={{0,48},{1,17},{2,50},{3,19},{4,52},{5,21},{6,54},{7,23},{8,56},{9,... | collective-permute-start | bytes 884744 | tf_op jit(solution)/shard_map/ppermute | solution.py:45
  490.5 23.5 %collective-permute-start.76 = (bf16[2,2,4,16,576]{4,3,2,1,0:T(8,128)(2,1)S(1)}, bf16[2,2,4,16,576]{4,3,2,1,0:T(8,128)(2,1)S(1)}, u32[]{:S(2)}, u32[]{:S(2)}) collective-permute-start(bf16[2,2,4,16,576]{4,3,2,1,0:T(8,128)(2,1)S(1)} %pad_maximum_fusion.5.refs_0_), channel_id=1, source_target_pairs={{0,16},{1,49},{2,18},{3,51},{4,20},{5,53},{6,22},{7,55},{8,24},{9,... | collective-permute-start | bytes 884744 | tf_op jit(solution)/shard_map/ppermute | solution.py:45
  (124 other events, 2134.5 us)
Sparse Core Ops, SparseCore 0:
  28.5 36.7 all-gather.6
  75.0 55.0 all-gather.10
  131.8 56.2 all-gather.8
  278.8 52.7 reduce-scatter.5
  333.8 37.9 reduce-scatter.3
  373.4 33.3 all-gather.12
  409.1 39.6 reduce-scatter.7

commit v9 on v8

--- a/solution.py
+++ b/solution.py
@@ -245,13 +245,13 @@
     for e, ref in enumerate((own_ref, other_ref)):
         for r in range(4):
             for m in range(3):
-                out_ref[m, halves[e], 0, 32 * r : 32 * (r + 1), :] = ref[r, m, 0]
+                out_ref[m, halves[e], 0, 32 * r : 32 * (r + 1), :] = ref[r, 0, m]
 
 
 def place_mlp(slot, halves, own, other):
     out = call(
         place_mlp_kernel, (slot, halves), (8,),
-        [pl.BlockSpec((4, 3, 1, 32, WIDE), lambda i, *_: (0, 0, i, 0, 0))] * 2,
+        [pl.BlockSpec((4, 1, 3, 32, WIDE), lambda i, *_: (0, i, 0, 0, 0))] * 2,
         pl.BlockSpec((3, 2, 1, 128, WIDE), lambda i, slot, *_: (0, 0, slot[i], 0, 0)),
         sds((3, 2, 8, 128, WIDE)), [], 6, (own, other),
     )
@@ -792,34 +792,34 @@
     scale_attn = rms_scale(rows_in)
 
 
-    def exchange(mine, other, axis, *first):
+    def exchange(mine, other, *first):
         got = swap(other)
-        own = jnp.stack([mine[0], got[0]], axis)
-        before = jnp.stack([mine[1], got[2]], axis)
-        forward = jnp.stack([mine[2], got[1]], axis)
-        far = jnp.stack([mine[3], got[3]], axis)
-        return jnp.concatenate(after(exchange_z(own, before, forward, far), first), axis)
+        own = jnp.stack([mine[0], got[0]])
+        before = jnp.stack([mine[1], got[2]])
+        forward = jnp.stack([mine[2], got[1]])
+        far = jnp.stack([mine[3], got[3]])
+        return jnp.concatenate(after(exchange_z(own, before, forward, far), first))
 
     def spread(part):
         half_rows = jnp.stack(ring_gather(part, "x"))
         return half_rows, step(half_rows, "y", 1)
 
     normed_own = (rows_in * scale_attn * gain_one).astype(BF)
-    attn_part = exchange(*pack_attn(spots, core, query_weight, key_weight, value_weight), 0)
+    attn_part = exchange(*pack_attn(spots, core, query_weight, key_weight, value_weight))
     normed_attn = lax.all_gather(
         after(normed_own, attn_part), "blk", axis=0, tiled=True, axis_index_groups=ZC_GROUPS
     )
     qkv_rows = spread(attn_part)
-    w_qkv = place_qkv(slot, xs, halves, *qkv_rows)
-
-    mlp_mine, mlp_other = pack_mlp(after(spots, attn_part), core, gate_weight, up_weight, down_weight)
     out_rows = lax.dynamic_slice_in_dim(output_weight, x * 32, 32, axis=0)
     out_part = send(
         out_rows.reshape(32, 8, QUERY).transpose(1, 0, 2),
         lambda yh, x, yl, z, c: (yh, x, c, 2 * yl + z // 2, z % 2),
     )
-    w_out = place_out(xs, halves, *spread(after(out_part, qkv_rows[0])))
-
+    out_half_rows, out_other_rows = spread(after(out_part, qkv_rows[0]))
+    w_out = place_out(xs, halves, out_half_rows, out_other_rows)
+    w_qkv = place_qkv(slot, after(xs, out_half_rows), halves, *qkv_rows)
+
+    mlp_mine, mlp_other = pack_mlp(after(spots, attn_part), core, gate_weight, up_weight, down_weight)
     grad_rows = lax.all_gather(
         after(cotangent[0], qkv_rows[1]), "blk", axis=0, tiled=True, axis_index_groups=ZC_GROUPS
     )
@@ -837,9 +837,9 @@
 
     queries, kv_own = project(chunk, normed_attn, w_qkv)
     mlp_half_rows = lax.all_gather(
-        exchange(mlp_mine, mlp_other, 1, kv_own), "batch", axis=0, axis_index_groups=X_GROUPS
-    )
-    kv_half = to_half(kv_own)
+        exchange(mlp_mine, mlp_other, kv_own), "batch", axis=0, axis_index_groups=X_GROUPS
+    )
+    kv_half = to_half(after(kv_own, out_other_rows))
     kv_mine = jnp.concatenate([kv_own[0], kv_half[0]], axis=0)
     kv_other = swap(jnp.concatenate([kv_own[1], kv_half[1]], axis=0))
     keys = jnp.where(first_core, kv_mine, kv_other)
@@ -926,7 +926,8 @@
     attn_outs = attn_grads(
         column, xs, yhs, core, halves, chunk, normed_attn, branch_parts, attended, query_grad_rows, kv_grad_rows
     )
-    low, high = after((low, high), attn_outs[0], branch)
+    attn_outs = after(attn_outs, low)
+    low, high = after((low, high), branch)
     mlp_sums, mlp_swapped = resplit_back([low[0], low[1], high[0], high[1]])
     attn_partial = after(attn_partial, attn_outs[0])
     normed_attn_grad = lax.psum_scatter(attn_partial, "blk", scatter_dimension=0, axis_index_groups=ZC_GROUPS)
@@ -943,19 +944,19 @@
     attn_sums = ring_scatter(attn_sums[0], attn_sums[2], attn_sums[3], attn_sums[1], "y").astype(BF)
     attn_sums = after(attn_sums, gain_grads)
     gain_grads = gain_grads + step(gain_grads, "x", 1)
-    mlp_sums = (mlp_sums, mlp_first, mlp_second, step(after(mlp_first, attn_sums), "x", 1))
     out_sums = send(
         attn_sums[..., :QUERY], lambda yh, x, yl, z, c: (yh, x, z // 2, 2 * (z % 2) + c, yl)
     )
     qkv_sums, _ = resplit_back(attn_sums[..., QUERY:])
     attn_sums = jnp.concatenate([out_sums.reshape(2, 4, 16, QUERY), qkv_sums], axis=-1)
+    tokens_grad = (
+        residual_grad + norm_back(rows_in, scale_attn, gain_one, after(normed_attn_grad, attn_sums).astype(F32))
+    ).astype(BF)[None]
     attn_across = across(attn_sums, "y")
-    attn_sums = ring_gather(jnp.stack([attn_sums, attn_across]), "x")
-    tokens_grad = (
-        residual_grad + norm_back(rows_in, scale_attn, gain_one, after(normed_attn_grad, attn_across).astype(F32))
-    ).astype(BF)[None]
+    mlp_sums = (mlp_sums, mlp_first, mlp_second, step(after(mlp_first, attn_across), "x", 1))
+    attn_sums = ring_gather(after(jnp.stack([attn_sums, attn_across]), tokens_grad), "x")
     gate_grad, up_grad, down_grad = finish_mlp(spots, xs, yhs, core, mlp_sums)
-    query_grad, key_grad, value_grad, output_grad = finish_attn(after(spots, tokens_grad), xs, yhs, core, attn_sums)
+    query_grad, key_grad, value_grad, output_grad = finish_attn(spots, xs, yhs, core, attn_sums)
     return (
         layer_out,
         tokens_grad,

time: 530 us -> 522 us (0.985)
  waiting for transfers between devices: 180 us -> 170 us
  starting transfers between devices: 105 us -> 112 us
    ppermute x83, waiting for transfers between devices: 162 us -> 145 us  [send(): return lax.ppermute(value, BOTH, pairs)]
    all_gather x1, waiting for transfers between devices: 15.7 us -> 24.7 us  [on_device(): lax.all_gather(exchange(mlp_mine, mlp_other, kv_own), 'batch', axis=0, ax...]
    ppermute x83, starting transfers between devices: 104 us -> 112 us  [send(): return lax.ppermute(value, BOTH, pairs)]
    unnamed x167 -> x165, local copies, waits for them, and re-layouts: 17.9 us -> 15.9 us
  transfers between devices with their start and end apart: 90 -> 90, of which waited for: 42 -> 37; matrix products, arithmetic and copies ran while one was open for 7% -> 7% of each run, Pallas kernels for 27% -> 27%
where the time goes in v9:
time: 522 us; the launch traced here: 513 us
  waiting for transfers between devices  170 us (33%)
  Pallas kernels  159 us (30%)
  starting transfers between devices  112 us (21%)
  other arithmetic  33 us (6%)
  local copies, waits for them, and re-layouts  23.1 us (4%)
  between operations  16 us (3%)
    pallas_call x20, Pallas kernels, call(): pl.pallas_call(body, grid_spec=pltpu.PrefetchScalarGridSpec(num_scalar_pr...  159 us
    ppermute x83, waiting for transfers between devices, send(): return lax.ppermute(value, BOTH, pairs)  145 us
    ppermute x83, starting transfers between devices, send(): return lax.ppermute(value, BOTH, pairs)  112 us
    all_gather x1, waiting for transfers between devices, on_device(): lax.all_gather(exchange(mlp_mine, mlp_other, kv_own), 'batch', axis=0, ax...  24.7 us
    unnamed x165, local copies, waits for them, and re-layouts  15.9 us
  transfers between devices with their start and end apart: 90, of which 37 were waited for; matrix products, arithmetic and copies ran while one was open for 7% of the time, Pallas kernels for 27%

profile of v9, /device:TPU:24, one launch (start us, length us, event | category | flops | bytes accessed | tf_op | source)
XLA Modules:
  0.0 513.3 jit_solution(3123278265683112793)
XLA Ops:
  22.2 3.7 collective-permute-done.3
  29.9 2.9 shard_map.220
  33.6 3.9 collective-permute-start.4
  37.7 3.1 collective-permute-start.7
  43.9 3.3 collective-permute-done.7
  47.2 3.3 collective-permute-done.6
  65.5 2.3 collective-permute-done.11.other_ref
  71.2 6.1 %shard_map.214 = (bf16[1024,256]{1,0:T(8,128)(2,1)S(1)}, bf16[2,1024,64]{2,1,0:T(8,128)(2,1)S(1)}) custom-call(s32[8]{0:T(128)S(1)} %stack.242.chunk.nat, bf16[1024,2048]{1,0:T(8,128)(2,1)} %all-gather.7.cloned.1.call-done.refs_0_.refs_1_.refs_2_.refs_3_.refs_4_.refs_5_.refs_6_.refs_7_, ...), custom_call_target="tpu_custom_call" | custom-call | flops 1000 | bytes 1500000 | tf_op jit(solution)/shard_map/pallas_call | solution.py:136
  81.2 7.8 %collective-permute-done.12.other_ref = bf16[4,8,32,256]{3,2,1,0:T(8,128)(2,1)S(1)} collective-permute-done((bf16[4,8,32,256]{3,2,1,0:T(8,128)(2,1)S(1)}, bf16[4,8,32,256]{3,2,1,0:T(8,128)(2,1)S(1)}, u32[]{:S(2)}, u32[]{:S(2)}) %collective-permute-start.12) | collective-permute-done | bytes 524320 | tf_op jit(solution)/shard_map/ppermute | solution.py:45
  89.7 7.4 %collective-permute-done.13 = bf16[2,1024,64]{1,2,0:T(8,128)(2,1)S(1)} collective-permute-done((bf16[2,1024,64]{1,2,0:T(8,128)(2,1)S(1)}, bf16[2,1024,64]{1,2,0:T(8,128)(2,1)S(1)}, u32[]{:S(2)}, u32[]{:S(2)}) %collective-permute-start.13) | collective-permute-done | bytes 262176 | tf_op jit(solution)/shard_map/ppermute | solution.py:45
  99.8 5.6 %shard_map.216 = (bf16[256,256]{1,0:T(8,128)(2,1)S(1)}, bf16[128,2048]{1,0:T(8,128)(2,1)S(1)}, bf16[128,2048]{1,0:T(8,128)(2,1)S(1)}) custom-call(s32[8]{0:T(128)S(1)} %bitcast.187, s32[16]{0:T(128)S(1)} %select_reduce_fusion.1.key_slot, bf16[1024,256]{1,0:T(8,128)(2,1)S(1)} %get-tuple-element.139.q_ref.refs_0_, ...), custom_call_target="tpu_custom_call" | custom-call | flops 1000 | bytes 1800000 | tf_op jit(solution)/shard_map/pallas_call | solution.py:136
  108.1 24.7 %all-gather.11.cloned.1.call-done = bf16[32,3,32,704]{3,2,1,0:T(8,128)(2,1)} async-done(((bf16[8,3,32,704]{3,2,1,0:T(8,128)(2,1)}), bf16[32,3,32,704]{3,2,1,0:T(8,128)(2,1)}) %all-gather.11.cloned.1.call-update) | async-done | bytes 4325392 | tf_op jit(solution)/shard_map/all_gather | solution.py:839
  133.3 4.4 shard_map.218
  138.4 6.3 %shard_map.217 = (bf16[256,256]{1,0:T(8,128)(2,1)S(1)}, bf16[128,2048]{1,0:T(8,128)(2,1)S(1)}, bf16[128,2048]{1,0:T(8,128)(2,1)S(1)}) custom-call(s32[8]{0:T(128)S(1)} %bitcast.189, s32[16]{0:T(128)S(1)} %select_reduce_fusion.1.key_slot, bf16[1024,256]{1,0:T(8,128)(2,1)S(1)} %get-tuple-element.139.q_ref.refs_0_, ...), custom_call_target="tpu_custom_call" | custom-call | flops 1000 | bytes 1800000 | tf_op jit(solution)/shard_map/pallas_call | solution.py:136
  145.4 3.0 collective-permute-start.21
  153.2 4.9 shard_map.219
  158.2 14.6 %collective-permute-done.21 = bf16[128,2048]{1,0:T(8,128)(2,1)S(1)} collective-permute-done((bf16[128,2048]{1,0:T(8,128)(2,1)S(1)}, bf16[128,2048]{1,0:T(8,128)(2,1)S(1)}, u32[]{:S(2)}, u32[]{:S(2)}) %collective-permute-start.21) | collective-permute-done | bytes 524320 | tf_op jit(solution)/shard_map/ppermute | solution.py:45
  172.8 12.1 %collective-permute-done.20 = bf16[128,2048]{1,0:T(8,128)(2,1)S(1)} collective-permute-done((bf16[128,2048]{1,0:T(8,128)(2,1)S(1)}, bf16[128,2048]{1,0:T(8,128)(2,1)S(1)}, u32[]{:S(2)}, u32[]{:S(2)}) %collective-permute-start.20) | collective-permute-done | bytes 524320 | tf_op jit(solution)/shard_map/ppermute | solution.py:45
  189.3 8.4 %shard_map.221 = bf16[3,2,8,128,704]{4,3,2,1,0:T(8,128)(2,1)} custom-call(s32[8]{0:T(128)S(1)} %stack.254.slot, s32[2]{0:T(128)S(1)} %pad_add_fusion.2.halves, bf16[4,8,3,32,704]{4,3,2,1,0:T(8,128)(2,1)S(1)} %bitcast.186, bf16[4,8,3,32,704]{4,3,2,1,0:T(8,128)(2,1)} %collective-permute-done.28.other_ref), custom_call_target="tpu_custom_call" | custom-call | flops 1000 | bytes 1800000 | tf_op jit(solution)/shard_map/pallas_call | solution.py:136
  202.4 18.7 %shard_map.222 = (bf16[1024,704]{1,0:T(8,128)(2,1)S(1)}, bf16[1024,704]{1,0:T(8,128)(2,1)}, bf16[1024,704]{1,0:T(8,128)(2,1)}, bf16[128,2048]{1,0:T(8,128)(2,1)S...) custom-call(s32[8]{0:T(128)S(1)} %stack.242.chunk.nat, ...), custom_call_target="tpu_custom_call" | custom-call | flops 1000 | bytes 5400000 | tf_op jit(solution)/shard_map/pallas_call | solution.py:136
  222.4 8.7 %collective-permute-start.34 = (bf16[128,2048]{1,0:T(8,128)(2,1)}, bf16[128,2048]{1,0:T(8,128)(2,1)S(1)}, u32[]{:S(2)}, u32[]{:S(2)}) collective-permute-start(bf16[128,2048]{1,0:T(8,128)(2,1)} %collective-permute-done.31.refs_2_.refs_6_), channel_id=1, source_target_pairs={{0,1},{1,0},{2,3},{3,2},{4,5},{5,4},{6,7},{7,6},{8,9},{9,8},{10,11... | collective-permute-start | bytes 1572872 | tf_op jit(solution)/shard_map/ppermute | solution.py:45
  233.1 18.6 %shard_map.223 = (bf16[1024,704]{1,0:T(8,128)(2,1)S(1)}, bf16[1024,704]{1,0:T(8,128)(2,1)}, bf16[1024,704]{1,0:T(8,128)(2,1)}, bf16[128,2048]{1,0:T(8,128)(2,1)S...) custom-call(s32[8]{0:T(128)S(1)} %stack.242.chunk.nat, ...), custom_call_target="tpu_custom_call", output_to_operand_aliasing={{0}: (10, {}), {1}: (11, {}), {2}: (12, {}), {6}: (13, {})} | custom-call | flops 1000 | bytes 5400000 | tf_op jit(solution)/shard_map/pallas_call | solution.py:136
  259.5 19.5 %shard_map.224 = (bf16[4,4,2,2,3,16,704]{6,5,4,3,2,1,0:T(8,128)(2,1)}, bf16[4,2,2,3,16,704]{5,4,3,2,1,0:T(8,128)(2,1)S(1)}, bf16[4,2,2,3,16,704]{5,4,3,2,1,0:T(8...) custom-call(s32[8]{0:T(128)S(1)} %stack.284.column, s32[4]{0:T(128)S(1)} %pad_add_fusion.1.xs, ...), custom_call_target="tpu_custom_call" | custom-call | flops 1000 | bytes 5100000 | tf_op jit(solution)/shard_map/pallas_call | solution.py:136
  281.5 3.1 multiply_reduce_fusion
  289.4 6.5 %shard_map.225 = (bf16[256,256]{1,0:T(8,128)(2,1)S(1)}, f32[2048,64]{1,0:T(8,128)S(1)}, f32[2048,64]{1,0:T(8,128)S(1)}) custom-call(s32[8]{0:T(128)S(1)} %bitcast.191, s32[16]{0:T(128)S(1)} %select_reduce_fusion.1.key_slot, s32[1]{0:T(128)} %bitcast.16.core, s32[16]{0:T(128)S(1)} %copy-done.50, bf16[1024,256]{1,0:T(8,128)(2,1)S(1)} %get-tuple-element.139.q_ref.refs_0_, ...), custom_call_target="tpu_custom_call" | custom-call | flops 1000 | bytes 2400000 | tf_op jit(solution)/shard_map/pallas_call | solution.py:136
  296.9 4.2 collective-permute-done.41.refs_3_.refs_12_
  309.4 17.9 %shard_map.226 = (bf16[512,256]{1,0:T(8,128)(2,1)S(1)}, f32[2048,64]{1,0:T(8,128)S(1)}, f32[2048,64]{1,0:T(8,128)}) custom-call(s32[8]{0:T(128)S(1)} %bitcast.192, s32[16]{0:T(128)S(1)} %select_reduce_fusion.1.key_slot, s32[1]{0:T(128)} %bitcast.16.core, s32[16]{0:T(128)S(1)} %copy-done.50, bf16[1024,256]{1,0:T(8,128)(2,1)S(1)} %get-tuple-element.139.q_ref.refs_0_, ...), custom_call_target="tpu_custom_call" | custom-call | flops 1000 | bytes 4800000 | tf_op jit(solution)/shard_map/pallas_call | solution.py:136
  329.4 2.5 collective-permute-done.47
  331.9 7.4 %shard_map.227 = (bf16[256,256]{1,0:T(8,128)(2,1)S(1)}, bf16[2048,64]{1,0:T(8,128)(2,1)S(1)}, bf16[2048,64]{1,0:T(8,128)(2,1)S(1)}) custom-call(s32[8]{0:T(128)S(1)} %bitcast.193, s32[16]{0:T(128)S(1)} %select_reduce_fusion.1.key_slot, s32[1]{0:T(128)} %bitcast.16.core, s32[16]{0:T(128)S(1)} %copy-done.50, ...), custom_call_target="tpu_custom_call" | custom-call | flops 1000 | bytes 2400000 | tf_op jit(solution)/shard_map/pallas_call | solution.py:136
  340.0 8.6 %collective-permute-start.51 = (bf16[2,2,3,16,704]{4,3,2,1,0:T(8,128)(2,1)S(1)}, bf16[2,2,3,16,704]{4,3,2,1,0:T(8,128)(2,1)S(1)}, u32[]{:S(2)}, u32[]{:S(2)}) collective-permute-start(bf16[2,2,3,16,704]{4,3,2,1,0:T(8,128)(2,1)S(1)} %get-tuple-element.261), channel_id=1, source_target_pairs={{0,32},{1,33},{2,34},{3,35},{4,36},{5,37},{6,38},{7,39},{8,40},{9,... | collective-permute-start | bytes 811016 | tf_op jit(solution)/shard_map/ppermute | solution.py:45
  348.6 3.2 collective-permute-start.52
  352.1 4.4 collective-permute-done.51
  356.5 6.1 %collective-permute-done.53 = bf16[2,2,3,16,704]{4,3,2,1,0:T(8,128)(2,1)S(1)} collective-permute-done((bf16[2,2,3,16,704]{4,3,2,1,0:T(8,128)(2,1)S(1)}, bf16[2,2,3,16,704]{4,3,2,1,0:T(8,128)(2,1)S(1)}, u32[]{:S(2)}, u32[]{:S(2)}) %collective-permute-start.53) | collective-permute-done | bytes 270368 | tf_op jit(solution)/shard_map/ppermute | solution.py:45
  362.9 7.0 %shard_map.229 = (bf16[8,128,2048]{2,1,0:T(8,128)(2,1)}, f32[8,2048]{1,0:T(8,128)S(1)}) custom-call(s32[8]{0:T(128)S(1)} %stack.242.chunk.nat, bf16[256,256]{1,0:T(8,128)(2,1)S(1)} %get-tuple-element.193.refs_20_.dq0_ref, bf16[512,256]{1,0:T(8,128)(2,1)S(1)} %get-tuple-element.202.refs_21_.dq1_ref, bf16[256,256]{1,0:T(8,128)(2,1)S(1)} %get-tuple-element.213.refs_22_.dq2_ref, ...), custom_call_target="tpu_custom_call" | custom-call | flops 1000 | bytes 1500000 | tf_op jit(solution)/shard_map/pallas_call | solution.py:136
  371.9 4.6 collective-permute-start.54
  378.7 11.8 %shard_map.228 = (bf16[4,4,2,16,576]{4,3,2,1,0:T(8,128)(2,1)}, bf16[4,4,2,16,576]{4,3,2,1,0:T(8,128)(2,1)}, bf16[4,4,2,16,576]{4,3,2,1,0:T(8,128)(2,1)}, bf16[4,4,2,16,576]{4,3,2,1,0:T(8,128)(2,1)}) custom-call(s32[8]{0:T(128)} %copy-done.52, s32[4]{0:T(128)} %copy-done.43, s32[4]{0:T(128)} %copy-done.45, s32[1]{0:T(128)} %bitcast.16.core, s32[2]{0:T(128)} %copy-done.51, ...), custom_call_target="tpu_custom_call" | custom-call | flops 1000 | bytes 3000000 | tf_op jit(solution)/shard_map/pallas_call | solution.py:136
  395.2 2.5 collective-permute-start.57
  397.7 2.6 collective-permute-done.60
  400.3 2.4 collective-permute-done.61
  402.7 10.1 %collective-permute-done.58 = bf16[4,4,2,16,576]{4,3,2,1,0:T(8,128)(2,1)S(1)} collective-permute-done((bf16[4,4,2,16,576]{4,3,2,1,0:T(8,128)(2,1)}, bf16[4,4,2,16,576]{4,3,2,1,0:T(8,128)(2,1)S(1)}, u32[]{:S(2)}, u32[]{:S(2)}) %collective-permute-start.58) | collective-permute-done | bytes 589856 | tf_op jit(solution)/shard_map/ppermute | solution.py:45
  422.3 3.7 collective-permute-done.59
  427.3 7.4 %collective-permute-done.64 = f32[2,2048]{1,0:T(2,128)S(1)} collective-permute-done((f32[2,2048]{1,0:T(2,128)S(1)}, f32[2,2048]{1,0:T(2,128)S(1)}, u32[]{:S(2)}, u32[]{:S(2)}) %collective-permute-start.64) | collective-permute-done | bytes 16416 | tf_op jit(solution)/shard_map/ppermute | solution.py:45
  450.6 2.7 collective-permute-start.69
  455.6 3.6 collective-permute-done.69
  463.8 2.4 collective-permute-done.75
  470.1 2.9 collective-permute-start.78
  475.6 21.1 %collective-permute-done.81.refs_2_ = bf16[2,2,4,3,16,704]{5,4,3,2,1,0:T(8,128)(2,1)} collective-permute-done((bf16[2,2,4,3,16,704]{5,4,3,2,1,0:T(8,128)(2,1)S(1)}, bf16[2,2,4,3,16,704]{5,4,3,2,1,0:T(8,128)(2,1)}, u32[]{:S(2)}, u32[]{:S(2)}) %collective-permute-start.81) | collective-permute-done | bytes 1081376 | tf_op jit(solution)/shard_map/ppermute | solution.py:45
  496.8 6.4 %shard_map.231 = (f32[128,5632]{1,0:T(8,128)}, f32[128,5632]{1,0:T(8,128)}, f32[5632,128]{1,0:T(8,128)}) custom-call(s32[5]{0:T(128)S(1)} %copy-done.48, s32[4]{0:T(128)S(1)} %copy-done.44, s32[4]{0:T(128)S(1)} %copy-done.46, s32[1]{0:T(128)} %bitcast.16.core, bf16[2,2,4,3,16,704]{5,4,3,2,1,0:T(8,128)(2,1)S(1)} %pad_maximum_fusion.1.refs_0_, ...), custom_call_target="tpu_custom_call" | custom-call | flops 1000 | bytes 1500000 | tf_op jit(solution)/shard_map/pallas_call | solution.py:136
  (425 shorter events, 148.7 us)
Async XLA Ops:
  7.2 64.0 %all-gather.7.cloned.1.call-start = ((), (), s32[]{:S(2)}) async-start(), calls=%async_computation.3 | async-start | bytes 4718592 | tf_op jit(solution)/shard_map/all_gather | solution.py:809
  28.4 104.4 %all-gather.11.cloned.1.call-start = ((), (), s32[]{:S(2)}) async-start(), calls=%async_computation.8 | async-start | bytes 5898240 | tf_op jit(solution)/shard_map/all_gather | solution.py:839
  33.6 22.3 %collective-permute-start.24 = (bf16[4,3,32,704]{3,2,1,0:T(8,128)(2,1)}, bf16[4,3,32,704]{3,2,1,0:T(8,128)(2,1)}, u32[]{:S(2)}, u32[]{:S(2)}) collective-permute-start(bf16[4,3,32,704]{3,2,1,0:T(8,128)(2,1)} %get-tuple-element.153), channel_id=1, source_target_pairs={{0,1},{1,0},{2,3},{3,2},{4,5},{5,4},{6,7},{7,6},{8,9},{9,8},{10,11... | collective-permute-start | bytes 1622024 | tf_op jit(solution)/shard_map/ppermute | solution.py:45
  33.6 18.0 %collective-permute-start.4 = (bf16[8,32,256]{2,1,0:T(8,128)(2,1)S(1)}, bf16[8,32,256]{2,1,0:T(8,128)(2,1)S(1)}, u32[]{:S(2)}, u32[]{:S(2)}) collective-permute-start(bf16[8,32,256]{2,1,0:T(8,128)(2,1)S(1)} %bitcast.209), channel_id=1, source_target_pairs={{0,0},{1,8},{2,1},{3,9},{4,2},{5,10},{6,3},{7,11},{8,4},{9,12},{10... | collective-permute-start | bytes 393224 | tf_op jit(solution)/shard_map/ppermute | solution.py:45
  57.8 19.5 %collective-permute-start.25 = (bf16[2,3,32,704]{3,2,1,0:T(8,128)(2,1)}, bf16[2,3,32,704]{3,2,1,0:T(8,128)(2,1)}, u32[]{:S(2)}, u32[]{:S(2)}) collective-permute-start(bf16[2,3,32,704]{3,2,1,0:T(8,128)(2,1)} %pad_maximum_fusion.7), channel_id=1, source_target_pairs={{0,2},{1,7},{2,4},{3,1},{4,6},{5,3},{6,0},{7,5},{8,10},{9,15},{10,... | collective-permute-start | bytes 811016 | tf_op jit(solution)/shard_map/ppermute | solution.py:45
  60.7 16.6 %collective-permute-start.26 = (bf16[2,3,32,704]{3,2,1,0:T(8,128)(2,1)}, bf16[2,3,32,704]{3,2,1,0:T(8,128)(2,1)}, u32[]{:S(2)}, u32[]{:S(2)}) collective-permute-start(bf16[2,3,32,704]{3,2,1,0:T(8,128)(2,1)} %pad_maximum_fusion.8), channel_id=1, source_target_pairs={{0,6},{1,3},{2,0},{3,5},{4,2},{5,7},{6,4},{7,1},{8,14},{9,11},{10,... | collective-permute-start | bytes 811016 | tf_op jit(solution)/shard_map/ppermute | solution.py:45
  62.6 14.8 %collective-permute-start.27 = (bf16[2,3,32,704]{3,2,1,0:T(8,128)(2,1)}, bf16[2,3,32,704]{3,2,1,0:T(8,128)(2,1)}, u32[]{:S(2)}, u32[]{:S(2)}) collective-permute-start(bf16[2,3,32,704]{3,2,1,0:T(8,128)(2,1)} %pad_maximum_fusion.9), channel_id=1, source_target_pairs={{0,4},{1,5},{2,6},{3,7},{4,0},{5,1},{6,2},{7,3},{8,12},{9,13},{10,... | collective-permute-start | bytes 811016 | tf_op jit(solution)/shard_map/ppermute | solution.py:45
  79.7 122.6 %all-gather.9.cloned.1.call-start = ((), (), s32[]{:S(2)}) async-start(), calls=%async_computation.4 | async-start | bytes 4718592 | tf_op jit(solution)/shard_map/all_gather | solution.py:823
  81.1 281.8 %reduce-scatter.6.cloned.1.call-start = ((), (), s32[]{:S(2)}) async-start(), calls=%async_computation.6 | async-start | bytes 5898240 | tf_op jit(solution)/shard_map/reduce_scatter | solution.py:883
  132.8 56.5 %collective-permute-start.28 = (bf16[4,8,3,32,704]{4,3,2,1,0:T(8,128)(2,1)}, bf16[4,8,3,32,704]{4,3,2,1,0:T(8,128)(2,1)}, u32[]{:S(2)}, u32[]{:S(2)}) collective-permute-start(bf16[4,8,3,32,704]{4,3,2,1,0:T(8,128)(2,1)} %bitcast.183), channel_id=1, source_target_pairs={{0,8},{1,73},{2,10},{3,75},{4,12},{5,77},{6,14},{7,79},{8,64},{9,1... | collective-permute-start | bytes 12976136 | tf_op jit(solution)/shard_map/ppermute | solution.py:45
  145.4 27.4 %collective-permute-start.21 = (bf16[128,2048]{1,0:T(8,128)(2,1)S(1)}, bf16[128,2048]{1,0:T(8,128)(2,1)S(1)}, u32[]{:S(2)}, u32[]{:S(2)}) collective-permute-start(bf16[128,2048]{1,0:T(8,128)(2,1)S(1)} %add_convert_fusion.6), channel_id=1, source_target_pairs={{0,4},{1,5},{2,6},{3,7},{4,0},{5,1},{6,2},{7,3},{8,12},{9,13},{10,... | collective-permute-start | bytes 1572872 | tf_op jit(solution)/shard_map/ppermute | solution.py:45
  148.6 36.3 %collective-permute-start.20 = (bf16[128,2048]{1,0:T(8,128)(2,1)S(1)}, bf16[128,2048]{1,0:T(8,128)(2,1)S(1)}, u32[]{:S(2)}, u32[]{:S(2)}) collective-permute-start(bf16[128,2048]{1,0:T(8,128)(2,1)S(1)} %add_convert_fusion.7), channel_id=1, source_target_pairs={{0,2},{1,7},{2,4},{3,1},{4,6},{5,3},{6,0},{7,5},{8,10},{9,15},{10,... | collective-permute-start | bytes 1572872 | tf_op jit(solution)/shard_map/ppermute | solution.py:45
  151.4 35.6 %collective-permute-start.19 = (bf16[128,2048]{1,0:T(8,128)(2,1)S(1)}, bf16[128,2048]{1,0:T(8,128)(2,1)S(1)}, u32[]{:S(2)}, u32[]{:S(2)}) collective-permute-start(bf16[128,2048]{1,0:T(8,128)(2,1)S(1)} %add_convert_fusion.8), channel_id=1, source_target_pairs={{0,6},{1,3},{2,0},{3,5},{4,2},{5,7},{6,4},{7,1},{8,14},{9,11},{10,... | collective-permute-start | bytes 1572872 | tf_op jit(solution)/shard_map/ppermute | solution.py:45
  158.1 28.9 %collective-permute-start.18 = (bf16[128,2048]{1,0:T(8,128)(2,1)S(1)}, bf16[128,2048]{1,0:T(8,128)(2,1)S(1)}, u32[]{:S(2)}, u32[]{:S(2)}) collective-permute-start(bf16[128,2048]{1,0:T(8,128)(2,1)S(1)} %get-tuple-element.150), channel_id=1, source_target_pairs={{0,1},{1,0},{2,3},{3,2},{4,5},{5,4},{6,7},{7,6},{8,9},{9,8},{10,11... | collective-permute-start | bytes 1572872 | tf_op jit(solution)/shard_map/ppermute | solution.py:45
  188.5 13.8 %collective-permute-start.22 = (bf16[128,2048]{1,0:T(8,128)(2,1)S(1)}, bf16[128,2048]{1,0:T(8,128)(2,1)}, u32[]{:S(2)}, u32[]{:S(2)}) collective-permute-start(bf16[128,2048]{1,0:T(8,128)(2,1)S(1)} %multiply_convert_fusion.refs_0_), channel_id=1, source_target_pairs={{0,1},{1,0},{2,3},{3,2},{4,5},{5,4},{6,7},{7,6},{8,9},{9,8},{10,11... | collective-permute-start | bytes 1572872 | tf_op jit(solution)/shard_map/ppermute | solution.py:45
  198.4 23.5 %collective-permute-start.31 = (bf16[128,2048]{1,0:T(8,128)(2,1)S(1)}, bf16[128,2048]{1,0:T(8,128)(2,1)}, u32[]{:S(2)}, u32[]{:S(2)}) collective-permute-start(bf16[128,2048]{1,0:T(8,128)(2,1)S(1)} %multiply_convert_fusion.refs_0_), channel_id=1, source_target_pairs={{0,4},{1,5},{2,6},{3,7},{4,0},{5,1},{6,2},{7,3},{8,12},{9,13},{10,... | collective-permute-start | bytes 1572872 | tf_op jit(solution)/shard_map/ppermute | solution.py:45
  200.1 21.8 %collective-permute-start.30 = (bf16[128,2048]{1,0:T(8,128)(2,1)S(1)}, bf16[128,2048]{1,0:T(8,128)(2,1)}, u32[]{:S(2)}, u32[]{:S(2)}) collective-permute-start(bf16[128,2048]{1,0:T(8,128)(2,1)S(1)} %multiply_convert_fusion.refs_0_), channel_id=1, source_target_pairs={{0,6},{1,3},{2,0},{3,5},{4,2},{5,7},{6,4},{7,1},{8,14},{9,11},{10,... | collective-permute-start | bytes 1572872 | tf_op jit(solution)/shard_map/ppermute | solution.py:45
  253.1 26.9 %collective-permute-start.36 = (bf16[128,2048]{1,0:T(8,128)(2,1)}, bf16[128,2048]{1,0:T(8,128)(2,1)}, u32[]{:S(2)}, u32[]{:S(2)}) collective-permute-start(bf16[128,2048]{1,0:T(8,128)(2,1)} %fusion.11), channel_id=1, source_target_pairs={{0,6},{1,3},{2,0},{3,5},{4,2},{5,7},{6,4},{7,1},{8,14},{9,11},{10,... | collective-permute-start | bytes 1572872 | tf_op jit(solution)/shard_map/ppermute | solution.py:45
  255.9 24.2 %collective-permute-start.38 = (bf16[128,2048]{1,0:T(8,128)(2,1)}, bf16[128,2048]{1,0:T(8,128)(2,1)}, u32[]{:S(2)}, u32[]{:S(2)}) collective-permute-start(bf16[128,2048]{1,0:T(8,128)(2,1)} %get-tuple-element.264), channel_id=1, source_target_pairs={{0,4},{1,5},{2,6},{3,7},{4,0},{5,1},{6,2},{7,3},{8,12},{9,13},{10,... | collective-permute-start | bytes 1572872 | tf_op jit(solution)/shard_map/ppermute | solution.py:45
  256.6 23.5 %collective-permute-start.37 = (bf16[128,2048]{1,0:T(8,128)(2,1)}, bf16[128,2048]{1,0:T(8,128)(2,1)}, u32[]{:S(2)}, u32[]{:S(2)}) collective-permute-start(bf16[128,2048]{1,0:T(8,128)(2,1)} %get-tuple-element.265), channel_id=1, source_target_pairs={{0,2},{1,7},{2,4},{3,1},{4,6},{5,3},{6,0},{7,5},{8,10},{9,15},{10,... | collective-permute-start | bytes 1572872 | tf_op jit(solution)/shard_map/ppermute | solution.py:45
  280.1 112.6 %reduce-scatter.4.cloned.1.call-start = ((), (), s32[]{:S(2)}) async-start(), calls=%async_computation.5 | async-start | bytes 4718592 | tf_op jit(solution)/shard_map/reduce_scatter | solution.py:884
  280.7 138.6 %all-gather.13.cloned.1.call-start = ((), (), s32[]{:S(2)}) async-start(), calls=%async_computation.9 | async-start | bytes 1114112 | tf_op jit(solution)/shard_map/all_gather | solution.py:925
  280.7 24.0 %collective-permute-start.45 = (bf16[4,2,2,3,16,704]{5,4,3,2,1,0:T(8,128)(2,1)}, bf16[4,2,2,3,16,704]{5,4,3,2,1,0:T(8,128)(2,1)S(1)}, u32[]{:S(2)}, u32[]{:S(2)}) collective-permute-start(bf16[4,2,2,3,16,704]{5,4,3,2,1,0:T(8,128)(2,1)} %get-tuple-element.188), channel_id=1, source_target_pairs={{0,8},{1,73},{2,10},{3,75},{4,12},{5,77},{6,14},{7,79},{8,64},{9,1... | collective-permute-start | bytes 3244040 | tf_op jit(solution)/shard_map/ppermute | solution.py:45
  286.6 14.6 %collective-permute-start.41 = (bf16[128,2048]{1,0:T(8,128)(2,1)S(1)}, bf16[128,2048]{1,0:T(8,128)(2,1)S(1)}, u32[]{:S(2)}, u32[]{:S(2)}) collective-permute-start(bf16[128,2048]{1,0:T(8,128)(2,1)S(1)} %get-tuple-element.253.refs_1_.refs_8_), channel_id=1, source_target_pairs={{0,6},{1,3},{2,0},{3,5},{4,2},{5,7},{6,4},{7,1},{8,14},{9,11},{10,... | collective-permute-start | bytes 1572872 | tf_op jit(solution)/shard_map/ppermute | solution.py:45
  288.9 12.7 %collective-permute-start.40 = (bf16[128,2048]{1,0:T(8,128)(2,1)S(1)}, bf16[128,2048]{1,0:T(8,128)(2,1)S(1)}, u32[]{:S(2)}, u32[]{:S(2)}) collective-permute-start(bf16[128,2048]{1,0:T(8,128)(2,1)S(1)} %get-tuple-element.253.refs_1_.refs_8_), channel_id=1, source_target_pairs={{0,2},{1,7},{2,4},{3,1},{4,6},{5,3},{6,0},{7,5},{8,10},{9,15},{10,... | collective-permute-start | bytes 1572872 | tf_op jit(solution)/shard_map/ppermute | solution.py:45
  303.5 28.4 %collective-permute-start.47 = (bf16[4,2,2,3,16,704]{5,4,3,2,1,0:T(8,128)(2,1)S(1)}, bf16[4,2,2,3,16,704]{5,4,3,2,1,0:T(8,128)(2,1)S(1)}, u32[]{:S(2)}, u32[]{:S(2)}) collective-permute-start(bf16[4,2,2,3,16,704]{5,4,3,2,1,0:T(8,128)(2,1)S(1)} %copy-done.78), channel_id=1, source_target_pairs={{0,72},{1,9},{2,74},{3,11},{4,76},{5,13},{6,78},{7,15},{8,0},{9,65... | collective-permute-start | bytes 3244040 | tf_op jit(solution)/shard_map/ppermute | solution.py:45
  305.1 34.3 %collective-permute-start.48 = (bf16[4,2,2,3,16,704]{5,4,3,2,1,0:T(8,128)(2,1)S(1)}, bf16[4,2,2,3,16,704]{5,4,3,2,1,0:T(8,128)(2,1)S(1)}, u32[]{:S(2)}, u32[]{:S(2)}) collective-permute-start(bf16[4,2,2,3,16,704]{5,4,3,2,1,0:T(8,128)(2,1)S(1)} %add_convert_fusion.1), channel_id=1, source_target_pairs={{0,8},{1,73},{2,10},{3,75},{4,12},{5,77},{6,14},{7,79},{8,64},{9,1... | collective-permute-start | bytes 3244040 | tf_op jit(solution)/shard_map/ppermute | solution.py:45
  307.2 20.2 %collective-permute-start.44 = (bf16[128,2048]{1,0:T(8,128)(2,1)S(1)}, bf16[128,2048]{1,0:T(8,128)(2,1)S(1)}, u32[]{:S(2)}, u32[]{:S(2)}) collective-permute-start(bf16[128,2048]{1,0:T(8,128)(2,1)S(1)} %get-tuple-element.253.refs_1_.refs_8_), channel_id=1, source_target_pairs={{0,4},{1,5},{2,6},{3,7},{4,0},{5,1},{6,2},{7,3},{8,12},{9,13},{10,... | collective-permute-start | bytes 1572872 | tf_op jit(solution)/shard_map/ppermute | solution.py:45
  339.3 12.5 %collective-permute-start.49 = (bf16[2048,64]{1,0:T(8,128)(2,1)S(1)}, bf16[2048,64]{1,0:T(8,128)(2,1)S(1)}, u32[]{:S(2)}, u32[]{:S(2)}) collective-permute-start(bf16[2048,64]{1,0:T(8,128)(2,1)S(1)} %get-tuple-element.217), channel_id=1, source_target_pairs={{0,1},{1,0},{2,3},{3,2},{4,5},{5,4},{6,7},{7,6},{8,9},{9,8},{10,11... | collective-permute-start | bytes 786440 | tf_op jit(solution)/shard_map/ppermute | solution.py:45
  340.0 16.5 %collective-permute-start.51 = (bf16[2,2,3,16,704]{4,3,2,1,0:T(8,128)(2,1)S(1)}, bf16[2,2,3,16,704]{4,3,2,1,0:T(8,128)(2,1)S(1)}, u32[]{:S(2)}, u32[]{:S(2)}) collective-permute-start(bf16[2,2,3,16,704]{4,3,2,1,0:T(8,128)(2,1)S(1)} %get-tuple-element.261), channel_id=1, source_target_pairs={{0,32},{1,33},{2,34},{3,35},{4,36},{5,37},{6,38},{7,39},{8,40},{9,... | collective-permute-start | bytes 811016 | tf_op jit(solution)/shard_map/ppermute | solution.py:45
  348.6 14.0 %collective-permute-start.53 = (bf16[2,2,3,16,704]{4,3,2,1,0:T(8,128)(2,1)S(1)}, bf16[2,2,3,16,704]{4,3,2,1,0:T(8,128)(2,1)S(1)}, u32[]{:S(2)}, u32[]{:S(2)}) collective-permute-start(bf16[2,2,3,16,704]{4,3,2,1,0:T(8,128)(2,1)S(1)} %get-tuple-element.262), channel_id=1, source_target_pairs={{0,16},{1,49},{2,18},{3,51},{4,20},{5,53},{6,22},{7,55},{8,24},{9,... | collective-permute-start | bytes 811016 | tf_op jit(solution)/shard_map/ppermute | solution.py:45
  348.6 14.0 %collective-permute-start.52 = (bf16[2,2,3,16,704]{4,3,2,1,0:T(8,128)(2,1)S(1)}, bf16[2,2,3,16,704]{4,3,2,1,0:T(8,128)(2,1)S(1)}, u32[]{:S(2)}, u32[]{:S(2)}) collective-permute-start(bf16[2,2,3,16,704]{4,3,2,1,0:T(8,128)(2,1)S(1)} %get-tuple-element.263), channel_id=1, source_target_pairs={{0,48},{1,17},{2,50},{3,19},{4,52},{5,21},{6,54},{7,23},{8,56},{9,... | collective-permute-start | bytes 811016 | tf_op jit(solution)/shard_map/ppermute | solution.py:45
  370.6 95.6 %reduce-scatter.8.cloned.1.call-start = ((), (), s32[]{:S(2)}) async-start(), calls=%async_computation.7 | async-start | bytes 4718592 | tf_op jit(solution)/shard_map/reduce_scatter | solution.py:933
  371.9 18.6 %collective-permute-start.54 = (bf16[2,2,3,16,704]{4,3,2,1,0:T(8,128)(2,1)S(1)}, bf16[2,2,3,16,704]{4,3,2,1,0:T(8,128)(2,1)S(1)}, u32[]{:S(2)}, u32[]{:S(2)}) collective-permute-start(bf16[2,2,3,16,704]{4,3,2,1,0:T(8,128)(2,1)S(1)} %get-tuple-element.258), channel_id=1, source_target_pairs={{0,64},{1,65},{2,66},{3,67},{4,68},{5,69},{6,70},{7,71},{8,72},{9,... | collective-permute-start | bytes 811016 | tf_op jit(solution)/shard_map/ppermute | solution.py:45
  376.5 14.0 %collective-permute-start.56 = (bf16[2,2,3,16,704]{4,3,2,1,0:T(8,128)(2,1)S(1)}, bf16[2,2,3,16,704]{4,3,2,1,0:T(8,128)(2,1)S(1)}, u32[]{:S(2)}, u32[]{:S(2)}) collective-permute-start(bf16[2,2,3,16,704]{4,3,2,1,0:T(8,128)(2,1)S(1)} %get-tuple-element.259), channel_id=1, source_target_pairs={{0,8},{1,73},{2,10},{3,75},{4,12},{5,77},{6,14},{7,79},{8,64},{9,1... | collective-permute-start | bytes 811016 | tf_op jit(solution)/shard_map/ppermute | solution.py:45
  376.7 14.8 %collective-permute-start.55 = (bf16[2,2,3,16,704]{4,3,2,1,0:T(8,128)(2,1)S(1)}, bf16[2,2,3,16,704]{4,3,2,1,0:T(8,128)(2,1)S(1)}, u32[]{:S(2)}, u32[]{:S(2)}) collective-permute-start(bf16[2,2,3,16,704]{4,3,2,1,0:T(8,128)(2,1)S(1)} %get-tuple-element.260), channel_id=1, source_target_pairs={{0,72},{1,9},{2,74},{3,11},{4,76},{5,13},{6,78},{7,15},{8,0},{9,65... | collective-permute-start | bytes 811016 | tf_op jit(solution)/shard_map/ppermute | solution.py:45
  394.9 19.0 %collective-permute-start.62 = (bf16[2,3,16,704]{3,2,1,0:T(8,128)(2,1)S(1)}, bf16[2,3,16,704]{3,2,1,0:T(8,128)(2,1)S(1)}, u32[]{:S(2)}, u32[]{:S(2)}) collective-permute-start(bf16[2,3,16,704]{3,2,1,0:T(8,128)(2,1)S(1)} %get-tuple-element.284), channel_id=1, source_target_pairs={{0,4},{1,5},{2,6},{3,7},{4,0},{5,1},{6,2},{7,3},{8,12},{9,13},{10,... | collective-permute-start | bytes 405512 | tf_op jit(solution)/shard_map/ppermute | solution.py:45
  395.2 27.1 %collective-permute-start.57 = (bf16[4,4,2,16,576]{4,3,2,1,0:T(8,128)(2,1)}, bf16[4,4,2,16,576]{4,3,2,1,0:T(8,128)(2,1)S(1)}, u32[]{:S(2)}, u32[]{:S(2)}) collective-permute-start(bf16[4,4,2,16,576]{4,3,2,1,0:T(8,128)(2,1)} %get-tuple-element.229), channel_id=1, source_target_pairs={{0,48},{1,17},{2,50},{3,19},{4,52},{5,21},{6,54},{7,23},{8,56},{9,... | collective-permute-start | bytes 1769480 | tf_op jit(solution)/shard_map/ppermute | solution.py:45
  397.7 15.2 %collective-permute-start.58 = (bf16[4,4,2,16,576]{4,3,2,1,0:T(8,128)(2,1)}, bf16[4,4,2,16,576]{4,3,2,1,0:T(8,128)(2,1)S(1)}, u32[]{:S(2)}, u32[]{:S(2)}) collective-permute-start(bf16[4,4,2,16,576]{4,3,2,1,0:T(8,128)(2,1)} %get-tuple-element.232), channel_id=1, source_target_pairs={{0,16},{1,49},{2,18},{3,51},{4,20},{5,53},{6,22},{7,55},{8,24},{9,... | collective-permute-start | bytes 1769480 | tf_op jit(solution)/shard_map/ppermute | solution.py:45
  417.2 23.2 %collective-permute-start.79 = (bf16[2,4,3,16,704]{4,3,2,1,0:T(8,128)(2,1)S(1)}, bf16[2,4,3,16,704]{4,3,2,1,0:T(8,128)(2,1)}, u32[]{:S(2)}, u32[]{:S(2)}) collective-permute-start(bf16[2,4,3,16,704]{4,3,2,1,0:T(8,128)(2,1)S(1)} %get-tuple-element.270), channel_id=1, source_target_pairs={{0,64},{1,65},{2,66},{3,67},{4,68},{5,69},{6,70},{7,71},{8,72},{9,... | collective-permute-start | bytes 1622024 | tf_op jit(solution)/shard_map/ppermute | solution.py:45
  420.7 14.0 %collective-permute-start.64 = (f32[2,2048]{1,0:T(2,128)S(1)}, f32[2,2048]{1,0:T(2,128)S(1)}, u32[]{:S(2)}, u32[]{:S(2)}) collective-permute-start(f32[2,2048]{1,0:T(2,128)S(1)} %slice.317), channel_id=1, source_target_pairs={{0,64},{1,65},{2,66},{3,67},{4,68},{5,69},{6,70},{7,71},{8,72},{9,... | collective-permute-start | bytes 49160 | tf_op jit(solution)/shard_map/ppermute | solution.py:45
  441.6 22.1 %collective-permute-start.80 = (bf16[2,2,4,3,16,704]{5,4,3,2,1,0:T(8,128)(2,1)S(1)}, bf16[2,2,4,3,16,704]{5,4,3,2,1,0:T(8,128)(2,1)S(1)}, u32[]{:S(2)}, u32[]{:S(2)}) collective-permute-start(bf16[2,2,4,3,16,704]{5,4,3,2,1,0:T(8,128)(2,1)S(1)} %pad_maximum_fusion.1.refs_0_), channel_id=1, source_target_pairs={{0,16},{1,49},{2,18},{3,51},{4,20},{5,53},{6,22},{7,55},{8,24},{9,... | collective-permute-start | bytes 3244040 | tf_op jit(solution)/shard_map/ppermute | solution.py:45
  444.2 19.5 %collective-permute-start.74 = (f32[2,2048]{1,0:T(2,128)S(1)}, f32[2,2048]{1,0:T(2,128)S(1)}, u32[]{:S(2)}, u32[]{:S(2)}) collective-permute-start(f32[2,2048]{1,0:T(2,128)S(1)} %add.347), channel_id=1, source_target_pairs={{0,16},{1,49},{2,18},{3,51},{4,20},{5,53},{6,22},{7,55},{8,24},{9,... | collective-permute-start | bytes 49160 | tf_op jit(solution)/shard_map/ppermute | solution.py:45
  461.6 35.2 %collective-permute-start.81 = (bf16[2,2,4,3,16,704]{5,4,3,2,1,0:T(8,128)(2,1)S(1)}, bf16[2,2,4,3,16,704]{5,4,3,2,1,0:T(8,128)(2,1)}, u32[]{:S(2)}, u32[]{:S(2)}) collective-permute-start(bf16[2,2,4,3,16,704]{5,4,3,2,1,0:T(8,128)(2,1)S(1)} %pad_maximum_fusion.1.refs_0_), channel_id=1, source_target_pairs={{0,48},{1,17},{2,50},{3,19},{4,52},{5,21},{6,54},{7,23},{8,56},{9,... | collective-permute-start | bytes 3244040 | tf_op jit(solution)/shard_map/ppermute | solution.py:45
  466.2 30.6 %collective-permute-start.82 = (bf16[2,2,4,3,16,704]{5,4,3,2,1,0:T(8,128)(2,1)S(1)}, bf16[2,2,4,3,16,704]{5,4,3,2,1,0:T(8,128)(2,1)}, u32[]{:S(2)}, u32[]{:S(2)}) collective-permute-start(bf16[2,2,4,3,16,704]{5,4,3,2,1,0:T(8,128)(2,1)S(1)} %collective-permute-done.80.refs_1_), channel_id=1, source_target_pairs={{0,16},{1,49},{2,18},{3,51},{4,20},{5,53},{6,22},{7,55},{8,24},{9,... | collective-permute-start | bytes 3244040 | tf_op jit(solution)/shard_map/ppermute | solution.py:45
  470.1 33.1 %collective-permute-start.78 = (bf16[2,2,4,16,576]{4,3,2,1,0:T(8,128)(2,1)S(1)}, bf16[2,2,4,16,576]{4,3,2,1,0:T(8,128)(2,1)S(1)}, u32[]{:S(2)}, u32[]{:S(2)}) collective-permute-start(bf16[2,2,4,16,576]{4,3,2,1,0:T(8,128)(2,1)S(1)} %pad_maximum_fusion.5.refs_0_), channel_id=1, source_target_pairs={{0,32},{1,33},{2,34},{3,35},{4,36},{5,37},{6,38},{7,39},{8,40},{9,... | collective-permute-start | bytes 884744 | tf_op jit(solution)/shard_map/ppermute | solution.py:45
  473.0 31.1 %collective-permute-start.77 = (bf16[2,2,4,16,576]{4,3,2,1,0:T(8,128)(2,1)S(1)}, bf16[2,2,4,16,576]{4,3,2,1,0:T(8,128)(2,1)S(1)}, u32[]{:S(2)}, u32[]{:S(2)}) collective-permute-start(bf16[2,2,4,16,576]{4,3,2,1,0:T(8,128)(2,1)S(1)} %pad_maximum_fusion.5.refs_0_), channel_id=1, source_target_pairs={{0,48},{1,17},{2,50},{3,19},{4,52},{5,21},{6,54},{7,23},{8,56},{9,... | collective-permute-start | bytes 884744 | tf_op jit(solution)/shard_map/ppermute | solution.py:45
  474.6 29.5 %collective-permute-start.76 = (bf16[2,2,4,16,576]{4,3,2,1,0:T(8,128)(2,1)S(1)}, bf16[2,2,4,16,576]{4,3,2,1,0:T(8,128)(2,1)S(1)}, u32[]{:S(2)}, u32[]{:S(2)}) collective-permute-start(bf16[2,2,4,16,576]{4,3,2,1,0:T(8,128)(2,1)S(1)} %pad_maximum_fusion.5.refs_0_), channel_id=1, source_target_pairs={{0,16},{1,49},{2,18},{3,51},{4,20},{5,53},{6,22},{7,55},{8,24},{9,... | collective-permute-start | bytes 884744 | tf_op jit(solution)/shard_map/ppermute | solution.py:45
  (123 other events, 2050.1 us)
Sparse Core Ops, SparseCore 0:
  28.5 32.7 all-gather.6
  79.8 52.9 all-gather.10
  134.5 55.2 all-gather.8
  280.2 52.8 reduce-scatter.5
  335.4 38.1 reduce-scatter.3
  375.1 32.3 all-gather.12
  409.9 39.4 reduce-scatter.7

commit v10 on v9

--- a/solution.py
+++ b/solution.py
@@ -849,7 +849,7 @@
         at = after(query_place, *sums[1:]) if g == 0 else query_place
         attended[g], mine, peer = attend(g, at, key_slot, queries, keys, values, w_out)
         peer = swap(peer)
-        if g == 1:
+        if g == 2:
             mlp_half_rows = after(mlp_half_rows, peer)
             mlp_other_rows = step(mlp_half_rows, "y", 1)
             w_mlp = place_mlp(slot, halves, mlp_half_rows, mlp_other_rows)
@@ -893,7 +893,7 @@
         got = exchange_z(part[0], part[1], part[2], part[3])
         mine = jnp.stack([each[0] for each in got])
         other = swap(jnp.stack([got[p][1] for p in (0, 2, 1, 3)]))
-        return jnp.stack([mine, other]), other
+        return jnp.stack([mine, other]), other, got[1]
 
 
     def back(start, parts, sums, last):
@@ -928,33 +928,32 @@
     )
     attn_outs = after(attn_outs, low)
     low, high = after((low, high), branch)
-    mlp_sums, mlp_swapped = resplit_back([low[0], low[1], high[0], high[1]])
+    mlp_sums, mlp_swapped, _ = resplit_back([low[0], low[1], high[0], high[1]])
     attn_partial = after(attn_partial, attn_outs[0])
     normed_attn_grad = lax.psum_scatter(attn_partial, "blk", scatter_dimension=0, axis_index_groups=ZC_GROUPS)
 
     layer_out = (residual + after(branch, attn_outs[0]).astype(F32)).astype(BF)[None]
-    gain_grads = jnp.sum(after(gain_grads, mlp_swapped), axis=0)[:2]
+    mlp_across = across(mlp_sums, "y")
+    gain_grads = jnp.sum(after(gain_grads, mlp_across), axis=0)[:2]
     gain_grads = gain_grads + across(gain_grads, "y")
-    mlp_across = across(mlp_sums, "y")
     mlp_sums = jnp.stack([mlp_sums, mlp_across])
     mlp_first, mlp_second = step(mlp_sums, "x", 1), step(mlp_sums, "x", -1)
     attn_sums = ring_scatter(*attn_outs, "x", attn_outs[0]).astype(BF)
+    attn_sums = ring_scatter(attn_sums[0], attn_sums[2], attn_sums[3], attn_sums[1], "y").astype(BF)
     attn_sums = after(attn_sums, gain_grads)
     gain_grads = gain_grads + across(gain_grads, "x")
-    attn_sums = ring_scatter(attn_sums[0], attn_sums[2], attn_sums[3], attn_sums[1], "y").astype(BF)
-    attn_sums = after(attn_sums, gain_grads)
-    gain_grads = gain_grads + step(gain_grads, "x", 1)
+    qkv_sums, _, arrived = resplit_back(attn_sums[..., QUERY:])
     out_sums = send(
-        attn_sums[..., :QUERY], lambda yh, x, yl, z, c: (yh, x, z // 2, 2 * (z % 2) + c, yl)
-    )
-    qkv_sums, _ = resplit_back(attn_sums[..., QUERY:])
+        after(attn_sums[..., :QUERY], arrived), lambda yh, x, yl, z, c: (yh, x, z // 2, 2 * (z % 2) + c, yl)
+    )
     attn_sums = jnp.concatenate([out_sums.reshape(2, 4, 16, QUERY), qkv_sums], axis=-1)
     tokens_grad = (
         residual_grad + norm_back(rows_in, scale_attn, gain_one, after(normed_attn_grad, attn_sums).astype(F32))
     ).astype(BF)[None]
     attn_across = across(attn_sums, "y")
-    mlp_sums = (mlp_sums, mlp_first, mlp_second, step(after(mlp_first, attn_across), "x", 1))
-    attn_sums = ring_gather(after(jnp.stack([attn_sums, attn_across]), tokens_grad), "x")
+    mlp_sums = (mlp_sums, mlp_first, mlp_second, step(after(mlp_first, mlp_second, attn_across), "x", 1))
+    attn_sums = ring_gather(after(jnp.stack([attn_sums, attn_across]), tokens_grad, gain_grads), "x")
+    gain_grads = gain_grads + step(gain_grads, "x", 1)
     gate_grad, up_grad, down_grad = finish_mlp(spots, xs, yhs, core, mlp_sums)
     query_grad, key_grad, value_grad, output_grad = finish_attn(spots, xs, yhs, core, attn_sums)
     return (

time: 522 us -> 532 us (1.019)
  Pallas kernels: 159 us -> 174 us
  waiting for transfers between devices: 170 us -> 163 us
  starting transfers between devices: 112 us -> 118 us
    pallas_call x20, Pallas kernels: 159 us -> 174 us  [call(): pl.pallas_call(body, grid_spec=pltpu.PrefetchScalarGridSpec(num_scalar_pr...]
    ppermute x83, starting transfers between devices: 112 us -> 118 us  [send(): return lax.ppermute(value, BOTH, pairs)]
    unnamed x165 -> x169, local copies, waits for them, and re-layouts: 15.9 us -> 15.9 us
  transfers between devices with their start and end apart: 90 -> 90, of which waited for: 37 -> 37; matrix products, arithmetic and copies ran while one was open for 7% -> 7% of each run, Pallas kernels for 27% -> 29%
where the time goes in v10:
time: 532 us; the launch traced here: 525 us
  Pallas kernels  174 us (33%)
  waiting for transfers between devices  163 us (31%)
  starting transfers between devices  118 us (22%)
  other arithmetic  30.9 us (6%)
  local copies, waits for them, and re-layouts  23.1 us (4%)
  between operations  16 us (3%)
    pallas_call x20, Pallas kernels, call(): pl.pallas_call(body, grid_spec=pltpu.PrefetchScalarGridSpec(num_scalar_pr...  174 us
    ppermute x83, waiting for transfers between devices, send(): return lax.ppermute(value, BOTH, pairs)  140 us
    ppermute x83, starting transfers between devices, send(): return lax.ppermute(value, BOTH, pairs)  118 us
    all_gather x1, waiting for transfers between devices, on_device(): lax.all_gather(exchange(mlp_mine, mlp_other, kv_own), 'batch', axis=0, ax...  22 us
    unnamed x169, local copies, waits for them, and re-layouts  15.9 us
  transfers between devices with their start and end apart: 90, of which 37 were waited for; matrix products, arithmetic and copies ran while one was open for 7% of the time, Pallas kernels for 29%

profile of v10, /device:TPU:24, one launch (start us, length us, event | category | flops | bytes accessed | tf_op | source)
XLA Modules:
  0.0 524.5 jit_solution(8856579301749886475)
XLA Ops:
  22.2 3.7 collective-permute-done.3
  29.9 2.9 shard_map.220
  33.7 3.9 collective-permute-start.4
  37.8 3.1 collective-permute-start.7
  44.0 3.3 collective-permute-done.7
  47.3 3.3 collective-permute-done.6
  71.3 6.1 %shard_map.214 = (bf16[1024,256]{1,0:T(8,128)(2,1)S(1)}, bf16[2,1024,64]{2,1,0:T(8,128)(2,1)S(1)}) custom-call(s32[8]{0:T(128)S(1)} %stack.242.chunk.nat, bf16[1024,2048]{1,0:T(8,128)(2,1)} %all-gather.7.cloned.1.call-done.refs_0_.refs_1_.refs_2_.refs_3_.refs_4_.refs_5_.refs_6_.refs_7_, ...), custom_call_target="tpu_custom_call" | custom-call | flops 1000 | bytes 1500000 | tf_op jit(solution)/shard_map/pallas_call | solution.py:136
  81.3 7.8 %collective-permute-done.12.other_ref = bf16[4,8,32,256]{3,2,1,0:T(8,128)(2,1)S(1)} collective-permute-done((bf16[4,8,32,256]{3,2,1,0:T(8,128)(2,1)S(1)}, bf16[4,8,32,256]{3,2,1,0:T(8,128)(2,1)S(1)}, u32[]{:S(2)}, u32[]{:S(2)}) %collective-permute-start.12) | collective-permute-done | bytes 524320 | tf_op jit(solution)/shard_map/ppermute | solution.py:45
  89.8 7.4 %collective-permute-done.13 = bf16[2,1024,64]{1,2,0:T(8,128)(2,1)S(1)} collective-permute-done((bf16[2,1024,64]{1,2,0:T(8,128)(2,1)S(1)}, bf16[2,1024,64]{1,2,0:T(8,128)(2,1)S(1)}, u32[]{:S(2)}, u32[]{:S(2)}) %collective-permute-start.13) | collective-permute-done | bytes 262176 | tf_op jit(solution)/shard_map/ppermute | solution.py:45
  99.8 8.3 %shard_map.217 = (bf16[256,256]{1,0:T(8,128)(2,1)S(1)}, bf16[128,2048]{1,0:T(8,128)(2,1)S(1)}, bf16[128,2048]{1,0:T(8,128)(2,1)S(1)}) custom-call(s32[8]{0:T(128)S(1)} %bitcast.189, s32[16]{0:T(128)S(1)} %select_reduce_fusion.1.key_slot, bf16[1024,256]{1,0:T(8,128)(2,1)S(1)} %get-tuple-element.139.q_ref.refs_0_, ...), custom_call_target="tpu_custom_call" | custom-call | flops 1000 | bytes 1800000 | tf_op jit(solution)/shard_map/pallas_call | solution.py:136
  110.8 22.0 %all-gather.11.cloned.1.call-done = bf16[32,3,32,704]{3,2,1,0:T(8,128)(2,1)} async-done(((bf16[8,3,32,704]{3,2,1,0:T(8,128)(2,1)}), bf16[32,3,32,704]{3,2,1,0:T(8,128)(2,1)}) %all-gather.11.cloned.1.call-update) | async-done | bytes 4325392 | tf_op jit(solution)/shard_map/all_gather | solution.py:839
  133.3 6.4 %shard_map.218 = (bf16[256,256]{1,0:T(8,128)(2,1)S(1)}, bf16[128,2048]{1,0:T(8,128)(2,1)S(1)}, bf16[128,2048]{1,0:T(8,128)(2,1)S(1)}) custom-call(s32[8]{0:T(128)S(1)} %bitcast.190, s32[16]{0:T(128)S(1)} %select_reduce_fusion.1.key_slot, bf16[1024,256]{1,0:T(8,128)(2,1)S(1)} %get-tuple-element.139.q_ref.refs_0_, ...), custom_call_target="tpu_custom_call" | custom-call | flops 1000 | bytes 1800000 | tf_op jit(solution)/shard_map/pallas_call | solution.py:136
  140.4 5.6 %shard_map.216 = (bf16[256,256]{1,0:T(8,128)(2,1)S(1)}, bf16[128,2048]{1,0:T(8,128)(2,1)S(1)}, bf16[128,2048]{1,0:T(8,128)(2,1)S(1)}) custom-call(s32[8]{0:T(128)S(1)} %bitcast.191, s32[16]{0:T(128)S(1)} %select_reduce_fusion.1.key_slot, bf16[1024,256]{1,0:T(8,128)(2,1)S(1)} %get-tuple-element.139.q_ref.refs_0_, ...), custom_call_target="tpu_custom_call" | custom-call | flops 1000 | bytes 1800000 | tf_op jit(solution)/shard_map/pallas_call | solution.py:136
  146.7 6.6 %collective-permute-start.21 = (bf16[128,2048]{1,0:T(8,128)(2,1)S(1)}, bf16[128,2048]{1,0:T(8,128)(2,1)S(1)}, u32[]{:S(2)}, u32[]{:S(2)}) collective-permute-start(bf16[128,2048]{1,0:T(8,128)(2,1)S(1)} %add_convert_fusion.6), channel_id=1, source_target_pairs={{0,4},{1,5},{2,6},{3,7},{4,0},{5,1},{6,2},{7,3},{8,12},{9,13},{10,... | collective-permute-start | bytes 1572872 | tf_op jit(solution)/shard_map/ppermute | solution.py:45
  154.7 3.3 collective-permute-start.19
  158.0 7.1 %shard_map.219 = (bf16[256,256]{1,0:T(8,128)(2,1)S(1)}, bf16[128,2048]{1,0:T(8,128)(2,1)S(1)}, bf16[128,2048]{1,0:T(8,128)(2,1)S(1)}) custom-call(s32[8]{0:T(128)S(1)} %bitcast.192, s32[16]{0:T(128)S(1)} %select_reduce_fusion.1.key_slot, bf16[1024,256]{1,0:T(8,128)(2,1)S(1)} %get-tuple-element.139.q_ref.refs_0_, ...), custom_call_target="tpu_custom_call" | custom-call | flops 1000 | bytes 1800000 | tf_op jit(solution)/shard_map/pallas_call | solution.py:136
  165.2 12.0 %collective-permute-done.21 = bf16[128,2048]{1,0:T(8,128)(2,1)S(1)} collective-permute-done((bf16[128,2048]{1,0:T(8,128)(2,1)S(1)}, bf16[128,2048]{1,0:T(8,128)(2,1)S(1)}, u32[]{:S(2)}, u32[]{:S(2)}) %collective-permute-start.21) | collective-permute-done | bytes 524320 | tf_op jit(solution)/shard_map/ppermute | solution.py:45
  177.2 11.0 %collective-permute-done.20 = bf16[128,2048]{1,0:T(8,128)(2,1)S(1)} collective-permute-done((bf16[128,2048]{1,0:T(8,128)(2,1)S(1)}, bf16[128,2048]{1,0:T(8,128)(2,1)S(1)}, u32[]{:S(2)}, u32[]{:S(2)}) %collective-permute-start.20) | collective-permute-done | bytes 524320 | tf_op jit(solution)/shard_map/ppermute | solution.py:45
  189.6 8.4 %shard_map.221 = bf16[3,2,8,128,704]{4,3,2,1,0:T(8,128)(2,1)} custom-call(s32[8]{0:T(128)S(1)} %stack.254.slot, s32[2]{0:T(128)S(1)} %pad_add_fusion.2.halves, bf16[4,8,3,32,704]{4,3,2,1,0:T(8,128)(2,1)S(1)} %bitcast.188, bf16[4,8,3,32,704]{4,3,2,1,0:T(8,128)(2,1)} %collective-permute-done.28.other_ref), custom_call_target="tpu_custom_call" | custom-call | flops 1000 | bytes 1800000 | tf_op jit(solution)/shard_map/pallas_call | solution.py:136
  202.4 18.7 %shard_map.222 = (bf16[1024,704]{1,0:T(8,128)(2,1)S(1)}, bf16[1024,704]{1,0:T(8,128)(2,1)}, bf16[1024,704]{1,0:T(8,128)(2,1)}, bf16[128,2048]{1,0:T(8,128)(2,1)S...) custom-call(s32[8]{0:T(128)S(1)} %stack.242.chunk.nat, ...), custom_call_target="tpu_custom_call" | custom-call | flops 1000 | bytes 5400000 | tf_op jit(solution)/shard_map/pallas_call | solution.py:136
  222.5 8.7 %collective-permute-start.34 = (bf16[128,2048]{1,0:T(8,128)(2,1)}, bf16[128,2048]{1,0:T(8,128)(2,1)S(1)}, u32[]{:S(2)}, u32[]{:S(2)}) collective-permute-start(bf16[128,2048]{1,0:T(8,128)(2,1)} %collective-permute-done.31.refs_2_.refs_6_), channel_id=1, source_target_pairs={{0,1},{1,0},{2,3},{3,2},{4,5},{5,4},{6,7},{7,6},{8,9},{9,8},{10,11... | collective-permute-start | bytes 1572872 | tf_op jit(solution)/shard_map/ppermute | solution.py:45
  233.2 18.6 %shard_map.223 = (bf16[1024,704]{1,0:T(8,128)(2,1)S(1)}, bf16[1024,704]{1,0:T(8,128)(2,1)}, bf16[1024,704]{1,0:T(8,128)(2,1)}, bf16[128,2048]{1,0:T(8,128)(2,1)S...) custom-call(s32[8]{0:T(128)S(1)} %stack.242.chunk.nat, ...), custom_call_target="tpu_custom_call", output_to_operand_aliasing={{0}: (10, {}), {1}: (11, {}), {2}: (12, {}), {6}: (13, {})} | custom-call | flops 1000 | bytes 5400000 | tf_op jit(solution)/shard_map/pallas_call | solution.py:136
  260.4 19.5 %shard_map.224 = (bf16[4,4,2,2,3,16,704]{6,5,4,3,2,1,0:T(8,128)(2,1)}, bf16[4,2,2,3,16,704]{5,4,3,2,1,0:T(8,128)(2,1)S(1)}, bf16[4,2,2,3,16,704]{5,4,3,2,1,0:T(8...) custom-call(s32[8]{0:T(128)S(1)} %stack.284.column, s32[4]{0:T(128)S(1)} %pad_add_fusion.1.xs, ...), custom_call_target="tpu_custom_call" | custom-call | flops 1000 | bytes 5100000 | tf_op jit(solution)/shard_map/pallas_call | solution.py:136
  282.1 3.1 multiply_reduce_fusion
  290.0 9.7 %shard_map.225 = (bf16[256,256]{1,0:T(8,128)(2,1)S(1)}, f32[2048,64]{1,0:T(8,128)S(1)}, f32[2048,64]{1,0:T(8,128)S(1)}) custom-call(s32[8]{0:T(128)S(1)} %bitcast.193, s32[16]{0:T(128)S(1)} %select_reduce_fusion.1.key_slot, s32[1]{0:T(128)} %bitcast.16.core, s32[16]{0:T(128)S(1)} %copy-done.50, bf16[1024,256]{1,0:T(8,128)(2,1)S(1)} %get-tuple-element.139.q_ref.refs_0_, ...), custom_call_target="tpu_custom_call" | custom-call | flops 1000 | bytes 2400000 | tf_op jit(solution)/shard_map/pallas_call | solution.py:136
  309.6 20.9 %shard_map.226 = (bf16[512,256]{1,0:T(8,128)(2,1)S(1)}, f32[2048,64]{1,0:T(8,128)S(1)}, f32[2048,64]{1,0:T(8,128)}) custom-call(s32[8]{0:T(128)S(1)} %bitcast.194, s32[16]{0:T(128)S(1)} %select_reduce_fusion.1.key_slot, s32[1]{0:T(128)} %bitcast.16.core, s32[16]{0:T(128)S(1)} %copy-done.50, bf16[1024,256]{1,0:T(8,128)(2,1)S(1)} %get-tuple-element.139.q_ref.refs_0_, ...), custom_call_target="tpu_custom_call" | custom-call | flops 1000 | bytes 4800000 | tf_op jit(solution)/shard_map/pallas_call | solution.py:136
  332.6 10.3 %shard_map.227 = (bf16[256,256]{1,0:T(8,128)(2,1)S(1)}, bf16[2048,64]{1,0:T(8,128)(2,1)S(1)}, bf16[2048,64]{1,0:T(8,128)(2,1)S(1)}) custom-call(s32[8]{0:T(128)S(1)} %bitcast.195, s32[16]{0:T(128)S(1)} %select_reduce_fusion.1.key_slot, s32[1]{0:T(128)} %bitcast.16.core, s32[16]{0:T(128)S(1)} %copy-done.50, ...), custom_call_target="tpu_custom_call" | custom-call | flops 1000 | bytes 2400000 | tf_op jit(solution)/shard_map/pallas_call | solution.py:136
  343.6 5.1 collective-permute-start.51
  352.3 4.4 collective-permute-done.51
  356.7 6.1 %collective-permute-done.53 = bf16[2,2,3,16,704]{4,3,2,1,0:T(8,128)(2,1)S(1)} collective-permute-done((bf16[2,2,3,16,704]{4,3,2,1,0:T(8,128)(2,1)S(1)}, bf16[2,2,3,16,704]{4,3,2,1,0:T(8,128)(2,1)S(1)}, u32[]{:S(2)}, u32[]{:S(2)}) %collective-permute-start.53) | collective-permute-done | bytes 270368 | tf_op jit(solution)/shard_map/ppermute | solution.py:45
  363.9 7.0 %shard_map.229 = (bf16[8,128,2048]{2,1,0:T(8,128)(2,1)}, f32[8,2048]{1,0:T(8,128)S(1)}) custom-call(s32[8]{0:T(128)S(1)} %stack.242.chunk.nat, bf16[256,256]{1,0:T(8,128)(2,1)S(1)} %get-tuple-element.193.refs_20_.dq0_ref, bf16[512,256]{1,0:T(8,128)(2,1)S(1)} %get-tuple-element.202.refs_21_.dq1_ref, bf16[256,256]{1,0:T(8,128)(2,1)S(1)} %get-tuple-element.213.refs_22_.dq2_ref, ...), custom_call_target="tpu_custom_call" | custom-call | flops 1000 | bytes 1500000 | tf_op jit(solution)/shard_map/pallas_call | solution.py:136
  377.2 11.8 %shard_map.228 = (bf16[4,4,2,16,576]{4,3,2,1,0:T(8,128)(2,1)}, bf16[4,4,2,16,576]{4,3,2,1,0:T(8,128)(2,1)}, bf16[4,4,2,16,576]{4,3,2,1,0:T(8,128)(2,1)}, bf16[4,4,2,16,576]{4,3,2,1,0:T(8,128)(2,1)}) custom-call(s32[8]{0:T(128)} %copy-done.52, s32[4]{0:T(128)} %copy-done.43, s32[4]{0:T(128)} %copy-done.45, s32[1]{0:T(128)} %bitcast.16.core, s32[2]{0:T(128)} %copy-done.51, ...), custom_call_target="tpu_custom_call" | custom-call | flops 1000 | bytes 3000000 | tf_op jit(solution)/shard_map/pallas_call | solution.py:136
  390.8 5.0 collective-permute-start.64
  399.9 3.3 collective-permute-done.63
  403.2 10.1 %collective-permute-done.58 = bf16[4,4,2,16,576]{4,3,2,1,0:T(8,128)(2,1)S(1)} collective-permute-done((bf16[4,4,2,16,576]{4,3,2,1,0:T(8,128)(2,1)}, bf16[4,4,2,16,576]{4,3,2,1,0:T(8,128)(2,1)S(1)}, u32[]{:S(2)}, u32[]{:S(2)}) %collective-permute-start.58) | collective-permute-done | bytes 589856 | tf_op jit(solution)/shard_map/ppermute | solution.py:45
  417.4 2.6 collective-permute-start.67
  420.0 5.4 %collective-permute-done.59 = bf16[4,4,2,16,576]{4,3,2,1,0:T(8,128)(2,1)S(1)} collective-permute-done((bf16[4,4,2,16,576]{4,3,2,1,0:T(8,128)(2,1)S(1)}, bf16[4,4,2,16,576]{4,3,2,1,0:T(8,128)(2,1)S(1)}, u32[]{:S(2)}, u32[]{:S(2)}) %collective-permute-start.59) | collective-permute-done | bytes 589856 | tf_op jit(solution)/shard_map/ppermute | solution.py:45
  425.7 3.1 collective-permute-start.60
  430.8 4.5 collective-permute-done.67
  438.8 2.6 collective-permute-start.68
  445.6 2.7 collective-permute-start.72
  448.3 14.6 %collective-permute-done.74 = f32[2,2048]{1,0:T(2,128)S(1)} collective-permute-done((f32[2,2048]{1,0:T(2,128)S(1)}, f32[2,2048]{1,0:T(2,128)S(1)}, u32[]{:S(2)}, u32[]{:S(2)}) %collective-permute-start.74) | collective-permute-done | bytes 16416 | tf_op jit(solution)/shard_map/ppermute | solution.py:45
  468.0 3.1 collective-permute-start.70
  471.2 5.4 %collective-permute-done.70 = bf16[4,2,16,256]{3,2,1,0:T(8,128)(2,1)S(1)} collective-permute-done((bf16[4,2,16,256]{3,2,1,0:T(8,128)(2,1)S(1)}, bf16[4,2,16,256]{3,2,1,0:T(8,128)(2,1)S(1)}, u32[]{:S(2)}, u32[]{:S(2)}) %collective-permute-start.70) | collective-permute-done | bytes 65568 | tf_op jit(solution)/shard_map/ppermute | solution.py:45
  476.6 3.2 collective-permute-start.76
  480.8 2.8 collective-permute-done.76
  494.2 14.2 %collective-permute-done.82.refs_3_ = bf16[2,2,4,3,16,704]{5,4,3,2,1,0:T(8,128)(2,1)} collective-permute-done((bf16[2,2,4,3,16,704]{5,4,3,2,1,0:T(8,128)(2,1)}, bf16[2,2,4,3,16,704]{5,4,3,2,1,0:T(8,128)(2,1)}, u32[]{:S(2)}, u32[]{:S(2)}) %collective-permute-start.82) | collective-permute-done | bytes 1081376 | tf_op jit(solution)/shard_map/ppermute | solution.py:45
  508.5 6.4 %shard_map.231 = (f32[128,5632]{1,0:T(8,128)}, f32[128,5632]{1,0:T(8,128)}, f32[5632,128]{1,0:T(8,128)}) custom-call(s32[5]{0:T(128)S(1)} %copy-done.48, s32[4]{0:T(128)S(1)} %copy-done.44, s32[4]{0:T(128)S(1)} %copy-done.46, s32[1]{0:T(128)} %bitcast.16.core, bf16[2,2,4,3,16,704]{5,4,3,2,1,0:T(8,128)(2,1)S(1)} %pad_maximum_fusion.1.refs_0_, ...), custom_call_target="tpu_custom_call" | custom-call | flops 1000 | bytes 1500000 | tf_op jit(solution)/shard_map/pallas_call | solution.py:136
  (429 shorter events, 143.8 us)
Async XLA Ops:
  7.2 64.1 %all-gather.7.cloned.1.call-start = ((), (), s32[]{:S(2)}) async-start(), calls=%async_computation.3 | async-start | bytes 4718592 | tf_op jit(solution)/shard_map/all_gather | solution.py:809
  28.5 104.4 %all-gather.11.cloned.1.call-start = ((), (), s32[]{:S(2)}) async-start(), calls=%async_computation.8 | async-start | bytes 5898240 | tf_op jit(solution)/shard_map/all_gather | solution.py:839
  33.6 22.3 %collective-permute-start.24 = (bf16[4,3,32,704]{3,2,1,0:T(8,128)(2,1)}, bf16[4,3,32,704]{3,2,1,0:T(8,128)(2,1)}, u32[]{:S(2)}, u32[]{:S(2)}) collective-permute-start(bf16[4,3,32,704]{3,2,1,0:T(8,128)(2,1)} %get-tuple-element.153), channel_id=1, source_target_pairs={{0,1},{1,0},{2,3},{3,2},{4,5},{5,4},{6,7},{7,6},{8,9},{9,8},{10,11... | collective-permute-start | bytes 1622024 | tf_op jit(solution)/shard_map/ppermute | solution.py:45
  33.7 18.0 %collective-permute-start.4 = (bf16[8,32,256]{2,1,0:T(8,128)(2,1)S(1)}, bf16[8,32,256]{2,1,0:T(8,128)(2,1)S(1)}, u32[]{:S(2)}, u32[]{:S(2)}) collective-permute-start(bf16[8,32,256]{2,1,0:T(8,128)(2,1)S(1)} %bitcast.212), channel_id=1, source_target_pairs={{0,0},{1,8},{2,1},{3,9},{4,2},{5,10},{6,3},{7,11},{8,4},{9,12},{10... | collective-permute-start | bytes 393224 | tf_op jit(solution)/shard_map/ppermute | solution.py:45
  57.9 19.5 %collective-permute-start.25 = (bf16[2,3,32,704]{3,2,1,0:T(8,128)(2,1)}, bf16[2,3,32,704]{3,2,1,0:T(8,128)(2,1)}, u32[]{:S(2)}, u32[]{:S(2)}) collective-permute-start(bf16[2,3,32,704]{3,2,1,0:T(8,128)(2,1)} %pad_maximum_fusion.7), channel_id=1, source_target_pairs={{0,2},{1,7},{2,4},{3,1},{4,6},{5,3},{6,0},{7,5},{8,10},{9,15},{10,... | collective-permute-start | bytes 811016 | tf_op jit(solution)/shard_map/ppermute | solution.py:45
  60.8 16.6 %collective-permute-start.26 = (bf16[2,3,32,704]{3,2,1,0:T(8,128)(2,1)}, bf16[2,3,32,704]{3,2,1,0:T(8,128)(2,1)}, u32[]{:S(2)}, u32[]{:S(2)}) collective-permute-start(bf16[2,3,32,704]{3,2,1,0:T(8,128)(2,1)} %pad_maximum_fusion.8), channel_id=1, source_target_pairs={{0,6},{1,3},{2,0},{3,5},{4,2},{5,7},{6,4},{7,1},{8,14},{9,11},{10,... | collective-permute-start | bytes 811016 | tf_op jit(solution)/shard_map/ppermute | solution.py:45
  62.6 14.8 %collective-permute-start.27 = (bf16[2,3,32,704]{3,2,1,0:T(8,128)(2,1)}, bf16[2,3,32,704]{3,2,1,0:T(8,128)(2,1)}, u32[]{:S(2)}, u32[]{:S(2)}) collective-permute-start(bf16[2,3,32,704]{3,2,1,0:T(8,128)(2,1)} %pad_maximum_fusion.9), channel_id=1, source_target_pairs={{0,4},{1,5},{2,6},{3,7},{4,0},{5,1},{6,2},{7,3},{8,12},{9,13},{10,... | collective-permute-start | bytes 811016 | tf_op jit(solution)/shard_map/ppermute | solution.py:45
  79.8 122.6 %all-gather.9.cloned.1.call-start = ((), (), s32[]{:S(2)}) async-start(), calls=%async_computation.4 | async-start | bytes 4718592 | tf_op jit(solution)/shard_map/all_gather | solution.py:823
  81.1 282.6 %reduce-scatter.6.cloned.1.call-start = ((), (), s32[]{:S(2)}) async-start(), calls=%async_computation.6 | async-start | bytes 5898240 | tf_op jit(solution)/shard_map/reduce_scatter | solution.py:883
  132.8 56.7 %collective-permute-start.28 = (bf16[4,8,3,32,704]{4,3,2,1,0:T(8,128)(2,1)}, bf16[4,8,3,32,704]{4,3,2,1,0:T(8,128)(2,1)}, u32[]{:S(2)}, u32[]{:S(2)}) collective-permute-start(bf16[4,8,3,32,704]{4,3,2,1,0:T(8,128)(2,1)} %bitcast.185), channel_id=1, source_target_pairs={{0,8},{1,73},{2,10},{3,75},{4,12},{5,77},{6,14},{7,79},{8,64},{9,1... | collective-permute-start | bytes 12976136 | tf_op jit(solution)/shard_map/ppermute | solution.py:45
  146.7 30.4 %collective-permute-start.21 = (bf16[128,2048]{1,0:T(8,128)(2,1)S(1)}, bf16[128,2048]{1,0:T(8,128)(2,1)S(1)}, u32[]{:S(2)}, u32[]{:S(2)}) collective-permute-start(bf16[128,2048]{1,0:T(8,128)(2,1)S(1)} %add_convert_fusion.6), channel_id=1, source_target_pairs={{0,4},{1,5},{2,6},{3,7},{4,0},{5,1},{6,2},{7,3},{8,12},{9,13},{10,... | collective-permute-start | bytes 1572872 | tf_op jit(solution)/shard_map/ppermute | solution.py:45
  154.5 33.7 %collective-permute-start.20 = (bf16[128,2048]{1,0:T(8,128)(2,1)S(1)}, bf16[128,2048]{1,0:T(8,128)(2,1)S(1)}, u32[]{:S(2)}, u32[]{:S(2)}) collective-permute-start(bf16[128,2048]{1,0:T(8,128)(2,1)S(1)} %add_convert_fusion.7), channel_id=1, source_target_pairs={{0,2},{1,7},{2,4},{3,1},{4,6},{5,3},{6,0},{7,5},{8,10},{9,15},{10,... | collective-permute-start | bytes 1572872 | tf_op jit(solution)/shard_map/ppermute | solution.py:45
  154.7 33.4 %collective-permute-start.19 = (bf16[128,2048]{1,0:T(8,128)(2,1)S(1)}, bf16[128,2048]{1,0:T(8,128)(2,1)S(1)}, u32[]{:S(2)}, u32[]{:S(2)}) collective-permute-start(bf16[128,2048]{1,0:T(8,128)(2,1)S(1)} %add_convert_fusion.8), channel_id=1, source_target_pairs={{0,6},{1,3},{2,0},{3,5},{4,2},{5,7},{6,4},{7,1},{8,14},{9,11},{10,... | collective-permute-start | bytes 1572872 | tf_op jit(solution)/shard_map/ppermute | solution.py:45
  165.1 23.1 %collective-permute-start.18 = (bf16[128,2048]{1,0:T(8,128)(2,1)S(1)}, bf16[128,2048]{1,0:T(8,128)(2,1)S(1)}, u32[]{:S(2)}, u32[]{:S(2)}) collective-permute-start(bf16[128,2048]{1,0:T(8,128)(2,1)S(1)} %get-tuple-element.150), channel_id=1, source_target_pairs={{0,1},{1,0},{2,3},{3,2},{4,5},{5,4},{6,7},{7,6},{8,9},{9,8},{10,11... | collective-permute-start | bytes 1572872 | tf_op jit(solution)/shard_map/ppermute | solution.py:45
  199.6 22.4 %collective-permute-start.31 = (bf16[128,2048]{1,0:T(8,128)(2,1)S(1)}, bf16[128,2048]{1,0:T(8,128)(2,1)}, u32[]{:S(2)}, u32[]{:S(2)}) collective-permute-start(bf16[128,2048]{1,0:T(8,128)(2,1)S(1)} %multiply_convert_fusion.refs_0_), channel_id=1, source_target_pairs={{0,4},{1,5},{2,6},{3,7},{4,0},{5,1},{6,2},{7,3},{8,12},{9,13},{10,... | collective-permute-start | bytes 1572872 | tf_op jit(solution)/shard_map/ppermute | solution.py:45
  200.2 21.8 %collective-permute-start.30 = (bf16[128,2048]{1,0:T(8,128)(2,1)S(1)}, bf16[128,2048]{1,0:T(8,128)(2,1)}, u32[]{:S(2)}, u32[]{:S(2)}) collective-permute-start(bf16[128,2048]{1,0:T(8,128)(2,1)S(1)} %multiply_convert_fusion.refs_0_), channel_id=1, source_target_pairs={{0,6},{1,3},{2,0},{3,5},{4,2},{5,7},{6,4},{7,1},{8,14},{9,11},{10,... | collective-permute-start | bytes 1572872 | tf_op jit(solution)/shard_map/ppermute | solution.py:45
  253.2 27.7 %collective-permute-start.36 = (bf16[128,2048]{1,0:T(8,128)(2,1)}, bf16[128,2048]{1,0:T(8,128)(2,1)}, u32[]{:S(2)}, u32[]{:S(2)}) collective-permute-start(bf16[128,2048]{1,0:T(8,128)(2,1)} %fusion.11), channel_id=1, source_target_pairs={{0,6},{1,3},{2,0},{3,5},{4,2},{5,7},{6,4},{7,1},{8,14},{9,11},{10,... | collective-permute-start | bytes 1572872 | tf_op jit(solution)/shard_map/ppermute | solution.py:45
  256.0 24.9 %collective-permute-start.38 = (bf16[128,2048]{1,0:T(8,128)(2,1)}, bf16[128,2048]{1,0:T(8,128)(2,1)}, u32[]{:S(2)}, u32[]{:S(2)}) collective-permute-start(bf16[128,2048]{1,0:T(8,128)(2,1)} %get-tuple-element.264), channel_id=1, source_target_pairs={{0,4},{1,5},{2,6},{3,7},{4,0},{5,1},{6,2},{7,3},{8,12},{9,13},{10,... | collective-permute-start | bytes 1572872 | tf_op jit(solution)/shard_map/ppermute | solution.py:45
  257.8 23.1 %collective-permute-start.37 = (bf16[128,2048]{1,0:T(8,128)(2,1)}, bf16[128,2048]{1,0:T(8,128)(2,1)}, u32[]{:S(2)}, u32[]{:S(2)}) collective-permute-start(bf16[128,2048]{1,0:T(8,128)(2,1)} %get-tuple-element.265), channel_id=1, source_target_pairs={{0,2},{1,7},{2,4},{3,1},{4,6},{5,3},{6,0},{7,5},{8,10},{9,15},{10,... | collective-permute-start | bytes 1572872 | tf_op jit(solution)/shard_map/ppermute | solution.py:45
  280.9 109.9 %reduce-scatter.4.cloned.1.call-start = ((), (), s32[]{:S(2)}) async-start(), calls=%async_computation.5 | async-start | bytes 4718592 | tf_op jit(solution)/shard_map/reduce_scatter | solution.py:884
  281.5 156.0 %all-gather.13.cloned.1.call-start = ((), (), s32[]{:S(2)}) async-start(), calls=%async_computation.9 | async-start | bytes 1114112 | tf_op jit(solution)/shard_map/all_gather | solution.py:925
  281.5 24.0 %collective-permute-start.45 = (bf16[4,2,2,3,16,704]{5,4,3,2,1,0:T(8,128)(2,1)}, bf16[4,2,2,3,16,704]{5,4,3,2,1,0:T(8,128)(2,1)S(1)}, u32[]{:S(2)}, u32[]{:S(2)}) collective-permute-start(bf16[4,2,2,3,16,704]{5,4,3,2,1,0:T(8,128)(2,1)} %get-tuple-element.188), channel_id=1, source_target_pairs={{0,8},{1,73},{2,10},{3,75},{4,12},{5,77},{6,14},{7,79},{8,64},{9,1... | collective-permute-start | bytes 3244040 | tf_op jit(solution)/shard_map/ppermute | solution.py:45
  287.0 14.8 %collective-permute-start.41 = (bf16[128,2048]{1,0:T(8,128)(2,1)S(1)}, bf16[128,2048]{1,0:T(8,128)(2,1)S(1)}, u32[]{:S(2)}, u32[]{:S(2)}) collective-permute-start(bf16[128,2048]{1,0:T(8,128)(2,1)S(1)} %get-tuple-element.253.refs_1_.refs_8_), channel_id=1, source_target_pairs={{0,6},{1,3},{2,0},{3,5},{4,2},{5,7},{6,4},{7,1},{8,14},{9,11},{10,... | collective-permute-start | bytes 1572872 | tf_op jit(solution)/shard_map/ppermute | solution.py:45
  304.0 28.5 %collective-permute-start.47 = (bf16[4,2,2,3,16,704]{5,4,3,2,1,0:T(8,128)(2,1)S(1)}, bf16[4,2,2,3,16,704]{5,4,3,2,1,0:T(8,128)(2,1)S(1)}, u32[]{:S(2)}, u32[]{:S(2)}) collective-permute-start(bf16[4,2,2,3,16,704]{5,4,3,2,1,0:T(8,128)(2,1)S(1)} %copy-done.79), channel_id=1, source_target_pairs={{0,72},{1,9},{2,74},{3,11},{4,76},{5,13},{6,78},{7,15},{8,0},{9,65... | collective-permute-start | bytes 3244040 | tf_op jit(solution)/shard_map/ppermute | solution.py:45
  305.9 37.1 %collective-permute-start.48 = (bf16[4,2,2,3,16,704]{5,4,3,2,1,0:T(8,128)(2,1)S(1)}, bf16[4,2,2,3,16,704]{5,4,3,2,1,0:T(8,128)(2,1)S(1)}, u32[]{:S(2)}, u32[]{:S(2)}) collective-permute-start(bf16[4,2,2,3,16,704]{5,4,3,2,1,0:T(8,128)(2,1)S(1)} %add_convert_fusion.1), channel_id=1, source_target_pairs={{0,8},{1,73},{2,10},{3,75},{4,12},{5,77},{6,14},{7,79},{8,64},{9,1... | collective-permute-start | bytes 3244040 | tf_op jit(solution)/shard_map/ppermute | solution.py:45
  307.7 22.8 %collective-permute-start.44 = (bf16[128,2048]{1,0:T(8,128)(2,1)S(1)}, bf16[128,2048]{1,0:T(8,128)(2,1)S(1)}, u32[]{:S(2)}, u32[]{:S(2)}) collective-permute-start(bf16[128,2048]{1,0:T(8,128)(2,1)S(1)} %get-tuple-element.253.refs_1_.refs_8_), channel_id=1, source_target_pairs={{0,4},{1,5},{2,6},{3,7},{4,0},{5,1},{6,2},{7,3},{8,12},{9,13},{10,... | collective-permute-start | bytes 1572872 | tf_op jit(solution)/shard_map/ppermute | solution.py:45
  343.6 13.0 %collective-permute-start.51 = (bf16[2,2,3,16,704]{4,3,2,1,0:T(8,128)(2,1)S(1)}, bf16[2,2,3,16,704]{4,3,2,1,0:T(8,128)(2,1)S(1)}, u32[]{:S(2)}, u32[]{:S(2)}) collective-permute-start(bf16[2,2,3,16,704]{4,3,2,1,0:T(8,128)(2,1)S(1)} %get-tuple-element.261), channel_id=1, source_target_pairs={{0,32},{1,33},{2,34},{3,35},{4,36},{5,37},{6,38},{7,39},{8,40},{9,... | collective-permute-start | bytes 811016 | tf_op jit(solution)/shard_map/ppermute | solution.py:45
  348.8 14.0 %collective-permute-start.53 = (bf16[2,2,3,16,704]{4,3,2,1,0:T(8,128)(2,1)S(1)}, bf16[2,2,3,16,704]{4,3,2,1,0:T(8,128)(2,1)S(1)}, u32[]{:S(2)}, u32[]{:S(2)}) collective-permute-start(bf16[2,2,3,16,704]{4,3,2,1,0:T(8,128)(2,1)S(1)} %get-tuple-element.262), channel_id=1, source_target_pairs={{0,16},{1,49},{2,18},{3,51},{4,20},{5,53},{6,22},{7,55},{8,24},{9,... | collective-permute-start | bytes 811016 | tf_op jit(solution)/shard_map/ppermute | solution.py:45
  349.8 13.7 %collective-permute-start.52 = (bf16[2,2,3,16,704]{4,3,2,1,0:T(8,128)(2,1)S(1)}, bf16[2,2,3,16,704]{4,3,2,1,0:T(8,128)(2,1)S(1)}, u32[]{:S(2)}, u32[]{:S(2)}) collective-permute-start(bf16[2,2,3,16,704]{4,3,2,1,0:T(8,128)(2,1)S(1)} %get-tuple-element.263), channel_id=1, source_target_pairs={{0,48},{1,17},{2,50},{3,19},{4,52},{5,21},{6,54},{7,23},{8,56},{9,... | collective-permute-start | bytes 811016 | tf_op jit(solution)/shard_map/ppermute | solution.py:45
  371.6 113.9 %reduce-scatter.8.cloned.1.call-start = ((), (), s32[]{:S(2)}) async-start(), calls=%async_computation.7 | async-start | bytes 4718592 | tf_op jit(solution)/shard_map/reduce_scatter | solution.py:933
  372.8 16.1 %collective-permute-start.54 = (bf16[2,2,3,16,704]{4,3,2,1,0:T(8,128)(2,1)S(1)}, bf16[2,2,3,16,704]{4,3,2,1,0:T(8,128)(2,1)S(1)}, u32[]{:S(2)}, u32[]{:S(2)}) collective-permute-start(bf16[2,2,3,16,704]{4,3,2,1,0:T(8,128)(2,1)S(1)} %get-tuple-element.258), channel_id=1, source_target_pairs={{0,64},{1,65},{2,66},{3,67},{4,68},{5,69},{6,70},{7,71},{8,72},{9,... | collective-permute-start | bytes 811016 | tf_op jit(solution)/shard_map/ppermute | solution.py:45
  375.0 14.0 %collective-permute-start.56 = (bf16[2,2,3,16,704]{4,3,2,1,0:T(8,128)(2,1)S(1)}, bf16[2,2,3,16,704]{4,3,2,1,0:T(8,128)(2,1)S(1)}, u32[]{:S(2)}, u32[]{:S(2)}) collective-permute-start(bf16[2,2,3,16,704]{4,3,2,1,0:T(8,128)(2,1)S(1)} %get-tuple-element.259), channel_id=1, source_target_pairs={{0,8},{1,73},{2,10},{3,75},{4,12},{5,77},{6,14},{7,79},{8,64},{9,1... | collective-permute-start | bytes 811016 | tf_op jit(solution)/shard_map/ppermute | solution.py:45
  375.2 14.4 %collective-permute-start.55 = (bf16[2,2,3,16,704]{4,3,2,1,0:T(8,128)(2,1)S(1)}, bf16[2,2,3,16,704]{4,3,2,1,0:T(8,128)(2,1)S(1)}, u32[]{:S(2)}, u32[]{:S(2)}) collective-permute-start(bf16[2,2,3,16,704]{4,3,2,1,0:T(8,128)(2,1)S(1)} %get-tuple-element.260), channel_id=1, source_target_pairs={{0,72},{1,9},{2,74},{3,11},{4,76},{5,13},{6,78},{7,15},{8,0},{9,65... | collective-permute-start | bytes 811016 | tf_op jit(solution)/shard_map/ppermute | solution.py:45
  395.9 17.7 %collective-permute-start.65 = (bf16[2,3,16,704]{3,2,1,0:T(8,128)(2,1)S(1)}, bf16[2,3,16,704]{3,2,1,0:T(8,128)(2,1)S(1)}, u32[]{:S(2)}, u32[]{:S(2)}) collective-permute-start(bf16[2,3,16,704]{3,2,1,0:T(8,128)(2,1)S(1)} %get-tuple-element.284), channel_id=1, source_target_pairs={{0,4},{1,5},{2,6},{3,7},{4,0},{5,1},{6,2},{7,3},{8,12},{9,13},{10,... | collective-permute-start | bytes 405512 | tf_op jit(solution)/shard_map/ppermute | solution.py:45
  397.3 22.6 %collective-permute-start.57 = (bf16[4,4,2,16,576]{4,3,2,1,0:T(8,128)(2,1)S(1)}, bf16[4,4,2,16,576]{4,3,2,1,0:T(8,128)(2,1)S(1)}, u32[]{:S(2)}, u32[]{:S(2)}) collective-permute-start(bf16[4,4,2,16,576]{4,3,2,1,0:T(8,128)(2,1)S(1)} %copy-done.80), channel_id=1, source_target_pairs={{0,48},{1,17},{2,50},{3,19},{4,52},{5,21},{6,54},{7,23},{8,56},{9,... | collective-permute-start | bytes 1769480 | tf_op jit(solution)/shard_map/ppermute | solution.py:45
  397.3 16.0 %collective-permute-start.58 = (bf16[4,4,2,16,576]{4,3,2,1,0:T(8,128)(2,1)}, bf16[4,4,2,16,576]{4,3,2,1,0:T(8,128)(2,1)S(1)}, u32[]{:S(2)}, u32[]{:S(2)}) collective-permute-start(bf16[4,4,2,16,576]{4,3,2,1,0:T(8,128)(2,1)} %get-tuple-element.232), channel_id=1, source_target_pairs={{0,16},{1,49},{2,18},{3,51},{4,20},{5,53},{6,22},{7,55},{8,24},{9,... | collective-permute-start | bytes 1769480 | tf_op jit(solution)/shard_map/ppermute | solution.py:45
  417.4 17.8 %collective-permute-start.67 = (bf16[2,4,3,16,704]{4,3,2,1,0:T(8,128)(2,1)S(1)}, bf16[2,4,3,16,704]{4,3,2,1,0:T(8,128)(2,1)S(1)}, u32[]{:S(2)}, u32[]{:S(2)}) collective-permute-start(bf16[2,4,3,16,704]{4,3,2,1,0:T(8,128)(2,1)S(1)} %get-tuple-element.270), channel_id=1, source_target_pairs={{0,64},{1,65},{2,66},{3,67},{4,68},{5,69},{6,70},{7,71},{8,72},{9,... | collective-permute-start | bytes 1622024 | tf_op jit(solution)/shard_map/ppermute | solution.py:45
  425.7 13.1 %collective-permute-start.60 = (bf16[4,2,16,576]{3,2,1,0:T(8,128)(2,1)S(1)}, bf16[4,2,16,576]{3,2,1,0:T(8,128)(2,1)S(1)}, u32[]{:S(2)}, u32[]{:S(2)}) collective-permute-start(bf16[4,2,16,576]{3,2,1,0:T(8,128)(2,1)S(1)} %get-tuple-element.266), channel_id=1, source_target_pairs={{0,64},{1,65},{2,66},{3,67},{4,68},{5,69},{6,70},{7,71},{8,72},{9,... | collective-permute-start | bytes 442376 | tf_op jit(solution)/shard_map/ppermute | solution.py:45
  435.4 48.2 %collective-permute-start.81 = (bf16[2,2,4,3,16,704]{5,4,3,2,1,0:T(8,128)(2,1)S(1)}, bf16[2,2,4,3,16,704]{5,4,3,2,1,0:T(8,128)(2,1)S(1)}, u32[]{:S(2)}, u32[]{:S(2)}) collective-permute-start(bf16[2,2,4,3,16,704]{5,4,3,2,1,0:T(8,128)(2,1)S(1)} %pad_maximum_fusion.1.refs_0_), channel_id=1, source_target_pairs={{0,48},{1,17},{2,50},{3,19},{4,52},{5,21},{6,54},{7,23},{8,56},{9,... | collective-permute-start | bytes 3244040 | tf_op jit(solution)/shard_map/ppermute | solution.py:45
  436.7 46.9 %collective-permute-start.80 = (bf16[2,2,4,3,16,704]{5,4,3,2,1,0:T(8,128)(2,1)S(1)}, bf16[2,2,4,3,16,704]{5,4,3,2,1,0:T(8,128)(2,1)}, u32[]{:S(2)}, u32[]{:S(2)}) collective-permute-start(bf16[2,2,4,3,16,704]{5,4,3,2,1,0:T(8,128)(2,1)S(1)} %pad_maximum_fusion.1.refs_0_), channel_id=1, source_target_pairs={{0,16},{1,49},{2,18},{3,51},{4,20},{5,53},{6,22},{7,55},{8,24},{9,... | collective-permute-start | bytes 3244040 | tf_op jit(solution)/shard_map/ppermute | solution.py:45
  444.1 18.7 %collective-permute-start.74 = (f32[2,2048]{1,0:T(2,128)S(1)}, f32[2,2048]{1,0:T(2,128)S(1)}, u32[]{:S(2)}, u32[]{:S(2)}) collective-permute-start(f32[2,2048]{1,0:T(2,128)S(1)} %slice_add_fusion.1), channel_id=1, source_target_pairs={{0,32},{1,33},{2,34},{3,35},{4,36},{5,37},{6,38},{7,39},{8,40},{9,... | collective-permute-start | bytes 49160 | tf_op jit(solution)/shard_map/ppermute | solution.py:45
  445.0 18.9 %collective-permute-start.71 = (bf16[2,16,320]{2,1,0:T(8,128)(2,1)S(1)}, bf16[2,16,320]{2,1,0:T(8,128)(2,1)S(1)}, u32[]{:S(2)}, u32[]{:S(2)}) collective-permute-start(bf16[2,16,320]{2,1,0:T(8,128)(2,1)S(1)} %get-tuple-element.293), channel_id=1, source_target_pairs={{0,6},{1,3},{2,0},{3,5},{4,2},{5,7},{6,4},{7,1},{8,14},{9,11},{10,... | collective-permute-start | bytes 61448 | tf_op jit(solution)/shard_map/ppermute | solution.py:45
  445.6 22.3 %collective-permute-start.72 = (bf16[2,16,320]{2,1,0:T(8,128)(2,1)S(1)}, bf16[2,16,320]{2,1,0:T(8,128)(2,1)S(1)}, u32[]{:S(2)}, u32[]{:S(2)}) collective-permute-start(bf16[2,16,320]{2,1,0:T(8,128)(2,1)S(1)} %get-tuple-element.294), channel_id=1, source_target_pairs={{0,4},{1,5},{2,6},{3,7},{4,0},{5,1},{6,2},{7,3},{8,12},{9,13},{10,... | collective-permute-start | bytes 61448 | tf_op jit(solution)/shard_map/ppermute | solution.py:45
  463.9 16.8 %collective-permute-start.75 = (f32[2,2048]{1,0:T(2,128)S(1)}, f32[2,2048]{1,0:T(2,128)S(1)}, u32[]{:S(2)}, u32[]{:S(2)}) collective-permute-start(f32[2,2048]{1,0:T(2,128)S(1)} %add.348), channel_id=1, source_target_pairs={{0,16},{1,49},{2,18},{3,51},{4,20},{5,53},{6,22},{7,55},{8,24},{9,... | collective-permute-start | bytes 49160 | tf_op jit(solution)/shard_map/ppermute | solution.py:45
  483.6 24.8 %collective-permute-start.82 = (bf16[2,2,4,3,16,704]{5,4,3,2,1,0:T(8,128)(2,1)}, bf16[2,2,4,3,16,704]{5,4,3,2,1,0:T(8,128)(2,1)}, u32[]{:S(2)}, u32[]{:S(2)}) collective-permute-start(bf16[2,2,4,3,16,704]{5,4,3,2,1,0:T(8,128)(2,1)} %collective-permute-done.80.refs_1_), channel_id=1, source_target_pairs={{0,16},{1,49},{2,18},{3,51},{4,20},{5,53},{6,22},{7,55},{8,24},{9,... | collective-permute-start | bytes 3244040 | tf_op jit(solution)/shard_map/ppermute | solution.py:45
  489.3 25.6 %collective-permute-start.79 = (bf16[2,2,4,16,576]{4,3,2,1,0:T(8,128)(2,1)S(1)}, bf16[2,2,4,16,576]{4,3,2,1,0:T(8,128)(2,1)S(1)}, u32[]{:S(2)}, u32[]{:S(2)}) collective-permute-start(bf16[2,2,4,16,576]{4,3,2,1,0:T(8,128)(2,1)S(1)} %pad_maximum_fusion.5.refs_0_), channel_id=1, source_target_pairs={{0,32},{1,33},{2,34},{3,35},{4,36},{5,37},{6,38},{7,39},{8,40},{9,... | collective-permute-start | bytes 884744 | tf_op jit(solution)/shard_map/ppermute | solution.py:45
  491.5 23.3 %collective-permute-start.78 = (bf16[2,2,4,16,576]{4,3,2,1,0:T(8,128)(2,1)S(1)}, bf16[2,2,4,16,576]{4,3,2,1,0:T(8,128)(2,1)S(1)}, u32[]{:S(2)}, u32[]{:S(2)}) collective-permute-start(bf16[2,2,4,16,576]{4,3,2,1,0:T(8,128)(2,1)S(1)} %pad_maximum_fusion.5.refs_0_), channel_id=1, source_target_pairs={{0,48},{1,17},{2,50},{3,19},{4,52},{5,21},{6,54},{7,23},{8,56},{9,... | collective-permute-start | bytes 884744 | tf_op jit(solution)/shard_map/ppermute | solution.py:45
  492.0 23.3 %collective-permute-start.77 = (bf16[2,2,4,16,576]{4,3,2,1,0:T(8,128)(2,1)S(1)}, bf16[2,2,4,16,576]{4,3,2,1,0:T(8,128)(2,1)S(1)}, u32[]{:S(2)}, u32[]{:S(2)}) collective-permute-start(bf16[2,2,4,16,576]{4,3,2,1,0:T(8,128)(2,1)S(1)} %pad_maximum_fusion.5.refs_0_), channel_id=1, source_target_pairs={{0,16},{1,49},{2,18},{3,51},{4,20},{5,53},{6,22},{7,55},{8,24},{9,... | collective-permute-start | bytes 884744 | tf_op jit(solution)/shard_map/ppermute | solution.py:45
  (125 other events, 2123.8 us)
Sparse Core Ops, SparseCore 0:
  28.6 32.7 all-gather.6
  79.9 52.9 all-gather.10
  134.6 53.3 all-gather.8
  281.0 51.8 reduce-scatter.5
  335.1 38.2 reduce-scatter.3
  375.0 31.6 all-gather.12
  409.1 40.3 reduce-scatter.7

commit v11 on v10

--- a/solution.py
+++ b/solution.py
@@ -844,13 +844,14 @@
     kv_other = swap(jnp.concatenate([kv_own[1], kv_half[1]], axis=0))
     keys = jnp.where(first_core, kv_mine, kv_other)
     values = jnp.where(usable, jnp.where(first_core, kv_other, kv_mine), 0)
-    attended, sums, got = [None] * 4, [None] * 4, [None] * 4
+    attended, sums, got, peers = [None] * 4, [None] * 4, [None] * 4, []
     for g in (3, 1, 2, 0):
         at = after(query_place, *sums[1:]) if g == 0 else query_place
         attended[g], mine, peer = attend(g, at, key_slot, queries, keys, values, w_out)
         peer = swap(peer)
+        peers.append(peer)
         if g == 2:
-            mlp_half_rows = after(mlp_half_rows, peer)
+            mlp_half_rows = after(mlp_half_rows, peers)
             mlp_other_rows = step(mlp_half_rows, "y", 1)
             w_mlp = place_mlp(slot, halves, mlp_half_rows, mlp_other_rows)
         sums[g] = add(mine, peer).astype(BF)
@@ -928,20 +929,21 @@
     )
     attn_outs = after(attn_outs, low)
     low, high = after((low, high), branch)
-    mlp_sums, mlp_swapped, _ = resplit_back([low[0], low[1], high[0], high[1]])
+    mlp_sums, mlp_swapped, mlp_arrived = resplit_back([low[0], low[1], high[0], high[1]])
     attn_partial = after(attn_partial, attn_outs[0])
     normed_attn_grad = lax.psum_scatter(attn_partial, "blk", scatter_dimension=0, axis_index_groups=ZC_GROUPS)
 
     layer_out = (residual + after(branch, attn_outs[0]).astype(F32)).astype(BF)[None]
     mlp_across = across(mlp_sums, "y")
-    gain_grads = jnp.sum(after(gain_grads, mlp_across), axis=0)[:2]
+    gain_grads = jnp.sum(after(gain_grads, mlp_arrived), axis=0)[:2]
     gain_grads = gain_grads + across(gain_grads, "y")
+    gain_grads = after(gain_grads, mlp_swapped)
+    gain_grads = gain_grads + across(gain_grads, "x")
+    gain_grads = gain_grads + step(gain_grads, "x", 1)
     mlp_sums = jnp.stack([mlp_sums, mlp_across])
     mlp_first, mlp_second = step(mlp_sums, "x", 1), step(mlp_sums, "x", -1)
-    attn_sums = ring_scatter(*attn_outs, "x", attn_outs[0]).astype(BF)
+    attn_sums = after(ring_scatter(*attn_outs, "x", attn_outs[0]).astype(BF), gain_grads)
     attn_sums = ring_scatter(attn_sums[0], attn_sums[2], attn_sums[3], attn_sums[1], "y").astype(BF)
-    attn_sums = after(attn_sums, gain_grads)
-    gain_grads = gain_grads + across(gain_grads, "x")
     qkv_sums, _, arrived = resplit_back(attn_sums[..., QUERY:])
     out_sums = send(
         after(attn_sums[..., :QUERY], arrived), lambda yh, x, yl, z, c: (yh, x, z // 2, 2 * (z % 2) + c, yl)
@@ -951,9 +953,8 @@
         residual_grad + norm_back(rows_in, scale_attn, gain_one, after(normed_attn_grad, attn_sums).astype(F32))
     ).astype(BF)[None]
     attn_across = across(attn_sums, "y")
-    mlp_sums = (mlp_sums, mlp_first, mlp_second, step(after(mlp_first, mlp_second, attn_across), "x", 1))
-    attn_sums = ring_gather(after(jnp.stack([attn_sums, attn_across]), tokens_grad, gain_grads), "x")
-    gain_grads = gain_grads + step(gain_grads, "x", 1)
+    mlp_sums = (mlp_sums, mlp_first, mlp_second, step(after(mlp_first, mlp_second, arrived), "x", 1))
+    attn_sums = ring_gather(after(jnp.stack([attn_sums, attn_across]), tokens_grad), "x")
     gate_grad, up_grad, down_grad = finish_mlp(spots, xs, yhs, core, mlp_sums)
     query_grad, key_grad, value_grad, output_grad = finish_attn(spots, xs, yhs, core, attn_sums)
     return (

time: 532 us -> 520 us (0.977)
  starting transfers between devices: 118 us -> 107 us
  Pallas kernels: 174 us -> 167 us
    ppermute x83, waiting for transfers between devices: 140 us -> 158 us  [send(): return lax.ppermute(value, BOTH, pairs)]
    all_gather x1, waiting for transfers between devices: 22 us -> 5.24 us  [on_device(): lax.all_gather(exchange(mlp_mine, mlp_other, kv_own), 'batch', axis=0, ax...]
    ppermute x83, starting transfers between devices: 118 us -> 106 us  [send(): return lax.ppermute(value, BOTH, pairs)]
    pallas_call x20, Pallas kernels: 174 us -> 167 us  [call(): pl.pallas_call(body, grid_spec=pltpu.PrefetchScalarGridSpec(num_scalar_pr...]
    unnamed x169 -> x177, local copies, waits for them, and re-layouts: 15.9 us -> 19.7 us
  transfers between devices with their start and end apart: 90 -> 90, of which waited for: 37 -> 36; matrix products, arithmetic and copies ran while one was open for 7% -> 7% of each run, Pallas kernels for 29% -> 28%
where the time goes in v11:
time: 520 us; the launch traced here: 512 us
  Pallas kernels  167 us (32%)
  waiting for transfers between devices  164 us (32%)
  starting transfers between devices  107 us (21%)
  other arithmetic  31.4 us (6%)
  local copies, waits for them, and re-layouts  26.9 us (5%)
  between operations  16 us (3%)
    pallas_call x20, Pallas kernels, call(): pl.pallas_call(body, grid_spec=pltpu.PrefetchScalarGridSpec(num_scalar_pr...  167 us
    ppermute x83, waiting for transfers between devices, send(): return lax.ppermute(value, BOTH, pairs)  158 us
    ppermute x83, starting transfers between devices, send(): return lax.ppermute(value, BOTH, pairs)  106 us
    unnamed x177, local copies, waits for them, and re-layouts  19.7 us
  transfers between devices with their start and end apart: 90, of which 36 were waited for; matrix products, arithmetic and copies ran while one was open for 7% of the time, Pallas kernels for 28%

profile of v11, /device:TPU:24, one launch (start us, length us, event | category | flops | bytes accessed | tf_op | source)
XLA Modules:
  0.0 511.5 jit_solution(3162293552848965588)
XLA Ops:
  22.2 3.7 collective-permute-done.3
  33.7 3.9 collective-permute-start.4
  37.7 3.1 collective-permute-start.7
  44.0 3.3 collective-permute-done.7
  47.3 3.3 collective-permute-done.6
  71.3 6.1 %shard_map.214 = (bf16[1024,256]{1,0:T(8,128)(2,1)S(1)}, bf16[2,1024,64]{2,1,0:T(8,128)(2,1)S(1)}) custom-call(s32[8]{0:T(128)S(1)} %stack.242.chunk.nat, bf16[1024,2048]{1,0:T(8,128)(2,1)} %all-gather.7.cloned.1.call-done.refs_0_.refs_1_.refs_2_.refs_3_.refs_4_.refs_5_.refs_6_.refs_7_, ...), custom_call_target="tpu_custom_call" | custom-call | flops 1000 | bytes 1500000 | tf_op jit(solution)/shard_map/pallas_call | solution.py:136
  81.3 7.8 %collective-permute-done.12.other_ref = bf16[4,8,32,256]{3,2,1,0:T(8,128)(2,1)S(1)} collective-permute-done((bf16[4,8,32,256]{3,2,1,0:T(8,128)(2,1)S(1)}, bf16[4,8,32,256]{3,2,1,0:T(8,128)(2,1)S(1)}, u32[]{:S(2)}, u32[]{:S(2)}) %collective-permute-start.12) | collective-permute-done | bytes 524320 | tf_op jit(solution)/shard_map/ppermute | solution.py:45
  89.8 7.4 %collective-permute-done.13 = bf16[2,1024,64]{1,2,0:T(8,128)(2,1)S(1)} collective-permute-done((bf16[2,1024,64]{1,2,0:T(8,128)(2,1)S(1)}, bf16[2,1024,64]{1,2,0:T(8,128)(2,1)S(1)}, u32[]{:S(2)}, u32[]{:S(2)}) %collective-permute-start.13) | collective-permute-done | bytes 262176 | tf_op jit(solution)/shard_map/ppermute | solution.py:45
  99.8 7.9 %shard_map.218 = (bf16[256,256]{1,0:T(8,128)(2,1)S(1)}, bf16[128,2048]{1,0:T(8,128)(2,1)S(1)}, bf16[128,2048]{1,0:T(8,128)(2,1)S(1)}) custom-call(s32[8]{0:T(128)S(1)} %bitcast.187, s32[16]{0:T(128)S(1)} %select_reduce_fusion.1.key_slot, bf16[1024,256]{1,0:T(8,128)(2,1)S(1)} %get-tuple-element.140.q_ref.refs_0_, ...), custom_call_target="tpu_custom_call" | custom-call | flops 1000 | bytes 1800000 | tf_op jit(solution)/shard_map/pallas_call | solution.py:136
  109.2 6.3 %shard_map.217 = (bf16[256,256]{1,0:T(8,128)(2,1)S(1)}, bf16[128,2048]{1,0:T(8,128)(2,1)S(1)}, bf16[128,2048]{1,0:T(8,128)(2,1)S(1)}) custom-call(s32[8]{0:T(128)S(1)} %bitcast.188, s32[16]{0:T(128)S(1)} %select_reduce_fusion.1.key_slot, bf16[1024,256]{1,0:T(8,128)(2,1)S(1)} %get-tuple-element.140.q_ref.refs_0_, ...), custom_call_target="tpu_custom_call" | custom-call | flops 1000 | bytes 1800000 | tf_op jit(solution)/shard_map/pallas_call | solution.py:136
  116.7 7.4 %shard_map.216 = (bf16[256,256]{1,0:T(8,128)(2,1)S(1)}, bf16[128,2048]{1,0:T(8,128)(2,1)S(1)}, bf16[128,2048]{1,0:T(8,128)(2,1)S(1)}) custom-call(s32[8]{0:T(128)S(1)} %bitcast.189, s32[16]{0:T(128)S(1)} %select_reduce_fusion.1.key_slot, bf16[1024,256]{1,0:T(8,128)(2,1)S(1)} %get-tuple-element.140.q_ref.refs_0_, ...), custom_call_target="tpu_custom_call" | custom-call | flops 1000 | bytes 1800000 | tf_op jit(solution)/shard_map/pallas_call | solution.py:136
  127.6 5.2 %all-gather.11.cloned.1.call-done = bf16[32,3,32,704]{3,2,1,0:T(8,128)(2,1)} async-done(((bf16[8,3,32,704]{3,2,1,0:T(8,128)(2,1)}), bf16[32,3,32,704]{3,2,1,0:T(8,128)(2,1)}) %all-gather.11.cloned.1.call-update) | async-done | bytes 4325392 | tf_op jit(solution)/shard_map/all_gather | solution.py:839
  134.8 3.2 collective-permute-start.21
  142.8 3.0 shard_map.219
  145.9 9.4 %collective-permute-done.21 = bf16[128,2048]{1,0:T(8,128)(2,1)S(1)} collective-permute-done((bf16[128,2048]{1,0:T(8,128)(2,1)S(1)}, bf16[128,2048]{1,0:T(8,128)(2,1)S(1)}, u32[]{:S(2)}, u32[]{:S(2)}) %collective-permute-start.21) | collective-permute-done | bytes 524320 | tf_op jit(solution)/shard_map/ppermute | solution.py:45
  155.3 21.4 %collective-permute-done.20 = bf16[128,2048]{1,0:T(8,128)(2,1)S(1)} collective-permute-done((bf16[128,2048]{1,0:T(8,128)(2,1)S(1)}, bf16[128,2048]{1,0:T(8,128)(2,1)S(1)}, u32[]{:S(2)}, u32[]{:S(2)}) %collective-permute-start.20) | collective-permute-done | bytes 524320 | tf_op jit(solution)/shard_map/ppermute | solution.py:45
  180.0 7.3 %collective-permute-done.28.other_ref = bf16[4,8,3,32,704]{4,3,2,1,0:T(8,128)(2,1)} collective-permute-done((bf16[4,8,3,32,704]{4,3,2,1,0:T(8,128)(2,1)}, bf16[4,8,3,32,704]{4,3,2,1,0:T(8,128)(2,1)}, u32[]{:S(2)}, u32[]{:S(2)}) %collective-permute-start.28) | collective-permute-done | bytes 4325408 | tf_op jit(solution)/shard_map/ppermute | solution.py:45
  187.3 8.4 %shard_map.221 = bf16[3,2,8,128,704]{4,3,2,1,0:T(8,128)(2,1)} custom-call(s32[8]{0:T(128)S(1)} %stack.254.slot, s32[2]{0:T(128)S(1)} %pad_add_fusion.2.halves, bf16[4,8,3,32,704]{4,3,2,1,0:T(8,128)(2,1)S(1)} %bitcast.186, bf16[4,8,3,32,704]{4,3,2,1,0:T(8,128)(2,1)} %collective-permute-done.28.other_ref), custom_call_target="tpu_custom_call" | custom-call | flops 1000 | bytes 1800000 | tf_op jit(solution)/shard_map/pallas_call | solution.py:136
  195.9 3.0 collective-permute-start.31
  200.0 18.7 %shard_map.222 = (bf16[1024,704]{1,0:T(8,128)(2,1)S(1)}, bf16[1024,704]{1,0:T(8,128)(2,1)}, bf16[1024,704]{1,0:T(8,128)(2,1)}, bf16[128,2048]{1,0:T(8,128)(2,1)S...) custom-call(s32[8]{0:T(128)S(1)} %stack.242.chunk.nat, ...), custom_call_target="tpu_custom_call" | custom-call | flops 1000 | bytes 5400000 | tf_op jit(solution)/shard_map/pallas_call | solution.py:136
  220.1 8.7 %collective-permute-start.34 = (bf16[128,2048]{1,0:T(8,128)(2,1)}, bf16[128,2048]{1,0:T(8,128)(2,1)S(1)}, u32[]{:S(2)}, u32[]{:S(2)}) collective-permute-start(bf16[128,2048]{1,0:T(8,128)(2,1)} %collective-permute-done.31.refs_2_.refs_6_), channel_id=1, source_target_pairs={{0,1},{1,0},{2,3},{3,2},{4,5},{5,4},{6,7},{7,6},{8,9},{9,8},{10,11... | collective-permute-start | bytes 1572872 | tf_op jit(solution)/shard_map/ppermute | solution.py:45
  230.8 18.6 %shard_map.223 = (bf16[1024,704]{1,0:T(8,128)(2,1)S(1)}, bf16[1024,704]{1,0:T(8,128)(2,1)}, bf16[1024,704]{1,0:T(8,128)(2,1)}, bf16[128,2048]{1,0:T(8,128)(2,1)S...) custom-call(s32[8]{0:T(128)S(1)} %stack.242.chunk.nat, ...), custom_call_target="tpu_custom_call", output_to_operand_aliasing={{0}: (10, {}), {1}: (11, {}), {2}: (12, {}), {6}: (13, {})} | custom-call | flops 1000 | bytes 5400000 | tf_op jit(solution)/shard_map/pallas_call | solution.py:136
  258.4 19.5 %shard_map.224 = (bf16[4,4,2,2,3,16,704]{6,5,4,3,2,1,0:T(8,128)(2,1)}, bf16[4,2,2,3,16,704]{5,4,3,2,1,0:T(8,128)(2,1)S(1)}, bf16[4,2,2,3,16,704]{5,4,3,2,1,0:T(8...) custom-call(s32[8]{0:T(128)S(1)} %stack.284.column, s32[4]{0:T(128)S(1)} %pad_add_fusion.1.xs, ...), custom_call_target="tpu_custom_call" | custom-call | flops 1000 | bytes 5100000 | tf_op jit(solution)/shard_map/pallas_call | solution.py:136
  281.3 3.1 multiply_reduce_fusion
  288.6 3.6 shard_map.225
  293.3 6.7 %collective-permute-done.41.refs_3_.refs_12_ = bf16[128,2048]{1,0:T(8,128)(2,1)S(1)} collective-permute-done((bf16[128,2048]{1,0:T(8,128)(2,1)S(1)}, bf16[128,2048]{1,0:T(8,128)(2,1)S(1)}, u32[]{:S(2)}, u32[]{:S(2)}) %collective-permute-start.41) | collective-permute-done | bytes 524320 | tf_op jit(solution)/shard_map/ppermute | solution.py:45
  303.9 3.0 collective-permute-start.48
  308.9 20.5 %shard_map.226 = (bf16[512,256]{1,0:T(8,128)(2,1)S(1)}, f32[2048,64]{1,0:T(8,128)S(1)}, f32[2048,64]{1,0:T(8,128)}) custom-call(s32[8]{0:T(128)S(1)} %bitcast.192, s32[16]{0:T(128)S(1)} %select_reduce_fusion.1.key_slot, s32[1]{0:T(128)} %bitcast.16.core, s32[16]{0:T(128)S(1)} %copy-done.53, bf16[1024,256]{1,0:T(8,128)(2,1)S(1)} %get-tuple-element.140.q_ref.refs_0_, ...), custom_call_target="tpu_custom_call" | custom-call | flops 1000 | bytes 4800000 | tf_op jit(solution)/shard_map/pallas_call | solution.py:136
  332.7 12.4 %shard_map.227 = (bf16[256,256]{1,0:T(8,128)(2,1)S(1)}, bf16[2048,64]{1,0:T(8,128)(2,1)S(1)}, bf16[2048,64]{1,0:T(8,128)(2,1)S(1)}) custom-call(s32[8]{0:T(128)S(1)} %bitcast.193, s32[16]{0:T(128)S(1)} %select_reduce_fusion.1.key_slot, s32[1]{0:T(128)} %bitcast.16.core, s32[16]{0:T(128)S(1)} %copy-done.53, ...), custom_call_target="tpu_custom_call" | custom-call | flops 1000 | bytes 2400000 | tf_op jit(solution)/shard_map/pallas_call | solution.py:136
  346.0 3.2 collective-permute-start.52
  351.0 6.3 %collective-permute-done.51 = bf16[2,2,3,16,704]{4,3,2,1,0:T(8,128)(2,1)S(1)} collective-permute-done((bf16[2,2,3,16,704]{4,3,2,1,0:T(8,128)(2,1)S(1)}, bf16[2,2,3,16,704]{4,3,2,1,0:T(8,128)(2,1)S(1)}, u32[]{:S(2)}, u32[]{:S(2)}) %collective-permute-start.51) | collective-permute-done | bytes 270368 | tf_op jit(solution)/shard_map/ppermute | solution.py:45
  357.3 5.9 %collective-permute-done.53 = bf16[2,2,3,16,704]{4,3,2,1,0:T(8,128)(2,1)S(1)} collective-permute-done((bf16[2,2,3,16,704]{4,3,2,1,0:T(8,128)(2,1)S(1)}, bf16[2,2,3,16,704]{4,3,2,1,0:T(8,128)(2,1)S(1)}, u32[]{:S(2)}, u32[]{:S(2)}) %collective-permute-start.53) | collective-permute-done | bytes 270368 | tf_op jit(solution)/shard_map/ppermute | solution.py:45
  363.5 7.0 %shard_map.229 = (bf16[8,128,2048]{2,1,0:T(8,128)(2,1)}, f32[8,2048]{1,0:T(8,128)S(1)}) custom-call(s32[8]{0:T(128)S(1)} %stack.242.chunk.nat, bf16[256,256]{1,0:T(8,128)(2,1)S(1)} %get-tuple-element.194.refs_20_.dq0_ref, bf16[512,256]{1,0:T(8,128)(2,1)S(1)} %get-tuple-element.203.refs_21_.dq1_ref, bf16[256,256]{1,0:T(8,128)(2,1)S(1)} %get-tuple-element.214.refs_22_.dq2_ref, ...), custom_call_target="tpu_custom_call" | custom-call | flops 1000 | bytes 1500000 | tf_op jit(solution)/shard_map/pallas_call | solution.py:136
  374.8 11.8 %shard_map.228 = (bf16[4,4,2,16,576]{4,3,2,1,0:T(8,128)(2,1)}, bf16[4,4,2,16,576]{4,3,2,1,0:T(8,128)(2,1)}, bf16[4,4,2,16,576]{4,3,2,1,0:T(8,128)(2,1)}, bf16[4,4,2,16,576]{4,3,2,1,0:T(8,128)(2,1)}) custom-call(s32[8]{0:T(128)} %copy-done.55, s32[4]{0:T(128)} %copy-done.46, s32[4]{0:T(128)} %copy-done.48, s32[1]{0:T(128)} %bitcast.16.core, s32[2]{0:T(128)} %copy-done.54, ...), custom_call_target="tpu_custom_call" | custom-call | flops 1000 | bytes 3000000 | tf_op jit(solution)/shard_map/pallas_call | solution.py:136
  386.6 3.2 collective-permute-done.56
  391.0 4.0 collective-permute-start.62
  398.1 4.1 collective-permute-done.62
  404.3 9.8 %collective-permute-done.58 = bf16[4,4,2,16,576]{4,3,2,1,0:T(8,128)(2,1)S(1)} collective-permute-done((bf16[4,4,2,16,576]{4,3,2,1,0:T(8,128)(2,1)}, bf16[4,4,2,16,576]{4,3,2,1,0:T(8,128)(2,1)S(1)}, u32[]{:S(2)}, u32[]{:S(2)}) %collective-permute-start.58) | collective-permute-done | bytes 589856 | tf_op jit(solution)/shard_map/ppermute | solution.py:45
  418.0 3.0 collective-permute-done.61
  427.9 3.6 collective-permute-done.66
  435.8 4.4 collective-permute-done.79
  447.7 3.1 collective-permute-start.73
  450.8 5.0 collective-permute-done.70
  458.5 6.0 %collective-permute-done.71 = bf16[4,2,16,256]{3,2,1,0:T(8,128)(2,1)S(1)} collective-permute-done((bf16[4,2,16,256]{3,2,1,0:T(8,128)(2,1)S(1)}, bf16[4,2,16,256]{3,2,1,0:T(8,128)(2,1)S(1)}, u32[]{:S(2)}, u32[]{:S(2)}) %collective-permute-start.71) | collective-permute-done | bytes 65568 | tf_op jit(solution)/shard_map/ppermute | solution.py:45
  468.2 3.3 collective-permute-done.75
  475.3 3.2 collective-permute-start.78
  481.2 14.7 %collective-permute-done.82.refs_3_ = bf16[2,2,4,3,16,704]{5,4,3,2,1,0:T(8,128)(2,1)} collective-permute-done((bf16[2,2,4,3,16,704]{5,4,3,2,1,0:T(8,128)(2,1)}, bf16[2,2,4,3,16,704]{5,4,3,2,1,0:T(8,128)(2,1)}, u32[]{:S(2)}, u32[]{:S(2)}) %collective-permute-start.82) | collective-permute-done | bytes 1081376 | tf_op jit(solution)/shard_map/ppermute | solution.py:45
  495.9 6.4 %shard_map.231 = (f32[128,5632]{1,0:T(8,128)}, f32[128,5632]{1,0:T(8,128)}, f32[5632,128]{1,0:T(8,128)}) custom-call(s32[5]{0:T(128)S(1)} %copy-done.51, s32[4]{0:T(128)S(1)} %copy-done.47, s32[4]{0:T(128)S(1)} %copy-done.49, s32[1]{0:T(128)} %bitcast.16.core, bf16[2,2,4,3,16,704]{5,4,3,2,1,0:T(8,128)(2,1)S(1)} %pad_maximum_fusion.1.refs_0_, ...), custom_call_target="tpu_custom_call" | custom-call | flops 1000 | bytes 1500000 | tf_op jit(solution)/shard_map/pallas_call | solution.py:136
  (437 shorter events, 151.8 us)
Async XLA Ops:
  7.2 64.0 %all-gather.7.cloned.1.call-start = ((), (), s32[]{:S(2)}) async-start(), calls=%async_computation.3 | async-start | bytes 4718592 | tf_op jit(solution)/shard_map/all_gather | solution.py:809
  28.5 104.4 %all-gather.11.cloned.1.call-start = ((), (), s32[]{:S(2)}) async-start(), calls=%async_computation.8 | async-start | bytes 5898240 | tf_op jit(solution)/shard_map/all_gather | solution.py:839
  33.6 22.3 %collective-permute-start.24 = (bf16[4,3,32,704]{3,2,1,0:T(8,128)(2,1)}, bf16[4,3,32,704]{3,2,1,0:T(8,128)(2,1)}, u32[]{:S(2)}, u32[]{:S(2)}) collective-permute-start(bf16[4,3,32,704]{3,2,1,0:T(8,128)(2,1)} %get-tuple-element.154), channel_id=1, source_target_pairs={{0,1},{1,0},{2,3},{3,2},{4,5},{5,4},{6,7},{7,6},{8,9},{9,8},{10,11... | collective-permute-start | bytes 1622024 | tf_op jit(solution)/shard_map/ppermute | solution.py:45
  33.7 18.0 %collective-permute-start.4 = (bf16[8,32,256]{2,1,0:T(8,128)(2,1)S(1)}, bf16[8,32,256]{2,1,0:T(8,128)(2,1)S(1)}, u32[]{:S(2)}, u32[]{:S(2)}) collective-permute-start(bf16[8,32,256]{2,1,0:T(8,128)(2,1)S(1)} %bitcast.210), channel_id=1, source_target_pairs={{0,0},{1,8},{2,1},{3,9},{4,2},{5,10},{6,3},{7,11},{8,4},{9,12},{10... | collective-permute-start | bytes 393224 | tf_op jit(solution)/shard_map/ppermute | solution.py:45
  57.9 19.5 %collective-permute-start.25 = (bf16[2,3,32,704]{3,2,1,0:T(8,128)(2,1)}, bf16[2,3,32,704]{3,2,1,0:T(8,128)(2,1)}, u32[]{:S(2)}, u32[]{:S(2)}) collective-permute-start(bf16[2,3,32,704]{3,2,1,0:T(8,128)(2,1)} %pad_maximum_fusion.7), channel_id=1, source_target_pairs={{0,2},{1,7},{2,4},{3,1},{4,6},{5,3},{6,0},{7,5},{8,10},{9,15},{10,... | collective-permute-start | bytes 811016 | tf_op jit(solution)/shard_map/ppermute | solution.py:45
  60.8 16.6 %collective-permute-start.26 = (bf16[2,3,32,704]{3,2,1,0:T(8,128)(2,1)}, bf16[2,3,32,704]{3,2,1,0:T(8,128)(2,1)}, u32[]{:S(2)}, u32[]{:S(2)}) collective-permute-start(bf16[2,3,32,704]{3,2,1,0:T(8,128)(2,1)} %pad_maximum_fusion.8), channel_id=1, source_target_pairs={{0,6},{1,3},{2,0},{3,5},{4,2},{5,7},{6,4},{7,1},{8,14},{9,11},{10,... | collective-permute-start | bytes 811016 | tf_op jit(solution)/shard_map/ppermute | solution.py:45
  62.6 14.8 %collective-permute-start.27 = (bf16[2,3,32,704]{3,2,1,0:T(8,128)(2,1)}, bf16[2,3,32,704]{3,2,1,0:T(8,128)(2,1)}, u32[]{:S(2)}, u32[]{:S(2)}) collective-permute-start(bf16[2,3,32,704]{3,2,1,0:T(8,128)(2,1)} %pad_maximum_fusion.9), channel_id=1, source_target_pairs={{0,4},{1,5},{2,6},{3,7},{4,0},{5,1},{6,2},{7,3},{8,12},{9,13},{10,... | collective-permute-start | bytes 811016 | tf_op jit(solution)/shard_map/ppermute | solution.py:45
  79.8 120.3 %all-gather.9.cloned.1.call-start = ((), (), s32[]{:S(2)}) async-start(), calls=%async_computation.4 | async-start | bytes 4718592 | tf_op jit(solution)/shard_map/all_gather | solution.py:823
  81.1 282.3 %reduce-scatter.6.cloned.1.call-start = ((), (), s32[]{:S(2)}) async-start(), calls=%async_computation.6 | async-start | bytes 5898240 | tf_op jit(solution)/shard_map/reduce_scatter | solution.py:884
  132.8 54.4 %collective-permute-start.28 = (bf16[4,8,3,32,704]{4,3,2,1,0:T(8,128)(2,1)}, bf16[4,8,3,32,704]{4,3,2,1,0:T(8,128)(2,1)}, u32[]{:S(2)}, u32[]{:S(2)}) collective-permute-start(bf16[4,8,3,32,704]{4,3,2,1,0:T(8,128)(2,1)} %bitcast.183), channel_id=1, source_target_pairs={{0,8},{1,73},{2,10},{3,75},{4,12},{5,77},{6,14},{7,79},{8,64},{9,1... | collective-permute-start | bytes 12976136 | tf_op jit(solution)/shard_map/ppermute | solution.py:45
  134.8 20.5 %collective-permute-start.21 = (bf16[128,2048]{1,0:T(8,128)(2,1)S(1)}, bf16[128,2048]{1,0:T(8,128)(2,1)S(1)}, u32[]{:S(2)}, u32[]{:S(2)}) collective-permute-start(bf16[128,2048]{1,0:T(8,128)(2,1)S(1)} %add_convert_fusion.6), channel_id=1, source_target_pairs={{0,4},{1,5},{2,6},{3,7},{4,0},{5,1},{6,2},{7,3},{8,12},{9,13},{10,... | collective-permute-start | bytes 1572872 | tf_op jit(solution)/shard_map/ppermute | solution.py:45
  138.2 38.5 %collective-permute-start.20 = (bf16[128,2048]{1,0:T(8,128)(2,1)S(1)}, bf16[128,2048]{1,0:T(8,128)(2,1)S(1)}, u32[]{:S(2)}, u32[]{:S(2)}) collective-permute-start(bf16[128,2048]{1,0:T(8,128)(2,1)S(1)} %add_convert_fusion.7), channel_id=1, source_target_pairs={{0,2},{1,7},{2,4},{3,1},{4,6},{5,3},{6,0},{7,5},{8,10},{9,15},{10,... | collective-permute-start | bytes 1572872 | tf_op jit(solution)/shard_map/ppermute | solution.py:45
  140.1 36.5 %collective-permute-start.19 = (bf16[128,2048]{1,0:T(8,128)(2,1)S(1)}, bf16[128,2048]{1,0:T(8,128)(2,1)S(1)}, u32[]{:S(2)}, u32[]{:S(2)}) collective-permute-start(bf16[128,2048]{1,0:T(8,128)(2,1)S(1)} %add_convert_fusion.8), channel_id=1, source_target_pairs={{0,6},{1,3},{2,0},{3,5},{4,2},{5,7},{6,4},{7,1},{8,14},{9,11},{10,... | collective-permute-start | bytes 1572872 | tf_op jit(solution)/shard_map/ppermute | solution.py:45
  145.7 30.9 %collective-permute-start.18 = (bf16[128,2048]{1,0:T(8,128)(2,1)S(1)}, bf16[128,2048]{1,0:T(8,128)(2,1)S(1)}, u32[]{:S(2)}, u32[]{:S(2)}) collective-permute-start(bf16[128,2048]{1,0:T(8,128)(2,1)S(1)} %get-tuple-element.151), channel_id=1, source_target_pairs={{0,1},{1,0},{2,3},{3,2},{4,5},{5,4},{6,7},{7,6},{8,9},{9,8},{10,11... | collective-permute-start | bytes 1572872 | tf_op jit(solution)/shard_map/ppermute | solution.py:45
  177.5 18.3 %collective-permute-start.23 = (bf16[128,2048]{1,0:T(8,128)(2,1)S(1)}, bf16[128,2048]{1,0:T(8,128)(2,1)}, u32[]{:S(2)}, u32[]{:S(2)}) collective-permute-start(bf16[128,2048]{1,0:T(8,128)(2,1)S(1)} %multiply_convert_fusion.refs_0_), channel_id=1, source_target_pairs={{0,2},{1,7},{2,4},{3,1},{4,6},{5,3},{6,0},{7,5},{8,10},{9,15},{10,... | collective-permute-start | bytes 1572872 | tf_op jit(solution)/shard_map/ppermute | solution.py:45
  180.0 20.0 %collective-permute-start.22 = (bf16[128,2048]{1,0:T(8,128)(2,1)S(1)}, bf16[128,2048]{1,0:T(8,128)(2,1)}, u32[]{:S(2)}, u32[]{:S(2)}) collective-permute-start(bf16[128,2048]{1,0:T(8,128)(2,1)S(1)} %multiply_convert_fusion.refs_0_), channel_id=1, source_target_pairs={{0,1},{1,0},{2,3},{3,2},{4,5},{5,4},{6,7},{7,6},{8,9},{9,8},{10,11... | collective-permute-start | bytes 1572872 | tf_op jit(solution)/shard_map/ppermute | solution.py:45
  195.9 23.7 %collective-permute-start.31 = (bf16[128,2048]{1,0:T(8,128)(2,1)S(1)}, bf16[128,2048]{1,0:T(8,128)(2,1)}, u32[]{:S(2)}, u32[]{:S(2)}) collective-permute-start(bf16[128,2048]{1,0:T(8,128)(2,1)S(1)} %multiply_convert_fusion.refs_0_), channel_id=1, source_target_pairs={{0,4},{1,5},{2,6},{3,7},{4,0},{5,1},{6,2},{7,3},{8,12},{9,13},{10,... | collective-permute-start | bytes 1572872 | tf_op jit(solution)/shard_map/ppermute | solution.py:45
  198.9 20.7 %collective-permute-start.30 = (bf16[128,2048]{1,0:T(8,128)(2,1)S(1)}, bf16[128,2048]{1,0:T(8,128)(2,1)}, u32[]{:S(2)}, u32[]{:S(2)}) collective-permute-start(bf16[128,2048]{1,0:T(8,128)(2,1)S(1)} %multiply_convert_fusion.refs_0_), channel_id=1, source_target_pairs={{0,6},{1,3},{2,0},{3,5},{4,2},{5,7},{6,4},{7,1},{8,14},{9,11},{10,... | collective-permute-start | bytes 1572872 | tf_op jit(solution)/shard_map/ppermute | solution.py:45
  250.8 28.1 %collective-permute-start.36 = (bf16[128,2048]{1,0:T(8,128)(2,1)}, bf16[128,2048]{1,0:T(8,128)(2,1)}, u32[]{:S(2)}, u32[]{:S(2)}) collective-permute-start(bf16[128,2048]{1,0:T(8,128)(2,1)} %fusion.11), channel_id=1, source_target_pairs={{0,6},{1,3},{2,0},{3,5},{4,2},{5,7},{6,4},{7,1},{8,14},{9,11},{10,... | collective-permute-start | bytes 1572872 | tf_op jit(solution)/shard_map/ppermute | solution.py:45
  253.9 25.0 %collective-permute-start.38 = (bf16[128,2048]{1,0:T(8,128)(2,1)}, bf16[128,2048]{1,0:T(8,128)(2,1)}, u32[]{:S(2)}, u32[]{:S(2)}) collective-permute-start(bf16[128,2048]{1,0:T(8,128)(2,1)} %get-tuple-element.266), channel_id=1, source_target_pairs={{0,4},{1,5},{2,6},{3,7},{4,0},{5,1},{6,2},{7,3},{8,12},{9,13},{10,... | collective-permute-start | bytes 1572872 | tf_op jit(solution)/shard_map/ppermute | solution.py:45
  255.2 23.7 %collective-permute-start.37 = (bf16[128,2048]{1,0:T(8,128)(2,1)}, bf16[128,2048]{1,0:T(8,128)(2,1)}, u32[]{:S(2)}, u32[]{:S(2)}) collective-permute-start(bf16[128,2048]{1,0:T(8,128)(2,1)} %get-tuple-element.267), channel_id=1, source_target_pairs={{0,2},{1,7},{2,4},{3,1},{4,6},{5,3},{6,0},{7,5},{8,10},{9,15},{10,... | collective-permute-start | bytes 1572872 | tf_op jit(solution)/shard_map/ppermute | solution.py:45
  278.9 112.1 %reduce-scatter.4.cloned.1.call-start = ((), (), s32[]{:S(2)}) async-start(), calls=%async_computation.5 | async-start | bytes 4718592 | tf_op jit(solution)/shard_map/reduce_scatter | solution.py:885
  279.5 134.8 %all-gather.13.cloned.1.call-start = ((), (), s32[]{:S(2)}) async-start(), calls=%async_computation.9 | async-start | bytes 1114112 | tf_op jit(solution)/shard_map/all_gather | solution.py:926
  279.6 24.0 %collective-permute-start.45 = (bf16[4,2,2,3,16,704]{5,4,3,2,1,0:T(8,128)(2,1)}, bf16[4,2,2,3,16,704]{5,4,3,2,1,0:T(8,128)(2,1)S(1)}, u32[]{:S(2)}, u32[]{:S(2)}) collective-permute-start(bf16[4,2,2,3,16,704]{5,4,3,2,1,0:T(8,128)(2,1)} %get-tuple-element.189), channel_id=1, source_target_pairs={{0,8},{1,73},{2,10},{3,75},{4,12},{5,77},{6,14},{7,79},{8,64},{9,1... | collective-permute-start | bytes 3244040 | tf_op jit(solution)/shard_map/ppermute | solution.py:45
  285.8 14.2 %collective-permute-start.41 = (bf16[128,2048]{1,0:T(8,128)(2,1)S(1)}, bf16[128,2048]{1,0:T(8,128)(2,1)S(1)}, u32[]{:S(2)}, u32[]{:S(2)}) collective-permute-start(bf16[128,2048]{1,0:T(8,128)(2,1)S(1)} %get-tuple-element.255.refs_1_.refs_8_), channel_id=1, source_target_pairs={{0,6},{1,3},{2,0},{3,5},{4,2},{5,7},{6,4},{7,1},{8,14},{9,11},{10,... | collective-permute-start | bytes 1572872 | tf_op jit(solution)/shard_map/ppermute | solution.py:45
  288.2 13.2 %collective-permute-start.40 = (bf16[128,2048]{1,0:T(8,128)(2,1)S(1)}, bf16[128,2048]{1,0:T(8,128)(2,1)S(1)}, u32[]{:S(2)}, u32[]{:S(2)}) collective-permute-start(bf16[128,2048]{1,0:T(8,128)(2,1)S(1)} %get-tuple-element.255.refs_1_.refs_8_), channel_id=1, source_target_pairs={{0,2},{1,7},{2,4},{3,1},{4,6},{5,3},{6,0},{7,5},{8,10},{9,15},{10,... | collective-permute-start | bytes 1572872 | tf_op jit(solution)/shard_map/ppermute | solution.py:45
  303.3 29.4 %collective-permute-start.47 = (bf16[4,2,2,3,16,704]{5,4,3,2,1,0:T(8,128)(2,1)S(1)}, bf16[4,2,2,3,16,704]{5,4,3,2,1,0:T(8,128)(2,1)S(1)}, u32[]{:S(2)}, u32[]{:S(2)}) collective-permute-start(bf16[4,2,2,3,16,704]{5,4,3,2,1,0:T(8,128)(2,1)S(1)} %copy-done.84), channel_id=1, source_target_pairs={{0,72},{1,9},{2,74},{3,11},{4,76},{5,13},{6,78},{7,15},{8,0},{9,65... | collective-permute-start | bytes 3244040 | tf_op jit(solution)/shard_map/ppermute | solution.py:45
  303.9 41.3 %collective-permute-start.48 = (bf16[4,2,2,3,16,704]{5,4,3,2,1,0:T(8,128)(2,1)S(1)}, bf16[4,2,2,3,16,704]{5,4,3,2,1,0:T(8,128)(2,1)S(1)}, u32[]{:S(2)}, u32[]{:S(2)}) collective-permute-start(bf16[4,2,2,3,16,704]{5,4,3,2,1,0:T(8,128)(2,1)S(1)} %add_convert_fusion.1), channel_id=1, source_target_pairs={{0,8},{1,73},{2,10},{3,75},{4,12},{5,77},{6,14},{7,79},{8,64},{9,1... | collective-permute-start | bytes 3244040 | tf_op jit(solution)/shard_map/ppermute | solution.py:45
  306.9 22.4 %collective-permute-start.44 = (bf16[128,2048]{1,0:T(8,128)(2,1)S(1)}, bf16[128,2048]{1,0:T(8,128)(2,1)S(1)}, u32[]{:S(2)}, u32[]{:S(2)}) collective-permute-start(bf16[128,2048]{1,0:T(8,128)(2,1)S(1)} %get-tuple-element.255.refs_1_.refs_8_), channel_id=1, source_target_pairs={{0,4},{1,5},{2,6},{3,7},{4,0},{5,1},{6,2},{7,3},{8,12},{9,13},{10,... | collective-permute-start | bytes 1572872 | tf_op jit(solution)/shard_map/ppermute | solution.py:45
  345.9 17.2 %collective-permute-start.53 = (bf16[2,2,3,16,704]{4,3,2,1,0:T(8,128)(2,1)S(1)}, bf16[2,2,3,16,704]{4,3,2,1,0:T(8,128)(2,1)S(1)}, u32[]{:S(2)}, u32[]{:S(2)}) collective-permute-start(bf16[2,2,3,16,704]{4,3,2,1,0:T(8,128)(2,1)S(1)} %get-tuple-element.264), channel_id=1, source_target_pairs={{0,16},{1,49},{2,18},{3,51},{4,20},{5,53},{6,22},{7,55},{8,24},{9,... | collective-permute-start | bytes 811016 | tf_op jit(solution)/shard_map/ppermute | solution.py:45
  346.0 17.1 %collective-permute-start.52 = (bf16[2,2,3,16,704]{4,3,2,1,0:T(8,128)(2,1)S(1)}, bf16[2,2,3,16,704]{4,3,2,1,0:T(8,128)(2,1)S(1)}, u32[]{:S(2)}, u32[]{:S(2)}) collective-permute-start(bf16[2,2,3,16,704]{4,3,2,1,0:T(8,128)(2,1)S(1)} %get-tuple-element.265), channel_id=1, source_target_pairs={{0,48},{1,17},{2,50},{3,19},{4,52},{5,21},{6,54},{7,23},{8,56},{9,... | collective-permute-start | bytes 811016 | tf_op jit(solution)/shard_map/ppermute | solution.py:45
  349.4 13.9 %collective-permute-start.50 = (bf16[1024,64]{1,0:T(8,128)(2,1)S(1)}, bf16[1024,64]{1,0:T(8,128)(2,1)S(1)}, u32[]{:S(2)}, u32[]{:S(2)}) collective-permute-start(bf16[1024,64]{1,0:T(8,128)(2,1)S(1)} %slice.380), channel_id=1, source_target_pairs={{0,8},{1,9},{2,10},{3,11},{4,12},{5,13},{6,14},{7,15},{8,0},{9,1},... | collective-permute-start | bytes 393224 | tf_op jit(solution)/shard_map/ppermute | solution.py:45
  371.2 100.3 %reduce-scatter.8.cloned.1.call-start = ((), (), s32[]{:S(2)}) async-start(), calls=%async_computation.7 | async-start | bytes 4718592 | tf_op jit(solution)/shard_map/reduce_scatter | solution.py:934
  372.5 14.1 %collective-permute-start.54 = (bf16[2,2,3,16,704]{4,3,2,1,0:T(8,128)(2,1)S(1)}, bf16[2,2,3,16,704]{4,3,2,1,0:T(8,128)(2,1)S(1)}, u32[]{:S(2)}, u32[]{:S(2)}) collective-permute-start(bf16[2,2,3,16,704]{4,3,2,1,0:T(8,128)(2,1)S(1)} %get-tuple-element.260), channel_id=1, source_target_pairs={{0,64},{1,65},{2,66},{3,67},{4,68},{5,69},{6,70},{7,71},{8,72},{9,... | collective-permute-start | bytes 811016 | tf_op jit(solution)/shard_map/ppermute | solution.py:45
  372.6 17.3 %collective-permute-start.56 = (bf16[2,2,3,16,704]{4,3,2,1,0:T(8,128)(2,1)S(1)}, bf16[2,2,3,16,704]{4,3,2,1,0:T(8,128)(2,1)S(1)}, u32[]{:S(2)}, u32[]{:S(2)}) collective-permute-start(bf16[2,2,3,16,704]{4,3,2,1,0:T(8,128)(2,1)S(1)} %get-tuple-element.261), channel_id=1, source_target_pairs={{0,8},{1,73},{2,10},{3,75},{4,12},{5,77},{6,14},{7,79},{8,64},{9,1... | collective-permute-start | bytes 811016 | tf_op jit(solution)/shard_map/ppermute | solution.py:45
  374.1 15.7 %collective-permute-start.55 = (bf16[2,2,3,16,704]{4,3,2,1,0:T(8,128)(2,1)S(1)}, bf16[2,2,3,16,704]{4,3,2,1,0:T(8,128)(2,1)S(1)}, u32[]{:S(2)}, u32[]{:S(2)}) collective-permute-start(bf16[2,2,3,16,704]{4,3,2,1,0:T(8,128)(2,1)S(1)} %get-tuple-element.262), channel_id=1, source_target_pairs={{0,72},{1,9},{2,74},{3,11},{4,76},{5,13},{6,78},{7,15},{8,0},{9,65... | collective-permute-start | bytes 811016 | tf_op jit(solution)/shard_map/ppermute | solution.py:45
  396.0 31.6 %collective-permute-start.57 = (bf16[4,4,2,16,576]{4,3,2,1,0:T(8,128)(2,1)}, bf16[4,4,2,16,576]{4,3,2,1,0:T(8,128)(2,1)S(1)}, u32[]{:S(2)}, u32[]{:S(2)}) collective-permute-start(bf16[4,4,2,16,576]{4,3,2,1,0:T(8,128)(2,1)} %get-tuple-element.230), channel_id=1, source_target_pairs={{0,48},{1,17},{2,50},{3,19},{4,52},{5,21},{6,54},{7,23},{8,56},{9,... | collective-permute-start | bytes 1769480 | tf_op jit(solution)/shard_map/ppermute | solution.py:45
  396.3 17.8 %collective-permute-start.58 = (bf16[4,4,2,16,576]{4,3,2,1,0:T(8,128)(2,1)}, bf16[4,4,2,16,576]{4,3,2,1,0:T(8,128)(2,1)S(1)}, u32[]{:S(2)}, u32[]{:S(2)}) collective-permute-start(bf16[4,4,2,16,576]{4,3,2,1,0:T(8,128)(2,1)} %get-tuple-element.233), channel_id=1, source_target_pairs={{0,16},{1,49},{2,18},{3,51},{4,20},{5,53},{6,22},{7,55},{8,24},{9,... | collective-permute-start | bytes 1769480 | tf_op jit(solution)/shard_map/ppermute | solution.py:45
  404.2 16.8 %collective-permute-start.64 = (bf16[4,3,16,704]{3,2,1,0:T(8,128)(2,1)S(1)}, bf16[4,3,16,704]{3,2,1,0:T(8,128)(2,1)S(1)}, u32[]{:S(2)}, u32[]{:S(2)}) collective-permute-start(bf16[4,3,16,704]{3,2,1,0:T(8,128)(2,1)S(1)} %pad_maximum_fusion.10), channel_id=1, source_target_pairs={{0,1},{1,0},{2,3},{3,2},{4,5},{5,4},{6,7},{7,6},{8,9},{9,8},{10,11... | collective-permute-start | bytes 811016 | tf_op jit(solution)/shard_map/ppermute | solution.py:45
  414.2 13.4 %collective-permute-start.59 = (bf16[4,4,2,16,576]{4,3,2,1,0:T(8,128)(2,1)S(1)}, bf16[4,4,2,16,576]{4,3,2,1,0:T(8,128)(2,1)S(1)}, u32[]{:S(2)}, u32[]{:S(2)}) collective-permute-start(bf16[4,4,2,16,576]{4,3,2,1,0:T(8,128)(2,1)S(1)} %add_convert_fusion.3), channel_id=1, source_target_pairs={{0,16},{1,49},{2,18},{3,51},{4,20},{5,53},{6,22},{7,55},{8,24},{9,... | collective-permute-start | bytes 1769480 | tf_op jit(solution)/shard_map/ppermute | solution.py:45
  422.2 17.9 %collective-permute-start.79 = (bf16[2,4,3,16,704]{4,3,2,1,0:T(8,128)(2,1)S(1)}, bf16[2,4,3,16,704]{4,3,2,1,0:T(8,128)(2,1)S(1)}, u32[]{:S(2)}, u32[]{:S(2)}) collective-permute-start(bf16[2,4,3,16,704]{4,3,2,1,0:T(8,128)(2,1)S(1)} %get-tuple-element.272), channel_id=1, source_target_pairs={{0,64},{1,65},{2,66},{3,67},{4,68},{5,69},{6,70},{7,71},{8,72},{9,... | collective-permute-start | bytes 1622024 | tf_op jit(solution)/shard_map/ppermute | solution.py:45
  433.7 12.1 %collective-permute-start.69 = (bf16[4,2,16,576]{3,2,1,0:T(8,128)(2,1)S(1)}, bf16[4,2,16,576]{3,2,1,0:T(8,128)(2,1)S(1)}, u32[]{:S(2)}, u32[]{:S(2)}) collective-permute-start(bf16[4,2,16,576]{3,2,1,0:T(8,128)(2,1)S(1)} %get-tuple-element.269), channel_id=1, source_target_pairs={{0,8},{1,73},{2,10},{3,75},{4,12},{5,77},{6,14},{7,79},{8,64},{9,1... | collective-permute-start | bytes 442376 | tf_op jit(solution)/shard_map/ppermute | solution.py:45
  440.3 27.3 %collective-permute-start.81 = (bf16[2,2,4,3,16,704]{5,4,3,2,1,0:T(8,128)(2,1)S(1)}, bf16[2,2,4,3,16,704]{5,4,3,2,1,0:T(8,128)(2,1)S(1)}, u32[]{:S(2)}, u32[]{:S(2)}) collective-permute-start(bf16[2,2,4,3,16,704]{5,4,3,2,1,0:T(8,128)(2,1)S(1)} %pad_maximum_fusion.1.refs_0_), channel_id=1, source_target_pairs={{0,48},{1,17},{2,50},{3,19},{4,52},{5,21},{6,54},{7,23},{8,56},{9,... | collective-permute-start | bytes 3244040 | tf_op jit(solution)/shard_map/ppermute | solution.py:45
  442.5 25.1 %collective-permute-start.80 = (bf16[2,2,4,3,16,704]{5,4,3,2,1,0:T(8,128)(2,1)S(1)}, bf16[2,2,4,3,16,704]{5,4,3,2,1,0:T(8,128)(2,1)}, u32[]{:S(2)}, u32[]{:S(2)}) collective-permute-start(bf16[2,2,4,3,16,704]{5,4,3,2,1,0:T(8,128)(2,1)S(1)} %pad_maximum_fusion.1.refs_0_), channel_id=1, source_target_pairs={{0,16},{1,49},{2,18},{3,51},{4,20},{5,53},{6,22},{7,55},{8,24},{9,... | collective-permute-start | bytes 3244040 | tf_op jit(solution)/shard_map/ppermute | solution.py:45
  467.6 28.3 %collective-permute-start.82 = (bf16[2,2,4,3,16,704]{5,4,3,2,1,0:T(8,128)(2,1)}, bf16[2,2,4,3,16,704]{5,4,3,2,1,0:T(8,128)(2,1)}, u32[]{:S(2)}, u32[]{:S(2)}) collective-permute-start(bf16[2,2,4,3,16,704]{5,4,3,2,1,0:T(8,128)(2,1)} %collective-permute-done.80.refs_1_), channel_id=1, source_target_pairs={{0,16},{1,49},{2,18},{3,51},{4,20},{5,53},{6,22},{7,55},{8,24},{9,... | collective-permute-start | bytes 3244040 | tf_op jit(solution)/shard_map/ppermute | solution.py:45
  475.3 27.0 %collective-permute-start.78 = (bf16[2,2,4,16,576]{4,3,2,1,0:T(8,128)(2,1)S(1)}, bf16[2,2,4,16,576]{4,3,2,1,0:T(8,128)(2,1)S(1)}, u32[]{:S(2)}, u32[]{:S(2)}) collective-permute-start(bf16[2,2,4,16,576]{4,3,2,1,0:T(8,128)(2,1)S(1)} %pad_maximum_fusion.5.refs_0_), channel_id=1, source_target_pairs={{0,32},{1,33},{2,34},{3,35},{4,36},{5,37},{6,38},{7,39},{8,40},{9,... | collective-permute-start | bytes 884744 | tf_op jit(solution)/shard_map/ppermute | solution.py:45
  478.6 23.7 %collective-permute-start.77 = (bf16[2,2,4,16,576]{4,3,2,1,0:T(8,128)(2,1)S(1)}, bf16[2,2,4,16,576]{4,3,2,1,0:T(8,128)(2,1)S(1)}, u32[]{:S(2)}, u32[]{:S(2)}) collective-permute-start(bf16[2,2,4,16,576]{4,3,2,1,0:T(8,128)(2,1)S(1)} %pad_maximum_fusion.5.refs_0_), channel_id=1, source_target_pairs={{0,48},{1,17},{2,50},{3,19},{4,52},{5,21},{6,54},{7,23},{8,56},{9,... | collective-permute-start | bytes 884744 | tf_op jit(solution)/shard_map/ppermute | solution.py:45
  479.0 23.3 %collective-permute-start.76 = (bf16[2,2,4,16,576]{4,3,2,1,0:T(8,128)(2,1)S(1)}, bf16[2,2,4,16,576]{4,3,2,1,0:T(8,128)(2,1)S(1)}, u32[]{:S(2)}, u32[]{:S(2)}) collective-permute-start(bf16[2,2,4,16,576]{4,3,2,1,0:T(8,128)(2,1)S(1)} %pad_maximum_fusion.5.refs_0_), channel_id=1, source_target_pairs={{0,16},{1,49},{2,18},{3,51},{4,20},{5,53},{6,22},{7,55},{8,24},{9,... | collective-permute-start | bytes 884744 | tf_op jit(solution)/shard_map/ppermute | solution.py:45
  (129 other events, 2114.8 us)
Sparse Core Ops, SparseCore 0:
  28.6 32.7 all-gather.6
  79.9 52.9 all-gather.10
  134.5 45.8 all-gather.8
  279.0 50.8 reduce-scatter.5
  332.2 38.1 reduce-scatter.3
  372.0 32.7 all-gather.12
  407.2 40.0 reduce-scatter.7

commit v12 on v11

--- a/solution.py
+++ b/solution.py
@@ -678,27 +678,31 @@
 
 
 def finish_mlp_kernel(spots, xs, yhs, core, *refs):
-    parts, (gate_ref, up_ref, down_ref), (rows,) = refs[:4], refs[4:7], refs[7:]
+    parts, down_parts, (gate_ref, up_ref, down_ref), (rows,) = refs[:4], refs[4:6], refs[6:9], refs[9:]
     first = core[0] == 0
-    for m, out_ref in enumerate((gate_ref, up_ref, rows)):
-        for r in range(4):
-            for h in range(2):
-                at = at_rows(yhs[h] * 64 + xs[r] * 16, 16)
-                own = parts[r][h, 0, 0, m].astype(F32)
-                other = parts[r][h, 1, 0, m].astype(F32)
-                low, high = jnp.where(first, own, other), jnp.where(first, other, own)
-                out_ref[at, :] = jnp.concatenate([low, high], axis=1)
+
+    def put(out_ref, r, h, own, other):
+        own, other = own.astype(F32), other.astype(F32)
+        low, high = jnp.where(first, own, other), jnp.where(first, other, own)
+        out_ref[at_rows(yhs[h] * 64 + xs[r] * 16, 16), :] = jnp.concatenate([low, high], axis=1)
+
+    for r in range(4):
+        for h in range(2):
+            for m, out_ref in enumerate((gate_ref, up_ref)):
+                put(out_ref, r, h, parts[r][h, 0, 0, m], parts[r][h, 1, 0, m])
+            put(rows, r, h, down_parts[h][r, 0, 0], down_parts[h][r, 1, 0])
     down_ref[...] = rows[...].T
 
 
-def finish_mlp(spots, xs, yhs, core, parts):
+def finish_mlp(spots, xs, yhs, core, parts, down_parts):
     side = pl.BlockSpec((128, 2 * WIDE), lambda p, spots, *_: (0, spots[1 + p]))
     return call(
         finish_mlp_kernel, (spots, xs, yhs, core), (4,),
-        [pl.BlockSpec((2, 2, 1, 3, 16, WIDE), lambda p, *_: (0, 0, p, 0, 0, 0))] * 4,
+        [pl.BlockSpec((2, 2, 1, 2, 16, WIDE), lambda p, *_: (0, 0, p, 0, 0, 0))] * 4
+        + [pl.BlockSpec((4, 2, 1, 16, WIDE), lambda p, *_: (0, 0, p, 0, 0))] * 2,
         [side, side, pl.BlockSpec((2 * WIDE, 128), lambda p, spots, *_: (spots[1 + p], 0))],
         [sds((128, FF), F32), sds((128, FF), F32), sds((FF, 128), F32)], [pltpu.VMEM((128, 2 * WIDE), F32)],
-        5, tuple(parts),
+        5, tuple(parts) + tuple(down_parts),
     )
 
 
@@ -934,16 +938,21 @@
     normed_attn_grad = lax.psum_scatter(attn_partial, "blk", scatter_dimension=0, axis_index_groups=ZC_GROUPS)
 
     layer_out = (residual + after(branch, attn_outs[0]).astype(F32)).astype(BF)[None]
+    down_parts = ring_gather(mlp_sums[:, :, 2], "x")
+    mlp_sums = mlp_sums[:, :, :2]
     mlp_across = across(mlp_sums, "y")
-    gain_grads = jnp.sum(after(gain_grads, mlp_arrived), axis=0)[:2]
+    gain_grads = jnp.sum(after(gain_grads, mlp_swapped), axis=0)[:2]
     gain_grads = gain_grads + across(gain_grads, "y")
-    gain_grads = after(gain_grads, mlp_swapped)
-    gain_grads = gain_grads + across(gain_grads, "x")
-    gain_grads = gain_grads + step(gain_grads, "x", 1)
     mlp_sums = jnp.stack([mlp_sums, mlp_across])
     mlp_first, mlp_second = step(mlp_sums, "x", 1), step(mlp_sums, "x", -1)
-    attn_sums = after(ring_scatter(*attn_outs, "x", attn_outs[0]).astype(BF), gain_grads)
+    down_own = jnp.stack(down_parts)
+    down_other = across(down_own, "y")
+    attn_sums = after(ring_scatter(*attn_outs, "x", attn_outs[0]).astype(BF), gain_grads, *down_parts[1:])
+    gain_grads = gain_grads + across(gain_grads, "x")
     attn_sums = ring_scatter(attn_sums[0], attn_sums[2], attn_sums[3], attn_sums[1], "y").astype(BF)
+    attn_sums = after(attn_sums, gain_grads, down_other)
+    gain_grads = gain_grads + step(gain_grads, "x", 1)
+
     qkv_sums, _, arrived = resplit_back(attn_sums[..., QUERY:])
     out_sums = send(
         after(attn_sums[..., :QUERY], arrived), lambda yh, x, yl, z, c: (yh, x, z // 2, 2 * (z % 2) + c, yl)
@@ -955,7 +964,7 @@
     attn_across = across(attn_sums, "y")
     mlp_sums = (mlp_sums, mlp_first, mlp_second, step(after(mlp_first, mlp_second, arrived), "x", 1))
     attn_sums = ring_gather(after(jnp.stack([attn_sums, attn_across]), tokens_grad), "x")
-    gate_grad, up_grad, down_grad = finish_mlp(spots, xs, yhs, core, mlp_sums)
+    gate_grad, up_grad, down_grad = finish_mlp(spots, xs, yhs, core, mlp_sums, (down_own, down_other))
     query_grad, key_grad, value_grad, output_grad = finish_attn(spots, xs, yhs, core, attn_sums)
     return (
         layer_out,

time: 520 us -> 538 us (1.035)
  Pallas kernels: 167 us -> 155 us
  waiting for transfers between devices: 164 us -> 176 us
  local copies, waits for them, and re-layouts: 26.9 us -> 34.7 us
    pallas_call x20, Pallas kernels: 167 us -> 155 us  [call(): pl.pallas_call(body, grid_spec=pltpu.PrefetchScalarGridSpec(num_scalar_pr...]
    optimization_barrier x1 -> x4, local copies, waits for them, and re-layouts: 0.19 us -> 6.85 us  [after(): return lax.optimization_barrier((value, others))[0]]
    all_gather x1, waiting for transfers between devices: 5.24 us -> 11.8 us  [on_device(): lax.all_gather(exchange(mlp_mine, mlp_other, kv_own), 'batch', axis=0, ax...]
    ppermute x83 -> x87, starting transfers between devices: 106 us -> 112 us  [send(): return lax.ppermute(value, BOTH, pairs)]
    ppermute x83 -> x87, waiting for transfers between devices: 158 us -> 164 us  [send(): return lax.ppermute(value, BOTH, pairs)]
    unnamed x177 -> x187, local copies, waits for them, and re-layouts: 19.7 us -> 18.7 us
  transfers between devices with their start and end apart: 90 -> 94, of which waited for: 36 -> 42; matrix products, arithmetic and copies ran while one was open for 7% -> 7% of each run, Pallas kernels for 28% -> 25%
where the time goes in v12:
time: 538 us; the launch traced here: 528 us
  waiting for transfers between devices  176 us (33%)
  Pallas kernels  155 us (29%)
  starting transfers between devices  112 us (21%)
  local copies, waits for them, and re-layouts  34.7 us (6%)
  other arithmetic  34.3 us (6%)
  between operations  16 us (3%)
    ppermute x87, waiting for transfers between devices, send(): return lax.ppermute(value, BOTH, pairs)  164 us
    pallas_call x20, Pallas kernels, call(): pl.pallas_call(body, grid_spec=pltpu.PrefetchScalarGridSpec(num_scalar_pr...  155 us
    ppermute x87, starting transfers between devices, send(): return lax.ppermute(value, BOTH, pairs)  112 us
    unnamed x187, local copies, waits for them, and re-layouts  18.7 us
    all_gather x1, waiting for transfers between devices, on_device(): lax.all_gather(exchange(mlp_mine, mlp_other, kv_own), 'batch', axis=0, ax...  11.8 us
  transfers between devices with their start and end apart: 94, of which 42 were waited for; matrix products, arithmetic and copies ran while one was open for 7% of the time, Pallas kernels for 25%

profile of v12, /device:TPU:24, one launch (start us, length us, event | category | flops | bytes accessed | tf_op | source)
XLA Modules:
  0.0 528.2 jit_solution(12892203396774949695)
XLA Ops:
  22.2 3.7 collective-permute-done.3
  29.9 2.9 shard_map.220
  33.7 3.9 collective-permute-start.4
  37.8 3.1 collective-permute-start.7
  44.0 3.3 collective-permute-done.7
  47.3 3.3 collective-permute-done.6
  71.3 6.1 %shard_map.214 = (bf16[1024,256]{1,0:T(8,128)(2,1)S(1)}, bf16[2,1024,64]{2,1,0:T(8,128)(2,1)S(1)}) custom-call(s32[8]{0:T(128)S(1)} %stack.254.chunk.nat, bf16[1024,2048]{1,0:T(8,128)(2,1)} %all-gather.7.cloned.1.call-done.refs_0_.refs_1_.refs_2_.refs_3_.refs_4_.refs_5_.refs_6_.refs_7_, ...), custom_call_target="tpu_custom_call" | custom-call | flops 1000 | bytes 1500000 | tf_op jit(solution)/shard_map/pallas_call | solution.py:136
  81.3 7.8 %collective-permute-done.12.other_ref = bf16[4,8,32,256]{3,2,1,0:T(8,128)(2,1)S(1)} collective-permute-done((bf16[4,8,32,256]{3,2,1,0:T(8,128)(2,1)S(1)}, bf16[4,8,32,256]{3,2,1,0:T(8,128)(2,1)S(1)}, u32[]{:S(2)}, u32[]{:S(2)}) %collective-permute-start.12) | collective-permute-done | bytes 524320 | tf_op jit(solution)/shard_map/ppermute | solution.py:45
  89.8 7.4 %collective-permute-done.13 = bf16[2,1024,64]{1,2,0:T(8,128)(2,1)S(1)} collective-permute-done((bf16[2,1024,64]{1,2,0:T(8,128)(2,1)S(1)}, bf16[2,1024,64]{1,2,0:T(8,128)(2,1)S(1)}, u32[]{:S(2)}, u32[]{:S(2)}) %collective-permute-start.13) | collective-permute-done | bytes 262176 | tf_op jit(solution)/shard_map/ppermute | solution.py:45
  104.1 5.4 %shard_map.217 = (bf16[256,256]{1,0:T(8,128)(2,1)S(1)}, bf16[128,2048]{1,0:T(8,128)(2,1)S(1)}, bf16[128,2048]{1,0:T(8,128)(2,1)S(1)}) custom-call(s32[8]{0:T(128)S(1)} %bitcast.201, s32[16]{0:T(128)S(1)} %select_reduce_fusion.1.key_slot, bf16[1024,256]{1,0:T(8,128)(2,1)S(1)} %get-tuple-element.140.q_ref.refs_0_, ...), custom_call_target="tpu_custom_call" | custom-call | flops 1000 | bytes 1800000 | tf_op jit(solution)/shard_map/pallas_call | solution.py:136
  110.7 6.8 %shard_map.216 = (bf16[256,256]{1,0:T(8,128)(2,1)S(1)}, bf16[128,2048]{1,0:T(8,128)(2,1)S(1)}, bf16[128,2048]{1,0:T(8,128)(2,1)S(1)}) custom-call(s32[8]{0:T(128)S(1)} %bitcast.202, s32[16]{0:T(128)S(1)} %select_reduce_fusion.1.key_slot, bf16[1024,256]{1,0:T(8,128)(2,1)S(1)} %get-tuple-element.140.q_ref.refs_0_, ...), custom_call_target="tpu_custom_call" | custom-call | flops 1000 | bytes 1800000 | tf_op jit(solution)/shard_map/pallas_call | solution.py:136
  121.0 11.8 %all-gather.11.cloned.1.call-done = bf16[32,3,32,704]{3,2,1,0:T(8,128)(2,1)} async-done(((bf16[8,3,32,704]{3,2,1,0:T(8,128)(2,1)}), bf16[32,3,32,704]{3,2,1,0:T(8,128)(2,1)}) %all-gather.11.cloned.1.call-update) | async-done | bytes 4325392 | tf_op jit(solution)/shard_map/all_gather | solution.py:843
  134.8 3.2 collective-permute-start.21
  142.8 5.4 %shard_map.219 = (bf16[256,256]{1,0:T(8,128)(2,1)S(1)}, bf16[128,2048]{1,0:T(8,128)(2,1)S(1)}, bf16[128,2048]{1,0:T(8,128)(2,1)S(1)}) custom-call(s32[8]{0:T(128)S(1)} %bitcast.203, s32[16]{0:T(128)S(1)} %select_reduce_fusion.1.key_slot, bf16[1024,256]{1,0:T(8,128)(2,1)S(1)} %get-tuple-element.140.q_ref.refs_0_, ...), custom_call_target="tpu_custom_call" | custom-call | flops 1000 | bytes 1800000 | tf_op jit(solution)/shard_map/pallas_call | solution.py:136
  148.3 6.9 %collective-permute-done.21 = bf16[128,2048]{1,0:T(8,128)(2,1)S(1)} collective-permute-done((bf16[128,2048]{1,0:T(8,128)(2,1)S(1)}, bf16[128,2048]{1,0:T(8,128)(2,1)S(1)}, u32[]{:S(2)}, u32[]{:S(2)}) %collective-permute-start.21) | collective-permute-done | bytes 524320 | tf_op jit(solution)/shard_map/ppermute | solution.py:45
  155.3 21.4 %collective-permute-done.20 = bf16[128,2048]{1,0:T(8,128)(2,1)S(1)} collective-permute-done((bf16[128,2048]{1,0:T(8,128)(2,1)S(1)}, bf16[128,2048]{1,0:T(8,128)(2,1)S(1)}, u32[]{:S(2)}, u32[]{:S(2)}) %collective-permute-start.20) | collective-permute-done | bytes 524320 | tf_op jit(solution)/shard_map/ppermute | solution.py:45
  180.0 7.3 %collective-permute-done.28.other_ref = bf16[4,8,3,32,704]{4,3,2,1,0:T(8,128)(2,1)} collective-permute-done((bf16[4,8,3,32,704]{4,3,2,1,0:T(8,128)(2,1)}, bf16[4,8,3,32,704]{4,3,2,1,0:T(8,128)(2,1)}, u32[]{:S(2)}, u32[]{:S(2)}) %collective-permute-start.28) | collective-permute-done | bytes 4325408 | tf_op jit(solution)/shard_map/ppermute | solution.py:45
  187.3 8.3 %shard_map.221 = bf16[3,2,8,128,704]{4,3,2,1,0:T(8,128)(2,1)} custom-call(s32[8]{0:T(128)S(1)} %stack.266.slot, s32[2]{0:T(128)S(1)} %pad_add_fusion.2.halves, bf16[4,8,3,32,704]{4,3,2,1,0:T(8,128)(2,1)S(1)} %bitcast.199, bf16[4,8,3,32,704]{4,3,2,1,0:T(8,128)(2,1)} %collective-permute-done.28.other_ref), custom_call_target="tpu_custom_call" | custom-call | flops 1000 | bytes 1800000 | tf_op jit(solution)/shard_map/pallas_call | solution.py:136
  196.0 2.9 collective-permute-start.31
  200.1 18.8 %shard_map.222 = (bf16[1024,704]{1,0:T(8,128)(2,1)S(1)}, bf16[1024,704]{1,0:T(8,128)(2,1)}, bf16[1024,704]{1,0:T(8,128)(2,1)}, bf16[128,2048]{1,0:T(8,128)(2,1)S...) custom-call(s32[8]{0:T(128)S(1)} %stack.254.chunk.nat, ...), custom_call_target="tpu_custom_call" | custom-call | flops 1000 | bytes 5400000 | tf_op jit(solution)/shard_map/pallas_call | solution.py:136
  224.1 18.7 %shard_map.223 = (bf16[1024,704]{1,0:T(8,128)(2,1)S(1)}, bf16[1024,704]{1,0:T(8,128)(2,1)}, bf16[1024,704]{1,0:T(8,128)(2,1)}, bf16[128,2048]{1,0:T(8,128)(2,1)S...) custom-call(s32[8]{0:T(128)S(1)} %stack.254.chunk.nat, ...), custom_call_target="tpu_custom_call", output_to_operand_aliasing={{0}: (10, {}), {1}: (11, {}), {2}: (12, {}), {6}: (13, {})} | custom-call | flops 1000 | bytes 5400000 | tf_op jit(solution)/shard_map/pallas_call | solution.py:136
  251.6 19.5 %shard_map.224 = (bf16[4,4,2,2,3,16,704]{6,5,4,3,2,1,0:T(8,128)(2,1)}, bf16[4,2,2,3,16,704]{5,4,3,2,1,0:T(8,128)(2,1)S(1)}, bf16[4,2,2,3,16,704]{5,4,3,2,1,0:T(8...) custom-call(s32[8]{0:T(128)S(1)} %stack.296.column, s32[4]{0:T(128)S(1)} %pad_add_fusion.1.xs, ...), custom_call_target="tpu_custom_call" | custom-call | flops 1000 | bytes 5100000 | tf_op jit(solution)/shard_map/pallas_call | solution.py:136
  272.1 5.0 copy.138
  287.9 7.3 %shard_map.225 = (bf16[256,256]{1,0:T(8,128)(2,1)S(1)}, f32[2048,64]{1,0:T(8,128)S(1)}, f32[2048,64]{1,0:T(8,128)S(1)}) custom-call(s32[8]{0:T(128)S(1)} %bitcast.204, s32[16]{0:T(128)S(1)} %select_reduce_fusion.1.key_slot, s32[1]{0:T(128)} %bitcast.16.core, s32[16]{0:T(128)S(1)} %copy-done.57, bf16[1024,256]{1,0:T(8,128)(2,1)S(1)} %get-tuple-element.140.q_ref.refs_0_, ...), custom_call_target="tpu_custom_call" | custom-call | flops 1000 | bytes 2400000 | tf_op jit(solution)/shard_map/pallas_call | solution.py:136
  295.2 4.8 collective-permute-done.41.refs_3_.refs_12_
  303.8 3.0 collective-permute-start.48
  308.8 18.4 %shard_map.226 = (bf16[512,256]{1,0:T(8,128)(2,1)S(1)}, f32[2048,64]{1,0:T(8,128)S(1)}, f32[2048,64]{1,0:T(8,128)}) custom-call(s32[8]{0:T(128)S(1)} %bitcast.205, s32[16]{0:T(128)S(1)} %select_reduce_fusion.1.key_slot, s32[1]{0:T(128)} %bitcast.16.core, s32[16]{0:T(128)S(1)} %copy-done.57, bf16[1024,256]{1,0:T(8,128)(2,1)S(1)} %get-tuple-element.140.q_ref.refs_0_, ...), custom_call_target="tpu_custom_call" | custom-call | flops 1000 | bytes 4800000 | tf_op jit(solution)/shard_map/pallas_call | solution.py:136
  329.2 3.2 collective-permute-done.47
  332.5 4.7 shard_map.227
  338.0 7.3 %collective-permute-start.51 = (bf16[2,2,3,16,704]{4,3,1,2,0:T(8,128)(2,1)S(1)}, bf16[2,2,3,16,704]{4,3,1,2,0:T(8,128)(2,1)S(1)}, u32[]{:S(2)}, u32[]{:S(2)}) collective-permute-start(bf16[2,2,3,16,704]{4,3,1,2,0:T(8,128)(2,1)S(1)} %get-tuple-element.263), channel_id=1, source_target_pairs={{0,32},{1,33},{2,34},{3,35},{4,36},{5,37},{6,38},{7,39},{8,40},{9,... | collective-permute-start | bytes 811016 | tf_op jit(solution)/shard_map/ppermute | solution.py:45
  349.2 4.0 collective-permute-done.51
  353.2 6.1 %collective-permute-done.53 = bf16[2,2,3,16,704]{4,3,1,2,0:T(8,128)(2,1)S(1)} collective-permute-done((bf16[2,2,3,16,704]{4,3,1,2,0:T(8,128)(2,1)S(1)}, bf16[2,2,3,16,704]{4,3,1,2,0:T(8,128)(2,1)S(1)}, u32[]{:S(2)}, u32[]{:S(2)}) %collective-permute-start.53) | collective-permute-done | bytes 270368 | tf_op jit(solution)/shard_map/ppermute | solution.py:45
  360.1 7.0 %shard_map.229 = (bf16[8,128,2048]{2,1,0:T(8,128)(2,1)}, f32[8,2048]{1,0:T(8,128)S(1)}) custom-call(s32[8]{0:T(128)S(1)} %stack.254.chunk.nat, bf16[256,256]{1,0:T(8,128)(2,1)S(1)} %get-tuple-element.194.refs_20_.dq0_ref, bf16[512,256]{1,0:T(8,128)(2,1)S(1)} %get-tuple-element.203.refs_21_.dq1_ref, bf16[256,256]{1,0:T(8,128)(2,1)S(1)} %get-tuple-element.214.refs_22_.dq2_ref, ...), custom_call_target="tpu_custom_call" | custom-call | flops 1000 | bytes 1500000 | tf_op jit(solution)/shard_map/pallas_call | solution.py:136
  369.2 6.1 %collective-permute-start.54 = (bf16[2,2,3,16,704]{4,3,1,2,0:T(8,128)(2,1)S(1)}, bf16[2,2,3,16,704]{4,3,1,2,0:T(8,128)(2,1)S(1)}, u32[]{:S(2)}, u32[]{:S(2)}) collective-permute-start(bf16[2,2,3,16,704]{4,3,1,2,0:T(8,128)(2,1)S(1)} %get-tuple-element.260), channel_id=1, source_target_pairs={{0,64},{1,65},{2,66},{3,67},{4,68},{5,69},{6,70},{7,71},{8,72},{9,... | collective-permute-start | bytes 811016 | tf_op jit(solution)/shard_map/ppermute | solution.py:45
  377.3 11.8 %shard_map.228 = (bf16[4,4,2,16,576]{4,3,2,1,0:T(8,128)(2,1)}, bf16[4,4,2,16,576]{4,3,2,1,0:T(8,128)(2,1)}, bf16[4,4,2,16,576]{4,3,2,1,0:T(8,128)(2,1)}, bf16[4,4,2,16,576]{4,3,2,1,0:T(8,128)(2,1)}) custom-call(s32[8]{0:T(128)} %copy-done.59, s32[4]{0:T(128)} %copy-done.50, s32[4]{0:T(128)} %copy-done.52, s32[1]{0:T(128)} %bitcast.16.core, s32[2]{0:T(128)} %copy-done.58, ...), custom_call_target="tpu_custom_call" | custom-call | flops 1000 | bytes 3000000 | tf_op jit(solution)/shard_map/pallas_call | solution.py:136
  396.9 3.4 collective-permute-done.60
  402.6 10.2 %collective-permute-done.58 = bf16[4,4,2,16,576]{4,3,2,1,0:T(8,128)(2,1)S(1)} collective-permute-done((bf16[4,4,2,16,576]{4,3,2,1,0:T(8,128)(2,1)S(1)}, bf16[4,4,2,16,576]{4,3,2,1,0:T(8,128)(2,1)S(1)}, u32[]{:S(2)}, u32[]{:S(2)}) %collective-permute-start.58) | collective-permute-done | bytes 589856 | tf_op jit(solution)/shard_map/ppermute | solution.py:45
  418.9 11.1 %collective-permute-done.67 = bf16[2,4,16,704]{3,2,1,0:T(8,128)(2,1)S(1)} collective-permute-done((bf16[2,4,16,704]{3,2,1,0:T(8,128)(2,1)S(1)}, bf16[2,4,16,704]{3,2,1,0:T(8,128)(2,1)S(1)}, u32[]{:S(2)}, u32[]{:S(2)}) %collective-permute-start.67) | collective-permute-done | bytes 180256 | tf_op jit(solution)/shard_map/ppermute | solution.py:45
  430.3 4.0 collective-permute-done.65
  436.1 3.4 collective-permute-start.64
  441.0 15.8 %collective-permute-done.64 = f32[2,2048]{1,0:T(2,128)S(1)} collective-permute-done((f32[2,2048]{1,0:T(2,128)S(1)}, f32[2,2048]{1,0:T(2,128)S(1)}, u32[]{:S(2)}, u32[]{:S(2)}) %collective-permute-start.64) | collective-permute-done | bytes 16416 | tf_op jit(solution)/shard_map/ppermute | solution.py:45
  457.2 4.6 collective-permute-start.70
  464.3 2.9 collective-permute-done.71
  475.7 3.1 collective-permute-done.73
  480.9 3.3 collective-permute-done.85
  494.5 3.2 collective-permute-done.86
  507.4 4.8 shard_map.231
  514.8 4.2 collective-permute-done.81.refs_2_
  (465 shorter events, 171.3 us)
Async XLA Ops:
  7.2 64.1 %all-gather.7.cloned.1.call-start = ((), (), s32[]{:S(2)}) async-start(), calls=%async_computation.3 | async-start | bytes 4718592 | tf_op jit(solution)/shard_map/all_gather | solution.py:813
  28.5 104.4 %all-gather.11.cloned.1.call-start = ((), (), s32[]{:S(2)}) async-start(), calls=%async_computation.8 | async-start | bytes 5898240 | tf_op jit(solution)/shard_map/all_gather | solution.py:843
  33.6 22.3 %collective-permute-start.24 = (bf16[4,3,32,704]{3,2,1,0:T(8,128)(2,1)}, bf16[4,3,32,704]{3,2,1,0:T(8,128)(2,1)}, u32[]{:S(2)}, u32[]{:S(2)}) collective-permute-start(bf16[4,3,32,704]{3,2,1,0:T(8,128)(2,1)} %get-tuple-element.154), channel_id=1, source_target_pairs={{0,1},{1,0},{2,3},{3,2},{4,5},{5,4},{6,7},{7,6},{8,9},{9,8},{10,11... | collective-permute-start | bytes 1622024 | tf_op jit(solution)/shard_map/ppermute | solution.py:45
  33.7 18.0 %collective-permute-start.4 = (bf16[8,32,256]{2,1,0:T(8,128)(2,1)S(1)}, bf16[8,32,256]{2,1,0:T(8,128)(2,1)S(1)}, u32[]{:S(2)}, u32[]{:S(2)}) collective-permute-start(bf16[8,32,256]{2,1,0:T(8,128)(2,1)S(1)} %bitcast.228), channel_id=1, source_target_pairs={{0,0},{1,8},{2,1},{3,9},{4,2},{5,10},{6,3},{7,11},{8,4},{9,12},{10... | collective-permute-start | bytes 393224 | tf_op jit(solution)/shard_map/ppermute | solution.py:45
  57.9 19.5 %collective-permute-start.25 = (bf16[2,3,32,704]{3,2,1,0:T(8,128)(2,1)}, bf16[2,3,32,704]{3,2,1,0:T(8,128)(2,1)}, u32[]{:S(2)}, u32[]{:S(2)}) collective-permute-start(bf16[2,3,32,704]{3,2,1,0:T(8,128)(2,1)} %pad_maximum_fusion.8), channel_id=1, source_target_pairs={{0,2},{1,7},{2,4},{3,1},{4,6},{5,3},{6,0},{7,5},{8,10},{9,15},{10,... | collective-permute-start | bytes 811016 | tf_op jit(solution)/shard_map/ppermute | solution.py:45
  60.8 16.6 %collective-permute-start.26 = (bf16[2,3,32,704]{3,2,1,0:T(8,128)(2,1)}, bf16[2,3,32,704]{3,2,1,0:T(8,128)(2,1)}, u32[]{:S(2)}, u32[]{:S(2)}) collective-permute-start(bf16[2,3,32,704]{3,2,1,0:T(8,128)(2,1)} %pad_maximum_fusion.9), channel_id=1, source_target_pairs={{0,6},{1,3},{2,0},{3,5},{4,2},{5,7},{6,4},{7,1},{8,14},{9,11},{10,... | collective-permute-start | bytes 811016 | tf_op jit(solution)/shard_map/ppermute | solution.py:45
  62.6 14.8 %collective-permute-start.27 = (bf16[2,3,32,704]{3,2,1,0:T(8,128)(2,1)}, bf16[2,3,32,704]{3,2,1,0:T(8,128)(2,1)}, u32[]{:S(2)}, u32[]{:S(2)}) collective-permute-start(bf16[2,3,32,704]{3,2,1,0:T(8,128)(2,1)} %pad_maximum_fusion.10), channel_id=1, source_target_pairs={{0,4},{1,5},{2,6},{3,7},{4,0},{5,1},{6,2},{7,3},{8,12},{9,13},{10,... | collective-permute-start | bytes 811016 | tf_op jit(solution)/shard_map/ppermute | solution.py:45
  79.8 120.3 %all-gather.9.cloned.1.call-start = ((), (), s32[]{:S(2)}) async-start(), calls=%async_computation.4 | async-start | bytes 4718592 | tf_op jit(solution)/shard_map/all_gather | solution.py:827
  81.1 278.9 %reduce-scatter.6.cloned.1.call-start = ((), (), s32[]{:S(2)}) async-start(), calls=%async_computation.6 | async-start | bytes 5898240 | tf_op jit(solution)/shard_map/reduce_scatter | solution.py:888
  132.8 54.4 %collective-permute-start.28 = (bf16[4,8,3,32,704]{4,3,2,1,0:T(8,128)(2,1)}, bf16[4,8,3,32,704]{4,3,2,1,0:T(8,128)(2,1)}, u32[]{:S(2)}, u32[]{:S(2)}) collective-permute-start(bf16[4,8,3,32,704]{4,3,2,1,0:T(8,128)(2,1)} %bitcast.196), channel_id=1, source_target_pairs={{0,8},{1,73},{2,10},{3,75},{4,12},{5,77},{6,14},{7,79},{8,64},{9,1... | collective-permute-start | bytes 12976136 | tf_op jit(solution)/shard_map/ppermute | solution.py:45
  134.8 20.5 %collective-permute-start.21 = (bf16[128,2048]{1,0:T(8,128)(2,1)S(1)}, bf16[128,2048]{1,0:T(8,128)(2,1)S(1)}, u32[]{:S(2)}, u32[]{:S(2)}) collective-permute-start(bf16[128,2048]{1,0:T(8,128)(2,1)S(1)} %add_convert_fusion.6), channel_id=1, source_target_pairs={{0,4},{1,5},{2,6},{3,7},{4,0},{5,1},{6,2},{7,3},{8,12},{9,13},{10,... | collective-permute-start | bytes 1572872 | tf_op jit(solution)/shard_map/ppermute | solution.py:45
  138.2 38.5 %collective-permute-start.20 = (bf16[128,2048]{1,0:T(8,128)(2,1)S(1)}, bf16[128,2048]{1,0:T(8,128)(2,1)S(1)}, u32[]{:S(2)}, u32[]{:S(2)}) collective-permute-start(bf16[128,2048]{1,0:T(8,128)(2,1)S(1)} %add_convert_fusion.7), channel_id=1, source_target_pairs={{0,2},{1,7},{2,4},{3,1},{4,6},{5,3},{6,0},{7,5},{8,10},{9,15},{10,... | collective-permute-start | bytes 1572872 | tf_op jit(solution)/shard_map/ppermute | solution.py:45
  140.1 36.5 %collective-permute-start.19 = (bf16[128,2048]{1,0:T(8,128)(2,1)S(1)}, bf16[128,2048]{1,0:T(8,128)(2,1)S(1)}, u32[]{:S(2)}, u32[]{:S(2)}) collective-permute-start(bf16[128,2048]{1,0:T(8,128)(2,1)S(1)} %add_convert_fusion.8), channel_id=1, source_target_pairs={{0,6},{1,3},{2,0},{3,5},{4,2},{5,7},{6,4},{7,1},{8,14},{9,11},{10,... | collective-permute-start | bytes 1572872 | tf_op jit(solution)/shard_map/ppermute | solution.py:45
  148.2 28.4 %collective-permute-start.18 = (bf16[128,2048]{1,0:T(8,128)(2,1)S(1)}, bf16[128,2048]{1,0:T(8,128)(2,1)S(1)}, u32[]{:S(2)}, u32[]{:S(2)}) collective-permute-start(bf16[128,2048]{1,0:T(8,128)(2,1)S(1)} %get-tuple-element.151), channel_id=1, source_target_pairs={{0,1},{1,0},{2,3},{3,2},{4,5},{5,4},{6,7},{7,6},{8,9},{9,8},{10,11... | collective-permute-start | bytes 1572872 | tf_op jit(solution)/shard_map/ppermute | solution.py:45
  177.5 18.2 %collective-permute-start.23 = (bf16[128,2048]{1,0:T(8,128)(2,1)S(1)}, bf16[128,2048]{1,0:T(8,128)(2,1)}, u32[]{:S(2)}, u32[]{:S(2)}) collective-permute-start(bf16[128,2048]{1,0:T(8,128)(2,1)S(1)} %multiply_convert_fusion.refs_0_), channel_id=1, source_target_pairs={{0,2},{1,7},{2,4},{3,1},{4,6},{5,3},{6,0},{7,5},{8,10},{9,15},{10,... | collective-permute-start | bytes 1572872 | tf_op jit(solution)/shard_map/ppermute | solution.py:45
  180.0 20.1 %collective-permute-start.22 = (bf16[128,2048]{1,0:T(8,128)(2,1)S(1)}, bf16[128,2048]{1,0:T(8,128)(2,1)}, u32[]{:S(2)}, u32[]{:S(2)}) collective-permute-start(bf16[128,2048]{1,0:T(8,128)(2,1)S(1)} %multiply_convert_fusion.refs_0_), channel_id=1, source_target_pairs={{0,1},{1,0},{2,3},{3,2},{4,5},{5,4},{6,7},{7,6},{8,9},{9,8},{10,11... | collective-permute-start | bytes 1572872 | tf_op jit(solution)/shard_map/ppermute | solution.py:45
  196.0 23.7 %collective-permute-start.31 = (bf16[128,2048]{1,0:T(8,128)(2,1)S(1)}, bf16[128,2048]{1,0:T(8,128)(2,1)}, u32[]{:S(2)}, u32[]{:S(2)}) collective-permute-start(bf16[128,2048]{1,0:T(8,128)(2,1)S(1)} %multiply_convert_fusion.refs_0_), channel_id=1, source_target_pairs={{0,4},{1,5},{2,6},{3,7},{4,0},{5,1},{6,2},{7,3},{8,12},{9,13},{10,... | collective-permute-start | bytes 1572872 | tf_op jit(solution)/shard_map/ppermute | solution.py:45
  198.9 20.8 %collective-permute-start.30 = (bf16[128,2048]{1,0:T(8,128)(2,1)S(1)}, bf16[128,2048]{1,0:T(8,128)(2,1)}, u32[]{:S(2)}, u32[]{:S(2)}) collective-permute-start(bf16[128,2048]{1,0:T(8,128)(2,1)S(1)} %multiply_convert_fusion.refs_0_), channel_id=1, source_target_pairs={{0,6},{1,3},{2,0},{3,5},{4,2},{5,7},{6,4},{7,1},{8,14},{9,11},{10,... | collective-permute-start | bytes 1572872 | tf_op jit(solution)/shard_map/ppermute | solution.py:45
  244.2 28.0 %collective-permute-start.36 = (bf16[128,2048]{1,0:T(8,128)(2,1)}, bf16[128,2048]{1,0:T(8,128)(2,1)}, u32[]{:S(2)}, u32[]{:S(2)}) collective-permute-start(bf16[128,2048]{1,0:T(8,128)(2,1)} %fusion.11), channel_id=1, source_target_pairs={{0,6},{1,3},{2,0},{3,5},{4,2},{5,7},{6,4},{7,1},{8,14},{9,11},{10,... | collective-permute-start | bytes 1572872 | tf_op jit(solution)/shard_map/ppermute | solution.py:45
  247.1 25.0 %collective-permute-start.38 = (bf16[128,2048]{1,0:T(8,128)(2,1)}, bf16[128,2048]{1,0:T(8,128)(2,1)}, u32[]{:S(2)}, u32[]{:S(2)}) collective-permute-start(bf16[128,2048]{1,0:T(8,128)(2,1)} %get-tuple-element.266), channel_id=1, source_target_pairs={{0,4},{1,5},{2,6},{3,7},{4,0},{5,1},{6,2},{7,3},{8,12},{9,13},{10,... | collective-permute-start | bytes 1572872 | tf_op jit(solution)/shard_map/ppermute | solution.py:45
  248.4 23.8 %collective-permute-start.37 = (bf16[128,2048]{1,0:T(8,128)(2,1)}, bf16[128,2048]{1,0:T(8,128)(2,1)}, u32[]{:S(2)}, u32[]{:S(2)}) collective-permute-start(bf16[128,2048]{1,0:T(8,128)(2,1)} %get-tuple-element.267), channel_id=1, source_target_pairs={{0,2},{1,7},{2,4},{3,1},{4,6},{5,3},{6,0},{7,5},{8,10},{9,15},{10,... | collective-permute-start | bytes 1572872 | tf_op jit(solution)/shard_map/ppermute | solution.py:45
  277.2 115.4 %reduce-scatter.4.cloned.1.call-start = ((), (), s32[]{:S(2)}) async-start(), calls=%async_computation.5 | async-start | bytes 4718592 | tf_op jit(solution)/shard_map/reduce_scatter | solution.py:889
  277.8 156.9 %all-gather.13.cloned.1.call-start = ((), (), s32[]{:S(2)}) async-start(), calls=%async_computation.9 | async-start | bytes 1114112 | tf_op jit(solution)/shard_map/all_gather | solution.py:930
  279.4 24.1 %collective-permute-start.45 = (bf16[4,2,2,3,16,704]{5,4,2,3,1,0:T(8,128)(2,1)S(1)}, bf16[4,2,2,3,16,704]{5,4,2,3,1,0:T(8,128)(2,1)S(1)}, u32[]{:S(2)}, u32[]{:S(2)}) collective-permute-start(bf16[4,2,2,3,16,704]{5,4,2,3,1,0:T(8,128)(2,1)S(1)} %copy.131), channel_id=1, source_target_pairs={{0,8},{1,73},{2,10},{3,75},{4,12},{5,77},{6,14},{7,79},{8,64},{9,1... | collective-permute-start | bytes 3244040 | tf_op jit(solution)/shard_map/ppermute | solution.py:45
  285.5 14.5 %collective-permute-start.41 = (bf16[128,2048]{1,0:T(8,128)(2,1)S(1)}, bf16[128,2048]{1,0:T(8,128)(2,1)S(1)}, u32[]{:S(2)}, u32[]{:S(2)}) collective-permute-start(bf16[128,2048]{1,0:T(8,128)(2,1)S(1)} %get-tuple-element.255.refs_1_.refs_8_), channel_id=1, source_target_pairs={{0,6},{1,3},{2,0},{3,5},{4,2},{5,7},{6,4},{7,1},{8,14},{9,11},{10,... | collective-permute-start | bytes 1572872 | tf_op jit(solution)/shard_map/ppermute | solution.py:45
  303.1 29.4 %collective-permute-start.47 = (bf16[4,2,2,3,16,704]{5,4,2,3,1,0:T(8,128)(2,1)S(1)}, bf16[4,2,2,3,16,704]{5,4,2,3,1,0:T(8,128)(2,1)S(1)}, u32[]{:S(2)}, u32[]{:S(2)}) collective-permute-start(bf16[4,2,2,3,16,704]{5,4,2,3,1,0:T(8,128)(2,1)S(1)} %copy.134), channel_id=1, source_target_pairs={{0,72},{1,9},{2,74},{3,11},{4,76},{5,13},{6,78},{7,15},{8,0},{9,65... | collective-permute-start | bytes 3244040 | tf_op jit(solution)/shard_map/ppermute | solution.py:45
  303.8 33.5 %collective-permute-start.48 = (bf16[4,2,2,3,16,704]{5,4,2,3,1,0:T(8,128)(2,1)S(1)}, bf16[4,2,2,3,16,704]{5,4,2,3,1,0:T(8,128)(2,1)S(1)}, u32[]{:S(2)}, u32[]{:S(2)}) collective-permute-start(bf16[4,2,2,3,16,704]{5,4,2,3,1,0:T(8,128)(2,1)S(1)} %add_convert_fusion.1), channel_id=1, source_target_pairs={{0,8},{1,73},{2,10},{3,75},{4,12},{5,77},{6,14},{7,79},{8,64},{9,1... | collective-permute-start | bytes 3244040 | tf_op jit(solution)/shard_map/ppermute | solution.py:45
  306.8 20.4 %collective-permute-start.44 = (bf16[128,2048]{1,0:T(8,128)(2,1)S(1)}, bf16[128,2048]{1,0:T(8,128)(2,1)S(1)}, u32[]{:S(2)}, u32[]{:S(2)}) collective-permute-start(bf16[128,2048]{1,0:T(8,128)(2,1)S(1)} %get-tuple-element.255.refs_1_.refs_8_), channel_id=1, source_target_pairs={{0,4},{1,5},{2,6},{3,7},{4,0},{5,1},{6,2},{7,3},{8,12},{9,13},{10,... | collective-permute-start | bytes 1572872 | tf_op jit(solution)/shard_map/ppermute | solution.py:45
  338.0 15.2 %collective-permute-start.51 = (bf16[2,2,3,16,704]{4,3,1,2,0:T(8,128)(2,1)S(1)}, bf16[2,2,3,16,704]{4,3,1,2,0:T(8,128)(2,1)S(1)}, u32[]{:S(2)}, u32[]{:S(2)}) collective-permute-start(bf16[2,2,3,16,704]{4,3,1,2,0:T(8,128)(2,1)S(1)} %get-tuple-element.263), channel_id=1, source_target_pairs={{0,32},{1,33},{2,34},{3,35},{4,36},{5,37},{6,38},{7,39},{8,40},{9,... | collective-permute-start | bytes 811016 | tf_op jit(solution)/shard_map/ppermute | solution.py:45
  345.3 14.0 %collective-permute-start.53 = (bf16[2,2,3,16,704]{4,3,1,2,0:T(8,128)(2,1)S(1)}, bf16[2,2,3,16,704]{4,3,1,2,0:T(8,128)(2,1)S(1)}, u32[]{:S(2)}, u32[]{:S(2)}) collective-permute-start(bf16[2,2,3,16,704]{4,3,1,2,0:T(8,128)(2,1)S(1)} %get-tuple-element.264), channel_id=1, source_target_pairs={{0,16},{1,49},{2,18},{3,51},{4,20},{5,53},{6,22},{7,55},{8,24},{9,... | collective-permute-start | bytes 811016 | tf_op jit(solution)/shard_map/ppermute | solution.py:45
  346.1 13.7 %collective-permute-start.52 = (bf16[2,2,3,16,704]{4,3,1,2,0:T(8,128)(2,1)S(1)}, bf16[2,2,3,16,704]{4,3,1,2,0:T(8,128)(2,1)S(1)}, u32[]{:S(2)}, u32[]{:S(2)}) collective-permute-start(bf16[2,2,3,16,704]{4,3,1,2,0:T(8,128)(2,1)S(1)} %get-tuple-element.265), channel_id=1, source_target_pairs={{0,48},{1,17},{2,50},{3,19},{4,52},{5,21},{6,54},{7,23},{8,56},{9,... | collective-permute-start | bytes 811016 | tf_op jit(solution)/shard_map/ppermute | solution.py:45
  367.9 130.8 %reduce-scatter.8.cloned.1.call-start = ((), (), s32[]{:S(2)}) async-start(), calls=%async_computation.7 | async-start | bytes 4718592 | tf_op jit(solution)/shard_map/reduce_scatter | solution.py:938
  369.2 19.9 %collective-permute-start.54 = (bf16[2,2,3,16,704]{4,3,1,2,0:T(8,128)(2,1)S(1)}, bf16[2,2,3,16,704]{4,3,1,2,0:T(8,128)(2,1)S(1)}, u32[]{:S(2)}, u32[]{:S(2)}) collective-permute-start(bf16[2,2,3,16,704]{4,3,1,2,0:T(8,128)(2,1)S(1)} %get-tuple-element.260), channel_id=1, source_target_pairs={{0,64},{1,65},{2,66},{3,67},{4,68},{5,69},{6,70},{7,71},{8,72},{9,... | collective-permute-start | bytes 811016 | tf_op jit(solution)/shard_map/ppermute | solution.py:45
  375.3 13.8 %collective-permute-start.56 = (bf16[2,2,3,16,704]{4,3,1,2,0:T(8,128)(2,1)S(1)}, bf16[2,2,3,16,704]{4,3,1,2,0:T(8,128)(2,1)S(1)}, u32[]{:S(2)}, u32[]{:S(2)}) collective-permute-start(bf16[2,2,3,16,704]{4,3,1,2,0:T(8,128)(2,1)S(1)} %get-tuple-element.261), channel_id=1, source_target_pairs={{0,8},{1,73},{2,10},{3,75},{4,12},{5,77},{6,14},{7,79},{8,64},{9,1... | collective-permute-start | bytes 811016 | tf_op jit(solution)/shard_map/ppermute | solution.py:45
  375.3 16.1 %collective-permute-start.55 = (bf16[2,2,3,16,704]{4,3,1,2,0:T(8,128)(2,1)S(1)}, bf16[2,2,3,16,704]{4,3,1,2,0:T(8,128)(2,1)S(1)}, u32[]{:S(2)}, u32[]{:S(2)}) collective-permute-start(bf16[2,2,3,16,704]{4,3,1,2,0:T(8,128)(2,1)S(1)} %get-tuple-element.262), channel_id=1, source_target_pairs={{0,72},{1,9},{2,74},{3,11},{4,76},{5,13},{6,78},{7,15},{8,0},{9,65... | collective-permute-start | bytes 811016 | tf_op jit(solution)/shard_map/ppermute | solution.py:45
  394.8 44.6 %collective-permute-start.57 = (bf16[4,4,2,16,576]{4,3,2,1,0:T(8,128)(2,1)}, bf16[4,4,2,16,576]{4,3,2,1,0:T(8,128)(2,1)}, u32[]{:S(2)}, u32[]{:S(2)}) collective-permute-start(bf16[4,4,2,16,576]{4,3,2,1,0:T(8,128)(2,1)} %get-tuple-element.230), channel_id=1, source_target_pairs={{0,48},{1,17},{2,50},{3,19},{4,52},{5,21},{6,54},{7,23},{8,56},{9,... | collective-permute-start | bytes 1769480 | tf_op jit(solution)/shard_map/ppermute | solution.py:45
  396.1 16.8 %collective-permute-start.58 = (bf16[4,4,2,16,576]{4,3,2,1,0:T(8,128)(2,1)S(1)}, bf16[4,4,2,16,576]{4,3,2,1,0:T(8,128)(2,1)S(1)}, u32[]{:S(2)}, u32[]{:S(2)}) collective-permute-start(bf16[4,4,2,16,576]{4,3,2,1,0:T(8,128)(2,1)S(1)} %copy-done.89), channel_id=1, source_target_pairs={{0,16},{1,49},{2,18},{3,51},{4,20},{5,53},{6,22},{7,55},{8,24},{9,... | collective-permute-start | bytes 1769480 | tf_op jit(solution)/shard_map/ppermute | solution.py:45
  413.9 25.6 %collective-permute-start.59 = (bf16[4,4,2,16,576]{4,3,2,1,0:T(8,128)(2,1)}, bf16[4,4,2,16,576]{4,3,2,1,0:T(8,128)(2,1)}, u32[]{:S(2)}, u32[]{:S(2)}) collective-permute-start(bf16[4,4,2,16,576]{4,3,2,1,0:T(8,128)(2,1)} %add_convert_fusion.3), channel_id=1, source_target_pairs={{0,16},{1,49},{2,18},{3,51},{4,20},{5,53},{6,22},{7,55},{8,24},{9,... | collective-permute-start | bytes 1769480 | tf_op jit(solution)/shard_map/ppermute | solution.py:45
  414.0 16.1 %collective-permute-start.67 = (bf16[2,4,16,704]{3,2,1,0:T(8,128)(2,1)S(1)}, bf16[2,4,16,704]{3,2,1,0:T(8,128)(2,1)S(1)}, u32[]{:S(2)}, u32[]{:S(2)}) collective-permute-start(bf16[2,4,16,704]{3,2,1,0:T(8,128)(2,1)S(1)} %get-tuple-element.272), channel_id=1, source_target_pairs={{0,32},{1,33},{2,34},{3,35},{4,36},{5,37},{6,38},{7,39},{8,40},{9,... | collective-permute-start | bytes 540680 | tf_op jit(solution)/shard_map/ppermute | solution.py:45
  415.1 15.3 %collective-permute-start.66 = (bf16[2,4,16,704]{3,2,1,0:T(8,128)(2,1)S(1)}, bf16[2,4,16,704]{3,2,1,0:T(8,128)(2,1)S(1)}, u32[]{:S(2)}, u32[]{:S(2)}) collective-permute-start(bf16[2,4,16,704]{3,2,1,0:T(8,128)(2,1)S(1)} %get-tuple-element.272), channel_id=1, source_target_pairs={{0,48},{1,17},{2,50},{3,19},{4,52},{5,21},{6,54},{7,23},{8,56},{9,... | collective-permute-start | bytes 540680 | tf_op jit(solution)/shard_map/ppermute | solution.py:45
  417.4 16.9 %collective-permute-start.65 = (bf16[2,4,16,704]{3,2,1,0:T(8,128)(2,1)S(1)}, bf16[2,4,16,704]{3,2,1,0:T(8,128)(2,1)S(1)}, u32[]{:S(2)}, u32[]{:S(2)}) collective-permute-start(bf16[2,4,16,704]{3,2,1,0:T(8,128)(2,1)S(1)} %get-tuple-element.272), channel_id=1, source_target_pairs={{0,16},{1,49},{2,18},{3,51},{4,20},{5,53},{6,22},{7,55},{8,24},{9,... | collective-permute-start | bytes 540680 | tf_op jit(solution)/shard_map/ppermute | solution.py:45
  430.1 31.8 %collective-permute-start.83 = (bf16[2,4,2,16,704]{4,3,1,0,2:T(8,128)(2,1)}, bf16[2,4,2,16,704]{4,3,1,0,2:T(8,128)(2,1)S(1)}, u32[]{:S(2)}, u32[]{:S(2)}) collective-permute-start(bf16[2,4,2,16,704]{4,3,1,0,2:T(8,128)(2,1)} %pad_maximum_fusion.5), channel_id=1, source_target_pairs={{0,64},{1,65},{2,66},{3,67},{4,68},{5,69},{6,70},{7,71},{8,72},{9,... | collective-permute-start | bytes 1081352 | tf_op jit(solution)/shard_map/ppermute | solution.py:45
  434.4 35.3 %collective-permute-start.72 = (bf16[4,2,4,16,704]{4,3,2,1,0:T(8,128)(2,1)S(1)}, bf16[4,2,4,16,704]{4,3,2,1,0:T(8,128)(2,1)S(1)}, u32[]{:S(2)}, u32[]{:S(2)}) collective-permute-start(bf16[4,2,4,16,704]{4,3,2,1,0:T(8,128)(2,1)S(1)} %pad_maximum_fusion.2.refs_4_), channel_id=1, source_target_pairs={{0,64},{1,65},{2,66},{3,67},{4,68},{5,69},{6,70},{7,71},{8,72},{9,... | collective-permute-start | bytes 2162696 | tf_op jit(solution)/shard_map/ppermute | solution.py:45
  436.1 20.7 %collective-permute-start.64 = (f32[2,2048]{1,0:T(2,128)S(1)}, f32[2,2048]{1,0:T(2,128)S(1)}, u32[]{:S(2)}, u32[]{:S(2)}) collective-permute-start(f32[2,2048]{1,0:T(2,128)S(1)} %slice.325), channel_id=1, source_target_pairs={{0,64},{1,65},{2,66},{3,67},{4,68},{5,69},{6,70},{7,71},{8,72},{9,... | collective-permute-start | bytes 49160 | tf_op jit(solution)/shard_map/ppermute | solution.py:45
  467.2 17.1 %collective-permute-start.85 = (bf16[2,2,4,2,16,704]{5,4,2,1,3,0:T(8,128)(2,1)S(1)}, bf16[2,2,4,2,16,704]{5,4,2,1,3,0:T(8,128)(2,1)S(1)}, u32[]{:S(2)}, u32[]{:S(2)}) collective-permute-start(bf16[2,2,4,2,16,704]{5,4,2,1,3,0:T(8,128)(2,1)S(1)} %pad_maximum_fusion.3), channel_id=1, source_target_pairs={{0,48},{1,17},{2,50},{3,19},{4,52},{5,21},{6,54},{7,23},{8,56},{9,... | collective-permute-start | bytes 2162696 | tf_op jit(solution)/shard_map/ppermute | solution.py:45
  467.2 17.4 %collective-permute-start.84 = (bf16[2,2,4,2,16,704]{5,4,2,1,3,0:T(8,128)(2,1)S(1)}, bf16[2,2,4,2,16,704]{5,4,2,1,3,0:T(8,128)(2,1)S(1)}, u32[]{:S(2)}, u32[]{:S(2)}) collective-permute-start(bf16[2,2,4,2,16,704]{5,4,2,1,3,0:T(8,128)(2,1)S(1)} %pad_maximum_fusion.3), channel_id=1, source_target_pairs={{0,16},{1,49},{2,18},{3,51},{4,20},{5,53},{6,22},{7,55},{8,24},{9,... | collective-permute-start | bytes 2162696 | tf_op jit(solution)/shard_map/ppermute | solution.py:45
  469.3 23.1 %collective-permute-start.78 = (f32[2,2048]{1,0:T(2,128)S(1)}, f32[2,2048]{1,0:T(2,128)S(1)}, u32[]{:S(2)}, u32[]{:S(2)}) collective-permute-start(f32[2,2048]{1,0:T(2,128)S(1)} %add.347), channel_id=1, source_target_pairs={{0,16},{1,49},{2,18},{3,51},{4,20},{5,53},{6,22},{7,55},{8,24},{9,... | collective-permute-start | bytes 49160 | tf_op jit(solution)/shard_map/ppermute | solution.py:45
  504.7 14.3 %collective-permute-start.81 = (bf16[2,2,4,16,576]{4,3,2,1,0:T(8,128)(2,1)S(1)}, bf16[2,2,4,16,576]{4,3,2,1,0:T(8,128)(2,1)S(1)}, u32[]{:S(2)}, u32[]{:S(2)}) collective-permute-start(bf16[2,2,4,16,576]{4,3,2,1,0:T(8,128)(2,1)S(1)} %pad_maximum_fusion.6.refs_0_), channel_id=1, source_target_pairs={{0,48},{1,17},{2,50},{3,19},{4,52},{5,21},{6,54},{7,23},{8,56},{9,... | collective-permute-start | bytes 884744 | tf_op jit(solution)/shard_map/ppermute | solution.py:45
  (138 other events, 2119.9 us)
Sparse Core Ops, SparseCore 0:
  28.6 32.7 all-gather.6
  79.9 52.9 all-gather.10
  134.6 45.8 all-gather.8
  277.3 50.8 reduce-scatter.5
  330.4 38.1 reduce-scatter.3
  370.2 32.3 all-gather.12
  405.0 39.4 reduce-scatter.7
